TPU v7x, 32 devices: a whole 2x2x4 slice. The times are simulated.
32 devices in a mesh: body: 2 (over core), sub: 16 (over z, y, x).
Axes of the slice: x: 2, y: 2, z: 4, core: 2. Of those that a mesh axis runs over, the one named last changes fastest.
Arguments:
- rhs: float32 [8, 1024, 256], P(None, 'sub'), may hold values from -50 to 50
- compliance: float32 [1024, 256], P('sub'), may hold values from 0.5 to 2
- plate_owner: int32 [1024, 1], P('sub'), may hold values from 0 to 15; in each aligned block of 64 rows (0 to 63, 64 to 127, ...) at most 8 rows name the same one
- found_owner: int32 [1024, 1], P('sub'), may hold values from 0 to 15; in each aligned block of 64 rows (0 to 63, 64 to 127, ...) at most 8 rows name the same one
- slot_pairs: int32 [1024, 2], P('sub'), may hold values from 0 to 7
- active: int32 [1024], P('sub'), may hold values 0 or 1
- inverse: bfloat16 [2, 16, 2048, 2048], P('body', 'sub'), may hold values from -0.06 to 4, as said below
Outputs:
- multipliers: float32 [8, 1024, 256], P(None, 'sub')
Inputs may be any that keep to these rules, and one draw needn't show every extreme that they name: `plate_owner`: at most 8 patches among the list of one index of sub name the same plate substructure; some list names one exactly 8 times. `found_owner`: at most 8 patches among the list of one index of sub name the same foundation substructure; some list names one exactly 8 times. Each block inverse[b, t] is symmetric positive definite.
All inputs are finite; a program needn't handle non-finite values. No bound on the sum of `active` on one device may be relied on, other than what follows from the above.
Results may differ from a plain program's by a relative error of at most 0.0055.
Values sent between devices are 32-bit elements; how exact they have to be, the bound alone decides.
No kernel may reach another device: no remote copies, remote signals or barrier semaphores. Data moves between devices by JAX's collectives and lax.ppermute only.
A program may use at most 64 MiB of HBM per device.

v0:
```python
import jax
import jax.numpy as jnp
from jax import lax
from jax.sharding import PartitionSpec as P

ITERS = 4


def products(left, right):
    return jnp.sum(left * right, axis=(1, 2))


def squares(residual):
    return lax.psum(products(residual, residual), "sub")


def on_device(rhs, compliance, plate_owner, found_owner, slot_pairs, active, inverse):
    nsub = lax.axis_size("sub")
    side = lax.axis_index("body")
    ncase, npatch, block_width = rhs.shape
    local_inverse_block = inverse[0, 0]
    number_of_slots = local_inverse_block.shape[0] // block_width
    room = max(2, 2 * npatch // nsub)
    nrow = nsub * room
    owner = jnp.where(side == 0, plate_owner[:, 0], found_owner[:, 0])
    slot = jnp.where(side == 0, slot_pairs[:, 0], slot_pairs[:, 1])
    patch_index = jnp.arange(npatch, dtype=jnp.int32)
    earlier = patch_index[None, :] < patch_index[:, None]
    same_owner = owner[None, :] == owner[:, None]
    rank = jnp.sum(jnp.where(earlier & same_owner, 1, 0), axis=1).astype(jnp.int32)
    dest_row = owner * room + rank
    placed = dest_row[None, :] == jnp.arange(nrow, dtype=jnp.int32)[:, None]
    source = jnp.sum(jnp.where(placed, patch_index[None, :], 0), axis=1)
    filled = jnp.any(placed, axis=1)
    sent_slot = jnp.where(filled, jnp.take(slot, source), -1)
    received_slot = lax.all_to_all(sent_slot, "sub", split_axis=0, concat_axis=0, tiled=True)
    slot_lookup_table = (
        received_slot[None, :] == jnp.arange(number_of_slots, dtype=jnp.int32)[:, None]
    ).astype(jnp.float32)
    send_valid = filled.astype(jnp.float32)[None, :, None]
    keep = active.astype(jnp.float32)[None, :, None]
    residual = keep * rhs
    solution = jnp.zeros_like(rhs)
    direction = residual
    norm_now = squares(residual)
    for step in range(ITERS):
        outgoing = jnp.take(direction, source, axis=1) * send_valid
        column_entries = lax.all_to_all(outgoing, "sub", split_axis=1, concat_axis=1, tiled=True)
        load_vectors = jnp.einsum(
            "sb,rbk->rsk", slot_lookup_table, column_entries, precision=lax.Precision.HIGHEST
        )
        load_vectors = load_vectors.reshape(
            column_entries.shape[0], number_of_slots * block_width
        ).astype(jnp.bfloat16)
        response = jnp.dot(load_vectors, local_inverse_block, preferred_element_type=jnp.float32)
        plate_piece = lax.all_gather(response[None], "sub", axis=0, tiled=True)
        start = jnp.int32(0)
        slot_count = plate_piece.shape[0]
        local = jnp.clip(owner, 0, slot_count - 1)
        block_list = plate_piece.reshape(
            slot_count, plate_piece.shape[1], number_of_slots, block_width
        )
        chosen = block_list[local, :, slot, :]
        inside = (owner >= start) & (owner < start + slot_count)
        own_part = jnp.transpose(jnp.where(inside[:, None, None], chosen, 0.0), (1, 0, 2))
        total = lax.psum(own_part, "body")
        image = keep * (total + compliance[None] * direction)
        alpha = norm_now / lax.psum(products(direction, image), "sub")
        solution = solution + alpha[:, None, None] * direction
        residual = residual - alpha[:, None, None] * image
        norm_next = squares(residual)
        direction = residual + (norm_next / norm_now)[:, None, None] * direction
        norm_now = norm_next
    return solution


def solution(mesh):
    in_specs = (
        P(None, "sub", None),
        P("sub", None),
        P("sub", None),
        P("sub", None),
        P("sub", None),
        P("sub"),
        P("body", "sub", None, None),
    )
    out_specs = P(None, "sub", None)
    return jax.shard_map(
        on_device, mesh=mesh, in_specs=in_specs, out_specs=out_specs, check_vma=False
    )
```

profile of v0, /device:TPU:0, one launch (start us, length us, event | category | flops | bytes accessed | tf_op | source)
XLA Modules:
  0.0 742.0 jit_solution(12994702143923376687)
XLA Ops:
  10.5 8.3 %all-to-all-start.1 = ((s32[16,8,1]{1,2,0:T(1,128)}), s32[16,8,1]{1,2,0:T(1,128)S(1)}, u32[]{:S(2)}, u32[]{:S(2)}) async-start(s32[16,8,1]{1,2,0:T(1,128)} %bitcast.5), calls=%async_computation.1 | async-start | bytes 16384 | tf_op jit(solution)/shard_map/all_to_all | solution.py:36
  23.0 3.0 all-to-all-done.1
  26.0 3.9 all-to-all-start
  31.2 22.5 %all-to-all-done = f32[8,128,256]{2,0,1:T(8,128)S(1)} async-done(((f32[8,128,256]{2,0,1:T(8,128)}), f32[8,128,256]{2,0,1:T(8,128)S(1)}, u32[]{:S(2)}, u32[]{:S(2)}) %all-to-all-start) | async-done | bytes 1048608 | tf_op jit(solution)/shard_map/all_to_all | solution.py:48
  54.5 5.3 fusion.6
  59.8 55.6 %all-gather.9.cloned.1.call-done = f32[128,2048]{1,0:T(8,128)} async-done(((f32[8,2048]{1,0:T(8,128)}), f32[128,2048]{1,0:T(8,128)}) %all-gather.9.cloned.1.call-update) | async-done | bytes 1048592 | tf_op jit(solution)/shard_map/all_gather | solution.py:56
  115.4 1.9 gather_fusion.1
  118.4 17.6 %all-reduce.6.cloned.1.call-done = f32[8,64,256]{2,0,1:T(8,128)} async-done(((f32[8,64,256]{2,0,1:T(8,128)}), f32[8,64,256]{2,0,1:T(8,128)}) %all-reduce.6.cloned.1.call-update) | async-done | bytes 524304 | tf_op jit(solution)/shard_map/psum | solution.py:66
  137.7 42.0 %all-reduce = (f32[8]{0:T(128)S(1)}, f32[8]{0:T(128)S(1)}) all-reduce(f32[8]{0:T(128)S(1)} %get-tuple-element.7, f32[8]{0:T(128)S(1)} %get-tuple-element.6), channel_id=1, replica_groups=mesh['body'=2,'sub'=16] {'sub'}, use_global_device_ids=true, to_apply=%region_1.2 | all-reduce | flops 16 | bytes 128 | tf_op jit(solution)/shard_map/psum | solution.py:14
  181.2 36.9 %psum.87 = f32[8]{0:T(128)S(1)} all-reduce(f32[8]{0:T(128)S(1)} %multiply_reduce_fusion.5), channel_id=1, replica_groups=mesh['body'=2,'sub'=16] {'sub'}, use_global_device_ids=true, to_apply=%region_9.11 | all-reduce | flops 8 | bytes 64 | tf_op jit(solution)/shard_map/psum | solution.py:14
  220.7 19.9 %all_to_all.26 = f32[8,128,256]{2,0,1:T(8,128)S(1)} all-to-all(f32[8,128,256]{2,0,1:T(8,128)S(1)} %bitcast_multiply_fusion.2), channel_id=1, replica_groups=mesh['body'=2,'sub'=16] {'sub'}, dimensions={1} | all-to-all | bytes 2097152 | tf_op jit(solution)/shard_map/all_to_all | solution.py:48
  241.3 5.3 fusion.4
  246.7 53.7 %all-gather.11.cloned.1.call-done = f32[128,2048]{1,0:T(8,128)} async-done(((f32[8,2048]{1,0:T(8,128)}), f32[128,2048]{1,0:T(8,128)}) %all-gather.11.cloned.1.call-update) | async-done | bytes 1048592 | tf_op jit(solution)/shard_map/all_gather | solution.py:56
  300.3 1.9 gather_fusion.2
  303.3 17.6 %all-reduce.8.cloned.1.call-done = f32[8,64,256]{2,0,1:T(8,128)} async-done(((f32[8,64,256]{2,0,1:T(8,128)}), f32[8,64,256]{2,0,1:T(8,128)}) %all-reduce.8.cloned.1.call-update) | async-done | bytes 524304 | tf_op jit(solution)/shard_map/psum | solution.py:66
  322.3 42.0 %psum.89 = f32[8]{0:T(128)S(1)} all-reduce(f32[8]{0:T(128)S(1)} %multiply_reduce_fusion.4), channel_id=1, replica_groups=mesh['body'=2,'sub'=16] {'sub'}, use_global_device_ids=true, to_apply=%region_12.14 | all-reduce | flops 8 | bytes 64 | tf_op jit(solution)/shard_map/psum | solution.py:68
  364.2 1.7 multiply_reduce_fusion.3
  365.9 37.0 %psum.90 = f32[8]{0:T(128)S(1)} all-reduce(f32[8]{0:T(128)S(1)} %get-tuple-element.10), channel_id=1, replica_groups=mesh['body'=2,'sub'=16] {'sub'}, use_global_device_ids=true, to_apply=%region_14.16 | all-reduce | flops 8 | bytes 64 | tf_op jit(solution)/shard_map/psum | solution.py:14
  404.2 19.6 %all_to_all.27 = f32[8,128,256]{2,0,1:T(8,128)S(1)} all-to-all(f32[8,128,256]{2,0,1:T(8,128)S(1)} %bitcast_multiply_fusion.1), channel_id=1, replica_groups=mesh['body'=2,'sub'=16] {'sub'}, dimensions={1} | all-to-all | bytes 2097152 | tf_op jit(solution)/shard_map/all_to_all | solution.py:48
  424.4 5.2 fusion.2
  429.7 53.7 %all-gather.13.cloned.1.call-done = f32[128,2048]{1,0:T(8,128)} async-done(((f32[8,2048]{1,0:T(8,128)}), f32[128,2048]{1,0:T(8,128)}) %all-gather.13.cloned.1.call-update) | async-done | bytes 1048592 | tf_op jit(solution)/shard_map/all_gather | solution.py:56
  483.4 1.9 gather_fusion.3
  486.3 17.6 %all-reduce.10.cloned.1.call-done = f32[8,64,256]{2,0,1:T(8,128)} async-done(((f32[8,64,256]{2,0,1:T(8,128)}), f32[8,64,256]{2,0,1:T(8,128)}) %all-reduce.10.cloned.1.call-update) | async-done | bytes 524304 | tf_op jit(solution)/shard_map/psum | solution.py:66
  505.3 42.0 %psum.92 = f32[8]{0:T(128)S(1)} all-reduce(f32[8]{0:T(128)S(1)} %multiply_reduce_fusion.2), channel_id=1, replica_groups=mesh['body'=2,'sub'=16] {'sub'}, use_global_device_ids=true, to_apply=%region_17.19 | all-reduce | flops 8 | bytes 64 | tf_op jit(solution)/shard_map/psum | solution.py:68
  548.7 36.8 %psum.93 = f32[8]{0:T(128)S(1)} all-reduce(f32[8]{0:T(128)S(1)} %multiply_reduce_fusion.1), channel_id=1, replica_groups=mesh['body'=2,'sub'=16] {'sub'}, use_global_device_ids=true, to_apply=%region_19.21 | all-reduce | flops 8 | bytes 64 | tf_op jit(solution)/shard_map/psum | solution.py:14
  586.7 1.7 gather_fusion.8
  590.0 20.2 %all_to_all.28 = f32[8,128,256]{2,0,1:T(8,128)S(1)} all-to-all(f32[8,128,256]{2,0,1:T(8,128)S(1)} %bitcast_multiply_fusion), channel_id=1, replica_groups=mesh['body'=2,'sub'=16] {'sub'}, dimensions={1} | all-to-all | bytes 2097152 | tf_op jit(solution)/shard_map/all_to_all | solution.py:48
  610.9 5.2 fusion
  616.2 53.7 %all-gather.15.cloned.1.call-done = f32[128,2048]{1,0:T(8,128)} async-done(((f32[8,2048]{1,0:T(8,128)}), f32[128,2048]{1,0:T(8,128)}) %all-gather.15.cloned.1.call-update) | async-done | bytes 1048592 | tf_op jit(solution)/shard_map/all_gather | solution.py:56
  669.9 1.9 gather_fusion.4
  672.8 17.7 %all-reduce.12.cloned.1.call-done = f32[8,64,256]{2,0,1:T(8,128)} async-done(((f32[8,64,256]{2,0,1:T(8,128)}), f32[8,64,256]{2,0,1:T(8,128)}) %all-reduce.12.cloned.1.call-update) | async-done | bytes 524304 | tf_op jit(solution)/shard_map/psum | solution.py:66
  691.8 42.0 %psum.95 = f32[8]{0:T(128)S(1)} all-reduce(f32[8]{0:T(128)S(1)} %multiply_reduce_fusion), channel_id=1, replica_groups=mesh['body'=2,'sub'=16] {'sub'}, use_global_device_ids=true, to_apply=%region_22.24 | all-reduce | flops 8 | bytes 64 | tf_op jit(solution)/shard_map/psum | solution.py:68
  (81 shorter events, 33.1 us)
Async XLA Ops:
  10.5 15.5 %all-to-all-start.1 = ((s32[16,8,1]{1,2,0:T(1,128)}), s32[16,8,1]{1,2,0:T(1,128)S(1)}, u32[]{:S(2)}, u32[]{:S(2)}) async-start(s32[16,8,1]{1,2,0:T(1,128)} %bitcast.5), calls=%async_computation.1 | async-start | bytes 16384 | tf_op jit(solution)/shard_map/all_to_all | solution.py:36
  26.0 27.7 %all-to-all-start = ((f32[8,128,256]{2,0,1:T(8,128)}), f32[8,128,256]{2,0,1:T(8,128)S(1)}, u32[]{:S(2)}, u32[]{:S(2)}) async-start(f32[8,128,256]{2,0,1:T(8,128)} %bitcast_multiply_fusion.3), calls=%async_computation | async-start | bytes 2097152 | tf_op jit(solution)/shard_map/all_to_all | solution.py:48
  29.9 85.6 %all-gather.9.cloned.1.call-start = ((), (), s32[]{:S(2)}) async-start(), calls=%async_computation.9 | async-start | bytes 1114112 | tf_op jit(solution)/shard_map/all_gather | solution.py:56
  54.5 81.5 %copy-start = (f32[8,64,256]{2,1,0:T(8,128)S(1)}, f32[8,64,256]{2,1,0:T(8,128)}, u32[]{:S(2)}) copy-start(f32[8,64,256]{2,1,0:T(8,128)} %param.9) | copy-start | bytes 1572868
  54.5 81.5 %copy-start.2 = (f32[64,256]{1,0:T(8,128)S(1)}, f32[64,256]{1,0:T(8,128)}, u32[]{:S(2)}) copy-start(f32[64,256]{1,0:T(8,128)} %param.10) | copy-start | bytes 196612
  59.8 76.2 %all-reduce.6.cloned.1.call-start = ((), (), s32[]{:S(2)}) async-start(), calls=%async_computation.5 | async-start | bytes 1048576 | tf_op jit(solution)/shard_map/psum | solution.py:66
  118.3 182.0 %all-gather.11.cloned.1.call-start = ((), (), s32[]{:S(2)}) async-start(), calls=%async_computation.10 | async-start | bytes 1114112 | tf_op jit(solution)/shard_map/all_gather | solution.py:56
  241.3 122.9 %copy-start.1 = (f32[8,64,256]{2,0,1:T(8,128)S(1)}, f32[8,64,256]{2,0,1:T(8,128)}, u32[]{:S(2)}) copy-start(f32[8,64,256]{2,0,1:T(8,128)} %all-reduce.6.cloned.1.call-done) | copy-start | bytes 1572868
  246.6 74.3 %all-reduce.8.cloned.1.call-start = ((), (), s32[]{:S(2)}) async-start(), calls=%async_computation.6 | async-start | bytes 1048576 | tf_op jit(solution)/shard_map/psum | solution.py:66
  303.2 180.2 %all-gather.13.cloned.1.call-start = ((), (), s32[]{:S(2)}) async-start(), calls=%async_computation.11 | async-start | bytes 1114112 | tf_op jit(solution)/shard_map/all_gather | solution.py:56
  429.7 74.3 %all-reduce.10.cloned.1.call-start = ((), (), s32[]{:S(2)}) async-start(), calls=%async_computation.7 | async-start | bytes 1048576 | tf_op jit(solution)/shard_map/psum | solution.py:66
  486.3 183.6 %all-gather.15.cloned.1.call-start = ((), (), s32[]{:S(2)}) async-start(), calls=%async_computation.12 | async-start | bytes 1114112 | tf_op jit(solution)/shard_map/all_gather | solution.py:56
  616.2 74.3 %all-reduce.12.cloned.1.call-start = ((), (), s32[]{:S(2)}) async-start(), calls=%async_computation.8 | async-start | bytes 1048576 | tf_op jit(solution)/shard_map/psum | solution.py:66
Sparse Core Ops, SparseCore 0:
  59.9 55.4 all-gather.8
  118.4 17.5 all-reduce.5
  246.7 53.5 all-gather.10
  303.3 17.5 all-reduce.7
  429.8 53.5 all-gather.12
  486.4 17.5 all-reduce.9
  616.3 53.5 all-gather.14
  672.9 17.5 all-reduce.11
where the time goes:
time: 743 us; the launch traced here: 742 us
  blocking collectives  338 us (45%)
  waiting for transfers between devices  313 us (42%)
  other arithmetic  26 us (3%)
  matrix products  23.8 us (3%)
  local copies, waits for them, and re-layouts  14.8 us (2%)
  between operations  13.8 us (2%)
  starting transfers between devices  12.5 us (2%)
    all_gather x4, waiting for transfers between devices, on_device(): plate_piece = lax.all_gather(response[None], 'sub', axis=0, tiled=True)  217 us
    psum x4, blocking collectives, squares(): return lax.psum(products(residual, residual), 'sub')  153 us
    psum x3, blocking collectives, on_device(): alpha = norm_now / lax.psum(products(direction, image), 'sub')  126 us
    psum x4, waiting for transfers between devices, on_device(): total = lax.psum(own_part, 'body')  70.6 us
    all_to_all x3, blocking collectives, on_device(): lax.all_to_all(outgoing, 'sub', split_axis=1, concat_axis=1, tiled=True)  59.7 us
    all_to_all x1, waiting for transfers between devices, on_device(): lax.all_to_all(outgoing, 'sub', split_axis=1, concat_axis=1, tiled=True)  22.5 us
    dot_general x4, matrix products, on_device(): jnp.dot(load_vectors, local_inverse_block, preferred_element_type=jnp.flo...  21 us
  transfers between devices with their start and end apart: 10, of which 10 were waited for; matrix products, arithmetic and copies ran while one was open for 1% of the time, Pallas kernels for 0%

commit v1 on v0

v1 whole, which is shorter than its diff:
```python
import functools

import jax
import jax.numpy as jnp
from jax import lax
from jax.experimental import pallas as pl
from jax.experimental.pallas import tpu as pltpu
from jax.sharding import PartitionSpec as P

ITERS = 4
AXES = ("body", "sub")
VMEM = pl.BlockSpec(memory_space=pltpu.VMEM)
SMEM = pl.BlockSpec(memory_space=pltpu.SMEM)
ANY = pl.BlockSpec(memory_space=pl.ANY)
PARAMS = pltpu.CompilerParams(vmem_limit_bytes=40 * 1024 * 1024)


def f32(*shape):
    return jax.ShapeDtypeStruct(shape, jnp.float32)


def lanes(parts):
    lane = lax.broadcasted_iota(jnp.int32, parts[0].shape, 1)
    tile = jnp.zeros_like(parts[0])
    for i, part in enumerate(parts):
        tile = jnp.where(lane == i, jnp.sum(part, axis=1, keepdims=True), tile)
    return tile


def load_kernel(ndest, per, unroll, place, field, send):
    npatch, ncase, width = field.shape
    send[...] = jnp.zeros_like(send)

    def body(p, carry):
        value = field[p]
        send[place[0, p]] += value
        send[place[1, p]] += value
        return carry

    lax.fori_loop(0, npatch, body, 0, unroll=unroll)


def patch_kernel(
    first, ndest, per, unroll, place, keep, coef, resp, comp, r, d, x, q, r_out, d_out, x_out, q_out, send
):
    npatch, ncase, width = d.shape
    send[...] = jnp.zeros_like(send)
    alpha, beta = coef[0], coef[1]
    zero = jnp.zeros((ncase, width), jnp.float32)

    def body(p, sums):
        rp, dp = r[p], d[p]
        if first:
            x_out[p] = zero
        else:
            x_out[p] = x[p] + alpha * dp
            rp = rp - alpha * q[p]
            dp = rp + beta * dp
        r_out[p] = rp
        d_out[p] = dp
        image = resp[place[2, p]] + resp[place[3, p]] + comp[pl.ds(p, 1), :] * dp
        image = keep[p] * image
        q_out[p] = image
        send[place[0, p]] += image
        send[place[1, p]] += image
        rr, dq, qq, rq = sums
        return rr + rp * rp, dq + dp * image, qq + image * image, rq + rp * image

    sums = lax.fori_loop(0, npatch, body, (zero,) * 4, unroll=unroll)
    tile = lanes(sums)
    for i in range(ndest):
        send[i * per + per - 1] = tile


def last_patch_kernel(unroll, coef, comp, r, d, x, q, d_out, x_out, sums_out):
    npatch, ncase, width = d.shape
    alpha, beta = coef[0], coef[1]
    zero = jnp.zeros((ncase, width), jnp.float32)

    def body(p, sums):
        dp = d[p]
        x_out[p] = x[p] + alpha * dp
        rp = r[p] - alpha * q[p]
        dp = rp + beta * dp
        d_out[p] = dp
        rr, dq = sums
        return rr + rp * rp, dq + comp[pl.ds(p, 1), :] * dp * dp

    sums_out[...] = lanes(lax.fori_loop(0, npatch, body, (zero,) * 2, unroll=unroll))


def owner_kernel(first, last, nsub, nbody, recv, load_r, load_d, block, *refs):
    if last:
        sums_out, held, sems = refs
    else:
        resp, r_out, d_out, coef, held, sems = refs
    if last:
        r_out, d_out, coef = None, None, refs[0]
    per, ncase, width = recv.shape[1:]
    nslot = per - 1
    gap = nbody * width
    copies = []
    for j in range(nslot):
        rows = pl.ds(j * gap, gap)
        copies.append(pltpu.make_async_copy(block.at[rows], held.at[rows], sems.at[j]))
        copies[-1].start()
    if not first:
        dots = recv[0, nslot]
        for i in range(1, nbody * nsub):
            dots = dots + recv[i, nslot]
        rr, dq, qq, rq = (dots[:, i : i + 1] for i in range(4))
        alpha = rr / dq
        beta = (rr - 2.0 * alpha * rq + alpha * alpha * qq) / rr
    total = jnp.zeros((ncase, nslot * gap), jnp.float32)
    loads = []
    for j in range(nslot):
        pieces = []
        for h in range(nbody):
            piece = recv[h * nsub, j]
            for i in range(1, nsub):
                piece = piece + recv[h * nsub + i, j]
            columns = slice(j * gap + h * width, j * gap + (h + 1) * width)
            if not first:
                residual = load_r[:, columns] - alpha * piece
                direction = residual + beta * load_d[:, columns]
            else:
                residual = direction = piece
            if not last:
                r_out[:, columns] = residual
                d_out[:, columns] = direction
            pieces.append(direction)
        load = jnp.concatenate(pieces, axis=1)
        loads.append(load)
        copies[j].wait()
        total = total + jnp.dot(
            load.astype(jnp.bfloat16),
            held[j * gap : (j + 1) * gap, :],
            preferred_element_type=jnp.float32,
        )
    if last:
        product = jnp.concatenate(loads, axis=1) * total
        sums = product[:, :width]
        for i in range(1, nslot * nbody):
            sums = sums + product[:, i * width : (i + 1) * width]
        lane = lax.broadcasted_iota(jnp.int32, sums.shape, 1)
        sums_out[0] = jnp.where(lane == 1, jnp.sum(sums, axis=1, keepdims=True), 0.0)
        sums_out[1] = jnp.broadcast_to(alpha, sums.shape)
        sums_out[2] = jnp.broadcast_to(beta, sums.shape)
        return
    if first:
        coef[...] = jnp.zeros_like(coef)
    else:
        coef[0] = jnp.broadcast_to(alpha, coef.shape[1:])
        coef[1] = jnp.broadcast_to(beta, coef.shape[1:])
    for j in range(nslot):
        for h in range(nbody):
            tile = total[:, j * gap + h * width : j * gap + (h + 1) * width]
            for i in range(nsub):
                resp[h * nsub + i, j] = tile


def exchange(messages):
    return lax.all_to_all(messages, AXES, split_axis=0, concat_axis=0, tiled=True)


def on_device(rhs, compliance, plate_owner, found_owner, slot_pairs, active, inverse):
    nsub = lax.axis_size("sub")
    nbody = lax.axis_size("body")
    side = lax.axis_index("body")
    ncase, npatch, gap = rhs.shape
    block = inverse[0, 0]
    iface = block.shape[0]
    nslot = iface // gap
    width = gap // nbody
    ndest = nbody * nsub
    per = nslot + 1
    unroll = 4

    keep = active.astype(jnp.float32)
    owners = jnp.stack([plate_owner[:, 0], found_owner[:, 0] + nsub])
    slots = slot_pairs.T
    place = jnp.concatenate([owners * per + slots, owners * nslot + slots]).astype(jnp.int32)
    comp = lax.dynamic_slice_in_dim(compliance, side * width, width, axis=1)
    part = lax.dynamic_slice_in_dim(rhs, side * width, width, axis=2)
    start = jnp.transpose(keep[None, :, None] * part, (1, 0, 2))

    field = f32(npatch, ncase, width)
    message = f32(ndest * per, ncase, width)
    coefs = f32(2, ncase, width)
    loads = f32(ncase, iface)
    scratch = [pltpu.VMEM((iface, iface), jnp.bfloat16), pltpu.SemaphoreType.DMA((nslot,))]

    send = pl.pallas_call(
        functools.partial(load_kernel, ndest, per, unroll),
        out_shape=message,
        in_specs=[SMEM, VMEM],
        out_specs=VMEM,
        compiler_params=PARAMS,
    )(place, start)
    r = d = x = q = start
    load_r = load_d = jnp.zeros((ncase, iface), jnp.float32)
    for step in range(ITERS):
        first, last = step == 0, step == ITERS - 1
        recv = exchange(send.reshape(ndest, per, ncase, width))
        owner_call = functools.partial(
            pl.pallas_call,
            functools.partial(owner_kernel, first, last, nsub, nbody),
            in_specs=[VMEM, VMEM, VMEM, ANY],
            scratch_shapes=scratch,
            compiler_params=PARAMS,
        )
        if last:
            ends = owner_call(out_shape=f32(3, ncase, width), out_specs=VMEM)(recv, load_r, load_d, block)
            break
        resp, load_r, load_d, coef = owner_call(
            out_shape=(f32(ndest, nslot, ncase, width), loads, loads, coefs), out_specs=(VMEM,) * 4
        )(recv, load_r, load_d, block)
        resp = exchange(resp).reshape(ndest * nslot, ncase, width)
        r, d, x, q, send = pl.pallas_call(
            functools.partial(patch_kernel, first, ndest, per, unroll),
            out_shape=(field,) * 4 + (message,),
            in_specs=[SMEM, SMEM] + [VMEM] * 7,
            out_specs=(VMEM,) * 5,
            compiler_params=PARAMS,
        )(place, keep, coef, resp, comp, r, d, x, q)
    d, x, sums = pl.pallas_call(
        functools.partial(last_patch_kernel, unroll),
        out_shape=(field, field, f32(ncase, width)),
        in_specs=[VMEM] * 6,
        out_specs=(VMEM,) * 3,
        compiler_params=PARAMS,
    )(ends[1:], comp, r, d, x, q)
    swap = [(i, nbody - 1 - i) for i in range(nbody)]
    other_d, other_x = lax.ppermute(d, "body", swap), lax.ppermute(x, "body", swap)
    sums = exchange(jnp.broadcast_to((sums + ends[0])[None], (ndest, ncase, width)))
    sums = jnp.sum(sums, axis=0)
    alpha = sums[:, 0:1] / sums[:, 1:2]
    mine, other = x + alpha[None] * d, other_x + alpha[None] * other_d
    both = jnp.stack([jnp.where(side == 0, mine, other), jnp.where(side == 0, other, mine)])
    return jnp.transpose(both, (2, 1, 0, 3)).reshape(ncase, npatch, gap)


def solution(mesh):
    in_specs = (
        P(None, "sub", None),
        P("sub", None),
        P("sub", None),
        P("sub", None),
        P("sub", None),
        P("sub"),
        P("body", "sub", None, None),
    )
    out_specs = P(None, "sub", None)
    return jax.shard_map(
        on_device, mesh=mesh, in_specs=in_specs, out_specs=out_specs, check_vma=False
    )
```

time: 743 us -> 264 us (0.36)
  waiting for transfers between devices: 313 us -> 35.4 us
  blocking collectives: 338 us -> 195 us
  matrix products: 23.8 us -> 0 us
  other arithmetic: 26 us -> 2.65 us
  Pallas kernels: 0 us -> 15.1 us
  between operations: 13.8 us -> 0.17 us
    psum x7 -> x0, blocking collectives: 279 us -> none  [the longest x4 153 us: squares(): return lax.psum(products(residual, residual), 'sub')]
    all_gather x4 -> x0, waiting for transfers between devices: 217 us -> none  [on_device(): plate_piece = lax.all_gather(response[None], 'sub', axis=0, tiled=True)]
    all_to_all x3 -> x6, blocking collectives: 59.7 us -> 195 us  [exchange(): lax.all_to_all(messages, AXES, split_axis=0, concat_axis=0, tiled=True)]
    psum x4 -> x0, waiting for transfers between devices: 70.6 us -> none  [on_device(): total = lax.psum(own_part, 'body')]
    dot_general x8 -> x0, matrix products: 23.8 us -> none  [the longest x4 21 us: on_device(): jnp.dot(load_vectors, local_inverse_block, preferred_element_type=jnp.flo...]
    pallas_call x0 -> x9, Pallas kernels: none -> 15.1 us  [the longest x3 7.3 us: on_device(): owner_call(out_shape=(f32(ndest, nslot, ncase, width), loads, loads, coef...]
    gather x10 -> x0, local copies, waits for them, and re-layouts: 13 us -> none  [the longest x4 7.67 us: on_device(): chosen = block_list[local, :, slot, :]]
    reduce_sum x9 -> x1, other arithmetic: 10.6 us -> 0.04 us  [on_device(): sums = jnp.sum(sums, axis=0)]
  transfers between devices with their start and end apart: 10 -> 4, of which waited for: 10 -> 2; matrix products, arithmetic and copies ran while one was open for 1% -> 0% of each run, Pallas kernels for 0% -> 0%
where the time goes in v1:
time: 264 us
  blocking collectives  195 us (74%)
  waiting for transfers between devices  35.4 us (13%)
  Pallas kernels  15.1 us (6%)
  local copies, waits for them, and re-layouts  9.11 us (3%)
  starting transfers between devices  5.94 us (2%)
  other arithmetic  2.65 us (1%)
    all_to_all x6, blocking collectives, exchange(): lax.all_to_all(messages, AXES, split_axis=0, concat_axis=0, tiled=True)  195 us
    all_to_all x2, waiting for transfers between devices, exchange(): lax.all_to_all(messages, AXES, split_axis=0, concat_axis=0, tiled=True)  35.4 us
    pallas_call x3, Pallas kernels, on_device(): owner_call(out_shape=(f32(ndest, nslot, ncase, width), loads, loads, coef...  7.3 us
    unnamed x10, local copies, waits for them, and re-layouts  6.77 us
    all_to_all x2, starting transfers between devices, exchange(): lax.all_to_all(messages, AXES, split_axis=0, concat_axis=0, tiled=True)  5.37 us
  transfers between devices with their start and end apart: 4, of which 2 were waited for; matrix products, arithmetic and copies ran while one was open for 0% of the time, Pallas kernels for 0%

profile of v1, /device:TPU:0, one launch (start us, length us, event | category | flops | bytes accessed | tf_op | source)
XLA Modules:
  0.0 263.9 jit_solution(9623219137432631171)
XLA Ops:
  0.0 0.7 convert_element_type.3.keep
  0.7 0.7 add_bitcast_fusion
  1.4 0.7 bitcast_add_fusion.1
  2.1 0.2 fusion.field.r.d.x.q
  2.3 1.1 shard_map.73
  3.4 38.0 %all_to_all.40.recv = f32[32,9,8,128]{3,2,1,0:T(8,128)S(1)} all-to-all(f32[32,9,8,128]{3,2,1,0:T(8,128)S(1)} %bitcast.30), channel_id=1, replica_groups=mesh['body'=2,'sub'=16] {'body','sub'}, dimensions={0} | all-to-all | bytes 2359296 | tf_op jit(solution)/shard_map/all_to_all | solution.py:163
  41.4 3.4 %copy-done.1 = bf16[1,1,2048,2048]{3,2,1,0:T(8,128)(2,1)S(1)} copy-done((bf16[1,1,2048,2048]{3,2,1,0:T(8,128)(2,1)S(1)}, bf16[1,1,2048,2048]{3,2,1,0:T(8,128)(2,1)}, u32[]{:S(2)}) %copy-start.1) | copy-done | bytes 8388632
  44.8 3.0 %shard_map.74 = (f32[32,8,8,128]{3,2,1,0:T(8,128)}, f32[8,2048]{1,0:T(8,128)S(1)}, f32[8,2048]{1,0:T(8,128)S(1)}, f32[2,8,128]{2,1,0:T(8,128)S(1)}) custom-call(f32[32,9,8,128]{3,2,1,0:T(8,128)S(1)} %all_to_all.40.recv, f32[8,2048]{1,0:T(8,128)S(1)} %broadcast_in_dim.4.load_r.load_d, f32[8,2048]{1,0:T(8,128)S(1)} %broadcast_in_dim.4.load_r.load_d, ...), custom_call_target="tpu_custom_call" | custom-call | tf_op jit(solution)/shard_map/pallas_call | solution.py:215
  47.8 2.8 %all-to-all-start.1 = ((f32[32,8,8,128]{3,2,1,0:T(8,128)}), f32[32,8,8,128]{3,2,1,0:T(8,128)S(1)}, u32[]{:S(2)}, u32[]{:S(2)}) async-start(f32[32,8,8,128]{3,2,1,0:T(8,128)} %get-tuple-element.36), calls=%async_computation.1 | async-start | bytes 2097152 | tf_op jit(solution)/shard_map/all_to_all | solution.py:163
  50.6 28.0 %all-to-all-done.1 = f32[32,8,8,128]{3,2,1,0:T(8,128)S(1)} async-done(((f32[32,8,8,128]{3,2,1,0:T(8,128)}), f32[32,8,8,128]{3,2,1,0:T(8,128)S(1)}, u32[]{:S(2)}, u32[]{:S(2)}) %all-to-all-start.1) | async-done | bytes 1048608 | tf_op jit(solution)/shard_map/all_to_all | solution.py:163
  78.7 1.4 shard_map.75
  80.0 32.6 %all_to_all.41.recv = f32[32,9,8,128]{3,2,1,0:T(8,128)S(1)} all-to-all(f32[32,9,8,128]{3,2,1,0:T(8,128)S(1)} %bitcast.36), channel_id=1, replica_groups=mesh['body'=2,'sub'=16] {'body','sub'}, dimensions={0} | all-to-all | bytes 2359296 | tf_op jit(solution)/shard_map/all_to_all | solution.py:163
  112.6 3.4 %copy-done.2 = bf16[1,1,2048,2048]{3,2,1,0:T(8,128)(2,1)S(1)} copy-done((bf16[1,1,2048,2048]{3,2,1,0:T(8,128)(2,1)S(1)}, bf16[1,1,2048,2048]{3,2,1,0:T(8,128)(2,1)}, u32[]{:S(2)}) %copy-start.2) | copy-done | bytes 8388632
  116.0 2.2 shard_map.76
  118.2 29.9 %all_to_all.42 = f32[32,8,8,128]{3,2,1,0:T(8,128)S(1)} all-to-all(f32[32,8,8,128]{3,2,1,0:T(8,128)S(1)} %get-tuple-element.41), channel_id=1, replica_groups=mesh['body'=2,'sub'=16] {'body','sub'}, dimensions={0} | all-to-all | bytes 2097152 | tf_op jit(solution)/shard_map/all_to_all | solution.py:163
  148.1 1.4 shard_map.77
  149.5 32.6 %all_to_all.43.recv = f32[32,9,8,128]{3,2,1,0:T(8,128)S(1)} all-to-all(f32[32,9,8,128]{3,2,1,0:T(8,128)S(1)} %bitcast.35), channel_id=1, replica_groups=mesh['body'=2,'sub'=16] {'body','sub'}, dimensions={0} | all-to-all | bytes 2359296 | tf_op jit(solution)/shard_map/all_to_all | solution.py:163
  182.1 2.2 shard_map.78
  184.3 29.8 %all_to_all.44 = f32[32,8,8,128]{3,2,1,0:T(8,128)S(1)} all-to-all(f32[32,8,8,128]{3,2,1,0:T(8,128)S(1)} %get-tuple-element.50), channel_id=1, replica_groups=mesh['body'=2,'sub'=16] {'body','sub'}, dimensions={0} | all-to-all | bytes 2097152 | tf_op jit(solution)/shard_map/all_to_all | solution.py:163
  214.1 1.4 shard_map.79
  215.5 32.6 %all_to_all.45.recv = f32[32,9,8,128]{3,2,1,0:T(8,128)S(1)} all-to-all(f32[32,9,8,128]{3,2,1,0:T(8,128)S(1)} %bitcast.34), channel_id=1, replica_groups=mesh['body'=2,'sub'=16] {'body','sub'}, dimensions={0} | all-to-all | bytes 2359296 | tf_op jit(solution)/shard_map/all_to_all | solution.py:163
  248.1 2.2 shard_map.80
  250.3 0.3 shard_map.81
  250.6 0.7 broadcast_in_dim.5
  251.3 2.6 all-to-all-start.7
  253.9 0.2 collective-permute-start
  254.1 0.4 collective-permute-start.1
  254.5 7.3 %all-to-all-done.7 = f32[32,8,128]{2,1,0:T(8,128)S(1)} async-done(((f32[32,8,128]{2,1,0:T(8,128)}), f32[32,8,128]{2,1,0:T(8,128)S(1)}, u32[]{:S(2)}, u32[]{:S(2)}) %all-to-all-start.7) | async-done | bytes 131104 | tf_op jit(solution)/shard_map/all_to_all | solution.py:163
  261.8 0.2 divide_reduce_fusion
  262.0 0.1 select_bitcast_fusion.1
  262.2 0.4 copy.14
  262.6 1.2 reshape.46
  (18 shorter events, 0.2 us)
Async XLA Ops:
  0.0 2.1 copy-start
  41.4 3.4 %copy-start.1 = (bf16[1,1,2048,2048]{3,2,1,0:T(8,128)(2,1)S(1)}, bf16[1,1,2048,2048]{3,2,1,0:T(8,128)(2,1)}, u32[]{:S(2)}) copy-start(bf16[1,1,2048,2048]{3,2,1,0:T(8,128)(2,1)} %param.13) | copy-start | bytes 25165828
  47.8 2.8 %copy-start.4 = (f32[64,256]{1,0:T(8,128)S(1)}, f32[64,256]{1,0:T(8,128)}, u32[]{:S(2)}) copy-start(f32[64,256]{1,0:T(8,128)} %param.8) | copy-start | bytes 196612
  47.8 30.9 %all-to-all-start.1 = ((f32[32,8,8,128]{3,2,1,0:T(8,128)}), f32[32,8,8,128]{3,2,1,0:T(8,128)S(1)}, u32[]{:S(2)}, u32[]{:S(2)}) async-start(f32[32,8,8,128]{3,2,1,0:T(8,128)} %get-tuple-element.36), calls=%async_computation.1 | async-start | bytes 2097152 | tf_op jit(solution)/shard_map/all_to_all | solution.py:163
  112.6 3.4 %copy-start.2 = (bf16[1,1,2048,2048]{3,2,1,0:T(8,128)(2,1)S(1)}, bf16[1,1,2048,2048]{3,2,1,0:T(8,128)(2,1)}, u32[]{:S(2)}) copy-start(bf16[1,1,2048,2048]{3,2,1,0:T(8,128)(2,1)} %param.13) | copy-start | bytes 25165828
  116.0 66.1 %copy-start.3 = (bf16[1,1,2048,2048]{3,2,1,0:T(8,128)(2,1)S(1)}, bf16[1,1,2048,2048]{3,2,1,0:T(8,128)(2,1)}, u32[]{:S(2)}) copy-start(bf16[1,1,2048,2048]{3,2,1,0:T(8,128)(2,1)} %param.13) | copy-start | bytes 25165828
  251.3 10.5 %all-to-all-start.7 = ((f32[32,8,128]{2,1,0:T(8,128)}), f32[32,8,128]{2,1,0:T(8,128)S(1)}, u32[]{:S(2)}, u32[]{:S(2)}) async-start(f32[32,8,128]{2,1,0:T(8,128)} %broadcast_in_dim.5), calls=%async_computation.7 | async-start | bytes 262144 | tf_op jit(solution)/shard_map/all_to_all | solution.py:163
  253.9 8.1 %collective-permute-start = (f32[64,8,128]{2,1,0:T(8,128)S(1)}, f32[64,8,128]{2,1,0:T(8,128)S(1)}, u32[]{:S(2)}, u32[]{:S(2)}) collective-permute-start(f32[64,8,128]{2,1,0:T(8,128)S(1)} %get-tuple-element.62), channel_id=1, source_target_pairs={{0,16},{16,0},{1,17},{17,1},{2,18},{18,2},{3,19},{19,3},{4,20},{20... | collective-permute-start | bytes 786440 | tf_op jit(solution)/shard_map/ppermute | solution.py:234
  254.1 8.0 %collective-permute-start.1 = (f32[64,8,128]{2,1,0:T(8,128)S(1)}, f32[64,8,128]{2,1,0:T(8,128)S(1)}, u32[]{:S(2)}, u32[]{:S(2)}) collective-permute-start(f32[64,8,128]{2,1,0:T(8,128)S(1)} %get-tuple-element.64), channel_id=1, source_target_pairs={{0,16},{16,0},{1,17},{17,1},{2,18},{18,2},{3,19},{19,3},{4,20},{20... | collective-permute-start | bytes 786440 | tf_op jit(solution)/shard_map/ppermute | solution.py:234

commit v2 on v1

v2 whole, which is shorter than its diff:
```python
import functools

import jax
import jax.numpy as jnp
from jax import lax
from jax.experimental import pallas as pl
from jax.experimental.pallas import tpu as pltpu
from jax.sharding import PartitionSpec as P

ITERS = 4
AXES = ("body", "sub")
VMEM = pl.BlockSpec(memory_space=pltpu.VMEM)
SMEM = pl.BlockSpec(memory_space=pltpu.SMEM)
ANY = pl.BlockSpec(memory_space=pl.ANY)
PARAMS = pltpu.CompilerParams(vmem_limit_bytes=40 * 1024 * 1024)


def f32(*shape):
    return jax.ShapeDtypeStruct(shape, jnp.float32)


def lanes(parts):
    lane = lax.broadcasted_iota(jnp.int32, parts[0].shape, 1)
    tile = jnp.zeros_like(parts[0])
    for i, part in enumerate(parts):
        tile = jnp.where(lane == i, jnp.sum(part, axis=1, keepdims=True), tile)
    return tile


def split_message(total, keep_a, send_a, keep_b, send_b):
    rows = keep_a.shape[0]
    for i, out in enumerate((keep_a, send_a, keep_b, send_b)):
        out[...] = total[i * rows : (i + 1) * rows]


def load_kernel(unroll, place, field, keep_a, send_a, keep_b, send_b, total):
    total[...] = jnp.zeros_like(total)

    def body(p, carry):
        value = field[p]
        total[place[0, p]] += value
        total[place[1, p]] += value
        return carry

    lax.fori_loop(0, field.shape[0], body, 0, unroll=unroll)
    split_message(total, keep_a, send_a, keep_b, send_b)


def patch_kernel(first, per, nparts, unroll, place, keep, coef, comp, r, d, x, q, *refs):
    parts, refs = refs[:nparts], refs[nparts:]
    r_out, d_out, x_out, q_out, keep_a, send_a, keep_b, send_b, total, resp = refs
    npatch, ncase, width = d.shape
    at = 0
    for part in parts:
        resp[at : at + part.shape[0]] = part[...]
        at += part.shape[0]
    total[...] = jnp.zeros_like(total)
    alpha, beta = coef[0], coef[1]
    zero = jnp.zeros((ncase, width), jnp.float32)

    def body(p, sums):
        rp, dp = r[p], d[p]
        if first:
            x_out[p] = zero
        else:
            x_out[p] = x[p] + alpha * dp
            rp = rp - alpha * q[p]
            dp = rp + beta * dp
        r_out[p] = rp
        d_out[p] = dp
        image = resp[place[2, p]] + resp[place[3, p]] + comp[pl.ds(p, 1), :] * dp
        image = keep[p] * image
        q_out[p] = image
        total[place[0, p]] += image
        total[place[1, p]] += image
        rr, dq, qq, rq = sums
        return rr + rp * rp, dq + dp * image, qq + image * image, rq + rp * image

    sums = lax.fori_loop(0, npatch, body, (zero,) * 4, unroll=unroll)
    tile = lanes(sums)
    for i in range(total.shape[0] // per):
        total[i * per + per - 1] = tile
    split_message(total, keep_a, send_a, keep_b, send_b)


def last_patch_kernel(unroll, coef, comp, r, d, x, q, d_out, x_out, sums_out):
    npatch, ncase, width = d.shape
    alpha, beta = coef[0], coef[1]
    zero = jnp.zeros((ncase, width), jnp.float32)

    def body(p, sums):
        dp = d[p]
        x_out[p] = x[p] + alpha * dp
        rp = r[p] - alpha * q[p]
        dp = rp + beta * dp
        d_out[p] = dp
        rr, dq = sums
        return rr + rp * rp, dq + comp[pl.ds(p, 1), :] * dp * dp

    sums_out[...] = lanes(lax.fori_loop(0, npatch, body, (zero,) * 2, unroll=unroll))


def second_kernel(keep_a, recv_a, keep_b, recv_b, send_a, send_b):
    rows = send_a.shape[0]
    send_a[...] = keep_a[rows:] + recv_a[rows:]
    send_b[...] = keep_b[rows:] + recv_b[rows:]


def third_kernel(per, keep_a, one_a, two_a, keep_b, one_b, two_b, *outs):
    nz = len(outs) // 2
    for side, (keep, one, two) in enumerate(((keep_a, one_a, two_a), (keep_b, one_b, two_b))):
        for z in range(nz):
            rows = slice(z * per, (z + 1) * per)
            outs[side * nz + z][...] = keep[rows] + one[rows] + two[rows]


def owner_kernel(first, last, nbody, nz, side, load_r, load_d, block, *refs):
    recv, refs = refs[: nbody * nz], refs[nbody * nz :]
    if last:
        sums_out, held, sems = refs
    else:
        own, other, r_out, d_out, coef, held, sems = refs
    per, ncase, width = recv[0].shape
    nslot = per - 1
    gap = nbody * width
    copies = []
    for j in range(nslot):
        rows = pl.ds(j * gap, gap)
        copies.append(pltpu.make_async_copy(block.at[rows], held.at[rows], sems.at[j]))
        copies[-1].start()
    is_first_half = jnp.full((ncase, width), side[0], jnp.int32) == 0
    if not first:
        dots = recv[0][nslot]
        for part in recv[1:]:
            dots = dots + part[nslot]
        rr, dq, qq, rq = (dots[:, i : i + 1] for i in range(4))
        alpha = rr / dq
        beta = (rr - 2.0 * alpha * rq + alpha * alpha * qq) / rr
    total = jnp.zeros((ncase, nslot * gap), jnp.float32)
    loads = []
    for j in range(nslot):
        mine, far = recv[0][j], recv[nz][j]
        for z in range(1, nz):
            mine, far = mine + recv[z][j], far + recv[nz + z][j]
        piece = jnp.concatenate(
            [jnp.where(is_first_half, mine, far), jnp.where(is_first_half, far, mine)], axis=1
        )
        columns = slice(j * gap, (j + 1) * gap)
        if first:
            residual = direction = piece
        else:
            residual = load_r[:, columns] - alpha * piece
            direction = residual + beta * load_d[:, columns]
        if not last:
            r_out[:, columns] = residual
            d_out[:, columns] = direction
        loads.append(direction)
        copies[j].wait()
        total = total + jnp.dot(
            direction.astype(jnp.bfloat16), held[columns, :], preferred_element_type=jnp.float32
        )
    if last:
        product = jnp.concatenate(loads, axis=1) * total
        sums = product[:, :width]
        for i in range(1, nslot * nbody):
            sums = sums + product[:, i * width : (i + 1) * width]
        lane = lax.broadcasted_iota(jnp.int32, sums.shape, 1)
        sums_out[0] = jnp.where(lane == 1, jnp.sum(sums, axis=1, keepdims=True), 0.0)
        sums_out[1] = jnp.broadcast_to(alpha, sums.shape)
        sums_out[2] = jnp.broadcast_to(beta, sums.shape)
        return
    if first:
        coef[...] = jnp.zeros_like(coef)
    else:
        coef[0] = jnp.broadcast_to(alpha, coef.shape[1:])
        coef[1] = jnp.broadcast_to(beta, coef.shape[1:])
    for j in range(nslot):
        one = total[:, j * gap : j * gap + width]
        two = total[:, j * gap + width : (j + 1) * gap]
        own[j] = jnp.where(is_first_half, one, two)
        other[j] = jnp.where(is_first_half, two, one)


def tree(values):
    while len(values) > 1:
        values = [a + b for a, b in zip(values[::2], values[1::2])]
    return values[0]


def call(kernel, out_shape, specs, *operands, scratch=()):
    several = isinstance(out_shape, (tuple, list))
    return pl.pallas_call(
        kernel,
        out_shape=tuple(out_shape) if several else out_shape,
        in_specs=specs,
        out_specs=(VMEM,) * len(out_shape) if several else VMEM,
        scratch_shapes=list(scratch),
        compiler_params=PARAMS,
    )(*operands)


def on_device(rhs, compliance, plate_owner, found_owner, slot_pairs, active, inverse):
    nsub = lax.axis_size("sub")
    nbody = lax.axis_size("body")
    side = lax.axis_index("body")
    me = lax.axis_index("sub")
    ncase, npatch, gap = rhs.shape
    block = inverse[0, 0]
    iface = block.shape[0]
    nslot = iface // gap
    width = gap // nbody
    per = nslot + 1
    nz = nsub // 4
    unroll = 4

    def swap(value, far_body, far_sub):
        pairs = [
            (b * nsub + s, (b ^ far_body) * nsub + (s ^ far_sub)) for b in range(nbody) for s in range(nsub)
        ]
        return lax.ppermute(value, AXES, pairs)

    keep = active.astype(jnp.float32)
    owners = jnp.stack([plate_owner[:, 0], found_owner[:, 0]])
    slots = slot_pairs.T
    owners = jnp.where(side == 0, owners, owners[::-1])
    slots = jnp.where(side == 0, slots, slots[::-1])
    away = owners ^ me
    x_bit, y_bit, z_part = away & 1, (away >> 1) & 1, away >> 2
    order = jnp.stack([x_bit[0] * 2 + y_bit[0], nbody * 2 + y_bit[1] * 2 + x_bit[1]]) * nz + z_part
    place = jnp.concatenate([order * per + slots, order * nslot + slots]).astype(jnp.int32)
    comp = lax.dynamic_slice_in_dim(compliance, side * width, width, axis=1)
    part = lax.dynamic_slice_in_dim(rhs, side * width, width, axis=2)
    start = jnp.transpose(keep[None, :, None] * part, (1, 0, 2))
    which = side.astype(jnp.int32).reshape(1)

    field = f32(npatch, ncase, width)
    half = f32(2 * nz * per, ncase, width)
    quarter = f32(nz * per, ncase, width)
    one = f32(per, ncase, width)
    answer = f32(nslot, ncase, width)
    coefs = f32(2, ncase, width)
    loads = f32(ncase, iface)
    whole = pltpu.VMEM((nbody * nsub * per, ncase, width), jnp.float32)
    whole_resp = pltpu.VMEM((nbody * nsub * nslot, ncase, width), jnp.float32)

    def gather_loads(parts):
        keep_a, send_a, keep_b, send_b = parts
        one_a, one_b = swap(send_a, 0, 1), swap(send_b, 0, 2)
        send_a, send_b = call(second_kernel, (quarter,) * 2, [VMEM] * 4, keep_a, one_a, keep_b, one_b)
        two_a, two_b = swap(send_a, 0, 2), swap(send_b, 0, 1)
        blocks = call(
            functools.partial(third_kernel, per),
            (one,) * (2 * nz),
            [VMEM] * 6,
            keep_a,
            one_a,
            two_a,
            keep_b,
            one_b,
            two_b,
        )
        mine = [blocks[0]] + [swap(blocks[z], 0, 4 * z) for z in range(1, nz)]
        return mine + [swap(blocks[nz + z], 1, 4 * z) for z in range(nz)]

    def spread(own, other):
        a = jnp.concatenate([own] + [swap(own, 0, 4 * z) for z in range(1, nz)])
        b = jnp.concatenate([swap(other, 1, 4 * z) for z in range(nz)])
        a = jnp.concatenate([a, swap(a, 0, 2)])
        b = jnp.concatenate([b, swap(b, 0, 1)])
        return [a, swap(a, 0, 1), b, swap(b, 0, 2)]

    parts = call(
        functools.partial(load_kernel, unroll), (half,) * 4, [SMEM, VMEM], place, start, scratch=[whole]
    )
    r = d = x = q = start
    load_r = load_d = jnp.zeros((ncase, iface), jnp.float32)
    for step in range(ITERS):
        first, last = step == 0, step == ITERS - 1
        recv = gather_loads(parts)
        owned = call(
            functools.partial(owner_kernel, first, last, nbody, nz),
            f32(3, ncase, width) if last else (answer, answer, loads, loads, coefs),
            [SMEM, VMEM, VMEM, ANY] + [VMEM] * len(recv),
            which,
            load_r,
            load_d,
            block,
            *recv,
            scratch=[pltpu.VMEM((iface, iface), jnp.bfloat16), pltpu.SemaphoreType.DMA((nslot,))],
        )
        if last:
            break
        own, other, load_r, load_d, coef = owned
        resp = spread(own, other)
        r, d, x, q, *parts = call(
            functools.partial(patch_kernel, first, per, len(resp), unroll),
            (field,) * 4 + (half,) * 4,
            [SMEM, SMEM] + [VMEM] * (6 + len(resp)),
            place,
            keep,
            coef,
            comp,
            r,
            d,
            x,
            q,
            *resp,
            scratch=[whole, whole_resp],
        )
    d, x, sums = call(
        functools.partial(last_patch_kernel, unroll),
        (field, field, f32(ncase, width)),
        [VMEM] * 6,
        owned[1:],
        comp,
        r,
        d,
        x,
        q,
    )
    other_d, other_x = swap(d, 1, 0), swap(x, 1, 0)
    sums = sums + owned[0]
    sums = tree([sums] + [swap(sums, b, s) for b in range(nbody) for s in range(4) if b + s > 0])
    sums = tree([sums] + [swap(sums, 0, 4 * z) for z in range(1, nz)])
    alpha = sums[:, 0:1] / sums[:, 1:2]
    mine, theirs = x + alpha[None] * d, other_x + alpha[None] * other_d
    both = jnp.stack([jnp.where(side == 0, mine, theirs), jnp.where(side == 0, theirs, mine)])
    return jnp.transpose(both, (2, 1, 0, 3)).reshape(ncase, npatch, gap)


def solution(mesh):
    in_specs = (
        P(None, "sub", None),
        P("sub", None),
        P("sub", None),
        P("sub", None),
        P("sub", None),
        P("sub"),
        P("body", "sub", None, None),
    )
    out_specs = P(None, "sub", None)
    return jax.shard_map(
        on_device, mesh=mesh, in_specs=in_specs, out_specs=out_specs, check_vma=False
    )
```

time: 264 us -> 225 us (0.85)
  blocking collectives: 195 us -> 0 us
  starting transfers between devices: 5.94 us -> 97.1 us
  waiting for transfers between devices: 35.4 us -> 103 us
  local copies, waits for them, and re-layouts: 9.11 us -> 5.94 us
    all_to_all x6 -> x0, blocking collectives: 195 us -> none  [exchange(): lax.all_to_all(messages, AXES, split_axis=0, concat_axis=0, tiled=True)]
    ppermute x2 -> x89, waiting for transfers between devices: 0.01 us -> 103 us  [swap(): return lax.ppermute(value, AXES, pairs)]
    ppermute x2 -> x89, starting transfers between devices: 0.58 us -> 97.1 us  [swap(): return lax.ppermute(value, AXES, pairs)]
    all_to_all x2 -> x0, waiting for transfers between devices: 35.4 us -> none  [exchange(): lax.all_to_all(messages, AXES, split_axis=0, concat_axis=0, tiled=True)]
    all_to_all x2 -> x0, starting transfers between devices: 5.37 us -> none  [exchange(): lax.all_to_all(messages, AXES, split_axis=0, concat_axis=0, tiled=True)]
    unnamed x10 -> x32, local copies, waits for them, and re-layouts: 6.77 us -> 3.49 us
    pallas_call x9 -> x17, Pallas kernels: 15.1 us -> 14.8 us  [call(): pl.pallas_call(kernel, out_shape=tuple(out_shape) if several else out_sha...]
  transfers between devices with their start and end apart: 4 -> 89, of which waited for: 2 -> 52; matrix products, arithmetic and copies ran while one was open for 0% -> 0% of each run, Pallas kernels for 0% -> 0%
where the time goes in v2:
time: 225 us
  waiting for transfers between devices  103 us (46%)
  starting transfers between devices  97.1 us (43%)
  Pallas kernels  14.8 us (7%)
  local copies, waits for them, and re-layouts  5.94 us (3%)
  other arithmetic  3.41 us (2%)
    ppermute x89, waiting for transfers between devices, swap(): return lax.ppermute(value, AXES, pairs)  103 us
    ppermute x89, starting transfers between devices, swap(): return lax.ppermute(value, AXES, pairs)  97.1 us
    pallas_call x17, Pallas kernels, call(): pl.pallas_call(kernel, out_shape=tuple(out_shape) if several else out_sha...  14.8 us
  transfers between devices with their start and end apart: 89, of which 52 were waited for; matrix products, arithmetic and copies ran while one was open for 0% of the time, Pallas kernels for 0%

profile of v2, /device:TPU:0, one launch (start us, length us, event | category | flops | bytes accessed | tf_op | source)
XLA Modules:
  0.0 224.9 jit_solution(9059599205379814264)
XLA Ops:
  4.9 3.0 %collective-permute-start = (f32[72,8,128]{2,1,0:T(8,128)S(1)}, f32[72,8,128]{2,1,0:T(8,128)S(1)}, u32[]{:S(2)}, u32[]{:S(2)}) collective-permute-start(f32[72,8,128]{2,1,0:T(8,128)S(1)} %get-tuple-element.92), channel_id=1, source_target_pairs={{0,1},{1,0},{2,3},{3,2},{4,5},{5,4},{6,7},{7,6},{8,9},{9,8},{10,11... | collective-permute-start | bytes 884744 | tf_op jit(solution)/shard_map/ppermute | solution.py:220
  9.5 5.5 %collective-permute-done.recv_a.one_a = f32[72,8,128]{2,1,0:T(8,128)S(1)} collective-permute-done((f32[72,8,128]{2,1,0:T(8,128)S(1)}, f32[72,8,128]{2,1,0:T(8,128)S(1)}, u32[]{:S(2)}, u32[]{:S(2)}) %collective-permute-start) | collective-permute-done | bytes 294944 | tf_op jit(solution)/shard_map/ppermute | solution.py:220
  18.6 3.1 %collective-permute-done.2.two_a = f32[36,8,128]{2,1,0:T(8,128)S(1)} collective-permute-done((f32[36,8,128]{2,1,0:T(8,128)S(1)}, f32[36,8,128]{2,1,0:T(8,128)S(1)}, u32[]{:S(2)}, u32[]{:S(2)}) %collective-permute-start.2) | collective-permute-done | bytes 147488 | tf_op jit(solution)/shard_map/ppermute | solution.py:220
  24.9 2.6 %collective-permute-start.5 = (f32[9,8,128]{2,1,0:T(8,128)S(1)}, f32[9,8,128]{2,1,0:T(8,128)S(1)}, u32[]{:S(2)}, u32[]{:S(2)}) collective-permute-start(f32[9,8,128]{2,1,0:T(8,128)S(1)} %get-tuple-element.99), channel_id=1, source_target_pairs={{0,8},{1,9},{2,10},{3,11},{4,12},{5,13},{6,14},{7,15},{8,0},{9,1},... | collective-permute-start | bytes 110600 | tf_op jit(solution)/shard_map/ppermute | solution.py:220
  28.5 3.1 %collective-permute-start.9 = (f32[9,8,128]{2,1,0:T(8,128)S(1)}, f32[9,8,128]{2,1,0:T(8,128)S(1)}, u32[]{:S(2)}, u32[]{:S(2)}) collective-permute-start(f32[9,8,128]{2,1,0:T(8,128)S(1)} %get-tuple-element.103), channel_id=1, source_target_pairs={{0,24},{1,25},{2,26},{3,27},{4,28},{5,29},{6,30},{7,31},{8,16},{9,... | collective-permute-start | bytes 110600 | tf_op jit(solution)/shard_map/ppermute | solution.py:220
  34.1 2.7 %collective-permute-done.10.refs_7_ = f32[9,8,128]{2,1,0:T(8,128)S(1)} collective-permute-done((f32[9,8,128]{2,1,0:T(8,128)S(1)}, f32[9,8,128]{2,1,0:T(8,128)S(1)}, u32[]{:S(2)}, u32[]{:S(2)}) %collective-permute-start.10) | collective-permute-done | bytes 36896 | tf_op jit(solution)/shard_map/ppermute | solution.py:220
  36.8 3.4 %copy-done.1 = bf16[1,1,2048,2048]{3,2,1,0:T(8,128)(2,1)S(1)} copy-done((bf16[1,1,2048,2048]{3,2,1,0:T(8,128)(2,1)S(1)}, bf16[1,1,2048,2048]{3,2,1,0:T(8,128)(2,1)}, u32[]{:S(2)}) %copy-start.1) | copy-done | bytes 8388632
  43.3 3.1 %collective-permute-start.17 = (f32[8,8,128]{2,1,0:T(8,128)S(1)}, f32[8,8,128]{2,1,0:T(8,128)S(1)}, u32[]{:S(2)}, u32[]{:S(2)}) collective-permute-start(f32[8,8,128]{2,1,0:T(8,128)S(1)} %get-tuple-element.109), channel_id=1, source_target_pairs={{0,20},{1,21},{2,22},{3,23},{4,16},{5,17},{6,18},{7,19},{8,28},{9,... | collective-permute-start | bytes 98312 | tf_op jit(solution)/shard_map/ppermute | solution.py:220
  54.2 4.7 %collective-permute-done.14 = f32[32,8,128]{2,1,0:T(8,128)S(1)} collective-permute-done((f32[32,8,128]{2,1,0:T(8,128)S(1)}, f32[32,8,128]{2,1,0:T(8,128)S(1)}, u32[]{:S(2)}, u32[]{:S(2)}) %collective-permute-start.14) | collective-permute-done | bytes 131104 | tf_op jit(solution)/shard_map/ppermute | solution.py:220
  60.1 6.1 %collective-permute-done.15.refs_1_ = f32[64,8,128]{2,1,0:T(8,128)S(1)} collective-permute-done((f32[64,8,128]{2,1,0:T(8,128)S(1)}, f32[64,8,128]{2,1,0:T(8,128)S(1)}, u32[]{:S(2)}, u32[]{:S(2)}) %collective-permute-start.15) | collective-permute-done | bytes 262176 | tf_op jit(solution)/shard_map/ppermute | solution.py:220
  70.1 4.7 %collective-permute-done.22.recv_a.one_a = f32[72,8,128]{2,1,0:T(8,128)S(1)} collective-permute-done((f32[72,8,128]{2,1,0:T(8,128)S(1)}, f32[72,8,128]{2,1,0:T(8,128)S(1)}, u32[]{:S(2)}, u32[]{:S(2)}) %collective-permute-start.22) | collective-permute-done | bytes 294944 | tf_op jit(solution)/shard_map/ppermute | solution.py:220
  78.0 4.1 %collective-permute-done.24.two_a = f32[36,8,128]{2,1,0:T(8,128)S(1)} collective-permute-done((f32[36,8,128]{2,1,0:T(8,128)S(1)}, f32[36,8,128]{2,1,0:T(8,128)S(1)}, u32[]{:S(2)}, u32[]{:S(2)}) %collective-permute-start.24) | collective-permute-done | bytes 147488 | tf_op jit(solution)/shard_map/ppermute | solution.py:220
  84.9 2.3 %collective-permute-start.28 = (f32[9,8,128]{2,1,0:T(8,128)S(1)}, f32[9,8,128]{2,1,0:T(8,128)S(1)}, u32[]{:S(2)}, u32[]{:S(2)}) collective-permute-start(f32[9,8,128]{2,1,0:T(8,128)S(1)} %get-tuple-element.119), channel_id=1, source_target_pairs={{0,12},{1,13},{2,14},{3,15},{4,8},{5,9},{6,10},{7,11},{8,4},{9,5},... | collective-permute-start | bytes 110600 | tf_op jit(solution)/shard_map/ppermute | solution.py:220
  92.1 2.3 %collective-permute-done.32.refs_7_ = f32[9,8,128]{2,1,0:T(8,128)S(1)} collective-permute-done((f32[9,8,128]{2,1,0:T(8,128)S(1)}, f32[9,8,128]{2,1,0:T(8,128)S(1)}, u32[]{:S(2)}, u32[]{:S(2)}) %collective-permute-start.32) | collective-permute-done | bytes 36896 | tf_op jit(solution)/shard_map/ppermute | solution.py:220
  94.5 2.1 shard_map.80
  96.6 2.1 collective-permute-start.41
  109.7 3.4 %collective-permute-done.36 = f32[32,8,128]{2,1,0:T(8,128)S(1)} collective-permute-done((f32[32,8,128]{2,1,0:T(8,128)S(1)}, f32[32,8,128]{2,1,0:T(8,128)S(1)}, u32[]{:S(2)}, u32[]{:S(2)}) %collective-permute-start.36) | collective-permute-done | bytes 131104 | tf_op jit(solution)/shard_map/ppermute | solution.py:220
  115.3 4.2 %collective-permute-done.37.refs_1_ = f32[64,8,128]{2,1,0:T(8,128)S(1)} collective-permute-done((f32[64,8,128]{2,1,0:T(8,128)S(1)}, f32[64,8,128]{2,1,0:T(8,128)S(1)}, u32[]{:S(2)}, u32[]{:S(2)}) %collective-permute-start.37) | collective-permute-done | bytes 262176 | tf_op jit(solution)/shard_map/ppermute | solution.py:220
  124.7 3.7 %collective-permute-done.44.recv_a.one_a = f32[72,8,128]{2,1,0:T(8,128)S(1)} collective-permute-done((f32[72,8,128]{2,1,0:T(8,128)S(1)}, f32[72,8,128]{2,1,0:T(8,128)S(1)}, u32[]{:S(2)}, u32[]{:S(2)}) %collective-permute-start.44) | collective-permute-done | bytes 294944 | tf_op jit(solution)/shard_map/ppermute | solution.py:220
  128.4 3.0 %collective-permute-done.45.recv_b.one_b = f32[72,8,128]{2,1,0:T(8,128)S(1)} collective-permute-done((f32[72,8,128]{2,1,0:T(8,128)S(1)}, f32[72,8,128]{2,1,0:T(8,128)S(1)}, u32[]{:S(2)}, u32[]{:S(2)}) %collective-permute-start.45) | collective-permute-done | bytes 294944 | tf_op jit(solution)/shard_map/ppermute | solution.py:220
  133.7 3.0 %collective-permute-done.46.two_a = f32[36,8,128]{2,1,0:T(8,128)S(1)} collective-permute-done((f32[36,8,128]{2,1,0:T(8,128)S(1)}, f32[36,8,128]{2,1,0:T(8,128)S(1)}, u32[]{:S(2)}, u32[]{:S(2)}) %collective-permute-start.46) | collective-permute-done | bytes 147488 | tf_op jit(solution)/shard_map/ppermute | solution.py:220
  147.6 2.5 %collective-permute-done.54.refs_7_ = f32[9,8,128]{2,1,0:T(8,128)S(1)} collective-permute-done((f32[9,8,128]{2,1,0:T(8,128)S(1)}, f32[9,8,128]{2,1,0:T(8,128)S(1)}, u32[]{:S(2)}, u32[]{:S(2)}) %collective-permute-start.54) | collective-permute-done | bytes 36896 | tf_op jit(solution)/shard_map/ppermute | solution.py:220
  150.1 2.1 shard_map.84
  154.3 2.2 collective-permute-start.61
  164.4 4.6 %collective-permute-done.58 = f32[32,8,128]{2,1,0:T(8,128)S(1)} collective-permute-done((f32[32,8,128]{2,1,0:T(8,128)S(1)}, f32[32,8,128]{2,1,0:T(8,128)S(1)}, u32[]{:S(2)}, u32[]{:S(2)}) %collective-permute-start.58) | collective-permute-done | bytes 131104 | tf_op jit(solution)/shard_map/ppermute | solution.py:220
  170.2 6.0 %collective-permute-done.59.refs_1_ = f32[64,8,128]{2,1,0:T(8,128)S(1)} collective-permute-done((f32[64,8,128]{2,1,0:T(8,128)S(1)}, f32[64,8,128]{2,1,0:T(8,128)S(1)}, u32[]{:S(2)}, u32[]{:S(2)}) %collective-permute-start.59) | collective-permute-done | bytes 262176 | tf_op jit(solution)/shard_map/ppermute | solution.py:220
  180.2 4.6 %collective-permute-done.66.recv_a.one_a = f32[72,8,128]{2,1,0:T(8,128)S(1)} collective-permute-done((f32[72,8,128]{2,1,0:T(8,128)S(1)}, f32[72,8,128]{2,1,0:T(8,128)S(1)}, u32[]{:S(2)}, u32[]{:S(2)}) %collective-permute-start.66) | collective-permute-done | bytes 294944 | tf_op jit(solution)/shard_map/ppermute | solution.py:220
  184.7 2.3 %collective-permute-done.67.recv_b.one_b = f32[72,8,128]{2,1,0:T(8,128)S(1)} collective-permute-done((f32[72,8,128]{2,1,0:T(8,128)S(1)}, f32[72,8,128]{2,1,0:T(8,128)S(1)}, u32[]{:S(2)}, u32[]{:S(2)}) %collective-permute-start.67) | collective-permute-done | bytes 294944 | tf_op jit(solution)/shard_map/ppermute | solution.py:220
  188.0 4.3 %collective-permute-done.68.two_a = f32[36,8,128]{2,1,0:T(8,128)S(1)} collective-permute-done((f32[36,8,128]{2,1,0:T(8,128)S(1)}, f32[36,8,128]{2,1,0:T(8,128)S(1)}, u32[]{:S(2)}, u32[]{:S(2)}) %collective-permute-start.68) | collective-permute-done | bytes 147488 | tf_op jit(solution)/shard_map/ppermute | solution.py:220
  202.3 2.4 %collective-permute-done.76.refs_7_ = f32[9,8,128]{2,1,0:T(8,128)S(1)} collective-permute-done((f32[9,8,128]{2,1,0:T(8,128)S(1)}, f32[9,8,128]{2,1,0:T(8,128)S(1)}, u32[]{:S(2)}, u32[]{:S(2)}) %collective-permute-start.76) | collective-permute-done | bytes 36896 | tf_op jit(solution)/shard_map/ppermute | solution.py:220
  204.6 2.4 %shard_map.88 = f32[3,8,128]{2,1,0:T(8,128)S(1)} custom-call(s32[1]{0:T(128)} %bitcast.side, f32[8,2048]{1,0:T(8,128)S(1)} %get-tuple-element.147.load_r, f32[8,2048]{1,0:T(8,128)S(1)} %get-tuple-element.148.load_d, bf16[2048,2048]{1,0:T(8,128)(2,1)S(1)} %bitcast.22, f32[9,8,128]{2,1,0:T(8,128)S(1)} %get-tuple-element.162.refs_0_, ...), custom_call_target="tpu_custom_call" | custom-call | tf_op jit(solution)/shard_map/pallas_call | solution.py:192
  218.4 2.4 %collective-permute-start.84 = (f32[8,128]{1,0:T(8,128)S(1)}, f32[8,128]{1,0:T(8,128)S(1)}, u32[]{:S(2)}, u32[]{:S(2)}) collective-permute-start(f32[8,128]{1,0:T(8,128)S(1)} %add_add_fusion.1), channel_id=1, source_target_pairs={{0,4},{1,5},{2,6},{3,7},{4,0},{5,1},{6,2},{7,3},{8,12},{9,13},{10,... | collective-permute-start | bytes 12296 | tf_op jit(solution)/shard_map/ppermute | solution.py:220
  (229 shorter events, 116.5 us)
Async XLA Ops:
  4.9 10.0 %collective-permute-start = (f32[72,8,128]{2,1,0:T(8,128)S(1)}, f32[72,8,128]{2,1,0:T(8,128)S(1)}, u32[]{:S(2)}, u32[]{:S(2)}) collective-permute-start(f32[72,8,128]{2,1,0:T(8,128)S(1)} %get-tuple-element.92), channel_id=1, source_target_pairs={{0,1},{1,0},{2,3},{3,2},{4,5},{5,4},{6,7},{7,6},{8,9},{9,8},{10,11... | collective-permute-start | bytes 884744 | tf_op jit(solution)/shard_map/ppermute | solution.py:220
  7.9 8.5 %collective-permute-start.1 = (f32[72,8,128]{2,1,0:T(8,128)S(1)}, f32[72,8,128]{2,1,0:T(8,128)S(1)}, u32[]{:S(2)}, u32[]{:S(2)}) collective-permute-start(f32[72,8,128]{2,1,0:T(8,128)S(1)} %get-tuple-element.94), channel_id=1, source_target_pairs={{0,2},{1,3},{2,0},{3,1},{4,6},{5,7},{6,4},{7,5},{8,10},{9,11},{10,... | collective-permute-start | bytes 884744 | tf_op jit(solution)/shard_map/ppermute | solution.py:220
  24.9 6.7 %collective-permute-start.5 = (f32[9,8,128]{2,1,0:T(8,128)S(1)}, f32[9,8,128]{2,1,0:T(8,128)S(1)}, u32[]{:S(2)}, u32[]{:S(2)}) collective-permute-start(f32[9,8,128]{2,1,0:T(8,128)S(1)} %get-tuple-element.99), channel_id=1, source_target_pairs={{0,8},{1,9},{2,10},{3,11},{4,12},{5,13},{6,14},{7,15},{8,0},{9,1},... | collective-permute-start | bytes 110600 | tf_op jit(solution)/shard_map/ppermute | solution.py:220
  27.5 6.2 %collective-permute-start.6 = (f32[9,8,128]{2,1,0:T(8,128)S(1)}, f32[9,8,128]{2,1,0:T(8,128)S(1)}, u32[]{:S(2)}, u32[]{:S(2)}) collective-permute-start(f32[9,8,128]{2,1,0:T(8,128)S(1)} %get-tuple-element.100), channel_id=1, source_target_pairs={{0,12},{1,13},{2,14},{3,15},{4,8},{5,9},{6,10},{7,11},{8,4},{9,5},... | collective-permute-start | bytes 110600 | tf_op jit(solution)/shard_map/ppermute | solution.py:220
  27.7 6.0 %collective-permute-start.7 = (f32[9,8,128]{2,1,0:T(8,128)S(1)}, f32[9,8,128]{2,1,0:T(8,128)S(1)}, u32[]{:S(2)}, u32[]{:S(2)}) collective-permute-start(f32[9,8,128]{2,1,0:T(8,128)S(1)} %get-tuple-element.101), channel_id=1, source_target_pairs={{0,16},{1,17},{2,18},{3,19},{4,20},{5,21},{6,22},{7,23},{8,24},{9,... | collective-permute-start | bytes 110600 | tf_op jit(solution)/shard_map/ppermute | solution.py:220
  27.7 6.0 %collective-permute-start.8 = (f32[9,8,128]{2,1,0:T(8,128)S(1)}, f32[9,8,128]{2,1,0:T(8,128)S(1)}, u32[]{:S(2)}, u32[]{:S(2)}) collective-permute-start(f32[9,8,128]{2,1,0:T(8,128)S(1)} %get-tuple-element.102), channel_id=1, source_target_pairs={{0,20},{1,21},{2,22},{3,23},{4,16},{5,17},{6,18},{7,19},{8,28},{9,... | collective-permute-start | bytes 110600 | tf_op jit(solution)/shard_map/ppermute | solution.py:220
  42.1 5.8 %collective-permute-start.19 = (f32[8,8,128]{2,1,0:T(8,128)S(1)}, f32[8,8,128]{2,1,0:T(8,128)S(1)}, u32[]{:S(2)}, u32[]{:S(2)}) collective-permute-start(f32[8,8,128]{2,1,0:T(8,128)S(1)} %get-tuple-element.109), channel_id=1, source_target_pairs={{0,28},{1,29},{2,30},{3,31},{4,24},{5,25},{6,26},{7,27},{8,20},{9,... | collective-permute-start | bytes 98312 | tf_op jit(solution)/shard_map/ppermute | solution.py:220
  43.3 7.5 %collective-permute-start.17 = (f32[8,8,128]{2,1,0:T(8,128)S(1)}, f32[8,8,128]{2,1,0:T(8,128)S(1)}, u32[]{:S(2)}, u32[]{:S(2)}) collective-permute-start(f32[8,8,128]{2,1,0:T(8,128)S(1)} %get-tuple-element.109), channel_id=1, source_target_pairs={{0,20},{1,21},{2,22},{3,23},{4,16},{5,17},{6,18},{7,19},{8,28},{9,... | collective-permute-start | bytes 98312 | tf_op jit(solution)/shard_map/ppermute | solution.py:220
  46.4 6.0 %collective-permute-start.13 = (f32[8,8,128]{2,1,0:T(8,128)S(1)}, f32[8,8,128]{2,1,0:T(8,128)S(1)}, u32[]{:S(2)}, u32[]{:S(2)}) collective-permute-start(f32[8,8,128]{2,1,0:T(8,128)S(1)} %get-tuple-element.108), channel_id=1, source_target_pairs={{0,12},{1,13},{2,14},{3,15},{4,8},{5,9},{6,10},{7,11},{8,4},{9,5},... | collective-permute-start | bytes 98312 | tf_op jit(solution)/shard_map/ppermute | solution.py:220
  50.8 8.7 %collective-permute-start.20 = (f32[32,8,128]{2,1,0:T(8,128)S(1)}, f32[32,8,128]{2,1,0:T(8,128)S(1)}, u32[]{:S(2)}, u32[]{:S(2)}) collective-permute-start(f32[32,8,128]{2,1,0:T(8,128)S(1)} %pad_maximum_fusion.1), channel_id=1, source_target_pairs={{0,1},{1,0},{2,3},{3,2},{4,5},{5,4},{6,7},{7,6},{8,9},{9,8},{10,11... | collective-permute-start | bytes 393224 | tf_op jit(solution)/shard_map/ppermute | solution.py:220
  58.9 7.3 %collective-permute-start.15 = (f32[64,8,128]{2,1,0:T(8,128)S(1)}, f32[64,8,128]{2,1,0:T(8,128)S(1)}, u32[]{:S(2)}, u32[]{:S(2)}) collective-permute-start(f32[64,8,128]{2,1,0:T(8,128)S(1)} %constant_dynamic-update-slice_fusion.refs_0_), channel_id=1, source_target_pairs={{0,1},{1,0},{2,3},{3,2},{4,5},{5,4},{6,7},{7,6},{8,9},{9,8},{10,11... | collective-permute-start | bytes 786440 | tf_op jit(solution)/shard_map/ppermute | solution.py:220
  59.6 7.0 %collective-permute-start.21 = (f32[64,8,128]{2,1,0:T(8,128)S(1)}, f32[64,8,128]{2,1,0:T(8,128)S(1)}, u32[]{:S(2)}, u32[]{:S(2)}) collective-permute-start(f32[64,8,128]{2,1,0:T(8,128)S(1)} %constant_dynamic-update-slice_fusion.5.refs_2_), channel_id=1, source_target_pairs={{0,2},{1,3},{2,0},{3,1},{4,6},{5,7},{6,4},{7,5},{8,10},{9,11},{10,... | collective-permute-start | bytes 786440 | tf_op jit(solution)/shard_map/ppermute | solution.py:220
  68.0 6.8 %collective-permute-start.22 = (f32[72,8,128]{2,1,0:T(8,128)S(1)}, f32[72,8,128]{2,1,0:T(8,128)S(1)}, u32[]{:S(2)}, u32[]{:S(2)}) collective-permute-start(f32[72,8,128]{2,1,0:T(8,128)S(1)} %get-tuple-element.111), channel_id=1, source_target_pairs={{0,1},{1,0},{2,3},{3,2},{4,5},{5,4},{6,7},{7,6},{8,9},{9,8},{10,11... | collective-permute-start | bytes 884744 | tf_op jit(solution)/shard_map/ppermute | solution.py:220
  69.6 7.3 %collective-permute-start.23 = (f32[72,8,128]{2,1,0:T(8,128)S(1)}, f32[72,8,128]{2,1,0:T(8,128)S(1)}, u32[]{:S(2)}, u32[]{:S(2)}) collective-permute-start(f32[72,8,128]{2,1,0:T(8,128)S(1)} %get-tuple-element.113), channel_id=1, source_target_pairs={{0,2},{1,3},{2,0},{3,1},{4,6},{5,7},{6,4},{7,5},{8,10},{9,11},{10,... | collective-permute-start | bytes 884744 | tf_op jit(solution)/shard_map/ppermute | solution.py:220
  84.9 6.5 %collective-permute-start.28 = (f32[9,8,128]{2,1,0:T(8,128)S(1)}, f32[9,8,128]{2,1,0:T(8,128)S(1)}, u32[]{:S(2)}, u32[]{:S(2)}) collective-permute-start(f32[9,8,128]{2,1,0:T(8,128)S(1)} %get-tuple-element.119), channel_id=1, source_target_pairs={{0,12},{1,13},{2,14},{3,15},{4,8},{5,9},{6,10},{7,11},{8,4},{9,5},... | collective-permute-start | bytes 110600 | tf_op jit(solution)/shard_map/ppermute | solution.py:220
  96.6 6.3 %collective-permute-start.41 = (f32[8,8,128]{2,1,0:T(8,128)S(1)}, f32[8,8,128]{2,1,0:T(8,128)S(1)}, u32[]{:S(2)}, u32[]{:S(2)}) collective-permute-start(f32[8,8,128]{2,1,0:T(8,128)S(1)} %get-tuple-element.132), channel_id=1, source_target_pairs={{0,28},{1,29},{2,30},{3,31},{4,24},{5,25},{6,26},{7,27},{8,20},{9,... | collective-permute-start | bytes 98312 | tf_op jit(solution)/shard_map/ppermute | solution.py:220
  98.7 6.5 %collective-permute-start.39 = (f32[8,8,128]{2,1,0:T(8,128)S(1)}, f32[8,8,128]{2,1,0:T(8,128)S(1)}, u32[]{:S(2)}, u32[]{:S(2)}) collective-permute-start(f32[8,8,128]{2,1,0:T(8,128)S(1)} %get-tuple-element.132), channel_id=1, source_target_pairs={{0,20},{1,21},{2,22},{3,23},{4,16},{5,17},{6,18},{7,19},{8,28},{9,... | collective-permute-start | bytes 98312 | tf_op jit(solution)/shard_map/ppermute | solution.py:220
  105.3 8.4 %collective-permute-start.42 = (f32[32,8,128]{2,1,0:T(8,128)S(1)}, f32[32,8,128]{2,1,0:T(8,128)S(1)}, u32[]{:S(2)}, u32[]{:S(2)}) collective-permute-start(f32[32,8,128]{2,1,0:T(8,128)S(1)} %pad_maximum_fusion.3), channel_id=1, source_target_pairs={{0,1},{1,0},{2,3},{3,2},{4,5},{5,4},{6,7},{7,6},{8,9},{9,8},{10,11... | collective-permute-start | bytes 393224 | tf_op jit(solution)/shard_map/ppermute | solution.py:220
  113.1 6.4 %collective-permute-start.37 = (f32[64,8,128]{2,1,0:T(8,128)S(1)}, f32[64,8,128]{2,1,0:T(8,128)S(1)}, u32[]{:S(2)}, u32[]{:S(2)}) collective-permute-start(f32[64,8,128]{2,1,0:T(8,128)S(1)} %constant_dynamic-update-slice_fusion.10.refs_0_), channel_id=1, source_target_pairs={{0,1},{1,0},{2,3},{3,2},{4,5},{5,4},{6,7},{7,6},{8,9},{9,8},{10,11... | collective-permute-start | bytes 786440 | tf_op jit(solution)/shard_map/ppermute | solution.py:220
  113.7 6.4 %collective-permute-start.43 = (f32[64,8,128]{2,1,0:T(8,128)S(1)}, f32[64,8,128]{2,1,0:T(8,128)S(1)}, u32[]{:S(2)}, u32[]{:S(2)}) collective-permute-start(f32[64,8,128]{2,1,0:T(8,128)S(1)} %constant_dynamic-update-slice_fusion.15.refs_2_), channel_id=1, source_target_pairs={{0,2},{1,3},{2,0},{3,1},{4,6},{5,7},{6,4},{7,5},{8,10},{9,11},{10,... | collective-permute-start | bytes 786440 | tf_op jit(solution)/shard_map/ppermute | solution.py:220
  121.6 6.8 %collective-permute-start.44 = (f32[72,8,128]{2,1,0:T(8,128)S(1)}, f32[72,8,128]{2,1,0:T(8,128)S(1)}, u32[]{:S(2)}, u32[]{:S(2)}) collective-permute-start(f32[72,8,128]{2,1,0:T(8,128)S(1)} %get-tuple-element.134), channel_id=1, source_target_pairs={{0,1},{1,0},{2,3},{3,2},{4,5},{5,4},{6,7},{7,6},{8,9},{9,8},{10,11... | collective-permute-start | bytes 884744 | tf_op jit(solution)/shard_map/ppermute | solution.py:220
  123.2 8.2 %collective-permute-start.45 = (f32[72,8,128]{2,1,0:T(8,128)S(1)}, f32[72,8,128]{2,1,0:T(8,128)S(1)}, u32[]{:S(2)}, u32[]{:S(2)}) collective-permute-start(f32[72,8,128]{2,1,0:T(8,128)S(1)} %get-tuple-element.136), channel_id=1, source_target_pairs={{0,2},{1,3},{2,0},{3,1},{4,6},{5,7},{6,4},{7,5},{8,10},{9,11},{10,... | collective-permute-start | bytes 884744 | tf_op jit(solution)/shard_map/ppermute | solution.py:220
  140.8 6.1 %collective-permute-start.50 = (f32[9,8,128]{2,1,0:T(8,128)S(1)}, f32[9,8,128]{2,1,0:T(8,128)S(1)}, u32[]{:S(2)}, u32[]{:S(2)}) collective-permute-start(f32[9,8,128]{2,1,0:T(8,128)S(1)} %get-tuple-element.142), channel_id=1, source_target_pairs={{0,12},{1,13},{2,14},{3,15},{4,8},{5,9},{6,10},{7,11},{8,4},{9,5},... | collective-permute-start | bytes 110600 | tf_op jit(solution)/shard_map/ppermute | solution.py:220
  152.2 6.2 %collective-permute-start.63 = (f32[8,8,128]{2,1,0:T(8,128)S(1)}, f32[8,8,128]{2,1,0:T(8,128)S(1)}, u32[]{:S(2)}, u32[]{:S(2)}) collective-permute-start(f32[8,8,128]{2,1,0:T(8,128)S(1)} %get-tuple-element.155), channel_id=1, source_target_pairs={{0,28},{1,29},{2,30},{3,31},{4,24},{5,25},{6,26},{7,27},{8,20},{9,... | collective-permute-start | bytes 98312 | tf_op jit(solution)/shard_map/ppermute | solution.py:220
  154.3 6.6 %collective-permute-start.61 = (f32[8,8,128]{2,1,0:T(8,128)S(1)}, f32[8,8,128]{2,1,0:T(8,128)S(1)}, u32[]{:S(2)}, u32[]{:S(2)}) collective-permute-start(f32[8,8,128]{2,1,0:T(8,128)S(1)} %get-tuple-element.155), channel_id=1, source_target_pairs={{0,20},{1,21},{2,22},{3,23},{4,16},{5,17},{6,18},{7,19},{8,28},{9,... | collective-permute-start | bytes 98312 | tf_op jit(solution)/shard_map/ppermute | solution.py:220
  156.5 6.0 %collective-permute-start.57 = (f32[8,8,128]{2,1,0:T(8,128)S(1)}, f32[8,8,128]{2,1,0:T(8,128)S(1)}, u32[]{:S(2)}, u32[]{:S(2)}) collective-permute-start(f32[8,8,128]{2,1,0:T(8,128)S(1)} %get-tuple-element.154), channel_id=1, source_target_pairs={{0,12},{1,13},{2,14},{3,15},{4,8},{5,9},{6,10},{7,11},{8,4},{9,5},... | collective-permute-start | bytes 98312 | tf_op jit(solution)/shard_map/ppermute | solution.py:220
  160.9 8.7 %collective-permute-start.64 = (f32[32,8,128]{2,1,0:T(8,128)S(1)}, f32[32,8,128]{2,1,0:T(8,128)S(1)}, u32[]{:S(2)}, u32[]{:S(2)}) collective-permute-start(f32[32,8,128]{2,1,0:T(8,128)S(1)} %pad_maximum_fusion.5), channel_id=1, source_target_pairs={{0,1},{1,0},{2,3},{3,2},{4,5},{5,4},{6,7},{7,6},{8,9},{9,8},{10,11... | collective-permute-start | bytes 393224 | tf_op jit(solution)/shard_map/ppermute | solution.py:220
  169.1 7.2 %collective-permute-start.59 = (f32[64,8,128]{2,1,0:T(8,128)S(1)}, f32[64,8,128]{2,1,0:T(8,128)S(1)}, u32[]{:S(2)}, u32[]{:S(2)}) collective-permute-start(f32[64,8,128]{2,1,0:T(8,128)S(1)} %constant_dynamic-update-slice_fusion.20.refs_0_), channel_id=1, source_target_pairs={{0,1},{1,0},{2,3},{3,2},{4,5},{5,4},{6,7},{7,6},{8,9},{9,8},{10,11... | collective-permute-start | bytes 786440 | tf_op jit(solution)/shard_map/ppermute | solution.py:220
  169.6 6.8 %collective-permute-start.65 = (f32[64,8,128]{2,1,0:T(8,128)S(1)}, f32[64,8,128]{2,1,0:T(8,128)S(1)}, u32[]{:S(2)}, u32[]{:S(2)}) collective-permute-start(f32[64,8,128]{2,1,0:T(8,128)S(1)} %constant_dynamic-update-slice_fusion.25.refs_2_), channel_id=1, source_target_pairs={{0,2},{1,3},{2,0},{3,1},{4,6},{5,7},{6,4},{7,5},{8,10},{9,11},{10,... | collective-permute-start | bytes 786440 | tf_op jit(solution)/shard_map/ppermute | solution.py:220
  178.0 6.8 %collective-permute-start.66 = (f32[72,8,128]{2,1,0:T(8,128)S(1)}, f32[72,8,128]{2,1,0:T(8,128)S(1)}, u32[]{:S(2)}, u32[]{:S(2)}) collective-permute-start(f32[72,8,128]{2,1,0:T(8,128)S(1)} %get-tuple-element.157), channel_id=1, source_target_pairs={{0,1},{1,0},{2,3},{3,2},{4,5},{5,4},{6,7},{7,6},{8,9},{9,8},{10,11... | collective-permute-start | bytes 884744 | tf_op jit(solution)/shard_map/ppermute | solution.py:220
  179.6 7.4 %collective-permute-start.67 = (f32[72,8,128]{2,1,0:T(8,128)S(1)}, f32[72,8,128]{2,1,0:T(8,128)S(1)}, u32[]{:S(2)}, u32[]{:S(2)}) collective-permute-start(f32[72,8,128]{2,1,0:T(8,128)S(1)} %get-tuple-element.159), channel_id=1, source_target_pairs={{0,2},{1,3},{2,0},{3,1},{4,6},{5,7},{6,4},{7,5},{8,10},{9,11},{10,... | collective-permute-start | bytes 884744 | tf_op jit(solution)/shard_map/ppermute | solution.py:220
  195.3 6.2 %collective-permute-start.72 = (f32[9,8,128]{2,1,0:T(8,128)S(1)}, f32[9,8,128]{2,1,0:T(8,128)S(1)}, u32[]{:S(2)}, u32[]{:S(2)}) collective-permute-start(f32[9,8,128]{2,1,0:T(8,128)S(1)} %get-tuple-element.165), channel_id=1, source_target_pairs={{0,12},{1,13},{2,14},{3,15},{4,8},{5,9},{6,10},{7,11},{8,4},{9,5},... | collective-permute-start | bytes 110600 | tf_op jit(solution)/shard_map/ppermute | solution.py:220
  (61 other events, 391.3 us)

commit v3 on v0

v3 whole, which is shorter than its diff:
```python
import functools

import jax
import jax.numpy as jnp
from jax import lax
from jax.experimental import pallas as pl
from jax.experimental.pallas import tpu as pltpu
from jax.sharding import PartitionSpec as P

ITERS = 4
LANES = 128
SUBLANES = 8
VMEM = pl.BlockSpec(memory_space=pltpu.VMEM)
SMEM = pl.BlockSpec(memory_space=pltpu.SMEM)
ANY = pl.BlockSpec(memory_space=pl.ANY)
PARAMS = pltpu.CompilerParams(vmem_limit_bytes=40 * 1024 * 1024)


def f32(*shape):
    return jax.ShapeDtypeStruct(shape, jnp.float32)


def call(kernel, out_shape, specs, *operands, scratch=()):
    several = isinstance(out_shape, (tuple, list))
    return pl.pallas_call(
        kernel,
        out_shape=tuple(out_shape) if several else out_shape,
        in_specs=specs,
        out_specs=(VMEM,) * len(out_shape) if several else VMEM,
        scratch_shapes=list(scratch),
        compiler_params=PARAMS,
    )(*operands)


def fetch(block, held, sems):
    pieces = sems.shape[0]
    size = block.shape[0] // pieces
    copies = []
    for j in range(pieces):
        rows = pl.ds(j * size, size)
        copies.append(pltpu.make_async_copy(block.at[rows], held.at[rows], sems.at[j]))
        copies[-1].start()
    return copies


def per_case(value):
    return jnp.sum(value, axis=1, keepdims=True)


def respond(copies, held, load, gamma, energy, answer):
    ntile, ncase, width = load.shape
    npiece = len(copies)
    each = ntile // npiece
    total = jnp.zeros((2 * ncase, ntile * width), jnp.float32)
    for j in range(npiece):
        value = jnp.concatenate([load[j * each + i] for i in range(each)], axis=1)
        high = value.astype(jnp.bfloat16)
        low = (value - high.astype(jnp.float32)).astype(jnp.bfloat16)
        copies[j].wait()
        total = total + jnp.dot(
            jnp.concatenate([high, low], axis=0),
            held[j * each * width : (j + 1) * each * width, :],
            preferred_element_type=jnp.float32,
        )
    total = total[:ncase] + total[ncase:]
    work = 0.5 * energy
    for i in range(ntile):
        tile = total[:, i * width : (i + 1) * width]
        answer[i] = tile
        work = work + load[i] * tile
    lane = lax.broadcasted_iota(jnp.int32, work.shape, 1)
    sums = jnp.where(lane == 0, per_case(0.5 * gamma), 0.0)
    answer[ntile] = jnp.where(lane == 1, per_case(work), sums)


def pack_kernel(nh, tiles, place, field, table, message):
    ndest = message.shape[0] // tiles
    extra = table.shape[1]
    message[...] = jnp.zeros_like(message)

    def body(p, carry):
        message[pl.ds(place[p], nh)] = field[p]
        return carry

    lax.fori_loop(0, field.shape[0], body, 0, unroll=4)
    for i in range(ndest):
        message[(i + 1) * tiles - extra : (i + 1) * tiles] = table[i]


def start_kernel(nh, room, tiles, place, comp, message, block, r_out, answer, load, held, sems):
    copies = fetch(block, held, sems)
    load[...] = jnp.zeros_like(load)
    nrow = r_out.shape[0]
    zero = jnp.zeros(r_out.shape[2:], jnp.float32)

    def pair(i, sums):
        gamma, energy = sums
        for j in range(room):
            row = i * room + j
            r = message[pl.ds(i * tiles + j * nh, nh)]
            r_out[row] = r
            load[pl.ds(place[0, row], nh)] += r
            c = comp[row]
            for h in range(nh):
                square = r[h] * r[h]
                gamma = gamma + square
                energy = energy + c[h : h + 1] * square
        return gamma, energy

    gamma, energy = lax.fori_loop(0, nrow // room, pair, (zero, zero))
    respond(copies, held, load, gamma, energy, answer)


def share_kernel(own, other, message):
    last = own.shape[0] - 1
    sums = own[last] + other[last]
    for i in range(message.shape[0]):
        message[i, :last] = other[:last]
        message[i, last] = sums


def steps(first, sums, known):
    gamma, delta = sums[:, 0:1], sums[:, 1:2]
    if first:
        return gamma, gamma / delta, jnp.zeros_like(gamma)
    beta = gamma / known[:, 0:1]
    return gamma, gamma / (delta - beta * gamma / known[:, 1:2]), beta


def home_kernel(first, nh, per, unroll, place, keep, comp, own, recv, known, block, *refs):
    if first:
        r_in, r, d, x, s, answer, known_out, load, held, sems = refs
    else:
        r_in, d_in, x_in, s_in, r, d, x, s, answer, known_out, load, held, sems = refs
    copies = fetch(block, held, sems)
    load[...] = jnp.zeros_like(load)
    ncase, width = r.shape[2:]
    sums = recv[per - 1]
    for i in range(1, recv.shape[0] // per):
        sums = sums + recv[(i + 1) * per - 1]
    gamma, alpha, beta = steps(first, sums, known[...])
    lane = lax.broadcasted_iota(jnp.int32, (ncase, width), 1)
    known_out[...] = jnp.where(lane == 0, gamma, alpha)
    alpha = jnp.broadcast_to(alpha, (ncase, width))
    beta = jnp.broadcast_to(beta, (ncase, width))
    zero = jnp.zeros((ncase, width), jnp.float32)

    def body(row, sums):
        gamma, energy = sums
        near, far, on = place[0, row], place[1, row], keep[row]
        c = comp[row]
        for h in range(nh):
            residual = r_in[row, h]
            image = on * (own[near + h] + recv[far + h] + c[h : h + 1] * residual)
            if first:
                direction, moved = residual, alpha * residual
            else:
                direction = residual + beta * d_in[row, h]
                image = image + beta * s_in[row, h]
                moved = x_in[row, h] + alpha * direction
            residual = residual - alpha * image
            r[row, h], d[row, h], x[row, h], s[row, h] = residual, direction, moved, image
            load[near + h] += residual
            square = residual * residual
            gamma = gamma + square
            energy = energy + c[h : h + 1] * square
        return gamma, energy

    gamma, energy = lax.fori_loop(0, r.shape[0], body, (zero, zero), unroll=unroll)
    respond(copies, held, load, gamma, energy, answer)


def end_kernel(nbody, unroll, side, sums, known, r, d, x, message):
    nrow, nh, ncase, width = r.shape
    total = sums[0]
    for i in range(1, sums.shape[0]):
        total = total + sums[i]
    gamma, alpha, beta = steps(False, total, known[...])
    alpha = jnp.broadcast_to(alpha, (ncase, width))
    beta = jnp.broadcast_to(beta, (ncase, width))
    share = ncase // nbody
    which = jnp.full((nh * share, width), side[0], jnp.int32)

    def body(row, carry):
        moved = [x[row, h] + alpha * (r[row, h] + beta * d[row, h]) for h in range(nh)]
        tile = None
        for b in range(nbody):
            part = jnp.concatenate([value[b * share : (b + 1) * share] for value in moved], axis=0)
            tile = part if tile is None else jnp.where(which == b, part, tile)
        message[row] = tile
        return carry

    lax.fori_loop(0, nrow, body, 0, unroll=unroll)


def take_kernel(row, recv, out):
    def body(p, carry):
        out[p] = recv[row[p]]
        return carry

    lax.fori_loop(0, out.shape[0], body, 0, unroll=8)


def on_device(rhs, compliance, plate_owner, found_owner, slot_pairs, active, inverse):
    nsub = lax.axis_size("sub")
    nbody = lax.axis_size("body")
    side = lax.axis_index("body")
    ncase, npatch, gap = rhs.shape
    block = inverse[0, 0]
    nslot = block.shape[0] // gap
    nh = gap // LANES
    per = nslot * nh + 1
    room = max(2, 2 * npatch // nsub)
    nrow = nsub * room
    lines = -(-room * nh // SUBLANES)
    deep = -(-room // SUBLANES)
    tiles = room * nh + lines + deep
    unroll = 4

    def exchange(message):
        return lax.all_to_all(message, "sub", split_axis=0, concat_axis=0, tiled=True)

    def sibling(value):
        return lax.ppermute(value, "body", [(i, nbody - 1 - i) for i in range(nbody)])

    keep = active.astype(jnp.float32)
    owners = jnp.stack([plate_owner[:, 0], found_owner[:, 0]])
    slots = slot_pairs.T
    owner, other = jnp.where(side == 0, owners, owners[::-1])
    slot, other_slot = jnp.where(side == 0, slots, slots[::-1])
    index = jnp.arange(npatch, dtype=jnp.int32)
    earlier = (owner[None, :] == owner[:, None]) & (index[None, :] < index[:, None])
    rank = jnp.sum(earlier.astype(jnp.int32), axis=1)
    row = owner * room + rank
    place = owner * tiles + rank * nh

    facts = jnp.stack([slot * nh, other * per + other_slot * nh], axis=1).astype(jnp.float32)
    facts = jnp.concatenate([facts, keep[:, None]], axis=1)
    facts = jnp.concatenate([compliance, jnp.pad(facts, ((0, 0), (0, LANES - 3)))], axis=1)
    placed = (row[None, :] == jnp.arange(nrow, dtype=jnp.int32)[:, None]).astype(jnp.float32)
    facts = jnp.dot(placed, facts, precision=lax.Precision.HIGHEST).reshape(nsub, room, gap + LANES)
    lined = facts[:, :, :gap].reshape(nsub, room * nh, LANES)
    lined = jnp.pad(lined, ((0, 0), (0, lines * SUBLANES - room * nh), (0, 0)))
    named = jnp.pad(facts[:, :, gap:], ((0, 0), (0, deep * SUBLANES - room), (0, 0)))
    table = jnp.concatenate([lined, named], axis=1).reshape(nsub, lines + deep, SUBLANES, LANES)
    start = (keep[None, :, None] * rhs).reshape(ncase, npatch, nh, LANES)
    start = jnp.transpose(start, (1, 2, 0, 3))

    message = call(
        functools.partial(pack_kernel, nh, tiles),
        f32(nsub * tiles, ncase, LANES),
        [SMEM, VMEM, VMEM],
        place,
        start,
        table,
    )
    message = exchange(message.reshape(nsub, tiles, ncase, LANES))
    told = message[:, room * nh :].reshape(nsub, (lines + deep) * SUBLANES, LANES)
    comp = told[:, : room * nh].reshape(nrow, nh, LANES)
    named = told[:, lines * SUBLANES : lines * SUBLANES + room, :3].reshape(nrow, 3).T
    home = named[:2].astype(jnp.int32)
    on = named[2]

    field = f32(nrow, nh, ncase, LANES)
    answer = f32(per, ncase, LANES)
    held = [
        pltpu.VMEM((nslot * nh, ncase, LANES), jnp.float32),
        pltpu.VMEM(block.shape, block.dtype),
        pltpu.SemaphoreType.DMA((nslot,)),
    ]
    r, own = call(
        functools.partial(start_kernel, nh, room, tiles),
        (field, answer),
        [SMEM, VMEM, VMEM, ANY],
        home,
        comp,
        message.reshape(nsub * tiles, ncase, LANES),
        block,
        scratch=held,
    )
    known = jnp.zeros((ncase, LANES), jnp.float32)
    state = [r]
    for step in range(ITERS - 1):
        message = call(share_kernel, f32(nsub, per, ncase, LANES), [VMEM] * 2, own, sibling(own))
        recv = exchange(message).reshape(nsub * per, ncase, LANES)
        *state, own, known = call(
            functools.partial(home_kernel, step == 0, nh, per, unroll),
            (field,) * 4 + (answer, f32(ncase, LANES)),
            [SMEM, SMEM] + [VMEM] * 4 + [ANY] + [VMEM] * len(state),
            home,
            on,
            comp,
            own,
            recv,
            known,
            block,
            *state,
            scratch=held,
        )
    r, d, x, _ = state
    sums = own[per - 1]
    sums = sums + sibling(sums)
    sums = exchange(jnp.broadcast_to(sums[None], (nsub, ncase, LANES)))
    message = call(
        functools.partial(end_kernel, nbody, unroll),
        f32(nrow, nh * ncase // nbody, LANES),
        [SMEM] + [VMEM] * 5,
        side.astype(jnp.int32).reshape(1),
        sums,
        known,
        r,
        d,
        x,
    )
    recv = exchange(message)
    mine = call(take_kernel, f32(npatch, nh * ncase // nbody, LANES), [SMEM, VMEM], row, recv)
    theirs = sibling(mine)
    both = jnp.stack([jnp.where(side == 0, mine, theirs), jnp.where(side == 0, theirs, mine)])
    both = both.reshape(nbody, npatch, nh, ncase // nbody, LANES)
    return jnp.transpose(both, (0, 3, 1, 2, 4)).reshape(ncase, npatch, gap)


def solution(mesh):
    in_specs = (
        P(None, "sub", None),
        P("sub", None),
        P("sub", None),
        P("sub", None),
        P("sub", None),
        P("sub"),
        P("body", "sub", None, None),
    )
    out_specs = P(None, "sub", None)
    return jax.shard_map(
        on_device, mesh=mesh, in_specs=in_specs, out_specs=out_specs, check_vma=False
    )
```

time: 743 us -> 202 us (0.27)
  waiting for transfers between devices: 313 us -> 32.3 us
  blocking collectives: 338 us -> 134 us
  other arithmetic: 26 us -> 2.6 us
  matrix products: 23.8 us -> 1.07 us
  Pallas kernels: 0 us -> 20.4 us
  between operations: 13.8 us -> 0.28 us
  starting transfers between devices: 12.5 us -> 4.05 us
  local copies, waits for them, and re-layouts: 14.8 us -> 6.43 us
    psum x7 -> x0, blocking collectives: 279 us -> none  [the longest x4 153 us: squares(): return lax.psum(products(residual, residual), 'sub')]
    all_gather x4 -> x0, waiting for transfers between devices: 217 us -> none  [on_device(): plate_piece = lax.all_gather(response[None], 'sub', axis=0, tiled=True)]
    all_to_all x3 -> x5, blocking collectives: 59.7 us -> 134 us  [exchange(): lax.all_to_all(message, 'sub', split_axis=0, concat_axis=0, tiled=True)]
    psum x4 -> x0, waiting for transfers between devices: 70.6 us -> none  [on_device(): total = lax.psum(own_part, 'body')]
    dot_general x8 -> x1, matrix products: 23.8 us -> 1.07 us  [on_device(): jnp.dot(placed, facts, precision=lax.Precision.HIGHEST)]
    pallas_call x0 -> x10, Pallas kernels: none -> 20.4 us  [call(): pl.pallas_call(kernel, out_shape=tuple(out_shape) if several else out_sha...]
    gather x10 -> x0, local copies, waits for them, and re-layouts: 13 us -> none  [the longest x4 7.67 us: on_device(): chosen = block_list[local, :, slot, :]]
    reduce_sum x9 -> x1, other arithmetic: 10.6 us -> 0.17 us  [on_device(): rank = jnp.sum(earlier.astype(jnp.int32), axis=1)]
  transfers between devices with their start and end apart: 10 -> 6, of which waited for: 10 -> 6; matrix products, arithmetic and copies ran while one was open for 1% -> 0% of each run, Pallas kernels for 0% -> 0%
where the time goes in v3:
time: 202 us; the launch traced here: 201 us
  blocking collectives  134 us (66%)
  waiting for transfers between devices  32.3 us (16%)
  Pallas kernels  20.4 us (10%)
  local copies, waits for them, and re-layouts  6.43 us (3%)
  starting transfers between devices  4.05 us (2%)
  other arithmetic  2.6 us (1%)
    all_to_all x5, blocking collectives, exchange(): lax.all_to_all(message, 'sub', split_axis=0, concat_axis=0, tiled=True)  134 us
    all_to_all x1, waiting for transfers between devices, exchange(): lax.all_to_all(message, 'sub', split_axis=0, concat_axis=0, tiled=True)  25.9 us
    pallas_call x10, Pallas kernels, call(): pl.pallas_call(kernel, out_shape=tuple(out_shape) if several else out_sha...  20.4 us
    ppermute x5, waiting for transfers between devices, sibling(): lax.ppermute(value, 'body', [(i, nbody - 1 - i) for i in range(nbody)])  6.42 us
  transfers between devices with their start and end apart: 6, of which 6 were waited for; matrix products, arithmetic and copies ran while one was open for 0% of the time, Pallas kernels for 0%

profile of v3, /device:TPU:0, one launch (start us, length us, event | category | flops | bytes accessed | tf_op | source)
XLA Modules:
  0.0 201.5 jit_solution(11263616437290262737)
XLA Ops:
  0.0 0.7 pad_add_fusion
  0.8 0.7 rev.7
  1.5 0.7 broadcast_select_fusion.2
  2.2 0.2 convert_reduce_fusion
  2.4 0.7 convert_bitcast_fusion
  3.2 1.1 convolution_bitcast_fusion
  4.4 0.3 reshape.92
  4.7 0.3 copy.27
  5.0 0.8 shard_map.73
  5.8 39.4 %all_to_all.30 = f32[16,19,8,128]{3,2,1,0:T(8,128)S(1)} all-to-all(f32[16,19,8,128]{3,2,1,0:T(8,128)S(1)} %bitcast.57), channel_id=1, replica_groups=mesh['body'=2,'sub'=16] {'sub'}, dimensions={0} | all-to-all | bytes 2490368 | tf_op jit(solution)/shard_map/all_to_all | solution.py:221
  45.3 3.4 %copy-done = bf16[1,1,2048,2048]{3,2,1,0:T(8,128)(2,1)S(1)} copy-done((bf16[1,1,2048,2048]{3,2,1,0:T(8,128)(2,1)S(1)}, bf16[1,1,2048,2048]{3,2,1,0:T(8,128)(2,1)}, u32[]{:S(2)}) %copy-start) | copy-done | bytes 8388632
  48.7 3.4 %shard_map.74 = (f32[128,2,8,128]{3,2,1,0:T(8,128)S(1)}, f32[17,8,128]{2,1,0:T(8,128)S(1)}) custom-call(s32[2,128]{1,0:T(2,128)S(1)} %slice_convert_fusion.place, f32[128,2,128]{2,1,0:T(2,128)S(1)} %bitcast.61, f32[304,8,128]{2,1,0:T(8,128)S(1)} %bitcast.56, bf16[2048,2048]{1,0:T(8,128)(2,1)S(1)} %bitcast.55), custom_call_target="tpu_custom_call" | custom-call | tf_op jit(solution)/shard_map/pallas_call | solution.py:25
  52.2 1.2 collective-permute-done.other
  53.4 1.1 shard_map.75
  54.5 3.7 %all-to-all-start.1 = ((f32[16,17,8,128]{3,2,1,0:T(8,128)}), f32[16,17,8,128]{3,2,1,0:T(8,128)S(1)}, u32[]{:S(2)}, u32[]{:S(2)}) async-start(f32[16,17,8,128]{3,2,1,0:T(8,128)} %shard_map.75), calls=%async_computation.1 | async-start | bytes 2228224 | tf_op jit(solution)/shard_map/all_to_all | solution.py:221
  58.2 25.9 %all-to-all-done.1 = f32[16,17,8,128]{3,2,1,0:T(8,128)S(1)} async-done(((f32[16,17,8,128]{3,2,1,0:T(8,128)}), f32[16,17,8,128]{3,2,1,0:T(8,128)S(1)}, u32[]{:S(2)}, u32[]{:S(2)}) %all-to-all-start.1) | async-done | bytes 1114144 | tf_op jit(solution)/shard_map/all_to_all | solution.py:221
  84.0 4.4 %shard_map.76 = (f32[128,2,8,128]{3,2,1,0:T(8,128)S(1)}, f32[128,2,8,128]{3,2,1,0:T(8,128)S(1)}, f32[128,2,8,128]{3,2,1,0:T(8,128)S(1)}, f32[128,2,8,128]{3,2,1,...) custom-call(s32[2,128]{1,0:T(2,128)S(1)} %slice_convert_fusion.place, f32[128]{0:T(128)S(1)} %slice_bitcast_fusion.3.keep, ...), custom_call_target="tpu_custom_call" | custom-call | tf_op jit(solution)/shard_map/pallas_call | solution.py:25
  88.5 1.2 collective-permute-done.1.other
  89.8 35.8 %all_to_all.31 = f32[16,17,8,128]{3,2,1,0:T(8,128)S(1)} all-to-all(f32[16,17,8,128]{3,2,1,0:T(8,128)S(1)} %shard_map.77), channel_id=1, replica_groups=mesh['body'=2,'sub'=16] {'sub'}, dimensions={0} | all-to-all | bytes 2228224 | tf_op jit(solution)/shard_map/all_to_all | solution.py:221
  125.6 4.4 %shard_map.78 = (f32[128,2,8,128]{3,2,1,0:T(8,128)S(1)}, f32[128,2,8,128]{3,2,1,0:T(8,128)S(1)}, f32[128,2,8,128]{3,2,1,0:T(8,128)S(1)}, f32[128,2,8,128]{3,2,1,...) custom-call(s32[2,128]{1,0:T(2,128)S(1)} %slice_convert_fusion.place, f32[128]{0:T(128)S(1)} %slice_bitcast_fusion.3.keep, ...), custom_call_target="tpu_custom_call" | custom-call | tf_op jit(solution)/shard_map/pallas_call | solution.py:25
  130.1 1.2 collective-permute-done.2.other
  131.4 31.9 %all_to_all.32 = f32[16,17,8,128]{3,2,1,0:T(8,128)S(1)} all-to-all(f32[16,17,8,128]{3,2,1,0:T(8,128)S(1)} %shard_map.79), channel_id=1, replica_groups=mesh['body'=2,'sub'=16] {'sub'}, dimensions={0} | all-to-all | bytes 2228224 | tf_op jit(solution)/shard_map/all_to_all | solution.py:221
  163.3 5.0 %shard_map.80 = (f32[128,2,8,128]{3,2,1,0:T(8,128)S(1)}, f32[128,2,8,128]{3,2,1,0:T(8,128)S(1)}, f32[128,2,8,128]{3,2,1,0:T(8,128)S(1)}, f32[128,2,8,128]{3,2,1,...) custom-call(s32[2,128]{1,0:T(2,128)S(1)} %slice_convert_fusion.place, f32[128]{0:T(128)S(1)} %slice_bitcast_fusion.3.keep, ...), custom_call_target="tpu_custom_call" | custom-call | tf_op jit(solution)/shard_map/pallas_call | solution.py:25
  168.4 1.2 collective-permute-done.3
  169.5 10.3 %all_to_all.33.sums = f32[16,8,128]{2,1,0:T(8,128)S(1)} all-to-all(f32[16,8,128]{2,1,0:T(8,128)S(1)} %broadcast_in_dim.8), channel_id=1, replica_groups=mesh['body'=2,'sub'=16] {'sub'}, dimensions={0} | all-to-all | bytes 131072 | tf_op jit(solution)/shard_map/all_to_all | solution.py:221
  179.8 0.7 shard_map.81
  180.5 17.1 %all_to_all.34.recv = f32[128,8,128]{2,1,0:T(8,128)S(1)} all-to-all(f32[128,8,128]{2,1,0:T(8,128)S(1)} %shard_map.81), channel_id=1, replica_groups=mesh['body'=2,'sub'=16] {'sub'}, dimensions={0} | all-to-all | bytes 1048576 | tf_op jit(solution)/shard_map/all_to_all | solution.py:221
  197.6 0.6 shard_map.82
  198.3 1.5 collective-permute-done.4
  199.9 0.1 maximum_bitcast_fusion
  200.0 0.3 copy.23
  200.3 1.2 reshape.104
  (33 shorter events, 1.0 us)
Async XLA Ops:
  0.0 4.3 %copy-start.1 = (f32[8,64,256]{2,1,0:T(8,128)S(1)}, f32[8,64,256]{2,1,0:T(8,128)}, u32[]{:S(2)}) copy-start(f32[8,64,256]{2,1,0:T(8,128)} %param.7) | copy-start | bytes 1572868
  45.3 3.4 %copy-start = (bf16[1,1,2048,2048]{3,2,1,0:T(8,128)(2,1)S(1)}, bf16[1,1,2048,2048]{3,2,1,0:T(8,128)(2,1)}, u32[]{:S(2)}) copy-start(bf16[1,1,2048,2048]{3,2,1,0:T(8,128)(2,1)} %param.13) | copy-start | bytes 25165828
  52.1 1.3 collective-permute-start
  54.5 29.6 %all-to-all-start.1 = ((f32[16,17,8,128]{3,2,1,0:T(8,128)}), f32[16,17,8,128]{3,2,1,0:T(8,128)S(1)}, u32[]{:S(2)}, u32[]{:S(2)}) async-start(f32[16,17,8,128]{3,2,1,0:T(8,128)} %shard_map.75), calls=%async_computation.1 | async-start | bytes 2228224 | tf_op jit(solution)/shard_map/all_to_all | solution.py:221
  88.4 1.3 collective-permute-start.1
  130.0 1.3 collective-permute-start.2
  168.3 1.2 collective-permute-start.3
  198.2 1.6 collective-permute-start.4

commit v4 on v3

--- a/solution.py
+++ b/solution.py
@@ -12,7 +12,6 @@
 SUBLANES = 8
 VMEM = pl.BlockSpec(memory_space=pltpu.VMEM)
 SMEM = pl.BlockSpec(memory_space=pltpu.SMEM)
-ANY = pl.BlockSpec(memory_space=pl.ANY)
 PARAMS = pltpu.CompilerParams(vmem_limit_bytes=40 * 1024 * 1024)
 
 
@@ -32,34 +31,21 @@
     )(*operands)
 
 
-def fetch(block, held, sems):
-    pieces = sems.shape[0]
-    size = block.shape[0] // pieces
-    copies = []
-    for j in range(pieces):
-        rows = pl.ds(j * size, size)
-        copies.append(pltpu.make_async_copy(block.at[rows], held.at[rows], sems.at[j]))
-        copies[-1].start()
-    return copies
-
-
 def per_case(value):
     return jnp.sum(value, axis=1, keepdims=True)
 
 
-def respond(copies, held, load, gamma, energy, answer):
+def respond(block, load, gamma, energy, answer):
     ntile, ncase, width = load.shape
-    npiece = len(copies)
-    each = ntile // npiece
+    each = 2
     total = jnp.zeros((2 * ncase, ntile * width), jnp.float32)
-    for j in range(npiece):
+    for j in range(ntile // each):
         value = jnp.concatenate([load[j * each + i] for i in range(each)], axis=1)
         high = value.astype(jnp.bfloat16)
         low = (value - high.astype(jnp.float32)).astype(jnp.bfloat16)
-        copies[j].wait()
         total = total + jnp.dot(
             jnp.concatenate([high, low], axis=0),
-            held[j * each * width : (j + 1) * each * width, :],
+            block[j * each * width : (j + 1) * each * width, :],
             preferred_element_type=jnp.float32,
         )
     total = total[:ncase] + total[ncase:]
@@ -73,9 +59,7 @@
     answer[ntile] = jnp.where(lane == 1, per_case(work), sums)
 
 
-def pack_kernel(nh, tiles, place, field, table, message):
-    ndest = message.shape[0] // tiles
-    extra = table.shape[1]
+def pack_kernel(nh, place, field, message):
     message[...] = jnp.zeros_like(message)
 
     def body(p, carry):
@@ -83,22 +67,18 @@
         return carry
 
     lax.fori_loop(0, field.shape[0], body, 0, unroll=4)
-    for i in range(ndest):
-        message[(i + 1) * tiles - extra : (i + 1) * tiles] = table[i]
-
-
-def start_kernel(nh, room, tiles, place, comp, message, block, r_out, answer, load, held, sems):
-    copies = fetch(block, held, sems)
+
+
+def start_kernel(nh, room, place, comp, message, block, answer, load):
     load[...] = jnp.zeros_like(load)
-    nrow = r_out.shape[0]
-    zero = jnp.zeros(r_out.shape[2:], jnp.float32)
+    nrow = message.shape[0]
+    zero = jnp.zeros(message.shape[2:], jnp.float32)
 
     def pair(i, sums):
         gamma, energy = sums
         for j in range(room):
             row = i * room + j
-            r = message[pl.ds(i * tiles + j * nh, nh)]
-            r_out[row] = r
+            r = message[row]
             load[pl.ds(place[0, row], nh)] += r
             c = comp[row]
             for h in range(nh):
@@ -108,15 +88,13 @@
         return gamma, energy
 
     gamma, energy = lax.fori_loop(0, nrow // room, pair, (zero, zero))
-    respond(copies, held, load, gamma, energy, answer)
-
-
-def share_kernel(own, other, message):
-    last = own.shape[0] - 1
-    sums = own[last] + other[last]
-    for i in range(message.shape[0]):
-        message[i, :last] = other[:last]
-        message[i, last] = sums
+    respond(block, load, gamma, energy, answer)
+
+
+def tree(values):
+    while len(values) > 1:
+        values = [a + b for a, b in zip(values[::2], values[1::2])]
+    return values[0]
 
 
 def steps(first, sums, known):
@@ -127,17 +105,19 @@
     return gamma, gamma / (delta - beta * gamma / known[:, 1:2]), beta
 
 
-def home_kernel(first, nh, per, unroll, place, keep, comp, own, recv, known, block, *refs):
+def home_kernel(first, nh, unroll, place, keep, comp, own, near_a, far_a, near_b, far_b, known, block, *refs):
     if first:
-        r_in, r, d, x, s, answer, known_out, load, held, sems = refs
+        r_in, r, d, x, s, answer, known_out, load, resp = refs
     else:
-        r_in, d_in, x_in, s_in, r, d, x, s, answer, known_out, load, held, sems = refs
-    copies = fetch(block, held, sems)
+        r_in, d_in, x_in, s_in, r, d, x, s, answer, known_out, load, resp = refs
     load[...] = jnp.zeros_like(load)
     ncase, width = r.shape[2:]
-    sums = recv[per - 1]
-    for i in range(1, recv.shape[0] // per):
-        sums = sums + recv[(i + 1) * per - 1]
+    at = 0
+    for part in (near_a, far_a, near_b, far_b):
+        resp[at : at + part.shape[0]] = part[...]
+        at += part.shape[0]
+    each = own.shape[0] // 2 + 1
+    sums = tree([part[i + each - 1] for part in (near_b, far_b) for i in range(0, part.shape[0], each)])
     gamma, alpha, beta = steps(first, sums, known[...])
     lane = lax.broadcasted_iota(jnp.int32, (ncase, width), 1)
     known_out[...] = jnp.where(lane == 0, gamma, alpha)
@@ -151,7 +131,7 @@
         c = comp[row]
         for h in range(nh):
             residual = r_in[row, h]
-            image = on * (own[near + h] + recv[far + h] + c[h : h + 1] * residual)
+            image = on * (own[near + h] + resp[far + h] + c[h : h + 1] * residual)
             if first:
                 direction, moved = residual, alpha * residual
             else:
@@ -167,15 +147,12 @@
         return gamma, energy
 
     gamma, energy = lax.fori_loop(0, r.shape[0], body, (zero, zero), unroll=unroll)
-    respond(copies, held, load, gamma, energy, answer)
+    respond(block, load, gamma, energy, answer)
 
 
 def end_kernel(nbody, unroll, side, sums, known, r, d, x, message):
     nrow, nh, ncase, width = r.shape
-    total = sums[0]
-    for i in range(1, sums.shape[0]):
-        total = total + sums[i]
-    gamma, alpha, beta = steps(False, total, known[...])
+    gamma, alpha, beta = steps(False, sums[...], known[...])
     alpha = jnp.broadcast_to(alpha, (ncase, width))
     beta = jnp.broadcast_to(beta, (ncase, width))
     share = ncase // nbody
@@ -214,11 +191,15 @@
     nrow = nsub * room
     lines = -(-room * nh // SUBLANES)
     deep = -(-room // SUBLANES)
-    tiles = room * nh + lines + deep
+    nz = nsub // 4
+    half = nslot // 2 * nh
     unroll = 4
 
     def exchange(message):
         return lax.all_to_all(message, "sub", split_axis=0, concat_axis=0, tiled=True)
+
+    def swap(value, far):
+        return lax.ppermute(value, "sub", [(i, i ^ far) for i in range(nsub)])
 
     def sibling(value):
         return lax.ppermute(value, "body", [(i, nbody - 1 - i) for i in range(nbody)])
@@ -232,9 +213,15 @@
     earlier = (owner[None, :] == owner[:, None]) & (index[None, :] < index[:, None])
     rank = jnp.sum(earlier.astype(jnp.int32), axis=1)
     row = owner * room + rank
-    place = owner * tiles + rank * nh
-
-    facts = jnp.stack([slot * nh, other * per + other_slot * nh], axis=1).astype(jnp.float32)
+    place = row * nh
+
+    away = owner ^ other
+    x_bit, y_bit, z_part = away & 1, (away >> 1) & 1, away >> 2
+    found_a = ((y_bit * 2 + x_bit) * nz + z_part) * half + other_slot * nh
+    found_b = ((x_bit * 2 + y_bit) * nz + z_part) * (half + 1) + (other_slot - nslot // 2) * nh
+    found = jnp.where(other_slot < nslot // 2, found_a, nsub * half + found_b)
+
+    facts = jnp.stack([slot * nh, found], axis=1).astype(jnp.float32)
     facts = jnp.concatenate([facts, keep[:, None]], axis=1)
     facts = jnp.concatenate([compliance, jnp.pad(facts, ((0, 0), (0, LANES - 3)))], axis=1)
     placed = (row[None, :] == jnp.arange(nrow, dtype=jnp.int32)[:, None]).astype(jnp.float32)
@@ -246,61 +233,65 @@
     start = (keep[None, :, None] * rhs).reshape(ncase, npatch, nh, LANES)
     start = jnp.transpose(start, (1, 2, 0, 3))
 
-    message = call(
-        functools.partial(pack_kernel, nh, tiles),
-        f32(nsub * tiles, ncase, LANES),
-        [SMEM, VMEM, VMEM],
-        place,
-        start,
-        table,
-    )
-    message = exchange(message.reshape(nsub, tiles, ncase, LANES))
-    told = message[:, room * nh :].reshape(nsub, (lines + deep) * SUBLANES, LANES)
+    told = exchange(table).reshape(nsub, (lines + deep) * SUBLANES, LANES)
     comp = told[:, : room * nh].reshape(nrow, nh, LANES)
     named = told[:, lines * SUBLANES : lines * SUBLANES + room, :3].reshape(nrow, 3).T
     home = named[:2].astype(jnp.int32)
     on = named[2]
+    message = call(
+        functools.partial(pack_kernel, nh), f32(nrow * nh, ncase, LANES), [SMEM, VMEM], place, start
+    )
+    r = exchange(message).reshape(nrow, nh, ncase, LANES)
 
     field = f32(nrow, nh, ncase, LANES)
     answer = f32(per, ncase, LANES)
-    held = [
-        pltpu.VMEM((nslot * nh, ncase, LANES), jnp.float32),
-        pltpu.VMEM(block.shape, block.dtype),
-        pltpu.SemaphoreType.DMA((nslot,)),
-    ]
-    r, own = call(
-        functools.partial(start_kernel, nh, room, tiles),
-        (field, answer),
-        [SMEM, VMEM, VMEM, ANY],
+    load = pltpu.VMEM((nslot * nh, ncase, LANES), jnp.float32)
+    spread = pltpu.VMEM((nsub * per, ncase, LANES), jnp.float32)
+    own = call(
+        functools.partial(start_kernel, nh, room),
+        answer,
+        [SMEM, VMEM, VMEM, VMEM],
         home,
         comp,
-        message.reshape(nsub * tiles, ncase, LANES),
+        r,
         block,
-        scratch=held,
+        scratch=[load],
     )
     known = jnp.zeros((ncase, LANES), jnp.float32)
     state = [r]
     for step in range(ITERS - 1):
-        message = call(share_kernel, f32(nsub, per, ncase, LANES), [VMEM] * 2, own, sibling(own))
-        recv = exchange(message).reshape(nsub * per, ncase, LANES)
+        other = sibling(own)
+        other = jnp.concatenate([other[: per - 1], own[per - 1 :] + other[per - 1 :]])
+        parts = [other] + [swap(other, 4 * z) for z in range(1, nz)]
+        a = jnp.concatenate([part[:half] for part in parts])
+        b = jnp.concatenate([part[half:] for part in parts])
+        far_a, far_b = swap(a, 1), swap(b, 2)
+        a, b = jnp.concatenate([a, far_a]), jnp.concatenate([b, far_b])
+        far_a, far_b = swap(a, 2), swap(b, 1)
         *state, own, known = call(
-            functools.partial(home_kernel, step == 0, nh, per, unroll),
+            functools.partial(home_kernel, step == 0, nh, unroll),
             (field,) * 4 + (answer, f32(ncase, LANES)),
-            [SMEM, SMEM] + [VMEM] * 4 + [ANY] + [VMEM] * len(state),
+            [SMEM, SMEM] + [VMEM] * (8 + len(state)),
             home,
             on,
             comp,
             own,
-            recv,
+            a,
+            far_a,
+            b,
+            far_b,
             known,
             block,
             *state,
-            scratch=held,
+            scratch=[load, spread],
         )
     r, d, x, _ = state
     sums = own[per - 1]
     sums = sums + sibling(sums)
-    sums = exchange(jnp.broadcast_to(sums[None], (nsub, ncase, LANES)))
+    far = 1
+    while far < nsub:
+        sums = sums + swap(sums, far)
+        far *= 2
     message = call(
         functools.partial(end_kernel, nbody, unroll),
         f32(nrow, nh * ncase // nbody, LANES),

time: 202 us -> 185 us (0.916)
  blocking collectives: 134 us -> 14.6 us
  waiting for transfers between devices: 32.3 us -> 90.1 us
  starting transfers between devices: 4.05 us -> 43.3 us
  Pallas kernels: 20.4 us -> 23.5 us
    all_to_all x5 -> x1, blocking collectives: 134 us -> 14.6 us  [exchange(): lax.all_to_all(message, 'sub', split_axis=0, concat_axis=0, tiled=True)]
    ppermute x0 -> x25, waiting for transfers between devices: none -> 54.9 us  [swap(): return lax.ppermute(value, 'sub', [(i, i ^ far) for i in range(nsub)])]
    ppermute x0 -> x25, starting transfers between devices: none -> 31.3 us  [swap(): return lax.ppermute(value, 'sub', [(i, i ^ far) for i in range(nsub)])]
    all_to_all x1 -> x2, starting transfers between devices: 3.7 us -> 12 us  [exchange(): lax.all_to_all(message, 'sub', split_axis=0, concat_axis=0, tiled=True)]
    pallas_call x10 -> x7, Pallas kernels: 20.4 us -> 23.5 us  [call(): pl.pallas_call(kernel, out_shape=tuple(out_shape) if several else out_sha...]
    all_to_all x1 -> x2, waiting for transfers between devices: 25.9 us -> 28.7 us  [exchange(): lax.all_to_all(message, 'sub', split_axis=0, concat_axis=0, tiled=True)]
  transfers between devices with their start and end apart: 6 -> 32, of which waited for: 6 -> 24; matrix products, arithmetic and copies ran while one was open for 0% -> 1% of each run, Pallas kernels for 0% -> 1%
where the time goes in v4:
time: 185 us; the launch traced here: 184 us
  waiting for transfers between devices  90.1 us (49%)
  starting transfers between devices  43.3 us (23%)
  Pallas kernels  23.5 us (13%)
  blocking collectives  14.6 us (8%)
  local copies, waits for them, and re-layouts  6.59 us (4%)
  other arithmetic  4.41 us (2%)
    ppermute x25, waiting for transfers between devices, swap(): return lax.ppermute(value, 'sub', [(i, i ^ far) for i in range(nsub)])  54.9 us
    ppermute x25, starting transfers between devices, swap(): return lax.ppermute(value, 'sub', [(i, i ^ far) for i in range(nsub)])  31.3 us
    all_to_all x2, waiting for transfers between devices, exchange(): lax.all_to_all(message, 'sub', split_axis=0, concat_axis=0, tiled=True)  28.7 us
    pallas_call x7, Pallas kernels, call(): pl.pallas_call(kernel, out_shape=tuple(out_shape) if several else out_sha...  23.5 us
    all_to_all x1, blocking collectives, exchange(): lax.all_to_all(message, 'sub', split_axis=0, concat_axis=0, tiled=True)  14.6 us
    all_to_all x2, starting transfers between devices, exchange(): lax.all_to_all(message, 'sub', split_axis=0, concat_axis=0, tiled=True)  12 us
    ppermute x5, waiting for transfers between devices, sibling(): lax.ppermute(value, 'body', [(i, nbody - 1 - i) for i in range(nbody)])  6.44 us
  transfers between devices with their start and end apart: 32, of which 24 were waited for; matrix products, arithmetic and copies ran while one was open for 1% of the time, Pallas kernels for 1%

profile of v4, /device:TPU:0, one launch (start us, length us, event | category | flops | bytes accessed | tf_op | source)
XLA Modules:
  0.0 184.1 jit_solution(3409057705890363253)
XLA Ops:
  4.9 8.3 %all-to-all-start = ((f32[16,3,8,128]{3,2,1,0:T(8,128)}), f32[16,3,8,128]{3,2,1,0:T(8,128)S(1)}, u32[]{:S(2)}, u32[]{:S(2)}) async-start(f32[16,3,8,128]{3,2,1,0:T(8,128)} %maximum_bitcast_fusion.1), calls=%async_computation | async-start | bytes 393216 | tf_op jit(solution)/shard_map/all_to_all | solution.py:199
  15.0 1.8 shard_map.73
  16.8 5.1 %all-to-all-done = f32[16,3,8,128]{3,2,1,0:T(8,128)S(1)} async-done(((f32[16,3,8,128]{3,2,1,0:T(8,128)}), f32[16,3,8,128]{3,2,1,0:T(8,128)S(1)}, u32[]{:S(2)}, u32[]{:S(2)}) %all-to-all-start) | async-done | bytes 196640 | tf_op jit(solution)/shard_map/all_to_all | solution.py:199
  21.9 3.7 %all-to-all-start.1 = ((f32[256,8,128]{2,1,0:T(8,128)}), f32[256,8,128]{2,1,0:T(8,128)S(1)}, u32[]{:S(2)}, u32[]{:S(2)}) async-start(f32[256,8,128]{2,1,0:T(8,128)} %shard_map.73), calls=%async_computation.1 | async-start | bytes 2097152 | tf_op jit(solution)/shard_map/all_to_all | solution.py:199
  25.7 23.6 %all-to-all-done.1 = f32[256,8,128]{2,1,0:T(8,128)S(1)} async-done(((f32[256,8,128]{2,1,0:T(8,128)}), f32[256,8,128]{2,1,0:T(8,128)S(1)}, u32[]{:S(2)}, u32[]{:S(2)}) %all-to-all-start.1) | async-done | bytes 1048608 | tf_op jit(solution)/shard_map/all_to_all | solution.py:199
  49.3 3.4 %copy-done = bf16[1,1,2048,2048]{3,2,1,0:T(8,128)(2,1)S(1)} copy-done((bf16[1,1,2048,2048]{3,2,1,0:T(8,128)(2,1)S(1)}, bf16[1,1,2048,2048]{3,2,1,0:T(8,128)(2,1)}, u32[]{:S(2)}) %copy-start) | copy-done | bytes 8388632
  52.7 2.6 %shard_map.74.own = f32[17,8,128]{2,1,0:T(8,128)S(1)} custom-call(s32[2,128]{1,0:T(2,128)S(1)} %slice_convert_fusion.place, f32[128,2,128]{2,1,0:T(2,128)S(1)} %bitcast.91, f32[128,2,8,128]{3,2,1,0:T(8,128)S(1)} %bitcast.89, bf16[2048,2048]{1,0:T(8,128)(2,1)S(1)} %bitcast.88), custom_call_target="tpu_custom_call" | custom-call | tf_op jit(solution)/shard_map/pallas_call | solution.py:24
  56.6 3.0 %collective-permute-start.3 = (f32[17,8,128]{2,1,0:T(8,128)S(1)}, f32[17,8,128]{2,1,0:T(8,128)S(1)}, u32[]{:S(2)}, u32[]{:S(2)}) collective-permute-start(f32[17,8,128]{2,1,0:T(8,128)S(1)} %pad_maximum_fusion.6), channel_id=1, source_target_pairs={{0,12},{1,13},{2,14},{3,15},{4,8},{5,9},{6,10},{7,11},{8,4},{9,5},... | collective-permute-start | bytes 208904 | tf_op jit(solution)/shard_map/ppermute | solution.py:202
  61.0 4.2 %collective-permute-done.1 = f32[17,8,128]{2,1,0:T(8,128)S(1)} collective-permute-done((f32[17,8,128]{2,1,0:T(8,128)S(1)}, f32[17,8,128]{2,1,0:T(8,128)S(1)}, u32[]{:S(2)}, u32[]{:S(2)}) %collective-permute-start.1) | collective-permute-done | bytes 69664 | tf_op jit(solution)/shard_map/ppermute | solution.py:202
  65.3 1.9 %collective-permute-done.2 = f32[17,8,128]{2,1,0:T(8,128)S(1)} collective-permute-done((f32[17,8,128]{2,1,0:T(8,128)S(1)}, f32[17,8,128]{2,1,0:T(8,128)S(1)}, u32[]{:S(2)}, u32[]{:S(2)}) %collective-permute-start.2) | collective-permute-done | bytes 69664 | tf_op jit(solution)/shard_map/ppermute | solution.py:202
  67.2 2.0 %collective-permute-start.6 = (f32[36,8,128]{2,1,0:T(8,128)S(1)}, f32[36,8,128]{2,1,0:T(8,128)S(1)}, u32[]{:S(2)}, u32[]{:S(2)}) collective-permute-start(f32[36,8,128]{2,1,0:T(8,128)S(1)} %pad_maximum_fusion), channel_id=1, source_target_pairs={{0,2},{1,3},{2,0},{3,1},{4,6},{5,7},{6,4},{7,5},{8,10},{9,11},{10,... | collective-permute-start | bytes 442376 | tf_op jit(solution)/shard_map/ppermute | solution.py:202
  69.8 3.3 %collective-permute-done.6 = f32[36,8,128]{2,1,0:T(8,128)S(1)} collective-permute-done((f32[36,8,128]{2,1,0:T(8,128)S(1)}, f32[36,8,128]{2,1,0:T(8,128)S(1)}, u32[]{:S(2)}, u32[]{:S(2)}) %collective-permute-start.6) | collective-permute-done | bytes 147488 | tf_op jit(solution)/shard_map/ppermute | solution.py:202
  75.4 5.9 %collective-permute-done.5.far_a = f32[64,8,128]{2,1,0:T(8,128)S(1)} collective-permute-done((f32[64,8,128]{2,1,0:T(8,128)S(1)}, f32[64,8,128]{2,1,0:T(8,128)S(1)}, u32[]{:S(2)}, u32[]{:S(2)}) %collective-permute-start.5) | collective-permute-done | bytes 262176 | tf_op jit(solution)/shard_map/ppermute | solution.py:202
  81.3 5.8 %shard_map.75 = (f32[128,2,8,128]{3,2,1,0:T(8,128)S(1)}, f32[128,2,8,128]{3,2,1,0:T(8,128)S(1)}, f32[128,2,8,128]{3,2,1,0:T(8,128)S(1)}, f32[128,2,8,128]{3,2,1,...) custom-call(s32[2,128]{1,0:T(2,128)S(1)} %slice_convert_fusion.place, f32[128]{0:T(128)S(1)} %slice_bitcast_fusion.2.keep, ...), custom_call_target="tpu_custom_call" | custom-call | tf_op jit(solution)/shard_map/pallas_call | solution.py:24
  88.4 2.3 %collective-permute-start.11 = (f32[17,8,128]{2,1,0:T(8,128)S(1)}, f32[17,8,128]{2,1,0:T(8,128)S(1)}, u32[]{:S(2)}, u32[]{:S(2)}) collective-permute-start(f32[17,8,128]{2,1,0:T(8,128)S(1)} %pad_maximum_fusion.7), channel_id=1, source_target_pairs={{0,12},{1,13},{2,14},{3,15},{4,8},{5,9},{6,10},{7,11},{8,4},{9,5},... | collective-permute-start | bytes 208904 | tf_op jit(solution)/shard_map/ppermute | solution.py:202
  90.8 2.1 %collective-permute-start.9 = (f32[17,8,128]{2,1,0:T(8,128)S(1)}, f32[17,8,128]{2,1,0:T(8,128)S(1)}, u32[]{:S(2)}, u32[]{:S(2)}) collective-permute-start(f32[17,8,128]{2,1,0:T(8,128)S(1)} %pad_maximum_fusion.7), channel_id=1, source_target_pairs={{0,4},{1,5},{2,6},{3,7},{4,0},{5,1},{6,2},{7,3},{8,12},{9,13},{10,... | collective-permute-start | bytes 208904 | tf_op jit(solution)/shard_map/ppermute | solution.py:202
  92.9 3.8 %collective-permute-done.9 = f32[17,8,128]{2,1,0:T(8,128)S(1)} collective-permute-done((f32[17,8,128]{2,1,0:T(8,128)S(1)}, f32[17,8,128]{2,1,0:T(8,128)S(1)}, u32[]{:S(2)}, u32[]{:S(2)}) %collective-permute-start.9) | collective-permute-done | bytes 69664 | tf_op jit(solution)/shard_map/ppermute | solution.py:202
  97.6 1.5 collective-permute-start.14
  100.4 3.0 %collective-permute-done.14 = f32[36,8,128]{2,1,0:T(8,128)S(1)} collective-permute-done((f32[36,8,128]{2,1,0:T(8,128)S(1)}, f32[36,8,128]{2,1,0:T(8,128)S(1)}, u32[]{:S(2)}, u32[]{:S(2)}) %collective-permute-start.14) | collective-permute-done | bytes 147488 | tf_op jit(solution)/shard_map/ppermute | solution.py:202
  106.2 5.6 %collective-permute-done.13.far_a = f32[64,8,128]{2,1,0:T(8,128)S(1)} collective-permute-done((f32[64,8,128]{2,1,0:T(8,128)S(1)}, f32[64,8,128]{2,1,0:T(8,128)S(1)}, u32[]{:S(2)}, u32[]{:S(2)}) %collective-permute-start.13) | collective-permute-done | bytes 262176 | tf_op jit(solution)/shard_map/ppermute | solution.py:202
  111.8 6.0 %shard_map.76 = (f32[128,2,8,128]{3,2,1,0:T(8,128)S(1)}, f32[128,2,8,128]{3,2,1,0:T(8,128)S(1)}, f32[128,2,8,128]{3,2,1,0:T(8,128)S(1)}, f32[128,2,8,128]{3,2,1,...) custom-call(s32[2,128]{1,0:T(2,128)S(1)} %slice_convert_fusion.place, f32[128]{0:T(128)S(1)} %slice_bitcast_fusion.2.keep, ...), custom_call_target="tpu_custom_call" | custom-call | tf_op jit(solution)/shard_map/pallas_call | solution.py:24
  119.1 2.1 %collective-permute-start.19 = (f32[17,8,128]{2,1,0:T(8,128)S(1)}, f32[17,8,128]{2,1,0:T(8,128)S(1)}, u32[]{:S(2)}, u32[]{:S(2)}) collective-permute-start(f32[17,8,128]{2,1,0:T(8,128)S(1)} %pad_maximum_fusion.8), channel_id=1, source_target_pairs={{0,12},{1,13},{2,14},{3,15},{4,8},{5,9},{6,10},{7,11},{8,4},{9,5},... | collective-permute-start | bytes 208904 | tf_op jit(solution)/shard_map/ppermute | solution.py:202
  121.2 2.4 %collective-permute-start.17 = (f32[17,8,128]{2,1,0:T(8,128)S(1)}, f32[17,8,128]{2,1,0:T(8,128)S(1)}, u32[]{:S(2)}, u32[]{:S(2)}) collective-permute-start(f32[17,8,128]{2,1,0:T(8,128)S(1)} %pad_maximum_fusion.8), channel_id=1, source_target_pairs={{0,4},{1,5},{2,6},{3,7},{4,0},{5,1},{6,2},{7,3},{8,12},{9,13},{10,... | collective-permute-start | bytes 208904 | tf_op jit(solution)/shard_map/ppermute | solution.py:202
  123.6 3.9 %collective-permute-done.17 = f32[17,8,128]{2,1,0:T(8,128)S(1)} collective-permute-done((f32[17,8,128]{2,1,0:T(8,128)S(1)}, f32[17,8,128]{2,1,0:T(8,128)S(1)}, u32[]{:S(2)}, u32[]{:S(2)}) %collective-permute-start.17) | collective-permute-done | bytes 69664 | tf_op jit(solution)/shard_map/ppermute | solution.py:202
  130.7 3.3 %collective-permute-done.22 = f32[36,8,128]{2,1,0:T(8,128)S(1)} collective-permute-done((f32[36,8,128]{2,1,0:T(8,128)S(1)}, f32[36,8,128]{2,1,0:T(8,128)S(1)}, u32[]{:S(2)}, u32[]{:S(2)}) %collective-permute-start.22) | collective-permute-done | bytes 147488 | tf_op jit(solution)/shard_map/ppermute | solution.py:202
  136.6 5.7 %collective-permute-done.21.far_a = f32[64,8,128]{2,1,0:T(8,128)S(1)} collective-permute-done((f32[64,8,128]{2,1,0:T(8,128)S(1)}, f32[64,8,128]{2,1,0:T(8,128)S(1)}, u32[]{:S(2)}, u32[]{:S(2)}) %collective-permute-start.21) | collective-permute-done | bytes 262176 | tf_op jit(solution)/shard_map/ppermute | solution.py:202
  142.3 6.0 %shard_map.77 = (f32[128,2,8,128]{3,2,1,0:T(8,128)S(1)}, f32[128,2,8,128]{3,2,1,0:T(8,128)S(1)}, f32[128,2,8,128]{3,2,1,0:T(8,128)S(1)}, f32[128,2,8,128]{3,2,1,...) custom-call(s32[2,128]{1,0:T(2,128)S(1)} %slice_convert_fusion.place, f32[128]{0:T(128)S(1)} %slice_bitcast_fusion.2.keep, ...), custom_call_target="tpu_custom_call" | custom-call | tf_op jit(solution)/shard_map/pallas_call | solution.py:24
  150.6 2.5 %collective-permute-done.25 = f32[8,128]{1,0:T(8,128)S(1)} collective-permute-done((f32[8,128]{1,0:T(8,128)S(1)}, f32[8,128]{1,0:T(8,128)S(1)}, u32[]{:S(2)}, u32[]{:S(2)}) %collective-permute-start.25) | collective-permute-done | bytes 4128 | tf_op jit(solution)/shard_map/ppermute | solution.py:202
  154.5 2.2 %collective-permute-done.26 = f32[8,128]{1,0:T(8,128)S(1)} collective-permute-done((f32[8,128]{1,0:T(8,128)S(1)}, f32[8,128]{1,0:T(8,128)S(1)}, u32[]{:S(2)}, u32[]{:S(2)}) %collective-permute-start.26) | collective-permute-done | bytes 4128 | tf_op jit(solution)/shard_map/ppermute | solution.py:202
  156.7 3.6 %collective-permute-done.27 = f32[8,128]{1,0:T(8,128)S(1)} collective-permute-done((f32[8,128]{1,0:T(8,128)S(1)}, f32[8,128]{1,0:T(8,128)S(1)}, u32[]{:S(2)}, u32[]{:S(2)}) %collective-permute-start.27) | collective-permute-done | bytes 4128 | tf_op jit(solution)/shard_map/ppermute | solution.py:202
  161.1 3.7 %collective-permute-done.28 = f32[8,128]{1,0:T(8,128)S(1)} collective-permute-done((f32[8,128]{1,0:T(8,128)S(1)}, f32[8,128]{1,0:T(8,128)S(1)}, u32[]{:S(2)}, u32[]{:S(2)}) %collective-permute-start.28) | collective-permute-done | bytes 4128 | tf_op jit(solution)/shard_map/ppermute | solution.py:202
  165.5 14.6 %all_to_all.15.recv = f32[128,8,128]{2,1,0:T(8,128)S(1)} all-to-all(f32[128,8,128]{2,1,0:T(8,128)S(1)} %shard_map.78), channel_id=1, replica_groups=mesh['body'=2,'sub'=16] {'sub'}, dimensions={0} | all-to-all | bytes 1048576 | tf_op jit(solution)/shard_map/all_to_all | solution.py:199
  (125 shorter events, 34.7 us)
Async XLA Ops:
  4.9 17.0 %all-to-all-start = ((f32[16,3,8,128]{3,2,1,0:T(8,128)}), f32[16,3,8,128]{3,2,1,0:T(8,128)S(1)}, u32[]{:S(2)}, u32[]{:S(2)}) async-start(f32[16,3,8,128]{3,2,1,0:T(8,128)} %maximum_bitcast_fusion.1), calls=%async_computation | async-start | bytes 393216 | tf_op jit(solution)/shard_map/all_to_all | solution.py:199
  21.9 27.4 %all-to-all-start.1 = ((f32[256,8,128]{2,1,0:T(8,128)}), f32[256,8,128]{2,1,0:T(8,128)S(1)}, u32[]{:S(2)}, u32[]{:S(2)}) async-start(f32[256,8,128]{2,1,0:T(8,128)} %shard_map.73), calls=%async_computation.1 | async-start | bytes 2097152 | tf_op jit(solution)/shard_map/all_to_all | solution.py:199
  55.3 1.3 collective-permute-start
  56.6 10.6 %collective-permute-start.3 = (f32[17,8,128]{2,1,0:T(8,128)S(1)}, f32[17,8,128]{2,1,0:T(8,128)S(1)}, u32[]{:S(2)}, u32[]{:S(2)}) collective-permute-start(f32[17,8,128]{2,1,0:T(8,128)S(1)} %pad_maximum_fusion.6), channel_id=1, source_target_pairs={{0,12},{1,13},{2,14},{3,15},{4,8},{5,9},{6,10},{7,11},{8,4},{9,5},... | collective-permute-start | bytes 208904 | tf_op jit(solution)/shard_map/ppermute | solution.py:202
  59.5 7.6 %collective-permute-start.2 = (f32[17,8,128]{2,1,0:T(8,128)S(1)}, f32[17,8,128]{2,1,0:T(8,128)S(1)}, u32[]{:S(2)}, u32[]{:S(2)}) collective-permute-start(f32[17,8,128]{2,1,0:T(8,128)S(1)} %pad_maximum_fusion.6), channel_id=1, source_target_pairs={{0,8},{1,9},{2,10},{3,11},{4,12},{5,13},{6,14},{7,15},{8,0},{9,1},... | collective-permute-start | bytes 208904 | tf_op jit(solution)/shard_map/ppermute | solution.py:202
  61.0 4.3 %collective-permute-start.1 = (f32[17,8,128]{2,1,0:T(8,128)S(1)}, f32[17,8,128]{2,1,0:T(8,128)S(1)}, u32[]{:S(2)}, u32[]{:S(2)}) collective-permute-start(f32[17,8,128]{2,1,0:T(8,128)S(1)} %pad_maximum_fusion.6), channel_id=1, source_target_pairs={{0,4},{1,5},{2,6},{3,7},{4,0},{5,1},{6,2},{7,3},{8,12},{9,13},{10,... | collective-permute-start | bytes 208904 | tf_op jit(solution)/shard_map/ppermute | solution.py:202
  67.2 5.9 %collective-permute-start.6 = (f32[36,8,128]{2,1,0:T(8,128)S(1)}, f32[36,8,128]{2,1,0:T(8,128)S(1)}, u32[]{:S(2)}, u32[]{:S(2)}) collective-permute-start(f32[36,8,128]{2,1,0:T(8,128)S(1)} %pad_maximum_fusion), channel_id=1, source_target_pairs={{0,2},{1,3},{2,0},{3,1},{4,6},{5,7},{6,4},{7,5},{8,10},{9,11},{10,... | collective-permute-start | bytes 442376 | tf_op jit(solution)/shard_map/ppermute | solution.py:202
  69.2 5.1 %collective-permute-start.4 = (f32[32,8,128]{2,1,0:T(8,128)S(1)}, f32[32,8,128]{2,1,0:T(8,128)S(1)}, u32[]{:S(2)}, u32[]{:S(2)}) collective-permute-start(f32[32,8,128]{2,1,0:T(8,128)S(1)} %pad_maximum_fusion.3), channel_id=1, source_target_pairs={{0,1},{1,0},{2,3},{3,2},{4,5},{5,4},{6,7},{7,6},{8,9},{9,8},{10,11... | collective-permute-start | bytes 393224 | tf_op jit(solution)/shard_map/ppermute | solution.py:202
  73.1 8.2 %collective-permute-start.7 = (f32[72,8,128]{2,1,0:T(8,128)S(1)}, f32[72,8,128]{2,1,0:T(8,128)S(1)}, u32[]{:S(2)}, u32[]{:S(2)}) collective-permute-start(f32[72,8,128]{2,1,0:T(8,128)S(1)} %constant_dynamic-update-slice_fusion.5.near_b), channel_id=1, source_target_pairs={{0,1},{1,0},{2,3},{3,2},{4,5},{5,4},{6,7},{7,6},{8,9},{9,8},{10,11... | collective-permute-start | bytes 884744 | tf_op jit(solution)/shard_map/ppermute | solution.py:202
  74.3 7.0 %collective-permute-start.5 = (f32[64,8,128]{2,1,0:T(8,128)S(1)}, f32[64,8,128]{2,1,0:T(8,128)S(1)}, u32[]{:S(2)}, u32[]{:S(2)}) collective-permute-start(f32[64,8,128]{2,1,0:T(8,128)S(1)} %constant_dynamic-update-slice_fusion.near_a), channel_id=1, source_target_pairs={{0,2},{1,3},{2,0},{3,1},{4,6},{5,7},{6,4},{7,5},{8,10},{9,11},{10,... | collective-permute-start | bytes 786440 | tf_op jit(solution)/shard_map/ppermute | solution.py:202
  87.1 1.3 collective-permute-start.8
  88.4 9.1 %collective-permute-start.11 = (f32[17,8,128]{2,1,0:T(8,128)S(1)}, f32[17,8,128]{2,1,0:T(8,128)S(1)}, u32[]{:S(2)}, u32[]{:S(2)}) collective-permute-start(f32[17,8,128]{2,1,0:T(8,128)S(1)} %pad_maximum_fusion.7), channel_id=1, source_target_pairs={{0,12},{1,13},{2,14},{3,15},{4,8},{5,9},{6,10},{7,11},{8,4},{9,5},... | collective-permute-start | bytes 208904 | tf_op jit(solution)/shard_map/ppermute | solution.py:202
  90.7 6.8 %collective-permute-start.10 = (f32[17,8,128]{2,1,0:T(8,128)S(1)}, f32[17,8,128]{2,1,0:T(8,128)S(1)}, u32[]{:S(2)}, u32[]{:S(2)}) collective-permute-start(f32[17,8,128]{2,1,0:T(8,128)S(1)} %pad_maximum_fusion.7), channel_id=1, source_target_pairs={{0,8},{1,9},{2,10},{3,11},{4,12},{5,13},{6,14},{7,15},{8,0},{9,1},... | collective-permute-start | bytes 208904 | tf_op jit(solution)/shard_map/ppermute | solution.py:202
  90.8 5.9 %collective-permute-start.9 = (f32[17,8,128]{2,1,0:T(8,128)S(1)}, f32[17,8,128]{2,1,0:T(8,128)S(1)}, u32[]{:S(2)}, u32[]{:S(2)}) collective-permute-start(f32[17,8,128]{2,1,0:T(8,128)S(1)} %pad_maximum_fusion.7), channel_id=1, source_target_pairs={{0,4},{1,5},{2,6},{3,7},{4,0},{5,1},{6,2},{7,3},{8,12},{9,13},{10,... | collective-permute-start | bytes 208904 | tf_op jit(solution)/shard_map/ppermute | solution.py:202
  97.6 5.8 %collective-permute-start.14 = (f32[36,8,128]{2,1,0:T(8,128)S(1)}, f32[36,8,128]{2,1,0:T(8,128)S(1)}, u32[]{:S(2)}, u32[]{:S(2)}) collective-permute-start(f32[36,8,128]{2,1,0:T(8,128)S(1)} %pad_maximum_fusion.1), channel_id=1, source_target_pairs={{0,2},{1,3},{2,0},{3,1},{4,6},{5,7},{6,4},{7,5},{8,10},{9,11},{10,... | collective-permute-start | bytes 442376 | tf_op jit(solution)/shard_map/ppermute | solution.py:202
  99.1 5.5 %collective-permute-start.12 = (f32[32,8,128]{2,1,0:T(8,128)S(1)}, f32[32,8,128]{2,1,0:T(8,128)S(1)}, u32[]{:S(2)}, u32[]{:S(2)}) collective-permute-start(f32[32,8,128]{2,1,0:T(8,128)S(1)} %pad_maximum_fusion.4), channel_id=1, source_target_pairs={{0,1},{1,0},{2,3},{3,2},{4,5},{5,4},{6,7},{7,6},{8,9},{9,8},{10,11... | collective-permute-start | bytes 393224 | tf_op jit(solution)/shard_map/ppermute | solution.py:202
  103.4 8.4 %collective-permute-start.15 = (f32[72,8,128]{2,1,0:T(8,128)S(1)}, f32[72,8,128]{2,1,0:T(8,128)S(1)}, u32[]{:S(2)}, u32[]{:S(2)}) collective-permute-start(f32[72,8,128]{2,1,0:T(8,128)S(1)} %constant_dynamic-update-slice_fusion.15.near_b), channel_id=1, source_target_pairs={{0,1},{1,0},{2,3},{3,2},{4,5},{5,4},{6,7},{7,6},{8,9},{9,8},{10,11... | collective-permute-start | bytes 884744 | tf_op jit(solution)/shard_map/ppermute | solution.py:202
  104.6 7.2 %collective-permute-start.13 = (f32[64,8,128]{2,1,0:T(8,128)S(1)}, f32[64,8,128]{2,1,0:T(8,128)S(1)}, u32[]{:S(2)}, u32[]{:S(2)}) collective-permute-start(f32[64,8,128]{2,1,0:T(8,128)S(1)} %constant_dynamic-update-slice_fusion.10.near_a), channel_id=1, source_target_pairs={{0,2},{1,3},{2,0},{3,1},{4,6},{5,7},{6,4},{7,5},{8,10},{9,11},{10,... | collective-permute-start | bytes 786440 | tf_op jit(solution)/shard_map/ppermute | solution.py:202
  117.8 1.3 collective-permute-start.16
  119.1 9.1 %collective-permute-start.19 = (f32[17,8,128]{2,1,0:T(8,128)S(1)}, f32[17,8,128]{2,1,0:T(8,128)S(1)}, u32[]{:S(2)}, u32[]{:S(2)}) collective-permute-start(f32[17,8,128]{2,1,0:T(8,128)S(1)} %pad_maximum_fusion.8), channel_id=1, source_target_pairs={{0,12},{1,13},{2,14},{3,15},{4,8},{5,9},{6,10},{7,11},{8,4},{9,5},... | collective-permute-start | bytes 208904 | tf_op jit(solution)/shard_map/ppermute | solution.py:202
  121.2 7.0 %collective-permute-start.18 = (f32[17,8,128]{2,1,0:T(8,128)S(1)}, f32[17,8,128]{2,1,0:T(8,128)S(1)}, u32[]{:S(2)}, u32[]{:S(2)}) collective-permute-start(f32[17,8,128]{2,1,0:T(8,128)S(1)} %pad_maximum_fusion.8), channel_id=1, source_target_pairs={{0,8},{1,9},{2,10},{3,11},{4,12},{5,13},{6,14},{7,15},{8,0},{9,1},... | collective-permute-start | bytes 208904 | tf_op jit(solution)/shard_map/ppermute | solution.py:202
  121.2 6.2 %collective-permute-start.17 = (f32[17,8,128]{2,1,0:T(8,128)S(1)}, f32[17,8,128]{2,1,0:T(8,128)S(1)}, u32[]{:S(2)}, u32[]{:S(2)}) collective-permute-start(f32[17,8,128]{2,1,0:T(8,128)S(1)} %pad_maximum_fusion.8), channel_id=1, source_target_pairs={{0,4},{1,5},{2,6},{3,7},{4,0},{5,1},{6,2},{7,3},{8,12},{9,13},{10,... | collective-permute-start | bytes 208904 | tf_op jit(solution)/shard_map/ppermute | solution.py:202
  128.3 5.8 %collective-permute-start.22 = (f32[36,8,128]{2,1,0:T(8,128)S(1)}, f32[36,8,128]{2,1,0:T(8,128)S(1)}, u32[]{:S(2)}, u32[]{:S(2)}) collective-permute-start(f32[36,8,128]{2,1,0:T(8,128)S(1)} %pad_maximum_fusion.2), channel_id=1, source_target_pairs={{0,2},{1,3},{2,0},{3,1},{4,6},{5,7},{6,4},{7,5},{8,10},{9,11},{10,... | collective-permute-start | bytes 442376 | tf_op jit(solution)/shard_map/ppermute | solution.py:202
  129.8 5.3 %collective-permute-start.20 = (f32[32,8,128]{2,1,0:T(8,128)S(1)}, f32[32,8,128]{2,1,0:T(8,128)S(1)}, u32[]{:S(2)}, u32[]{:S(2)}) collective-permute-start(f32[32,8,128]{2,1,0:T(8,128)S(1)} %pad_maximum_fusion.5), channel_id=1, source_target_pairs={{0,1},{1,0},{2,3},{3,2},{4,5},{5,4},{6,7},{7,6},{8,9},{9,8},{10,11... | collective-permute-start | bytes 393224 | tf_op jit(solution)/shard_map/ppermute | solution.py:202
  134.1 8.2 %collective-permute-start.23 = (f32[72,8,128]{2,1,0:T(8,128)S(1)}, f32[72,8,128]{2,1,0:T(8,128)S(1)}, u32[]{:S(2)}, u32[]{:S(2)}) collective-permute-start(f32[72,8,128]{2,1,0:T(8,128)S(1)} %constant_dynamic-update-slice_fusion.25.near_b), channel_id=1, source_target_pairs={{0,1},{1,0},{2,3},{3,2},{4,5},{5,4},{6,7},{7,6},{8,9},{9,8},{10,11... | collective-permute-start | bytes 884744 | tf_op jit(solution)/shard_map/ppermute | solution.py:202
  135.1 7.2 %collective-permute-start.21 = (f32[64,8,128]{2,1,0:T(8,128)S(1)}, f32[64,8,128]{2,1,0:T(8,128)S(1)}, u32[]{:S(2)}, u32[]{:S(2)}) collective-permute-start(f32[64,8,128]{2,1,0:T(8,128)S(1)} %constant_dynamic-update-slice_fusion.20.near_a), channel_id=1, source_target_pairs={{0,2},{1,3},{2,0},{3,1},{4,6},{5,7},{6,4},{7,5},{8,10},{9,11},{10,... | collective-permute-start | bytes 786440 | tf_op jit(solution)/shard_map/ppermute | solution.py:202
  148.3 1.2 collective-permute-start.24
  149.5 3.6 %collective-permute-start.25 = (f32[8,128]{1,0:T(8,128)S(1)}, f32[8,128]{1,0:T(8,128)S(1)}, u32[]{:S(2)}, u32[]{:S(2)}) collective-permute-start(f32[8,128]{1,0:T(8,128)S(1)} %fusion.19), channel_id=1, source_target_pairs={{0,1},{1,0},{2,3},{3,2},{4,5},{5,4},{6,7},{7,6},{8,9},{9,8},{10,11... | collective-permute-start | bytes 12296 | tf_op jit(solution)/shard_map/ppermute | solution.py:202
  153.1 3.6 %collective-permute-start.26 = (f32[8,128]{1,0:T(8,128)S(1)}, f32[8,128]{1,0:T(8,128)S(1)}, u32[]{:S(2)}, u32[]{:S(2)}) collective-permute-start(f32[8,128]{1,0:T(8,128)S(1)} %add.127), channel_id=1, source_target_pairs={{0,2},{1,3},{2,0},{3,1},{4,6},{5,7},{6,4},{7,5},{8,10},{9,11},{10,... | collective-permute-start | bytes 12296 | tf_op jit(solution)/shard_map/ppermute | solution.py:202
  156.7 3.6 %collective-permute-start.27 = (f32[8,128]{1,0:T(8,128)S(1)}, f32[8,128]{1,0:T(8,128)S(1)}, u32[]{:S(2)}, u32[]{:S(2)}) collective-permute-start(f32[8,128]{1,0:T(8,128)S(1)} %add.128), channel_id=1, source_target_pairs={{0,4},{1,5},{2,6},{3,7},{4,0},{5,1},{6,2},{7,3},{8,12},{9,13},{10,... | collective-permute-start | bytes 12296 | tf_op jit(solution)/shard_map/ppermute | solution.py:202
  160.3 4.5 %collective-permute-start.28 = (f32[8,128]{1,0:T(8,128)S(1)}, f32[8,128]{1,0:T(8,128)S(1)}, u32[]{:S(2)}, u32[]{:S(2)}) collective-permute-start(f32[8,128]{1,0:T(8,128)S(1)} %add.129), channel_id=1, source_target_pairs={{0,8},{1,9},{2,10},{3,11},{4,12},{5,13},{6,14},{7,15},{8,0},{9,1},... | collective-permute-start | bytes 12296 | tf_op jit(solution)/shard_map/ppermute | solution.py:202
  180.8 1.6 collective-permute-start.29
  (1 other events, 3.4 us)

commit v5 on v4

v5 whole, which is shorter than its diff:
```python
import functools

import jax
import jax.numpy as jnp
from jax import lax
from jax.experimental import pallas as pl
from jax.experimental.pallas import tpu as pltpu
from jax.sharding import PartitionSpec as P

ITERS = 4
LANES = 128
SUBLANES = 8
VMEM = pl.BlockSpec(memory_space=pltpu.VMEM)
SMEM = pl.BlockSpec(memory_space=pltpu.SMEM)
HBM = pl.BlockSpec(memory_space=pltpu.HBM)
PARAMS = pltpu.CompilerParams(vmem_limit_bytes=20 * 1024 * 1024)


def f32(*shape):
    return jax.ShapeDtypeStruct(shape, jnp.float32)


def call(kernel, out_shape, specs, *operands, scratch=()):
    several = isinstance(out_shape, (tuple, list))
    return pl.pallas_call(
        kernel,
        out_shape=tuple(out_shape) if several else out_shape,
        in_specs=specs,
        out_specs=(VMEM,) * len(out_shape) if several else VMEM,
        scratch_shapes=list(scratch),
        compiler_params=PARAMS,
    )(*operands)


def per_case(value):
    return jnp.sum(value, axis=1, keepdims=True)


def respond(block, load, gamma, energy, answer, copies=()):
    ntile, ncase, width = load.shape
    each = 2
    total = jnp.zeros((2 * ncase, ntile * width), jnp.float32)
    for j in range(ntile // each):
        value = jnp.concatenate([load[j * each + i] for i in range(each)], axis=1)
        high = value.astype(jnp.bfloat16)
        low = (value - high.astype(jnp.float32)).astype(jnp.bfloat16)
        if copies:
            copies[j].wait()
        total = total + jnp.dot(
            jnp.concatenate([high, low], axis=0),
            block[j * each * width : (j + 1) * each * width, :],
            preferred_element_type=jnp.float32,
        )
    total = total[:ncase] + total[ncase:]
    work = 0.5 * energy
    for i in range(ntile):
        tile = total[:, i * width : (i + 1) * width]
        answer[i] = tile
        work = work + load[i] * tile
    lane = lax.broadcasted_iota(jnp.int32, work.shape, 1)
    sums = jnp.where(lane == 0, per_case(0.5 * gamma), 0.0)
    answer[ntile] = jnp.where(lane == 1, per_case(work), sums)


def pack_kernel(nh, tiles, place, field, table, message):
    ndest = message.shape[0] // tiles
    extra = table.shape[1]
    message[...] = jnp.zeros_like(message)

    def body(p, carry):
        message[pl.ds(place[p], nh)] = field[p]
        return carry

    lax.fori_loop(0, field.shape[0], body, 0, unroll=4)
    for i in range(ndest):
        message[(i + 1) * tiles - extra : (i + 1) * tiles] = table[i]


def start_kernel(nh, room, tiles, place, comp, message, block, r_out, answer, load, held, sems):
    pieces = sems.shape[0]
    size = block.shape[0] // pieces
    copies = []
    for j in range(pieces):
        rows = pl.ds(j * size, size)
        copies.append(pltpu.make_async_copy(block.at[rows], held.at[rows], sems.at[j]))
        copies[-1].start()
    load[...] = jnp.zeros_like(load)
    nrow = r_out.shape[0]
    zero = jnp.zeros(r_out.shape[2:], jnp.float32)

    def pair(i, sums):
        gamma, energy = sums
        for j in range(room):
            row = i * room + j
            r = message[pl.ds(i * tiles + j * nh, nh)]
            r_out[row] = r
            load[pl.ds(place[0, row], nh)] += r
            c = comp[row]
            for h in range(nh):
                square = r[h] * r[h]
                gamma = gamma + square
                energy = energy + c[h : h + 1] * square
        return gamma, energy

    gamma, energy = lax.fori_loop(0, nrow // room, pair, (zero, zero))
    respond(held, load, gamma, energy, answer, copies)


def tree(values):
    while len(values) > 1:
        values = [a + b for a, b in zip(values[::2], values[1::2])]
    return values[0]


def steps(first, sums, known):
    gamma, delta = sums[:, 0:1], sums[:, 1:2]
    if first:
        return gamma, gamma / delta, jnp.zeros_like(gamma)
    beta = gamma / known[:, 0:1]
    return gamma, gamma / (delta - beta * gamma / known[:, 1:2]), beta


def home_kernel(first, nh, unroll, place, keep, picked, comp, own, near_a, far_a, near_b, far_b, known, block, *refs):
    if first:
        r_in, r, s, answer, part, known_out, load, resp = refs
    else:
        r_in, s_in, r, s, answer, part, known_out, load, resp = refs
    load[...] = jnp.zeros_like(load)
    ncase, width = r.shape[2:]
    at = 0
    for piece in (near_a, far_a, near_b, far_b):
        resp[at : at + piece.shape[0]] = piece[...]
        at += piece.shape[0]
    each = own.shape[0] // 2 + 1
    sums = tree([piece[i + each - 1] for piece in (near_b, far_b) for i in range(0, piece.shape[0], each)])
    gamma, alpha, beta = steps(first, sums, known[...])
    lane = lax.broadcasted_iota(jnp.int32, (ncase, width), 1)
    known_out[...] = jnp.where(lane == 0, gamma, jnp.where(lane == 1, alpha, beta))
    alpha = jnp.broadcast_to(alpha, (ncase, width))
    beta = jnp.broadcast_to(beta, (ncase, width))
    zero = jnp.zeros((ncase, width), jnp.float32)

    def pick(p, carry):
        part[p] = resp[pl.ds(picked[p], nh)]
        return carry

    lax.fori_loop(0, part.shape[0], pick, 0, unroll=8)

    def body(row, sums):
        gamma, energy = sums
        near, far, on = place[0, row], place[1, row], keep[row]
        c = comp[row]
        for h in range(nh):
            residual = r_in[row, h]
            image = on * (own[near + h] + resp[far + h] + c[h : h + 1] * residual)
            if not first:
                image = image + beta * s_in[row, h]
            residual = residual - alpha * image
            r[row, h], s[row, h] = residual, image
            load[near + h] += residual
            square = residual * residual
            gamma = gamma + square
            energy = energy + c[h : h + 1] * square
        return gamma, energy

    gamma, energy = lax.fori_loop(0, r.shape[0], body, (zero, zero), unroll=unroll)
    respond(block, load, gamma, energy, answer)


def on_device(rhs, compliance, plate_owner, found_owner, slot_pairs, active, inverse):
    nsub = lax.axis_size("sub")
    nbody = lax.axis_size("body")
    side = lax.axis_index("body")
    me = lax.axis_index("sub")
    ncase, npatch, gap = rhs.shape
    block = inverse[0, 0]
    nslot = block.shape[0] // gap
    nh = gap // LANES
    per = nslot * nh + 1
    room = max(2, 2 * npatch // nsub)
    nrow = nsub * room
    lines = -(-room * nh // SUBLANES)
    deep = -(-room // SUBLANES)
    tiles = room * nh + lines + deep
    nz = nsub // 4
    half = nslot // 2 * nh
    unroll = 4

    def exchange(message):
        return lax.all_to_all(message, "sub", split_axis=0, concat_axis=0, tiled=True)

    def swap(value, far):
        return lax.ppermute(value, "sub", [(i, i ^ far) for i in range(nsub)])

    def sibling(value):
        return lax.ppermute(value, "body", [(i, nbody - 1 - i) for i in range(nbody)])

    keep = active.astype(jnp.float32)
    owners = jnp.stack([plate_owner[:, 0], found_owner[:, 0]])
    slots = slot_pairs.T
    owner, other = jnp.where(side == 0, owners, owners[::-1])
    slot, other_slot = jnp.where(side == 0, slots, slots[::-1])
    index = jnp.arange(npatch, dtype=jnp.int32)
    earlier = (owner[None, :] == owner[:, None]) & (index[None, :] < index[:, None])
    rank = jnp.sum(earlier.astype(jnp.int32), axis=1)
    row = owner * room + rank
    place = owner * tiles + rank * nh

    def found(away):
        x_bit, y_bit, z_part = away & 1, (away >> 1) & 1, away >> 2
        found_a = ((y_bit * 2 + x_bit) * nz + z_part) * half + other_slot * nh
        found_b = ((x_bit * 2 + y_bit) * nz + z_part) * (half + 1) + (other_slot - nslot // 2) * nh
        return jnp.where(other_slot < nslot // 2, found_a, nsub * half + found_b)

    facts = jnp.stack([slot * nh, found(owner ^ other)], axis=1).astype(jnp.float32)
    facts = jnp.concatenate([facts, keep[:, None]], axis=1)
    facts = jnp.concatenate([compliance, jnp.pad(facts, ((0, 0), (0, LANES - 3)))], axis=1)
    placed = (row[None, :] == jnp.arange(nrow, dtype=jnp.int32)[:, None]).astype(jnp.float32)
    facts = jnp.dot(placed, facts, precision=lax.Precision.HIGHEST).reshape(nsub, room, gap + LANES)
    lined = facts[:, :, :gap].reshape(nsub, room * nh, LANES)
    lined = jnp.pad(lined, ((0, 0), (0, lines * SUBLANES - room * nh), (0, 0)))
    named = jnp.pad(facts[:, :, gap:], ((0, 0), (0, deep * SUBLANES - room), (0, 0)))
    table = jnp.concatenate([lined, named], axis=1).reshape(nsub, lines + deep, SUBLANES, LANES)
    start = keep[None, :, None] * rhs
    by_patch = jnp.transpose(start.reshape(ncase, npatch, nh, LANES), (1, 2, 0, 3))

    message = call(
        functools.partial(pack_kernel, nh, tiles),
        f32(nsub * tiles, ncase, LANES),
        [SMEM, VMEM, VMEM],
        place,
        by_patch,
        table,
    )
    message = exchange(message.reshape(nsub, tiles, ncase, LANES))
    told = message[:, room * nh :].reshape(nsub, (lines + deep) * SUBLANES, LANES)
    comp = told[:, : room * nh].reshape(nrow, nh, LANES)
    named = told[:, lines * SUBLANES : lines * SUBLANES + room, :3].reshape(nrow, 3).T
    home = named[:2].astype(jnp.int32)
    on = named[2]

    field = f32(nrow, nh, ncase, LANES)
    answer = f32(per, ncase, LANES)
    load = pltpu.VMEM((nslot * nh, ncase, LANES), jnp.float32)
    spread = pltpu.VMEM((nsub * per, ncase, LANES), jnp.float32)
    home_r, own = call(
        functools.partial(start_kernel, nh, room, tiles),
        (field, answer),
        [SMEM, VMEM, VMEM, HBM],
        home,
        comp,
        message.reshape(nsub * tiles, ncase, LANES),
        block,
        scratch=[load, pltpu.VMEM(block.shape, block.dtype), pltpu.SemaphoreType.DMA((nslot,))],
    )
    known = jnp.zeros((ncase, LANES), jnp.float32)
    state = [home_r]
    picked = found(me ^ other).astype(jnp.int32)
    r, d, x, s = start, None, None, None
    for step in range(ITERS - 1):
        far = sibling(own)
        far = jnp.concatenate([far[: per - 1], own[per - 1 :] + far[per - 1 :]])
        parts = [far] + [swap(far, 4 * z) for z in range(1, nz)]
        a = jnp.concatenate([part[:half] for part in parts])
        b = jnp.concatenate([part[half:] for part in parts])
        far_a, far_b = swap(a, 1), swap(b, 2)
        a, b = jnp.concatenate([a, far_a]), jnp.concatenate([b, far_b])
        far_a, far_b = swap(a, 2), swap(b, 1)
        *state, own, part, known = call(
            functools.partial(home_kernel, step == 0, nh, unroll),
            (field,) * 2 + (answer, f32(npatch, nh, ncase, LANES), f32(ncase, LANES)),
            [SMEM] * 3 + [VMEM] * (8 + len(state)),
            home,
            on,
            picked,
            comp,
            own,
            a,
            far_a,
            b,
            far_b,
            known,
            block,
            *state,
            scratch=[load, spread],
        )
        image = jnp.transpose(part + sibling(part), (2, 0, 1, 3)).reshape(ncase, npatch, gap)
        image = keep[None, :, None] * (image + compliance[None] * r)
        alpha, beta = known[:, 1].reshape(ncase, 1, 1), known[:, 2].reshape(ncase, 1, 1)
        if step == 0:
            d, s = r, image
            x = alpha * d
        else:
            d, s = r + beta * d, image + beta * s
            x = x + alpha * d
        r = r - alpha * s
    sums = own[per - 1]
    sums = sums + sibling(sums)
    sums = tree([sums] + [swap(sums, i) for i in range(1, 4)])
    sums = tree([sums] + [swap(sums, 4 * z) for z in range(1, nz)])
    _, alpha, beta = steps(False, sums, known)
    return x + alpha[:, :, None] * (r + beta[:, :, None] * d)


def solution(mesh):
    in_specs = (
        P(None, "sub", None),
        P("sub", None),
        P("sub", None),
        P("sub", None),
        P("sub", None),
        P("sub"),
        P("body", "sub", None, None),
    )
    out_specs = P(None, "sub", None)
    return jax.shard_map(
        on_device, mesh=mesh, in_specs=in_specs, out_specs=out_specs, check_vma=False
    )
```

time: 185 us -> 155 us (0.84)
  waiting for transfers between devices: 90.1 us -> 52.5 us
  blocking collectives: 14.6 us -> 39.4 us
  starting transfers between devices: 43.3 us -> 32.2 us
  Pallas kernels: 23.5 us -> 13.8 us
  local copies, waits for them, and re-layouts: 6.59 us -> 11.1 us
    all_to_all x2 -> x0, waiting for transfers between devices: 28.7 us -> none  [exchange(): lax.all_to_all(message, 'sub', split_axis=0, concat_axis=0, tiled=True)]
    all_to_all x1, blocking collectives: 14.6 us -> 39.4 us  [exchange(): lax.all_to_all(message, 'sub', split_axis=0, concat_axis=0, tiled=True)]
    all_to_all x2 -> x0, starting transfers between devices: 12 us -> none  [exchange(): lax.all_to_all(message, 'sub', split_axis=0, concat_axis=0, tiled=True)]
    pallas_call x7 -> x5, Pallas kernels: 23.5 us -> 13.8 us  [call(): pl.pallas_call(kernel, out_shape=tuple(out_shape) if several else out_sha...]
    ppermute x25 -> x27, waiting for transfers between devices: 54.9 us -> 48.7 us  [swap(): return lax.ppermute(value, 'sub', [(i, i ^ far) for i in range(nsub)])]
    unnamed x3 -> x9, local copies, waits for them, and re-layouts: 3.48 us -> 7.01 us
    ppermute x5 -> x7, waiting for transfers between devices: 6.44 us -> 3.77 us  [sibling(): lax.ppermute(value, 'body', [(i, nbody - 1 - i) for i in range(nbody)])]
    ppermute x25 -> x27, starting transfers between devices: 31.3 us -> 31.4 us  [swap(): return lax.ppermute(value, 'sub', [(i, i ^ far) for i in range(nsub)])]
  transfers between devices with their start and end apart: 32 -> 34, of which waited for: 24 -> 21; matrix products, arithmetic and copies ran while one was open for 1% -> 2% of each run, Pallas kernels for 1% -> 2%
where the time goes in v5:
time: 155 us
  waiting for transfers between devices  52.5 us (34%)
  blocking collectives  39.4 us (25%)
  starting transfers between devices  32.2 us (21%)
  Pallas kernels  13.8 us (9%)
  local copies, waits for them, and re-layouts  11.1 us (7%)
  other arithmetic  4.57 us (3%)
    ppermute x27, waiting for transfers between devices, swap(): return lax.ppermute(value, 'sub', [(i, i ^ far) for i in range(nsub)])  48.7 us
    all_to_all x1, blocking collectives, exchange(): lax.all_to_all(message, 'sub', split_axis=0, concat_axis=0, tiled=True)  39.4 us
    ppermute x27, starting transfers between devices, swap(): return lax.ppermute(value, 'sub', [(i, i ^ far) for i in range(nsub)])  31.4 us
    pallas_call x5, Pallas kernels, call(): pl.pallas_call(kernel, out_shape=tuple(out_shape) if several else out_sha...  13.8 us
    unnamed x9, local copies, waits for them, and re-layouts  7.01 us
    ppermute x7, waiting for transfers between devices, sibling(): lax.ppermute(value, 'body', [(i, nbody - 1 - i) for i in range(nbody)])  3.77 us
  transfers between devices with their start and end apart: 34, of which 21 were waited for; matrix products, arithmetic and copies ran while one was open for 2% of the time, Pallas kernels for 2%

profile of v5, /device:TPU:0, one launch (start us, length us, event | category | flops | bytes accessed | tf_op | source)
XLA Modules:
  0.0 155.1 jit_solution(10348348990264358347)
XLA Ops:
  5.8 39.4 %all_to_all.5 = f32[16,19,8,128]{3,2,1,0:T(8,128)S(1)} all-to-all(f32[16,19,8,128]{3,2,1,0:T(8,128)S(1)} %bitcast.133), channel_id=1, replica_groups=mesh['body'=2,'sub'=16] {'sub'}, dimensions={0} | all-to-all | bytes 2490368 | tf_op jit(solution)/shard_map/all_to_all | solution.py:190
  45.3 3.4 %copy-done = bf16[1,1,2048,2048]{3,2,1,0:T(8,128)(2,1)S(1)} copy-done((bf16[1,1,2048,2048]{3,2,1,0:T(8,128)(2,1)S(1)}, bf16[1,1,2048,2048]{3,2,1,0:T(8,128)(2,1)}, u32[]{:S(2)}) %copy-start) | copy-done | bytes 8388632
  48.7 3.4 %shard_map.74 = (f32[128,2,8,128]{3,2,1,0:T(8,128)S(1)}, f32[17,8,128]{2,1,0:T(8,128)S(1)}) custom-call(s32[2,128]{1,0:T(2,128)S(1)} %slice_convert_fusion.place, f32[128,2,128]{2,1,0:T(2,128)S(1)} %bitcast.134, f32[304,8,128]{2,1,0:T(8,128)S(1)} %bitcast.132, bf16[2048,2048]{1,0:T(8,128)(2,1)S(1)} %bitcast.128), custom_call_target="tpu_custom_call" | custom-call | tf_op jit(solution)/shard_map/pallas_call | solution.py:25
  52.2 1.2 collective-permute-done
  53.5 1.7 %collective-permute-start.3 = (f32[17,8,128]{2,1,0:T(8,128)S(1)}, f32[17,8,128]{2,1,0:T(8,128)S(1)}, u32[]{:S(2)}, u32[]{:S(2)}) collective-permute-start(f32[17,8,128]{2,1,0:T(8,128)S(1)} %pad_maximum_fusion.6), channel_id=1, source_target_pairs={{0,12},{1,13},{2,14},{3,15},{4,8},{5,9},{6,10},{7,11},{8,4},{9,5},... | collective-permute-start | bytes 208904 | tf_op jit(solution)/shard_map/ppermute | solution.py:193
  55.7 2.2 %collective-permute-start.1 = (f32[17,8,128]{2,1,0:T(8,128)S(1)}, f32[17,8,128]{2,1,0:T(8,128)S(1)}, u32[]{:S(2)}, u32[]{:S(2)}) collective-permute-start(f32[17,8,128]{2,1,0:T(8,128)S(1)} %pad_maximum_fusion.6), channel_id=1, source_target_pairs={{0,4},{1,5},{2,6},{3,7},{4,0},{5,1},{6,2},{7,3},{8,12},{9,13},{10,... | collective-permute-start | bytes 208904 | tf_op jit(solution)/shard_map/ppermute | solution.py:193
  57.9 3.9 %collective-permute-done.1 = f32[17,8,128]{2,1,0:T(8,128)S(1)} collective-permute-done((f32[17,8,128]{2,1,0:T(8,128)S(1)}, f32[17,8,128]{2,1,0:T(8,128)S(1)}, u32[]{:S(2)}, u32[]{:S(2)}) %collective-permute-start.1) | collective-permute-done | bytes 69664 | tf_op jit(solution)/shard_map/ppermute | solution.py:193
  64.0 4.4 %collective-permute-done.6 = f32[36,8,128]{2,1,0:T(8,128)S(1)} collective-permute-done((f32[36,8,128]{2,1,0:T(8,128)S(1)}, f32[36,8,128]{2,1,0:T(8,128)S(1)}, u32[]{:S(2)}, u32[]{:S(2)}) %collective-permute-start.6) | collective-permute-done | bytes 147488 | tf_op jit(solution)/shard_map/ppermute | solution.py:193
  70.0 6.4 %collective-permute-done.5.far_a = f32[64,8,128]{2,1,0:T(8,128)S(1)} collective-permute-done((f32[64,8,128]{2,1,0:T(8,128)S(1)}, f32[64,8,128]{2,1,0:T(8,128)S(1)}, u32[]{:S(2)}, u32[]{:S(2)}) %collective-permute-start.5) | collective-permute-done | bytes 262176 | tf_op jit(solution)/shard_map/ppermute | solution.py:193
  76.6 3.4 %copy-done.1 = bf16[1,1,2048,2048]{3,2,1,0:T(8,128)(2,1)S(1)} copy-done((bf16[1,1,2048,2048]{3,2,1,0:T(8,128)(2,1)S(1)}, bf16[1,1,2048,2048]{3,2,1,0:T(8,128)(2,1)}, u32[]{:S(2)}) %copy-start.1) | copy-done | bytes 8388632
  80.0 3.1 %shard_map.75 = (f32[128,2,8,128]{3,2,1,0:T(8,128)S(1)}, f32[128,2,8,128]{3,2,1,0:T(8,128)S(1)}, f32[17,8,128]{2,1,0:T(8,128)S(1)}, f32[64,2,8,128]{3,2,1,0:T(8,128)S(1)}, f32[8,128]{1,0:T(8,128)S(1)}) custom-call(s32[2,128]{1,0:T(2,128)S(1)} %slice_convert_fusion.place, f32[128]{0:T(128)S(1)} %slice_bitcast_fusion.3.keep, s32[64]{0:T(128)S(1)} %get-tuple-element.89.picked, ...), custom_call_target="tpu_custom_call" | custom-call | tf_op jit(solution)/shard_map/pallas_call | solution.py:25
  83.1 1.3 collective-permute-done.8
  84.4 1.7 %collective-permute-start.11 = (f32[17,8,128]{2,1,0:T(8,128)S(1)}, f32[17,8,128]{2,1,0:T(8,128)S(1)}, u32[]{:S(2)}, u32[]{:S(2)}) collective-permute-start(f32[17,8,128]{2,1,0:T(8,128)S(1)} %pad_maximum_fusion.7), channel_id=1, source_target_pairs={{0,12},{1,13},{2,14},{3,15},{4,8},{5,9},{6,10},{7,11},{8,4},{9,5},... | collective-permute-start | bytes 208904 | tf_op jit(solution)/shard_map/ppermute | solution.py:193
  86.0 2.8 %collective-permute-start.9 = (f32[17,8,128]{2,1,0:T(8,128)S(1)}, f32[17,8,128]{2,1,0:T(8,128)S(1)}, u32[]{:S(2)}, u32[]{:S(2)}) collective-permute-start(f32[17,8,128]{2,1,0:T(8,128)S(1)} %pad_maximum_fusion.7), channel_id=1, source_target_pairs={{0,4},{1,5},{2,6},{3,7},{4,0},{5,1},{6,2},{7,3},{8,12},{9,13},{10,... | collective-permute-start | bytes 208904 | tf_op jit(solution)/shard_map/ppermute | solution.py:193
  88.8 3.9 %collective-permute-done.9 = f32[17,8,128]{2,1,0:T(8,128)S(1)} collective-permute-done((f32[17,8,128]{2,1,0:T(8,128)S(1)}, f32[17,8,128]{2,1,0:T(8,128)S(1)}, u32[]{:S(2)}, u32[]{:S(2)}) %collective-permute-start.9) | collective-permute-done | bytes 69664 | tf_op jit(solution)/shard_map/ppermute | solution.py:193
  94.3 1.2 collective-permute-start.12
  95.5 3.9 %collective-permute-done.14 = f32[36,8,128]{2,1,0:T(8,128)S(1)} collective-permute-done((f32[36,8,128]{2,1,0:T(8,128)S(1)}, f32[36,8,128]{2,1,0:T(8,128)S(1)}, u32[]{:S(2)}, u32[]{:S(2)}) %collective-permute-start.14) | collective-permute-done | bytes 147488 | tf_op jit(solution)/shard_map/ppermute | solution.py:193
  101.3 6.4 %collective-permute-done.13.far_a = f32[64,8,128]{2,1,0:T(8,128)S(1)} collective-permute-done((f32[64,8,128]{2,1,0:T(8,128)S(1)}, f32[64,8,128]{2,1,0:T(8,128)S(1)}, u32[]{:S(2)}, u32[]{:S(2)}) %collective-permute-start.13) | collective-permute-done | bytes 262176 | tf_op jit(solution)/shard_map/ppermute | solution.py:193
  107.7 3.3 %shard_map.76 = (f32[128,2,8,128]{3,2,1,0:T(8,128)S(1)}, f32[128,2,8,128]{3,2,1,0:T(8,128)S(1)}, f32[17,8,128]{2,1,0:T(8,128)S(1)}, f32[64,2,8,128]{3,2,1,0:T(8,128)S(1)}, f32[8,128]{1,0:T(8,128)S(1)}) custom-call(s32[2,128]{1,0:T(2,128)S(1)} %slice_convert_fusion.place, f32[128]{0:T(128)S(1)} %slice_bitcast_fusion.3.keep, s32[64]{0:T(128)S(1)} %get-tuple-element.89.picked, ...), custom_call_target="tpu_custom_call" | custom-call | tf_op jit(solution)/shard_map/pallas_call | solution.py:25
  111.0 1.3 collective-permute-done.17
  112.3 1.6 %collective-permute-start.20 = (f32[17,8,128]{2,1,0:T(8,128)S(1)}, f32[17,8,128]{2,1,0:T(8,128)S(1)}, u32[]{:S(2)}, u32[]{:S(2)}) collective-permute-start(f32[17,8,128]{2,1,0:T(8,128)S(1)} %pad_maximum_fusion.8), channel_id=1, source_target_pairs={{0,12},{1,13},{2,14},{3,15},{4,8},{5,9},{6,10},{7,11},{8,4},{9,5},... | collective-permute-start | bytes 208904 | tf_op jit(solution)/shard_map/ppermute | solution.py:193
  113.9 2.8 %collective-permute-start.18 = (f32[17,8,128]{2,1,0:T(8,128)S(1)}, f32[17,8,128]{2,1,0:T(8,128)S(1)}, u32[]{:S(2)}, u32[]{:S(2)}) collective-permute-start(f32[17,8,128]{2,1,0:T(8,128)S(1)} %pad_maximum_fusion.8), channel_id=1, source_target_pairs={{0,4},{1,5},{2,6},{3,7},{4,0},{5,1},{6,2},{7,3},{8,12},{9,13},{10,... | collective-permute-start | bytes 208904 | tf_op jit(solution)/shard_map/ppermute | solution.py:193
  116.8 3.9 %collective-permute-done.18 = f32[17,8,128]{2,1,0:T(8,128)S(1)} collective-permute-done((f32[17,8,128]{2,1,0:T(8,128)S(1)}, f32[17,8,128]{2,1,0:T(8,128)S(1)}, u32[]{:S(2)}, u32[]{:S(2)}) %collective-permute-start.18) | collective-permute-done | bytes 69664 | tf_op jit(solution)/shard_map/ppermute | solution.py:193
  123.2 4.1 %collective-permute-done.23 = f32[36,8,128]{2,1,0:T(8,128)S(1)} collective-permute-done((f32[36,8,128]{2,1,0:T(8,128)S(1)}, f32[36,8,128]{2,1,0:T(8,128)S(1)}, u32[]{:S(2)}, u32[]{:S(2)}) %collective-permute-start.23) | collective-permute-done | bytes 147488 | tf_op jit(solution)/shard_map/ppermute | solution.py:193
  129.2 6.2 %collective-permute-done.22.far_a = f32[64,8,128]{2,1,0:T(8,128)S(1)} collective-permute-done((f32[64,8,128]{2,1,0:T(8,128)S(1)}, f32[64,8,128]{2,1,0:T(8,128)S(1)}, u32[]{:S(2)}, u32[]{:S(2)}) %collective-permute-start.22) | collective-permute-done | bytes 262176 | tf_op jit(solution)/shard_map/ppermute | solution.py:193
  135.4 3.4 %shard_map.77 = (f32[128,2,8,128]{3,2,1,0:T(8,128)}, f32[128,2,8,128]{3,2,1,0:T(8,128)}, f32[17,8,128]{2,1,0:T(8,128)S(1)}, f32[64,2,8,128]{3,2,1,0:T(8,128)S(1)}, f32[8,128]{1,0:T(8,128)S(1)}) custom-call(s32[2,128]{1,0:T(2,128)S(1)} %slice_convert_fusion.place, f32[128]{0:T(128)S(1)} %slice_bitcast_fusion.3.keep, s32[64]{0:T(128)S(1)} %get-tuple-element.89.picked, ...), custom_call_target="tpu_custom_call" | custom-call | tf_op jit(solution)/shard_map/pallas_call | solution.py:25
  140.1 1.2 collective-permute-start.29
  141.4 1.3 collective-permute-start.28
  145.0 1.3 collective-permute-done.27
  146.3 1.5 collective-permute-start.32
  147.9 2.9 %collective-permute-start.30 = (f32[8,128]{1,0:T(8,128)S(1)}, f32[8,128]{1,0:T(8,128)S(1)}, u32[]{:S(2)}, u32[]{:S(2)}) collective-permute-start(f32[8,128]{1,0:T(8,128)S(1)} %add_add_fusion.1), channel_id=1, source_target_pairs={{0,4},{1,5},{2,6},{3,7},{4,0},{5,1},{6,2},{7,3},{8,12},{9,13},{10,... | collective-permute-start | bytes 12296 | tf_op jit(solution)/shard_map/ppermute | solution.py:193
  153.5 1.5 multiply_add_fusion
  (141 shorter events, 24.7 us)
Async XLA Ops:
  52.1 1.3 collective-permute-start
  53.5 9.1 %collective-permute-start.3 = (f32[17,8,128]{2,1,0:T(8,128)S(1)}, f32[17,8,128]{2,1,0:T(8,128)S(1)}, u32[]{:S(2)}, u32[]{:S(2)}) collective-permute-start(f32[17,8,128]{2,1,0:T(8,128)S(1)} %pad_maximum_fusion.6), channel_id=1, source_target_pairs={{0,12},{1,13},{2,14},{3,15},{4,8},{5,9},{6,10},{7,11},{8,4},{9,5},... | collective-permute-start | bytes 208904 | tf_op jit(solution)/shard_map/ppermute | solution.py:193
  55.1 7.4 %collective-permute-start.2 = (f32[17,8,128]{2,1,0:T(8,128)S(1)}, f32[17,8,128]{2,1,0:T(8,128)S(1)}, u32[]{:S(2)}, u32[]{:S(2)}) collective-permute-start(f32[17,8,128]{2,1,0:T(8,128)S(1)} %pad_maximum_fusion.6), channel_id=1, source_target_pairs={{0,8},{1,9},{2,10},{3,11},{4,12},{5,13},{6,14},{7,15},{8,0},{9,1},... | collective-permute-start | bytes 208904 | tf_op jit(solution)/shard_map/ppermute | solution.py:193
  55.7 6.1 %collective-permute-start.1 = (f32[17,8,128]{2,1,0:T(8,128)S(1)}, f32[17,8,128]{2,1,0:T(8,128)S(1)}, u32[]{:S(2)}, u32[]{:S(2)}) collective-permute-start(f32[17,8,128]{2,1,0:T(8,128)S(1)} %pad_maximum_fusion.6), channel_id=1, source_target_pairs={{0,4},{1,5},{2,6},{3,7},{4,0},{5,1},{6,2},{7,3},{8,12},{9,13},{10,... | collective-permute-start | bytes 208904 | tf_op jit(solution)/shard_map/ppermute | solution.py:193
  62.6 5.8 %collective-permute-start.6 = (f32[36,8,128]{2,1,0:T(8,128)S(1)}, f32[36,8,128]{2,1,0:T(8,128)S(1)}, u32[]{:S(2)}, u32[]{:S(2)}) collective-permute-start(f32[36,8,128]{2,1,0:T(8,128)S(1)} %pad_maximum_fusion), channel_id=1, source_target_pairs={{0,2},{1,3},{2,0},{3,1},{4,6},{5,7},{6,4},{7,5},{8,10},{9,11},{10,... | collective-permute-start | bytes 442376 | tf_op jit(solution)/shard_map/ppermute | solution.py:193
  63.4 5.8 %collective-permute-start.4 = (f32[32,8,128]{2,1,0:T(8,128)S(1)}, f32[32,8,128]{2,1,0:T(8,128)S(1)}, u32[]{:S(2)}, u32[]{:S(2)}) collective-permute-start(f32[32,8,128]{2,1,0:T(8,128)S(1)} %pad_maximum_fusion.3), channel_id=1, source_target_pairs={{0,1},{1,0},{2,3},{3,2},{4,5},{5,4},{6,7},{7,6},{8,9},{9,8},{10,11... | collective-permute-start | bytes 393224 | tf_op jit(solution)/shard_map/ppermute | solution.py:193
  68.5 8.2 %collective-permute-start.7 = (f32[72,8,128]{2,1,0:T(8,128)S(1)}, f32[72,8,128]{2,1,0:T(8,128)S(1)}, u32[]{:S(2)}, u32[]{:S(2)}) collective-permute-start(f32[72,8,128]{2,1,0:T(8,128)S(1)} %constant_dynamic-update-slice_fusion.5.near_b), channel_id=1, source_target_pairs={{0,1},{1,0},{2,3},{3,2},{4,5},{5,4},{6,7},{7,6},{8,9},{9,8},{10,11... | collective-permute-start | bytes 884744 | tf_op jit(solution)/shard_map/ppermute | solution.py:193
  69.2 7.3 %collective-permute-start.5 = (f32[64,8,128]{2,1,0:T(8,128)S(1)}, f32[64,8,128]{2,1,0:T(8,128)S(1)}, u32[]{:S(2)}, u32[]{:S(2)}) collective-permute-start(f32[64,8,128]{2,1,0:T(8,128)S(1)} %constant_dynamic-update-slice_fusion.near_a), channel_id=1, source_target_pairs={{0,2},{1,3},{2,0},{3,1},{4,6},{5,7},{6,4},{7,5},{8,10},{9,11},{10,... | collective-permute-start | bytes 786440 | tf_op jit(solution)/shard_map/ppermute | solution.py:193
  84.4 9.1 %collective-permute-start.11 = (f32[17,8,128]{2,1,0:T(8,128)S(1)}, f32[17,8,128]{2,1,0:T(8,128)S(1)}, u32[]{:S(2)}, u32[]{:S(2)}) collective-permute-start(f32[17,8,128]{2,1,0:T(8,128)S(1)} %pad_maximum_fusion.7), channel_id=1, source_target_pairs={{0,12},{1,13},{2,14},{3,15},{4,8},{5,9},{6,10},{7,11},{8,4},{9,5},... | collective-permute-start | bytes 208904 | tf_op jit(solution)/shard_map/ppermute | solution.py:193
  86.0 7.4 %collective-permute-start.10 = (f32[17,8,128]{2,1,0:T(8,128)S(1)}, f32[17,8,128]{2,1,0:T(8,128)S(1)}, u32[]{:S(2)}, u32[]{:S(2)}) collective-permute-start(f32[17,8,128]{2,1,0:T(8,128)S(1)} %pad_maximum_fusion.7), channel_id=1, source_target_pairs={{0,8},{1,9},{2,10},{3,11},{4,12},{5,13},{6,14},{7,15},{8,0},{9,1},... | collective-permute-start | bytes 208904 | tf_op jit(solution)/shard_map/ppermute | solution.py:193
  86.0 6.7 %collective-permute-start.9 = (f32[17,8,128]{2,1,0:T(8,128)S(1)}, f32[17,8,128]{2,1,0:T(8,128)S(1)}, u32[]{:S(2)}, u32[]{:S(2)}) collective-permute-start(f32[17,8,128]{2,1,0:T(8,128)S(1)} %pad_maximum_fusion.7), channel_id=1, source_target_pairs={{0,4},{1,5},{2,6},{3,7},{4,0},{5,1},{6,2},{7,3},{8,12},{9,13},{10,... | collective-permute-start | bytes 208904 | tf_op jit(solution)/shard_map/ppermute | solution.py:193
  93.5 5.8 %collective-permute-start.14 = (f32[36,8,128]{2,1,0:T(8,128)S(1)}, f32[36,8,128]{2,1,0:T(8,128)S(1)}, u32[]{:S(2)}, u32[]{:S(2)}) collective-permute-start(f32[36,8,128]{2,1,0:T(8,128)S(1)} %pad_maximum_fusion.1), channel_id=1, source_target_pairs={{0,2},{1,3},{2,0},{3,1},{4,6},{5,7},{6,4},{7,5},{8,10},{9,11},{10,... | collective-permute-start | bytes 442376 | tf_op jit(solution)/shard_map/ppermute | solution.py:193
  94.3 6.3 %collective-permute-start.12 = (f32[32,8,128]{2,1,0:T(8,128)S(1)}, f32[32,8,128]{2,1,0:T(8,128)S(1)}, u32[]{:S(2)}, u32[]{:S(2)}) collective-permute-start(f32[32,8,128]{2,1,0:T(8,128)S(1)} %pad_maximum_fusion.4), channel_id=1, source_target_pairs={{0,1},{1,0},{2,3},{3,2},{4,5},{5,4},{6,7},{7,6},{8,9},{9,8},{10,11... | collective-permute-start | bytes 393224 | tf_op jit(solution)/shard_map/ppermute | solution.py:193
  99.4 8.4 %collective-permute-start.15 = (f32[72,8,128]{2,1,0:T(8,128)S(1)}, f32[72,8,128]{2,1,0:T(8,128)S(1)}, u32[]{:S(2)}, u32[]{:S(2)}) collective-permute-start(f32[72,8,128]{2,1,0:T(8,128)S(1)} %constant_dynamic-update-slice_fusion.15.near_b), channel_id=1, source_target_pairs={{0,1},{1,0},{2,3},{3,2},{4,5},{5,4},{6,7},{7,6},{8,9},{9,8},{10,11... | collective-permute-start | bytes 884744 | tf_op jit(solution)/shard_map/ppermute | solution.py:193
  100.5 7.2 %collective-permute-start.13 = (f32[64,8,128]{2,1,0:T(8,128)S(1)}, f32[64,8,128]{2,1,0:T(8,128)S(1)}, u32[]{:S(2)}, u32[]{:S(2)}) collective-permute-start(f32[64,8,128]{2,1,0:T(8,128)S(1)} %constant_dynamic-update-slice_fusion.10.near_a), channel_id=1, source_target_pairs={{0,2},{1,3},{2,0},{3,1},{4,6},{5,7},{6,4},{7,5},{8,10},{9,11},{10,... | collective-permute-start | bytes 786440 | tf_op jit(solution)/shard_map/ppermute | solution.py:193
  112.3 9.1 %collective-permute-start.20 = (f32[17,8,128]{2,1,0:T(8,128)S(1)}, f32[17,8,128]{2,1,0:T(8,128)S(1)}, u32[]{:S(2)}, u32[]{:S(2)}) collective-permute-start(f32[17,8,128]{2,1,0:T(8,128)S(1)} %pad_maximum_fusion.8), channel_id=1, source_target_pairs={{0,12},{1,13},{2,14},{3,15},{4,8},{5,9},{6,10},{7,11},{8,4},{9,5},... | collective-permute-start | bytes 208904 | tf_op jit(solution)/shard_map/ppermute | solution.py:193
  113.9 7.5 %collective-permute-start.19 = (f32[17,8,128]{2,1,0:T(8,128)S(1)}, f32[17,8,128]{2,1,0:T(8,128)S(1)}, u32[]{:S(2)}, u32[]{:S(2)}) collective-permute-start(f32[17,8,128]{2,1,0:T(8,128)S(1)} %pad_maximum_fusion.8), channel_id=1, source_target_pairs={{0,8},{1,9},{2,10},{3,11},{4,12},{5,13},{6,14},{7,15},{8,0},{9,1},... | collective-permute-start | bytes 208904 | tf_op jit(solution)/shard_map/ppermute | solution.py:193
  113.9 6.8 %collective-permute-start.18 = (f32[17,8,128]{2,1,0:T(8,128)S(1)}, f32[17,8,128]{2,1,0:T(8,128)S(1)}, u32[]{:S(2)}, u32[]{:S(2)}) collective-permute-start(f32[17,8,128]{2,1,0:T(8,128)S(1)} %pad_maximum_fusion.8), channel_id=1, source_target_pairs={{0,4},{1,5},{2,6},{3,7},{4,0},{5,1},{6,2},{7,3},{8,12},{9,13},{10,... | collective-permute-start | bytes 208904 | tf_op jit(solution)/shard_map/ppermute | solution.py:193
  121.4 5.8 %collective-permute-start.23 = (f32[36,8,128]{2,1,0:T(8,128)S(1)}, f32[36,8,128]{2,1,0:T(8,128)S(1)}, u32[]{:S(2)}, u32[]{:S(2)}) collective-permute-start(f32[36,8,128]{2,1,0:T(8,128)S(1)} %pad_maximum_fusion.2), channel_id=1, source_target_pairs={{0,2},{1,3},{2,0},{3,1},{4,6},{5,7},{6,4},{7,5},{8,10},{9,11},{10,... | collective-permute-start | bytes 442376 | tf_op jit(solution)/shard_map/ppermute | solution.py:193
  122.2 6.0 %collective-permute-start.21 = (f32[32,8,128]{2,1,0:T(8,128)S(1)}, f32[32,8,128]{2,1,0:T(8,128)S(1)}, u32[]{:S(2)}, u32[]{:S(2)}) collective-permute-start(f32[32,8,128]{2,1,0:T(8,128)S(1)} %pad_maximum_fusion.5), channel_id=1, source_target_pairs={{0,1},{1,0},{2,3},{3,2},{4,5},{5,4},{6,7},{7,6},{8,9},{9,8},{10,11... | collective-permute-start | bytes 393224 | tf_op jit(solution)/shard_map/ppermute | solution.py:193
  123.2 15.6 %collective-permute-start.16 = (f32[64,2,8,128]{3,2,1,0:T(8,128)S(1)}, f32[64,2,8,128]{3,2,1,0:T(8,128)S(1)}, u32[]{:S(2)}, u32[]{:S(2)}) collective-permute-start(f32[64,2,8,128]{3,2,1,0:T(8,128)S(1)} %get-tuple-element.27), channel_id=1, source_target_pairs={{0,16},{16,0},{1,17},{17,1},{2,18},{18,2},{3,19},{19,3},{4,20},{20... | collective-permute-start | bytes 1572872 | tf_op jit(solution)/shard_map/ppermute | solution.py:196
  127.3 8.2 %collective-permute-start.24 = (f32[72,8,128]{2,1,0:T(8,128)S(1)}, f32[72,8,128]{2,1,0:T(8,128)S(1)}, u32[]{:S(2)}, u32[]{:S(2)}) collective-permute-start(f32[72,8,128]{2,1,0:T(8,128)S(1)} %constant_dynamic-update-slice_fusion.25.near_b), channel_id=1, source_target_pairs={{0,1},{1,0},{2,3},{3,2},{4,5},{5,4},{6,7},{7,6},{8,9},{9,8},{10,11... | collective-permute-start | bytes 884744 | tf_op jit(solution)/shard_map/ppermute | solution.py:193
  128.2 7.2 %collective-permute-start.22 = (f32[64,8,128]{2,1,0:T(8,128)S(1)}, f32[64,8,128]{2,1,0:T(8,128)S(1)}, u32[]{:S(2)}, u32[]{:S(2)}) collective-permute-start(f32[64,8,128]{2,1,0:T(8,128)S(1)} %constant_dynamic-update-slice_fusion.20.near_a), channel_id=1, source_target_pairs={{0,2},{1,3},{2,0},{3,1},{4,6},{5,7},{6,4},{7,5},{8,10},{9,11},{10,... | collective-permute-start | bytes 786440 | tf_op jit(solution)/shard_map/ppermute | solution.py:193
  138.8 1.4 collective-permute-start.26
  139.6 11.1 %collective-permute-start.25 = (f32[64,2,8,128]{3,2,1,0:T(8,128)S(1)}, f32[64,2,8,128]{3,2,1,0:T(8,128)S(1)}, u32[]{:S(2)}, u32[]{:S(2)}) collective-permute-start(f32[64,2,8,128]{3,2,1,0:T(8,128)S(1)} %get-tuple-element.32), channel_id=1, source_target_pairs={{0,16},{16,0},{1,17},{17,1},{2,18},{18,2},{3,19},{19,3},{4,20},{20... | collective-permute-start | bytes 1572872 | tf_op jit(solution)/shard_map/ppermute | solution.py:196
  140.1 4.5 %collective-permute-start.29 = (f32[8,128]{1,0:T(8,128)S(1)}, f32[8,128]{1,0:T(8,128)S(1)}, u32[]{:S(2)}, u32[]{:S(2)}) collective-permute-start(f32[8,128]{1,0:T(8,128)S(1)} %fusion.25), channel_id=1, source_target_pairs={{0,3},{1,2},{2,1},{3,0},{4,7},{5,6},{6,5},{7,4},{8,11},{9,10},{10,... | collective-permute-start | bytes 12296 | tf_op jit(solution)/shard_map/ppermute | solution.py:193
  141.4 3.6 %collective-permute-start.28 = (f32[8,128]{1,0:T(8,128)S(1)}, f32[8,128]{1,0:T(8,128)S(1)}, u32[]{:S(2)}, u32[]{:S(2)}) collective-permute-start(f32[8,128]{1,0:T(8,128)S(1)} %fusion.25), channel_id=1, source_target_pairs={{0,2},{1,3},{2,0},{3,1},{4,6},{5,7},{6,4},{7,5},{8,10},{9,11},{10,... | collective-permute-start | bytes 12296 | tf_op jit(solution)/shard_map/ppermute | solution.py:193
  142.7 3.6 %collective-permute-start.27 = (f32[8,128]{1,0:T(8,128)S(1)}, f32[8,128]{1,0:T(8,128)S(1)}, u32[]{:S(2)}, u32[]{:S(2)}) collective-permute-start(f32[8,128]{1,0:T(8,128)S(1)} %fusion.25), channel_id=1, source_target_pairs={{0,1},{1,0},{2,3},{3,2},{4,5},{5,4},{6,7},{7,6},{8,9},{9,8},{10,11... | collective-permute-start | bytes 12296 | tf_op jit(solution)/shard_map/ppermute | solution.py:193
  143.9 8.8 %collective-permute-start.33 = (f32[64,2,8,128]{3,2,1,0:T(8,128)S(1)}, f32[64,2,8,128]{3,2,1,0:T(8,128)S(1)}, u32[]{:S(2)}, u32[]{:S(2)}) collective-permute-start(f32[64,2,8,128]{3,2,1,0:T(8,128)S(1)} %get-tuple-element.34), channel_id=1, source_target_pairs={{0,16},{16,0},{1,17},{17,1},{2,18},{18,2},{3,19},{19,3},{4,20},{20... | collective-permute-start | bytes 1572872 | tf_op jit(solution)/shard_map/ppermute | solution.py:196
  146.3 5.4 %collective-permute-start.32 = (f32[8,128]{1,0:T(8,128)S(1)}, f32[8,128]{1,0:T(8,128)S(1)}, u32[]{:S(2)}, u32[]{:S(2)}) collective-permute-start(f32[8,128]{1,0:T(8,128)S(1)} %add_add_fusion.1), channel_id=1, source_target_pairs={{0,12},{1,13},{2,14},{3,15},{4,8},{5,9},{6,10},{7,11},{8,4},{9,5},... | collective-permute-start | bytes 12296 | tf_op jit(solution)/shard_map/ppermute | solution.py:193
  147.9 4.5 %collective-permute-start.31 = (f32[8,128]{1,0:T(8,128)S(1)}, f32[8,128]{1,0:T(8,128)S(1)}, u32[]{:S(2)}, u32[]{:S(2)}) collective-permute-start(f32[8,128]{1,0:T(8,128)S(1)} %add_add_fusion.1), channel_id=1, source_target_pairs={{0,8},{1,9},{2,10},{3,11},{4,12},{5,13},{6,14},{7,15},{8,0},{9,1},... | collective-permute-start | bytes 12296 | tf_op jit(solution)/shard_map/ppermute | solution.py:193
  147.9 4.5 %collective-permute-start.30 = (f32[8,128]{1,0:T(8,128)S(1)}, f32[8,128]{1,0:T(8,128)S(1)}, u32[]{:S(2)}, u32[]{:S(2)}) collective-permute-start(f32[8,128]{1,0:T(8,128)S(1)} %add_add_fusion.1), channel_id=1, source_target_pairs={{0,4},{1,5},{2,6},{3,7},{4,0},{5,1},{6,2},{7,3},{8,12},{9,13},{10,... | collective-permute-start | bytes 12296 | tf_op jit(solution)/shard_map/ppermute | solution.py:193
  (6 other events, 14.5 us)

commit v6 on v5

v6 whole, which is shorter than its diff:
```python
import functools

import jax
import jax.numpy as jnp
from jax import lax
from jax.experimental import pallas as pl
from jax.experimental.pallas import tpu as pltpu
from jax.sharding import PartitionSpec as P

ITERS = 4
LANES = 128
SUBLANES = 8
VMEM = pl.BlockSpec(memory_space=pltpu.VMEM)
SMEM = pl.BlockSpec(memory_space=pltpu.SMEM)
HBM = pl.BlockSpec(memory_space=pltpu.HBM)
PARAMS = pltpu.CompilerParams(vmem_limit_bytes=20 * 1024 * 1024)


def f32(*shape):
    return jax.ShapeDtypeStruct(shape, jnp.float32)


def call(kernel, out_shape, specs, *operands, scratch=()):
    several = isinstance(out_shape, (tuple, list))
    return pl.pallas_call(
        kernel,
        out_shape=tuple(out_shape) if several else out_shape,
        in_specs=specs,
        out_specs=(VMEM,) * len(out_shape) if several else VMEM,
        scratch_shapes=list(scratch),
        compiler_params=PARAMS,
    )(*operands)


def per_case(value):
    return jnp.sum(value, axis=1, keepdims=True)


def respond(block, load, gamma, energy, answer, copies=()):
    ntile, ncase, width = load.shape
    each = 2
    total = jnp.zeros((2 * ncase, ntile * width), jnp.float32)
    for j in range(ntile // each):
        value = jnp.concatenate([load[j * each + i] for i in range(each)], axis=1)
        high = value.astype(jnp.bfloat16)
        low = (value - high.astype(jnp.float32)).astype(jnp.bfloat16)
        if copies:
            copies[j].wait()
        total = total + jnp.dot(
            jnp.concatenate([high, low], axis=0),
            block[j * each * width : (j + 1) * each * width, :],
            preferred_element_type=jnp.float32,
        )
    total = total[:ncase] + total[ncase:]
    work = 0.5 * energy
    for i in range(ntile):
        tile = total[:, i * width : (i + 1) * width]
        answer[i] = tile
        work = work + load[i] * tile
    lane = lax.broadcasted_iota(jnp.int32, work.shape, 1)
    sums = jnp.where(lane == 0, per_case(0.5 * gamma), 0.0)
    answer[ntile] = jnp.where(lane == 1, per_case(work), sums)


def found(away, slot, nh, nz, nslot):
    half = nslot // 2 * nh
    x_bit, y_bit, z_part = away & 1, (away >> 1) & 1, away >> 2
    found_a = ((y_bit * 2 + x_bit) * nz + z_part) * half + slot * nh
    found_b = ((x_bit * 2 + y_bit) * nz + z_part) * (half + 1) + (slot - nslot // 2) * nh
    return jnp.where(slot < nslot // 2, found_a, 4 * nz * half + found_b)


def pack_kernel(nh, nslot, room, tiles, lines, plate, foundation, slots, active, field, comp, picked, *refs):
    *messages, whole, count = refs
    nsub = len(messages)
    nz = nsub // 4
    side, me = lax.axis_index("body"), lax.axis_index("sub")
    whole[...] = jnp.zeros_like(whole)
    lane = lax.broadcasted_iota(jnp.int32, (1, LANES), 1)

    def clear(i, carry):
        count[i] = 0
        return carry

    lax.fori_loop(0, nsub, clear, 0)

    def body(p, carry):
        owners, places = (plate[p], foundation[p]), (slots[2 * p], slots[2 * p + 1])
        owner, other = (jnp.where(side == 0, owners[i], owners[1 - i]) for i in range(2))
        slot, other_slot = (jnp.where(side == 0, places[i], places[1 - i]) for i in range(2))
        rank = count[owner]
        count[owner] = rank + 1
        on = active[p].astype(jnp.float32)
        base = (owner ^ me) * tiles
        whole[pl.ds(base + rank * nh, nh)] = on * field[p]
        base = base + room * nh
        line = rank * nh
        for h in range(nh):
            whole[base + (line + h) // SUBLANES, pl.ds((line + h) % SUBLANES, 1), :] = comp[p, h : h + 1, :]
        base = base + lines
        far = found(owner ^ other, other_slot, nh, nz, nslot).astype(jnp.float32)
        near = (slot * nh).astype(jnp.float32)
        fact = jnp.where(lane == 0, near, jnp.where(lane == 1, far, jnp.where(lane == 2, on, 0.0)))
        whole[base + rank // SUBLANES, pl.ds(rank % SUBLANES, 1), :] = fact
        picked[p] = found(me ^ other, other_slot, nh, nz, nslot)
        return carry

    lax.fori_loop(0, field.shape[0], body, 0)
    for i, message in enumerate(messages):
        message[...] = whole[i * tiles : (i + 1) * tiles]


def start_kernel(nh, room, lines, place, *refs):
    *messages, block, r_out, comp, answer, held, load, sems = refs
    pieces = sems.shape[0]
    size = block.shape[0] // pieces
    copies = []
    for j in range(pieces):
        rows = pl.ds(j * size, size)
        copies.append(pltpu.make_async_copy(block.at[rows], held.at[rows], sems.at[j]))
        copies[-1].start()
    load[...] = jnp.zeros_like(load)
    gamma = energy = jnp.zeros(r_out.shape[2:], jnp.float32)
    for i, message in enumerate(messages):
        comp[i * lines : (i + 1) * lines] = message[room * nh : room * nh + lines]
        for j in range(room):
            row = i * room + j
            r = message[j * nh : (j + 1) * nh]
            r_out[row] = r
            load[pl.ds(place[0, row], nh)] += r
            for h in range(nh):
                line, sub = divmod(j * nh + h, SUBLANES)
                square = r[h] * r[h]
                gamma = gamma + square
                energy = energy + message[room * nh + line, sub : sub + 1, :] * square
    respond(held, load, gamma, energy, answer, copies)


def tree(values):
    while len(values) > 1:
        values = [a + b for a, b in zip(values[::2], values[1::2])]
    return values[0]


def steps(first, sums, known):
    gamma, delta = sums[:, 0:1], sums[:, 1:2]
    if first:
        return gamma, gamma / delta, jnp.zeros_like(gamma)
    beta = gamma / known[:, 0:1]
    return gamma, gamma / (delta - beta * gamma / known[:, 1:2]), beta


def home_kernel(first, nh, room, lines, place, keep, picked, comp, own, near_a, far_a, near_b, far_b, known, block, *refs):
    if first:
        r_in, r, s, answer, part, known_out, load, resp = refs
    else:
        r_in, s_in, r, s, answer, part, known_out, load, resp = refs
    load[...] = jnp.zeros_like(load)
    ncase, width = r.shape[2:]
    at = 0
    for piece in (near_a, far_a, near_b, far_b):
        resp[at : at + piece.shape[0]] = piece[...]
        at += piece.shape[0]
    each = own.shape[0] // 2 + 1
    sums = tree([piece[i + each - 1] for piece in (near_b, far_b) for i in range(0, piece.shape[0], each)])
    gamma, alpha, beta = steps(first, sums, known[...])
    lane = lax.broadcasted_iota(jnp.int32, (ncase, width), 1)
    known_out[...] = jnp.where(lane == 0, gamma, jnp.where(lane == 1, alpha, beta))
    alpha = jnp.broadcast_to(alpha, (ncase, width))
    beta = jnp.broadcast_to(beta, (ncase, width))
    zero = jnp.zeros((ncase, width), jnp.float32)

    def pick(p, carry):
        part[p] = resp[pl.ds(picked[p], nh)]
        return carry

    lax.fori_loop(0, part.shape[0], pick, 0, unroll=8)

    def pair(i, sums):
        gamma, energy = sums
        for j in range(room):
            row = i * room + j
            near, far, on = place[0, row], place[1, row], keep[row]
            for h in range(nh):
                line, sub = divmod(j * nh + h, SUBLANES)
                c = comp[i * lines + line, sub : sub + 1, :]
                residual = r_in[row, h]
                image = on * (own[near + h] + resp[far + h] + c * residual)
                if not first:
                    image = image + beta * s_in[row, h]
                residual = residual - alpha * image
                r[row, h], s[row, h] = residual, image
                load[near + h] += residual
                square = residual * residual
                gamma = gamma + square
                energy = energy + c * square
        return gamma, energy

    gamma, energy = lax.fori_loop(0, r.shape[0] // room, pair, (zero, zero))
    respond(block, load, gamma, energy, answer)


def on_device(rhs, compliance, plate_owner, found_owner, slot_pairs, active, inverse):
    nsub = lax.axis_size("sub")
    nbody = lax.axis_size("body")
    ncase, npatch, gap = rhs.shape
    block = inverse[0, 0]
    nslot = block.shape[0] // gap
    nh = gap // LANES
    per = nslot * nh + 1
    room = max(2, 2 * npatch // nsub)
    nrow = nsub * room
    lines = -(-room * nh // SUBLANES)
    deep = -(-room // SUBLANES)
    tiles = room * nh + lines + deep
    nz = nsub // 4
    half = nslot // 2 * nh

    def exchange(message):
        return lax.all_to_all(message, "sub", split_axis=0, concat_axis=0, tiled=True)

    def swap(value, far):
        return lax.ppermute(value, "sub", [(i, i ^ far) for i in range(nsub)])

    def sibling(value):
        return lax.ppermute(value, "body", [(i, nbody - 1 - i) for i in range(nbody)])

    keep = active.astype(jnp.float32)
    start = keep[None, :, None] * rhs
    by_patch = jnp.transpose(rhs.reshape(ncase, npatch, nh, LANES), (1, 2, 0, 3))
    picked, *messages = pl.pallas_call(
        functools.partial(pack_kernel, nh, nslot, room, tiles, lines),
        out_shape=(jax.ShapeDtypeStruct((npatch,), jnp.int32),) + (f32(tiles, ncase, LANES),) * nsub,
        in_specs=[SMEM] * 4 + [VMEM] * 2,
        out_specs=(SMEM,) + (VMEM,) * nsub,
        scratch_shapes=[pltpu.VMEM((nsub * tiles, ncase, LANES), jnp.float32), pltpu.SMEM((nsub,), jnp.int32)],
        compiler_params=PARAMS,
    )(
        plate_owner.reshape(npatch),
        found_owner.reshape(npatch),
        slot_pairs.reshape(2 * npatch),
        active,
        by_patch,
        compliance.reshape(npatch, nh, LANES),
    )
    sent = [swap(messages[i], i) for i in range(nsub - 1, 0, -1)]
    messages = messages[:1] + sent[::-1]
    facts = jnp.stack([message[room * nh + lines :] for message in messages])
    facts = facts.reshape(nsub, deep * SUBLANES, LANES)[:, :room, :3].reshape(nrow, 3).T
    home = facts[:2].astype(jnp.int32)
    on = facts[2]

    field = f32(nrow, nh, ncase, LANES)
    answer = f32(per, ncase, LANES)
    load = pltpu.VMEM((nslot * nh, ncase, LANES), jnp.float32)
    spread = pltpu.VMEM((nsub * per, ncase, LANES), jnp.float32)
    home_r, comp, own, block = call(
        functools.partial(start_kernel, nh, room, lines),
        (field, f32(nsub * lines, ncase, LANES), answer, jax.ShapeDtypeStruct(block.shape, block.dtype)),
        [SMEM] + [VMEM] * nsub + [HBM],
        home,
        *messages,
        pltpu.with_memory_space_constraint(block, pltpu.HBM),
        scratch=[load, pltpu.SemaphoreType.DMA((nslot,))],
    )
    known = jnp.zeros((ncase, LANES), jnp.float32)
    state = [home_r]
    r, d, x, s = start, None, None, None
    for step in range(ITERS - 1):
        far = sibling(own)
        far = jnp.concatenate([far[: per - 1], own[per - 1 :] + far[per - 1 :]])
        parts = [far] + [swap(far, 4 * z) for z in range(1, nz)]
        a = jnp.concatenate([part[:half] for part in parts])
        b = jnp.concatenate([part[half:] for part in parts])
        far_a, far_b = swap(a, 1), swap(b, 2)
        a, b = jnp.concatenate([a, far_a]), jnp.concatenate([b, far_b])
        far_a, far_b = swap(a, 2), swap(b, 1)
        *state, own, part, known = call(
            functools.partial(home_kernel, step == 0, nh, room, lines),
            (field,) * 2 + (answer, f32(npatch, nh, ncase, LANES), f32(ncase, LANES)),
            [SMEM] * 3 + [VMEM] * (8 + len(state)),
            home,
            on,
            picked,
            comp,
            own,
            a,
            far_a,
            b,
            far_b,
            known,
            block,
            *state,
            scratch=[load, spread],
        )
        image = jnp.transpose(part + sibling(part), (2, 0, 1, 3)).reshape(ncase, npatch, gap)
        image = keep[None, :, None] * (image + compliance[None] * r)
        alpha, beta = known[:, 1].reshape(ncase, 1, 1), known[:, 2].reshape(ncase, 1, 1)
        if step == 0:
            d, s = r, image
            x = alpha * d
        else:
            d, s = r + beta * d, image + beta * s
            x = x + alpha * d
        r = r - alpha * s
    sums = own[per - 1]
    sums = sums + sibling(sums)
    sums = jnp.sum(exchange(jnp.broadcast_to(sums[None], (nsub, ncase, LANES))), axis=0)
    _, alpha, beta = steps(False, sums, known)
    return x + alpha[:, :, None] * (r + beta[:, :, None] * d)


def solution(mesh):
    in_specs = (
        P(None, "sub", None),
        P("sub", None),
        P("sub", None),
        P("sub", None),
        P("sub", None),
        P("sub"),
        P("body", "sub", None, None),
    )
    out_specs = P(None, "sub", None)
    return jax.shard_map(
        on_device, mesh=mesh, in_specs=in_specs, out_specs=out_specs, check_vma=False
    )
```

time: 155 us -> 163 us (1.052)
  blocking collectives: 39.4 us -> 0 us
  starting transfers between devices: 32.2 us -> 65.4 us
  local copies, waits for them, and re-layouts: 11.1 us -> 17.9 us
  Pallas kernels: 13.8 us -> 18.4 us
  waiting for transfers between devices: 52.5 us -> 54.9 us
    all_to_all x1 -> x0, blocking collectives: 39.4 us -> none  [exchange(): lax.all_to_all(message, 'sub', split_axis=0, concat_axis=0, tiled=True)]
    ppermute x27 -> x36, starting transfers between devices: 31.4 us -> 59.6 us  [swap(): return lax.ppermute(value, 'sub', [(i, i ^ far) for i in range(nsub)])]
    all_to_all x0 -> x1, waiting for transfers between devices: none -> 5.64 us  [exchange(): lax.all_to_all(message, 'sub', split_axis=0, concat_axis=0, tiled=True)]
    all_to_all x0 -> x1, starting transfers between devices: none -> 4.6 us  [exchange(): lax.all_to_all(message, 'sub', split_axis=0, concat_axis=0, tiled=True)]
    pallas_call x0 -> x1, Pallas kernels: none -> 4.23 us  [on_device(): pl.pallas_call(functools.partial(pack_kernel, nh, nslot, room, tiles, lin...]
    ppermute x27 -> x36, waiting for transfers between devices: 48.7 us -> 46.2 us  [swap(): return lax.ppermute(value, 'sub', [(i, i ^ far) for i in range(nsub)])]
    reshape x6, local copies, waits for them, and re-layouts: 0.67 us -> 2.69 us  [the longest x2 1.61 us: on_device(): rhs.reshape(ncase, npatch, nh, LANES)]
    reshape x3, local copies, waits for them, and re-layouts: 1.26 us -> 3.1 us  [on_device(): jnp.transpose(part + sibling(part), (2, 0, 1, 3))]
  transfers between devices with their start and end apart: 34 -> 44, of which waited for: 21 -> 21; matrix products, arithmetic and copies ran while one was open for 2% -> 5% of each run, Pallas kernels for 2% -> 2%
where the time goes in v6:
time: 163 us; the launch traced here: 162 us
  starting transfers between devices  65.4 us (40%)
  waiting for transfers between devices  54.9 us (34%)
  Pallas kernels  18.4 us (11%)
  local copies, waits for them, and re-layouts  17.9 us (11%)
  other arithmetic  5.04 us (3%)
    ppermute x36, starting transfers between devices, swap(): return lax.ppermute(value, 'sub', [(i, i ^ far) for i in range(nsub)])  59.6 us
    ppermute x36, waiting for transfers between devices, swap(): return lax.ppermute(value, 'sub', [(i, i ^ far) for i in range(nsub)])  46.2 us
    pallas_call x4, Pallas kernels, call(): pl.pallas_call(kernel, out_shape=tuple(out_shape) if several else out_sha...  14.2 us
    unnamed x40, local copies, waits for them, and re-layouts  8.67 us
    all_to_all x1, waiting for transfers between devices, exchange(): lax.all_to_all(message, 'sub', split_axis=0, concat_axis=0, tiled=True)  5.64 us
    all_to_all x1, starting transfers between devices, exchange(): lax.all_to_all(message, 'sub', split_axis=0, concat_axis=0, tiled=True)  4.6 us
    pallas_call x1, Pallas kernels, on_device(): pl.pallas_call(functools.partial(pack_kernel, nh, nslot, room, tiles, lin...  4.23 us
  transfers between devices with their start and end apart: 44, of which 21 were waited for; matrix products, arithmetic and copies ran while one was open for 5% of the time, Pallas kernels for 2%

profile of v6, /device:TPU:0, one launch (start us, length us, event | category | flops | bytes accessed | tf_op | source)
XLA Modules:
  0.0 162.1 jit_solution(9170171547907082705)
XLA Ops:
  5.4 4.2 %shard_map.73 = (s32[64]{0:T(128)S(1)}, f32[19,8,128]{2,1,0:T(8,128)S(1)}, f32[19,8,128]{2,1,0:T(8,128)S(1)}, f32[19,8,128]{2,1,0:T(8,128)S(1)}, f32[19,8,128]{2...) custom-call(s32[64]{0:T(128)S(1)} %bitcast.85, ...), custom_call_target="tpu_custom_call" | custom-call | tf_op jit(solution)/shard_map/pallas_call | solution.py:231
  9.6 3.0 %collective-permute-start = (f32[19,8,128]{2,1,0:T(8,128)S(1)}, f32[19,8,128]{2,1,0:T(8,128)S(1)}, u32[]{:S(2)}, u32[]{:S(2)}) collective-permute-start(f32[19,8,128]{2,1,0:T(8,128)S(1)} %get-tuple-element.40), channel_id=1, source_target_pairs={{0,1},{1,0},{2,3},{3,2},{4,5},{5,4},{6,7},{7,6},{8,9},{9,8},{10,11... | collective-permute-start | bytes 233480 | tf_op jit(solution)/shard_map/ppermute | solution.py:223
  14.2 2.0 %collective-permute-start.3 = (f32[19,8,128]{2,1,0:T(8,128)S(1)}, f32[19,8,128]{2,1,0:T(8,128)S(1)}, u32[]{:S(2)}, u32[]{:S(2)}) collective-permute-start(f32[19,8,128]{2,1,0:T(8,128)S(1)} %get-tuple-element.43), channel_id=1, source_target_pairs={{0,4},{1,5},{2,6},{3,7},{4,0},{5,1},{6,2},{7,3},{8,12},{9,13},{10,... | collective-permute-start | bytes 233480 | tf_op jit(solution)/shard_map/ppermute | solution.py:223
  17.6 2.5 %collective-permute-start.5 = (f32[19,8,128]{2,1,0:T(8,128)S(1)}, f32[19,8,128]{2,1,0:T(8,128)S(1)}, u32[]{:S(2)}, u32[]{:S(2)}) collective-permute-start(f32[19,8,128]{2,1,0:T(8,128)S(1)} %get-tuple-element.45), channel_id=1, source_target_pairs={{0,6},{1,7},{2,4},{3,5},{4,2},{5,3},{6,0},{7,1},{8,14},{9,15},{10,... | collective-permute-start | bytes 233480 | tf_op jit(solution)/shard_map/ppermute | solution.py:223
  20.9 2.6 %collective-permute-start.7 = (f32[19,8,128]{2,1,0:T(8,128)S(1)}, f32[19,8,128]{2,1,0:T(8,128)S(1)}, u32[]{:S(2)}, u32[]{:S(2)}) collective-permute-start(f32[19,8,128]{2,1,0:T(8,128)S(1)} %get-tuple-element.47), channel_id=1, source_target_pairs={{0,8},{1,9},{2,10},{3,11},{4,12},{5,13},{6,14},{7,15},{8,0},{9,1},... | collective-permute-start | bytes 233480 | tf_op jit(solution)/shard_map/ppermute | solution.py:223
  24.3 3.5 %collective-permute-start.9 = (f32[19,8,128]{2,1,0:T(8,128)S(1)}, f32[19,8,128]{2,1,0:T(8,128)S(1)}, u32[]{:S(2)}, u32[]{:S(2)}) collective-permute-start(f32[19,8,128]{2,1,0:T(8,128)S(1)} %get-tuple-element.49), channel_id=1, source_target_pairs={{0,10},{1,11},{2,8},{3,9},{4,14},{5,15},{6,12},{7,13},{8,2},{9,3},... | collective-permute-start | bytes 233480 | tf_op jit(solution)/shard_map/ppermute | solution.py:223
  28.6 3.2 %collective-permute-start.11 = (f32[19,8,128]{2,1,0:T(8,128)S(1)}, f32[19,8,128]{2,1,0:T(8,128)S(1)}, u32[]{:S(2)}, u32[]{:S(2)}) collective-permute-start(f32[19,8,128]{2,1,0:T(8,128)S(1)} %get-tuple-element.51), channel_id=1, source_target_pairs={{0,12},{1,13},{2,14},{3,15},{4,8},{5,9},{6,10},{7,11},{8,4},{9,5},... | collective-permute-start | bytes 233480 | tf_op jit(solution)/shard_map/ppermute | solution.py:223
  33.3 4.5 %collective-permute-start.12 = (f32[19,8,128]{2,1,0:T(8,128)S(1)}, f32[19,8,128]{2,1,0:T(8,128)S(1)}, u32[]{:S(2)}, u32[]{:S(2)}) collective-permute-start(f32[19,8,128]{2,1,0:T(8,128)S(1)} %get-tuple-element.52), channel_id=1, source_target_pairs={{0,13},{1,12},{2,15},{3,14},{4,9},{5,8},{6,11},{7,10},{8,5},{9,4},... | collective-permute-start | bytes 233480 | tf_op jit(solution)/shard_map/ppermute | solution.py:223
  38.0 3.5 %collective-permute-start.13 = (f32[19,8,128]{2,1,0:T(8,128)S(1)}, f32[19,8,128]{2,1,0:T(8,128)S(1)}, u32[]{:S(2)}, u32[]{:S(2)}) collective-permute-start(f32[19,8,128]{2,1,0:T(8,128)S(1)} %get-tuple-element.53), channel_id=1, source_target_pairs={{0,14},{1,15},{2,12},{3,13},{4,10},{5,11},{6,8},{7,9},{8,6},{9,7},... | collective-permute-start | bytes 233480 | tf_op jit(solution)/shard_map/ppermute | solution.py:223
  41.5 2.4 %collective-permute-start.14 = (f32[19,8,128]{2,1,0:T(8,128)S(1)}, f32[19,8,128]{2,1,0:T(8,128)S(1)}, u32[]{:S(2)}, u32[]{:S(2)}) collective-permute-start(f32[19,8,128]{2,1,0:T(8,128)S(1)} %get-tuple-element.54), channel_id=1, source_target_pairs={{0,15},{1,14},{2,13},{3,12},{4,11},{5,10},{6,9},{7,8},{8,7},{9,6},... | collective-permute-start | bytes 233480 | tf_op jit(solution)/shard_map/ppermute | solution.py:223
  45.9 3.7 %collective-permute-done.14.refs_15_ = f32[19,8,128]{2,1,0:T(8,128)S(1)} collective-permute-done((f32[19,8,128]{2,1,0:T(8,128)S(1)}, f32[19,8,128]{2,1,0:T(8,128)S(1)}, u32[]{:S(2)}, u32[]{:S(2)}) %collective-permute-start.14) | collective-permute-done | bytes 77856 | tf_op jit(solution)/shard_map/ppermute | solution.py:223
  49.7 4.4 %shard_map.74 = (f32[128,2,8,128]{3,2,1,0:T(8,128)S(1)}, f32[32,8,128]{2,1,0:T(8,128)S(1)}, f32[17,8,128]{2,1,0:T(8,128)S(1)}, bf16[2048,2048]{1,0:T(8,128)(2,1)S(1)}) custom-call(s32[2,128]{1,0:T(2,128)S(1)} %slice_convert_fusion.place, f32[19,8,128]{2,1,0:T(8,128)S(1)} %get-tuple-element.39.refs_0_, f32[19,8,128]{2,1,0:T(8,128)S(1)} %collective-permute-done.refs_1_, ...), custom_call_target="tpu_custom_call" | custom-call | tf_op jit(solution)/shard_map/pallas_call | solution.py:25
  56.8 3.0 %collective-permute-start.17 = (f32[17,8,128]{2,1,0:T(8,128)S(1)}, f32[17,8,128]{2,1,0:T(8,128)S(1)}, u32[]{:S(2)}, u32[]{:S(2)}) collective-permute-start(f32[17,8,128]{2,1,0:T(8,128)S(1)} %pad_maximum_fusion.6), channel_id=1, source_target_pairs={{0,8},{1,9},{2,10},{3,11},{4,12},{5,13},{6,14},{7,15},{8,0},{9,1},... | collective-permute-start | bytes 208904 | tf_op jit(solution)/shard_map/ppermute | solution.py:223
  59.9 4.2 %collective-permute-done.16 = f32[17,8,128]{2,1,0:T(8,128)S(1)} collective-permute-done((f32[17,8,128]{2,1,0:T(8,128)S(1)}, f32[17,8,128]{2,1,0:T(8,128)S(1)}, u32[]{:S(2)}, u32[]{:S(2)}) %collective-permute-start.16) | collective-permute-done | bytes 69664 | tf_op jit(solution)/shard_map/ppermute | solution.py:223
  68.1 3.8 %collective-permute-done.21 = f32[36,8,128]{2,1,0:T(8,128)S(1)} collective-permute-done((f32[36,8,128]{2,1,0:T(8,128)S(1)}, f32[36,8,128]{2,1,0:T(8,128)S(1)}, u32[]{:S(2)}, u32[]{:S(2)}) %collective-permute-start.21) | collective-permute-done | bytes 147488 | tf_op jit(solution)/shard_map/ppermute | solution.py:223
  73.9 6.7 %collective-permute-done.20.far_a = f32[64,8,128]{2,1,0:T(8,128)S(1)} collective-permute-done((f32[64,8,128]{2,1,0:T(8,128)S(1)}, f32[64,8,128]{2,1,0:T(8,128)S(1)}, u32[]{:S(2)}, u32[]{:S(2)}) %collective-permute-start.20) | collective-permute-done | bytes 262176 | tf_op jit(solution)/shard_map/ppermute | solution.py:223
  80.6 2.9 %shard_map.75 = (f32[128,2,8,128]{3,2,1,0:T(8,128)S(1)}, f32[128,2,8,128]{3,2,1,0:T(8,128)S(1)}, f32[17,8,128]{2,1,0:T(8,128)S(1)}, f32[64,2,8,128]{3,2,1,0:T(8,128)S(1)}, f32[8,128]{1,0:T(8,128)S(1)}) custom-call(s32[2,128]{1,0:T(2,128)S(1)} %slice_convert_fusion.place, f32[128]{0:T(128)S(1)} %slice_bitcast_fusion.17.keep, s32[64]{0:T(128)S(1)} %get-tuple-element.55.picked, ...), custom_call_target="tpu_custom_call" | custom-call | tf_op jit(solution)/shard_map/pallas_call | solution.py:25
  85.7 3.6 %collective-permute-start.24 = (f32[17,8,128]{2,1,0:T(8,128)S(1)}, f32[17,8,128]{2,1,0:T(8,128)S(1)}, u32[]{:S(2)}, u32[]{:S(2)}) collective-permute-start(f32[17,8,128]{2,1,0:T(8,128)S(1)} %pad_maximum_fusion.7), channel_id=1, source_target_pairs={{0,4},{1,5},{2,6},{3,7},{4,0},{5,1},{6,2},{7,3},{8,12},{9,13},{10,... | collective-permute-start | bytes 208904 | tf_op jit(solution)/shard_map/ppermute | solution.py:223
  89.4 3.9 %collective-permute-done.24 = f32[17,8,128]{2,1,0:T(8,128)S(1)} collective-permute-done((f32[17,8,128]{2,1,0:T(8,128)S(1)}, f32[17,8,128]{2,1,0:T(8,128)S(1)}, u32[]{:S(2)}, u32[]{:S(2)}) %collective-permute-start.24) | collective-permute-done | bytes 69664 | tf_op jit(solution)/shard_map/ppermute | solution.py:223
  95.5 3.3 %collective-permute-done.29 = f32[36,8,128]{2,1,0:T(8,128)S(1)} collective-permute-done((f32[36,8,128]{2,1,0:T(8,128)S(1)}, f32[36,8,128]{2,1,0:T(8,128)S(1)}, u32[]{:S(2)}, u32[]{:S(2)}) %collective-permute-start.29) | collective-permute-done | bytes 147488 | tf_op jit(solution)/shard_map/ppermute | solution.py:223
  101.3 5.5 %collective-permute-done.28.far_a = f32[64,8,128]{2,1,0:T(8,128)S(1)} collective-permute-done((f32[64,8,128]{2,1,0:T(8,128)S(1)}, f32[64,8,128]{2,1,0:T(8,128)S(1)}, u32[]{:S(2)}, u32[]{:S(2)}) %collective-permute-start.28) | collective-permute-done | bytes 262176 | tf_op jit(solution)/shard_map/ppermute | solution.py:223
  106.8 3.2 %shard_map.76 = (f32[128,2,8,128]{3,2,1,0:T(8,128)S(1)}, f32[128,2,8,128]{3,2,1,0:T(8,128)S(1)}, f32[17,8,128]{2,1,0:T(8,128)S(1)}, f32[64,2,8,128]{3,2,1,0:T(8,128)S(1)}, f32[8,128]{1,0:T(8,128)S(1)}) custom-call(s32[2,128]{1,0:T(2,128)S(1)} %slice_convert_fusion.place, f32[128]{0:T(128)S(1)} %slice_bitcast_fusion.17.keep, s32[64]{0:T(128)S(1)} %get-tuple-element.55.picked, ...), custom_call_target="tpu_custom_call" | custom-call | tf_op jit(solution)/shard_map/pallas_call | solution.py:25
  113.3 2.5 %collective-permute-start.33 = (f32[17,8,128]{2,1,0:T(8,128)S(1)}, f32[17,8,128]{2,1,0:T(8,128)S(1)}, u32[]{:S(2)}, u32[]{:S(2)}) collective-permute-start(f32[17,8,128]{2,1,0:T(8,128)S(1)} %pad_maximum_fusion.8), channel_id=1, source_target_pairs={{0,4},{1,5},{2,6},{3,7},{4,0},{5,1},{6,2},{7,3},{8,12},{9,13},{10,... | collective-permute-start | bytes 208904 | tf_op jit(solution)/shard_map/ppermute | solution.py:223
  115.8 3.9 %collective-permute-done.33 = f32[17,8,128]{2,1,0:T(8,128)S(1)} collective-permute-done((f32[17,8,128]{2,1,0:T(8,128)S(1)}, f32[17,8,128]{2,1,0:T(8,128)S(1)}, u32[]{:S(2)}, u32[]{:S(2)}) %collective-permute-start.33) | collective-permute-done | bytes 69664 | tf_op jit(solution)/shard_map/ppermute | solution.py:223
  124.0 2.4 %collective-permute-done.38 = f32[36,8,128]{2,1,0:T(8,128)S(1)} collective-permute-done((f32[36,8,128]{2,1,0:T(8,128)S(1)}, f32[36,8,128]{2,1,0:T(8,128)S(1)}, u32[]{:S(2)}, u32[]{:S(2)}) %collective-permute-start.38) | collective-permute-done | bytes 147488 | tf_op jit(solution)/shard_map/ppermute | solution.py:223
  130.2 2.3 %reshape.47 = f32[8,64,256]{2,1,0:T(8,128)} reshape(f32[8,64,2,128]{3,2,1,0:T(2,128)} %copy.19) | data formatting | bytes 1048576 | tf_op jit(solution)/shard_map/reshape | solution.py:296
  132.5 2.2 %collective-permute-done.37.far_a = f32[64,8,128]{2,1,0:T(8,128)} collective-permute-done((f32[64,8,128]{2,1,0:T(8,128)S(1)}, f32[64,8,128]{2,1,0:T(8,128)}, u32[]{:S(2)}, u32[]{:S(2)}) %collective-permute-start.37) | collective-permute-done | bytes 262176 | tf_op jit(solution)/shard_map/ppermute | solution.py:223
  134.7 3.4 %copy-done.1 = bf16[2048,2048]{1,0:T(8,128)(2,1)S(1)} copy-done((bf16[2048,2048]{1,0:T(8,128)(2,1)S(1)}, bf16[2048,2048]{1,0:T(8,128)(2,1)}, u32[]{:S(2)}) %copy-start.1) | copy-done | bytes 8388632
  140.6 3.7 %shard_map.77 = (f32[128,2,8,128]{3,2,1,0:T(8,128)}, f32[128,2,8,128]{3,2,1,0:T(8,128)}, f32[17,8,128]{2,1,0:T(8,128)S(1)}, f32[64,2,8,128]{3,2,1,0:T(8,128)S(1)}, f32[8,128]{1,0:T(8,128)S(1)}) custom-call(s32[2,128]{1,0:T(2,128)S(1)} %slice_convert_fusion.place, f32[128]{0:T(128)S(1)} %copy-done.7, s32[64]{0:T(128)S(1)} %get-tuple-element.55.picked, ...), custom_call_target="tpu_custom_call" | custom-call | tf_op jit(solution)/shard_map/pallas_call | solution.py:25
  146.1 4.6 %all-to-all-start = ((f32[16,8,128]{2,1,0:T(8,128)}), f32[16,8,128]{2,1,0:T(8,128)S(1)}, u32[]{:S(2)}, u32[]{:S(2)}) async-start(f32[16,8,128]{2,1,0:T(8,128)} %broadcast_in_dim.5), calls=%async_computation | async-start | bytes 131072 | tf_op jit(solution)/shard_map/all_to_all | solution.py:220
  152.6 5.6 %all-to-all-done = f32[16,8,128]{2,1,0:T(8,128)S(1)} async-done(((f32[16,8,128]{2,1,0:T(8,128)}), f32[16,8,128]{2,1,0:T(8,128)S(1)}, u32[]{:S(2)}, u32[]{:S(2)}) %all-to-all-start) | async-done | bytes 65568 | tf_op jit(solution)/shard_map/all_to_all | solution.py:220
  159.3 2.8 %multiply_add_fusion = f32[8,64,256]{2,1,0:T(8,128)} fusion(f32[8,64,256]{2,1,0:T(8,128)S(1)} %reshape.49, f32[8,64,256]{2,1,0:T(8,128)S(1)} %reshape.48, f32[8,64,256]{2,1,0:T(8,128)} %reshape.47, f32[8,64,256]{2,1,0:T(8,128)} %param.7, f32[8]{0:T(128)S(1)} %get-tuple-element.74, f32[8]{0:T(128)S(1)} %get-tuple-element.73, f32[8]{0:T(128)S(1)} %get-tuple-element.78, ...), kind=kLoop, calls=%fused_computation.1 | loop fusion | flops 4325376 | bytes 2687456 | tf_op jit(solution)/shard_map/add | solution.py:310
  (174 shorter events, 48.4 us)
Async XLA Ops:
  9.6 8.0 %collective-permute-start = (f32[19,8,128]{2,1,0:T(8,128)S(1)}, f32[19,8,128]{2,1,0:T(8,128)S(1)}, u32[]{:S(2)}, u32[]{:S(2)}) collective-permute-start(f32[19,8,128]{2,1,0:T(8,128)S(1)} %get-tuple-element.40), channel_id=1, source_target_pairs={{0,1},{1,0},{2,3},{3,2},{4,5},{5,4},{6,7},{7,6},{8,9},{9,8},{10,11... | collective-permute-start | bytes 233480 | tf_op jit(solution)/shard_map/ppermute | solution.py:223
  12.6 7.5 %collective-permute-start.1 = (f32[19,8,128]{2,1,0:T(8,128)S(1)}, f32[19,8,128]{2,1,0:T(8,128)S(1)}, u32[]{:S(2)}, u32[]{:S(2)}) collective-permute-start(f32[19,8,128]{2,1,0:T(8,128)S(1)} %get-tuple-element.41), channel_id=1, source_target_pairs={{0,2},{1,3},{2,0},{3,1},{4,6},{5,7},{6,4},{7,5},{8,10},{9,11},{10,... | collective-permute-start | bytes 233480 | tf_op jit(solution)/shard_map/ppermute | solution.py:223
  14.2 9.3 %collective-permute-start.3 = (f32[19,8,128]{2,1,0:T(8,128)S(1)}, f32[19,8,128]{2,1,0:T(8,128)S(1)}, u32[]{:S(2)}, u32[]{:S(2)}) collective-permute-start(f32[19,8,128]{2,1,0:T(8,128)S(1)} %get-tuple-element.43), channel_id=1, source_target_pairs={{0,4},{1,5},{2,6},{3,7},{4,0},{5,1},{6,2},{7,3},{8,12},{9,13},{10,... | collective-permute-start | bytes 233480 | tf_op jit(solution)/shard_map/ppermute | solution.py:223
  16.2 8.2 %collective-permute-start.4 = (f32[19,8,128]{2,1,0:T(8,128)S(1)}, f32[19,8,128]{2,1,0:T(8,128)S(1)}, u32[]{:S(2)}, u32[]{:S(2)}) collective-permute-start(f32[19,8,128]{2,1,0:T(8,128)S(1)} %get-tuple-element.44), channel_id=1, source_target_pairs={{0,5},{1,4},{2,7},{3,6},{4,1},{5,0},{6,3},{7,2},{8,13},{9,12},{10,... | collective-permute-start | bytes 233480 | tf_op jit(solution)/shard_map/ppermute | solution.py:223
  17.6 10.3 %collective-permute-start.5 = (f32[19,8,128]{2,1,0:T(8,128)S(1)}, f32[19,8,128]{2,1,0:T(8,128)S(1)}, u32[]{:S(2)}, u32[]{:S(2)}) collective-permute-start(f32[19,8,128]{2,1,0:T(8,128)S(1)} %get-tuple-element.45), channel_id=1, source_target_pairs={{0,6},{1,7},{2,4},{3,5},{4,2},{5,3},{6,0},{7,1},{8,14},{9,15},{10,... | collective-permute-start | bytes 233480 | tf_op jit(solution)/shard_map/ppermute | solution.py:223
  20.1 8.5 %collective-permute-start.6 = (f32[19,8,128]{2,1,0:T(8,128)S(1)}, f32[19,8,128]{2,1,0:T(8,128)S(1)}, u32[]{:S(2)}, u32[]{:S(2)}) collective-permute-start(f32[19,8,128]{2,1,0:T(8,128)S(1)} %get-tuple-element.46), channel_id=1, source_target_pairs={{0,7},{1,6},{2,5},{3,4},{4,3},{5,2},{6,1},{7,0},{8,15},{9,14},{10,... | collective-permute-start | bytes 233480 | tf_op jit(solution)/shard_map/ppermute | solution.py:223
  20.9 12.4 %collective-permute-start.7 = (f32[19,8,128]{2,1,0:T(8,128)S(1)}, f32[19,8,128]{2,1,0:T(8,128)S(1)}, u32[]{:S(2)}, u32[]{:S(2)}) collective-permute-start(f32[19,8,128]{2,1,0:T(8,128)S(1)} %get-tuple-element.47), channel_id=1, source_target_pairs={{0,8},{1,9},{2,10},{3,11},{4,12},{5,13},{6,14},{7,15},{8,0},{9,1},... | collective-permute-start | bytes 233480 | tf_op jit(solution)/shard_map/ppermute | solution.py:223
  23.5 14.5 %collective-permute-start.8 = (f32[19,8,128]{2,1,0:T(8,128)S(1)}, f32[19,8,128]{2,1,0:T(8,128)S(1)}, u32[]{:S(2)}, u32[]{:S(2)}) collective-permute-start(f32[19,8,128]{2,1,0:T(8,128)S(1)} %get-tuple-element.48), channel_id=1, source_target_pairs={{0,9},{1,8},{2,11},{3,10},{4,13},{5,12},{6,15},{7,14},{8,1},{9,0},... | collective-permute-start | bytes 233480 | tf_op jit(solution)/shard_map/ppermute | solution.py:223
  24.3 17.2 %collective-permute-start.9 = (f32[19,8,128]{2,1,0:T(8,128)S(1)}, f32[19,8,128]{2,1,0:T(8,128)S(1)}, u32[]{:S(2)}, u32[]{:S(2)}) collective-permute-start(f32[19,8,128]{2,1,0:T(8,128)S(1)} %get-tuple-element.49), channel_id=1, source_target_pairs={{0,10},{1,11},{2,8},{3,9},{4,14},{5,15},{6,12},{7,13},{8,2},{9,3},... | collective-permute-start | bytes 233480 | tf_op jit(solution)/shard_map/ppermute | solution.py:223
  27.9 16.1 %collective-permute-start.10 = (f32[19,8,128]{2,1,0:T(8,128)S(1)}, f32[19,8,128]{2,1,0:T(8,128)S(1)}, u32[]{:S(2)}, u32[]{:S(2)}) collective-permute-start(f32[19,8,128]{2,1,0:T(8,128)S(1)} %get-tuple-element.50), channel_id=1, source_target_pairs={{0,11},{1,10},{2,9},{3,8},{4,15},{5,14},{6,13},{7,12},{8,3},{9,2},... | collective-permute-start | bytes 233480 | tf_op jit(solution)/shard_map/ppermute | solution.py:223
  28.6 15.4 %collective-permute-start.11 = (f32[19,8,128]{2,1,0:T(8,128)S(1)}, f32[19,8,128]{2,1,0:T(8,128)S(1)}, u32[]{:S(2)}, u32[]{:S(2)}) collective-permute-start(f32[19,8,128]{2,1,0:T(8,128)S(1)} %get-tuple-element.51), channel_id=1, source_target_pairs={{0,12},{1,13},{2,14},{3,15},{4,8},{5,9},{6,10},{7,11},{8,4},{9,5},... | collective-permute-start | bytes 233480 | tf_op jit(solution)/shard_map/ppermute | solution.py:223
  33.3 10.8 %collective-permute-start.12 = (f32[19,8,128]{2,1,0:T(8,128)S(1)}, f32[19,8,128]{2,1,0:T(8,128)S(1)}, u32[]{:S(2)}, u32[]{:S(2)}) collective-permute-start(f32[19,8,128]{2,1,0:T(8,128)S(1)} %get-tuple-element.52), channel_id=1, source_target_pairs={{0,13},{1,12},{2,15},{3,14},{4,9},{5,8},{6,11},{7,10},{8,5},{9,4},... | collective-permute-start | bytes 233480 | tf_op jit(solution)/shard_map/ppermute | solution.py:223
  38.0 7.9 %collective-permute-start.13 = (f32[19,8,128]{2,1,0:T(8,128)S(1)}, f32[19,8,128]{2,1,0:T(8,128)S(1)}, u32[]{:S(2)}, u32[]{:S(2)}) collective-permute-start(f32[19,8,128]{2,1,0:T(8,128)S(1)} %get-tuple-element.53), channel_id=1, source_target_pairs={{0,14},{1,15},{2,12},{3,13},{4,10},{5,11},{6,8},{7,9},{8,6},{9,7},... | collective-permute-start | bytes 233480 | tf_op jit(solution)/shard_map/ppermute | solution.py:223
  41.5 8.1 %collective-permute-start.14 = (f32[19,8,128]{2,1,0:T(8,128)S(1)}, f32[19,8,128]{2,1,0:T(8,128)S(1)}, u32[]{:S(2)}, u32[]{:S(2)}) collective-permute-start(f32[19,8,128]{2,1,0:T(8,128)S(1)} %get-tuple-element.54), channel_id=1, source_target_pairs={{0,15},{1,14},{2,13},{3,12},{4,11},{5,10},{6,9},{7,8},{8,7},{9,6},... | collective-permute-start | bytes 233480 | tf_op jit(solution)/shard_map/ppermute | solution.py:223
  55.5 10.6 %collective-permute-start.18 = (f32[17,8,128]{2,1,0:T(8,128)S(1)}, f32[17,8,128]{2,1,0:T(8,128)S(1)}, u32[]{:S(2)}, u32[]{:S(2)}) collective-permute-start(f32[17,8,128]{2,1,0:T(8,128)S(1)} %pad_maximum_fusion.6), channel_id=1, source_target_pairs={{0,12},{1,13},{2,14},{3,15},{4,8},{5,9},{6,10},{7,11},{8,4},{9,5},... | collective-permute-start | bytes 208904 | tf_op jit(solution)/shard_map/ppermute | solution.py:223
  56.8 9.3 %collective-permute-start.17 = (f32[17,8,128]{2,1,0:T(8,128)S(1)}, f32[17,8,128]{2,1,0:T(8,128)S(1)}, u32[]{:S(2)}, u32[]{:S(2)}) collective-permute-start(f32[17,8,128]{2,1,0:T(8,128)S(1)} %pad_maximum_fusion.6), channel_id=1, source_target_pairs={{0,8},{1,9},{2,10},{3,11},{4,12},{5,13},{6,14},{7,15},{8,0},{9,1},... | collective-permute-start | bytes 208904 | tf_op jit(solution)/shard_map/ppermute | solution.py:223
  66.4 7.0 %collective-permute-start.19 = (f32[32,8,128]{2,1,0:T(8,128)S(1)}, f32[32,8,128]{2,1,0:T(8,128)S(1)}, u32[]{:S(2)}, u32[]{:S(2)}) collective-permute-start(f32[32,8,128]{2,1,0:T(8,128)S(1)} %pad_maximum_fusion.3), channel_id=1, source_target_pairs={{0,1},{1,0},{2,3},{3,2},{4,5},{5,4},{6,7},{7,6},{8,9},{9,8},{10,11... | collective-permute-start | bytes 393224 | tf_op jit(solution)/shard_map/ppermute | solution.py:223
  71.9 8.7 %collective-permute-start.22 = (f32[72,8,128]{2,1,0:T(8,128)S(1)}, f32[72,8,128]{2,1,0:T(8,128)S(1)}, u32[]{:S(2)}, u32[]{:S(2)}) collective-permute-start(f32[72,8,128]{2,1,0:T(8,128)S(1)} %constant_dynamic-update-slice_fusion.21.near_b), channel_id=1, source_target_pairs={{0,1},{1,0},{2,3},{3,2},{4,5},{5,4},{6,7},{7,6},{8,9},{9,8},{10,11... | collective-permute-start | bytes 884744 | tf_op jit(solution)/shard_map/ppermute | solution.py:223
  73.4 7.2 %collective-permute-start.20 = (f32[64,8,128]{2,1,0:T(8,128)S(1)}, f32[64,8,128]{2,1,0:T(8,128)S(1)}, u32[]{:S(2)}, u32[]{:S(2)}) collective-permute-start(f32[64,8,128]{2,1,0:T(8,128)S(1)} %constant_dynamic-update-slice_fusion.16.near_a), channel_id=1, source_target_pairs={{0,2},{1,3},{2,0},{3,1},{4,6},{5,7},{6,4},{7,5},{8,10},{9,11},{10,... | collective-permute-start | bytes 786440 | tf_op jit(solution)/shard_map/ppermute | solution.py:223
  84.9 8.7 %collective-permute-start.26 = (f32[17,8,128]{2,1,0:T(8,128)S(1)}, f32[17,8,128]{2,1,0:T(8,128)S(1)}, u32[]{:S(2)}, u32[]{:S(2)}) collective-permute-start(f32[17,8,128]{2,1,0:T(8,128)S(1)} %pad_maximum_fusion.7), channel_id=1, source_target_pairs={{0,12},{1,13},{2,14},{3,15},{4,8},{5,9},{6,10},{7,11},{8,4},{9,5},... | collective-permute-start | bytes 208904 | tf_op jit(solution)/shard_map/ppermute | solution.py:223
  85.7 7.8 %collective-permute-start.25 = (f32[17,8,128]{2,1,0:T(8,128)S(1)}, f32[17,8,128]{2,1,0:T(8,128)S(1)}, u32[]{:S(2)}, u32[]{:S(2)}) collective-permute-start(f32[17,8,128]{2,1,0:T(8,128)S(1)} %pad_maximum_fusion.7), channel_id=1, source_target_pairs={{0,8},{1,9},{2,10},{3,11},{4,12},{5,13},{6,14},{7,15},{8,0},{9,1},... | collective-permute-start | bytes 208904 | tf_op jit(solution)/shard_map/ppermute | solution.py:223
  85.7 7.6 %collective-permute-start.24 = (f32[17,8,128]{2,1,0:T(8,128)S(1)}, f32[17,8,128]{2,1,0:T(8,128)S(1)}, u32[]{:S(2)}, u32[]{:S(2)}) collective-permute-start(f32[17,8,128]{2,1,0:T(8,128)S(1)} %pad_maximum_fusion.7), channel_id=1, source_target_pairs={{0,4},{1,5},{2,6},{3,7},{4,0},{5,1},{6,2},{7,3},{8,12},{9,13},{10,... | collective-permute-start | bytes 208904 | tf_op jit(solution)/shard_map/ppermute | solution.py:223
  98.8 8.0 %collective-permute-start.30 = (f32[72,8,128]{2,1,0:T(8,128)S(1)}, f32[72,8,128]{2,1,0:T(8,128)S(1)}, u32[]{:S(2)}, u32[]{:S(2)}) collective-permute-start(f32[72,8,128]{2,1,0:T(8,128)S(1)} %constant_dynamic-update-slice_fusion.31.near_b), channel_id=1, source_target_pairs={{0,1},{1,0},{2,3},{3,2},{4,5},{5,4},{6,7},{7,6},{8,9},{9,8},{10,11... | collective-permute-start | bytes 884744 | tf_op jit(solution)/shard_map/ppermute | solution.py:223
  99.8 7.0 %collective-permute-start.28 = (f32[64,8,128]{2,1,0:T(8,128)S(1)}, f32[64,8,128]{2,1,0:T(8,128)S(1)}, u32[]{:S(2)}, u32[]{:S(2)}) collective-permute-start(f32[64,8,128]{2,1,0:T(8,128)S(1)} %constant_dynamic-update-slice_fusion.26.near_a), channel_id=1, source_target_pairs={{0,2},{1,3},{2,0},{3,1},{4,6},{5,7},{6,4},{7,5},{8,10},{9,11},{10,... | collective-permute-start | bytes 786440 | tf_op jit(solution)/shard_map/ppermute | solution.py:223
  110.7 18.4 %collective-permute-start.31 = (f32[64,2,8,128]{3,2,1,0:T(8,128)S(1)}, f32[64,2,8,128]{3,2,1,0:T(8,128)S(1)}, u32[]{:S(2)}, u32[]{:S(2)}) collective-permute-start(f32[64,2,8,128]{3,2,1,0:T(8,128)S(1)} %get-tuple-element.65), channel_id=1, source_target_pairs={{0,16},{16,0},{1,17},{17,1},{2,18},{18,2},{3,19},{19,3},{4,20},{20... | collective-permute-start | bytes 1572872 | tf_op jit(solution)/shard_map/ppermute | solution.py:226
  111.3 9.1 %collective-permute-start.35 = (f32[17,8,128]{2,1,0:T(8,128)S(1)}, f32[17,8,128]{2,1,0:T(8,128)S(1)}, u32[]{:S(2)}, u32[]{:S(2)}) collective-permute-start(f32[17,8,128]{2,1,0:T(8,128)S(1)} %pad_maximum_fusion.8), channel_id=1, source_target_pairs={{0,12},{1,13},{2,14},{3,15},{4,8},{5,9},{6,10},{7,11},{8,4},{9,5},... | collective-permute-start | bytes 208904 | tf_op jit(solution)/shard_map/ppermute | solution.py:223
  113.3 7.2 %collective-permute-start.34 = (f32[17,8,128]{2,1,0:T(8,128)S(1)}, f32[17,8,128]{2,1,0:T(8,128)S(1)}, u32[]{:S(2)}, u32[]{:S(2)}) collective-permute-start(f32[17,8,128]{2,1,0:T(8,128)S(1)} %pad_maximum_fusion.8), channel_id=1, source_target_pairs={{0,8},{1,9},{2,10},{3,11},{4,12},{5,13},{6,14},{7,15},{8,0},{9,1},... | collective-permute-start | bytes 208904 | tf_op jit(solution)/shard_map/ppermute | solution.py:223
  126.3 8.3 %collective-permute-start.39 = (f32[72,8,128]{2,1,0:T(8,128)S(1)}, f32[72,8,128]{2,1,0:T(8,128)}, u32[]{:S(2)}, u32[]{:S(2)}) collective-permute-start(f32[72,8,128]{2,1,0:T(8,128)S(1)} %constant_dynamic-update-slice_fusion.41.near_b), channel_id=1, source_target_pairs={{0,1},{1,0},{2,3},{3,2},{4,5},{5,4},{6,7},{7,6},{8,9},{9,8},{10,11... | collective-permute-start | bytes 884744 | tf_op jit(solution)/shard_map/ppermute | solution.py:223
  127.4 7.3 %collective-permute-start.37 = (f32[64,8,128]{2,1,0:T(8,128)S(1)}, f32[64,8,128]{2,1,0:T(8,128)}, u32[]{:S(2)}, u32[]{:S(2)}) collective-permute-start(f32[64,8,128]{2,1,0:T(8,128)S(1)} %constant_dynamic-update-slice_fusion.36.near_a), channel_id=1, source_target_pairs={{0,2},{1,3},{2,0},{3,1},{4,6},{5,7},{6,4},{7,5},{8,10},{9,11},{10,... | collective-permute-start | bytes 786440 | tf_op jit(solution)/shard_map/ppermute | solution.py:223
  132.5 18.3 %collective-permute-start.40 = (f32[64,2,8,128]{3,2,1,0:T(8,128)S(1)}, f32[64,2,8,128]{3,2,1,0:T(8,128)}, u32[]{:S(2)}, u32[]{:S(2)}) collective-permute-start(f32[64,2,8,128]{3,2,1,0:T(8,128)S(1)} %get-tuple-element.70), channel_id=1, source_target_pairs={{0,16},{16,0},{1,17},{17,1},{2,18},{18,2},{3,19},{19,3},{4,20},{20... | collective-permute-start | bytes 1572872 | tf_op jit(solution)/shard_map/ppermute | solution.py:226
  144.5 14.0 %collective-permute-start.42 = (f32[64,2,8,128]{3,2,1,0:T(8,128)S(1)}, f32[64,2,8,128]{3,2,1,0:T(8,128)S(1)}, u32[]{:S(2)}, u32[]{:S(2)}) collective-permute-start(f32[64,2,8,128]{3,2,1,0:T(8,128)S(1)} %get-tuple-element.72), channel_id=1, source_target_pairs={{0,16},{16,0},{1,17},{17,1},{2,18},{18,2},{3,19},{19,3},{4,20},{20... | collective-permute-start | bytes 1572872 | tf_op jit(solution)/shard_map/ppermute | solution.py:226
  146.1 12.1 %all-to-all-start = ((f32[16,8,128]{2,1,0:T(8,128)}), f32[16,8,128]{2,1,0:T(8,128)S(1)}, u32[]{:S(2)}, u32[]{:S(2)}) async-start(f32[16,8,128]{2,1,0:T(8,128)} %broadcast_in_dim.5), calls=%async_computation | async-start | bytes 131072 | tf_op jit(solution)/shard_map/all_to_all | solution.py:220
  (24 other events, 203.9 us)

commit v7 on v5

--- a/solution.py
+++ b/solution.py
@@ -76,7 +76,7 @@
         message[(i + 1) * tiles - extra : (i + 1) * tiles] = table[i]
 
 
-def start_kernel(nh, room, tiles, place, comp, message, block, r_out, answer, load, held, sems):
+def start_kernel(nh, room, tiles, lines, place, message, block, r_out, comp, answer, held, load, sems):
     pieces = sems.shape[0]
     size = block.shape[0] // pieces
     copies = []
@@ -85,24 +85,25 @@
         copies.append(pltpu.make_async_copy(block.at[rows], held.at[rows], sems.at[j]))
         copies[-1].start()
     load[...] = jnp.zeros_like(load)
-    nrow = r_out.shape[0]
     zero = jnp.zeros(r_out.shape[2:], jnp.float32)
 
     def pair(i, sums):
         gamma, energy = sums
+        comp[pl.ds(i * lines, lines)] = message[pl.ds(i * tiles + room * nh, lines)]
         for j in range(room):
             row = i * room + j
             r = message[pl.ds(i * tiles + j * nh, nh)]
             r_out[row] = r
             load[pl.ds(place[0, row], nh)] += r
-            c = comp[row]
             for h in range(nh):
+                line, sub = divmod(j * nh + h, SUBLANES)
+                c = message[i * tiles + room * nh + line, sub : sub + 1, :]
                 square = r[h] * r[h]
                 gamma = gamma + square
-                energy = energy + c[h : h + 1] * square
+                energy = energy + c * square
         return gamma, energy
 
-    gamma, energy = lax.fori_loop(0, nrow // room, pair, (zero, zero))
+    gamma, energy = lax.fori_loop(0, r_out.shape[0] // room, pair, (zero, zero))
     respond(held, load, gamma, energy, answer, copies)
 
 
@@ -120,13 +121,15 @@
     return gamma, gamma / (delta - beta * gamma / known[:, 1:2]), beta
 
 
-def home_kernel(first, nh, unroll, place, keep, picked, comp, own, near_a, far_a, near_b, far_b, known, block, *refs):
-    if first:
-        r_in, r, s, answer, part, known_out, load, resp = refs
-    else:
-        r_in, s_in, r, s, answer, part, known_out, load, resp = refs
+def home_kernel(first, last, nh, room, lines, place, keep, picked, comp, own, near_a, far_a, near_b, far_b, known, block, *refs):
+    r_in, *refs = refs
+    if not first:
+        s_in, *refs = refs
+    if not last:
+        r, s, *refs = refs
+    answer, part, known_out, load, resp = refs
     load[...] = jnp.zeros_like(load)
-    ncase, width = r.shape[2:]
+    nrow, _, ncase, width = r_in.shape
     at = 0
     for piece in (near_a, far_a, near_b, far_b):
         resp[at : at + piece.shape[0]] = piece[...]
@@ -146,24 +149,28 @@
 
     lax.fori_loop(0, part.shape[0], pick, 0, unroll=8)
 
-    def body(row, sums):
+    def pair(i, sums):
         gamma, energy = sums
-        near, far, on = place[0, row], place[1, row], keep[row]
-        c = comp[row]
-        for h in range(nh):
-            residual = r_in[row, h]
-            image = on * (own[near + h] + resp[far + h] + c[h : h + 1] * residual)
-            if not first:
-                image = image + beta * s_in[row, h]
-            residual = residual - alpha * image
-            r[row, h], s[row, h] = residual, image
-            load[near + h] += residual
-            square = residual * residual
-            gamma = gamma + square
-            energy = energy + c[h : h + 1] * square
+        for j in range(room):
+            row = i * room + j
+            near, far, on = place[0, row], place[1, row], keep[row]
+            for h in range(nh):
+                line, sub = divmod(j * nh + h, SUBLANES)
+                c = comp[i * lines + line, sub : sub + 1, :]
+                residual = r_in[row, h]
+                image = on * (own[near + h] + resp[far + h] + c * residual)
+                if not first:
+                    image = image + beta * s_in[row, h]
+                residual = residual - alpha * image
+                if not last:
+                    r[row, h], s[row, h] = residual, image
+                load[near + h] += residual
+                square = residual * residual
+                gamma = gamma + square
+                energy = energy + c * square
         return gamma, energy
 
-    gamma, energy = lax.fori_loop(0, r.shape[0], body, (zero, zero), unroll=unroll)
+    gamma, energy = lax.fori_loop(0, nrow // room, pair, (zero, zero))
     respond(block, load, gamma, energy, answer)
 
 
@@ -184,7 +191,6 @@
     tiles = room * nh + lines + deep
     nz = nsub // 4
     half = nslot // 2 * nh
-    unroll = 4
 
     def exchange(message):
         return lax.all_to_all(message, "sub", split_axis=0, concat_axis=0, tiled=True)
@@ -196,10 +202,9 @@
         return lax.ppermute(value, "body", [(i, nbody - 1 - i) for i in range(nbody)])
 
     keep = active.astype(jnp.float32)
-    owners = jnp.stack([plate_owner[:, 0], found_owner[:, 0]])
-    slots = slot_pairs.T
-    owner, other = jnp.where(side == 0, owners, owners[::-1])
-    slot, other_slot = jnp.where(side == 0, slots, slots[::-1])
+    plate, foundation = plate_owner[:, 0], found_owner[:, 0]
+    owner, other = jnp.where(side == 0, plate, foundation), jnp.where(side == 0, foundation, plate)
+    slot, other_slot = (jnp.where(side == i, slot_pairs[:, 0], slot_pairs[:, 1]) for i in range(2))
     index = jnp.arange(npatch, dtype=jnp.int32)
     earlier = (owner[None, :] == owner[:, None]) & (index[None, :] < index[:, None])
     rank = jnp.sum(earlier.astype(jnp.int32), axis=1)
@@ -234,7 +239,6 @@
     )
     message = exchange(message.reshape(nsub, tiles, ncase, LANES))
     told = message[:, room * nh :].reshape(nsub, (lines + deep) * SUBLANES, LANES)
-    comp = told[:, : room * nh].reshape(nrow, nh, LANES)
     named = told[:, lines * SUBLANES : lines * SUBLANES + room, :3].reshape(nrow, 3).T
     home = named[:2].astype(jnp.int32)
     on = named[2]
@@ -243,21 +247,21 @@
     answer = f32(per, ncase, LANES)
     load = pltpu.VMEM((nslot * nh, ncase, LANES), jnp.float32)
     spread = pltpu.VMEM((nsub * per, ncase, LANES), jnp.float32)
-    home_r, own = call(
-        functools.partial(start_kernel, nh, room, tiles),
-        (field, answer),
-        [SMEM, VMEM, VMEM, HBM],
+    home_r, comp, own, block = call(
+        functools.partial(start_kernel, nh, room, tiles, lines),
+        (field, f32(nsub * lines, ncase, LANES), answer, jax.ShapeDtypeStruct(block.shape, block.dtype)),
+        [SMEM, VMEM, HBM],
         home,
-        comp,
         message.reshape(nsub * tiles, ncase, LANES),
-        block,
-        scratch=[load, pltpu.VMEM(block.shape, block.dtype), pltpu.SemaphoreType.DMA((nslot,))],
+        pltpu.with_memory_space_constraint(block, pltpu.HBM),
+        scratch=[load, pltpu.SemaphoreType.DMA((nslot,))],
     )
     known = jnp.zeros((ncase, LANES), jnp.float32)
     state = [home_r]
     picked = found(me ^ other).astype(jnp.int32)
     r, d, x, s = start, None, None, None
     for step in range(ITERS - 1):
+        last = step == ITERS - 2
         far = sibling(own)
         far = jnp.concatenate([far[: per - 1], own[per - 1 :] + far[per - 1 :]])
         parts = [far] + [swap(far, 4 * z) for z in range(1, nz)]
@@ -267,8 +271,8 @@
         a, b = jnp.concatenate([a, far_a]), jnp.concatenate([b, far_b])
         far_a, far_b = swap(a, 2), swap(b, 1)
         *state, own, part, known = call(
-            functools.partial(home_kernel, step == 0, nh, unroll),
-            (field,) * 2 + (answer, f32(npatch, nh, ncase, LANES), f32(ncase, LANES)),
+            functools.partial(home_kernel, step == 0, last, nh, room, lines),
+            (field,) * (0 if last else 2) + (answer, f32(npatch, nh, ncase, LANES), f32(ncase, LANES)),
             [SMEM] * 3 + [VMEM] * (8 + len(state)),
             home,
             on,
@@ -294,6 +298,7 @@
             d, s = r + beta * d, image + beta * s
             x = x + alpha * d
         r = r - alpha * s
+        r, d, x, s = lax.optimization_barrier((r, d, x, s))
     sums = own[per - 1]
     sums = sums + sibling(sums)
     sums = tree([sums] + [swap(sums, i) for i in range(1, 4)])

time: 155 us -> 165 us (1.065)
  local copies, waits for them, and re-layouts: 11.1 us -> 21.5 us
  waiting for transfers between devices: 52.5 us -> 43 us
  other arithmetic: 4.57 us -> 10 us
  starting transfers between devices: 32.2 us -> 34.6 us
    ppermute x27, waiting for transfers between devices: 48.7 us -> 38.4 us  [swap(): return lax.ppermute(value, 'sub', [(i, i ^ far) for i in range(nsub)])]
    unnamed x9 -> x43, local copies, waits for them, and re-layouts: 7.01 us -> 12.9 us
    ppermute x27, starting transfers between devices: 31.4 us -> 34.5 us  [swap(): return lax.ppermute(value, 'sub', [(i, i ^ far) for i in range(nsub)])]
    add x0 -> x3, other arithmetic: none -> 2.8 us  [the longest x2 2.79 us: on_device(): x = x + alpha * d]
    reshape x3, local copies, waits for them, and re-layouts: 1.26 us -> 3.89 us  [on_device(): jnp.transpose(part + sibling(part), (2, 0, 1, 3))]
    sub x0 -> x1, other arithmetic: none -> 2.56 us  [on_device(): r = r - alpha * s]
    concatenate x6, local copies, waits for them, and re-layouts: 0.06 us -> 1.88 us  [on_device(): a, b = (jnp.concatenate([a, far_a]), jnp.concatenate([b, far_b]))]
  transfers between devices with their start and end apart: 34 -> 34, of which waited for: 21 -> 18; matrix products, arithmetic and copies ran while one was open for 2% -> 9% of each run, Pallas kernels for 2% -> 4%
where the time goes in v7:
time: 165 us; the launch traced here: 164 us
  waiting for transfers between devices  43 us (26%)
  blocking collectives  39.4 us (24%)
  starting transfers between devices  34.6 us (21%)
  local copies, waits for them, and re-layouts  21.5 us (13%)
  Pallas kernels  14.4 us (9%)
  other arithmetic  10 us (6%)
    all_to_all x1, blocking collectives, exchange(): lax.all_to_all(message, 'sub', split_axis=0, concat_axis=0, tiled=True)  39.4 us
    ppermute x27, waiting for transfers between devices, swap(): return lax.ppermute(value, 'sub', [(i, i ^ far) for i in range(nsub)])  38.4 us
    ppermute x27, starting transfers between devices, swap(): return lax.ppermute(value, 'sub', [(i, i ^ far) for i in range(nsub)])  34.5 us
    pallas_call x5, Pallas kernels, call(): pl.pallas_call(kernel, out_shape=tuple(out_shape) if several else out_sha...  14.4 us
    unnamed x43, local copies, waits for them, and re-layouts  12.9 us
    ppermute x7, waiting for transfers between devices, sibling(): lax.ppermute(value, 'body', [(i, nbody - 1 - i) for i in range(nbody)])  4.54 us
    reshape x3, local copies, waits for them, and re-layouts, on_device(): jnp.transpose(part + sibling(part), (2, 0, 1, 3))  3.89 us
  transfers between devices with their start and end apart: 34, of which 18 were waited for; matrix products, arithmetic and copies ran while one was open for 9% of the time, Pallas kernels for 4%

profile of v7, /device:TPU:0, one launch (start us, length us, event | category | flops | bytes accessed | tf_op | source)
XLA Modules:
  0.0 164.4 jit_solution(11274554792958806828)
XLA Ops:
  4.6 39.4 %all_to_all.5 = f32[16,19,8,128]{3,2,1,0:T(8,128)S(1)} all-to-all(f32[16,19,8,128]{3,2,1,0:T(8,128)S(1)} %bitcast.74), channel_id=1, replica_groups=mesh['body'=2,'sub'=16] {'sub'}, dimensions={0} | all-to-all | bytes 2490368 | tf_op jit(solution)/shard_map/all_to_all | solution.py:196
  44.0 4.4 %shard_map.74 = (f32[128,2,8,128]{3,2,1,0:T(8,128)S(1)}, f32[32,8,128]{2,1,0:T(8,128)S(1)}, f32[17,8,128]{2,1,0:T(8,128)S(1)}, bf16[2048,2048]{1,0:T(8,128)(2,1)S(1)}) custom-call(s32[2,128]{1,0:T(2,128)S(1)} %slice_convert_fusion.place, f32[304,8,128]{2,1,0:T(8,128)S(1)} %bitcast.73, bf16[2048,2048]{1,0:T(8,128)(2,1)} %bitcast.76), custom_call_target="tpu_custom_call" | custom-call | tf_op jit(solution)/shard_map/pallas_call | solution.py:25
  48.4 3.3 %copy-done = bf16[2048,2048]{1,0:T(8,128)(2,1)} copy-done((bf16[2048,2048]{1,0:T(8,128)(2,1)}, bf16[2048,2048]{1,0:T(8,128)(2,1)S(1)}, u32[]{:S(2)}) %copy-start) | copy-done | bytes 8388632
  55.2 2.2 %collective-permute-start.3 = (f32[17,8,128]{2,1,0:T(8,128)S(1)}, f32[17,8,128]{2,1,0:T(8,128)S(1)}, u32[]{:S(2)}, u32[]{:S(2)}) collective-permute-start(f32[17,8,128]{2,1,0:T(8,128)S(1)} %pad_maximum_fusion.6), channel_id=1, source_target_pairs={{0,12},{1,13},{2,14},{3,15},{4,8},{5,9},{6,10},{7,11},{8,4},{9,5},... | collective-permute-start | bytes 208904 | tf_op jit(solution)/shard_map/ppermute | solution.py:199
  58.1 4.4 %collective-permute-done.2 = f32[17,8,128]{2,1,0:T(8,128)S(1)} collective-permute-done((f32[17,8,128]{2,1,0:T(8,128)S(1)}, f32[17,8,128]{2,1,0:T(8,128)S(1)}, u32[]{:S(2)}, u32[]{:S(2)}) %collective-permute-start.2) | collective-permute-done | bytes 69664 | tf_op jit(solution)/shard_map/ppermute | solution.py:199
  64.0 3.6 %collective-permute-done.4 = f32[32,8,128]{2,1,0:T(8,128)S(1)} collective-permute-done((f32[32,8,128]{2,1,0:T(8,128)S(1)}, f32[32,8,128]{2,1,0:T(8,128)S(1)}, u32[]{:S(2)}, u32[]{:S(2)}) %collective-permute-start.4) | collective-permute-done | bytes 131104 | tf_op jit(solution)/shard_map/ppermute | solution.py:199
  68.3 1.6 collective-permute-done.6
  70.0 1.6 collective-permute-start.7
  71.6 2.5 %collective-permute-done.5.far_a = f32[64,8,128]{2,1,0:T(8,128)S(1)} collective-permute-done((f32[64,8,128]{2,1,0:T(8,128)S(1)}, f32[64,8,128]{2,1,0:T(8,128)S(1)}, u32[]{:S(2)}, u32[]{:S(2)}) %collective-permute-start.5) | collective-permute-done | bytes 262176 | tf_op jit(solution)/shard_map/ppermute | solution.py:199
  74.1 2.7 %collective-permute-done.7.far_b = f32[72,8,128]{2,1,0:T(8,128)S(1)} collective-permute-done((f32[72,8,128]{2,1,0:T(8,128)S(1)}, f32[72,8,128]{2,1,0:T(8,128)S(1)}, u32[]{:S(2)}, u32[]{:S(2)}) %collective-permute-start.7) | collective-permute-done | bytes 294944 | tf_op jit(solution)/shard_map/ppermute | solution.py:199
  76.8 3.4 %copy-done.1 = bf16[2048,2048]{1,0:T(8,128)(2,1)S(1)} copy-done((bf16[2048,2048]{1,0:T(8,128)(2,1)S(1)}, bf16[2048,2048]{1,0:T(8,128)(2,1)}, u32[]{:S(2)}) %copy-start.1) | copy-done | bytes 8388632
  80.1 2.9 %shard_map.75 = (f32[128,2,8,128]{3,2,1,0:T(8,128)S(1)}, f32[128,2,8,128]{3,2,1,0:T(8,128)S(1)}, f32[17,8,128]{2,1,0:T(8,128)S(1)}, f32[64,2,8,128]{3,2,1,0:T(8,128)S(1)}, f32[8,128]{1,0:T(8,128)S(1)}) custom-call(s32[2,128]{1,0:T(2,128)S(1)} %slice_convert_fusion.place, f32[128]{0:T(128)S(1)} %slice_bitcast_fusion.3.keep, s32[64]{0:T(128)S(1)} %bitcast_select_fusion.picked, ...), custom_call_target="tpu_custom_call" | custom-call | tf_op jit(solution)/shard_map/pallas_call | solution.py:25
  84.9 1.7 %collective-permute-start.11 = (f32[17,8,128]{2,1,0:T(8,128)S(1)}, f32[17,8,128]{2,1,0:T(8,128)S(1)}, u32[]{:S(2)}, u32[]{:S(2)}) collective-permute-start(f32[17,8,128]{2,1,0:T(8,128)S(1)} %pad_maximum_fusion.7), channel_id=1, source_target_pairs={{0,8},{1,9},{2,10},{3,11},{4,12},{5,13},{6,14},{7,15},{8,0},{9,1},... | collective-permute-start | bytes 208904 | tf_op jit(solution)/shard_map/ppermute | solution.py:199
  86.6 2.3 %collective-permute-start.12 = (f32[17,8,128]{2,1,0:T(8,128)S(1)}, f32[17,8,128]{2,1,0:T(8,128)S(1)}, u32[]{:S(2)}, u32[]{:S(2)}) collective-permute-start(f32[17,8,128]{2,1,0:T(8,128)S(1)} %pad_maximum_fusion.7), channel_id=1, source_target_pairs={{0,12},{1,13},{2,14},{3,15},{4,8},{5,9},{6,10},{7,11},{8,4},{9,5},... | collective-permute-start | bytes 208904 | tf_op jit(solution)/shard_map/ppermute | solution.py:199
  89.6 3.9 %collective-permute-done.11 = f32[17,8,128]{2,1,0:T(8,128)S(1)} collective-permute-done((f32[17,8,128]{2,1,0:T(8,128)S(1)}, f32[17,8,128]{2,1,0:T(8,128)S(1)}, u32[]{:S(2)}, u32[]{:S(2)}) %collective-permute-start.11) | collective-permute-done | bytes 69664 | tf_op jit(solution)/shard_map/ppermute | solution.py:199
  94.5 1.7 %collective-permute-start.13 = (f32[32,8,128]{2,1,0:T(8,128)S(1)}, f32[32,8,128]{2,1,0:T(8,128)S(1)}, u32[]{:S(2)}, u32[]{:S(2)}) collective-permute-start(f32[32,8,128]{2,1,0:T(8,128)S(1)} %pad_maximum_fusion.4), channel_id=1, source_target_pairs={{0,1},{1,0},{2,3},{3,2},{4,5},{5,4},{6,7},{7,6},{8,9},{9,8},{10,11... | collective-permute-start | bytes 393224 | tf_op jit(solution)/shard_map/ppermute | solution.py:199
  96.2 2.5 %collective-permute-done.15 = f32[36,8,128]{2,1,0:T(8,128)S(1)} collective-permute-done((f32[36,8,128]{2,1,0:T(8,128)S(1)}, f32[36,8,128]{2,1,0:T(8,128)S(1)}, u32[]{:S(2)}, u32[]{:S(2)}) %collective-permute-start.15) | collective-permute-done | bytes 147488 | tf_op jit(solution)/shard_map/ppermute | solution.py:199
  98.7 2.0 %collective-permute-start.16 = (f32[72,8,128]{2,1,0:T(8,128)S(1)}, f32[72,8,128]{2,1,0:T(8,128)S(1)}, u32[]{:S(2)}, u32[]{:S(2)}) collective-permute-start(f32[72,8,128]{2,1,0:T(8,128)S(1)} %constant_dynamic-update-slice_fusion.15.near_b), channel_id=1, source_target_pairs={{0,1},{1,0},{2,3},{3,2},{4,5},{5,4},{6,7},{7,6},{8,9},{9,8},{10,11... | collective-permute-start | bytes 884744 | tf_op jit(solution)/shard_map/ppermute | solution.py:199
  101.4 5.8 %collective-permute-done.14.far_a = f32[64,8,128]{2,1,0:T(8,128)S(1)} collective-permute-done((f32[64,8,128]{2,1,0:T(8,128)S(1)}, f32[64,8,128]{2,1,0:T(8,128)S(1)}, u32[]{:S(2)}, u32[]{:S(2)}) %collective-permute-start.14) | collective-permute-done | bytes 262176 | tf_op jit(solution)/shard_map/ppermute | solution.py:199
  107.2 3.1 %shard_map.76 = (f32[128,2,8,128]{3,2,1,0:T(8,128)S(1)}, f32[128,2,8,128]{3,2,1,0:T(8,128)S(1)}, f32[17,8,128]{2,1,0:T(8,128)S(1)}, f32[64,2,8,128]{3,2,1,0:T(8,128)S(1)}, f32[8,128]{1,0:T(8,128)S(1)}) custom-call(s32[2,128]{1,0:T(2,128)S(1)} %slice_convert_fusion.place, f32[128]{0:T(128)S(1)} %slice_bitcast_fusion.3.keep, s32[64]{0:T(128)S(1)} %bitcast_select_fusion.picked, ...), custom_call_target="tpu_custom_call" | custom-call | tf_op jit(solution)/shard_map/pallas_call | solution.py:25
  111.6 1.4 collective-permute-start.19
  113.9 2.2 %collective-permute-start.21 = (f32[17,8,128]{2,1,0:T(8,128)S(1)}, f32[17,8,128]{2,1,0:T(8,128)S(1)}, u32[]{:S(2)}, u32[]{:S(2)}) collective-permute-start(f32[17,8,128]{2,1,0:T(8,128)S(1)} %pad_maximum_fusion.8), channel_id=1, source_target_pairs={{0,12},{1,13},{2,14},{3,15},{4,8},{5,9},{6,10},{7,11},{8,4},{9,5},... | collective-permute-start | bytes 208904 | tf_op jit(solution)/shard_map/ppermute | solution.py:199
  116.1 5.4 %collective-permute-done.20 = f32[17,8,128]{2,1,0:T(8,128)S(1)} collective-permute-done((f32[17,8,128]{2,1,0:T(8,128)S(1)}, f32[17,8,128]{2,1,0:T(8,128)S(1)}, u32[]{:S(2)}, u32[]{:S(2)}) %collective-permute-start.20) | collective-permute-done | bytes 69664 | tf_op jit(solution)/shard_map/ppermute | solution.py:199
  126.2 2.2 %reshape.93 = f32[8,64,256]{2,1,0:T(8,128)} reshape(f32[8,64,2,128]{3,2,1,0:T(2,128)} %copy.19) | data formatting | bytes 1048576 | tf_op jit(solution)/shard_map/reshape | solution.py:291
  132.3 2.6 %multiply_subtract_fusion.2 = (f32[8,64,256]{2,1,0:T(8,128)}, f32[8,64,256]{2,1,0:T(8,128)}, f32[8,64,256]{2,1,0:T(8,128)}) fusion(f32[8]{0:T(128)S(1)} %slice_reduce_fusion.3, f32[8,64,256]{2,1,0:T(8,128)} %reshape.93, f32[64,256]{1,0:T(8,128)S(1)} %copy-done.17, f32[64]{0:T(128)S(1)} %get-tuple-element.136, f32[8,64,256]{2,1,0:T(8,128)} %param.7), kind=kLoop, calls=%fused_computation.13 | loop fusion | flops 917504 | bytes 2687264 | tf_op jit(solution)/shard_map/sub | solution.py:300
  134.9 2.8 %collective-permute-done.23.far_a = f32[64,8,128]{2,1,0:T(8,128)S(1)} collective-permute-done((f32[64,8,128]{2,1,0:T(8,128)S(1)}, f32[64,8,128]{2,1,0:T(8,128)S(1)}, u32[]{:S(2)}, u32[]{:S(2)}) %collective-permute-start.23) | collective-permute-done | bytes 262176 | tf_op jit(solution)/shard_map/ppermute | solution.py:199
  137.7 3.4 %copy-done.3 = bf16[2048,2048]{1,0:T(8,128)(2,1)S(1)} copy-done((bf16[2048,2048]{1,0:T(8,128)(2,1)S(1)}, bf16[2048,2048]{1,0:T(8,128)(2,1)}, u32[]{:S(2)}) %copy-start.3) | copy-done | bytes 8388632
  143.0 3.2 %shard_map.77 = (f32[17,8,128]{2,1,0:T(8,128)S(1)}, f32[64,2,8,128]{3,2,1,0:T(8,128)S(1)}, f32[8,128]{1,0:T(8,128)S(1)}) custom-call(s32[2,128]{1,0:T(2,128)S(1)} %slice_convert_fusion.place, f32[128]{0:T(128)S(1)} %slice_bitcast_fusion.3.keep, s32[64]{0:T(128)S(1)} %bitcast_select_fusion.picked, f32[32,8,128]{2,1,0:T(8,128)S(1)} %get-tuple-element.33.comp, ...), custom_call_target="tpu_custom_call" | custom-call | tf_op jit(solution)/shard_map/pallas_call | solution.py:25
  149.0 1.8 %collective-permute-start.30 = (f32[8,128]{1,0:T(8,128)S(1)}, f32[8,128]{1,0:T(8,128)S(1)}, u32[]{:S(2)}, u32[]{:S(2)}) collective-permute-start(f32[8,128]{1,0:T(8,128)S(1)} %fusion.19), channel_id=1, source_target_pairs={{0,3},{1,2},{2,1},{3,0},{4,7},{5,6},{6,5},{7,4},{8,11},{9,10},{10,... | collective-permute-start | bytes 12296 | tf_op jit(solution)/shard_map/ppermute | solution.py:199
  153.5 2.1 %collective-permute-start.31 = (f32[8,128]{1,0:T(8,128)S(1)}, f32[8,128]{1,0:T(8,128)S(1)}, u32[]{:S(2)}, u32[]{:S(2)}) collective-permute-start(f32[8,128]{1,0:T(8,128)S(1)} %add_add_fusion.1), channel_id=1, source_target_pairs={{0,4},{1,5},{2,6},{3,7},{4,0},{5,1},{6,2},{7,3},{8,12},{9,13},{10,... | collective-permute-start | bytes 12296 | tf_op jit(solution)/shard_map/ppermute | solution.py:199
  156.0 2.1 %collective-permute-start.33 = (f32[8,128]{1,0:T(8,128)S(1)}, f32[8,128]{1,0:T(8,128)S(1)}, u32[]{:S(2)}, u32[]{:S(2)}) collective-permute-start(f32[8,128]{1,0:T(8,128)S(1)} %add_add_fusion.1), channel_id=1, source_target_pairs={{0,12},{1,13},{2,14},{3,15},{4,8},{5,9},{6,10},{7,11},{8,4},{9,5},... | collective-permute-start | bytes 12296 | tf_op jit(solution)/shard_map/ppermute | solution.py:199
  158.1 2.4 %multiply_add_fusion.4 = (f32[8,64,256]{2,1,0:T(8,128)S(1)}, f32[8,64,256]{2,1,0:T(8,128)}, f32[8,64,256]{2,1,0:T(8,128)}, f32[8,64,256]{2,1,0:T(8,128)}) fusion(f32[8,64,256]{2,1,0:T(8,128)S(1)} %copy-done.13, f32[8]{0:T(128)S(1)} %get-tuple-element.65, f32[8,64,256]{2,1,0:T(8,128)S(1)} %copy-done.11, f32[8,64,256]{2,1,0:T(8,128)S(1)} %copy-done.9, ...), kind=kLoop, calls=%fused_computation.8 | loop fusion | flops 1441792 | bytes 4784448 | tf_op jit(solution)/shard_map/add | solution.py:299
  (171 shorter events, 37.4 us)
Async XLA Ops:
  53.0 5.1 %collective-permute-start.1 = (f32[17,8,128]{2,1,0:T(8,128)S(1)}, f32[17,8,128]{2,1,0:T(8,128)S(1)}, u32[]{:S(2)}, u32[]{:S(2)}) collective-permute-start(f32[17,8,128]{2,1,0:T(8,128)S(1)} %pad_maximum_fusion.6), channel_id=1, source_target_pairs={{0,4},{1,5},{2,6},{3,7},{4,0},{5,1},{6,2},{7,3},{8,12},{9,13},{10,... | collective-permute-start | bytes 208904 | tf_op jit(solution)/shard_map/ppermute | solution.py:199
  53.9 8.6 %collective-permute-start.2 = (f32[17,8,128]{2,1,0:T(8,128)S(1)}, f32[17,8,128]{2,1,0:T(8,128)S(1)}, u32[]{:S(2)}, u32[]{:S(2)}) collective-permute-start(f32[17,8,128]{2,1,0:T(8,128)S(1)} %pad_maximum_fusion.6), channel_id=1, source_target_pairs={{0,8},{1,9},{2,10},{3,11},{4,12},{5,13},{6,14},{7,15},{8,0},{9,1},... | collective-permute-start | bytes 208904 | tf_op jit(solution)/shard_map/ppermute | solution.py:199
  55.2 7.3 %collective-permute-start.3 = (f32[17,8,128]{2,1,0:T(8,128)S(1)}, f32[17,8,128]{2,1,0:T(8,128)S(1)}, u32[]{:S(2)}, u32[]{:S(2)}) collective-permute-start(f32[17,8,128]{2,1,0:T(8,128)S(1)} %pad_maximum_fusion.6), channel_id=1, source_target_pairs={{0,12},{1,13},{2,14},{3,15},{4,8},{5,9},{6,10},{7,11},{8,4},{9,5},... | collective-permute-start | bytes 208904 | tf_op jit(solution)/shard_map/ppermute | solution.py:199
  62.5 5.1 %collective-permute-start.4 = (f32[32,8,128]{2,1,0:T(8,128)S(1)}, f32[32,8,128]{2,1,0:T(8,128)S(1)}, u32[]{:S(2)}, u32[]{:S(2)}) collective-permute-start(f32[32,8,128]{2,1,0:T(8,128)S(1)} %pad_maximum_fusion.3), channel_id=1, source_target_pairs={{0,1},{1,0},{2,3},{3,2},{4,5},{5,4},{6,7},{7,6},{8,9},{9,8},{10,11... | collective-permute-start | bytes 393224 | tf_op jit(solution)/shard_map/ppermute | solution.py:199
  63.2 6.7 %collective-permute-start.6 = (f32[36,8,128]{2,1,0:T(8,128)S(1)}, f32[36,8,128]{2,1,0:T(8,128)S(1)}, u32[]{:S(2)}, u32[]{:S(2)}) collective-permute-start(f32[36,8,128]{2,1,0:T(8,128)S(1)} %pad_maximum_fusion), channel_id=1, source_target_pairs={{0,2},{1,3},{2,0},{3,1},{4,6},{5,7},{6,4},{7,5},{8,10},{9,11},{10,... | collective-permute-start | bytes 442376 | tf_op jit(solution)/shard_map/ppermute | solution.py:199
  67.6 6.4 %collective-permute-start.5 = (f32[64,8,128]{2,1,0:T(8,128)S(1)}, f32[64,8,128]{2,1,0:T(8,128)S(1)}, u32[]{:S(2)}, u32[]{:S(2)}) collective-permute-start(f32[64,8,128]{2,1,0:T(8,128)S(1)} %constant_dynamic-update-slice_fusion.near_a), channel_id=1, source_target_pairs={{0,2},{1,3},{2,0},{3,1},{4,6},{5,7},{6,4},{7,5},{8,10},{9,11},{10,... | collective-permute-start | bytes 786440 | tf_op jit(solution)/shard_map/ppermute | solution.py:199
  70.0 6.8 %collective-permute-start.7 = (f32[72,8,128]{2,1,0:T(8,128)S(1)}, f32[72,8,128]{2,1,0:T(8,128)S(1)}, u32[]{:S(2)}, u32[]{:S(2)}) collective-permute-start(f32[72,8,128]{2,1,0:T(8,128)S(1)} %constant_dynamic-update-slice_fusion.5.near_b), channel_id=1, source_target_pairs={{0,1},{1,0},{2,3},{3,2},{4,5},{5,4},{6,7},{7,6},{8,9},{9,8},{10,11... | collective-permute-start | bytes 884744 | tf_op jit(solution)/shard_map/ppermute | solution.py:199
  83.1 1.3 collective-permute-start.9
  84.4 5.1 %collective-permute-start.10 = (f32[17,8,128]{2,1,0:T(8,128)S(1)}, f32[17,8,128]{2,1,0:T(8,128)S(1)}, u32[]{:S(2)}, u32[]{:S(2)}) collective-permute-start(f32[17,8,128]{2,1,0:T(8,128)S(1)} %pad_maximum_fusion.7), channel_id=1, source_target_pairs={{0,4},{1,5},{2,6},{3,7},{4,0},{5,1},{6,2},{7,3},{8,12},{9,13},{10,... | collective-permute-start | bytes 208904 | tf_op jit(solution)/shard_map/ppermute | solution.py:199
  84.9 8.6 %collective-permute-start.11 = (f32[17,8,128]{2,1,0:T(8,128)S(1)}, f32[17,8,128]{2,1,0:T(8,128)S(1)}, u32[]{:S(2)}, u32[]{:S(2)}) collective-permute-start(f32[17,8,128]{2,1,0:T(8,128)S(1)} %pad_maximum_fusion.7), channel_id=1, source_target_pairs={{0,8},{1,9},{2,10},{3,11},{4,12},{5,13},{6,14},{7,15},{8,0},{9,1},... | collective-permute-start | bytes 208904 | tf_op jit(solution)/shard_map/ppermute | solution.py:199
  86.6 6.9 %collective-permute-start.12 = (f32[17,8,128]{2,1,0:T(8,128)S(1)}, f32[17,8,128]{2,1,0:T(8,128)S(1)}, u32[]{:S(2)}, u32[]{:S(2)}) collective-permute-start(f32[17,8,128]{2,1,0:T(8,128)S(1)} %pad_maximum_fusion.7), channel_id=1, source_target_pairs={{0,12},{1,13},{2,14},{3,15},{4,8},{5,9},{6,10},{7,11},{8,4},{9,5},... | collective-permute-start | bytes 208904 | tf_op jit(solution)/shard_map/ppermute | solution.py:199
  93.5 5.2 %collective-permute-start.15 = (f32[36,8,128]{2,1,0:T(8,128)S(1)}, f32[36,8,128]{2,1,0:T(8,128)S(1)}, u32[]{:S(2)}, u32[]{:S(2)}) collective-permute-start(f32[36,8,128]{2,1,0:T(8,128)S(1)} %pad_maximum_fusion.1), channel_id=1, source_target_pairs={{0,2},{1,3},{2,0},{3,1},{4,6},{5,7},{6,4},{7,5},{8,10},{9,11},{10,... | collective-permute-start | bytes 442376 | tf_op jit(solution)/shard_map/ppermute | solution.py:199
  94.5 6.2 %collective-permute-start.13 = (f32[32,8,128]{2,1,0:T(8,128)S(1)}, f32[32,8,128]{2,1,0:T(8,128)S(1)}, u32[]{:S(2)}, u32[]{:S(2)}) collective-permute-start(f32[32,8,128]{2,1,0:T(8,128)S(1)} %pad_maximum_fusion.4), channel_id=1, source_target_pairs={{0,1},{1,0},{2,3},{3,2},{4,5},{5,4},{6,7},{7,6},{8,9},{9,8},{10,11... | collective-permute-start | bytes 393224 | tf_op jit(solution)/shard_map/ppermute | solution.py:199
  98.7 8.4 %collective-permute-start.16 = (f32[72,8,128]{2,1,0:T(8,128)S(1)}, f32[72,8,128]{2,1,0:T(8,128)S(1)}, u32[]{:S(2)}, u32[]{:S(2)}) collective-permute-start(f32[72,8,128]{2,1,0:T(8,128)S(1)} %constant_dynamic-update-slice_fusion.15.near_b), channel_id=1, source_target_pairs={{0,1},{1,0},{2,3},{3,2},{4,5},{5,4},{6,7},{7,6},{8,9},{9,8},{10,11... | collective-permute-start | bytes 884744 | tf_op jit(solution)/shard_map/ppermute | solution.py:199
  100.7 6.4 %collective-permute-start.14 = (f32[64,8,128]{2,1,0:T(8,128)S(1)}, f32[64,8,128]{2,1,0:T(8,128)S(1)}, u32[]{:S(2)}, u32[]{:S(2)}) collective-permute-start(f32[64,8,128]{2,1,0:T(8,128)S(1)} %constant_dynamic-update-slice_fusion.10.near_a), channel_id=1, source_target_pairs={{0,2},{1,3},{2,0},{3,1},{4,6},{5,7},{6,4},{7,5},{8,10},{9,11},{10,... | collective-permute-start | bytes 786440 | tf_op jit(solution)/shard_map/ppermute | solution.py:199
  101.4 23.7 %collective-permute-start.8 = (f32[64,2,8,128]{3,2,1,0:T(8,128)S(1)}, f32[64,2,8,128]{3,2,1,0:T(8,128)S(1)}, u32[]{:S(2)}, u32[]{:S(2)}) collective-permute-start(f32[64,2,8,128]{3,2,1,0:T(8,128)S(1)} %get-tuple-element.38), channel_id=1, source_target_pairs={{0,16},{16,0},{1,17},{17,1},{2,18},{18,2},{3,19},{19,3},{4,20},{20... | collective-permute-start | bytes 1572872 | tf_op jit(solution)/shard_map/ppermute | solution.py:202
  110.3 1.3 collective-permute-start.18
  111.6 4.5 %collective-permute-start.19 = (f32[17,8,128]{2,1,0:T(8,128)S(1)}, f32[17,8,128]{2,1,0:T(8,128)S(1)}, u32[]{:S(2)}, u32[]{:S(2)}) collective-permute-start(f32[17,8,128]{2,1,0:T(8,128)S(1)} %pad_maximum_fusion.8), channel_id=1, source_target_pairs={{0,4},{1,5},{2,6},{3,7},{4,0},{5,1},{6,2},{7,3},{8,12},{9,13},{10,... | collective-permute-start | bytes 208904 | tf_op jit(solution)/shard_map/ppermute | solution.py:199
  113.1 8.4 %collective-permute-start.20 = (f32[17,8,128]{2,1,0:T(8,128)S(1)}, f32[17,8,128]{2,1,0:T(8,128)S(1)}, u32[]{:S(2)}, u32[]{:S(2)}) collective-permute-start(f32[17,8,128]{2,1,0:T(8,128)S(1)} %pad_maximum_fusion.8), channel_id=1, source_target_pairs={{0,8},{1,9},{2,10},{3,11},{4,12},{5,13},{6,14},{7,15},{8,0},{9,1},... | collective-permute-start | bytes 208904 | tf_op jit(solution)/shard_map/ppermute | solution.py:199
  113.9 7.6 %collective-permute-start.21 = (f32[17,8,128]{2,1,0:T(8,128)S(1)}, f32[17,8,128]{2,1,0:T(8,128)S(1)}, u32[]{:S(2)}, u32[]{:S(2)}) collective-permute-start(f32[17,8,128]{2,1,0:T(8,128)S(1)} %pad_maximum_fusion.8), channel_id=1, source_target_pairs={{0,12},{1,13},{2,14},{3,15},{4,8},{5,9},{6,10},{7,11},{8,4},{9,5},... | collective-permute-start | bytes 208904 | tf_op jit(solution)/shard_map/ppermute | solution.py:199
  122.2 6.3 %collective-permute-start.24 = (f32[36,8,128]{2,1,0:T(8,128)}, f32[36,8,128]{2,1,0:T(8,128)}, u32[]{:S(2)}, u32[]{:S(2)}) collective-permute-start(f32[36,8,128]{2,1,0:T(8,128)} %pad_maximum_fusion.2), channel_id=1, source_target_pairs={{0,2},{1,3},{2,0},{3,1},{4,6},{5,7},{6,4},{7,5},{8,10},{9,11},{10,... | collective-permute-start | bytes 442376 | tf_op jit(solution)/shard_map/ppermute | solution.py:199
  123.9 6.4 %collective-permute-start.22 = (f32[32,8,128]{2,1,0:T(8,128)}, f32[32,8,128]{2,1,0:T(8,128)}, u32[]{:S(2)}, u32[]{:S(2)}) collective-permute-start(f32[32,8,128]{2,1,0:T(8,128)} %pad_maximum_fusion.5), channel_id=1, source_target_pairs={{0,1},{1,0},{2,3},{3,2},{4,5},{5,4},{6,7},{7,6},{8,9},{9,8},{10,11... | collective-permute-start | bytes 393224 | tf_op jit(solution)/shard_map/ppermute | solution.py:199
  129.4 8.3 %collective-permute-start.25 = (f32[72,8,128]{2,1,0:T(8,128)S(1)}, f32[72,8,128]{2,1,0:T(8,128)S(1)}, u32[]{:S(2)}, u32[]{:S(2)}) collective-permute-start(f32[72,8,128]{2,1,0:T(8,128)S(1)} %constant_dynamic-update-slice_fusion.25.near_b), channel_id=1, source_target_pairs={{0,1},{1,0},{2,3},{3,2},{4,5},{5,4},{6,7},{7,6},{8,9},{9,8},{10,11... | collective-permute-start | bytes 884744 | tf_op jit(solution)/shard_map/ppermute | solution.py:199
  131.2 6.4 %collective-permute-start.23 = (f32[64,8,128]{2,1,0:T(8,128)S(1)}, f32[64,8,128]{2,1,0:T(8,128)S(1)}, u32[]{:S(2)}, u32[]{:S(2)}) collective-permute-start(f32[64,8,128]{2,1,0:T(8,128)S(1)} %constant_dynamic-update-slice_fusion.20.near_a), channel_id=1, source_target_pairs={{0,2},{1,3},{2,0},{3,1},{4,6},{5,7},{6,4},{7,5},{8,10},{9,11},{10,... | collective-permute-start | bytes 786440 | tf_op jit(solution)/shard_map/ppermute | solution.py:199
  134.9 15.9 %collective-permute-start.17 = (f32[64,2,8,128]{3,2,1,0:T(8,128)S(1)}, f32[64,2,8,128]{3,2,1,0:T(8,128)S(1)}, u32[]{:S(2)}, u32[]{:S(2)}) collective-permute-start(f32[64,2,8,128]{3,2,1,0:T(8,128)S(1)} %get-tuple-element.44), channel_id=1, source_target_pairs={{0,16},{16,0},{1,17},{17,1},{2,18},{18,2},{3,19},{19,3},{4,20},{20... | collective-permute-start | bytes 1572872 | tf_op jit(solution)/shard_map/ppermute | solution.py:202
  147.3 5.1 %collective-permute-start.28 = (f32[8,128]{1,0:T(8,128)S(1)}, f32[8,128]{1,0:T(8,128)S(1)}, u32[]{:S(2)}, u32[]{:S(2)}) collective-permute-start(f32[8,128]{1,0:T(8,128)S(1)} %fusion.19), channel_id=1, source_target_pairs={{0,1},{1,0},{2,3},{3,2},{4,5},{5,4},{6,7},{7,6},{8,9},{9,8},{10,11... | collective-permute-start | bytes 12296 | tf_op jit(solution)/shard_map/ppermute | solution.py:199
  148.5 3.9 %collective-permute-start.29 = (f32[8,128]{1,0:T(8,128)S(1)}, f32[8,128]{1,0:T(8,128)S(1)}, u32[]{:S(2)}, u32[]{:S(2)}) collective-permute-start(f32[8,128]{1,0:T(8,128)S(1)} %fusion.19), channel_id=1, source_target_pairs={{0,2},{1,3},{2,0},{3,1},{4,6},{5,7},{6,4},{7,5},{8,10},{9,11},{10,... | collective-permute-start | bytes 12296 | tf_op jit(solution)/shard_map/ppermute | solution.py:199
  149.0 4.5 %collective-permute-start.30 = (f32[8,128]{1,0:T(8,128)S(1)}, f32[8,128]{1,0:T(8,128)S(1)}, u32[]{:S(2)}, u32[]{:S(2)}) collective-permute-start(f32[8,128]{1,0:T(8,128)S(1)} %fusion.19), channel_id=1, source_target_pairs={{0,3},{1,2},{2,1},{3,0},{4,7},{5,6},{6,5},{7,4},{8,11},{9,10},{10,... | collective-permute-start | bytes 12296 | tf_op jit(solution)/shard_map/ppermute | solution.py:199
  152.5 9.2 %collective-permute-start.26 = (f32[64,2,8,128]{3,2,1,0:T(8,128)S(1)}, f32[64,2,8,128]{3,2,1,0:T(8,128)S(1)}, u32[]{:S(2)}, u32[]{:S(2)}) collective-permute-start(f32[64,2,8,128]{3,2,1,0:T(8,128)S(1)} %get-tuple-element.53), channel_id=1, source_target_pairs={{0,16},{16,0},{1,17},{17,1},{2,18},{18,2},{3,19},{19,3},{4,20},{20... | collective-permute-start | bytes 1572872 | tf_op jit(solution)/shard_map/ppermute | solution.py:202
  153.5 7.0 %collective-permute-start.31 = (f32[8,128]{1,0:T(8,128)S(1)}, f32[8,128]{1,0:T(8,128)S(1)}, u32[]{:S(2)}, u32[]{:S(2)}) collective-permute-start(f32[8,128]{1,0:T(8,128)S(1)} %add_add_fusion.1), channel_id=1, source_target_pairs={{0,4},{1,5},{2,6},{3,7},{4,0},{5,1},{6,2},{7,3},{8,12},{9,13},{10,... | collective-permute-start | bytes 12296 | tf_op jit(solution)/shard_map/ppermute | solution.py:199
  155.7 4.9 %collective-permute-start.32 = (f32[8,128]{1,0:T(8,128)S(1)}, f32[8,128]{1,0:T(8,128)S(1)}, u32[]{:S(2)}, u32[]{:S(2)}) collective-permute-start(f32[8,128]{1,0:T(8,128)S(1)} %add_add_fusion.1), channel_id=1, source_target_pairs={{0,8},{1,9},{2,10},{3,11},{4,12},{5,13},{6,14},{7,15},{8,0},{9,1},... | collective-permute-start | bytes 12296 | tf_op jit(solution)/shard_map/ppermute | solution.py:199
  156.0 5.4 %collective-permute-start.33 = (f32[8,128]{1,0:T(8,128)S(1)}, f32[8,128]{1,0:T(8,128)S(1)}, u32[]{:S(2)}, u32[]{:S(2)}) collective-permute-start(f32[8,128]{1,0:T(8,128)S(1)} %add_add_fusion.1), channel_id=1, source_target_pairs={{0,12},{1,13},{2,14},{3,15},{4,8},{5,9},{6,10},{7,11},{8,4},{9,5},... | collective-permute-start | bytes 12296 | tf_op jit(solution)/shard_map/ppermute | solution.py:199
  (23 other events, 153.0 us)

commit v8 on v7

--- a/solution.py
+++ b/solution.py
@@ -13,7 +13,7 @@
 VMEM = pl.BlockSpec(memory_space=pltpu.VMEM)
 SMEM = pl.BlockSpec(memory_space=pltpu.SMEM)
 HBM = pl.BlockSpec(memory_space=pltpu.HBM)
-PARAMS = pltpu.CompilerParams(vmem_limit_bytes=20 * 1024 * 1024)
+PARAMS = pltpu.CompilerParams(vmem_limit_bytes=16 * 1024 * 1024)
 
 
 def f32(*shape):
@@ -94,7 +94,7 @@
             row = i * room + j
             r = message[pl.ds(i * tiles + j * nh, nh)]
             r_out[row] = r
-            load[pl.ds(place[0, row], nh)] += r
+            load[pl.ds(place[row], nh)] += r
             for h in range(nh):
                 line, sub = divmod(j * nh + h, SUBLANES)
                 c = message[i * tiles + room * nh + line, sub : sub + 1, :]
@@ -121,7 +121,7 @@
     return gamma, gamma / (delta - beta * gamma / known[:, 1:2]), beta
 
 
-def home_kernel(first, last, nh, room, lines, place, keep, picked, comp, own, near_a, far_a, near_b, far_b, known, block, *refs):
+def home_kernel(first, last, nh, room, lines, place, away, keep, picked, comp, own, near_a, far_a, near_b, far_b, known, block, *refs):
     r_in, *refs = refs
     if not first:
         s_in, *refs = refs
@@ -153,7 +153,7 @@
         gamma, energy = sums
         for j in range(room):
             row = i * room + j
-            near, far, on = place[0, row], place[1, row], keep[row]
+            near, far, on = place[row], away[row], keep[row]
             for h in range(nh):
                 line, sub = divmod(j * nh + h, SUBLANES)
                 c = comp[i * lines + line, sub : sub + 1, :]
@@ -172,6 +172,43 @@
 
     gamma, energy = lax.fori_loop(0, nrow // room, pair, (zero, zero))
     respond(block, load, gamma, energy, answer)
+
+
+def list_kernel(first, keep, known, comp, mine, theirs, *refs):
+    if first:
+        r_in, r, d, x, s = refs
+    else:
+        r_in, d_in, x_in, s_in, r, d, x, s = refs
+    npatch, nh, ncase, width = r.shape
+    alpha = jnp.broadcast_to(known[:, 1:2], (ncase, width))
+    beta = jnp.broadcast_to(known[:, 2:3], (ncase, width))
+
+    def body(p, carry):
+        on, row = keep[p], comp[pl.ds(p, 1), :]
+        for h in range(nh):
+            residual = r_in[p, h]
+            c = row[:, h * width : (h + 1) * width]
+            image = on * (mine[p, h] + theirs[p, h] + c * residual)
+            if first:
+                direction, moved = residual, alpha * residual
+            else:
+                direction = residual + beta * d_in[p, h]
+                image = image + beta * s_in[p, h]
+                moved = x_in[p, h] + alpha * direction
+            r[p, h], d[p, h], x[p, h], s[p, h] = residual - alpha * image, direction, moved, image
+        return carry
+
+    lax.fori_loop(0, npatch, body, 0, unroll=4)
+
+
+def end_kernel(sums, known, r, d, x, out):
+    npatch, nh, ncase, width = r.shape
+    _, alpha, beta = steps(False, sums[...], known[...])
+    alpha = jnp.broadcast_to(alpha, (ncase, width))[None]
+    beta = jnp.broadcast_to(beta, (ncase, width))[None]
+    for h in range(nh):
+        moved = x[:, h] + alpha * (r[:, h] + beta * d[:, h])
+        out[:, :, h * width : (h + 1) * width] = jnp.swapaxes(moved, 0, 1)
 
 
 def on_device(rhs, compliance, plate_owner, found_owner, slot_pairs, active, inverse):
@@ -226,22 +263,24 @@
     lined = jnp.pad(lined, ((0, 0), (0, lines * SUBLANES - room * nh), (0, 0)))
     named = jnp.pad(facts[:, :, gap:], ((0, 0), (0, deep * SUBLANES - room), (0, 0)))
     table = jnp.concatenate([lined, named], axis=1).reshape(nsub, lines + deep, SUBLANES, LANES)
-    start = keep[None, :, None] * rhs
-    by_patch = jnp.transpose(start.reshape(ncase, npatch, nh, LANES), (1, 2, 0, 3))
+    start = (keep[None, :, None] * rhs).reshape(ncase, npatch, nh, LANES)
+    start = jnp.transpose(start, (1, 2, 0, 3))
+    picked = found(me ^ other).astype(jnp.int32)
+    place, picked = lax.optimization_barrier((place, picked))
 
     message = call(
         functools.partial(pack_kernel, nh, tiles),
         f32(nsub * tiles, ncase, LANES),
         [SMEM, VMEM, VMEM],
         place,
-        by_patch,
+        start,
         table,
     )
     message = exchange(message.reshape(nsub, tiles, ncase, LANES))
-    told = message[:, room * nh :].reshape(nsub, (lines + deep) * SUBLANES, LANES)
-    named = told[:, lines * SUBLANES : lines * SUBLANES + room, :3].reshape(nrow, 3).T
-    home = named[:2].astype(jnp.int32)
-    on = named[2]
+    facts = message[:, room * nh + lines :].reshape(nsub, deep * SUBLANES, LANES)[:, :room]
+    near, far, on = (facts[:, :, i].reshape(nrow) for i in range(3))
+    near, far = near.astype(jnp.int32), far.astype(jnp.int32)
+    message, near, far, on = lax.optimization_barrier((message, near, far, on))
 
     field = f32(nrow, nh, ncase, LANES)
     answer = f32(per, ncase, LANES)
@@ -251,30 +290,48 @@
         functools.partial(start_kernel, nh, room, tiles, lines),
         (field, f32(nsub * lines, ncase, LANES), answer, jax.ShapeDtypeStruct(block.shape, block.dtype)),
         [SMEM, VMEM, HBM],
-        home,
+        near,
         message.reshape(nsub * tiles, ncase, LANES),
         pltpu.with_memory_space_constraint(block, pltpu.HBM),
         scratch=[load, pltpu.SemaphoreType.DMA((nslot,))],
     )
+    def update(step, lists, known, part):
+        return call(
+            functools.partial(list_kernel, step == 0),
+            (f32(npatch, nh, ncase, LANES),) * 4,
+            [SMEM] + [VMEM] * (4 + len(lists)),
+            keep,
+            known,
+            compliance,
+            part,
+            sibling(part),
+            *lists,
+        )
+
     known = jnp.zeros((ncase, LANES), jnp.float32)
     state = [home_r]
-    picked = found(me ^ other).astype(jnp.int32)
-    r, d, x, s = start, None, None, None
+    lists = [start]
     for step in range(ITERS - 1):
         last = step == ITERS - 2
-        far = sibling(own)
-        far = jnp.concatenate([far[: per - 1], own[per - 1 :] + far[per - 1 :]])
-        parts = [far] + [swap(far, 4 * z) for z in range(1, nz)]
+        spread_out = sibling(own)
+        if step > 0:
+            spread_out, part = lax.optimization_barrier((spread_out, part))
+            lists = update(step - 1, lists, known, part)
+        spread_out = jnp.concatenate([spread_out[: per - 1], own[per - 1 :] + spread_out[per - 1 :]])
+        parts = [spread_out] + [swap(spread_out, 4 * z) for z in range(1, nz)]
         a = jnp.concatenate([part[:half] for part in parts])
         b = jnp.concatenate([part[half:] for part in parts])
         far_a, far_b = swap(a, 1), swap(b, 2)
         a, b = jnp.concatenate([a, far_a]), jnp.concatenate([b, far_b])
+        if step > 0:
+            a, b, lists = lax.optimization_barrier((a, b, lists))
         far_a, far_b = swap(a, 2), swap(b, 1)
         *state, own, part, known = call(
             functools.partial(home_kernel, step == 0, last, nh, room, lines),
             (field,) * (0 if last else 2) + (answer, f32(npatch, nh, ncase, LANES), f32(ncase, LANES)),
-            [SMEM] * 3 + [VMEM] * (8 + len(state)),
-            home,
+            [SMEM] * 4 + [VMEM] * (8 + len(state)),
+            near,
+            far,
             on,
             picked,
             comp,
@@ -288,23 +345,14 @@
             *state,
             scratch=[load, spread],
         )
-        image = jnp.transpose(part + sibling(part), (2, 0, 1, 3)).reshape(ncase, npatch, gap)
-        image = keep[None, :, None] * (image + compliance[None] * r)
-        alpha, beta = known[:, 1].reshape(ncase, 1, 1), known[:, 2].reshape(ncase, 1, 1)
-        if step == 0:
-            d, s = r, image
-            x = alpha * d
-        else:
-            d, s = r + beta * d, image + beta * s
-            x = x + alpha * d
-        r = r - alpha * s
-        r, d, x, s = lax.optimization_barrier((r, d, x, s))
     sums = own[per - 1]
-    sums = sums + sibling(sums)
+    others = sibling(sums)
+    others, part = lax.optimization_barrier((others, part))
+    sums = sums + others
+    r, d, x, _ = update(ITERS - 2, lists, known, part)
     sums = tree([sums] + [swap(sums, i) for i in range(1, 4)])
     sums = tree([sums] + [swap(sums, 4 * z) for z in range(1, nz)])
-    _, alpha, beta = steps(False, sums, known)
-    return x + alpha[:, :, None] * (r + beta[:, :, None] * d)
+    return call(end_kernel, f32(ncase, npatch, gap), [VMEM] * 5, sums, known, r, d, x)
 
 
 def solution(mesh):

time: 165 us -> 153 us (0.927)
  local copies, waits for them, and re-layouts: 21.5 us -> 1.35 us
  waiting for transfers between devices: 43 us -> 56.2 us
  other arithmetic: 10 us -> 3.4 us
  Pallas kernels: 14.4 us -> 18.9 us
  starting transfers between devices: 34.6 us -> 31.7 us
    ppermute x27, waiting for transfers between devices: 38.4 us -> 51.3 us  [swap(): return lax.ppermute(value, 'sub', [(i, i ^ far) for i in range(nsub)])]
    unnamed x43 -> x5, local copies, waits for them, and re-layouts: 12.9 us -> 0.1 us
    pallas_call x5 -> x9, Pallas kernels: 14.4 us -> 18.9 us  [call(): pl.pallas_call(kernel, out_shape=tuple(out_shape) if several else out_sha...]
    reshape x8 -> x3, local copies, waits for them, and re-layouts: 4.55 us -> 0.59 us  [the longest x2 0.58 us: on_device(): start = (keep[None, :, None] * rhs).reshape(ncase, npatch, nh, LANES)]
    add x7 -> x4, other arithmetic: 3.76 us -> 0.01 us  [the longest x3 0.01 us: on_device(): own[per - 1:] + spread_out[per - 1:]]
    ppermute x27, starting transfers between devices: 34.5 us -> 31.4 us  [swap(): return lax.ppermute(value, 'sub', [(i, i ^ far) for i in range(nsub)])]
    sub x1 -> x0, other arithmetic: 2.56 us -> none  [on_device(): r = r - alpha * s]
    concatenate x6, local copies, waits for them, and re-layouts: 1.88 us -> 0.06 us  [on_device(): a, b = (jnp.concatenate([a, far_a]), jnp.concatenate([b, far_b]))]
  transfers between devices with their start and end apart: 34 -> 34, of which waited for: 18 -> 26; matrix products, arithmetic and copies ran while one was open for 9% -> 0% of each run, Pallas kernels for 4% -> 0%
where the time goes in v8:
time: 153 us; the launch traced here: 152 us
  waiting for transfers between devices  56.2 us (37%)
  blocking collectives  39.4 us (26%)
  starting transfers between devices  31.7 us (21%)
  Pallas kernels  18.9 us (12%)
  other arithmetic  3.4 us (2%)
    ppermute x27, waiting for transfers between devices, swap(): return lax.ppermute(value, 'sub', [(i, i ^ far) for i in range(nsub)])  51.3 us
    all_to_all x1, blocking collectives, exchange(): lax.all_to_all(message, 'sub', split_axis=0, concat_axis=0, tiled=True)  39.4 us
    ppermute x27, starting transfers between devices, swap(): return lax.ppermute(value, 'sub', [(i, i ^ far) for i in range(nsub)])  31.4 us
    pallas_call x9, Pallas kernels, call(): pl.pallas_call(kernel, out_shape=tuple(out_shape) if several else out_sha...  18.9 us
    ppermute x7, waiting for transfers between devices, sibling(): lax.ppermute(value, 'body', [(i, nbody - 1 - i) for i in range(nbody)])  4.91 us
  transfers between devices with their start and end apart: 34, of which 26 were waited for; matrix products, arithmetic and copies ran while one was open for 0% of the time, Pallas kernels for 0%

profile of v8, /device:TPU:0, one launch (start us, length us, event | category | flops | bytes accessed | tf_op | source)
XLA Modules:
  0.0 152.4 jit_solution(10939474134936061225)
XLA Ops:
  5.2 39.4 %all_to_all.5 = f32[16,19,8,128]{3,2,1,0:T(8,128)S(1)} all-to-all(f32[16,19,8,128]{3,2,1,0:T(8,128)S(1)} %bitcast.63), channel_id=1, replica_groups=mesh['body'=2,'sub'=16] {'sub'}, dimensions={0} | all-to-all | bytes 2490368 | tf_op jit(solution)/shard_map/all_to_all | solution.py:233
  45.7 4.4 %shard_map.74 = (f32[128,2,8,128]{3,2,1,0:T(8,128)S(1)}, f32[32,8,128]{2,1,0:T(8,128)S(1)}, f32[17,8,128]{2,1,0:T(8,128)S(1)}, bf16[2048,2048]{1,0:T(8,128)(2,1)S(1)}) custom-call(s32[128]{0:T(128)S(1)} %convert_element_type.28.place, f32[304,8,128]{2,1,0:T(8,128)S(1)} %bitcast.62, bf16[2048,2048]{1,0:T(8,128)(2,1)} %bitcast.66), custom_call_target="tpu_custom_call" | custom-call | tf_op jit(solution)/shard_map/pallas_call | solution.py:25
  50.1 1.2 collective-permute-done
  51.4 1.7 %collective-permute-start.3 = (f32[17,8,128]{2,1,0:T(8,128)S(1)}, f32[17,8,128]{2,1,0:T(8,128)S(1)}, u32[]{:S(2)}, u32[]{:S(2)}) collective-permute-start(f32[17,8,128]{2,1,0:T(8,128)S(1)} %pad_maximum_fusion.6), channel_id=1, source_target_pairs={{0,12},{1,13},{2,14},{3,15},{4,8},{5,9},{6,10},{7,11},{8,4},{9,5},... | collective-permute-start | bytes 208904 | tf_op jit(solution)/shard_map/ppermute | solution.py:236
  53.8 2.1 %collective-permute-start.1 = (f32[17,8,128]{2,1,0:T(8,128)S(1)}, f32[17,8,128]{2,1,0:T(8,128)S(1)}, u32[]{:S(2)}, u32[]{:S(2)}) collective-permute-start(f32[17,8,128]{2,1,0:T(8,128)S(1)} %pad_maximum_fusion.6), channel_id=1, source_target_pairs={{0,4},{1,5},{2,6},{3,7},{4,0},{5,1},{6,2},{7,3},{8,12},{9,13},{10,... | collective-permute-start | bytes 208904 | tf_op jit(solution)/shard_map/ppermute | solution.py:236
  55.9 3.9 %collective-permute-done.1 = f32[17,8,128]{2,1,0:T(8,128)S(1)} collective-permute-done((f32[17,8,128]{2,1,0:T(8,128)S(1)}, f32[17,8,128]{2,1,0:T(8,128)S(1)}, u32[]{:S(2)}, u32[]{:S(2)}) %collective-permute-start.1) | collective-permute-done | bytes 69664 | tf_op jit(solution)/shard_map/ppermute | solution.py:236
  62.0 4.4 %collective-permute-done.6 = f32[36,8,128]{2,1,0:T(8,128)S(1)} collective-permute-done((f32[36,8,128]{2,1,0:T(8,128)S(1)}, f32[36,8,128]{2,1,0:T(8,128)S(1)}, u32[]{:S(2)}, u32[]{:S(2)}) %collective-permute-start.6) | collective-permute-done | bytes 147488 | tf_op jit(solution)/shard_map/ppermute | solution.py:236
  68.0 6.3 %collective-permute-done.5.far_a = f32[64,8,128]{2,1,0:T(8,128)S(1)} collective-permute-done((f32[64,8,128]{2,1,0:T(8,128)S(1)}, f32[64,8,128]{2,1,0:T(8,128)S(1)}, u32[]{:S(2)}, u32[]{:S(2)}) %collective-permute-start.5) | collective-permute-done | bytes 262176 | tf_op jit(solution)/shard_map/ppermute | solution.py:236
  74.6 2.8 %shard_map.75 = (f32[128,2,8,128]{3,2,1,0:T(8,128)S(1)}, f32[128,2,8,128]{3,2,1,0:T(8,128)S(1)}, f32[17,8,128]{2,1,0:T(8,128)S(1)}, f32[64,2,8,128]{3,2,1,0:T(8,128)S(1)}, f32[8,128]{1,0:T(8,128)S(1)}) custom-call(s32[128]{0:T(128)S(1)} %convert_element_type.28.place, s32[128]{0:T(128)S(1)} %convert_element_type.30.away, f32[128]{0:T(128)S(1)} %reshape_squeeze.2.keep, ...), custom_call_target="tpu_custom_call" | custom-call | tf_op jit(solution)/shard_map/pallas_call | solution.py:25
  77.5 1.2 collective-permute-done.8
  78.7 1.6 %collective-permute-start.11 = (f32[17,8,128]{2,1,0:T(8,128)S(1)}, f32[17,8,128]{2,1,0:T(8,128)S(1)}, u32[]{:S(2)}, u32[]{:S(2)}) collective-permute-start(f32[17,8,128]{2,1,0:T(8,128)S(1)} %pad_maximum_fusion.7), channel_id=1, source_target_pairs={{0,12},{1,13},{2,14},{3,15},{4,8},{5,9},{6,10},{7,11},{8,4},{9,5},... | collective-permute-start | bytes 208904 | tf_op jit(solution)/shard_map/ppermute | solution.py:236
  80.3 2.8 %collective-permute-start.9 = (f32[17,8,128]{2,1,0:T(8,128)S(1)}, f32[17,8,128]{2,1,0:T(8,128)S(1)}, u32[]{:S(2)}, u32[]{:S(2)}) collective-permute-start(f32[17,8,128]{2,1,0:T(8,128)S(1)} %pad_maximum_fusion.7), channel_id=1, source_target_pairs={{0,4},{1,5},{2,6},{3,7},{4,0},{5,1},{6,2},{7,3},{8,12},{9,13},{10,... | collective-permute-start | bytes 208904 | tf_op jit(solution)/shard_map/ppermute | solution.py:236
  83.2 3.9 %collective-permute-done.9 = f32[17,8,128]{2,1,0:T(8,128)S(1)} collective-permute-done((f32[17,8,128]{2,1,0:T(8,128)S(1)}, f32[17,8,128]{2,1,0:T(8,128)S(1)}, u32[]{:S(2)}, u32[]{:S(2)}) %collective-permute-start.9) | collective-permute-done | bytes 69664 | tf_op jit(solution)/shard_map/ppermute | solution.py:236
  87.9 1.3 collective-permute-start.12
  89.9 3.4 %collective-permute-done.12 = f32[32,8,128]{2,1,0:T(8,128)S(1)} collective-permute-done((f32[32,8,128]{2,1,0:T(8,128)S(1)}, f32[32,8,128]{2,1,0:T(8,128)S(1)}, u32[]{:S(2)}, u32[]{:S(2)}) %collective-permute-start.12) | collective-permute-done | bytes 131104 | tf_op jit(solution)/shard_map/ppermute | solution.py:236
  93.4 1.4 collective-permute-done.13
  97.4 5.9 %collective-permute-done.15.far_a = f32[64,8,128]{2,1,0:T(8,128)S(1)} collective-permute-done((f32[64,8,128]{2,1,0:T(8,128)S(1)}, f32[64,8,128]{2,1,0:T(8,128)S(1)}, u32[]{:S(2)}, u32[]{:S(2)}) %collective-permute-start.15) | collective-permute-done | bytes 262176 | tf_op jit(solution)/shard_map/ppermute | solution.py:236
  103.6 3.0 %shard_map.77 = (f32[128,2,8,128]{3,2,1,0:T(8,128)S(1)}, f32[128,2,8,128]{3,2,1,0:T(8,128)S(1)}, f32[17,8,128]{2,1,0:T(8,128)S(1)}, f32[64,2,8,128]{3,2,1,0:T(8,128)S(1)}, f32[8,128]{1,0:T(8,128)S(1)}) custom-call(s32[128]{0:T(128)S(1)} %convert_element_type.28.place, s32[128]{0:T(128)S(1)} %convert_element_type.30.away, f32[128]{0:T(128)S(1)} %reshape_squeeze.2.keep, ...), custom_call_target="tpu_custom_call" | custom-call | tf_op jit(solution)/shard_map/pallas_call | solution.py:25
  106.6 1.3 collective-permute-done.17
  107.9 1.6 %collective-permute-start.20 = (f32[17,8,128]{2,1,0:T(8,128)S(1)}, f32[17,8,128]{2,1,0:T(8,128)S(1)}, u32[]{:S(2)}, u32[]{:S(2)}) collective-permute-start(f32[17,8,128]{2,1,0:T(8,128)S(1)} %pad_maximum_fusion.8), channel_id=1, source_target_pairs={{0,12},{1,13},{2,14},{3,15},{4,8},{5,9},{6,10},{7,11},{8,4},{9,5},... | collective-permute-start | bytes 208904 | tf_op jit(solution)/shard_map/ppermute | solution.py:236
  109.5 2.8 %collective-permute-start.18 = (f32[17,8,128]{2,1,0:T(8,128)S(1)}, f32[17,8,128]{2,1,0:T(8,128)S(1)}, u32[]{:S(2)}, u32[]{:S(2)}) collective-permute-start(f32[17,8,128]{2,1,0:T(8,128)S(1)} %pad_maximum_fusion.8), channel_id=1, source_target_pairs={{0,4},{1,5},{2,6},{3,7},{4,0},{5,1},{6,2},{7,3},{8,12},{9,13},{10,... | collective-permute-start | bytes 208904 | tf_op jit(solution)/shard_map/ppermute | solution.py:236
  112.4 3.9 %collective-permute-done.18 = f32[17,8,128]{2,1,0:T(8,128)S(1)} collective-permute-done((f32[17,8,128]{2,1,0:T(8,128)S(1)}, f32[17,8,128]{2,1,0:T(8,128)S(1)}, u32[]{:S(2)}, u32[]{:S(2)}) %collective-permute-start.18) | collective-permute-done | bytes 69664 | tf_op jit(solution)/shard_map/ppermute | solution.py:236
  118.9 3.6 %collective-permute-done.21 = f32[32,8,128]{2,1,0:T(8,128)S(1)} collective-permute-done((f32[32,8,128]{2,1,0:T(8,128)S(1)}, f32[32,8,128]{2,1,0:T(8,128)S(1)}, u32[]{:S(2)}, u32[]{:S(2)}) %collective-permute-start.21) | collective-permute-done | bytes 131104 | tf_op jit(solution)/shard_map/ppermute | solution.py:236
  122.5 1.3 collective-permute-done.22
  126.6 6.0 %collective-permute-done.24.far_a = f32[64,8,128]{2,1,0:T(8,128)S(1)} collective-permute-done((f32[64,8,128]{2,1,0:T(8,128)S(1)}, f32[64,8,128]{2,1,0:T(8,128)S(1)}, u32[]{:S(2)}, u32[]{:S(2)}) %collective-permute-start.24) | collective-permute-done | bytes 262176 | tf_op jit(solution)/shard_map/ppermute | solution.py:236
  132.7 3.0 %shard_map.79 = (f32[17,8,128]{2,1,0:T(8,128)S(1)}, f32[64,2,8,128]{3,2,1,0:T(8,128)S(1)}, f32[8,128]{1,0:T(8,128)S(1)}) custom-call(s32[128]{0:T(128)S(1)} %convert_element_type.28.place, s32[128]{0:T(128)S(1)} %convert_element_type.30.away, f32[128]{0:T(128)S(1)} %reshape_squeeze.2.keep, s32[64]{0:T(128)S(1)} %get-tuple-element.61.picked, ...), custom_call_target="tpu_custom_call" | custom-call | tf_op jit(solution)/shard_map/pallas_call | solution.py:25
  138.2 1.5 collective-permute-start.28
  141.8 1.5 collective-permute-done.27
  143.3 1.6 %collective-permute-start.32 = (f32[8,128]{1,0:T(8,128)S(1)}, f32[8,128]{1,0:T(8,128)S(1)}, u32[]{:S(2)}, u32[]{:S(2)}) collective-permute-start(f32[8,128]{1,0:T(8,128)S(1)} %add_add_fusion.1), channel_id=1, source_target_pairs={{0,12},{1,13},{2,14},{3,15},{4,8},{5,9},{6,10},{7,11},{8,4},{9,5},... | collective-permute-start | bytes 12296 | tf_op jit(solution)/shard_map/ppermute | solution.py:236
  144.9 2.8 %collective-permute-start.30 = (f32[8,128]{1,0:T(8,128)S(1)}, f32[8,128]{1,0:T(8,128)S(1)}, u32[]{:S(2)}, u32[]{:S(2)}) collective-permute-start(f32[8,128]{1,0:T(8,128)S(1)} %add_add_fusion.1), channel_id=1, source_target_pairs={{0,4},{1,5},{2,6},{3,7},{4,0},{5,1},{6,2},{7,3},{8,12},{9,13},{10,... | collective-permute-start | bytes 12296 | tf_op jit(solution)/shard_map/ppermute | solution.py:236
  149.4 1.8 %shard_map.80 = (f32[64,2,8,128]{3,2,1,0:T(8,128)S(1)}, f32[64,2,8,128]{3,2,1,0:T(8,128)S(1)}, f32[64,2,8,128]{3,2,1,0:T(8,128)S(1)}, f32[64,2,8,128]{3,2,1,0:T(8,128)}) custom-call(f32[64]{0:T(128)S(1)} %get-tuple-element.165.keep, f32[8,128]{1,0:T(8,128)S(1)} %get-tuple-element.100.known, f32[64,256]{1,0:T(8,128)S(1)} %copy-done, ...), custom_call_target="tpu_custom_call" | custom-call | tf_op jit(solution)/shard_map/pallas_call | solution.py:25
  151.2 1.3 shard_map.81
  (121 shorter events, 27.3 us)
Async XLA Ops:
  50.0 1.3 collective-permute-start
  51.4 9.1 %collective-permute-start.3 = (f32[17,8,128]{2,1,0:T(8,128)S(1)}, f32[17,8,128]{2,1,0:T(8,128)S(1)}, u32[]{:S(2)}, u32[]{:S(2)}) collective-permute-start(f32[17,8,128]{2,1,0:T(8,128)S(1)} %pad_maximum_fusion.6), channel_id=1, source_target_pairs={{0,12},{1,13},{2,14},{3,15},{4,8},{5,9},{6,10},{7,11},{8,4},{9,5},... | collective-permute-start | bytes 208904 | tf_op jit(solution)/shard_map/ppermute | solution.py:236
  53.1 7.5 %collective-permute-start.2 = (f32[17,8,128]{2,1,0:T(8,128)S(1)}, f32[17,8,128]{2,1,0:T(8,128)S(1)}, u32[]{:S(2)}, u32[]{:S(2)}) collective-permute-start(f32[17,8,128]{2,1,0:T(8,128)S(1)} %pad_maximum_fusion.6), channel_id=1, source_target_pairs={{0,8},{1,9},{2,10},{3,11},{4,12},{5,13},{6,14},{7,15},{8,0},{9,1},... | collective-permute-start | bytes 208904 | tf_op jit(solution)/shard_map/ppermute | solution.py:236
  53.8 6.0 %collective-permute-start.1 = (f32[17,8,128]{2,1,0:T(8,128)S(1)}, f32[17,8,128]{2,1,0:T(8,128)S(1)}, u32[]{:S(2)}, u32[]{:S(2)}) collective-permute-start(f32[17,8,128]{2,1,0:T(8,128)S(1)} %pad_maximum_fusion.6), channel_id=1, source_target_pairs={{0,4},{1,5},{2,6},{3,7},{4,0},{5,1},{6,2},{7,3},{8,12},{9,13},{10,... | collective-permute-start | bytes 208904 | tf_op jit(solution)/shard_map/ppermute | solution.py:236
  60.6 5.9 %collective-permute-start.6 = (f32[36,8,128]{2,1,0:T(8,128)S(1)}, f32[36,8,128]{2,1,0:T(8,128)S(1)}, u32[]{:S(2)}, u32[]{:S(2)}) collective-permute-start(f32[36,8,128]{2,1,0:T(8,128)S(1)} %pad_maximum_fusion), channel_id=1, source_target_pairs={{0,2},{1,3},{2,0},{3,1},{4,6},{5,7},{6,4},{7,5},{8,10},{9,11},{10,... | collective-permute-start | bytes 442376 | tf_op jit(solution)/shard_map/ppermute | solution.py:236
  61.4 5.7 %collective-permute-start.4 = (f32[32,8,128]{2,1,0:T(8,128)S(1)}, f32[32,8,128]{2,1,0:T(8,128)S(1)}, u32[]{:S(2)}, u32[]{:S(2)}) collective-permute-start(f32[32,8,128]{2,1,0:T(8,128)S(1)} %pad_maximum_fusion.3), channel_id=1, source_target_pairs={{0,1},{1,0},{2,3},{3,2},{4,5},{5,4},{6,7},{7,6},{8,9},{9,8},{10,11... | collective-permute-start | bytes 393224 | tf_op jit(solution)/shard_map/ppermute | solution.py:236
  66.4 8.2 %collective-permute-start.7 = (f32[72,8,128]{2,1,0:T(8,128)S(1)}, f32[72,8,128]{2,1,0:T(8,128)S(1)}, u32[]{:S(2)}, u32[]{:S(2)}) collective-permute-start(f32[72,8,128]{2,1,0:T(8,128)S(1)} %constant_dynamic-update-slice_fusion.5.near_b), channel_id=1, source_target_pairs={{0,1},{1,0},{2,3},{3,2},{4,5},{5,4},{6,7},{7,6},{8,9},{9,8},{10,11... | collective-permute-start | bytes 884744 | tf_op jit(solution)/shard_map/ppermute | solution.py:236
  67.1 7.2 %collective-permute-start.5 = (f32[64,8,128]{2,1,0:T(8,128)S(1)}, f32[64,8,128]{2,1,0:T(8,128)S(1)}, u32[]{:S(2)}, u32[]{:S(2)}) collective-permute-start(f32[64,8,128]{2,1,0:T(8,128)S(1)} %constant_dynamic-update-slice_fusion.near_a), channel_id=1, source_target_pairs={{0,2},{1,3},{2,0},{3,1},{4,6},{5,7},{6,4},{7,5},{8,10},{9,11},{10,... | collective-permute-start | bytes 786440 | tf_op jit(solution)/shard_map/ppermute | solution.py:236
  77.4 1.3 collective-permute-start.8
  78.7 9.1 %collective-permute-start.11 = (f32[17,8,128]{2,1,0:T(8,128)S(1)}, f32[17,8,128]{2,1,0:T(8,128)S(1)}, u32[]{:S(2)}, u32[]{:S(2)}) collective-permute-start(f32[17,8,128]{2,1,0:T(8,128)S(1)} %pad_maximum_fusion.7), channel_id=1, source_target_pairs={{0,12},{1,13},{2,14},{3,15},{4,8},{5,9},{6,10},{7,11},{8,4},{9,5},... | collective-permute-start | bytes 208904 | tf_op jit(solution)/shard_map/ppermute | solution.py:236
  80.3 7.5 %collective-permute-start.10 = (f32[17,8,128]{2,1,0:T(8,128)S(1)}, f32[17,8,128]{2,1,0:T(8,128)S(1)}, u32[]{:S(2)}, u32[]{:S(2)}) collective-permute-start(f32[17,8,128]{2,1,0:T(8,128)S(1)} %pad_maximum_fusion.7), channel_id=1, source_target_pairs={{0,8},{1,9},{2,10},{3,11},{4,12},{5,13},{6,14},{7,15},{8,0},{9,1},... | collective-permute-start | bytes 208904 | tf_op jit(solution)/shard_map/ppermute | solution.py:236
  80.3 6.8 %collective-permute-start.9 = (f32[17,8,128]{2,1,0:T(8,128)S(1)}, f32[17,8,128]{2,1,0:T(8,128)S(1)}, u32[]{:S(2)}, u32[]{:S(2)}) collective-permute-start(f32[17,8,128]{2,1,0:T(8,128)S(1)} %pad_maximum_fusion.7), channel_id=1, source_target_pairs={{0,4},{1,5},{2,6},{3,7},{4,0},{5,1},{6,2},{7,3},{8,12},{9,13},{10,... | collective-permute-start | bytes 208904 | tf_op jit(solution)/shard_map/ppermute | solution.py:236
  83.2 11.6 %collective-permute-start.14 = (f32[64,2,8,128]{3,2,1,0:T(8,128)S(1)}, f32[64,2,8,128]{3,2,1,0:T(8,128)S(1)}, u32[]{:S(2)}, u32[]{:S(2)}) collective-permute-start(f32[64,2,8,128]{3,2,1,0:T(8,128)S(1)} %get-tuple-element.71.mine), channel_id=1, source_target_pairs={{0,16},{16,0},{1,17},{17,1},{2,18},{18,2},{3,19},{19,3},{4,20},{20... | collective-permute-start | bytes 1572872 | tf_op jit(solution)/shard_map/ppermute | solution.py:239
  87.9 5.5 %collective-permute-start.12 = (f32[32,8,128]{2,1,0:T(8,128)S(1)}, f32[32,8,128]{2,1,0:T(8,128)S(1)}, u32[]{:S(2)}, u32[]{:S(2)}) collective-permute-start(f32[32,8,128]{2,1,0:T(8,128)S(1)} %pad_maximum_fusion.4), channel_id=1, source_target_pairs={{0,1},{1,0},{2,3},{3,2},{4,5},{5,4},{6,7},{7,6},{8,9},{9,8},{10,11... | collective-permute-start | bytes 393224 | tf_op jit(solution)/shard_map/ppermute | solution.py:236
  89.2 5.6 %collective-permute-start.13 = (f32[36,8,128]{2,1,0:T(8,128)S(1)}, f32[36,8,128]{2,1,0:T(8,128)S(1)}, u32[]{:S(2)}, u32[]{:S(2)}) collective-permute-start(f32[36,8,128]{2,1,0:T(8,128)S(1)} %pad_maximum_fusion.1), channel_id=1, source_target_pairs={{0,2},{1,3},{2,0},{3,1},{4,6},{5,7},{6,4},{7,5},{8,10},{9,11},{10,... | collective-permute-start | bytes 442376 | tf_op jit(solution)/shard_map/ppermute | solution.py:236
  95.7 7.8 %collective-permute-start.16 = (f32[72,8,128]{2,1,0:T(8,128)S(1)}, f32[72,8,128]{2,1,0:T(8,128)S(1)}, u32[]{:S(2)}, u32[]{:S(2)}) collective-permute-start(f32[72,8,128]{2,1,0:T(8,128)S(1)} %constant_dynamic-update-slice_fusion.15.near_b), channel_id=1, source_target_pairs={{0,1},{1,0},{2,3},{3,2},{4,5},{5,4},{6,7},{7,6},{8,9},{9,8},{10,11... | collective-permute-start | bytes 884744 | tf_op jit(solution)/shard_map/ppermute | solution.py:236
  96.5 6.8 %collective-permute-start.15 = (f32[64,8,128]{2,1,0:T(8,128)S(1)}, f32[64,8,128]{2,1,0:T(8,128)S(1)}, u32[]{:S(2)}, u32[]{:S(2)}) collective-permute-start(f32[64,8,128]{2,1,0:T(8,128)S(1)} %constant_dynamic-update-slice_fusion.10.near_a), channel_id=1, source_target_pairs={{0,2},{1,3},{2,0},{3,1},{4,6},{5,7},{6,4},{7,5},{8,10},{9,11},{10,... | collective-permute-start | bytes 786440 | tf_op jit(solution)/shard_map/ppermute | solution.py:236
  107.9 9.1 %collective-permute-start.20 = (f32[17,8,128]{2,1,0:T(8,128)S(1)}, f32[17,8,128]{2,1,0:T(8,128)S(1)}, u32[]{:S(2)}, u32[]{:S(2)}) collective-permute-start(f32[17,8,128]{2,1,0:T(8,128)S(1)} %pad_maximum_fusion.8), channel_id=1, source_target_pairs={{0,12},{1,13},{2,14},{3,15},{4,8},{5,9},{6,10},{7,11},{8,4},{9,5},... | collective-permute-start | bytes 208904 | tf_op jit(solution)/shard_map/ppermute | solution.py:236
  109.5 7.5 %collective-permute-start.19 = (f32[17,8,128]{2,1,0:T(8,128)S(1)}, f32[17,8,128]{2,1,0:T(8,128)S(1)}, u32[]{:S(2)}, u32[]{:S(2)}) collective-permute-start(f32[17,8,128]{2,1,0:T(8,128)S(1)} %pad_maximum_fusion.8), channel_id=1, source_target_pairs={{0,8},{1,9},{2,10},{3,11},{4,12},{5,13},{6,14},{7,15},{8,0},{9,1},... | collective-permute-start | bytes 208904 | tf_op jit(solution)/shard_map/ppermute | solution.py:236
  109.5 6.8 %collective-permute-start.18 = (f32[17,8,128]{2,1,0:T(8,128)S(1)}, f32[17,8,128]{2,1,0:T(8,128)S(1)}, u32[]{:S(2)}, u32[]{:S(2)}) collective-permute-start(f32[17,8,128]{2,1,0:T(8,128)S(1)} %pad_maximum_fusion.8), channel_id=1, source_target_pairs={{0,4},{1,5},{2,6},{3,7},{4,0},{5,1},{6,2},{7,3},{8,12},{9,13},{10,... | collective-permute-start | bytes 208904 | tf_op jit(solution)/shard_map/ppermute | solution.py:236
  112.3 11.5 %collective-permute-start.23 = (f32[64,2,8,128]{3,2,1,0:T(8,128)S(1)}, f32[64,2,8,128]{3,2,1,0:T(8,128)S(1)}, u32[]{:S(2)}, u32[]{:S(2)}) collective-permute-start(f32[64,2,8,128]{3,2,1,0:T(8,128)S(1)} %get-tuple-element.84.mine), channel_id=1, source_target_pairs={{0,16},{16,0},{1,17},{17,1},{2,18},{18,2},{3,19},{19,3},{4,20},{20... | collective-permute-start | bytes 1572872 | tf_op jit(solution)/shard_map/ppermute | solution.py:239
  117.0 5.5 %collective-permute-start.21 = (f32[32,8,128]{2,1,0:T(8,128)S(1)}, f32[32,8,128]{2,1,0:T(8,128)S(1)}, u32[]{:S(2)}, u32[]{:S(2)}) collective-permute-start(f32[32,8,128]{2,1,0:T(8,128)S(1)} %pad_maximum_fusion.5), channel_id=1, source_target_pairs={{0,1},{1,0},{2,3},{3,2},{4,5},{5,4},{6,7},{7,6},{8,9},{9,8},{10,11... | collective-permute-start | bytes 393224 | tf_op jit(solution)/shard_map/ppermute | solution.py:236
  118.3 5.6 %collective-permute-start.22 = (f32[36,8,128]{2,1,0:T(8,128)S(1)}, f32[36,8,128]{2,1,0:T(8,128)S(1)}, u32[]{:S(2)}, u32[]{:S(2)}) collective-permute-start(f32[36,8,128]{2,1,0:T(8,128)S(1)} %pad_maximum_fusion.2), channel_id=1, source_target_pairs={{0,2},{1,3},{2,0},{3,1},{4,6},{5,7},{6,4},{7,5},{8,10},{9,11},{10,... | collective-permute-start | bytes 442376 | tf_op jit(solution)/shard_map/ppermute | solution.py:236
  124.8 7.8 %collective-permute-start.25 = (f32[72,8,128]{2,1,0:T(8,128)S(1)}, f32[72,8,128]{2,1,0:T(8,128)S(1)}, u32[]{:S(2)}, u32[]{:S(2)}) collective-permute-start(f32[72,8,128]{2,1,0:T(8,128)S(1)} %constant_dynamic-update-slice_fusion.25.near_b), channel_id=1, source_target_pairs={{0,1},{1,0},{2,3},{3,2},{4,5},{5,4},{6,7},{7,6},{8,9},{9,8},{10,11... | collective-permute-start | bytes 884744 | tf_op jit(solution)/shard_map/ppermute | solution.py:236
  125.8 6.8 %collective-permute-start.24 = (f32[64,8,128]{2,1,0:T(8,128)S(1)}, f32[64,8,128]{2,1,0:T(8,128)S(1)}, u32[]{:S(2)}, u32[]{:S(2)}) collective-permute-start(f32[64,8,128]{2,1,0:T(8,128)S(1)} %constant_dynamic-update-slice_fusion.20.near_a), channel_id=1, source_target_pairs={{0,2},{1,3},{2,0},{3,1},{4,6},{5,7},{6,4},{7,5},{8,10},{9,11},{10,... | collective-permute-start | bytes 786440 | tf_op jit(solution)/shard_map/ppermute | solution.py:236
  136.9 12.5 %collective-permute-start.33 = (f32[64,2,8,128]{3,2,1,0:T(8,128)S(1)}, f32[64,2,8,128]{3,2,1,0:T(8,128)S(1)}, u32[]{:S(2)}, u32[]{:S(2)}) collective-permute-start(f32[64,2,8,128]{3,2,1,0:T(8,128)S(1)} %get-tuple-element.101.mine), channel_id=1, source_target_pairs={{0,16},{16,0},{1,17},{17,1},{2,18},{18,2},{3,19},{19,3},{4,20},{20... | collective-permute-start | bytes 1572872 | tf_op jit(solution)/shard_map/ppermute | solution.py:239
  137.0 4.5 %collective-permute-start.29 = (f32[8,128]{1,0:T(8,128)S(1)}, f32[8,128]{1,0:T(8,128)S(1)}, u32[]{:S(2)}, u32[]{:S(2)}) collective-permute-start(f32[8,128]{1,0:T(8,128)S(1)} %fusion.21), channel_id=1, source_target_pairs={{0,3},{1,2},{2,1},{3,0},{4,7},{5,6},{6,5},{7,4},{8,11},{9,10},{10,... | collective-permute-start | bytes 12296 | tf_op jit(solution)/shard_map/ppermute | solution.py:236
  138.2 3.6 %collective-permute-start.28 = (f32[8,128]{1,0:T(8,128)S(1)}, f32[8,128]{1,0:T(8,128)S(1)}, u32[]{:S(2)}, u32[]{:S(2)}) collective-permute-start(f32[8,128]{1,0:T(8,128)S(1)} %fusion.21), channel_id=1, source_target_pairs={{0,2},{1,3},{2,0},{3,1},{4,6},{5,7},{6,4},{7,5},{8,10},{9,11},{10,... | collective-permute-start | bytes 12296 | tf_op jit(solution)/shard_map/ppermute | solution.py:236
  139.6 3.6 %collective-permute-start.27 = (f32[8,128]{1,0:T(8,128)S(1)}, f32[8,128]{1,0:T(8,128)S(1)}, u32[]{:S(2)}, u32[]{:S(2)}) collective-permute-start(f32[8,128]{1,0:T(8,128)S(1)} %fusion.21), channel_id=1, source_target_pairs={{0,1},{1,0},{2,3},{3,2},{4,5},{5,4},{6,7},{7,6},{8,9},{9,8},{10,11... | collective-permute-start | bytes 12296 | tf_op jit(solution)/shard_map/ppermute | solution.py:236
  143.3 5.4 %collective-permute-start.32 = (f32[8,128]{1,0:T(8,128)S(1)}, f32[8,128]{1,0:T(8,128)S(1)}, u32[]{:S(2)}, u32[]{:S(2)}) collective-permute-start(f32[8,128]{1,0:T(8,128)S(1)} %add_add_fusion.1), channel_id=1, source_target_pairs={{0,12},{1,13},{2,14},{3,15},{4,8},{5,9},{6,10},{7,11},{8,4},{9,5},... | collective-permute-start | bytes 12296 | tf_op jit(solution)/shard_map/ppermute | solution.py:236
  144.9 4.5 %collective-permute-start.31 = (f32[8,128]{1,0:T(8,128)S(1)}, f32[8,128]{1,0:T(8,128)S(1)}, u32[]{:S(2)}, u32[]{:S(2)}) collective-permute-start(f32[8,128]{1,0:T(8,128)S(1)} %add_add_fusion.1), channel_id=1, source_target_pairs={{0,8},{1,9},{2,10},{3,11},{4,12},{5,13},{6,14},{7,15},{8,0},{9,1},... | collective-permute-start | bytes 12296 | tf_op jit(solution)/shard_map/ppermute | solution.py:236
  144.9 4.5 %collective-permute-start.30 = (f32[8,128]{1,0:T(8,128)S(1)}, f32[8,128]{1,0:T(8,128)S(1)}, u32[]{:S(2)}, u32[]{:S(2)}) collective-permute-start(f32[8,128]{1,0:T(8,128)S(1)} %add_add_fusion.1), channel_id=1, source_target_pairs={{0,4},{1,5},{2,6},{3,7},{4,0},{5,1},{6,2},{7,3},{8,12},{9,13},{10,... | collective-permute-start | bytes 12296 | tf_op jit(solution)/shard_map/ppermute | solution.py:236
  (4 other events, 23.6 us)

commit v9 on v8

--- a/solution.py
+++ b/solution.py
@@ -20,7 +20,7 @@
     return jax.ShapeDtypeStruct(shape, jnp.float32)
 
 
-def call(kernel, out_shape, specs, *operands, scratch=()):
+def call(kernel, out_shape, specs, *operands, scratch=(), cost=None):
     several = isinstance(out_shape, (tuple, list))
     return pl.pallas_call(
         kernel,
@@ -29,6 +29,7 @@
         out_specs=(VMEM,) * len(out_shape) if several else VMEM,
         scratch_shapes=list(scratch),
         compiler_params=PARAMS,
+        cost_estimate=cost,
     )(*operands)
 
 
@@ -36,7 +37,7 @@
     return jnp.sum(value, axis=1, keepdims=True)
 
 
-def respond(block, load, gamma, energy, answer, copies=()):
+def respond(block, load, gamma, energy, answer, copies=(), last=False):
     ntile, ncase, width = load.shape
     each = 2
     total = jnp.zeros((2 * ncase, ntile * width), jnp.float32)
@@ -55,11 +56,16 @@
     work = 0.5 * energy
     for i in range(ntile):
         tile = total[:, i * width : (i + 1) * width]
-        answer[i] = tile
+        if not last:
+            answer[i] = tile
         work = work + load[i] * tile
     lane = lax.broadcasted_iota(jnp.int32, work.shape, 1)
     sums = jnp.where(lane == 0, per_case(0.5 * gamma), 0.0)
-    answer[ntile] = jnp.where(lane == 1, per_case(work), sums)
+    sums = jnp.where(lane == 1, per_case(work), sums)
+    if last:
+        answer[...] = jnp.broadcast_to(sums[None], answer.shape)
+    else:
+        answer[ntile] = sums
 
 
 def pack_kernel(nh, tiles, place, field, table, message):
@@ -171,7 +177,7 @@
         return gamma, energy
 
     gamma, energy = lax.fori_loop(0, nrow // room, pair, (zero, zero))
-    respond(block, load, gamma, energy, answer)
+    respond(block, load, gamma, energy, answer, last=last)
 
 
 def list_kernel(first, keep, known, comp, mine, theirs, *refs):
@@ -201,14 +207,30 @@
     lax.fori_loop(0, npatch, body, 0, unroll=4)
 
 
-def end_kernel(sums, known, r, d, x, out):
-    npatch, nh, ncase, width = r.shape
-    _, alpha, beta = steps(False, sums[...], known[...])
-    alpha = jnp.broadcast_to(alpha, (ncase, width))[None]
-    beta = jnp.broadcast_to(beta, (ncase, width))[None]
+def end_kernel(keep, sums, known, comp, mine, theirs, r_in, d_in, x_in, s_in, out, moved):
+    npatch, nh, ncase, width = r_in.shape
+    total = sums[0]
+    for i in range(1, sums.shape[0]):
+        total = total + sums[i]
+    _, alpha, beta = steps(False, total, known[...])
+    one, two = jnp.broadcast_to(alpha, (ncase, width)), jnp.broadcast_to(beta, (ncase, width))
+    alpha = jnp.broadcast_to(known[:, 1:2], (ncase, width))
+    beta = jnp.broadcast_to(known[:, 2:3], (ncase, width))
+
+    def body(p, carry):
+        on, row = keep[p], comp[pl.ds(p, 1), :]
+        for h in range(nh):
+            residual = r_in[p, h]
+            c = row[:, h * width : (h + 1) * width]
+            image = on * (mine[p, h] + theirs[p, h] + c * residual) + beta * s_in[p, h]
+            direction = residual + beta * d_in[p, h]
+            residual = residual - alpha * image
+            moved[h, p] = x_in[p, h] + alpha * direction + one * (residual + two * direction)
+        return carry
+
+    lax.fori_loop(0, npatch, body, 0, unroll=4)
     for h in range(nh):
-        moved = x[:, h] + alpha * (r[:, h] + beta * d[:, h])
-        out[:, :, h * width : (h + 1) * width] = jnp.swapaxes(moved, 0, 1)
+        out[:, :, h * width : (h + 1) * width] = jnp.swapaxes(moved[h], 0, 1)
 
 
 def on_device(rhs, compliance, plate_owner, found_owner, slot_pairs, active, inverse):
@@ -306,6 +328,7 @@
             part,
             sibling(part),
             *lists,
+            cost=pl.CostEstimate(flops=16 * rhs.size, bytes_accessed=44 * rhs.size, transcendentals=0),
         )
 
     known = jnp.zeros((ncase, LANES), jnp.float32)
@@ -323,12 +346,12 @@
         b = jnp.concatenate([part[half:] for part in parts])
         far_a, far_b = swap(a, 1), swap(b, 2)
         a, b = jnp.concatenate([a, far_a]), jnp.concatenate([b, far_b])
+        far_a, far_b = swap(a, 2), swap(b, 1)
         if step > 0:
-            a, b, lists = lax.optimization_barrier((a, b, lists))
-        far_a, far_b = swap(a, 2), swap(b, 1)
+            far_a, far_b, lists = lax.optimization_barrier((far_a, far_b, lists))
         *state, own, part, known = call(
             functools.partial(home_kernel, step == 0, last, nh, room, lines),
-            (field,) * (0 if last else 2) + (answer, f32(npatch, nh, ncase, LANES), f32(ncase, LANES)),
+            (field,) * (0 if last else 2) + (f32(nbody * nsub, ncase, LANES) if last else answer, f32(npatch, nh, ncase, LANES), f32(ncase, LANES)),
             [SMEM] * 4 + [VMEM] * (8 + len(state)),
             near,
             far,
@@ -345,14 +368,20 @@
             *state,
             scratch=[load, spread],
         )
-    sums = own[per - 1]
-    others = sibling(sums)
-    others, part = lax.optimization_barrier((others, part))
-    sums = sums + others
-    r, d, x, _ = update(ITERS - 2, lists, known, part)
-    sums = tree([sums] + [swap(sums, i) for i in range(1, 4)])
-    sums = tree([sums] + [swap(sums, 4 * z) for z in range(1, nz)])
-    return call(end_kernel, f32(ncase, npatch, gap), [VMEM] * 5, sums, known, r, d, x)
+    sums = lax.all_to_all(own, ("body", "sub"), split_axis=0, concat_axis=0, tiled=True)
+    return call(
+        end_kernel,
+        f32(ncase, npatch, gap),
+        [SMEM] + [VMEM] * 9,
+        keep,
+        sums,
+        known,
+        compliance,
+        part,
+        sibling(part),
+        *lists,
+        scratch=[pltpu.VMEM((nh, npatch, ncase, LANES), jnp.float32)],
+    )
 
 
 def solution(mesh):

time: 153 us -> 146 us (0.954)
  blocking collectives: 39.4 us -> 50.5 us
  waiting for transfers between devices: 56.2 us -> 46.6 us
  starting transfers between devices: 31.7 us -> 24.2 us
    all_to_all x0 -> x1, blocking collectives: none -> 11.2 us  [on_device(): lax.all_to_all(own, ('body', 'sub'), split_axis=0, concat_axis=0, tiled=T...]
    ppermute x27 -> x21, waiting for transfers between devices: 51.3 us -> 42.8 us  [swap(): return lax.ppermute(value, 'sub', [(i, i ^ far) for i in range(nsub)])]
    ppermute x27 -> x21, starting transfers between devices: 31.4 us -> 24.1 us  [swap(): return lax.ppermute(value, 'sub', [(i, i ^ far) for i in range(nsub)])]
    ppermute x7 -> x6, waiting for transfers between devices: 4.91 us -> 3.76 us  [sibling(): lax.ppermute(value, 'body', [(i, nbody - 1 - i) for i in range(nbody)])]
    pallas_call x9 -> x8, Pallas kernels: 18.9 us -> 18.5 us  [call(): pl.pallas_call(kernel, out_shape=tuple(out_shape) if several else out_sha...]
  transfers between devices with their start and end apart: 34 -> 27, of which waited for: 26 -> 18; matrix products, arithmetic and copies ran while one was open for 0% -> 0% of each run, Pallas kernels for 0% -> 1%
where the time goes in v9:
time: 146 us
  blocking collectives  50.5 us (35%)
  waiting for transfers between devices  46.6 us (32%)
  starting transfers between devices  24.2 us (17%)
  Pallas kernels  18.5 us (13%)
  other arithmetic  3.37 us (2%)
    ppermute x21, waiting for transfers between devices, swap(): return lax.ppermute(value, 'sub', [(i, i ^ far) for i in range(nsub)])  42.8 us
    all_to_all x1, blocking collectives, exchange(): lax.all_to_all(message, 'sub', split_axis=0, concat_axis=0, tiled=True)  39.4 us
    ppermute x21, starting transfers between devices, swap(): return lax.ppermute(value, 'sub', [(i, i ^ far) for i in range(nsub)])  24.1 us
    pallas_call x8, Pallas kernels, call(): pl.pallas_call(kernel, out_shape=tuple(out_shape) if several else out_sha...  18.5 us
    all_to_all x1, blocking collectives, on_device(): lax.all_to_all(own, ('body', 'sub'), split_axis=0, concat_axis=0, tiled=T...  11.2 us
    ppermute x6, waiting for transfers between devices, sibling(): lax.ppermute(value, 'body', [(i, nbody - 1 - i) for i in range(nbody)])  3.76 us
  transfers between devices with their start and end apart: 27, of which 18 were waited for; matrix products, arithmetic and copies ran while one was open for 0% of the time, Pallas kernels for 1%

profile of v9, /device:TPU:0, one launch (start us, length us, event | category | flops | bytes accessed | tf_op | source)
XLA Modules:
  0.0 146.0 jit_solution(2123954564362404624)
XLA Ops:
  2.5 1.1 convolution_bitcast_fusion
  5.2 39.4 %all_to_all.10 = f32[16,19,8,128]{3,2,1,0:T(8,128)S(1)} all-to-all(f32[16,19,8,128]{3,2,1,0:T(8,128)S(1)} %bitcast.59), channel_id=1, replica_groups=mesh['body'=2,'sub'=16] {'sub'}, dimensions={0} | all-to-all | bytes 2490368 | tf_op jit(solution)/shard_map/all_to_all | solution.py:255
  45.7 4.4 %shard_map.74 = (f32[128,2,8,128]{3,2,1,0:T(8,128)S(1)}, f32[32,8,128]{2,1,0:T(8,128)S(1)}, f32[17,8,128]{2,1,0:T(8,128)S(1)}, bf16[2048,2048]{1,0:T(8,128)(2,1)S(1)}) custom-call(s32[128]{0:T(128)S(1)} %convert_element_type.28.place, f32[304,8,128]{2,1,0:T(8,128)S(1)} %bitcast.58, bf16[2048,2048]{1,0:T(8,128)(2,1)} %bitcast.62), custom_call_target="tpu_custom_call" | custom-call | tf_op jit(solution)/shard_map/pallas_call | solution.py:25
  50.1 1.2 collective-permute-done
  52.3 1.3 collective-permute-start.2
  53.6 2.2 %collective-permute-start.3 = (f32[17,8,128]{2,1,0:T(8,128)S(1)}, f32[17,8,128]{2,1,0:T(8,128)S(1)}, u32[]{:S(2)}, u32[]{:S(2)}) collective-permute-start(f32[17,8,128]{2,1,0:T(8,128)S(1)} %pad_maximum_fusion.6), channel_id=1, source_target_pairs={{0,12},{1,13},{2,14},{3,15},{4,8},{5,9},{6,10},{7,11},{8,4},{9,5},... | collective-permute-start | bytes 208904 | tf_op jit(solution)/shard_map/ppermute | solution.py:258
  56.5 4.4 %collective-permute-done.2 = f32[17,8,128]{2,1,0:T(8,128)S(1)} collective-permute-done((f32[17,8,128]{2,1,0:T(8,128)S(1)}, f32[17,8,128]{2,1,0:T(8,128)S(1)}, u32[]{:S(2)}, u32[]{:S(2)}) %collective-permute-start.2) | collective-permute-done | bytes 69664 | tf_op jit(solution)/shard_map/ppermute | solution.py:258
  62.3 4.0 %collective-permute-done.6 = f32[36,8,128]{2,1,0:T(8,128)S(1)} collective-permute-done((f32[36,8,128]{2,1,0:T(8,128)S(1)}, f32[36,8,128]{2,1,0:T(8,128)S(1)}, u32[]{:S(2)}, u32[]{:S(2)}) %collective-permute-start.6) | collective-permute-done | bytes 147488 | tf_op jit(solution)/shard_map/ppermute | solution.py:258
  66.8 1.3 collective-permute-done.4
  68.1 1.4 collective-permute-start.5
  69.5 5.0 %collective-permute-done.5.far_a = f32[64,8,128]{2,1,0:T(8,128)S(1)} collective-permute-done((f32[64,8,128]{2,1,0:T(8,128)S(1)}, f32[64,8,128]{2,1,0:T(8,128)S(1)}, u32[]{:S(2)}, u32[]{:S(2)}) %collective-permute-start.5) | collective-permute-done | bytes 262176 | tf_op jit(solution)/shard_map/ppermute | solution.py:258
  74.5 3.0 %shard_map.75 = (f32[128,2,8,128]{3,2,1,0:T(8,128)S(1)}, f32[128,2,8,128]{3,2,1,0:T(8,128)S(1)}, f32[17,8,128]{2,1,0:T(8,128)S(1)}, f32[64,2,8,128]{3,2,1,0:T(8,128)S(1)}, f32[8,128]{1,0:T(8,128)S(1)}) custom-call(s32[128]{0:T(128)S(1)} %convert_element_type.28.place, s32[128]{0:T(128)S(1)} %convert_element_type.30.away, f32[128]{0:T(128)S(1)} %reshape_squeeze.2.keep, ...), custom_call_target="tpu_custom_call" | custom-call | tf_op jit(solution)/shard_map/pallas_call | solution.py:25
  77.5 1.2 collective-permute-done.8
  78.9 1.3 collective-permute-start.10
  80.2 3.0 %collective-permute-start.11 = (f32[17,8,128]{2,1,0:T(8,128)S(1)}, f32[17,8,128]{2,1,0:T(8,128)S(1)}, u32[]{:S(2)}, u32[]{:S(2)}) collective-permute-start(f32[17,8,128]{2,1,0:T(8,128)S(1)} %pad_maximum_fusion.7), channel_id=1, source_target_pairs={{0,12},{1,13},{2,14},{3,15},{4,8},{5,9},{6,10},{7,11},{8,4},{9,5},... | collective-permute-start | bytes 208904 | tf_op jit(solution)/shard_map/ppermute | solution.py:258
  84.1 3.7 %collective-permute-done.10 = f32[17,8,128]{2,1,0:T(8,128)S(1)} collective-permute-done((f32[17,8,128]{2,1,0:T(8,128)S(1)}, f32[17,8,128]{2,1,0:T(8,128)S(1)}, u32[]{:S(2)}, u32[]{:S(2)}) %collective-permute-start.10) | collective-permute-done | bytes 69664 | tf_op jit(solution)/shard_map/ppermute | solution.py:258
  87.9 1.7 %collective-permute-start.14 = (f32[36,8,128]{2,1,0:T(8,128)S(1)}, f32[36,8,128]{2,1,0:T(8,128)S(1)}, u32[]{:S(2)}, u32[]{:S(2)}) collective-permute-start(f32[36,8,128]{2,1,0:T(8,128)S(1)} %pad_maximum_fusion.1), channel_id=1, source_target_pairs={{0,2},{1,3},{2,0},{3,1},{4,6},{5,7},{6,4},{7,5},{8,10},{9,11},{10,... | collective-permute-start | bytes 442376 | tf_op jit(solution)/shard_map/ppermute | solution.py:258
  90.2 2.9 %collective-permute-done.14 = f32[36,8,128]{2,1,0:T(8,128)S(1)} collective-permute-done((f32[36,8,128]{2,1,0:T(8,128)S(1)}, f32[36,8,128]{2,1,0:T(8,128)S(1)}, u32[]{:S(2)}, u32[]{:S(2)}) %collective-permute-start.14) | collective-permute-done | bytes 147488 | tf_op jit(solution)/shard_map/ppermute | solution.py:258
  93.1 1.0 collective-permute-start.15
  94.1 1.9 %collective-permute-done.12 = f32[32,8,128]{2,1,0:T(8,128)S(1)} collective-permute-done((f32[32,8,128]{2,1,0:T(8,128)S(1)}, f32[32,8,128]{2,1,0:T(8,128)S(1)}, u32[]{:S(2)}, u32[]{:S(2)}) %collective-permute-start.12) | collective-permute-done | bytes 131104 | tf_op jit(solution)/shard_map/ppermute | solution.py:258
  97.5 5.0 %collective-permute-done.13.far_a = f32[64,8,128]{2,1,0:T(8,128)S(1)} collective-permute-done((f32[64,8,128]{2,1,0:T(8,128)S(1)}, f32[64,8,128]{2,1,0:T(8,128)S(1)}, u32[]{:S(2)}, u32[]{:S(2)}) %collective-permute-start.13) | collective-permute-done | bytes 262176 | tf_op jit(solution)/shard_map/ppermute | solution.py:258
  102.5 3.1 %shard_map.77 = (f32[128,2,8,128]{3,2,1,0:T(8,128)S(1)}, f32[128,2,8,128]{3,2,1,0:T(8,128)S(1)}, f32[17,8,128]{2,1,0:T(8,128)S(1)}, f32[64,2,8,128]{3,2,1,0:T(8,128)S(1)}, f32[8,128]{1,0:T(8,128)S(1)}) custom-call(s32[128]{0:T(128)S(1)} %convert_element_type.28.place, s32[128]{0:T(128)S(1)} %convert_element_type.30.away, f32[128]{0:T(128)S(1)} %reshape_squeeze.2.keep, ...), custom_call_target="tpu_custom_call" | custom-call | tf_op jit(solution)/shard_map/pallas_call | solution.py:25
  105.7 1.3 collective-permute-done.17
  108.4 3.0 %collective-permute-start.20 = (f32[17,8,128]{2,1,0:T(8,128)S(1)}, f32[17,8,128]{2,1,0:T(8,128)S(1)}, u32[]{:S(2)}, u32[]{:S(2)}) collective-permute-start(f32[17,8,128]{2,1,0:T(8,128)S(1)} %pad_maximum_fusion.8), channel_id=1, source_target_pairs={{0,12},{1,13},{2,14},{3,15},{4,8},{5,9},{6,10},{7,11},{8,4},{9,5},... | collective-permute-start | bytes 208904 | tf_op jit(solution)/shard_map/ppermute | solution.py:258
  112.1 4.3 %collective-permute-done.19 = f32[17,8,128]{2,1,0:T(8,128)S(1)} collective-permute-done((f32[17,8,128]{2,1,0:T(8,128)S(1)}, f32[17,8,128]{2,1,0:T(8,128)S(1)}, u32[]{:S(2)}, u32[]{:S(2)}) %collective-permute-start.19) | collective-permute-done | bytes 69664 | tf_op jit(solution)/shard_map/ppermute | solution.py:258
  116.6 1.3 collective-permute-start.21
  117.9 4.0 %collective-permute-done.23 = f32[36,8,128]{2,1,0:T(8,128)S(1)} collective-permute-done((f32[36,8,128]{2,1,0:T(8,128)S(1)}, f32[36,8,128]{2,1,0:T(8,128)S(1)}, u32[]{:S(2)}, u32[]{:S(2)}) %collective-permute-start.23) | collective-permute-done | bytes 147488 | tf_op jit(solution)/shard_map/ppermute | solution.py:258
  122.8 2.2 %collective-permute-start.22 = (f32[64,8,128]{2,1,0:T(8,128)S(1)}, f32[64,8,128]{2,1,0:T(8,128)S(1)}, u32[]{:S(2)}, u32[]{:S(2)}) collective-permute-start(f32[64,8,128]{2,1,0:T(8,128)S(1)} %constant_dynamic-update-slice_fusion.20.near_a), channel_id=1, source_target_pairs={{0,2},{1,3},{2,0},{3,1},{4,6},{5,7},{6,4},{7,5},{8,10},{9,11},{10,... | collective-permute-start | bytes 786440 | tf_op jit(solution)/shard_map/ppermute | solution.py:258
  126.0 3.4 %collective-permute-done.22.far_a = f32[64,8,128]{2,1,0:T(8,128)S(1)} collective-permute-done((f32[64,8,128]{2,1,0:T(8,128)S(1)}, f32[64,8,128]{2,1,0:T(8,128)S(1)}, u32[]{:S(2)}, u32[]{:S(2)}) %collective-permute-start.22) | collective-permute-done | bytes 262176 | tf_op jit(solution)/shard_map/ppermute | solution.py:258
  129.4 3.2 %shard_map.79 = (f32[32,8,128]{2,1,0:T(8,128)S(1)}, f32[64,2,8,128]{3,2,1,0:T(8,128)S(1)}, f32[8,128]{1,0:T(8,128)S(1)}) custom-call(s32[128]{0:T(128)S(1)} %convert_element_type.28.place, s32[128]{0:T(128)S(1)} %convert_element_type.30.away, f32[128]{0:T(128)S(1)} %reshape_squeeze.2.keep, s32[64]{0:T(128)S(1)} %get-tuple-element.56.picked, ...), custom_call_target="tpu_custom_call" | custom-call | tf_op jit(solution)/shard_map/pallas_call | solution.py:25
  132.6 11.2 %all_to_all.11.sums = f32[32,8,128]{2,1,0:T(8,128)S(1)} all-to-all(f32[32,8,128]{2,1,0:T(8,128)S(1)} %get-tuple-element.92), channel_id=1, replica_groups=mesh['body'=2,'sub'=16] {'body','sub'}, dimensions={0} | all-to-all | bytes 262144 | tf_op jit(solution)/shard_map/all_to_all | solution.py:371
  143.8 2.2 %shard_map.80 = f32[8,64,256]{2,1,0:T(8,128)} custom-call(f32[64]{0:T(128)S(1)} %get-tuple-element.155.keep, f32[32,8,128]{2,1,0:T(8,128)S(1)} %all_to_all.11.sums, f32[8,128]{1,0:T(8,128)S(1)} %get-tuple-element.93.known, f32[64,256]{1,0:T(8,128)S(1)} %copy-done, f32[64,2,8,128]{3,2,1,0:T(8,128)S(1)} %get-tuple-element.94.mine, ...), custom_call_target="tpu_custom_call" | custom-call | tf_op jit(solution)/shard_map/pallas_call | solution.py:25
  (103 shorter events, 15.9 us)
Async XLA Ops:
  0.0 3.7 %copy-start.1 = (f32[8,64,256]{2,1,0:T(8,128)S(1)}, f32[8,64,256]{2,1,0:T(8,128)}, u32[]{:S(2)}) copy-start(f32[8,64,256]{2,1,0:T(8,128)} %param.7) | copy-start | bytes 1572868
  50.0 1.3 collective-permute-start
  51.4 5.1 %collective-permute-start.1 = (f32[17,8,128]{2,1,0:T(8,128)S(1)}, f32[17,8,128]{2,1,0:T(8,128)S(1)}, u32[]{:S(2)}, u32[]{:S(2)}) collective-permute-start(f32[17,8,128]{2,1,0:T(8,128)S(1)} %pad_maximum_fusion.6), channel_id=1, source_target_pairs={{0,4},{1,5},{2,6},{3,7},{4,0},{5,1},{6,2},{7,3},{8,12},{9,13},{10,... | collective-permute-start | bytes 208904 | tf_op jit(solution)/shard_map/ppermute | solution.py:258
  52.3 8.6 %collective-permute-start.2 = (f32[17,8,128]{2,1,0:T(8,128)S(1)}, f32[17,8,128]{2,1,0:T(8,128)S(1)}, u32[]{:S(2)}, u32[]{:S(2)}) collective-permute-start(f32[17,8,128]{2,1,0:T(8,128)S(1)} %pad_maximum_fusion.6), channel_id=1, source_target_pairs={{0,8},{1,9},{2,10},{3,11},{4,12},{5,13},{6,14},{7,15},{8,0},{9,1},... | collective-permute-start | bytes 208904 | tf_op jit(solution)/shard_map/ppermute | solution.py:258
  53.6 7.3 %collective-permute-start.3 = (f32[17,8,128]{2,1,0:T(8,128)S(1)}, f32[17,8,128]{2,1,0:T(8,128)S(1)}, u32[]{:S(2)}, u32[]{:S(2)}) collective-permute-start(f32[17,8,128]{2,1,0:T(8,128)S(1)} %pad_maximum_fusion.6), channel_id=1, source_target_pairs={{0,12},{1,13},{2,14},{3,15},{4,8},{5,9},{6,10},{7,11},{8,4},{9,5},... | collective-permute-start | bytes 208904 | tf_op jit(solution)/shard_map/ppermute | solution.py:258
  60.9 5.5 %collective-permute-start.6 = (f32[36,8,128]{2,1,0:T(8,128)S(1)}, f32[36,8,128]{2,1,0:T(8,128)S(1)}, u32[]{:S(2)}, u32[]{:S(2)}) collective-permute-start(f32[36,8,128]{2,1,0:T(8,128)S(1)} %pad_maximum_fusion), channel_id=1, source_target_pairs={{0,2},{1,3},{2,0},{3,1},{4,6},{5,7},{6,4},{7,5},{8,10},{9,11},{10,... | collective-permute-start | bytes 442376 | tf_op jit(solution)/shard_map/ppermute | solution.py:258
  61.7 6.3 %collective-permute-start.4 = (f32[32,8,128]{2,1,0:T(8,128)S(1)}, f32[32,8,128]{2,1,0:T(8,128)S(1)}, u32[]{:S(2)}, u32[]{:S(2)}) collective-permute-start(f32[32,8,128]{2,1,0:T(8,128)S(1)} %pad_maximum_fusion.3), channel_id=1, source_target_pairs={{0,1},{1,0},{2,3},{3,2},{4,5},{5,4},{6,7},{7,6},{8,9},{9,8},{10,11... | collective-permute-start | bytes 393224 | tf_op jit(solution)/shard_map/ppermute | solution.py:258
  66.4 8.1 %collective-permute-start.7 = (f32[72,8,128]{2,1,0:T(8,128)S(1)}, f32[72,8,128]{2,1,0:T(8,128)S(1)}, u32[]{:S(2)}, u32[]{:S(2)}) collective-permute-start(f32[72,8,128]{2,1,0:T(8,128)S(1)} %constant_dynamic-update-slice_fusion.5.near_b), channel_id=1, source_target_pairs={{0,1},{1,0},{2,3},{3,2},{4,5},{5,4},{6,7},{7,6},{8,9},{9,8},{10,11... | collective-permute-start | bytes 884744 | tf_op jit(solution)/shard_map/ppermute | solution.py:258
  68.1 6.4 %collective-permute-start.5 = (f32[64,8,128]{2,1,0:T(8,128)S(1)}, f32[64,8,128]{2,1,0:T(8,128)S(1)}, u32[]{:S(2)}, u32[]{:S(2)}) collective-permute-start(f32[64,8,128]{2,1,0:T(8,128)S(1)} %constant_dynamic-update-slice_fusion.near_a), channel_id=1, source_target_pairs={{0,2},{1,3},{2,0},{3,1},{4,6},{5,7},{6,4},{7,5},{8,10},{9,11},{10,... | collective-permute-start | bytes 786440 | tf_op jit(solution)/shard_map/ppermute | solution.py:258
  77.5 19.1 %copy-start = (f32[64,256]{1,0:T(8,128)S(1)}, f32[64,256]{1,0:T(8,128)}, u32[]{:S(2)}) copy-start(f32[64,256]{1,0:T(8,128)} %comp.5) | copy-start | bytes 196612
  77.5 1.3 collective-permute-start.8
  78.8 5.3 %collective-permute-start.9 = (f32[17,8,128]{2,1,0:T(8,128)S(1)}, f32[17,8,128]{2,1,0:T(8,128)S(1)}, u32[]{:S(2)}, u32[]{:S(2)}) collective-permute-start(f32[17,8,128]{2,1,0:T(8,128)S(1)} %pad_maximum_fusion.7), channel_id=1, source_target_pairs={{0,4},{1,5},{2,6},{3,7},{4,0},{5,1},{6,2},{7,3},{8,12},{9,13},{10,... | collective-permute-start | bytes 208904 | tf_op jit(solution)/shard_map/ppermute | solution.py:258
  78.9 9.0 %collective-permute-start.10 = (f32[17,8,128]{2,1,0:T(8,128)S(1)}, f32[17,8,128]{2,1,0:T(8,128)S(1)}, u32[]{:S(2)}, u32[]{:S(2)}) collective-permute-start(f32[17,8,128]{2,1,0:T(8,128)S(1)} %pad_maximum_fusion.7), channel_id=1, source_target_pairs={{0,8},{1,9},{2,10},{3,11},{4,12},{5,13},{6,14},{7,15},{8,0},{9,1},... | collective-permute-start | bytes 208904 | tf_op jit(solution)/shard_map/ppermute | solution.py:258
  80.2 7.6 %collective-permute-start.11 = (f32[17,8,128]{2,1,0:T(8,128)S(1)}, f32[17,8,128]{2,1,0:T(8,128)S(1)}, u32[]{:S(2)}, u32[]{:S(2)}) collective-permute-start(f32[17,8,128]{2,1,0:T(8,128)S(1)} %pad_maximum_fusion.7), channel_id=1, source_target_pairs={{0,12},{1,13},{2,14},{3,15},{4,8},{5,9},{6,10},{7,11},{8,4},{9,5},... | collective-permute-start | bytes 208904 | tf_op jit(solution)/shard_map/ppermute | solution.py:258
  83.3 13.3 %collective-permute-start.16 = (f32[64,2,8,128]{3,2,1,0:T(8,128)S(1)}, f32[64,2,8,128]{3,2,1,0:T(8,128)S(1)}, u32[]{:S(2)}, u32[]{:S(2)}) collective-permute-start(f32[64,2,8,128]{3,2,1,0:T(8,128)S(1)} %get-tuple-element.66.mine), channel_id=1, source_target_pairs={{0,16},{16,0},{1,17},{17,1},{2,18},{18,2},{3,19},{19,3},{4,20},{20... | collective-permute-start | bytes 1572872 | tf_op jit(solution)/shard_map/ppermute | solution.py:261
  87.9 5.2 %collective-permute-start.14 = (f32[36,8,128]{2,1,0:T(8,128)S(1)}, f32[36,8,128]{2,1,0:T(8,128)S(1)}, u32[]{:S(2)}, u32[]{:S(2)}) collective-permute-start(f32[36,8,128]{2,1,0:T(8,128)S(1)} %pad_maximum_fusion.1), channel_id=1, source_target_pairs={{0,2},{1,3},{2,0},{3,1},{4,6},{5,7},{6,4},{7,5},{8,10},{9,11},{10,... | collective-permute-start | bytes 442376 | tf_op jit(solution)/shard_map/ppermute | solution.py:258
  89.6 6.4 %collective-permute-start.12 = (f32[32,8,128]{2,1,0:T(8,128)S(1)}, f32[32,8,128]{2,1,0:T(8,128)S(1)}, u32[]{:S(2)}, u32[]{:S(2)}) collective-permute-start(f32[32,8,128]{2,1,0:T(8,128)S(1)} %pad_maximum_fusion.4), channel_id=1, source_target_pairs={{0,1},{1,0},{2,3},{3,2},{4,5},{5,4},{6,7},{7,6},{8,9},{9,8},{10,11... | collective-permute-start | bytes 393224 | tf_op jit(solution)/shard_map/ppermute | solution.py:258
  93.1 9.4 %collective-permute-start.15 = (f32[72,8,128]{2,1,0:T(8,128)S(1)}, f32[72,8,128]{2,1,0:T(8,128)S(1)}, u32[]{:S(2)}, u32[]{:S(2)}) collective-permute-start(f32[72,8,128]{2,1,0:T(8,128)S(1)} %constant_dynamic-update-slice_fusion.15.near_b), channel_id=1, source_target_pairs={{0,1},{1,0},{2,3},{3,2},{4,5},{5,4},{6,7},{7,6},{8,9},{9,8},{10,11... | collective-permute-start | bytes 884744 | tf_op jit(solution)/shard_map/ppermute | solution.py:258
  96.1 6.4 %collective-permute-start.13 = (f32[64,8,128]{2,1,0:T(8,128)S(1)}, f32[64,8,128]{2,1,0:T(8,128)S(1)}, u32[]{:S(2)}, u32[]{:S(2)}) collective-permute-start(f32[64,8,128]{2,1,0:T(8,128)S(1)} %constant_dynamic-update-slice_fusion.10.near_a), channel_id=1, source_target_pairs={{0,2},{1,3},{2,0},{3,1},{4,6},{5,7},{6,4},{7,5},{8,10},{9,11},{10,... | collective-permute-start | bytes 786440 | tf_op jit(solution)/shard_map/ppermute | solution.py:258
  105.7 1.3 collective-permute-start.17
  107.0 5.1 %collective-permute-start.18 = (f32[17,8,128]{2,1,0:T(8,128)S(1)}, f32[17,8,128]{2,1,0:T(8,128)S(1)}, u32[]{:S(2)}, u32[]{:S(2)}) collective-permute-start(f32[17,8,128]{2,1,0:T(8,128)S(1)} %pad_maximum_fusion.8), channel_id=1, source_target_pairs={{0,4},{1,5},{2,6},{3,7},{4,0},{5,1},{6,2},{7,3},{8,12},{9,13},{10,... | collective-permute-start | bytes 208904 | tf_op jit(solution)/shard_map/ppermute | solution.py:258
  107.8 8.6 %collective-permute-start.19 = (f32[17,8,128]{2,1,0:T(8,128)S(1)}, f32[17,8,128]{2,1,0:T(8,128)S(1)}, u32[]{:S(2)}, u32[]{:S(2)}) collective-permute-start(f32[17,8,128]{2,1,0:T(8,128)S(1)} %pad_maximum_fusion.8), channel_id=1, source_target_pairs={{0,8},{1,9},{2,10},{3,11},{4,12},{5,13},{6,14},{7,15},{8,0},{9,1},... | collective-permute-start | bytes 208904 | tf_op jit(solution)/shard_map/ppermute | solution.py:258
  108.4 8.0 %collective-permute-start.20 = (f32[17,8,128]{2,1,0:T(8,128)S(1)}, f32[17,8,128]{2,1,0:T(8,128)S(1)}, u32[]{:S(2)}, u32[]{:S(2)}) collective-permute-start(f32[17,8,128]{2,1,0:T(8,128)S(1)} %pad_maximum_fusion.8), channel_id=1, source_target_pairs={{0,12},{1,13},{2,14},{3,15},{4,8},{5,9},{6,10},{7,11},{8,4},{9,5},... | collective-permute-start | bytes 208904 | tf_op jit(solution)/shard_map/ppermute | solution.py:258
  111.4 13.6 %collective-permute-start.25 = (f32[64,2,8,128]{3,2,1,0:T(8,128)S(1)}, f32[64,2,8,128]{3,2,1,0:T(8,128)S(1)}, u32[]{:S(2)}, u32[]{:S(2)}) collective-permute-start(f32[64,2,8,128]{3,2,1,0:T(8,128)S(1)} %get-tuple-element.79.mine), channel_id=1, source_target_pairs={{0,16},{16,0},{1,17},{17,1},{2,18},{18,2},{3,19},{19,3},{4,20},{20... | collective-permute-start | bytes 1572872 | tf_op jit(solution)/shard_map/ppermute | solution.py:261
  116.4 5.5 %collective-permute-start.23 = (f32[36,8,128]{2,1,0:T(8,128)S(1)}, f32[36,8,128]{2,1,0:T(8,128)S(1)}, u32[]{:S(2)}, u32[]{:S(2)}) collective-permute-start(f32[36,8,128]{2,1,0:T(8,128)S(1)} %pad_maximum_fusion.2), channel_id=1, source_target_pairs={{0,2},{1,3},{2,0},{3,1},{4,6},{5,7},{6,4},{7,5},{8,10},{9,11},{10,... | collective-permute-start | bytes 442376 | tf_op jit(solution)/shard_map/ppermute | solution.py:258
  116.6 6.2 %collective-permute-start.21 = (f32[32,8,128]{2,1,0:T(8,128)S(1)}, f32[32,8,128]{2,1,0:T(8,128)S(1)}, u32[]{:S(2)}, u32[]{:S(2)}) collective-permute-start(f32[32,8,128]{2,1,0:T(8,128)S(1)} %pad_maximum_fusion.5), channel_id=1, source_target_pairs={{0,1},{1,0},{2,3},{3,2},{4,5},{5,4},{6,7},{7,6},{8,9},{9,8},{10,11... | collective-permute-start | bytes 393224 | tf_op jit(solution)/shard_map/ppermute | solution.py:258
  121.9 7.5 %collective-permute-start.24 = (f32[72,8,128]{2,1,0:T(8,128)S(1)}, f32[72,8,128]{2,1,0:T(8,128)S(1)}, u32[]{:S(2)}, u32[]{:S(2)}) collective-permute-start(f32[72,8,128]{2,1,0:T(8,128)S(1)} %constant_dynamic-update-slice_fusion.25.near_b), channel_id=1, source_target_pairs={{0,1},{1,0},{2,3},{3,2},{4,5},{5,4},{6,7},{7,6},{8,9},{9,8},{10,11... | collective-permute-start | bytes 884744 | tf_op jit(solution)/shard_map/ppermute | solution.py:258
  122.8 6.6 %collective-permute-start.22 = (f32[64,8,128]{2,1,0:T(8,128)S(1)}, f32[64,8,128]{2,1,0:T(8,128)S(1)}, u32[]{:S(2)}, u32[]{:S(2)}) collective-permute-start(f32[64,8,128]{2,1,0:T(8,128)S(1)} %constant_dynamic-update-slice_fusion.20.near_a), channel_id=1, source_target_pairs={{0,2},{1,3},{2,0},{3,1},{4,6},{5,7},{6,4},{7,5},{8,10},{9,11},{10,... | collective-permute-start | bytes 786440 | tf_op jit(solution)/shard_map/ppermute | solution.py:258
  132.6 11.3 %collective-permute-start.26 = (f32[64,2,8,128]{3,2,1,0:T(8,128)S(1)}, f32[64,2,8,128]{3,2,1,0:T(8,128)S(1)}, u32[]{:S(2)}, u32[]{:S(2)}) collective-permute-start(f32[64,2,8,128]{3,2,1,0:T(8,128)S(1)} %get-tuple-element.94.mine), channel_id=1, source_target_pairs={{0,16},{16,0},{1,17},{17,1},{2,18},{18,2},{3,19},{19,3},{4,20},{20... | collective-permute-start | bytes 1572872 | tf_op jit(solution)/shard_map/ppermute | solution.py:261

commit v10 on v9

--- a/solution.py
+++ b/solution.py
@@ -37,7 +37,7 @@
     return jnp.sum(value, axis=1, keepdims=True)
 
 
-def respond(block, load, gamma, energy, answer, copies=(), last=False):
+def respond(block, load, gamma, energy, answer, last=False):
     ntile, ncase, width = load.shape
     each = 2
     total = jnp.zeros((2 * ncase, ntile * width), jnp.float32)
@@ -45,8 +45,6 @@
         value = jnp.concatenate([load[j * each + i] for i in range(each)], axis=1)
         high = value.astype(jnp.bfloat16)
         low = (value - high.astype(jnp.float32)).astype(jnp.bfloat16)
-        if copies:
-            copies[j].wait()
         total = total + jnp.dot(
             jnp.concatenate([high, low], axis=0),
             block[j * each * width : (j + 1) * each * width, :],
@@ -68,21 +66,29 @@
         answer[ntile] = sums
 
 
-def pack_kernel(nh, tiles, place, field, table, message):
-    ndest = message.shape[0] // tiles
+def pack_kernel(nh, cut, room, place, field, table, *refs):
+    *outs, whole = refs
+    nz = len(outs) - 4
     extra = table.shape[1]
-    message[...] = jnp.zeros_like(message)
+    tiles = room * nh
+    whole[...] = jnp.zeros_like(whole)
 
     def body(p, carry):
-        message[pl.ds(place[p], nh)] = field[p]
+        whole[pl.ds(place[p], nh)] = field[p]
         return carry
 
     lax.fori_loop(0, field.shape[0], body, 0, unroll=4)
-    for i in range(ndest):
-        message[(i + 1) * tiles - extra : (i + 1) * tiles] = table[i]
-
-
-def start_kernel(nh, room, tiles, lines, place, message, block, r_out, comp, answer, held, load, sems):
+    first, second = cut * nh, tiles - cut * nh
+    for z in range(nz):
+        for m in range(4):
+            at = (z * 4 + m) * tiles
+            one, two = m * (first + extra), z * second
+            outs[z][one : one + first] = whole[at : at + first]
+            outs[z][one + first : one + first + extra] = table[z * 4 + m]
+            outs[nz + m][two : two + second] = whole[at + first : at + tiles]
+
+
+def block_kernel(block, held, sems):
     pieces = sems.shape[0]
     size = block.shape[0] // pieces
     copies = []
@@ -90,27 +96,51 @@
         rows = pl.ds(j * size, size)
         copies.append(pltpu.make_async_copy(block.at[rows], held.at[rows], sems.at[j]))
         copies[-1].start()
+    for copy in copies:
+        copy.wait()
+
+
+def start_kernel(nh, cut, room, lines, extra, nz, block, *refs):
+    a_z, refs = refs[:nz], refs[nz:]
+    a_far, refs = refs[:3], refs[3:]
+    b_near, refs = refs[:4], refs[4:]
+    b_far, refs = refs[: nz - 1], refs[nz - 1 :]
+    near, far, on, r_out, comp, answer, load, facts, sems = refs
+    copies = []
+    for z in range(nz):
+        for m in range(4):
+            part, at = (a_z[z], 0) if m == 0 else (a_far[m - 1], z * (cut * nh + extra))
+            rows = pl.ds(at + cut * nh + lines, extra - lines)
+            copies.append(pltpu.make_async_copy(part.at[rows], facts.at[z * 4 + m], sems.at[z * 4 + m]))
+            copies[-1].start()
     load[...] = jnp.zeros_like(load)
-    zero = jnp.zeros(r_out.shape[2:], jnp.float32)
-
-    def pair(i, sums):
-        gamma, energy = sums
-        comp[pl.ds(i * lines, lines)] = message[pl.ds(i * tiles + room * nh, lines)]
-        for j in range(room):
-            row = i * room + j
-            r = message[pl.ds(i * tiles + j * nh, nh)]
-            r_out[row] = r
-            load[pl.ds(place[row], nh)] += r
-            for h in range(nh):
-                line, sub = divmod(j * nh + h, SUBLANES)
-                c = message[i * tiles + room * nh + line, sub : sub + 1, :]
-                square = r[h] * r[h]
-                gamma = gamma + square
-                energy = energy + c * square
-        return gamma, energy
-
-    gamma, energy = lax.fori_loop(0, r_out.shape[0] // room, pair, (zero, zero))
-    respond(held, load, gamma, energy, answer, copies)
+    gamma = energy = jnp.zeros(r_out.shape[2:], jnp.float32)
+    first, second = cut * nh, (room - cut) * nh
+    for z in range(nz):
+        for m in range(4):
+            i = z * 4 + m
+            one, at_one = (a_z[z], 0) if m == 0 else (a_far[m - 1], z * (first + extra))
+            two, at_two = (b_near[m], 0) if z == 0 else (b_far[z - 1], m * second)
+            comp[i * lines : (i + 1) * lines] = one[at_one + first : at_one + first + lines]
+            copies[i].wait()
+            for j in range(room):
+                row = i * room + j
+                slot = facts[i, j // SUBLANES, j % SUBLANES, 0].astype(jnp.int32)
+                near[i, j] = slot
+                far[i, j] = facts[i, j // SUBLANES, j % SUBLANES, 1].astype(jnp.int32)
+                on[i, j] = facts[i, j // SUBLANES, j % SUBLANES, 2]
+                if j < cut:
+                    r = one[at_one + j * nh : at_one + (j + 1) * nh]
+                else:
+                    r = two[at_two + (j - cut) * nh : at_two + (j - cut + 1) * nh]
+                r_out[row] = r
+                load[pl.ds(slot, nh)] += r
+                for h in range(nh):
+                    line, sub = divmod(j * nh + h, SUBLANES)
+                    square = r[h] * r[h]
+                    gamma = gamma + square
+                    energy = energy + one[at_one + first + line, sub : sub + 1, :] * square
+    respond(block, load, gamma, energy, answer)
 
 
 def tree(values):
@@ -159,7 +189,7 @@
         gamma, energy = sums
         for j in range(room):
             row = i * room + j
-            near, far, on = place[row], away[row], keep[row]
+            near, far, on = place[i, j], away[i, j], keep[i, j]
             for h in range(nh):
                 line, sub = divmod(j * nh + h, SUBLANES)
                 c = comp[i * lines + line, sub : sub + 1, :]
@@ -247,12 +277,12 @@
     nrow = nsub * room
     lines = -(-room * nh // SUBLANES)
     deep = -(-room // SUBLANES)
-    tiles = room * nh + lines + deep
+    extra = lines + deep
+    cut = room // 2
+    first = cut * nh + extra
+    second = (room - cut) * nh
     nz = nsub // 4
     half = nslot // 2 * nh
-
-    def exchange(message):
-        return lax.all_to_all(message, "sub", split_axis=0, concat_axis=0, tiled=True)
 
     def swap(value, far):
         return lax.ppermute(value, "sub", [(i, i ^ far) for i in range(nsub)])
@@ -267,8 +297,7 @@
     index = jnp.arange(npatch, dtype=jnp.int32)
     earlier = (owner[None, :] == owner[:, None]) & (index[None, :] < index[:, None])
     rank = jnp.sum(earlier.astype(jnp.int32), axis=1)
-    row = owner * room + rank
-    place = owner * tiles + rank * nh
+    place = (owner ^ me) * room * nh + rank * nh
 
     def found(away):
         x_bit, y_bit, z_part = away & 1, (away >> 1) & 1, away >> 2
@@ -279,6 +308,7 @@
     facts = jnp.stack([slot * nh, found(owner ^ other)], axis=1).astype(jnp.float32)
     facts = jnp.concatenate([facts, keep[:, None]], axis=1)
     facts = jnp.concatenate([compliance, jnp.pad(facts, ((0, 0), (0, LANES - 3)))], axis=1)
+    row = (owner ^ me) * room + rank
     placed = (row[None, :] == jnp.arange(nrow, dtype=jnp.int32)[:, None]).astype(jnp.float32)
     facts = jnp.dot(placed, facts, precision=lax.Precision.HIGHEST).reshape(nsub, room, gap + LANES)
     lined = facts[:, :, :gap].reshape(nsub, room * nh, LANES)
@@ -290,33 +320,50 @@
     picked = found(me ^ other).astype(jnp.int32)
     place, picked = lax.optimization_barrier((place, picked))
 
-    message = call(
-        functools.partial(pack_kernel, nh, tiles),
-        f32(nsub * tiles, ncase, LANES),
+    packed = call(
+        functools.partial(pack_kernel, nh, cut, room),
+        (f32(4 * first, ncase, LANES),) * nz + (f32(nz * second, ncase, LANES),) * 4,
         [SMEM, VMEM, VMEM],
         place,
         start,
         table,
+        scratch=[pltpu.VMEM((nrow * nh, ncase, LANES), jnp.float32)],
     )
-    message = exchange(message.reshape(nsub, tiles, ncase, LANES))
-    facts = message[:, room * nh + lines :].reshape(nsub, deep * SUBLANES, LANES)[:, :room]
-    near, far, on = (facts[:, :, i].reshape(nrow) for i in range(3))
-    near, far = near.astype(jnp.int32), far.astype(jnp.int32)
-    message, near, far, on = lax.optimization_barrier((message, near, far, on))
-
+    a_z = [packed[0]] + [swap(packed[z], 4 * z) for z in range(1, nz)]
+    b_near = [packed[nz]] + [swap(packed[nz + m], m) for m in range(1, 4)]
+    b_far = [
+        swap(jnp.concatenate([part[z * second : (z + 1) * second] for part in b_near]), 4 * z)
+        for z in range(1, nz)
+    ]
+    a_far = [
+        swap(jnp.concatenate([part[m * first : (m + 1) * first] for part in a_z]), m) for m in range(1, 4)
+    ]
+    held = call(
+        block_kernel,
+        jax.ShapeDtypeStruct(block.shape, block.dtype),
+        [HBM],
+        pltpu.with_memory_space_constraint(block, pltpu.HBM),
+        scratch=[pltpu.SemaphoreType.DMA((nslot,))],
+        cost=pl.CostEstimate(flops=0, bytes_accessed=4 * block.size, transcendentals=0),
+    )
+    a_far, block = lax.optimization_barrier((a_far, held))
     field = f32(nrow, nh, ncase, LANES)
     answer = f32(per, ncase, LANES)
     load = pltpu.VMEM((nslot * nh, ncase, LANES), jnp.float32)
     spread = pltpu.VMEM((nsub * per, ncase, LANES), jnp.float32)
-    home_r, comp, own, block = call(
-        functools.partial(start_kernel, nh, room, tiles, lines),
-        (field, f32(nsub * lines, ncase, LANES), answer, jax.ShapeDtypeStruct(block.shape, block.dtype)),
-        [SMEM, VMEM, HBM],
-        near,
-        message.reshape(nsub * tiles, ncase, LANES),
-        pltpu.with_memory_space_constraint(block, pltpu.HBM),
-        scratch=[load, pltpu.SemaphoreType.DMA((nslot,))],
-    )
+    near, far, on, home_r, comp, own = pl.pallas_call(
+        functools.partial(start_kernel, nh, cut, room, lines, extra, nz),
+        out_shape=(jax.ShapeDtypeStruct((nsub, room), jnp.int32),) * 2
+        + (f32(nsub, room), field, f32(nsub * lines, ncase, LANES), answer),
+        in_specs=[VMEM] * (2 * nz + 7),
+        out_specs=(SMEM,) * 3 + (VMEM,) * 3,
+        scratch_shapes=[
+            load,
+            pltpu.SMEM((nsub, deep, SUBLANES, LANES), jnp.float32),
+            pltpu.SemaphoreType.DMA((nsub,)),
+        ],
+        compiler_params=PARAMS,
+    )(block, *a_z, *a_far, *b_near, *b_far)
     def update(step, lists, known, part):
         return call(
             functools.partial(list_kernel, step == 0),

time: 146 us -> 152 us (1.041)
  blocking collectives: 50.5 us -> 12.5 us
  starting transfers between devices: 24.2 us -> 52 us
  waiting for transfers between devices: 46.6 us -> 58.6 us
  Pallas kernels: 18.5 us -> 22.2 us
    all_to_all x1 -> x0, blocking collectives: 39.4 us -> none  [exchange(): lax.all_to_all(message, 'sub', split_axis=0, concat_axis=0, tiled=True)]
    ppermute x21 -> x33, starting transfers between devices: 24.1 us -> 51.8 us  [swap(): return lax.ppermute(value, 'sub', [(i, i ^ far) for i in range(nsub)])]
    ppermute x21 -> x33, waiting for transfers between devices: 42.8 us -> 54.8 us  [swap(): return lax.ppermute(value, 'sub', [(i, i ^ far) for i in range(nsub)])]
    pallas_call x0 -> x1, Pallas kernels: none -> 3.72 us  [on_device(): pl.pallas_call(functools.partial(start_kernel, nh, cut, room, lines, extr...]
  transfers between devices with their start and end apart: 27 -> 39, of which waited for: 18 -> 18; matrix products, arithmetic and copies ran while one was open for 0% -> 0% of each run, Pallas kernels for 1% -> 4%
where the time goes in v10:
time: 152 us
  waiting for transfers between devices  58.6 us (39%)
  starting transfers between devices  52 us (34%)
  Pallas kernels  22.2 us (15%)
  blocking collectives  12.5 us (8%)
  other arithmetic  3.77 us (2%)
    ppermute x33, waiting for transfers between devices, swap(): return lax.ppermute(value, 'sub', [(i, i ^ far) for i in range(nsub)])  54.8 us
    ppermute x33, starting transfers between devices, swap(): return lax.ppermute(value, 'sub', [(i, i ^ far) for i in range(nsub)])  51.8 us
    pallas_call x8, Pallas kernels, call(): pl.pallas_call(kernel, out_shape=tuple(out_shape) if several else out_sha...  18.4 us
    all_to_all x1, blocking collectives, on_device(): lax.all_to_all(own, ('body', 'sub'), split_axis=0, concat_axis=0, tiled=T...  12.5 us
    ppermute x6, waiting for transfers between devices, sibling(): lax.ppermute(value, 'body', [(i, nbody - 1 - i) for i in range(nbody)])  3.77 us
    pallas_call x1, Pallas kernels, on_device(): pl.pallas_call(functools.partial(start_kernel, nh, cut, room, lines, extr...  3.72 us
  transfers between devices with their start and end apart: 39, of which 18 were waited for; matrix products, arithmetic and copies ran while one was open for 0% of the time, Pallas kernels for 4%

profile of v10, /device:TPU:0, one launch (start us, length us, event | category | flops | bytes accessed | tf_op | source)
XLA Modules:
  0.0 151.6 jit_solution(3604993209904847045)
XLA Ops:
  6.2 3.0 %collective-permute-start.6 = (f32[32,8,128]{2,1,0:T(8,128)S(1)}, f32[32,8,128]{2,1,0:T(8,128)S(1)}, u32[]{:S(2)}, u32[]{:S(2)}) collective-permute-start(f32[32,8,128]{2,1,0:T(8,128)S(1)} %get-tuple-element.72), channel_id=1, source_target_pairs={{0,1},{1,0},{2,3},{3,2},{4,5},{5,4},{6,7},{7,6},{8,9},{9,8},{10,11... | collective-permute-start | bytes 393224 | tf_op jit(solution)/shard_map/ppermute | solution.py:288
  10.8 2.0 %collective-permute-start = (f32[44,8,128]{2,1,0:T(8,128)S(1)}, f32[44,8,128]{2,1,0:T(8,128)S(1)}, u32[]{:S(2)}, u32[]{:S(2)}) collective-permute-start(f32[44,8,128]{2,1,0:T(8,128)S(1)} %get-tuple-element.64), channel_id=1, source_target_pairs={{0,4},{1,5},{2,6},{3,7},{4,0},{5,1},{6,2},{7,3},{8,12},{9,13},{10,... | collective-permute-start | bytes 540680 | tf_op jit(solution)/shard_map/ppermute | solution.py:288
  12.8 2.6 %collective-permute-start.1 = (f32[44,8,128]{2,1,0:T(8,128)S(1)}, f32[44,8,128]{2,1,0:T(8,128)S(1)}, u32[]{:S(2)}, u32[]{:S(2)}) collective-permute-start(f32[44,8,128]{2,1,0:T(8,128)S(1)} %get-tuple-element.65), channel_id=1, source_target_pairs={{0,8},{1,9},{2,10},{3,11},{4,12},{5,13},{6,14},{7,15},{8,0},{9,1},... | collective-permute-start | bytes 540680 | tf_op jit(solution)/shard_map/ppermute | solution.py:288
  17.1 2.7 %collective-permute-start.10 = (f32[32,8,128]{2,1,0:T(8,128)S(1)}, f32[32,8,128]{2,1,0:T(8,128)S(1)}, u32[]{:S(2)}, u32[]{:S(2)}) collective-permute-start(f32[32,8,128]{2,1,0:T(8,128)S(1)} %pad_maximum_fusion.7), channel_id=1, source_target_pairs={{0,8},{1,9},{2,10},{3,11},{4,12},{5,13},{6,14},{7,15},{8,0},{9,1},... | collective-permute-start | bytes 393224 | tf_op jit(solution)/shard_map/ppermute | solution.py:288
  21.2 13.1 %collective-permute-done.1.refs_2_ = f32[44,8,128]{2,1,0:T(8,128)S(1)} collective-permute-done((f32[44,8,128]{2,1,0:T(8,128)S(1)}, f32[44,8,128]{2,1,0:T(8,128)S(1)}, u32[]{:S(2)}, u32[]{:S(2)}) %collective-permute-start.1) | collective-permute-done | bytes 180256 | tf_op jit(solution)/shard_map/ppermute | solution.py:288
  34.3 2.5 %collective-permute-start.5 = (f32[44,8,128]{2,1,0:T(8,128)S(1)}, f32[44,8,128]{2,1,0:T(8,128)S(1)}, u32[]{:S(2)}, u32[]{:S(2)}) collective-permute-start(f32[44,8,128]{2,1,0:T(8,128)S(1)} %pad_maximum_fusion.2), channel_id=1, source_target_pairs={{0,3},{1,2},{2,1},{3,0},{4,7},{5,6},{6,5},{7,4},{8,11},{9,10},{10,... | collective-permute-start | bytes 540680 | tf_op jit(solution)/shard_map/ppermute | solution.py:288
  38.0 2.8 %collective-permute-done.5.refs_6_ = f32[44,8,128]{2,1,0:T(8,128)S(1)} collective-permute-done((f32[44,8,128]{2,1,0:T(8,128)S(1)}, f32[44,8,128]{2,1,0:T(8,128)S(1)}, u32[]{:S(2)}, u32[]{:S(2)}) %collective-permute-start.5) | collective-permute-done | bytes 180256 | tf_op jit(solution)/shard_map/ppermute | solution.py:288
  40.8 4.4 %collective-permute-start.9 = (f32[32,8,128]{2,1,0:T(8,128)S(1)}, f32[32,8,128]{2,1,0:T(8,128)S(1)}, u32[]{:S(2)}, u32[]{:S(2)}) collective-permute-start(f32[32,8,128]{2,1,0:T(8,128)S(1)} %pad_maximum_fusion.6), channel_id=1, source_target_pairs={{0,4},{1,5},{2,6},{3,7},{4,0},{5,1},{6,2},{7,3},{8,12},{9,13},{10,... | collective-permute-start | bytes 393224 | tf_op jit(solution)/shard_map/ppermute | solution.py:288
  45.2 3.5 %shard_map.74.block = bf16[2048,2048]{1,0:T(8,128)(2,1)S(1)} custom-call(bf16[2048,2048]{1,0:T(8,128)(2,1)} %bitcast.56), custom_call_target="tpu_custom_call" | custom-call | bytes 16777216 | tf_op jit(solution)/shard_map/pallas_call | solution.py:25
  48.7 3.7 %shard_map.75 = (s32[16,8]{1,0:T(8,128)S(1)}, s32[16,8]{1,0:T(8,128)S(1)}, f32[16,8]{1,0:T(8,128)S(1)}, f32[128,2,8,128]{3,2,1,0:T(8,128)S(1)}, f32[32,8,128]{2,1,0:T(8,128)S(1)}, /*index=5*/f32[17,8,128]{2,1,0:T(8,128)S(1)}) custom-call(bf16[2048,2048]{1,0:T(8,128)(2,1)S(1)} %shard_map.74.block, f32[44,8,128]{2,1,0:T(8,128)S(1)} %get-tuple-element.63.refs_0_, ...), custom_call_target="tpu_custom_call" | custom-call | tf_op jit(solution)/shard_map/pallas_call | solution.py:354
  55.3 1.7 %collective-permute-start.14 = (f32[17,8,128]{2,1,0:T(8,128)S(1)}, f32[17,8,128]{2,1,0:T(8,128)S(1)}, u32[]{:S(2)}, u32[]{:S(2)}) collective-permute-start(f32[17,8,128]{2,1,0:T(8,128)S(1)} %pad_maximum_fusion.12), channel_id=1, source_target_pairs={{0,8},{1,9},{2,10},{3,11},{4,12},{5,13},{6,14},{7,15},{8,0},{9,1},... | collective-permute-start | bytes 208904 | tf_op jit(solution)/shard_map/ppermute | solution.py:288
  58.3 5.6 %collective-permute-done.14 = f32[17,8,128]{2,1,0:T(8,128)S(1)} collective-permute-done((f32[17,8,128]{2,1,0:T(8,128)S(1)}, f32[17,8,128]{2,1,0:T(8,128)S(1)}, u32[]{:S(2)}, u32[]{:S(2)}) %collective-permute-start.14) | collective-permute-done | bytes 69664 | tf_op jit(solution)/shard_map/ppermute | solution.py:288
  63.9 1.6 %collective-permute-start.18 = (f32[36,8,128]{2,1,0:T(8,128)S(1)}, f32[36,8,128]{2,1,0:T(8,128)S(1)}, u32[]{:S(2)}, u32[]{:S(2)}) collective-permute-start(f32[36,8,128]{2,1,0:T(8,128)S(1)} %pad_maximum_fusion.3), channel_id=1, source_target_pairs={{0,2},{1,3},{2,0},{3,1},{4,6},{5,7},{6,4},{7,5},{8,10},{9,11},{10,... | collective-permute-start | bytes 442376 | tf_op jit(solution)/shard_map/ppermute | solution.py:288
  65.6 1.6 %collective-permute-start.16 = (f32[32,8,128]{2,1,0:T(8,128)S(1)}, f32[32,8,128]{2,1,0:T(8,128)S(1)}, u32[]{:S(2)}, u32[]{:S(2)}) collective-permute-start(f32[32,8,128]{2,1,0:T(8,128)S(1)} %pad_maximum_fusion.9), channel_id=1, source_target_pairs={{0,1},{1,0},{2,3},{3,2},{4,5},{5,4},{6,7},{7,6},{8,9},{9,8},{10,11... | collective-permute-start | bytes 393224 | tf_op jit(solution)/shard_map/ppermute | solution.py:288
  67.1 2.0 %collective-permute-done.18 = f32[36,8,128]{2,1,0:T(8,128)S(1)} collective-permute-done((f32[36,8,128]{2,1,0:T(8,128)S(1)}, f32[36,8,128]{2,1,0:T(8,128)S(1)}, u32[]{:S(2)}, u32[]{:S(2)}) %collective-permute-start.18) | collective-permute-done | bytes 147488 | tf_op jit(solution)/shard_map/ppermute | solution.py:288
  69.2 1.6 %collective-permute-start.19 = (f32[72,8,128]{2,1,0:T(8,128)S(1)}, f32[72,8,128]{2,1,0:T(8,128)S(1)}, u32[]{:S(2)}, u32[]{:S(2)}) collective-permute-start(f32[72,8,128]{2,1,0:T(8,128)S(1)} %constant_dynamic-update-slice_fusion.5.near_b), channel_id=1, source_target_pairs={{0,1},{1,0},{2,3},{3,2},{4,5},{5,4},{6,7},{7,6},{8,9},{9,8},{10,11... | collective-permute-start | bytes 884744 | tf_op jit(solution)/shard_map/ppermute | solution.py:288
  72.5 5.9 %collective-permute-done.17.far_a = f32[64,8,128]{2,1,0:T(8,128)S(1)} collective-permute-done((f32[64,8,128]{2,1,0:T(8,128)S(1)}, f32[64,8,128]{2,1,0:T(8,128)S(1)}, u32[]{:S(2)}, u32[]{:S(2)}) %collective-permute-start.17) | collective-permute-done | bytes 262176 | tf_op jit(solution)/shard_map/ppermute | solution.py:288
  78.5 3.3 %shard_map.76 = (f32[128,2,8,128]{3,2,1,0:T(8,128)S(1)}, f32[128,2,8,128]{3,2,1,0:T(8,128)S(1)}, f32[17,8,128]{2,1,0:T(8,128)S(1)}, f32[64,2,8,128]{3,2,1,0:T(8,128)S(1)}, f32[8,128]{1,0:T(8,128)S(1)}) custom-call(s32[16,8]{1,0:T(8,128)S(1)} %get-tuple-element.75.place, s32[16,8]{1,0:T(8,128)S(1)} %get-tuple-element.76.away, ...), custom_call_target="tpu_custom_call" | custom-call | tf_op jit(solution)/shard_map/pallas_call | solution.py:25
  84.8 2.7 %collective-permute-start.23 = (f32[17,8,128]{2,1,0:T(8,128)S(1)}, f32[17,8,128]{2,1,0:T(8,128)S(1)}, u32[]{:S(2)}, u32[]{:S(2)}) collective-permute-start(f32[17,8,128]{2,1,0:T(8,128)S(1)} %pad_maximum_fusion.13), channel_id=1, source_target_pairs={{0,12},{1,13},{2,14},{3,15},{4,8},{5,9},{6,10},{7,11},{8,4},{9,5},... | collective-permute-start | bytes 208904 | tf_op jit(solution)/shard_map/ppermute | solution.py:288
  88.5 3.4 %collective-permute-done.22 = f32[17,8,128]{2,1,0:T(8,128)S(1)} collective-permute-done((f32[17,8,128]{2,1,0:T(8,128)S(1)}, f32[17,8,128]{2,1,0:T(8,128)S(1)}, u32[]{:S(2)}, u32[]{:S(2)}) %collective-permute-start.22) | collective-permute-done | bytes 69664 | tf_op jit(solution)/shard_map/ppermute | solution.py:288
  94.4 2.8 %collective-permute-done.26 = f32[36,8,128]{2,1,0:T(8,128)S(1)} collective-permute-done((f32[36,8,128]{2,1,0:T(8,128)S(1)}, f32[36,8,128]{2,1,0:T(8,128)S(1)}, u32[]{:S(2)}, u32[]{:S(2)}) %collective-permute-start.26) | collective-permute-done | bytes 147488 | tf_op jit(solution)/shard_map/ppermute | solution.py:288
  97.2 2.0 %collective-permute-start.27 = (f32[72,8,128]{2,1,0:T(8,128)S(1)}, f32[72,8,128]{2,1,0:T(8,128)S(1)}, u32[]{:S(2)}, u32[]{:S(2)}) collective-permute-start(f32[72,8,128]{2,1,0:T(8,128)S(1)} %constant_dynamic-update-slice_fusion.15.near_b), channel_id=1, source_target_pairs={{0,1},{1,0},{2,3},{3,2},{4,5},{5,4},{6,7},{7,6},{8,9},{9,8},{10,11... | collective-permute-start | bytes 884744 | tf_op jit(solution)/shard_map/ppermute | solution.py:288
  101.1 4.8 %collective-permute-done.25.far_a = f32[64,8,128]{2,1,0:T(8,128)S(1)} collective-permute-done((f32[64,8,128]{2,1,0:T(8,128)S(1)}, f32[64,8,128]{2,1,0:T(8,128)S(1)}, u32[]{:S(2)}, u32[]{:S(2)}) %collective-permute-start.25) | collective-permute-done | bytes 262176 | tf_op jit(solution)/shard_map/ppermute | solution.py:288
  105.9 3.4 %shard_map.78 = (f32[128,2,8,128]{3,2,1,0:T(8,128)S(1)}, f32[128,2,8,128]{3,2,1,0:T(8,128)S(1)}, f32[17,8,128]{2,1,0:T(8,128)S(1)}, f32[64,2,8,128]{3,2,1,0:T(8,128)S(1)}, f32[8,128]{1,0:T(8,128)S(1)}) custom-call(s32[16,8]{1,0:T(8,128)S(1)} %get-tuple-element.75.place, s32[16,8]{1,0:T(8,128)S(1)} %get-tuple-element.76.away, ...), custom_call_target="tpu_custom_call" | custom-call | tf_op jit(solution)/shard_map/pallas_call | solution.py:25
  113.4 1.7 %collective-permute-start.32 = (f32[17,8,128]{2,1,0:T(8,128)S(1)}, f32[17,8,128]{2,1,0:T(8,128)S(1)}, u32[]{:S(2)}, u32[]{:S(2)}) collective-permute-start(f32[17,8,128]{2,1,0:T(8,128)S(1)} %pad_maximum_fusion.14), channel_id=1, source_target_pairs={{0,12},{1,13},{2,14},{3,15},{4,8},{5,9},{6,10},{7,11},{8,4},{9,5},... | collective-permute-start | bytes 208904 | tf_op jit(solution)/shard_map/ppermute | solution.py:288
  115.1 5.4 %collective-permute-done.31 = f32[17,8,128]{2,1,0:T(8,128)S(1)} collective-permute-done((f32[17,8,128]{2,1,0:T(8,128)S(1)}, f32[17,8,128]{2,1,0:T(8,128)S(1)}, u32[]{:S(2)}, u32[]{:S(2)}) %collective-permute-start.31) | collective-permute-done | bytes 69664 | tf_op jit(solution)/shard_map/ppermute | solution.py:288
  122.8 2.9 %collective-permute-done.35 = f32[36,8,128]{2,1,0:T(8,128)S(1)} collective-permute-done((f32[36,8,128]{2,1,0:T(8,128)S(1)}, f32[36,8,128]{2,1,0:T(8,128)S(1)}, u32[]{:S(2)}, u32[]{:S(2)}) %collective-permute-start.35) | collective-permute-done | bytes 147488 | tf_op jit(solution)/shard_map/ppermute | solution.py:288
  127.0 1.9 %collective-permute-start.34 = (f32[64,8,128]{2,1,0:T(8,128)S(1)}, f32[64,8,128]{2,1,0:T(8,128)S(1)}, u32[]{:S(2)}, u32[]{:S(2)}) collective-permute-start(f32[64,8,128]{2,1,0:T(8,128)S(1)} %constant_dynamic-update-slice_fusion.20.near_a), channel_id=1, source_target_pairs={{0,2},{1,3},{2,0},{3,1},{4,6},{5,7},{6,4},{7,5},{8,10},{9,11},{10,... | collective-permute-start | bytes 786440 | tf_op jit(solution)/shard_map/ppermute | solution.py:288
  129.9 3.5 %collective-permute-done.34.far_a = f32[64,8,128]{2,1,0:T(8,128)S(1)} collective-permute-done((f32[64,8,128]{2,1,0:T(8,128)S(1)}, f32[64,8,128]{2,1,0:T(8,128)S(1)}, u32[]{:S(2)}, u32[]{:S(2)}) %collective-permute-start.34) | collective-permute-done | bytes 262176 | tf_op jit(solution)/shard_map/ppermute | solution.py:288
  133.4 3.4 %shard_map.80 = (f32[32,8,128]{2,1,0:T(8,128)S(1)}, f32[64,2,8,128]{3,2,1,0:T(8,128)S(1)}, f32[8,128]{1,0:T(8,128)S(1)}) custom-call(s32[16,8]{1,0:T(8,128)S(1)} %get-tuple-element.75.place, s32[16,8]{1,0:T(8,128)S(1)} %get-tuple-element.76.away, f32[16,8]{1,0:T(8,128)S(1)} %get-tuple-element.77.keep, s32[64]{0:T(128)S(1)} %get-tuple-element.78.picked, ...), custom_call_target="tpu_custom_call" | custom-call | tf_op jit(solution)/shard_map/pallas_call | solution.py:25
  137.0 12.5 %all_to_all.5.sums = f32[32,8,128]{2,1,0:T(8,128)S(1)} all-to-all(f32[32,8,128]{2,1,0:T(8,128)S(1)} %get-tuple-element.112), channel_id=1, replica_groups=mesh['body'=2,'sub'=16] {'body','sub'}, dimensions={0} | all-to-all | bytes 262144 | tf_op jit(solution)/shard_map/all_to_all | solution.py:418
  149.4 2.2 %shard_map.81 = f32[8,64,256]{2,1,0:T(8,128)} custom-call(f32[64]{0:T(128)S(1)} %get-tuple-element.197.keep, f32[32,8,128]{2,1,0:T(8,128)S(1)} %all_to_all.5.sums, f32[8,128]{1,0:T(8,128)S(1)} %get-tuple-element.113.known, f32[64,256]{1,0:T(8,128)S(1)} %copy-done, f32[64,2,8,128]{3,2,1,0:T(8,128)S(1)} %get-tuple-element.114.mine, ...), custom_call_target="tpu_custom_call" | custom-call | tf_op jit(solution)/shard_map/pallas_call | solution.py:25
  (133 shorter events, 35.1 us)
Async XLA Ops:
  6.2 9.2 %collective-permute-start.6 = (f32[32,8,128]{2,1,0:T(8,128)S(1)}, f32[32,8,128]{2,1,0:T(8,128)S(1)}, u32[]{:S(2)}, u32[]{:S(2)}) collective-permute-start(f32[32,8,128]{2,1,0:T(8,128)S(1)} %get-tuple-element.72), channel_id=1, source_target_pairs={{0,1},{1,0},{2,3},{3,2},{4,5},{5,4},{6,7},{7,6},{8,9},{9,8},{10,11... | collective-permute-start | bytes 393224 | tf_op jit(solution)/shard_map/ppermute | solution.py:288
  9.2 7.8 %collective-permute-start.7 = (f32[32,8,128]{2,1,0:T(8,128)S(1)}, f32[32,8,128]{2,1,0:T(8,128)S(1)}, u32[]{:S(2)}, u32[]{:S(2)}) collective-permute-start(f32[32,8,128]{2,1,0:T(8,128)S(1)} %get-tuple-element.73), channel_id=1, source_target_pairs={{0,2},{1,3},{2,0},{3,1},{4,6},{5,7},{6,4},{7,5},{8,10},{9,11},{10,... | collective-permute-start | bytes 393224 | tf_op jit(solution)/shard_map/ppermute | solution.py:288
  10.8 6.3 %collective-permute-start.8 = (f32[32,8,128]{2,1,0:T(8,128)S(1)}, f32[32,8,128]{2,1,0:T(8,128)S(1)}, u32[]{:S(2)}, u32[]{:S(2)}) collective-permute-start(f32[32,8,128]{2,1,0:T(8,128)S(1)} %get-tuple-element.74), channel_id=1, source_target_pairs={{0,3},{1,2},{2,1},{3,0},{4,7},{5,6},{6,5},{7,4},{8,11},{9,10},{10,... | collective-permute-start | bytes 393224 | tf_op jit(solution)/shard_map/ppermute | solution.py:288
  10.8 10.4 %collective-permute-start = (f32[44,8,128]{2,1,0:T(8,128)S(1)}, f32[44,8,128]{2,1,0:T(8,128)S(1)}, u32[]{:S(2)}, u32[]{:S(2)}) collective-permute-start(f32[44,8,128]{2,1,0:T(8,128)S(1)} %get-tuple-element.64), channel_id=1, source_target_pairs={{0,4},{1,5},{2,6},{3,7},{4,0},{5,1},{6,2},{7,3},{8,12},{9,13},{10,... | collective-permute-start | bytes 540680 | tf_op jit(solution)/shard_map/ppermute | solution.py:288
  12.8 21.4 %collective-permute-start.1 = (f32[44,8,128]{2,1,0:T(8,128)S(1)}, f32[44,8,128]{2,1,0:T(8,128)S(1)}, u32[]{:S(2)}, u32[]{:S(2)}) collective-permute-start(f32[44,8,128]{2,1,0:T(8,128)S(1)} %get-tuple-element.65), channel_id=1, source_target_pairs={{0,8},{1,9},{2,10},{3,11},{4,12},{5,13},{6,14},{7,15},{8,0},{9,1},... | collective-permute-start | bytes 540680 | tf_op jit(solution)/shard_map/ppermute | solution.py:288
  15.4 18.8 %collective-permute-start.2 = (f32[44,8,128]{2,1,0:T(8,128)S(1)}, f32[44,8,128]{2,1,0:T(8,128)S(1)}, u32[]{:S(2)}, u32[]{:S(2)}) collective-permute-start(f32[44,8,128]{2,1,0:T(8,128)S(1)} %get-tuple-element.66), channel_id=1, source_target_pairs={{0,12},{1,13},{2,14},{3,15},{4,8},{5,9},{6,10},{7,11},{8,4},{9,5},... | collective-permute-start | bytes 540680 | tf_op jit(solution)/shard_map/ppermute | solution.py:288
  17.1 31.6 %collective-permute-start.10 = (f32[32,8,128]{2,1,0:T(8,128)S(1)}, f32[32,8,128]{2,1,0:T(8,128)S(1)}, u32[]{:S(2)}, u32[]{:S(2)}) collective-permute-start(f32[32,8,128]{2,1,0:T(8,128)S(1)} %pad_maximum_fusion.7), channel_id=1, source_target_pairs={{0,8},{1,9},{2,10},{3,11},{4,12},{5,13},{6,14},{7,15},{8,0},{9,1},... | collective-permute-start | bytes 393224 | tf_op jit(solution)/shard_map/ppermute | solution.py:288
  19.7 29.0 %collective-permute-start.11 = (f32[32,8,128]{2,1,0:T(8,128)S(1)}, f32[32,8,128]{2,1,0:T(8,128)S(1)}, u32[]{:S(2)}, u32[]{:S(2)}) collective-permute-start(f32[32,8,128]{2,1,0:T(8,128)S(1)} %pad_maximum_fusion.8), channel_id=1, source_target_pairs={{0,12},{1,13},{2,14},{3,15},{4,8},{5,9},{6,10},{7,11},{8,4},{9,5},... | collective-permute-start | bytes 393224 | tf_op jit(solution)/shard_map/ppermute | solution.py:288
  34.3 6.5 %collective-permute-start.5 = (f32[44,8,128]{2,1,0:T(8,128)S(1)}, f32[44,8,128]{2,1,0:T(8,128)S(1)}, u32[]{:S(2)}, u32[]{:S(2)}) collective-permute-start(f32[44,8,128]{2,1,0:T(8,128)S(1)} %pad_maximum_fusion.2), channel_id=1, source_target_pairs={{0,3},{1,2},{2,1},{3,0},{4,7},{5,6},{6,5},{7,4},{8,11},{9,10},{10,... | collective-permute-start | bytes 540680 | tf_op jit(solution)/shard_map/ppermute | solution.py:288
  36.8 11.8 %collective-permute-start.4 = (f32[44,8,128]{2,1,0:T(8,128)S(1)}, f32[44,8,128]{2,1,0:T(8,128)S(1)}, u32[]{:S(2)}, u32[]{:S(2)}) collective-permute-start(f32[44,8,128]{2,1,0:T(8,128)S(1)} %pad_maximum_fusion.1), channel_id=1, source_target_pairs={{0,2},{1,3},{2,0},{3,1},{4,6},{5,7},{6,4},{7,5},{8,10},{9,11},{10,... | collective-permute-start | bytes 540680 | tf_op jit(solution)/shard_map/ppermute | solution.py:288
  37.4 11.3 %collective-permute-start.3 = (f32[44,8,128]{2,1,0:T(8,128)S(1)}, f32[44,8,128]{2,1,0:T(8,128)S(1)}, u32[]{:S(2)}, u32[]{:S(2)}) collective-permute-start(f32[44,8,128]{2,1,0:T(8,128)S(1)} %pad_maximum_fusion), channel_id=1, source_target_pairs={{0,1},{1,0},{2,3},{3,2},{4,5},{5,4},{6,7},{7,6},{8,9},{9,8},{10,11... | collective-permute-start | bytes 540680 | tf_op jit(solution)/shard_map/ppermute | solution.py:288
  40.8 7.9 %collective-permute-start.9 = (f32[32,8,128]{2,1,0:T(8,128)S(1)}, f32[32,8,128]{2,1,0:T(8,128)S(1)}, u32[]{:S(2)}, u32[]{:S(2)}) collective-permute-start(f32[32,8,128]{2,1,0:T(8,128)S(1)} %pad_maximum_fusion.6), channel_id=1, source_target_pairs={{0,4},{1,5},{2,6},{3,7},{4,0},{5,1},{6,2},{7,3},{8,12},{9,13},{10,... | collective-permute-start | bytes 393224 | tf_op jit(solution)/shard_map/ppermute | solution.py:288
  55.3 8.6 %collective-permute-start.14 = (f32[17,8,128]{2,1,0:T(8,128)S(1)}, f32[17,8,128]{2,1,0:T(8,128)S(1)}, u32[]{:S(2)}, u32[]{:S(2)}) collective-permute-start(f32[17,8,128]{2,1,0:T(8,128)S(1)} %pad_maximum_fusion.12), channel_id=1, source_target_pairs={{0,8},{1,9},{2,10},{3,11},{4,12},{5,13},{6,14},{7,15},{8,0},{9,1},... | collective-permute-start | bytes 208904 | tf_op jit(solution)/shard_map/ppermute | solution.py:288
  57.0 6.9 %collective-permute-start.15 = (f32[17,8,128]{2,1,0:T(8,128)S(1)}, f32[17,8,128]{2,1,0:T(8,128)S(1)}, u32[]{:S(2)}, u32[]{:S(2)}) collective-permute-start(f32[17,8,128]{2,1,0:T(8,128)S(1)} %pad_maximum_fusion.12), channel_id=1, source_target_pairs={{0,12},{1,13},{2,14},{3,15},{4,8},{5,9},{6,10},{7,11},{8,4},{9,5},... | collective-permute-start | bytes 208904 | tf_op jit(solution)/shard_map/ppermute | solution.py:288
  63.9 5.2 %collective-permute-start.18 = (f32[36,8,128]{2,1,0:T(8,128)S(1)}, f32[36,8,128]{2,1,0:T(8,128)S(1)}, u32[]{:S(2)}, u32[]{:S(2)}) collective-permute-start(f32[36,8,128]{2,1,0:T(8,128)S(1)} %pad_maximum_fusion.3), channel_id=1, source_target_pairs={{0,2},{1,3},{2,0},{3,1},{4,6},{5,7},{6,4},{7,5},{8,10},{9,11},{10,... | collective-permute-start | bytes 442376 | tf_op jit(solution)/shard_map/ppermute | solution.py:288
  65.6 6.4 %collective-permute-start.16 = (f32[32,8,128]{2,1,0:T(8,128)S(1)}, f32[32,8,128]{2,1,0:T(8,128)S(1)}, u32[]{:S(2)}, u32[]{:S(2)}) collective-permute-start(f32[32,8,128]{2,1,0:T(8,128)S(1)} %pad_maximum_fusion.9), channel_id=1, source_target_pairs={{0,1},{1,0},{2,3},{3,2},{4,5},{5,4},{6,7},{7,6},{8,9},{9,8},{10,11... | collective-permute-start | bytes 393224 | tf_op jit(solution)/shard_map/ppermute | solution.py:288
  69.2 9.3 %collective-permute-start.19 = (f32[72,8,128]{2,1,0:T(8,128)S(1)}, f32[72,8,128]{2,1,0:T(8,128)S(1)}, u32[]{:S(2)}, u32[]{:S(2)}) collective-permute-start(f32[72,8,128]{2,1,0:T(8,128)S(1)} %constant_dynamic-update-slice_fusion.5.near_b), channel_id=1, source_target_pairs={{0,1},{1,0},{2,3},{3,2},{4,5},{5,4},{6,7},{7,6},{8,9},{9,8},{10,11... | collective-permute-start | bytes 884744 | tf_op jit(solution)/shard_map/ppermute | solution.py:288
  72.0 6.4 %collective-permute-start.17 = (f32[64,8,128]{2,1,0:T(8,128)S(1)}, f32[64,8,128]{2,1,0:T(8,128)S(1)}, u32[]{:S(2)}, u32[]{:S(2)}) collective-permute-start(f32[64,8,128]{2,1,0:T(8,128)S(1)} %constant_dynamic-update-slice_fusion.near_a), channel_id=1, source_target_pairs={{0,2},{1,3},{2,0},{3,1},{4,6},{5,7},{6,4},{7,5},{8,10},{9,11},{10,... | collective-permute-start | bytes 786440 | tf_op jit(solution)/shard_map/ppermute | solution.py:288
  83.0 5.5 %collective-permute-start.21 = (f32[17,8,128]{2,1,0:T(8,128)S(1)}, f32[17,8,128]{2,1,0:T(8,128)S(1)}, u32[]{:S(2)}, u32[]{:S(2)}) collective-permute-start(f32[17,8,128]{2,1,0:T(8,128)S(1)} %pad_maximum_fusion.13), channel_id=1, source_target_pairs={{0,4},{1,5},{2,6},{3,7},{4,0},{5,1},{6,2},{7,3},{8,12},{9,13},{10,... | collective-permute-start | bytes 208904 | tf_op jit(solution)/shard_map/ppermute | solution.py:288
  83.4 8.6 %collective-permute-start.22 = (f32[17,8,128]{2,1,0:T(8,128)S(1)}, f32[17,8,128]{2,1,0:T(8,128)S(1)}, u32[]{:S(2)}, u32[]{:S(2)}) collective-permute-start(f32[17,8,128]{2,1,0:T(8,128)S(1)} %pad_maximum_fusion.13), channel_id=1, source_target_pairs={{0,8},{1,9},{2,10},{3,11},{4,12},{5,13},{6,14},{7,15},{8,0},{9,1},... | collective-permute-start | bytes 208904 | tf_op jit(solution)/shard_map/ppermute | solution.py:288
  84.8 7.2 %collective-permute-start.23 = (f32[17,8,128]{2,1,0:T(8,128)S(1)}, f32[17,8,128]{2,1,0:T(8,128)S(1)}, u32[]{:S(2)}, u32[]{:S(2)}) collective-permute-start(f32[17,8,128]{2,1,0:T(8,128)S(1)} %pad_maximum_fusion.13), channel_id=1, source_target_pairs={{0,12},{1,13},{2,14},{3,15},{4,8},{5,9},{6,10},{7,11},{8,4},{9,5},... | collective-permute-start | bytes 208904 | tf_op jit(solution)/shard_map/ppermute | solution.py:288
  87.5 12.7 %collective-permute-start.28 = (f32[64,2,8,128]{3,2,1,0:T(8,128)S(1)}, f32[64,2,8,128]{3,2,1,0:T(8,128)S(1)}, u32[]{:S(2)}, u32[]{:S(2)}) collective-permute-start(f32[64,2,8,128]{3,2,1,0:T(8,128)S(1)} %get-tuple-element.86.mine), channel_id=1, source_target_pairs={{0,16},{16,0},{1,17},{17,1},{2,18},{18,2},{3,19},{19,3},{4,20},{20... | collective-permute-start | bytes 1572872 | tf_op jit(solution)/shard_map/ppermute | solution.py:291
  93.6 5.9 %collective-permute-start.24 = (f32[32,8,128]{2,1,0:T(8,128)S(1)}, f32[32,8,128]{2,1,0:T(8,128)S(1)}, u32[]{:S(2)}, u32[]{:S(2)}) collective-permute-start(f32[32,8,128]{2,1,0:T(8,128)S(1)} %pad_maximum_fusion.10), channel_id=1, source_target_pairs={{0,1},{1,0},{2,3},{3,2},{4,5},{5,4},{6,7},{7,6},{8,9},{9,8},{10,11... | collective-permute-start | bytes 393224 | tf_op jit(solution)/shard_map/ppermute | solution.py:288
  97.2 8.6 %collective-permute-start.27 = (f32[72,8,128]{2,1,0:T(8,128)S(1)}, f32[72,8,128]{2,1,0:T(8,128)S(1)}, u32[]{:S(2)}, u32[]{:S(2)}) collective-permute-start(f32[72,8,128]{2,1,0:T(8,128)S(1)} %constant_dynamic-update-slice_fusion.15.near_b), channel_id=1, source_target_pairs={{0,1},{1,0},{2,3},{3,2},{4,5},{5,4},{6,7},{7,6},{8,9},{9,8},{10,11... | collective-permute-start | bytes 884744 | tf_op jit(solution)/shard_map/ppermute | solution.py:288
  99.4 6.4 %collective-permute-start.25 = (f32[64,8,128]{2,1,0:T(8,128)S(1)}, f32[64,8,128]{2,1,0:T(8,128)S(1)}, u32[]{:S(2)}, u32[]{:S(2)}) collective-permute-start(f32[64,8,128]{2,1,0:T(8,128)S(1)} %constant_dynamic-update-slice_fusion.10.near_a), channel_id=1, source_target_pairs={{0,2},{1,3},{2,0},{3,1},{4,6},{5,7},{6,4},{7,5},{8,10},{9,11},{10,... | collective-permute-start | bytes 786440 | tf_op jit(solution)/shard_map/ppermute | solution.py:288
  111.9 8.6 %collective-permute-start.31 = (f32[17,8,128]{2,1,0:T(8,128)S(1)}, f32[17,8,128]{2,1,0:T(8,128)S(1)}, u32[]{:S(2)}, u32[]{:S(2)}) collective-permute-start(f32[17,8,128]{2,1,0:T(8,128)S(1)} %pad_maximum_fusion.14), channel_id=1, source_target_pairs={{0,8},{1,9},{2,10},{3,11},{4,12},{5,13},{6,14},{7,15},{8,0},{9,1},... | collective-permute-start | bytes 208904 | tf_op jit(solution)/shard_map/ppermute | solution.py:288
  113.4 7.1 %collective-permute-start.32 = (f32[17,8,128]{2,1,0:T(8,128)S(1)}, f32[17,8,128]{2,1,0:T(8,128)S(1)}, u32[]{:S(2)}, u32[]{:S(2)}) collective-permute-start(f32[17,8,128]{2,1,0:T(8,128)S(1)} %pad_maximum_fusion.14), channel_id=1, source_target_pairs={{0,12},{1,13},{2,14},{3,15},{4,8},{5,9},{6,10},{7,11},{8,4},{9,5},... | collective-permute-start | bytes 208904 | tf_op jit(solution)/shard_map/ppermute | solution.py:288
  115.1 13.9 %collective-permute-start.37 = (f32[64,2,8,128]{3,2,1,0:T(8,128)S(1)}, f32[64,2,8,128]{3,2,1,0:T(8,128)S(1)}, u32[]{:S(2)}, u32[]{:S(2)}) collective-permute-start(f32[64,2,8,128]{3,2,1,0:T(8,128)S(1)} %get-tuple-element.99.mine), channel_id=1, source_target_pairs={{0,16},{16,0},{1,17},{17,1},{2,18},{18,2},{3,19},{19,3},{4,20},{20... | collective-permute-start | bytes 1572872 | tf_op jit(solution)/shard_map/ppermute | solution.py:291
  121.4 5.6 %collective-permute-start.33 = (f32[32,8,128]{2,1,0:T(8,128)S(1)}, f32[32,8,128]{2,1,0:T(8,128)S(1)}, u32[]{:S(2)}, u32[]{:S(2)}) collective-permute-start(f32[32,8,128]{2,1,0:T(8,128)S(1)} %pad_maximum_fusion.11), channel_id=1, source_target_pairs={{0,1},{1,0},{2,3},{3,2},{4,5},{5,4},{6,7},{7,6},{8,9},{9,8},{10,11... | collective-permute-start | bytes 393224 | tf_op jit(solution)/shard_map/ppermute | solution.py:288
  125.7 7.7 %collective-permute-start.36 = (f32[72,8,128]{2,1,0:T(8,128)S(1)}, f32[72,8,128]{2,1,0:T(8,128)S(1)}, u32[]{:S(2)}, u32[]{:S(2)}) collective-permute-start(f32[72,8,128]{2,1,0:T(8,128)S(1)} %constant_dynamic-update-slice_fusion.25.near_b), channel_id=1, source_target_pairs={{0,1},{1,0},{2,3},{3,2},{4,5},{5,4},{6,7},{7,6},{8,9},{9,8},{10,11... | collective-permute-start | bytes 884744 | tf_op jit(solution)/shard_map/ppermute | solution.py:288
  127.0 6.4 %collective-permute-start.34 = (f32[64,8,128]{2,1,0:T(8,128)S(1)}, f32[64,8,128]{2,1,0:T(8,128)S(1)}, u32[]{:S(2)}, u32[]{:S(2)}) collective-permute-start(f32[64,8,128]{2,1,0:T(8,128)S(1)} %constant_dynamic-update-slice_fusion.20.near_a), channel_id=1, source_target_pairs={{0,2},{1,3},{2,0},{3,1},{4,6},{5,7},{6,4},{7,5},{8,10},{9,11},{10,... | collective-permute-start | bytes 786440 | tf_op jit(solution)/shard_map/ppermute | solution.py:288
  136.9 12.5 %collective-permute-start.38 = (f32[64,2,8,128]{3,2,1,0:T(8,128)S(1)}, f32[64,2,8,128]{3,2,1,0:T(8,128)S(1)}, u32[]{:S(2)}, u32[]{:S(2)}) collective-permute-start(f32[64,2,8,128]{3,2,1,0:T(8,128)S(1)} %get-tuple-element.114.mine), channel_id=1, source_target_pairs={{0,16},{16,0},{1,17},{17,1},{2,18},{18,2},{3,19},{19,3},{4,20},{20... | collective-permute-start | bytes 1572872 | tf_op jit(solution)/shard_map/ppermute | solution.py:291
  (8 other events, 71.0 us)

commit v11 on v10

--- a/solution.py
+++ b/solution.py
@@ -66,11 +66,11 @@
         answer[ntile] = sums
 
 
-def pack_kernel(nh, cut, room, place, field, table, *refs):
+def pack_kernel(nh, nz, by_z, place, field, *refs):
+    if not by_z:
+        table, *refs = refs
     *outs, whole = refs
-    nz = len(outs) - 4
-    extra = table.shape[1]
-    tiles = room * nh
+    tiles = whole.shape[0] // (4 * nz + 1)
     whole[...] = jnp.zeros_like(whole)
 
     def body(p, carry):
@@ -78,14 +78,13 @@
         return carry
 
     lax.fori_loop(0, field.shape[0], body, 0, unroll=4)
-    first, second = cut * nh, tiles - cut * nh
-    for z in range(nz):
-        for m in range(4):
-            at = (z * 4 + m) * tiles
-            one, two = m * (first + extra), z * second
-            outs[z][one : one + first] = whole[at : at + first]
-            outs[z][one + first : one + first + extra] = table[z * 4 + m]
-            outs[nz + m][two : two + second] = whole[at + first : at + tiles]
+    for i, out in enumerate(outs):
+        size = out.shape[0] // (4 * nz // len(outs))
+        for k in range(out.shape[0] // size):
+            owner = i * 4 + k if by_z else k * 4 + i
+            out[k * size : k * size + tiles] = whole[owner * tiles : (owner + 1) * tiles]
+            if not by_z:
+                out[k * size + tiles : (k + 1) * size] = table[owner]
 
 
 def block_kernel(block, held, sems):
@@ -106,40 +105,41 @@
     b_near, refs = refs[:4], refs[4:]
     b_far, refs = refs[: nz - 1], refs[nz - 1 :]
     near, far, on, r_out, comp, answer, load, facts, sems = refs
-    copies = []
+    first, second = cut * nh, (room - cut) * nh
+    blocks = []
     for z in range(nz):
         for m in range(4):
-            part, at = (a_z[z], 0) if m == 0 else (a_far[m - 1], z * (cut * nh + extra))
-            rows = pl.ds(at + cut * nh + lines, extra - lines)
-            copies.append(pltpu.make_async_copy(part.at[rows], facts.at[z * 4 + m], sems.at[z * 4 + m]))
-            copies[-1].start()
+            one = (a_z[z], 0) if m == 0 else (a_far[m - 1], z * first)
+            two = (b_near[m], 0) if z == 0 else (b_far[z - 1], m * (second + extra))
+            blocks.append((*one, *two))
+    copies = []
+    for i, (_, _, two, at_two) in enumerate(blocks):
+        rows = pl.ds(at_two + second + lines, extra - lines)
+        copies.append(pltpu.make_async_copy(two.at[rows], facts.at[i], sems.at[i]))
+        copies[-1].start()
     load[...] = jnp.zeros_like(load)
     gamma = energy = jnp.zeros(r_out.shape[2:], jnp.float32)
-    first, second = cut * nh, (room - cut) * nh
-    for z in range(nz):
-        for m in range(4):
-            i = z * 4 + m
-            one, at_one = (a_z[z], 0) if m == 0 else (a_far[m - 1], z * (first + extra))
-            two, at_two = (b_near[m], 0) if z == 0 else (b_far[z - 1], m * second)
-            comp[i * lines : (i + 1) * lines] = one[at_one + first : at_one + first + lines]
-            copies[i].wait()
-            for j in range(room):
-                row = i * room + j
-                slot = facts[i, j // SUBLANES, j % SUBLANES, 0].astype(jnp.int32)
-                near[i, j] = slot
-                far[i, j] = facts[i, j // SUBLANES, j % SUBLANES, 1].astype(jnp.int32)
-                on[i, j] = facts[i, j // SUBLANES, j % SUBLANES, 2]
-                if j < cut:
-                    r = one[at_one + j * nh : at_one + (j + 1) * nh]
-                else:
-                    r = two[at_two + (j - cut) * nh : at_two + (j - cut + 1) * nh]
-                r_out[row] = r
-                load[pl.ds(slot, nh)] += r
-                for h in range(nh):
-                    line, sub = divmod(j * nh + h, SUBLANES)
-                    square = r[h] * r[h]
-                    gamma = gamma + square
-                    energy = energy + one[at_one + first + line, sub : sub + 1, :] * square
+    for i, (one, at_one, two, at_two) in enumerate(blocks):
+        at_comp = at_two + second
+        comp[i * lines : (i + 1) * lines] = two[at_comp : at_comp + lines]
+        copies[i].wait()
+        for j in range(room):
+            row = i * room + j
+            slot = facts[i, j // SUBLANES, j % SUBLANES, 0].astype(jnp.int32)
+            near[row] = slot
+            far[row] = facts[i, j // SUBLANES, j % SUBLANES, 1].astype(jnp.int32)
+            on[row] = facts[i, j // SUBLANES, j % SUBLANES, 2]
+            if j < cut:
+                r = one[at_one + j * nh : at_one + (j + 1) * nh]
+            else:
+                r = two[at_two + (j - cut) * nh : at_two + (j - cut + 1) * nh]
+            r_out[row] = r
+            load[pl.ds(slot, nh)] += r
+            for h in range(nh):
+                line, sub = divmod(j * nh + h, SUBLANES)
+                square = r[h] * r[h]
+                gamma = gamma + square
+                energy = energy + two[at_comp + line, sub : sub + 1, :] * square
     respond(block, load, gamma, energy, answer)
 
 
@@ -189,7 +189,7 @@
         gamma, energy = sums
         for j in range(room):
             row = i * room + j
-            near, far, on = place[i, j], away[i, j], keep[i, j]
+            near, far, on = place[row], away[row], keep[row]
             for h in range(nh):
                 line, sub = divmod(j * nh + h, SUBLANES)
                 c = comp[i * lines + line, sub : sub + 1, :]
@@ -279,8 +279,8 @@
     deep = -(-room // SUBLANES)
     extra = lines + deep
     cut = room // 2
-    first = cut * nh + extra
-    second = (room - cut) * nh
+    first = cut * nh
+    second = (room - cut) * nh + extra
     nz = nsub // 4
     half = nslot // 2 * nh
 
@@ -297,7 +297,9 @@
     index = jnp.arange(npatch, dtype=jnp.int32)
     earlier = (owner[None, :] == owner[:, None]) & (index[None, :] < index[:, None])
     rank = jnp.sum(earlier.astype(jnp.int32), axis=1)
-    place = (owner ^ me) * room * nh + rank * nh
+    base, none = owner ^ me, 4 * nz
+    place_a = jnp.where(rank < cut, base * cut + rank, none * cut) * nh
+    place_b = jnp.where(rank < cut, none * (room - cut), base * (room - cut) + rank - cut) * nh
 
     def found(away):
         x_bit, y_bit, z_part = away & 1, (away >> 1) & 1, away >> 2
@@ -318,19 +320,36 @@
     start = (keep[None, :, None] * rhs).reshape(ncase, npatch, nh, LANES)
     start = jnp.transpose(start, (1, 2, 0, 3))
     picked = found(me ^ other).astype(jnp.int32)
-    place, picked = lax.optimization_barrier((place, picked))
-
-    packed = call(
-        functools.partial(pack_kernel, nh, cut, room),
-        (f32(4 * first, ncase, LANES),) * nz + (f32(nz * second, ncase, LANES),) * 4,
+    place_a, place_b, picked = lax.optimization_barrier((place_a, place_b, picked))
+
+    a_z = call(
+        functools.partial(pack_kernel, nh, nz, True),
+        (f32(4 * first, ncase, LANES),) * nz,
+        [SMEM, VMEM],
+        place_a,
+        start,
+        scratch=[pltpu.VMEM(((nsub + 1) * cut * nh, ncase, LANES), jnp.float32)],
+    )
+    b_near = call(
+        functools.partial(pack_kernel, nh, nz, False),
+        (f32(nz * second, ncase, LANES),) * 4,
         [SMEM, VMEM, VMEM],
-        place,
+        place_b,
         start,
         table,
-        scratch=[pltpu.VMEM((nrow * nh, ncase, LANES), jnp.float32)],
-    )
-    a_z = [packed[0]] + [swap(packed[z], 4 * z) for z in range(1, nz)]
-    b_near = [packed[nz]] + [swap(packed[nz + m], m) for m in range(1, 4)]
+        scratch=[pltpu.VMEM(((nsub + 1) * (room - cut) * nh, ncase, LANES), jnp.float32)],
+    )
+    a_z = [a_z[0]] + [swap(a_z[z], 4 * z) for z in range(1, nz)]
+    b_near = [b_near[0]] + [swap(b_near[m], m) for m in range(1, 4)]
+    block = call(
+        block_kernel,
+        jax.ShapeDtypeStruct(block.shape, block.dtype),
+        [HBM],
+        pltpu.with_memory_space_constraint(block, pltpu.HBM),
+        scratch=[pltpu.SemaphoreType.DMA((nslot,))],
+        cost=pl.CostEstimate(flops=0, bytes_accessed=4 * block.size, transcendentals=0),
+    )
+    a_z, b_near, block = lax.optimization_barrier((a_z, b_near, block))
     b_far = [
         swap(jnp.concatenate([part[z * second : (z + 1) * second] for part in b_near]), 4 * z)
         for z in range(1, nz)
@@ -338,23 +357,14 @@
     a_far = [
         swap(jnp.concatenate([part[m * first : (m + 1) * first] for part in a_z]), m) for m in range(1, 4)
     ]
-    held = call(
-        block_kernel,
-        jax.ShapeDtypeStruct(block.shape, block.dtype),
-        [HBM],
-        pltpu.with_memory_space_constraint(block, pltpu.HBM),
-        scratch=[pltpu.SemaphoreType.DMA((nslot,))],
-        cost=pl.CostEstimate(flops=0, bytes_accessed=4 * block.size, transcendentals=0),
-    )
-    a_far, block = lax.optimization_barrier((a_far, held))
     field = f32(nrow, nh, ncase, LANES)
     answer = f32(per, ncase, LANES)
     load = pltpu.VMEM((nslot * nh, ncase, LANES), jnp.float32)
     spread = pltpu.VMEM((nsub * per, ncase, LANES), jnp.float32)
     near, far, on, home_r, comp, own = pl.pallas_call(
         functools.partial(start_kernel, nh, cut, room, lines, extra, nz),
-        out_shape=(jax.ShapeDtypeStruct((nsub, room), jnp.int32),) * 2
-        + (f32(nsub, room), field, f32(nsub * lines, ncase, LANES), answer),
+        out_shape=(jax.ShapeDtypeStruct((nrow,), jnp.int32),) * 2
+        + (f32(nrow), field, f32(nsub * lines, ncase, LANES), answer),
         in_specs=[VMEM] * (2 * nz + 7),
         out_specs=(SMEM,) * 3 + (VMEM,) * 3,
         scratch_shapes=[

time: 152 us -> 144 us (0.947)
  starting transfers between devices: 52 us -> 47.3 us
  waiting for transfers between devices: 58.6 us -> 56.8 us
    ppermute x33, starting transfers between devices: 51.8 us -> 47.1 us  [swap(): return lax.ppermute(value, 'sub', [(i, i ^ far) for i in range(nsub)])]
    ppermute x33, waiting for transfers between devices: 54.8 us -> 53 us  [swap(): return lax.ppermute(value, 'sub', [(i, i ^ far) for i in range(nsub)])]
    pallas_call x8 -> x9, Pallas kernels: 18.4 us -> 18.3 us  [call(): pl.pallas_call(kernel, out_shape=tuple(out_shape) if several else out_sha...]
  transfers between devices with their start and end apart: 39 -> 39, of which waited for: 18 -> 23; matrix products, arithmetic and copies ran while one was open for 0% -> 1% of each run, Pallas kernels for 4% -> 4%
where the time goes in v11:
time: 144 us
  waiting for transfers between devices  56.8 us (39%)
  starting transfers between devices  47.3 us (33%)
  Pallas kernels  21.7 us (15%)
  blocking collectives  11.7 us (8%)
  other arithmetic  3.76 us (3%)
    ppermute x33, waiting for transfers between devices, swap(): return lax.ppermute(value, 'sub', [(i, i ^ far) for i in range(nsub)])  53 us
    ppermute x33, starting transfers between devices, swap(): return lax.ppermute(value, 'sub', [(i, i ^ far) for i in range(nsub)])  47.1 us
    pallas_call x9, Pallas kernels, call(): pl.pallas_call(kernel, out_shape=tuple(out_shape) if several else out_sha...  18.3 us
    all_to_all x1, blocking collectives, on_device(): lax.all_to_all(own, ('body', 'sub'), split_axis=0, concat_axis=0, tiled=T...  11.7 us
    ppermute x6, waiting for transfers between devices, sibling(): lax.ppermute(value, 'body', [(i, nbody - 1 - i) for i in range(nbody)])  3.77 us
    pallas_call x1, Pallas kernels, on_device(): pl.pallas_call(functools.partial(start_kernel, nh, cut, room, lines, extr...  3.46 us
  transfers between devices with their start and end apart: 39, of which 23 were waited for; matrix products, arithmetic and copies ran while one was open for 1% of the time, Pallas kernels for 4%

profile of v11, /device:TPU:0, one launch (start us, length us, event | category | flops | bytes accessed | tf_op | source)
XLA Modules:
  0.0 143.8 jit_solution(15608660542613986140)
XLA Ops:
  4.9 3.1 %collective-permute-start = (f32[32,8,128]{2,1,0:T(8,128)S(1)}, f32[32,8,128]{2,1,0:T(8,128)S(1)}, u32[]{:S(2)}, u32[]{:S(2)}) collective-permute-start(f32[32,8,128]{2,1,0:T(8,128)S(1)} %get-tuple-element.70), channel_id=1, source_target_pairs={{0,4},{1,5},{2,6},{3,7},{4,0},{5,1},{6,2},{7,3},{8,12},{9,13},{10,... | collective-permute-start | bytes 393224 | tf_op jit(solution)/shard_map/ppermute | solution.py:288
  13.5 2.6 %collective-permute-start.1 = (f32[32,8,128]{2,1,0:T(8,128)S(1)}, f32[32,8,128]{2,1,0:T(8,128)S(1)}, u32[]{:S(2)}, u32[]{:S(2)}) collective-permute-start(f32[32,8,128]{2,1,0:T(8,128)S(1)} %get-tuple-element.71), channel_id=1, source_target_pairs={{0,8},{1,9},{2,10},{3,11},{4,12},{5,13},{6,14},{7,15},{8,0},{9,1},... | collective-permute-start | bytes 393224 | tf_op jit(solution)/shard_map/ppermute | solution.py:288
  16.1 3.5 %shard_map.75.block = bf16[2048,2048]{1,0:T(8,128)(2,1)S(1)} custom-call(bf16[2048,2048]{1,0:T(8,128)(2,1)} %bitcast.62), custom_call_target="tpu_custom_call" | custom-call | bytes 16777216 | tf_op jit(solution)/shard_map/pallas_call | solution.py:25
  19.6 5.1 %collective-permute-done.1.refs_2_ = f32[32,8,128]{2,1,0:T(8,128)S(1)} collective-permute-done((f32[32,8,128]{2,1,0:T(8,128)S(1)}, f32[32,8,128]{2,1,0:T(8,128)S(1)}, u32[]{:S(2)}, u32[]{:S(2)}) %collective-permute-start.1) | collective-permute-done | bytes 131104 | tf_op jit(solution)/shard_map/ppermute | solution.py:288
  24.9 3.1 %collective-permute-start.11 = (f32[44,8,128]{2,1,0:T(8,128)S(1)}, f32[44,8,128]{2,1,0:T(8,128)S(1)}, u32[]{:S(2)}, u32[]{:S(2)}) collective-permute-start(f32[44,8,128]{2,1,0:T(8,128)S(1)} %pad_maximum_fusion.2), channel_id=1, source_target_pairs={{0,12},{1,13},{2,14},{3,15},{4,8},{5,9},{6,10},{7,11},{8,4},{9,5},... | collective-permute-start | bytes 540680 | tf_op jit(solution)/shard_map/ppermute | solution.py:288
  29.6 2.8 %collective-permute-start.8 = (f32[32,8,128]{2,1,0:T(8,128)S(1)}, f32[32,8,128]{2,1,0:T(8,128)S(1)}, u32[]{:S(2)}, u32[]{:S(2)}) collective-permute-start(f32[32,8,128]{2,1,0:T(8,128)S(1)} %pad_maximum_fusion.8), channel_id=1, source_target_pairs={{0,3},{1,2},{2,1},{3,0},{4,7},{5,6},{6,5},{7,4},{8,11},{9,10},{10,... | collective-permute-start | bytes 393224 | tf_op jit(solution)/shard_map/ppermute | solution.py:288
  33.0 2.6 %collective-permute-done.8.refs_6_ = f32[32,8,128]{2,1,0:T(8,128)S(1)} collective-permute-done((f32[32,8,128]{2,1,0:T(8,128)S(1)}, f32[32,8,128]{2,1,0:T(8,128)S(1)}, u32[]{:S(2)}, u32[]{:S(2)}) %collective-permute-start.8) | collective-permute-done | bytes 131104 | tf_op jit(solution)/shard_map/ppermute | solution.py:288
  35.6 1.8 %collective-permute-start.6 = (f32[32,8,128]{2,1,0:T(8,128)S(1)}, f32[32,8,128]{2,1,0:T(8,128)S(1)}, u32[]{:S(2)}, u32[]{:S(2)}) collective-permute-start(f32[32,8,128]{2,1,0:T(8,128)S(1)} %pad_maximum_fusion.6), channel_id=1, source_target_pairs={{0,1},{1,0},{2,3},{3,2},{4,5},{5,4},{6,7},{7,6},{8,9},{9,8},{10,11... | collective-permute-start | bytes 393224 | tf_op jit(solution)/shard_map/ppermute | solution.py:288
  37.4 3.1 %collective-permute-done.6.refs_4_ = f32[32,8,128]{2,1,0:T(8,128)S(1)} collective-permute-done((f32[32,8,128]{2,1,0:T(8,128)S(1)}, f32[32,8,128]{2,1,0:T(8,128)S(1)}, u32[]{:S(2)}, u32[]{:S(2)}) %collective-permute-start.6) | collective-permute-done | bytes 131104 | tf_op jit(solution)/shard_map/ppermute | solution.py:288
  40.6 2.8 %collective-permute-done.10.refs_12_ = f32[44,8,128]{2,1,0:T(8,128)S(1)} collective-permute-done((f32[44,8,128]{2,1,0:T(8,128)S(1)}, f32[44,8,128]{2,1,0:T(8,128)S(1)}, u32[]{:S(2)}, u32[]{:S(2)}) %collective-permute-start.10) | collective-permute-done | bytes 180256 | tf_op jit(solution)/shard_map/ppermute | solution.py:288
  43.4 3.5 %shard_map.76 = (s32[128]{0:T(128)S(1)}, s32[128]{0:T(128)S(1)}, f32[128]{0:T(128)S(1)}, f32[128,2,8,128]{3,2,1,0:T(8,128)S(1)}, f32[32,8,128]{2,1,0:T(8,128)S(1)}, /*index=5*/f32[17,8,128]{2,1,0:T(8,128)S(1)}) custom-call(bf16[2048,2048]{1,0:T(8,128)(2,1)S(1)} %shard_map.75.block, f32[32,8,128]{2,1,0:T(8,128)S(1)} %get-tuple-element.79.refs_0_, ...), custom_call_target="tpu_custom_call" | custom-call | tf_op jit(solution)/shard_map/pallas_call | solution.py:364
  48.3 2.8 %collective-permute-start.14 = (f32[17,8,128]{2,1,0:T(8,128)S(1)}, f32[17,8,128]{2,1,0:T(8,128)S(1)}, u32[]{:S(2)}, u32[]{:S(2)}) collective-permute-start(f32[17,8,128]{2,1,0:T(8,128)S(1)} %pad_maximum_fusion.12), channel_id=1, source_target_pairs={{0,8},{1,9},{2,10},{3,11},{4,12},{5,13},{6,14},{7,15},{8,0},{9,1},... | collective-permute-start | bytes 208904 | tf_op jit(solution)/shard_map/ppermute | solution.py:288
  51.1 1.6 %collective-permute-start.15 = (f32[17,8,128]{2,1,0:T(8,128)S(1)}, f32[17,8,128]{2,1,0:T(8,128)S(1)}, u32[]{:S(2)}, u32[]{:S(2)}) collective-permute-start(f32[17,8,128]{2,1,0:T(8,128)S(1)} %pad_maximum_fusion.12), channel_id=1, source_target_pairs={{0,12},{1,13},{2,14},{3,15},{4,8},{5,9},{6,10},{7,11},{8,4},{9,5},... | collective-permute-start | bytes 208904 | tf_op jit(solution)/shard_map/ppermute | solution.py:288
  53.7 2.7 %collective-permute-done.14 = f32[17,8,128]{2,1,0:T(8,128)S(1)} collective-permute-done((f32[17,8,128]{2,1,0:T(8,128)S(1)}, f32[17,8,128]{2,1,0:T(8,128)S(1)}, u32[]{:S(2)}, u32[]{:S(2)}) %collective-permute-start.14) | collective-permute-done | bytes 69664 | tf_op jit(solution)/shard_map/ppermute | solution.py:288
  60.5 2.0 %collective-permute-done.18 = f32[36,8,128]{2,1,0:T(8,128)S(1)} collective-permute-done((f32[36,8,128]{2,1,0:T(8,128)S(1)}, f32[36,8,128]{2,1,0:T(8,128)S(1)}, u32[]{:S(2)}, u32[]{:S(2)}) %collective-permute-start.18) | collective-permute-done | bytes 147488 | tf_op jit(solution)/shard_map/ppermute | solution.py:288
  65.7 6.1 %collective-permute-done.17.far_a = f32[64,8,128]{2,1,0:T(8,128)S(1)} collective-permute-done((f32[64,8,128]{2,1,0:T(8,128)S(1)}, f32[64,8,128]{2,1,0:T(8,128)S(1)}, u32[]{:S(2)}, u32[]{:S(2)}) %collective-permute-start.17) | collective-permute-done | bytes 262176 | tf_op jit(solution)/shard_map/ppermute | solution.py:288
  71.8 3.0 %shard_map.77 = (f32[128,2,8,128]{3,2,1,0:T(8,128)S(1)}, f32[128,2,8,128]{3,2,1,0:T(8,128)S(1)}, f32[17,8,128]{2,1,0:T(8,128)S(1)}, f32[64,2,8,128]{3,2,1,0:T(8,128)S(1)}, f32[8,128]{1,0:T(8,128)S(1)}) custom-call(s32[128]{0:T(128)S(1)} %get-tuple-element.87.place, s32[128]{0:T(128)S(1)} %get-tuple-element.88.away, f32[128]{0:T(128)S(1)} %get-tuple-element.89.keep, ...), custom_call_target="tpu_custom_call" | custom-call | tf_op jit(solution)/shard_map/pallas_call | solution.py:25
  76.6 2.3 %collective-permute-start.22 = (f32[17,8,128]{2,1,0:T(8,128)S(1)}, f32[17,8,128]{2,1,0:T(8,128)S(1)}, u32[]{:S(2)}, u32[]{:S(2)}) collective-permute-start(f32[17,8,128]{2,1,0:T(8,128)S(1)} %pad_maximum_fusion.13), channel_id=1, source_target_pairs={{0,8},{1,9},{2,10},{3,11},{4,12},{5,13},{6,14},{7,15},{8,0},{9,1},... | collective-permute-start | bytes 208904 | tf_op jit(solution)/shard_map/ppermute | solution.py:288
  79.0 1.6 %collective-permute-start.23 = (f32[17,8,128]{2,1,0:T(8,128)S(1)}, f32[17,8,128]{2,1,0:T(8,128)S(1)}, u32[]{:S(2)}, u32[]{:S(2)}) collective-permute-start(f32[17,8,128]{2,1,0:T(8,128)S(1)} %pad_maximum_fusion.13), channel_id=1, source_target_pairs={{0,12},{1,13},{2,14},{3,15},{4,8},{5,9},{6,10},{7,11},{8,4},{9,5},... | collective-permute-start | bytes 208904 | tf_op jit(solution)/shard_map/ppermute | solution.py:288
  81.4 3.9 %collective-permute-done.22 = f32[17,8,128]{2,1,0:T(8,128)S(1)} collective-permute-done((f32[17,8,128]{2,1,0:T(8,128)S(1)}, f32[17,8,128]{2,1,0:T(8,128)S(1)}, u32[]{:S(2)}, u32[]{:S(2)}) %collective-permute-start.22) | collective-permute-done | bytes 69664 | tf_op jit(solution)/shard_map/ppermute | solution.py:288
  87.6 3.0 %collective-permute-done.26 = f32[36,8,128]{2,1,0:T(8,128)S(1)} collective-permute-done((f32[36,8,128]{2,1,0:T(8,128)S(1)}, f32[36,8,128]{2,1,0:T(8,128)S(1)}, u32[]{:S(2)}, u32[]{:S(2)}) %collective-permute-start.26) | collective-permute-done | bytes 147488 | tf_op jit(solution)/shard_map/ppermute | solution.py:288
  94.8 4.3 %collective-permute-done.25.far_a = f32[64,8,128]{2,1,0:T(8,128)S(1)} collective-permute-done((f32[64,8,128]{2,1,0:T(8,128)S(1)}, f32[64,8,128]{2,1,0:T(8,128)S(1)}, u32[]{:S(2)}, u32[]{:S(2)}) %collective-permute-start.25) | collective-permute-done | bytes 262176 | tf_op jit(solution)/shard_map/ppermute | solution.py:288
  99.1 3.2 %shard_map.79 = (f32[128,2,8,128]{3,2,1,0:T(8,128)S(1)}, f32[128,2,8,128]{3,2,1,0:T(8,128)S(1)}, f32[17,8,128]{2,1,0:T(8,128)S(1)}, f32[64,2,8,128]{3,2,1,0:T(8,128)S(1)}, f32[8,128]{1,0:T(8,128)S(1)}) custom-call(s32[128]{0:T(128)S(1)} %get-tuple-element.87.place, s32[128]{0:T(128)S(1)} %get-tuple-element.88.away, f32[128]{0:T(128)S(1)} %get-tuple-element.89.keep, ...), custom_call_target="tpu_custom_call" | custom-call | tf_op jit(solution)/shard_map/pallas_call | solution.py:25
  103.5 1.7 %collective-permute-start.30 = (f32[17,8,128]{2,1,0:T(8,128)S(1)}, f32[17,8,128]{2,1,0:T(8,128)S(1)}, u32[]{:S(2)}, u32[]{:S(2)}) collective-permute-start(f32[17,8,128]{2,1,0:T(8,128)S(1)} %pad_maximum_fusion.14), channel_id=1, source_target_pairs={{0,4},{1,5},{2,6},{3,7},{4,0},{5,1},{6,2},{7,3},{8,12},{9,13},{10,... | collective-permute-start | bytes 208904 | tf_op jit(solution)/shard_map/ppermute | solution.py:288
  106.2 1.7 %collective-permute-start.32 = (f32[17,8,128]{2,1,0:T(8,128)S(1)}, f32[17,8,128]{2,1,0:T(8,128)S(1)}, u32[]{:S(2)}, u32[]{:S(2)}) collective-permute-start(f32[17,8,128]{2,1,0:T(8,128)S(1)} %pad_maximum_fusion.14), channel_id=1, source_target_pairs={{0,12},{1,13},{2,14},{3,15},{4,8},{5,9},{6,10},{7,11},{8,4},{9,5},... | collective-permute-start | bytes 208904 | tf_op jit(solution)/shard_map/ppermute | solution.py:288
  108.0 5.6 %collective-permute-done.31 = f32[17,8,128]{2,1,0:T(8,128)S(1)} collective-permute-done((f32[17,8,128]{2,1,0:T(8,128)S(1)}, f32[17,8,128]{2,1,0:T(8,128)S(1)}, u32[]{:S(2)}, u32[]{:S(2)}) %collective-permute-start.31) | collective-permute-done | bytes 69664 | tf_op jit(solution)/shard_map/ppermute | solution.py:288
  115.7 3.2 %collective-permute-done.35 = f32[36,8,128]{2,1,0:T(8,128)S(1)} collective-permute-done((f32[36,8,128]{2,1,0:T(8,128)S(1)}, f32[36,8,128]{2,1,0:T(8,128)S(1)}, u32[]{:S(2)}, u32[]{:S(2)}) %collective-permute-start.35) | collective-permute-done | bytes 147488 | tf_op jit(solution)/shard_map/ppermute | solution.py:288
  120.2 2.1 %collective-permute-start.34 = (f32[64,8,128]{2,1,0:T(8,128)S(1)}, f32[64,8,128]{2,1,0:T(8,128)S(1)}, u32[]{:S(2)}, u32[]{:S(2)}) collective-permute-start(f32[64,8,128]{2,1,0:T(8,128)S(1)} %constant_dynamic-update-slice_fusion.20.near_a), channel_id=1, source_target_pairs={{0,2},{1,3},{2,0},{3,1},{4,6},{5,7},{6,4},{7,5},{8,10},{9,11},{10,... | collective-permute-start | bytes 786440 | tf_op jit(solution)/shard_map/ppermute | solution.py:288
  123.3 3.4 %collective-permute-done.34.far_a = f32[64,8,128]{2,1,0:T(8,128)S(1)} collective-permute-done((f32[64,8,128]{2,1,0:T(8,128)S(1)}, f32[64,8,128]{2,1,0:T(8,128)S(1)}, u32[]{:S(2)}, u32[]{:S(2)}) %collective-permute-start.34) | collective-permute-done | bytes 262176 | tf_op jit(solution)/shard_map/ppermute | solution.py:288
  126.7 3.2 %shard_map.81 = (f32[32,8,128]{2,1,0:T(8,128)S(1)}, f32[64,2,8,128]{3,2,1,0:T(8,128)S(1)}, f32[8,128]{1,0:T(8,128)S(1)}) custom-call(s32[128]{0:T(128)S(1)} %get-tuple-element.87.place, s32[128]{0:T(128)S(1)} %get-tuple-element.88.away, f32[128]{0:T(128)S(1)} %get-tuple-element.89.keep, s32[64]{0:T(128)S(1)} %get-tuple-element.90.picked, ...), custom_call_target="tpu_custom_call" | custom-call | tf_op jit(solution)/shard_map/pallas_call | solution.py:25
  129.9 11.7 %all_to_all.5.sums = f32[32,8,128]{2,1,0:T(8,128)S(1)} all-to-all(f32[32,8,128]{2,1,0:T(8,128)S(1)} %get-tuple-element.124), channel_id=1, replica_groups=mesh['body'=2,'sub'=16] {'body','sub'}, dimensions={0} | all-to-all | bytes 262144 | tf_op jit(solution)/shard_map/all_to_all | solution.py:428
  141.7 2.2 %shard_map.82 = f32[8,64,256]{2,1,0:T(8,128)} custom-call(f32[64]{0:T(128)S(1)} %get-tuple-element.210.keep, f32[32,8,128]{2,1,0:T(8,128)S(1)} %all_to_all.5.sums, f32[8,128]{1,0:T(8,128)S(1)} %get-tuple-element.125.known, f32[64,256]{1,0:T(8,128)S(1)} %copy-done, f32[64,2,8,128]{3,2,1,0:T(8,128)S(1)} %get-tuple-element.126.mine, ...), custom_call_target="tpu_custom_call" | custom-call | tf_op jit(solution)/shard_map/pallas_call | solution.py:25
  (134 shorter events, 38.0 us)
Async XLA Ops:
  4.9 11.3 %collective-permute-start = (f32[32,8,128]{2,1,0:T(8,128)S(1)}, f32[32,8,128]{2,1,0:T(8,128)S(1)}, u32[]{:S(2)}, u32[]{:S(2)}) collective-permute-start(f32[32,8,128]{2,1,0:T(8,128)S(1)} %get-tuple-element.70), channel_id=1, source_target_pairs={{0,4},{1,5},{2,6},{3,7},{4,0},{5,1},{6,2},{7,3},{8,12},{9,13},{10,... | collective-permute-start | bytes 393224 | tf_op jit(solution)/shard_map/ppermute | solution.py:288
  10.0 14.8 %collective-permute-start.3 = (f32[44,8,128]{2,1,0:T(8,128)S(1)}, f32[44,8,128]{2,1,0:T(8,128)S(1)}, u32[]{:S(2)}, u32[]{:S(2)}) collective-permute-start(f32[44,8,128]{2,1,0:T(8,128)S(1)} %get-tuple-element.75), channel_id=1, source_target_pairs={{0,1},{1,0},{2,3},{3,2},{4,5},{5,4},{6,7},{7,6},{8,9},{9,8},{10,11... | collective-permute-start | bytes 540680 | tf_op jit(solution)/shard_map/ppermute | solution.py:288
  11.5 13.2 %collective-permute-start.4 = (f32[44,8,128]{2,1,0:T(8,128)S(1)}, f32[44,8,128]{2,1,0:T(8,128)S(1)}, u32[]{:S(2)}, u32[]{:S(2)}) collective-permute-start(f32[44,8,128]{2,1,0:T(8,128)S(1)} %get-tuple-element.76), channel_id=1, source_target_pairs={{0,2},{1,3},{2,0},{3,1},{4,6},{5,7},{6,4},{7,5},{8,10},{9,11},{10,... | collective-permute-start | bytes 540680 | tf_op jit(solution)/shard_map/ppermute | solution.py:288
  13.1 11.7 %collective-permute-start.5 = (f32[44,8,128]{2,1,0:T(8,128)S(1)}, f32[44,8,128]{2,1,0:T(8,128)S(1)}, u32[]{:S(2)}, u32[]{:S(2)}) collective-permute-start(f32[44,8,128]{2,1,0:T(8,128)S(1)} %get-tuple-element.77), channel_id=1, source_target_pairs={{0,3},{1,2},{2,1},{3,0},{4,7},{5,6},{6,5},{7,4},{8,11},{9,10},{10,... | collective-permute-start | bytes 540680 | tf_op jit(solution)/shard_map/ppermute | solution.py:288
  13.5 11.2 %collective-permute-start.1 = (f32[32,8,128]{2,1,0:T(8,128)S(1)}, f32[32,8,128]{2,1,0:T(8,128)S(1)}, u32[]{:S(2)}, u32[]{:S(2)}) collective-permute-start(f32[32,8,128]{2,1,0:T(8,128)S(1)} %get-tuple-element.71), channel_id=1, source_target_pairs={{0,8},{1,9},{2,10},{3,11},{4,12},{5,13},{6,14},{7,15},{8,0},{9,1},... | collective-permute-start | bytes 393224 | tf_op jit(solution)/shard_map/ppermute | solution.py:288
  16.1 8.6 %collective-permute-start.2 = (f32[32,8,128]{2,1,0:T(8,128)S(1)}, f32[32,8,128]{2,1,0:T(8,128)S(1)}, u32[]{:S(2)}, u32[]{:S(2)}) collective-permute-start(f32[32,8,128]{2,1,0:T(8,128)S(1)} %get-tuple-element.72), channel_id=1, source_target_pairs={{0,12},{1,13},{2,14},{3,15},{4,8},{5,9},{6,10},{7,11},{8,4},{9,5},... | collective-permute-start | bytes 393224 | tf_op jit(solution)/shard_map/ppermute | solution.py:288
  24.9 15.7 %collective-permute-start.11 = (f32[44,8,128]{2,1,0:T(8,128)S(1)}, f32[44,8,128]{2,1,0:T(8,128)S(1)}, u32[]{:S(2)}, u32[]{:S(2)}) collective-permute-start(f32[44,8,128]{2,1,0:T(8,128)S(1)} %pad_maximum_fusion.2), channel_id=1, source_target_pairs={{0,12},{1,13},{2,14},{3,15},{4,8},{5,9},{6,10},{7,11},{8,4},{9,5},... | collective-permute-start | bytes 540680 | tf_op jit(solution)/shard_map/ppermute | solution.py:288
  28.0 15.4 %collective-permute-start.10 = (f32[44,8,128]{2,1,0:T(8,128)S(1)}, f32[44,8,128]{2,1,0:T(8,128)S(1)}, u32[]{:S(2)}, u32[]{:S(2)}) collective-permute-start(f32[44,8,128]{2,1,0:T(8,128)S(1)} %pad_maximum_fusion.1), channel_id=1, source_target_pairs={{0,8},{1,9},{2,10},{3,11},{4,12},{5,13},{6,14},{7,15},{8,0},{9,1},... | collective-permute-start | bytes 540680 | tf_op jit(solution)/shard_map/ppermute | solution.py:288
  29.1 14.3 %collective-permute-start.9 = (f32[44,8,128]{2,1,0:T(8,128)S(1)}, f32[44,8,128]{2,1,0:T(8,128)S(1)}, u32[]{:S(2)}, u32[]{:S(2)}) collective-permute-start(f32[44,8,128]{2,1,0:T(8,128)S(1)} %pad_maximum_fusion), channel_id=1, source_target_pairs={{0,4},{1,5},{2,6},{3,7},{4,0},{5,1},{6,2},{7,3},{8,12},{9,13},{10,... | collective-permute-start | bytes 540680 | tf_op jit(solution)/shard_map/ppermute | solution.py:288
  29.6 6.0 %collective-permute-start.8 = (f32[32,8,128]{2,1,0:T(8,128)S(1)}, f32[32,8,128]{2,1,0:T(8,128)S(1)}, u32[]{:S(2)}, u32[]{:S(2)}) collective-permute-start(f32[32,8,128]{2,1,0:T(8,128)S(1)} %pad_maximum_fusion.8), channel_id=1, source_target_pairs={{0,3},{1,2},{2,1},{3,0},{4,7},{5,6},{6,5},{7,4},{8,11},{9,10},{10,... | collective-permute-start | bytes 393224 | tf_op jit(solution)/shard_map/ppermute | solution.py:288
  48.2 5.4 %collective-permute-start.13 = (f32[17,8,128]{2,1,0:T(8,128)S(1)}, f32[17,8,128]{2,1,0:T(8,128)S(1)}, u32[]{:S(2)}, u32[]{:S(2)}) collective-permute-start(f32[17,8,128]{2,1,0:T(8,128)S(1)} %pad_maximum_fusion.12), channel_id=1, source_target_pairs={{0,4},{1,5},{2,6},{3,7},{4,0},{5,1},{6,2},{7,3},{8,12},{9,13},{10,... | collective-permute-start | bytes 208904 | tf_op jit(solution)/shard_map/ppermute | solution.py:288
  48.3 8.0 %collective-permute-start.14 = (f32[17,8,128]{2,1,0:T(8,128)S(1)}, f32[17,8,128]{2,1,0:T(8,128)S(1)}, u32[]{:S(2)}, u32[]{:S(2)}) collective-permute-start(f32[17,8,128]{2,1,0:T(8,128)S(1)} %pad_maximum_fusion.12), channel_id=1, source_target_pairs={{0,8},{1,9},{2,10},{3,11},{4,12},{5,13},{6,14},{7,15},{8,0},{9,1},... | collective-permute-start | bytes 208904 | tf_op jit(solution)/shard_map/ppermute | solution.py:288
  51.1 6.2 %collective-permute-start.15 = (f32[17,8,128]{2,1,0:T(8,128)S(1)}, f32[17,8,128]{2,1,0:T(8,128)S(1)}, u32[]{:S(2)}, u32[]{:S(2)}) collective-permute-start(f32[17,8,128]{2,1,0:T(8,128)S(1)} %pad_maximum_fusion.12), channel_id=1, source_target_pairs={{0,12},{1,13},{2,14},{3,15},{4,8},{5,9},{6,10},{7,11},{8,4},{9,5},... | collective-permute-start | bytes 208904 | tf_op jit(solution)/shard_map/ppermute | solution.py:288
  57.3 5.2 %collective-permute-start.18 = (f32[36,8,128]{2,1,0:T(8,128)S(1)}, f32[36,8,128]{2,1,0:T(8,128)S(1)}, u32[]{:S(2)}, u32[]{:S(2)}) collective-permute-start(f32[36,8,128]{2,1,0:T(8,128)S(1)} %pad_maximum_fusion.3), channel_id=1, source_target_pairs={{0,2},{1,3},{2,0},{3,1},{4,6},{5,7},{6,4},{7,5},{8,10},{9,11},{10,... | collective-permute-start | bytes 442376 | tf_op jit(solution)/shard_map/ppermute | solution.py:288
  58.9 6.4 %collective-permute-start.16 = (f32[32,8,128]{2,1,0:T(8,128)S(1)}, f32[32,8,128]{2,1,0:T(8,128)S(1)}, u32[]{:S(2)}, u32[]{:S(2)}) collective-permute-start(f32[32,8,128]{2,1,0:T(8,128)S(1)} %pad_maximum_fusion.9), channel_id=1, source_target_pairs={{0,1},{1,0},{2,3},{3,2},{4,5},{5,4},{6,7},{7,6},{8,9},{9,8},{10,11... | collective-permute-start | bytes 393224 | tf_op jit(solution)/shard_map/ppermute | solution.py:288
  62.5 9.3 %collective-permute-start.19 = (f32[72,8,128]{2,1,0:T(8,128)S(1)}, f32[72,8,128]{2,1,0:T(8,128)S(1)}, u32[]{:S(2)}, u32[]{:S(2)}) collective-permute-start(f32[72,8,128]{2,1,0:T(8,128)S(1)} %constant_dynamic-update-slice_fusion.5.near_b), channel_id=1, source_target_pairs={{0,1},{1,0},{2,3},{3,2},{4,5},{5,4},{6,7},{7,6},{8,9},{9,8},{10,11... | collective-permute-start | bytes 884744 | tf_op jit(solution)/shard_map/ppermute | solution.py:288
  65.4 6.4 %collective-permute-start.17 = (f32[64,8,128]{2,1,0:T(8,128)S(1)}, f32[64,8,128]{2,1,0:T(8,128)S(1)}, u32[]{:S(2)}, u32[]{:S(2)}) collective-permute-start(f32[64,8,128]{2,1,0:T(8,128)S(1)} %constant_dynamic-update-slice_fusion.near_a), channel_id=1, source_target_pairs={{0,2},{1,3},{2,0},{3,1},{4,6},{5,7},{6,4},{7,5},{8,10},{9,11},{10,... | collective-permute-start | bytes 786440 | tf_op jit(solution)/shard_map/ppermute | solution.py:288
  76.1 5.3 %collective-permute-start.21 = (f32[17,8,128]{2,1,0:T(8,128)S(1)}, f32[17,8,128]{2,1,0:T(8,128)S(1)}, u32[]{:S(2)}, u32[]{:S(2)}) collective-permute-start(f32[17,8,128]{2,1,0:T(8,128)S(1)} %pad_maximum_fusion.13), channel_id=1, source_target_pairs={{0,4},{1,5},{2,6},{3,7},{4,0},{5,1},{6,2},{7,3},{8,12},{9,13},{10,... | collective-permute-start | bytes 208904 | tf_op jit(solution)/shard_map/ppermute | solution.py:288
  76.6 8.7 %collective-permute-start.22 = (f32[17,8,128]{2,1,0:T(8,128)S(1)}, f32[17,8,128]{2,1,0:T(8,128)S(1)}, u32[]{:S(2)}, u32[]{:S(2)}) collective-permute-start(f32[17,8,128]{2,1,0:T(8,128)S(1)} %pad_maximum_fusion.13), channel_id=1, source_target_pairs={{0,8},{1,9},{2,10},{3,11},{4,12},{5,13},{6,14},{7,15},{8,0},{9,1},... | collective-permute-start | bytes 208904 | tf_op jit(solution)/shard_map/ppermute | solution.py:288
  79.0 6.4 %collective-permute-start.23 = (f32[17,8,128]{2,1,0:T(8,128)S(1)}, f32[17,8,128]{2,1,0:T(8,128)S(1)}, u32[]{:S(2)}, u32[]{:S(2)}) collective-permute-start(f32[17,8,128]{2,1,0:T(8,128)S(1)} %pad_maximum_fusion.13), channel_id=1, source_target_pairs={{0,12},{1,13},{2,14},{3,15},{4,8},{5,9},{6,10},{7,11},{8,4},{9,5},... | collective-permute-start | bytes 208904 | tf_op jit(solution)/shard_map/ppermute | solution.py:288
  80.6 13.3 %collective-permute-start.28 = (f32[64,2,8,128]{3,2,1,0:T(8,128)S(1)}, f32[64,2,8,128]{3,2,1,0:T(8,128)S(1)}, u32[]{:S(2)}, u32[]{:S(2)}) collective-permute-start(f32[64,2,8,128]{3,2,1,0:T(8,128)S(1)} %get-tuple-element.98.mine), channel_id=1, source_target_pairs={{0,16},{16,0},{1,17},{17,1},{2,18},{18,2},{3,19},{19,3},{4,20},{20... | collective-permute-start | bytes 1572872 | tf_op jit(solution)/shard_map/ppermute | solution.py:291
  85.4 5.2 %collective-permute-start.26 = (f32[36,8,128]{2,1,0:T(8,128)S(1)}, f32[36,8,128]{2,1,0:T(8,128)S(1)}, u32[]{:S(2)}, u32[]{:S(2)}) collective-permute-start(f32[36,8,128]{2,1,0:T(8,128)S(1)} %pad_maximum_fusion.4), channel_id=1, source_target_pairs={{0,2},{1,3},{2,0},{3,1},{4,6},{5,7},{6,4},{7,5},{8,10},{9,11},{10,... | collective-permute-start | bytes 442376 | tf_op jit(solution)/shard_map/ppermute | solution.py:288
  86.5 6.1 %collective-permute-start.24 = (f32[32,8,128]{2,1,0:T(8,128)S(1)}, f32[32,8,128]{2,1,0:T(8,128)S(1)}, u32[]{:S(2)}, u32[]{:S(2)}) collective-permute-start(f32[32,8,128]{2,1,0:T(8,128)S(1)} %pad_maximum_fusion.10), channel_id=1, source_target_pairs={{0,1},{1,0},{2,3},{3,2},{4,5},{5,4},{6,7},{7,6},{8,9},{9,8},{10,11... | collective-permute-start | bytes 393224 | tf_op jit(solution)/shard_map/ppermute | solution.py:288
  90.6 8.4 %collective-permute-start.27 = (f32[72,8,128]{2,1,0:T(8,128)S(1)}, f32[72,8,128]{2,1,0:T(8,128)S(1)}, u32[]{:S(2)}, u32[]{:S(2)}) collective-permute-start(f32[72,8,128]{2,1,0:T(8,128)S(1)} %constant_dynamic-update-slice_fusion.15.near_b), channel_id=1, source_target_pairs={{0,1},{1,0},{2,3},{3,2},{4,5},{5,4},{6,7},{7,6},{8,9},{9,8},{10,11... | collective-permute-start | bytes 884744 | tf_op jit(solution)/shard_map/ppermute | solution.py:288
  92.6 6.4 %collective-permute-start.25 = (f32[64,8,128]{2,1,0:T(8,128)S(1)}, f32[64,8,128]{2,1,0:T(8,128)S(1)}, u32[]{:S(2)}, u32[]{:S(2)}) collective-permute-start(f32[64,8,128]{2,1,0:T(8,128)S(1)} %constant_dynamic-update-slice_fusion.10.near_a), channel_id=1, source_target_pairs={{0,2},{1,3},{2,0},{3,1},{4,6},{5,7},{6,4},{7,5},{8,10},{9,11},{10,... | collective-permute-start | bytes 786440 | tf_op jit(solution)/shard_map/ppermute | solution.py:288
  105.2 8.5 %collective-permute-start.31 = (f32[17,8,128]{2,1,0:T(8,128)S(1)}, f32[17,8,128]{2,1,0:T(8,128)S(1)}, u32[]{:S(2)}, u32[]{:S(2)}) collective-permute-start(f32[17,8,128]{2,1,0:T(8,128)S(1)} %pad_maximum_fusion.14), channel_id=1, source_target_pairs={{0,8},{1,9},{2,10},{3,11},{4,12},{5,13},{6,14},{7,15},{8,0},{9,1},... | collective-permute-start | bytes 208904 | tf_op jit(solution)/shard_map/ppermute | solution.py:288
  106.2 7.4 %collective-permute-start.32 = (f32[17,8,128]{2,1,0:T(8,128)S(1)}, f32[17,8,128]{2,1,0:T(8,128)S(1)}, u32[]{:S(2)}, u32[]{:S(2)}) collective-permute-start(f32[17,8,128]{2,1,0:T(8,128)S(1)} %pad_maximum_fusion.14), channel_id=1, source_target_pairs={{0,12},{1,13},{2,14},{3,15},{4,8},{5,9},{6,10},{7,11},{8,4},{9,5},... | collective-permute-start | bytes 208904 | tf_op jit(solution)/shard_map/ppermute | solution.py:288
  108.0 14.4 %collective-permute-start.37 = (f32[64,2,8,128]{3,2,1,0:T(8,128)S(1)}, f32[64,2,8,128]{3,2,1,0:T(8,128)S(1)}, u32[]{:S(2)}, u32[]{:S(2)}) collective-permute-start(f32[64,2,8,128]{3,2,1,0:T(8,128)S(1)} %get-tuple-element.111.mine), channel_id=1, source_target_pairs={{0,16},{16,0},{1,17},{17,1},{2,18},{18,2},{3,19},{19,3},{4,20},{20... | collective-permute-start | bytes 1572872 | tf_op jit(solution)/shard_map/ppermute | solution.py:291
  114.3 5.9 %collective-permute-start.33 = (f32[32,8,128]{2,1,0:T(8,128)S(1)}, f32[32,8,128]{2,1,0:T(8,128)S(1)}, u32[]{:S(2)}, u32[]{:S(2)}) collective-permute-start(f32[32,8,128]{2,1,0:T(8,128)S(1)} %pad_maximum_fusion.11), channel_id=1, source_target_pairs={{0,1},{1,0},{2,3},{3,2},{4,5},{5,4},{6,7},{7,6},{8,9},{9,8},{10,11... | collective-permute-start | bytes 393224 | tf_op jit(solution)/shard_map/ppermute | solution.py:288
  118.9 7.8 %collective-permute-start.36 = (f32[72,8,128]{2,1,0:T(8,128)S(1)}, f32[72,8,128]{2,1,0:T(8,128)S(1)}, u32[]{:S(2)}, u32[]{:S(2)}) collective-permute-start(f32[72,8,128]{2,1,0:T(8,128)S(1)} %constant_dynamic-update-slice_fusion.25.near_b), channel_id=1, source_target_pairs={{0,1},{1,0},{2,3},{3,2},{4,5},{5,4},{6,7},{7,6},{8,9},{9,8},{10,11... | collective-permute-start | bytes 884744 | tf_op jit(solution)/shard_map/ppermute | solution.py:288
  120.2 6.5 %collective-permute-start.34 = (f32[64,8,128]{2,1,0:T(8,128)S(1)}, f32[64,8,128]{2,1,0:T(8,128)S(1)}, u32[]{:S(2)}, u32[]{:S(2)}) collective-permute-start(f32[64,8,128]{2,1,0:T(8,128)S(1)} %constant_dynamic-update-slice_fusion.20.near_a), channel_id=1, source_target_pairs={{0,2},{1,3},{2,0},{3,1},{4,6},{5,7},{6,4},{7,5},{8,10},{9,11},{10,... | collective-permute-start | bytes 786440 | tf_op jit(solution)/shard_map/ppermute | solution.py:288
  129.9 11.8 %collective-permute-start.38 = (f32[64,2,8,128]{3,2,1,0:T(8,128)S(1)}, f32[64,2,8,128]{3,2,1,0:T(8,128)S(1)}, u32[]{:S(2)}, u32[]{:S(2)}) collective-permute-start(f32[64,2,8,128]{3,2,1,0:T(8,128)S(1)} %get-tuple-element.126.mine), channel_id=1, source_target_pairs={{0,16},{16,0},{1,17},{17,1},{2,18},{18,2},{3,19},{19,3},{4,20},{20... | collective-permute-start | bytes 1572872 | tf_op jit(solution)/shard_map/ppermute | solution.py:291
  (8 other events, 70.6 us)

commit v12 on v11

--- a/solution.py
+++ b/solution.py
@@ -1,4 +1,5 @@
 import functools
+import math
 
 import jax
 import jax.numpy as jnp
@@ -66,11 +67,9 @@
         answer[ntile] = sums
 
 
-def pack_kernel(nh, nz, by_z, place, field, *refs):
-    if not by_z:
-        table, *refs = refs
+def pack_kernel(nh, tiles, place, field, table, *refs):
     *outs, whole = refs
-    tiles = whole.shape[0] // (4 * nz + 1)
+    extra = table.shape[1]
     whole[...] = jnp.zeros_like(whole)
 
     def body(p, carry):
@@ -79,12 +78,10 @@
 
     lax.fori_loop(0, field.shape[0], body, 0, unroll=4)
     for i, out in enumerate(outs):
-        size = out.shape[0] // (4 * nz // len(outs))
-        for k in range(out.shape[0] // size):
-            owner = i * 4 + k if by_z else k * 4 + i
-            out[k * size : k * size + tiles] = whole[owner * tiles : (owner + 1) * tiles]
-            if not by_z:
-                out[k * size + tiles : (k + 1) * size] = table[owner]
+        for k in range(len(outs)):
+            owner = i * len(outs) + k
+            out[k * tiles : (k + 1) * tiles - extra] = whole[owner * tiles : (owner + 1) * tiles - extra]
+            out[(k + 1) * tiles - extra : (k + 1) * tiles] = table[owner]
 
 
 def block_kernel(block, held, sems):
@@ -99,29 +96,23 @@
         copy.wait()
 
 
-def start_kernel(nh, cut, room, lines, extra, nz, block, *refs):
-    a_z, refs = refs[:nz], refs[nz:]
-    a_far, refs = refs[:3], refs[3:]
-    b_near, refs = refs[:4], refs[4:]
-    b_far, refs = refs[: nz - 1], refs[nz - 1 :]
+def start_kernel(nh, room, lines, tiles, side, block, *refs):
+    near_parts, refs = refs[:side], refs[side:]
+    far_parts, refs = refs[: side - 1], refs[side - 1 :]
     near, far, on, r_out, comp, answer, load, facts, sems = refs
-    first, second = cut * nh, (room - cut) * nh
-    blocks = []
-    for z in range(nz):
-        for m in range(4):
-            one = (a_z[z], 0) if m == 0 else (a_far[m - 1], z * first)
-            two = (b_near[m], 0) if z == 0 else (b_far[z - 1], m * (second + extra))
-            blocks.append((*one, *two))
+    blocks = [
+        (near_parts[i], 0) if k == 0 else (far_parts[k - 1], i * tiles) for i in range(side) for k in range(side)
+    ]
     copies = []
-    for i, (_, _, two, at_two) in enumerate(blocks):
-        rows = pl.ds(at_two + second + lines, extra - lines)
-        copies.append(pltpu.make_async_copy(two.at[rows], facts.at[i], sems.at[i]))
+    for i, (part, at) in enumerate(blocks):
+        rows = pl.ds(at + room * nh + lines, tiles - room * nh - lines)
+        copies.append(pltpu.make_async_copy(part.at[rows], facts.at[i], sems.at[i]))
         copies[-1].start()
     load[...] = jnp.zeros_like(load)
     gamma = energy = jnp.zeros(r_out.shape[2:], jnp.float32)
-    for i, (one, at_one, two, at_two) in enumerate(blocks):
-        at_comp = at_two + second
-        comp[i * lines : (i + 1) * lines] = two[at_comp : at_comp + lines]
+    for i, (part, at) in enumerate(blocks):
+        at_comp = at + room * nh
+        comp[i * lines : (i + 1) * lines] = part[at_comp : at_comp + lines]
         copies[i].wait()
         for j in range(room):
             row = i * room + j
@@ -129,17 +120,14 @@
             near[row] = slot
             far[row] = facts[i, j // SUBLANES, j % SUBLANES, 1].astype(jnp.int32)
             on[row] = facts[i, j // SUBLANES, j % SUBLANES, 2]
-            if j < cut:
-                r = one[at_one + j * nh : at_one + (j + 1) * nh]
-            else:
-                r = two[at_two + (j - cut) * nh : at_two + (j - cut + 1) * nh]
+            r = part[at + j * nh : at + (j + 1) * nh]
             r_out[row] = r
             load[pl.ds(slot, nh)] += r
             for h in range(nh):
                 line, sub = divmod(j * nh + h, SUBLANES)
                 square = r[h] * r[h]
                 gamma = gamma + square
-                energy = energy + two[at_comp + line, sub : sub + 1, :] * square
+                energy = energy + part[at_comp + line, sub : sub + 1, :] * square
     respond(block, load, gamma, energy, answer)
 
 
@@ -157,7 +145,7 @@
     return gamma, gamma / (delta - beta * gamma / known[:, 1:2]), beta
 
 
-def home_kernel(first, last, nh, room, lines, place, away, keep, picked, comp, own, near_a, far_a, near_b, far_b, known, block, *refs):
+def home_kernel(first, last, nh, room, lines, place, away, keep, picked, comp, own, near, far, known, block, *refs):
     r_in, *refs = refs
     if not first:
         s_in, *refs = refs
@@ -166,12 +154,11 @@
     answer, part, known_out, load, resp = refs
     load[...] = jnp.zeros_like(load)
     nrow, _, ncase, width = r_in.shape
-    at = 0
-    for piece in (near_a, far_a, near_b, far_b):
-        resp[at : at + piece.shape[0]] = piece[...]
-        at += piece.shape[0]
-    each = own.shape[0] // 2 + 1
-    sums = tree([piece[i + each - 1] for piece in (near_b, far_b) for i in range(0, piece.shape[0], each)])
+    size, each = near.shape[0], own.shape[0]
+    resp[:size], resp[size:] = near[...], far[...]
+    shares = [[part[i + each - 1] for i in range(0, size, each)] for part in (near, far)]
+    (one, two), (three, four) = [[tree(part[: len(part) // 2]), tree(part[len(part) // 2 :])] for part in shares]
+    sums = (one + four) + (two + three)
     gamma, alpha, beta = steps(first, sums, known[...])
     lane = lax.broadcasted_iota(jnp.int32, (ncase, width), 1)
     known_out[...] = jnp.where(lane == 0, gamma, jnp.where(lane == 1, alpha, beta))
@@ -189,18 +176,18 @@
         gamma, energy = sums
         for j in range(room):
             row = i * room + j
-            near, far, on = place[row], away[row], keep[row]
+            close, apart, on = place[row], away[row], keep[row]
             for h in range(nh):
                 line, sub = divmod(j * nh + h, SUBLANES)
                 c = comp[i * lines + line, sub : sub + 1, :]
                 residual = r_in[row, h]
-                image = on * (own[near + h] + resp[far + h] + c * residual)
+                image = on * (own[close + h] + resp[apart + h] + c * residual)
                 if not first:
                     image = image + beta * s_in[row, h]
                 residual = residual - alpha * image
                 if not last:
                     r[row, h], s[row, h] = residual, image
-                load[near + h] += residual
+                load[close + h] += residual
                 square = residual * residual
                 gamma = gamma + square
                 energy = energy + c * square
@@ -277,15 +264,16 @@
     nrow = nsub * room
     lines = -(-room * nh // SUBLANES)
     deep = -(-room // SUBLANES)
-    extra = lines + deep
-    cut = room // 2
-    first = cut * nh
-    second = (room - cut) * nh + extra
+    tiles = room * nh + lines + deep
     nz = nsub // 4
-    half = nslot // 2 * nh
+    width = math.isqrt(nsub)
 
     def swap(value, far):
         return lax.ppermute(value, "sub", [(i, i ^ far) for i in range(nsub)])
+
+    def cross(value, far_0, far_1):
+        pairs = [(b * nsub + i, b * nsub + (i ^ far)) for b, far in enumerate((far_0, far_1)) for i in range(nsub)]
+        return lax.ppermute(value, ("body", "sub"), pairs)
 
     def sibling(value):
         return lax.ppermute(value, "body", [(i, nbody - 1 - i) for i in range(nbody)])
@@ -297,20 +285,20 @@
     index = jnp.arange(npatch, dtype=jnp.int32)
     earlier = (owner[None, :] == owner[:, None]) & (index[None, :] < index[:, None])
     rank = jnp.sum(earlier.astype(jnp.int32), axis=1)
-    base, none = owner ^ me, 4 * nz
-    place_a = jnp.where(rank < cut, base * cut + rank, none * cut) * nh
-    place_b = jnp.where(rank < cut, none * (room - cut), base * (room - cut) + rank - cut) * nh
+    away = owner ^ me
+    high, low = away // width, away % width
+    order = jnp.where(side == 0, high * width + low, low * width + high)
+    place = order * tiles + rank * nh
 
     def found(away):
         x_bit, y_bit, z_part = away & 1, (away >> 1) & 1, away >> 2
-        found_a = ((y_bit * 2 + x_bit) * nz + z_part) * half + other_slot * nh
-        found_b = ((x_bit * 2 + y_bit) * nz + z_part) * (half + 1) + (other_slot - nslot // 2) * nh
-        return jnp.where(other_slot < nslot // 2, found_a, nsub * half + found_b)
+        plane = jnp.where(side == 0, y_bit * 2 + x_bit, x_bit * 2 + y_bit)
+        return (plane * nz + z_part) * per + other_slot * nh
 
     facts = jnp.stack([slot * nh, found(owner ^ other)], axis=1).astype(jnp.float32)
     facts = jnp.concatenate([facts, keep[:, None]], axis=1)
     facts = jnp.concatenate([compliance, jnp.pad(facts, ((0, 0), (0, LANES - 3)))], axis=1)
-    row = (owner ^ me) * room + rank
+    row = order * room + rank
     placed = (row[None, :] == jnp.arange(nrow, dtype=jnp.int32)[:, None]).astype(jnp.float32)
     facts = jnp.dot(placed, facts, precision=lax.Precision.HIGHEST).reshape(nsub, room, gap + LANES)
     lined = facts[:, :, :gap].reshape(nsub, room * nh, LANES)
@@ -320,27 +308,18 @@
     start = (keep[None, :, None] * rhs).reshape(ncase, npatch, nh, LANES)
     start = jnp.transpose(start, (1, 2, 0, 3))
     picked = found(me ^ other).astype(jnp.int32)
-    place_a, place_b, picked = lax.optimization_barrier((place_a, place_b, picked))
-
-    a_z = call(
-        functools.partial(pack_kernel, nh, nz, True),
-        (f32(4 * first, ncase, LANES),) * nz,
-        [SMEM, VMEM],
-        place_a,
-        start,
-        scratch=[pltpu.VMEM(((nsub + 1) * cut * nh, ncase, LANES), jnp.float32)],
-    )
-    b_near = call(
-        functools.partial(pack_kernel, nh, nz, False),
-        (f32(nz * second, ncase, LANES),) * 4,
+    place, picked = lax.optimization_barrier((place, picked))
+
+    packed = call(
+        functools.partial(pack_kernel, nh, tiles),
+        (f32(width * tiles, ncase, LANES),) * width,
         [SMEM, VMEM, VMEM],
-        place_b,
+        place,
         start,
         table,
-        scratch=[pltpu.VMEM(((nsub + 1) * (room - cut) * nh, ncase, LANES), jnp.float32)],
+        scratch=[pltpu.VMEM((nsub * tiles, ncase, LANES), jnp.float32)],
     )
-    a_z = [a_z[0]] + [swap(a_z[z], 4 * z) for z in range(1, nz)]
-    b_near = [b_near[0]] + [swap(b_near[m], m) for m in range(1, 4)]
+    near_parts = [packed[0]] + [cross(packed[i], i * width, i) for i in range(1, width)]
     block = call(
         block_kernel,
         jax.ShapeDtypeStruct(block.shape, block.dtype),
@@ -349,23 +328,21 @@
         scratch=[pltpu.SemaphoreType.DMA((nslot,))],
         cost=pl.CostEstimate(flops=0, bytes_accessed=4 * block.size, transcendentals=0),
     )
-    a_z, b_near, block = lax.optimization_barrier((a_z, b_near, block))
-    b_far = [
-        swap(jnp.concatenate([part[z * second : (z + 1) * second] for part in b_near]), 4 * z)
-        for z in range(1, nz)
+    near_parts, block = lax.optimization_barrier((near_parts, block))
+    far_parts = [
+        cross(jnp.concatenate([part[k * tiles : (k + 1) * tiles] for part in near_parts]), k, k * width)
+        for k in range(1, width)
     ]
-    a_far = [
-        swap(jnp.concatenate([part[m * first : (m + 1) * first] for part in a_z]), m) for m in range(1, 4)
-    ]
+
     field = f32(nrow, nh, ncase, LANES)
     answer = f32(per, ncase, LANES)
     load = pltpu.VMEM((nslot * nh, ncase, LANES), jnp.float32)
     spread = pltpu.VMEM((nsub * per, ncase, LANES), jnp.float32)
     near, far, on, home_r, comp, own = pl.pallas_call(
-        functools.partial(start_kernel, nh, cut, room, lines, extra, nz),
+        functools.partial(start_kernel, nh, room, lines, tiles, width),
         out_shape=(jax.ShapeDtypeStruct((nrow,), jnp.int32),) * 2
         + (f32(nrow), field, f32(nsub * lines, ncase, LANES), answer),
-        in_specs=[VMEM] * (2 * nz + 7),
+        in_specs=[VMEM] * (2 * width),
         out_specs=(SMEM,) * 3 + (VMEM,) * 3,
         scratch_shapes=[
             load,
@@ -373,7 +350,7 @@
             pltpu.SemaphoreType.DMA((nsub,)),
         ],
         compiler_params=PARAMS,
-    )(block, *a_z, *a_far, *b_near, *b_far)
+    )(block, *near_parts, *far_parts)
     def update(step, lists, known, part):
         return call(
             functools.partial(list_kernel, step == 0),
@@ -399,27 +376,23 @@
             lists = update(step - 1, lists, known, part)
         spread_out = jnp.concatenate([spread_out[: per - 1], own[per - 1 :] + spread_out[per - 1 :]])
         parts = [spread_out] + [swap(spread_out, 4 * z) for z in range(1, nz)]
-        a = jnp.concatenate([part[:half] for part in parts])
-        b = jnp.concatenate([part[half:] for part in parts])
-        far_a, far_b = swap(a, 1), swap(b, 2)
-        a, b = jnp.concatenate([a, far_a]), jnp.concatenate([b, far_b])
-        far_a, far_b = swap(a, 2), swap(b, 1)
+        close = jnp.concatenate(parts)
+        close = jnp.concatenate([close, cross(close, 1, 2)])
+        apart = cross(close, 2, 1)
         if step > 0:
-            far_a, far_b, lists = lax.optimization_barrier((far_a, far_b, lists))
+            apart, lists = lax.optimization_barrier((apart, lists))
         *state, own, part, known = call(
             functools.partial(home_kernel, step == 0, last, nh, room, lines),
             (field,) * (0 if last else 2) + (f32(nbody * nsub, ncase, LANES) if last else answer, f32(npatch, nh, ncase, LANES), f32(ncase, LANES)),
-            [SMEM] * 4 + [VMEM] * (8 + len(state)),
+            [SMEM] * 4 + [VMEM] * (6 + len(state)),
             near,
             far,
             on,
             picked,
             comp,
             own,
-            a,
-            far_a,
-            b,
-            far_b,
+            close,
+            apart,
             known,
             block,
             *state,

time: 144 us -> 155 us (1.076)
  waiting for transfers between devices: 56.8 us -> 74.2 us
  starting transfers between devices: 47.3 us -> 42.2 us
    ppermute x0 -> x12, waiting for transfers between devices: none -> 52.5 us  [cross(): return lax.ppermute(value, ('body', 'sub'), pairs)]
    ppermute x33 -> x9, waiting for transfers between devices: 53 us -> 14.5 us  [swap(): return lax.ppermute(value, 'sub', [(i, i ^ far) for i in range(nsub)])]
    ppermute x33 -> x9, starting transfers between devices: 47.1 us -> 24.7 us  [swap(): return lax.ppermute(value, 'sub', [(i, i ^ far) for i in range(nsub)])]
    ppermute x0 -> x12, starting transfers between devices: none -> 16.9 us  [cross(): return lax.ppermute(value, ('body', 'sub'), pairs)]
    ppermute x6, waiting for transfers between devices: 3.77 us -> 7.24 us  [sibling(): lax.ppermute(value, 'body', [(i, nbody - 1 - i) for i in range(nbody)])]
    pallas_call x9 -> x8, Pallas kernels: 18.3 us -> 17.6 us  [call(): pl.pallas_call(kernel, out_shape=tuple(out_shape) if several else out_sha...]
  transfers between devices with their start and end apart: 39 -> 27, of which waited for: 23 -> 20; matrix products, arithmetic and copies ran while one was open for 1% -> 0% of each run, Pallas kernels for 4% -> 3%
where the time goes in v12:
time: 155 us
  waiting for transfers between devices  74.2 us (48%)
  starting transfers between devices  42.2 us (27%)
  Pallas kernels  21.1 us (14%)
  blocking collectives  11.1 us (7%)
  other arithmetic  3.67 us (2%)
    ppermute x12, waiting for transfers between devices, cross(): return lax.ppermute(value, ('body', 'sub'), pairs)  52.5 us
    ppermute x9, starting transfers between devices, swap(): return lax.ppermute(value, 'sub', [(i, i ^ far) for i in range(nsub)])  24.7 us
    pallas_call x8, Pallas kernels, call(): pl.pallas_call(kernel, out_shape=tuple(out_shape) if several else out_sha...  17.6 us
    ppermute x12, starting transfers between devices, cross(): return lax.ppermute(value, ('body', 'sub'), pairs)  16.9 us
    ppermute x9, waiting for transfers between devices, swap(): return lax.ppermute(value, 'sub', [(i, i ^ far) for i in range(nsub)])  14.5 us
    all_to_all x1, blocking collectives, on_device(): lax.all_to_all(own, ('body', 'sub'), split_axis=0, concat_axis=0, tiled=T...  11.1 us
    ppermute x6, waiting for transfers between devices, sibling(): lax.ppermute(value, 'body', [(i, nbody - 1 - i) for i in range(nbody)])  7.24 us
    pallas_call x1, Pallas kernels, on_device(): pl.pallas_call(functools.partial(start_kernel, nh, room, lines, tiles, wi...  3.47 us
  transfers between devices with their start and end apart: 27, of which 20 were waited for; matrix products, arithmetic and copies ran while one was open for 0% of the time, Pallas kernels for 3%

profile of v12, /device:TPU:0, one launch (start us, length us, event | category | flops | bytes accessed | tf_op | source)
XLA Modules:
  0.0 154.7 jit_solution(2457024680076162095)
XLA Ops:
  6.2 3.1 %collective-permute-start = (f32[76,8,128]{2,1,0:T(8,128)S(1)}, f32[76,8,128]{2,1,0:T(8,128)S(1)}, u32[]{:S(2)}, u32[]{:S(2)}) collective-permute-start(f32[76,8,128]{2,1,0:T(8,128)S(1)} %get-tuple-element.59), channel_id=1, source_target_pairs={{0,4},{1,5},{2,6},{3,7},{4,0},{5,1},{6,2},{7,3},{8,12},{9,13},{10,... | collective-permute-start | bytes 933896 | tf_op jit(solution)/shard_map/ppermute | solution.py:276
  9.3 2.6 %collective-permute-start.1 = (f32[76,8,128]{2,1,0:T(8,128)S(1)}, f32[76,8,128]{2,1,0:T(8,128)S(1)}, u32[]{:S(2)}, u32[]{:S(2)}) collective-permute-start(f32[76,8,128]{2,1,0:T(8,128)S(1)} %get-tuple-element.60), channel_id=1, source_target_pairs={{0,8},{1,9},{2,10},{3,11},{4,12},{5,13},{6,14},{7,15},{8,0},{9,1},... | collective-permute-start | bytes 933896 | tf_op jit(solution)/shard_map/ppermute | solution.py:276
  11.9 3.5 %shard_map.74.block = bf16[2048,2048]{1,0:T(8,128)(2,1)S(1)} custom-call(bf16[2048,2048]{1,0:T(8,128)(2,1)} %bitcast.40), custom_call_target="tpu_custom_call" | custom-call | bytes 16777216 | tf_op jit(solution)/shard_map/pallas_call | solution.py:26
  15.4 1.7 %collective-permute-done.refs_1_ = f32[76,8,128]{2,1,0:T(8,128)S(1)} collective-permute-done((f32[76,8,128]{2,1,0:T(8,128)S(1)}, f32[76,8,128]{2,1,0:T(8,128)S(1)}, u32[]{:S(2)}, u32[]{:S(2)}) %collective-permute-start) | collective-permute-done | bytes 311328 | tf_op jit(solution)/shard_map/ppermute | solution.py:276
  17.2 7.1 %collective-permute-done.1.refs_2_ = f32[76,8,128]{2,1,0:T(8,128)S(1)} collective-permute-done((f32[76,8,128]{2,1,0:T(8,128)S(1)}, f32[76,8,128]{2,1,0:T(8,128)S(1)}, u32[]{:S(2)}, u32[]{:S(2)}) %collective-permute-start.1) | collective-permute-done | bytes 311328 | tf_op jit(solution)/shard_map/ppermute | solution.py:276
  26.0 2.1 %collective-permute-start.4 = (f32[76,8,128]{2,1,0:T(8,128)S(1)}, f32[76,8,128]{2,1,0:T(8,128)S(1)}, u32[]{:S(2)}, u32[]{:S(2)}) collective-permute-start(f32[76,8,128]{2,1,0:T(8,128)S(1)} %pad_maximum_fusion.1), channel_id=1, source_target_pairs={{0,2},{1,3},{2,0},{3,1},{4,6},{5,7},{6,4},{7,5},{8,10},{9,11},{10,... | collective-permute-start | bytes 933896 | tf_op jit(solution)/shard_map/ppermute | solution.py:276
  28.2 3.1 %collective-permute-done.3.refs_4_ = f32[76,8,128]{2,1,0:T(8,128)S(1)} collective-permute-done((f32[76,8,128]{2,1,0:T(8,128)S(1)}, f32[76,8,128]{2,1,0:T(8,128)S(1)}, u32[]{:S(2)}, u32[]{:S(2)}) %collective-permute-start.3) | collective-permute-done | bytes 311328 | tf_op jit(solution)/shard_map/ppermute | solution.py:276
  31.3 5.0 %collective-permute-done.4.refs_5_ = f32[76,8,128]{2,1,0:T(8,128)S(1)} collective-permute-done((f32[76,8,128]{2,1,0:T(8,128)S(1)}, f32[76,8,128]{2,1,0:T(8,128)S(1)}, u32[]{:S(2)}, u32[]{:S(2)}) %collective-permute-start.4) | collective-permute-done | bytes 311328 | tf_op jit(solution)/shard_map/ppermute | solution.py:276
  36.3 3.5 %shard_map.75 = (s32[128]{0:T(128)S(1)}, s32[128]{0:T(128)S(1)}, f32[128]{0:T(128)S(1)}, f32[128,2,8,128]{3,2,1,0:T(8,128)S(1)}, f32[32,8,128]{2,1,0:T(8,128)S(1)}, /*index=5*/f32[17,8,128]{2,1,0:T(8,128)S(1)}) custom-call(bf16[2048,2048]{1,0:T(8,128)(2,1)S(1)} %shard_map.74.block, f32[76,8,128]{2,1,0:T(8,128)S(1)} %get-tuple-element.63.refs_0_, ...), custom_call_target="tpu_custom_call" | custom-call | tf_op jit(solution)/shard_map/pallas_call | solution.py:341
  41.3 2.8 %collective-permute-start.9 = (f32[17,8,128]{2,1,0:T(8,128)S(1)}, f32[17,8,128]{2,1,0:T(8,128)S(1)}, u32[]{:S(2)}, u32[]{:S(2)}) collective-permute-start(f32[17,8,128]{2,1,0:T(8,128)S(1)} %pad_maximum_fusion.3), channel_id=1, source_target_pairs={{0,12},{1,13},{2,14},{3,15},{4,8},{5,9},{6,10},{7,11},{8,4},{9,5},... | collective-permute-start | bytes 208904 | tf_op jit(solution)/shard_map/ppermute | solution.py:272
  44.1 12.5 %collective-permute-start.8 = (f32[17,8,128]{2,1,0:T(8,128)S(1)}, f32[17,8,128]{2,1,0:T(8,128)S(1)}, u32[]{:S(2)}, u32[]{:S(2)}) collective-permute-start(f32[17,8,128]{2,1,0:T(8,128)S(1)} %pad_maximum_fusion.3), channel_id=1, source_target_pairs={{0,8},{1,9},{2,10},{3,11},{4,12},{5,13},{6,14},{7,15},{8,0},{9,1},... | collective-permute-start | bytes 208904 | tf_op jit(solution)/shard_map/ppermute | solution.py:272
  57.1 4.7 %collective-permute-done.7 = f32[17,8,128]{2,1,0:T(8,128)S(1)} collective-permute-done((f32[17,8,128]{2,1,0:T(8,128)S(1)}, f32[17,8,128]{2,1,0:T(8,128)S(1)}, u32[]{:S(2)}, u32[]{:S(2)}) %collective-permute-start.7) | collective-permute-done | bytes 69664 | tf_op jit(solution)/shard_map/ppermute | solution.py:272
  62.9 5.6 %collective-permute-done.10 = f32[68,8,128]{2,1,0:T(8,128)S(1)} collective-permute-done((f32[68,8,128]{2,1,0:T(8,128)S(1)}, f32[68,8,128]{2,1,0:T(8,128)S(1)}, u32[]{:S(2)}, u32[]{:S(2)}) %collective-permute-start.10) | collective-permute-done | bytes 278560 | tf_op jit(solution)/shard_map/ppermute | solution.py:276
  68.5 1.6 %collective-permute-start.11 = (f32[136,8,128]{2,1,0:T(8,128)S(1)}, f32[136,8,128]{2,1,0:T(8,128)S(1)}, u32[]{:S(2)}, u32[]{:S(2)}) collective-permute-start(f32[136,8,128]{2,1,0:T(8,128)S(1)} %constant_dynamic-update-slice_fusion.5.near), channel_id=1, source_target_pairs={{0,2},{1,3},{2,0},{3,1},{4,6},{5,7},{6,4},{7,5},{8,10},{9,11},{10,... | collective-permute-start | bytes 1671176 | tf_op jit(solution)/shard_map/ppermute | solution.py:276
  70.1 8.0 %collective-permute-done.11.far = f32[136,8,128]{2,1,0:T(8,128)S(1)} collective-permute-done((f32[136,8,128]{2,1,0:T(8,128)S(1)}, f32[136,8,128]{2,1,0:T(8,128)S(1)}, u32[]{:S(2)}, u32[]{:S(2)}) %collective-permute-start.11) | collective-permute-done | bytes 557088 | tf_op jit(solution)/shard_map/ppermute | solution.py:276
  78.1 3.0 %shard_map.76 = (f32[128,2,8,128]{3,2,1,0:T(8,128)S(1)}, f32[128,2,8,128]{3,2,1,0:T(8,128)S(1)}, f32[17,8,128]{2,1,0:T(8,128)S(1)}, f32[64,2,8,128]{3,2,1,0:T(8,128)S(1)}, f32[8,128]{1,0:T(8,128)S(1)}) custom-call(s32[128]{0:T(128)S(1)} %get-tuple-element.67.place, s32[128]{0:T(128)S(1)} %get-tuple-element.68.away, f32[128]{0:T(128)S(1)} %get-tuple-element.69.keep, ...), custom_call_target="tpu_custom_call" | custom-call | tf_op jit(solution)/shard_map/pallas_call | solution.py:26
  82.4 3.1 %collective-permute-start.15 = (f32[17,8,128]{2,1,0:T(8,128)S(1)}, f32[17,8,128]{2,1,0:T(8,128)S(1)}, u32[]{:S(2)}, u32[]{:S(2)}) collective-permute-start(f32[17,8,128]{2,1,0:T(8,128)S(1)} %pad_maximum_fusion.4), channel_id=1, source_target_pairs={{0,12},{1,13},{2,14},{3,15},{4,8},{5,9},{6,10},{7,11},{8,4},{9,5},... | collective-permute-start | bytes 208904 | tf_op jit(solution)/shard_map/ppermute | solution.py:272
  86.9 3.4 %collective-permute-done.13 = f32[17,8,128]{2,1,0:T(8,128)S(1)} collective-permute-done((f32[17,8,128]{2,1,0:T(8,128)S(1)}, f32[17,8,128]{2,1,0:T(8,128)S(1)}, u32[]{:S(2)}, u32[]{:S(2)}) %collective-permute-start.13) | collective-permute-done | bytes 69664 | tf_op jit(solution)/shard_map/ppermute | solution.py:272
  92.6 5.8 %collective-permute-done.16 = f32[68,8,128]{2,1,0:T(8,128)S(1)} collective-permute-done((f32[68,8,128]{2,1,0:T(8,128)S(1)}, f32[68,8,128]{2,1,0:T(8,128)S(1)}, u32[]{:S(2)}, u32[]{:S(2)}) %collective-permute-start.16) | collective-permute-done | bytes 278560 | tf_op jit(solution)/shard_map/ppermute | solution.py:276
  99.9 1.9 %collective-permute-done.18.theirs = f32[64,2,8,128]{3,2,1,0:T(8,128)S(1)} collective-permute-done((f32[64,2,8,128]{3,2,1,0:T(8,128)S(1)}, f32[64,2,8,128]{3,2,1,0:T(8,128)S(1)}, u32[]{:S(2)}, u32[]{:S(2)}) %collective-permute-start.18) | collective-permute-done | bytes 524320 | tf_op jit(solution)/shard_map/ppermute | solution.py:279
  102.7 5.2 %collective-permute-done.17.far = f32[136,8,128]{2,1,0:T(8,128)S(1)} collective-permute-done((f32[136,8,128]{2,1,0:T(8,128)S(1)}, f32[136,8,128]{2,1,0:T(8,128)S(1)}, u32[]{:S(2)}, u32[]{:S(2)}) %collective-permute-start.17) | collective-permute-done | bytes 557088 | tf_op jit(solution)/shard_map/ppermute | solution.py:276
  108.0 3.2 %shard_map.78 = (f32[128,2,8,128]{3,2,1,0:T(8,128)S(1)}, f32[128,2,8,128]{3,2,1,0:T(8,128)S(1)}, f32[17,8,128]{2,1,0:T(8,128)S(1)}, f32[64,2,8,128]{3,2,1,0:T(8,128)S(1)}, f32[8,128]{1,0:T(8,128)S(1)}) custom-call(s32[128]{0:T(128)S(1)} %get-tuple-element.67.place, s32[128]{0:T(128)S(1)} %get-tuple-element.68.away, f32[128]{0:T(128)S(1)} %get-tuple-element.69.keep, ...), custom_call_target="tpu_custom_call" | custom-call | tf_op jit(solution)/shard_map/pallas_call | solution.py:26
  112.4 2.6 %collective-permute-start.22 = (f32[17,8,128]{2,1,0:T(8,128)S(1)}, f32[17,8,128]{2,1,0:T(8,128)S(1)}, u32[]{:S(2)}, u32[]{:S(2)}) collective-permute-start(f32[17,8,128]{2,1,0:T(8,128)S(1)} %pad_maximum_fusion.5), channel_id=1, source_target_pairs={{0,12},{1,13},{2,14},{3,15},{4,8},{5,9},{6,10},{7,11},{8,4},{9,5},... | collective-permute-start | bytes 208904 | tf_op jit(solution)/shard_map/ppermute | solution.py:272
  115.1 1.8 %collective-permute-start.20 = (f32[17,8,128]{2,1,0:T(8,128)S(1)}, f32[17,8,128]{2,1,0:T(8,128)S(1)}, u32[]{:S(2)}, u32[]{:S(2)}) collective-permute-start(f32[17,8,128]{2,1,0:T(8,128)S(1)} %pad_maximum_fusion.5), channel_id=1, source_target_pairs={{0,4},{1,5},{2,6},{3,7},{4,0},{5,1},{6,2},{7,3},{8,12},{9,13},{10,... | collective-permute-start | bytes 208904 | tf_op jit(solution)/shard_map/ppermute | solution.py:272
  116.9 3.3 %collective-permute-done.20 = f32[17,8,128]{2,1,0:T(8,128)S(1)} collective-permute-done((f32[17,8,128]{2,1,0:T(8,128)S(1)}, f32[17,8,128]{2,1,0:T(8,128)S(1)}, u32[]{:S(2)}, u32[]{:S(2)}) %collective-permute-start.20) | collective-permute-done | bytes 69664 | tf_op jit(solution)/shard_map/ppermute | solution.py:272
  120.2 1.6 %collective-permute-done.21 = f32[17,8,128]{2,1,0:T(8,128)S(1)} collective-permute-done((f32[17,8,128]{2,1,0:T(8,128)S(1)}, f32[17,8,128]{2,1,0:T(8,128)S(1)}, u32[]{:S(2)}, u32[]{:S(2)}) %collective-permute-start.21) | collective-permute-done | bytes 69664 | tf_op jit(solution)/shard_map/ppermute | solution.py:272
  122.7 5.8 %collective-permute-done.23 = f32[68,8,128]{2,1,0:T(8,128)S(1)} collective-permute-done((f32[68,8,128]{2,1,0:T(8,128)S(1)}, f32[68,8,128]{2,1,0:T(8,128)S(1)}, u32[]{:S(2)}, u32[]{:S(2)}) %collective-permute-start.23) | collective-permute-done | bytes 278560 | tf_op jit(solution)/shard_map/ppermute | solution.py:276
  130.1 1.9 %collective-permute-done.25.theirs = f32[64,2,8,128]{3,2,1,0:T(8,128)S(1)} collective-permute-done((f32[64,2,8,128]{3,2,1,0:T(8,128)S(1)}, f32[64,2,8,128]{3,2,1,0:T(8,128)S(1)}, u32[]{:S(2)}, u32[]{:S(2)}) %collective-permute-start.25) | collective-permute-done | bytes 524320 | tf_op jit(solution)/shard_map/ppermute | solution.py:279
  133.0 5.1 %collective-permute-done.24.far = f32[136,8,128]{2,1,0:T(8,128)S(1)} collective-permute-done((f32[136,8,128]{2,1,0:T(8,128)S(1)}, f32[136,8,128]{2,1,0:T(8,128)S(1)}, u32[]{:S(2)}, u32[]{:S(2)}) %collective-permute-start.24) | collective-permute-done | bytes 557088 | tf_op jit(solution)/shard_map/ppermute | solution.py:276
  138.2 3.2 %shard_map.80 = (f32[32,8,128]{2,1,0:T(8,128)S(1)}, f32[64,2,8,128]{3,2,1,0:T(8,128)S(1)}, f32[8,128]{1,0:T(8,128)S(1)}) custom-call(s32[128]{0:T(128)S(1)} %get-tuple-element.67.place, s32[128]{0:T(128)S(1)} %get-tuple-element.68.away, f32[128]{0:T(128)S(1)} %get-tuple-element.69.keep, s32[64]{0:T(128)S(1)} %get-tuple-element.70.picked, ...), custom_call_target="tpu_custom_call" | custom-call | tf_op jit(solution)/shard_map/pallas_call | solution.py:26
  141.4 11.1 %all_to_all.5.sums = f32[32,8,128]{2,1,0:T(8,128)S(1)} all-to-all(f32[32,8,128]{2,1,0:T(8,128)S(1)} %get-tuple-element.102), channel_id=1, replica_groups=mesh['body'=2,'sub'=16] {'body','sub'}, dimensions={0} | all-to-all | bytes 262144 | tf_op jit(solution)/shard_map/all_to_all | solution.py:401
  152.5 2.1 %shard_map.81 = f32[8,64,256]{2,1,0:T(8,128)} custom-call(f32[64]{0:T(128)S(1)} %get-tuple-element.161.keep, f32[32,8,128]{2,1,0:T(8,128)S(1)} %all_to_all.5.sums, f32[8,128]{1,0:T(8,128)S(1)} %get-tuple-element.103.known, f32[64,256]{1,0:T(8,128)S(1)} %copy-done, f32[64,2,8,128]{3,2,1,0:T(8,128)S(1)} %get-tuple-element.104.mine, ...), custom_call_target="tpu_custom_call" | custom-call | tf_op jit(solution)/shard_map/pallas_call | solution.py:26
  (80 shorter events, 23.3 us)
Async XLA Ops:
  6.2 10.9 %collective-permute-start = (f32[76,8,128]{2,1,0:T(8,128)S(1)}, f32[76,8,128]{2,1,0:T(8,128)S(1)}, u32[]{:S(2)}, u32[]{:S(2)}) collective-permute-start(f32[76,8,128]{2,1,0:T(8,128)S(1)} %get-tuple-element.59), channel_id=1, source_target_pairs={{0,4},{1,5},{2,6},{3,7},{4,0},{5,1},{6,2},{7,3},{8,12},{9,13},{10,... | collective-permute-start | bytes 933896 | tf_op jit(solution)/shard_map/ppermute | solution.py:276
  9.3 14.9 %collective-permute-start.1 = (f32[76,8,128]{2,1,0:T(8,128)S(1)}, f32[76,8,128]{2,1,0:T(8,128)S(1)}, u32[]{:S(2)}, u32[]{:S(2)}) collective-permute-start(f32[76,8,128]{2,1,0:T(8,128)S(1)} %get-tuple-element.60), channel_id=1, source_target_pairs={{0,8},{1,9},{2,10},{3,11},{4,12},{5,13},{6,14},{7,15},{8,0},{9,1},... | collective-permute-start | bytes 933896 | tf_op jit(solution)/shard_map/ppermute | solution.py:276
  11.9 12.3 %collective-permute-start.2 = (f32[76,8,128]{2,1,0:T(8,128)S(1)}, f32[76,8,128]{2,1,0:T(8,128)S(1)}, u32[]{:S(2)}, u32[]{:S(2)}) collective-permute-start(f32[76,8,128]{2,1,0:T(8,128)S(1)} %get-tuple-element.61), channel_id=1, source_target_pairs={{0,12},{1,13},{2,14},{3,15},{4,8},{5,9},{6,10},{7,11},{8,4},{9,5},... | collective-permute-start | bytes 933896 | tf_op jit(solution)/shard_map/ppermute | solution.py:276
  24.3 7.0 %collective-permute-start.3 = (f32[76,8,128]{2,1,0:T(8,128)S(1)}, f32[76,8,128]{2,1,0:T(8,128)S(1)}, u32[]{:S(2)}, u32[]{:S(2)}) collective-permute-start(f32[76,8,128]{2,1,0:T(8,128)S(1)} %pad_maximum_fusion), channel_id=1, source_target_pairs={{0,1},{1,0},{2,3},{3,2},{4,5},{5,4},{6,7},{7,6},{8,9},{9,8},{10,11... | collective-permute-start | bytes 933896 | tf_op jit(solution)/shard_map/ppermute | solution.py:276
  26.0 10.3 %collective-permute-start.4 = (f32[76,8,128]{2,1,0:T(8,128)S(1)}, f32[76,8,128]{2,1,0:T(8,128)S(1)}, u32[]{:S(2)}, u32[]{:S(2)}) collective-permute-start(f32[76,8,128]{2,1,0:T(8,128)S(1)} %pad_maximum_fusion.1), channel_id=1, source_target_pairs={{0,2},{1,3},{2,0},{3,1},{4,6},{5,7},{6,4},{7,5},{8,10},{9,11},{10,... | collective-permute-start | bytes 933896 | tf_op jit(solution)/shard_map/ppermute | solution.py:276
  28.1 8.2 %collective-permute-start.5 = (f32[76,8,128]{2,1,0:T(8,128)S(1)}, f32[76,8,128]{2,1,0:T(8,128)S(1)}, u32[]{:S(2)}, u32[]{:S(2)}) collective-permute-start(f32[76,8,128]{2,1,0:T(8,128)S(1)} %pad_maximum_fusion.2), channel_id=1, source_target_pairs={{0,3},{1,2},{2,1},{3,0},{4,7},{5,6},{6,5},{7,4},{8,11},{9,10},{10,... | collective-permute-start | bytes 933896 | tf_op jit(solution)/shard_map/ppermute | solution.py:276
  39.8 62.1 %copy-start = (f32[64,256]{1,0:T(8,128)S(1)}, f32[64,256]{1,0:T(8,128)}, u32[]{:S(2)}) copy-start(f32[64,256]{1,0:T(8,128)} %comp.5) | copy-start | bytes 196612
  39.8 1.5 collective-permute-start.6
  41.3 20.5 %collective-permute-start.9 = (f32[17,8,128]{2,1,0:T(8,128)S(1)}, f32[17,8,128]{2,1,0:T(8,128)S(1)}, u32[]{:S(2)}, u32[]{:S(2)}) collective-permute-start(f32[17,8,128]{2,1,0:T(8,128)S(1)} %pad_maximum_fusion.3), channel_id=1, source_target_pairs={{0,12},{1,13},{2,14},{3,15},{4,8},{5,9},{6,10},{7,11},{8,4},{9,5},... | collective-permute-start | bytes 208904 | tf_op jit(solution)/shard_map/ppermute | solution.py:272
  44.1 17.7 %collective-permute-start.8 = (f32[17,8,128]{2,1,0:T(8,128)S(1)}, f32[17,8,128]{2,1,0:T(8,128)S(1)}, u32[]{:S(2)}, u32[]{:S(2)}) collective-permute-start(f32[17,8,128]{2,1,0:T(8,128)S(1)} %pad_maximum_fusion.3), channel_id=1, source_target_pairs={{0,8},{1,9},{2,10},{3,11},{4,12},{5,13},{6,14},{7,15},{8,0},{9,1},... | collective-permute-start | bytes 208904 | tf_op jit(solution)/shard_map/ppermute | solution.py:272
  56.6 5.2 %collective-permute-start.7 = (f32[17,8,128]{2,1,0:T(8,128)S(1)}, f32[17,8,128]{2,1,0:T(8,128)S(1)}, u32[]{:S(2)}, u32[]{:S(2)}) collective-permute-start(f32[17,8,128]{2,1,0:T(8,128)S(1)} %pad_maximum_fusion.3), channel_id=1, source_target_pairs={{0,4},{1,5},{2,6},{3,7},{4,0},{5,1},{6,2},{7,3},{8,12},{9,13},{10,... | collective-permute-start | bytes 208904 | tf_op jit(solution)/shard_map/ppermute | solution.py:272
  61.9 6.6 %collective-permute-start.10 = (f32[68,8,128]{2,1,0:T(8,128)S(1)}, f32[68,8,128]{2,1,0:T(8,128)S(1)}, u32[]{:S(2)}, u32[]{:S(2)}) collective-permute-start(f32[68,8,128]{2,1,0:T(8,128)S(1)} %get-tuple-element.147), channel_id=1, source_target_pairs={{0,1},{1,0},{2,3},{3,2},{4,5},{5,4},{6,7},{7,6},{8,9},{9,8},{10,11... | collective-permute-start | bytes 835592 | tf_op jit(solution)/shard_map/ppermute | solution.py:276
  68.5 9.6 %collective-permute-start.11 = (f32[136,8,128]{2,1,0:T(8,128)S(1)}, f32[136,8,128]{2,1,0:T(8,128)S(1)}, u32[]{:S(2)}, u32[]{:S(2)}) collective-permute-start(f32[136,8,128]{2,1,0:T(8,128)S(1)} %constant_dynamic-update-slice_fusion.5.near), channel_id=1, source_target_pairs={{0,2},{1,3},{2,0},{3,1},{4,6},{5,7},{6,4},{7,5},{8,10},{9,11},{10,... | collective-permute-start | bytes 1671176 | tf_op jit(solution)/shard_map/ppermute | solution.py:276
  81.1 1.3 collective-permute-start.12
  82.4 9.3 %collective-permute-start.15 = (f32[17,8,128]{2,1,0:T(8,128)S(1)}, f32[17,8,128]{2,1,0:T(8,128)S(1)}, u32[]{:S(2)}, u32[]{:S(2)}) collective-permute-start(f32[17,8,128]{2,1,0:T(8,128)S(1)} %pad_maximum_fusion.4), channel_id=1, source_target_pairs={{0,12},{1,13},{2,14},{3,15},{4,8},{5,9},{6,10},{7,11},{8,4},{9,5},... | collective-permute-start | bytes 208904 | tf_op jit(solution)/shard_map/ppermute | solution.py:272
  85.5 6.2 %collective-permute-start.14 = (f32[17,8,128]{2,1,0:T(8,128)S(1)}, f32[17,8,128]{2,1,0:T(8,128)S(1)}, u32[]{:S(2)}, u32[]{:S(2)}) collective-permute-start(f32[17,8,128]{2,1,0:T(8,128)S(1)} %pad_maximum_fusion.4), channel_id=1, source_target_pairs={{0,8},{1,9},{2,10},{3,11},{4,12},{5,13},{6,14},{7,15},{8,0},{9,1},... | collective-permute-start | bytes 208904 | tf_op jit(solution)/shard_map/ppermute | solution.py:272
  85.5 4.8 %collective-permute-start.13 = (f32[17,8,128]{2,1,0:T(8,128)S(1)}, f32[17,8,128]{2,1,0:T(8,128)S(1)}, u32[]{:S(2)}, u32[]{:S(2)}) collective-permute-start(f32[17,8,128]{2,1,0:T(8,128)S(1)} %pad_maximum_fusion.4), channel_id=1, source_target_pairs={{0,4},{1,5},{2,6},{3,7},{4,0},{5,1},{6,2},{7,3},{8,12},{9,13},{10,... | collective-permute-start | bytes 208904 | tf_op jit(solution)/shard_map/ppermute | solution.py:272
  91.7 6.6 %collective-permute-start.16 = (f32[68,8,128]{2,1,0:T(8,128)S(1)}, f32[68,8,128]{2,1,0:T(8,128)S(1)}, u32[]{:S(2)}, u32[]{:S(2)}) collective-permute-start(f32[68,8,128]{2,1,0:T(8,128)S(1)} %get-tuple-element.138), channel_id=1, source_target_pairs={{0,1},{1,0},{2,3},{3,2},{4,5},{5,4},{6,7},{7,6},{8,9},{9,8},{10,11... | collective-permute-start | bytes 835592 | tf_op jit(solution)/shard_map/ppermute | solution.py:276
  98.4 9.6 %collective-permute-start.17 = (f32[136,8,128]{2,1,0:T(8,128)S(1)}, f32[136,8,128]{2,1,0:T(8,128)S(1)}, u32[]{:S(2)}, u32[]{:S(2)}) collective-permute-start(f32[136,8,128]{2,1,0:T(8,128)S(1)} %constant_dynamic-update-slice_fusion.16.near), channel_id=1, source_target_pairs={{0,2},{1,3},{2,0},{3,1},{4,6},{5,7},{6,4},{7,5},{8,10},{9,11},{10,... | collective-permute-start | bytes 1671176 | tf_op jit(solution)/shard_map/ppermute | solution.py:276
  99.9 1.9 %collective-permute-start.18 = (f32[64,2,8,128]{3,2,1,0:T(8,128)S(1)}, f32[64,2,8,128]{3,2,1,0:T(8,128)S(1)}, u32[]{:S(2)}, u32[]{:S(2)}) collective-permute-start(f32[64,2,8,128]{3,2,1,0:T(8,128)S(1)} %get-tuple-element.78.mine), channel_id=1, source_target_pairs={{0,16},{16,0},{1,17},{17,1},{2,18},{18,2},{3,19},{19,3},{4,20},{20... | collective-permute-start | bytes 1572872 | tf_op jit(solution)/shard_map/ppermute | solution.py:279
  111.1 1.3 collective-permute-start.19
  112.4 9.5 %collective-permute-start.22 = (f32[17,8,128]{2,1,0:T(8,128)S(1)}, f32[17,8,128]{2,1,0:T(8,128)S(1)}, u32[]{:S(2)}, u32[]{:S(2)}) collective-permute-start(f32[17,8,128]{2,1,0:T(8,128)S(1)} %pad_maximum_fusion.5), channel_id=1, source_target_pairs={{0,12},{1,13},{2,14},{3,15},{4,8},{5,9},{6,10},{7,11},{8,4},{9,5},... | collective-permute-start | bytes 208904 | tf_op jit(solution)/shard_map/ppermute | solution.py:272
  115.0 6.9 %collective-permute-start.21 = (f32[17,8,128]{2,1,0:T(8,128)S(1)}, f32[17,8,128]{2,1,0:T(8,128)S(1)}, u32[]{:S(2)}, u32[]{:S(2)}) collective-permute-start(f32[17,8,128]{2,1,0:T(8,128)S(1)} %pad_maximum_fusion.5), channel_id=1, source_target_pairs={{0,8},{1,9},{2,10},{3,11},{4,12},{5,13},{6,14},{7,15},{8,0},{9,1},... | collective-permute-start | bytes 208904 | tf_op jit(solution)/shard_map/ppermute | solution.py:272
  115.1 5.1 %collective-permute-start.20 = (f32[17,8,128]{2,1,0:T(8,128)S(1)}, f32[17,8,128]{2,1,0:T(8,128)S(1)}, u32[]{:S(2)}, u32[]{:S(2)}) collective-permute-start(f32[17,8,128]{2,1,0:T(8,128)S(1)} %pad_maximum_fusion.5), channel_id=1, source_target_pairs={{0,4},{1,5},{2,6},{3,7},{4,0},{5,1},{6,2},{7,3},{8,12},{9,13},{10,... | collective-permute-start | bytes 208904 | tf_op jit(solution)/shard_map/ppermute | solution.py:272
  121.9 6.6 %collective-permute-start.23 = (f32[68,8,128]{2,1,0:T(8,128)S(1)}, f32[68,8,128]{2,1,0:T(8,128)S(1)}, u32[]{:S(2)}, u32[]{:S(2)}) collective-permute-start(f32[68,8,128]{2,1,0:T(8,128)S(1)} %get-tuple-element.129), channel_id=1, source_target_pairs={{0,1},{1,0},{2,3},{3,2},{4,5},{5,4},{6,7},{7,6},{8,9},{9,8},{10,11... | collective-permute-start | bytes 835592 | tf_op jit(solution)/shard_map/ppermute | solution.py:276
  128.6 9.6 %collective-permute-start.24 = (f32[136,8,128]{2,1,0:T(8,128)S(1)}, f32[136,8,128]{2,1,0:T(8,128)S(1)}, u32[]{:S(2)}, u32[]{:S(2)}) collective-permute-start(f32[136,8,128]{2,1,0:T(8,128)S(1)} %constant_dynamic-update-slice_fusion.27.near), channel_id=1, source_target_pairs={{0,2},{1,3},{2,0},{3,1},{4,6},{5,7},{6,4},{7,5},{8,10},{9,11},{10,... | collective-permute-start | bytes 1671176 | tf_op jit(solution)/shard_map/ppermute | solution.py:276
  130.1 1.9 %collective-permute-start.25 = (f32[64,2,8,128]{3,2,1,0:T(8,128)S(1)}, f32[64,2,8,128]{3,2,1,0:T(8,128)S(1)}, u32[]{:S(2)}, u32[]{:S(2)}) collective-permute-start(f32[64,2,8,128]{3,2,1,0:T(8,128)S(1)} %get-tuple-element.90.mine), channel_id=1, source_target_pairs={{0,16},{16,0},{1,17},{17,1},{2,18},{18,2},{3,19},{19,3},{4,20},{20... | collective-permute-start | bytes 1572872 | tf_op jit(solution)/shard_map/ppermute | solution.py:279
  141.3 11.2 %collective-permute-start.26 = (f32[64,2,8,128]{3,2,1,0:T(8,128)S(1)}, f32[64,2,8,128]{3,2,1,0:T(8,128)S(1)}, u32[]{:S(2)}, u32[]{:S(2)}) collective-permute-start(f32[64,2,8,128]{3,2,1,0:T(8,128)S(1)} %get-tuple-element.104.mine), channel_id=1, source_target_pairs={{0,16},{16,0},{1,17},{17,1},{2,18},{18,2},{3,19},{19,3},{4,20},{20... | collective-permute-start | bytes 1572872 | tf_op jit(solution)/shard_map/ppermute | solution.py:279

commit v13 on v12

--- a/solution.py
+++ b/solution.py
@@ -145,7 +145,7 @@
     return gamma, gamma / (delta - beta * gamma / known[:, 1:2]), beta
 
 
-def home_kernel(first, last, nh, room, lines, place, away, keep, picked, comp, own, near, far, known, block, *refs):
+def home_kernel(first, last, nh, room, lines, place, away, keep, picked, comp, own, near_a, far_a, near_b, far_b, known, block, *refs):
     r_in, *refs = refs
     if not first:
         s_in, *refs = refs
@@ -154,11 +154,12 @@
     answer, part, known_out, load, resp = refs
     load[...] = jnp.zeros_like(load)
     nrow, _, ncase, width = r_in.shape
-    size, each = near.shape[0], own.shape[0]
-    resp[:size], resp[size:] = near[...], far[...]
-    shares = [[part[i + each - 1] for i in range(0, size, each)] for part in (near, far)]
-    (one, two), (three, four) = [[tree(part[: len(part) // 2]), tree(part[len(part) // 2 :])] for part in shares]
-    sums = (one + four) + (two + three)
+    at = 0
+    for piece in (near_a, far_a, near_b, far_b):
+        resp[at : at + piece.shape[0]] = piece[...]
+        at += piece.shape[0]
+    each = own.shape[0] // 2 + 1
+    sums = tree([piece[i + each - 1] for piece in (near_b, far_b) for i in range(0, piece.shape[0], each)])
     gamma, alpha, beta = steps(first, sums, known[...])
     lane = lax.broadcasted_iota(jnp.int32, (ncase, width), 1)
     known_out[...] = jnp.where(lane == 0, gamma, jnp.where(lane == 1, alpha, beta))
@@ -266,6 +267,7 @@
     deep = -(-room // SUBLANES)
     tiles = room * nh + lines + deep
     nz = nsub // 4
+    half = nslot // 2 * nh
     width = math.isqrt(nsub)
 
     def swap(value, far):
@@ -292,8 +294,9 @@
 
     def found(away):
         x_bit, y_bit, z_part = away & 1, (away >> 1) & 1, away >> 2
-        plane = jnp.where(side == 0, y_bit * 2 + x_bit, x_bit * 2 + y_bit)
-        return (plane * nz + z_part) * per + other_slot * nh
+        found_a = ((y_bit * 2 + x_bit) * nz + z_part) * half + other_slot * nh
+        found_b = ((x_bit * 2 + y_bit) * nz + z_part) * (half + 1) + (other_slot - nslot // 2) * nh
+        return jnp.where(other_slot < nslot // 2, found_a, nsub * half + found_b)
 
     facts = jnp.stack([slot * nh, found(owner ^ other)], axis=1).astype(jnp.float32)
     facts = jnp.concatenate([facts, keep[:, None]], axis=1)
@@ -329,8 +332,9 @@
         cost=pl.CostEstimate(flops=0, bytes_accessed=4 * block.size, transcendentals=0),
     )
     near_parts, block = lax.optimization_barrier((near_parts, block))
+    signal = sibling(near_parts[width - 1][:1])
     far_parts = [
-        cross(jnp.concatenate([part[k * tiles : (k + 1) * tiles] for part in near_parts]), k, k * width)
+        cross(jnp.concatenate([part[k * tiles : (k + 1) * tiles] for part in near_parts] + [signal]), k, k * width)
         for k in range(1, width)
     ]
 
@@ -376,23 +380,27 @@
             lists = update(step - 1, lists, known, part)
         spread_out = jnp.concatenate([spread_out[: per - 1], own[per - 1 :] + spread_out[per - 1 :]])
         parts = [spread_out] + [swap(spread_out, 4 * z) for z in range(1, nz)]
-        close = jnp.concatenate(parts)
-        close = jnp.concatenate([close, cross(close, 1, 2)])
-        apart = cross(close, 2, 1)
+        a = jnp.concatenate([part[:half] for part in parts])
+        b = jnp.concatenate([part[half:] for part in parts])
+        far_a, far_b = swap(a, 1), swap(b, 2)
+        a, b = jnp.concatenate([a, far_a]), jnp.concatenate([b, far_b])
+        far_a, far_b = swap(a, 2), swap(b, 1)
         if step > 0:
-            apart, lists = lax.optimization_barrier((apart, lists))
+            far_a, far_b, lists = lax.optimization_barrier((far_a, far_b, lists))
         *state, own, part, known = call(
             functools.partial(home_kernel, step == 0, last, nh, room, lines),
             (field,) * (0 if last else 2) + (f32(nbody * nsub, ncase, LANES) if last else answer, f32(npatch, nh, ncase, LANES), f32(ncase, LANES)),
-            [SMEM] * 4 + [VMEM] * (6 + len(state)),
+            [SMEM] * 4 + [VMEM] * (8 + len(state)),
             near,
             far,
             on,
             picked,
             comp,
             own,
-            close,
-            apart,
+            a,
+            far_a,
+            b,
+            far_b,
             known,
             block,
             *state,

time: 155 us -> 147 us (0.948)
  waiting for transfers between devices: 74.2 us -> 63.7 us
  blocking collectives: 11.1 us -> 12.8 us
    ppermute x12 -> x6, waiting for transfers between devices: 52.5 us -> 16.8 us  [cross(): return lax.ppermute(value, ('body', 'sub'), pairs)]
    ppermute x9 -> x21, waiting for transfers between devices: 14.5 us -> 42.5 us  [swap(): return lax.ppermute(value, 'sub', [(i, i ^ far) for i in range(nsub)])]
    ppermute x12 -> x6, starting transfers between devices: 16.9 us -> 9.17 us  [cross(): return lax.ppermute(value, ('body', 'sub'), pairs)]
    ppermute x6 -> x7, starting transfers between devices: 0.68 us -> 5.71 us  [sibling(): lax.ppermute(value, 'body', [(i, nbody - 1 - i) for i in range(nbody)])]
    ppermute x9 -> x21, starting transfers between devices: 24.7 us -> 28.6 us  [swap(): return lax.ppermute(value, 'sub', [(i, i ^ far) for i in range(nsub)])]
    ppermute x6 -> x7, waiting for transfers between devices: 7.24 us -> 4.5 us  [sibling(): lax.ppermute(value, 'body', [(i, nbody - 1 - i) for i in range(nbody)])]
    all_to_all x1, blocking collectives: 11.1 us -> 12.8 us  [on_device(): lax.all_to_all(own, ('body', 'sub'), split_axis=0, concat_axis=0, tiled=T...]
  transfers between devices with their start and end apart: 27 -> 34, of which waited for: 20 -> 22; matrix products, arithmetic and copies ran while one was open for 0% -> 0% of each run, Pallas kernels for 3% -> 4%
where the time goes in v13:
time: 147 us
  waiting for transfers between devices  63.7 us (43%)
  starting transfers between devices  43.5 us (30%)
  Pallas kernels  21 us (14%)
  blocking collectives  12.8 us (9%)
  other arithmetic  3.7 us (3%)
    ppermute x21, waiting for transfers between devices, swap(): return lax.ppermute(value, 'sub', [(i, i ^ far) for i in range(nsub)])  42.5 us
    ppermute x21, starting transfers between devices, swap(): return lax.ppermute(value, 'sub', [(i, i ^ far) for i in range(nsub)])  28.6 us
    pallas_call x8, Pallas kernels, call(): pl.pallas_call(kernel, out_shape=tuple(out_shape) if several else out_sha...  17.5 us
    ppermute x6, waiting for transfers between devices, cross(): return lax.ppermute(value, ('body', 'sub'), pairs)  16.8 us
    all_to_all x1, blocking collectives, on_device(): lax.all_to_all(own, ('body', 'sub'), split_axis=0, concat_axis=0, tiled=T...  12.8 us
    ppermute x6, starting transfers between devices, cross(): return lax.ppermute(value, ('body', 'sub'), pairs)  9.17 us
    ppermute x7, starting transfers between devices, sibling(): lax.ppermute(value, 'body', [(i, nbody - 1 - i) for i in range(nbody)])  5.71 us
    ppermute x7, waiting for transfers between devices, sibling(): lax.ppermute(value, 'body', [(i, nbody - 1 - i) for i in range(nbody)])  4.5 us
  transfers between devices with their start and end apart: 34, of which 22 were waited for; matrix products, arithmetic and copies ran while one was open for 0% of the time, Pallas kernels for 4%

profile of v13, /device:TPU:0, one launch (start us, length us, event | category | flops | bytes accessed | tf_op | source)
XLA Modules:
  0.0 147.2 jit_solution(18371097048790399524)
XLA Ops:
  6.2 3.1 %collective-permute-start = (f32[76,8,128]{2,1,0:T(8,128)S(1)}, f32[76,8,128]{2,1,0:T(8,128)S(1)}, u32[]{:S(2)}, u32[]{:S(2)}) collective-permute-start(f32[76,8,128]{2,1,0:T(8,128)S(1)} %get-tuple-element.61), channel_id=1, source_target_pairs={{0,4},{1,5},{2,6},{3,7},{4,0},{5,1},{6,2},{7,3},{8,12},{9,13},{10,... | collective-permute-start | bytes 933896 | tf_op jit(solution)/shard_map/ppermute | solution.py:278
  9.3 2.6 %collective-permute-start.1 = (f32[76,8,128]{2,1,0:T(8,128)S(1)}, f32[76,8,128]{2,1,0:T(8,128)S(1)}, u32[]{:S(2)}, u32[]{:S(2)}) collective-permute-start(f32[76,8,128]{2,1,0:T(8,128)S(1)} %get-tuple-element.62), channel_id=1, source_target_pairs={{0,8},{1,9},{2,10},{3,11},{4,12},{5,13},{6,14},{7,15},{8,0},{9,1},... | collective-permute-start | bytes 933896 | tf_op jit(solution)/shard_map/ppermute | solution.py:278
  11.9 3.5 %shard_map.74.block = bf16[2048,2048]{1,0:T(8,128)(2,1)S(1)} custom-call(bf16[2048,2048]{1,0:T(8,128)(2,1)} %bitcast.56), custom_call_target="tpu_custom_call" | custom-call | bytes 16777216 | tf_op jit(solution)/shard_map/pallas_call | solution.py:26
  15.4 1.7 %collective-permute-done.refs_1_ = f32[76,8,128]{2,1,0:T(8,128)S(1)} collective-permute-done((f32[76,8,128]{2,1,0:T(8,128)S(1)}, f32[76,8,128]{2,1,0:T(8,128)S(1)}, u32[]{:S(2)}, u32[]{:S(2)}) %collective-permute-start) | collective-permute-done | bytes 311328 | tf_op jit(solution)/shard_map/ppermute | solution.py:278
  17.2 6.7 %collective-permute-done.1.refs_2_ = f32[76,8,128]{2,1,0:T(8,128)S(1)} collective-permute-done((f32[76,8,128]{2,1,0:T(8,128)S(1)}, f32[76,8,128]{2,1,0:T(8,128)S(1)}, u32[]{:S(2)}, u32[]{:S(2)}) %collective-permute-start.1) | collective-permute-done | bytes 311328 | tf_op jit(solution)/shard_map/ppermute | solution.py:278
  25.1 1.5 %collective-permute-start.4 = (f32[77,8,128]{2,1,0:T(8,128)S(1)}, f32[77,8,128]{2,1,0:T(8,128)S(1)}, u32[]{:S(2)}, u32[]{:S(2)}) collective-permute-start(f32[77,8,128]{2,1,0:T(8,128)S(1)} %get-tuple-element.179), channel_id=1, source_target_pairs={{0,1},{1,0},{2,3},{3,2},{4,5},{5,4},{6,7},{7,6},{8,9},{9,8},{10,11... | collective-permute-start | bytes 946184 | tf_op jit(solution)/shard_map/ppermute | solution.py:278
  26.6 1.5 %collective-permute-start.5 = (f32[77,8,128]{2,1,0:T(8,128)S(1)}, f32[77,8,128]{2,1,0:T(8,128)S(1)}, u32[]{:S(2)}, u32[]{:S(2)}) collective-permute-start(f32[77,8,128]{2,1,0:T(8,128)S(1)} %get-tuple-element.178), channel_id=1, source_target_pairs={{0,2},{1,3},{2,0},{3,1},{4,6},{5,7},{6,4},{7,5},{8,10},{9,11},{10,... | collective-permute-start | bytes 946184 | tf_op jit(solution)/shard_map/ppermute | solution.py:278
  28.6 3.5 %collective-permute-done.4.refs_4_ = f32[77,8,128]{2,1,0:T(8,128)S(1)} collective-permute-done((f32[77,8,128]{2,1,0:T(8,128)S(1)}, f32[77,8,128]{2,1,0:T(8,128)S(1)}, u32[]{:S(2)}, u32[]{:S(2)}) %collective-permute-start.4) | collective-permute-done | bytes 315424 | tf_op jit(solution)/shard_map/ppermute | solution.py:278
  32.1 4.9 %collective-permute-done.5.refs_5_ = f32[77,8,128]{2,1,0:T(8,128)S(1)} collective-permute-done((f32[77,8,128]{2,1,0:T(8,128)S(1)}, f32[77,8,128]{2,1,0:T(8,128)S(1)}, u32[]{:S(2)}, u32[]{:S(2)}) %collective-permute-start.5) | collective-permute-done | bytes 315424 | tf_op jit(solution)/shard_map/ppermute | solution.py:278
  36.9 3.5 %shard_map.75 = (s32[128]{0:T(128)S(1)}, s32[128]{0:T(128)S(1)}, f32[128]{0:T(128)S(1)}, f32[128,2,8,128]{3,2,1,0:T(8,128)S(1)}, f32[32,8,128]{2,1,0:T(8,128)S(1)}, /*index=5*/f32[17,8,128]{2,1,0:T(8,128)S(1)}) custom-call(bf16[2048,2048]{1,0:T(8,128)(2,1)S(1)} %shard_map.74.block, f32[76,8,128]{2,1,0:T(8,128)S(1)} %get-tuple-element.65.refs_0_, ...), custom_call_target="tpu_custom_call" | custom-call | tf_op jit(solution)/shard_map/pallas_call | solution.py:345
  40.4 5.5 %collective-permute-start.7 = (f32[17,8,128]{2,1,0:T(8,128)S(1)}, f32[17,8,128]{2,1,0:T(8,128)S(1)}, u32[]{:S(2)}, u32[]{:S(2)}) collective-permute-start(f32[17,8,128]{2,1,0:T(8,128)S(1)} %get-tuple-element.74.own), channel_id=1, source_target_pairs={{0,16},{16,0},{1,17},{17,1},{2,18},{18,2},{3,19},{19,3},{4,20},{20... | collective-permute-start | bytes 208904 | tf_op jit(solution)/shard_map/ppermute | solution.py:281
  46.9 4.0 %collective-permute-start.8 = (f32[17,8,128]{2,1,0:T(8,128)S(1)}, f32[17,8,128]{2,1,0:T(8,128)S(1)}, u32[]{:S(2)}, u32[]{:S(2)}) collective-permute-start(f32[17,8,128]{2,1,0:T(8,128)S(1)} %pad_maximum_fusion.6), channel_id=1, source_target_pairs={{0,4},{1,5},{2,6},{3,7},{4,0},{5,1},{6,2},{7,3},{8,12},{9,13},{10,... | collective-permute-start | bytes 208904 | tf_op jit(solution)/shard_map/ppermute | solution.py:274
  53.6 6.0 %collective-permute-done.9 = f32[17,8,128]{2,1,0:T(8,128)S(1)} collective-permute-done((f32[17,8,128]{2,1,0:T(8,128)S(1)}, f32[17,8,128]{2,1,0:T(8,128)S(1)}, u32[]{:S(2)}, u32[]{:S(2)}) %collective-permute-start.9) | collective-permute-done | bytes 69664 | tf_op jit(solution)/shard_map/ppermute | solution.py:274
  59.6 1.6 %collective-permute-start.13 = (f32[36,8,128]{2,1,0:T(8,128)S(1)}, f32[36,8,128]{2,1,0:T(8,128)S(1)}, u32[]{:S(2)}, u32[]{:S(2)}) collective-permute-start(f32[36,8,128]{2,1,0:T(8,128)S(1)} %pad_maximum_fusion), channel_id=1, source_target_pairs={{0,2},{1,3},{2,0},{3,1},{4,6},{5,7},{6,4},{7,5},{8,10},{9,11},{10,... | collective-permute-start | bytes 442376 | tf_op jit(solution)/shard_map/ppermute | solution.py:274
  61.2 1.6 %collective-permute-start.11 = (f32[32,8,128]{2,1,0:T(8,128)S(1)}, f32[32,8,128]{2,1,0:T(8,128)S(1)}, u32[]{:S(2)}, u32[]{:S(2)}) collective-permute-start(f32[32,8,128]{2,1,0:T(8,128)S(1)} %pad_maximum_fusion.3), channel_id=1, source_target_pairs={{0,1},{1,0},{2,3},{3,2},{4,5},{5,4},{6,7},{7,6},{8,9},{9,8},{10,11... | collective-permute-start | bytes 393224 | tf_op jit(solution)/shard_map/ppermute | solution.py:274
  62.8 2.0 %collective-permute-done.13 = f32[36,8,128]{2,1,0:T(8,128)S(1)} collective-permute-done((f32[36,8,128]{2,1,0:T(8,128)S(1)}, f32[36,8,128]{2,1,0:T(8,128)S(1)}, u32[]{:S(2)}, u32[]{:S(2)}) %collective-permute-start.13) | collective-permute-done | bytes 147488 | tf_op jit(solution)/shard_map/ppermute | solution.py:274
  64.8 1.6 %collective-permute-start.14 = (f32[72,8,128]{2,1,0:T(8,128)S(1)}, f32[72,8,128]{2,1,0:T(8,128)S(1)}, u32[]{:S(2)}, u32[]{:S(2)}) collective-permute-start(f32[72,8,128]{2,1,0:T(8,128)S(1)} %constant_dynamic-update-slice_fusion.20.near_b), channel_id=1, source_target_pairs={{0,1},{1,0},{2,3},{3,2},{4,5},{5,4},{6,7},{7,6},{8,9},{9,8},{10,11... | collective-permute-start | bytes 884744 | tf_op jit(solution)/shard_map/ppermute | solution.py:274
  68.0 5.9 %collective-permute-done.12.far_a = f32[64,8,128]{2,1,0:T(8,128)S(1)} collective-permute-done((f32[64,8,128]{2,1,0:T(8,128)S(1)}, f32[64,8,128]{2,1,0:T(8,128)S(1)}, u32[]{:S(2)}, u32[]{:S(2)}) %collective-permute-start.12) | collective-permute-done | bytes 262176 | tf_op jit(solution)/shard_map/ppermute | solution.py:274
  73.9 2.9 %shard_map.76 = (f32[128,2,8,128]{3,2,1,0:T(8,128)S(1)}, f32[128,2,8,128]{3,2,1,0:T(8,128)S(1)}, f32[17,8,128]{2,1,0:T(8,128)S(1)}, f32[64,2,8,128]{3,2,1,0:T(8,128)S(1)}, f32[8,128]{1,0:T(8,128)S(1)}) custom-call(s32[128]{0:T(128)S(1)} %get-tuple-element.69.place, s32[128]{0:T(128)S(1)} %get-tuple-element.70.away, f32[128]{0:T(128)S(1)} %get-tuple-element.71.keep, ...), custom_call_target="tpu_custom_call" | custom-call | tf_op jit(solution)/shard_map/pallas_call | solution.py:26
  80.4 2.2 %collective-permute-start.18 = (f32[17,8,128]{2,1,0:T(8,128)S(1)}, f32[17,8,128]{2,1,0:T(8,128)S(1)}, u32[]{:S(2)}, u32[]{:S(2)}) collective-permute-start(f32[17,8,128]{2,1,0:T(8,128)S(1)} %pad_maximum_fusion.7), channel_id=1, source_target_pairs={{0,12},{1,13},{2,14},{3,15},{4,8},{5,9},{6,10},{7,11},{8,4},{9,5},... | collective-permute-start | bytes 208904 | tf_op jit(solution)/shard_map/ppermute | solution.py:274
  82.7 5.0 %collective-permute-done.17 = f32[17,8,128]{2,1,0:T(8,128)S(1)} collective-permute-done((f32[17,8,128]{2,1,0:T(8,128)S(1)}, f32[17,8,128]{2,1,0:T(8,128)S(1)}, u32[]{:S(2)}, u32[]{:S(2)}) %collective-permute-start.17) | collective-permute-done | bytes 69664 | tf_op jit(solution)/shard_map/ppermute | solution.py:274
  90.3 2.6 %collective-permute-done.21 = f32[36,8,128]{2,1,0:T(8,128)S(1)} collective-permute-done((f32[36,8,128]{2,1,0:T(8,128)S(1)}, f32[36,8,128]{2,1,0:T(8,128)S(1)}, u32[]{:S(2)}, u32[]{:S(2)}) %collective-permute-start.21) | collective-permute-done | bytes 147488 | tf_op jit(solution)/shard_map/ppermute | solution.py:274
  92.9 1.4 collective-permute-start.22
  96.6 5.5 %collective-permute-done.20.far_a = f32[64,8,128]{2,1,0:T(8,128)S(1)} collective-permute-done((f32[64,8,128]{2,1,0:T(8,128)S(1)}, f32[64,8,128]{2,1,0:T(8,128)S(1)}, u32[]{:S(2)}, u32[]{:S(2)}) %collective-permute-start.20) | collective-permute-done | bytes 262176 | tf_op jit(solution)/shard_map/ppermute | solution.py:274
  102.0 3.1 %shard_map.78 = (f32[128,2,8,128]{3,2,1,0:T(8,128)S(1)}, f32[128,2,8,128]{3,2,1,0:T(8,128)S(1)}, f32[17,8,128]{2,1,0:T(8,128)S(1)}, f32[64,2,8,128]{3,2,1,0:T(8,128)S(1)}, f32[8,128]{1,0:T(8,128)S(1)}) custom-call(s32[128]{0:T(128)S(1)} %get-tuple-element.69.place, s32[128]{0:T(128)S(1)} %get-tuple-element.70.away, f32[128]{0:T(128)S(1)} %get-tuple-element.71.keep, ...), custom_call_target="tpu_custom_call" | custom-call | tf_op jit(solution)/shard_map/pallas_call | solution.py:26
  108.4 2.5 %collective-permute-start.27 = (f32[17,8,128]{2,1,0:T(8,128)S(1)}, f32[17,8,128]{2,1,0:T(8,128)S(1)}, u32[]{:S(2)}, u32[]{:S(2)}) collective-permute-start(f32[17,8,128]{2,1,0:T(8,128)S(1)} %pad_maximum_fusion.8), channel_id=1, source_target_pairs={{0,12},{1,13},{2,14},{3,15},{4,8},{5,9},{6,10},{7,11},{8,4},{9,5},... | collective-permute-start | bytes 208904 | tf_op jit(solution)/shard_map/ppermute | solution.py:274
  111.6 4.2 %collective-permute-done.26 = f32[17,8,128]{2,1,0:T(8,128)S(1)} collective-permute-done((f32[17,8,128]{2,1,0:T(8,128)S(1)}, f32[17,8,128]{2,1,0:T(8,128)S(1)}, u32[]{:S(2)}, u32[]{:S(2)}) %collective-permute-start.26) | collective-permute-done | bytes 69664 | tf_op jit(solution)/shard_map/ppermute | solution.py:274
  118.3 2.8 %collective-permute-done.30 = f32[36,8,128]{2,1,0:T(8,128)S(1)} collective-permute-done((f32[36,8,128]{2,1,0:T(8,128)S(1)}, f32[36,8,128]{2,1,0:T(8,128)S(1)}, u32[]{:S(2)}, u32[]{:S(2)}) %collective-permute-start.30) | collective-permute-done | bytes 147488 | tf_op jit(solution)/shard_map/ppermute | solution.py:274
  124.6 4.4 %collective-permute-done.29.far_a = f32[64,8,128]{2,1,0:T(8,128)S(1)} collective-permute-done((f32[64,8,128]{2,1,0:T(8,128)S(1)}, f32[64,8,128]{2,1,0:T(8,128)S(1)}, u32[]{:S(2)}, u32[]{:S(2)}) %collective-permute-start.29) | collective-permute-done | bytes 262176 | tf_op jit(solution)/shard_map/ppermute | solution.py:274
  129.0 3.1 %shard_map.80 = (f32[32,8,128]{2,1,0:T(8,128)S(1)}, f32[64,2,8,128]{3,2,1,0:T(8,128)S(1)}, f32[8,128]{1,0:T(8,128)S(1)}) custom-call(s32[128]{0:T(128)S(1)} %get-tuple-element.69.place, s32[128]{0:T(128)S(1)} %get-tuple-element.70.away, f32[128]{0:T(128)S(1)} %get-tuple-element.71.keep, s32[64]{0:T(128)S(1)} %get-tuple-element.72.picked, ...), custom_call_target="tpu_custom_call" | custom-call | tf_op jit(solution)/shard_map/pallas_call | solution.py:26
  132.3 12.8 %all_to_all.5.sums = f32[32,8,128]{2,1,0:T(8,128)S(1)} all-to-all(f32[32,8,128]{2,1,0:T(8,128)S(1)} %get-tuple-element.106), channel_id=1, replica_groups=mesh['body'=2,'sub'=16] {'body','sub'}, dimensions={0} | all-to-all | bytes 262144 | tf_op jit(solution)/shard_map/all_to_all | solution.py:409
  145.1 2.2 %shard_map.81 = f32[8,64,256]{2,1,0:T(8,128)} custom-call(f32[64]{0:T(128)S(1)} %get-tuple-element.182.keep, f32[32,8,128]{2,1,0:T(8,128)S(1)} %all_to_all.5.sums, f32[8,128]{1,0:T(8,128)S(1)} %get-tuple-element.107.known, f32[64,256]{1,0:T(8,128)S(1)} %copy-done, f32[64,2,8,128]{3,2,1,0:T(8,128)S(1)} %get-tuple-element.108.mine, ...), custom_call_target="tpu_custom_call" | custom-call | tf_op jit(solution)/shard_map/pallas_call | solution.py:26
  (116 shorter events, 31.5 us)
Async XLA Ops:
  6.2 10.9 %collective-permute-start = (f32[76,8,128]{2,1,0:T(8,128)S(1)}, f32[76,8,128]{2,1,0:T(8,128)S(1)}, u32[]{:S(2)}, u32[]{:S(2)}) collective-permute-start(f32[76,8,128]{2,1,0:T(8,128)S(1)} %get-tuple-element.61), channel_id=1, source_target_pairs={{0,4},{1,5},{2,6},{3,7},{4,0},{5,1},{6,2},{7,3},{8,12},{9,13},{10,... | collective-permute-start | bytes 933896 | tf_op jit(solution)/shard_map/ppermute | solution.py:278
  9.3 14.5 %collective-permute-start.1 = (f32[76,8,128]{2,1,0:T(8,128)S(1)}, f32[76,8,128]{2,1,0:T(8,128)S(1)}, u32[]{:S(2)}, u32[]{:S(2)}) collective-permute-start(f32[76,8,128]{2,1,0:T(8,128)S(1)} %get-tuple-element.62), channel_id=1, source_target_pairs={{0,8},{1,9},{2,10},{3,11},{4,12},{5,13},{6,14},{7,15},{8,0},{9,1},... | collective-permute-start | bytes 933896 | tf_op jit(solution)/shard_map/ppermute | solution.py:278
  11.9 11.9 %collective-permute-start.2 = (f32[76,8,128]{2,1,0:T(8,128)S(1)}, f32[76,8,128]{2,1,0:T(8,128)S(1)}, u32[]{:S(2)}, u32[]{:S(2)}) collective-permute-start(f32[76,8,128]{2,1,0:T(8,128)S(1)} %get-tuple-element.63), channel_id=1, source_target_pairs={{0,12},{1,13},{2,14},{3,15},{4,8},{5,9},{6,10},{7,11},{8,4},{9,5},... | collective-permute-start | bytes 933896 | tf_op jit(solution)/shard_map/ppermute | solution.py:278
  25.1 6.9 %collective-permute-start.4 = (f32[77,8,128]{2,1,0:T(8,128)S(1)}, f32[77,8,128]{2,1,0:T(8,128)S(1)}, u32[]{:S(2)}, u32[]{:S(2)}) collective-permute-start(f32[77,8,128]{2,1,0:T(8,128)S(1)} %get-tuple-element.179), channel_id=1, source_target_pairs={{0,1},{1,0},{2,3},{3,2},{4,5},{5,4},{6,7},{7,6},{8,9},{9,8},{10,11... | collective-permute-start | bytes 946184 | tf_op jit(solution)/shard_map/ppermute | solution.py:278
  26.6 10.3 %collective-permute-start.5 = (f32[77,8,128]{2,1,0:T(8,128)S(1)}, f32[77,8,128]{2,1,0:T(8,128)S(1)}, u32[]{:S(2)}, u32[]{:S(2)}) collective-permute-start(f32[77,8,128]{2,1,0:T(8,128)S(1)} %get-tuple-element.178), channel_id=1, source_target_pairs={{0,2},{1,3},{2,0},{3,1},{4,6},{5,7},{6,4},{7,5},{8,10},{9,11},{10,... | collective-permute-start | bytes 946184 | tf_op jit(solution)/shard_map/ppermute | solution.py:278
  28.1 8.8 %collective-permute-start.6 = (f32[77,8,128]{2,1,0:T(8,128)S(1)}, f32[77,8,128]{2,1,0:T(8,128)S(1)}, u32[]{:S(2)}, u32[]{:S(2)}) collective-permute-start(f32[77,8,128]{2,1,0:T(8,128)S(1)} %get-tuple-element.177), channel_id=1, source_target_pairs={{0,3},{1,2},{2,1},{3,0},{4,7},{5,6},{6,5},{7,4},{8,11},{9,10},{10,... | collective-permute-start | bytes 946184 | tf_op jit(solution)/shard_map/ppermute | solution.py:278
  40.4 6.4 %collective-permute-start.7 = (f32[17,8,128]{2,1,0:T(8,128)S(1)}, f32[17,8,128]{2,1,0:T(8,128)S(1)}, u32[]{:S(2)}, u32[]{:S(2)}) collective-permute-start(f32[17,8,128]{2,1,0:T(8,128)S(1)} %get-tuple-element.74.own), channel_id=1, source_target_pairs={{0,16},{16,0},{1,17},{17,1},{2,18},{18,2},{3,19},{19,3},{4,20},{20... | collective-permute-start | bytes 208904 | tf_op jit(solution)/shard_map/ppermute | solution.py:281
  46.9 6.7 %collective-permute-start.8 = (f32[17,8,128]{2,1,0:T(8,128)S(1)}, f32[17,8,128]{2,1,0:T(8,128)S(1)}, u32[]{:S(2)}, u32[]{:S(2)}) collective-permute-start(f32[17,8,128]{2,1,0:T(8,128)S(1)} %pad_maximum_fusion.6), channel_id=1, source_target_pairs={{0,4},{1,5},{2,6},{3,7},{4,0},{5,1},{6,2},{7,3},{8,12},{9,13},{10,... | collective-permute-start | bytes 208904 | tf_op jit(solution)/shard_map/ppermute | solution.py:274
  50.9 8.7 %collective-permute-start.9 = (f32[17,8,128]{2,1,0:T(8,128)S(1)}, f32[17,8,128]{2,1,0:T(8,128)S(1)}, u32[]{:S(2)}, u32[]{:S(2)}) collective-permute-start(f32[17,8,128]{2,1,0:T(8,128)S(1)} %pad_maximum_fusion.6), channel_id=1, source_target_pairs={{0,8},{1,9},{2,10},{3,11},{4,12},{5,13},{6,14},{7,15},{8,0},{9,1},... | collective-permute-start | bytes 208904 | tf_op jit(solution)/shard_map/ppermute | solution.py:274
  52.0 7.6 %collective-permute-start.10 = (f32[17,8,128]{2,1,0:T(8,128)S(1)}, f32[17,8,128]{2,1,0:T(8,128)S(1)}, u32[]{:S(2)}, u32[]{:S(2)}) collective-permute-start(f32[17,8,128]{2,1,0:T(8,128)S(1)} %pad_maximum_fusion.6), channel_id=1, source_target_pairs={{0,12},{1,13},{2,14},{3,15},{4,8},{5,9},{6,10},{7,11},{8,4},{9,5},... | collective-permute-start | bytes 208904 | tf_op jit(solution)/shard_map/ppermute | solution.py:274
  59.6 5.2 %collective-permute-start.13 = (f32[36,8,128]{2,1,0:T(8,128)S(1)}, f32[36,8,128]{2,1,0:T(8,128)S(1)}, u32[]{:S(2)}, u32[]{:S(2)}) collective-permute-start(f32[36,8,128]{2,1,0:T(8,128)S(1)} %pad_maximum_fusion), channel_id=1, source_target_pairs={{0,2},{1,3},{2,0},{3,1},{4,6},{5,7},{6,4},{7,5},{8,10},{9,11},{10,... | collective-permute-start | bytes 442376 | tf_op jit(solution)/shard_map/ppermute | solution.py:274
  61.2 6.2 %collective-permute-start.11 = (f32[32,8,128]{2,1,0:T(8,128)S(1)}, f32[32,8,128]{2,1,0:T(8,128)S(1)}, u32[]{:S(2)}, u32[]{:S(2)}) collective-permute-start(f32[32,8,128]{2,1,0:T(8,128)S(1)} %pad_maximum_fusion.3), channel_id=1, source_target_pairs={{0,1},{1,0},{2,3},{3,2},{4,5},{5,4},{6,7},{7,6},{8,9},{9,8},{10,11... | collective-permute-start | bytes 393224 | tf_op jit(solution)/shard_map/ppermute | solution.py:274
  64.8 9.1 %collective-permute-start.14 = (f32[72,8,128]{2,1,0:T(8,128)S(1)}, f32[72,8,128]{2,1,0:T(8,128)S(1)}, u32[]{:S(2)}, u32[]{:S(2)}) collective-permute-start(f32[72,8,128]{2,1,0:T(8,128)S(1)} %constant_dynamic-update-slice_fusion.20.near_b), channel_id=1, source_target_pairs={{0,1},{1,0},{2,3},{3,2},{4,5},{5,4},{6,7},{7,6},{8,9},{9,8},{10,11... | collective-permute-start | bytes 884744 | tf_op jit(solution)/shard_map/ppermute | solution.py:274
  67.5 6.4 %collective-permute-start.12 = (f32[64,8,128]{2,1,0:T(8,128)S(1)}, f32[64,8,128]{2,1,0:T(8,128)S(1)}, u32[]{:S(2)}, u32[]{:S(2)}) collective-permute-start(f32[64,8,128]{2,1,0:T(8,128)S(1)} %constant_dynamic-update-slice_fusion.15.near_a), channel_id=1, source_target_pairs={{0,2},{1,3},{2,0},{3,1},{4,6},{5,7},{6,4},{7,5},{8,10},{9,11},{10,... | collective-permute-start | bytes 786440 | tf_op jit(solution)/shard_map/ppermute | solution.py:274
  76.8 1.3 collective-permute-start.15
  78.2 4.5 %collective-permute-start.16 = (f32[17,8,128]{2,1,0:T(8,128)S(1)}, f32[17,8,128]{2,1,0:T(8,128)S(1)}, u32[]{:S(2)}, u32[]{:S(2)}) collective-permute-start(f32[17,8,128]{2,1,0:T(8,128)S(1)} %pad_maximum_fusion.7), channel_id=1, source_target_pairs={{0,4},{1,5},{2,6},{3,7},{4,0},{5,1},{6,2},{7,3},{8,12},{9,13},{10,... | collective-permute-start | bytes 208904 | tf_op jit(solution)/shard_map/ppermute | solution.py:274
  79.1 8.6 %collective-permute-start.17 = (f32[17,8,128]{2,1,0:T(8,128)S(1)}, f32[17,8,128]{2,1,0:T(8,128)S(1)}, u32[]{:S(2)}, u32[]{:S(2)}) collective-permute-start(f32[17,8,128]{2,1,0:T(8,128)S(1)} %pad_maximum_fusion.7), channel_id=1, source_target_pairs={{0,8},{1,9},{2,10},{3,11},{4,12},{5,13},{6,14},{7,15},{8,0},{9,1},... | collective-permute-start | bytes 208904 | tf_op jit(solution)/shard_map/ppermute | solution.py:274
  80.4 7.3 %collective-permute-start.18 = (f32[17,8,128]{2,1,0:T(8,128)S(1)}, f32[17,8,128]{2,1,0:T(8,128)S(1)}, u32[]{:S(2)}, u32[]{:S(2)}) collective-permute-start(f32[17,8,128]{2,1,0:T(8,128)S(1)} %pad_maximum_fusion.7), channel_id=1, source_target_pairs={{0,12},{1,13},{2,14},{3,15},{4,8},{5,9},{6,10},{7,11},{8,4},{9,5},... | collective-permute-start | bytes 208904 | tf_op jit(solution)/shard_map/ppermute | solution.py:274
  82.6 13.1 %collective-permute-start.23 = (f32[64,2,8,128]{3,2,1,0:T(8,128)S(1)}, f32[64,2,8,128]{3,2,1,0:T(8,128)S(1)}, u32[]{:S(2)}, u32[]{:S(2)}) collective-permute-start(f32[64,2,8,128]{3,2,1,0:T(8,128)S(1)} %get-tuple-element.80.mine), channel_id=1, source_target_pairs={{0,16},{16,0},{1,17},{17,1},{2,18},{18,2},{3,19},{19,3},{4,20},{20... | collective-permute-start | bytes 1572872 | tf_op jit(solution)/shard_map/ppermute | solution.py:281
  87.7 5.2 %collective-permute-start.21 = (f32[36,8,128]{2,1,0:T(8,128)S(1)}, f32[36,8,128]{2,1,0:T(8,128)S(1)}, u32[]{:S(2)}, u32[]{:S(2)}) collective-permute-start(f32[36,8,128]{2,1,0:T(8,128)S(1)} %pad_maximum_fusion.1), channel_id=1, source_target_pairs={{0,2},{1,3},{2,0},{3,1},{4,6},{5,7},{6,4},{7,5},{8,10},{9,11},{10,... | collective-permute-start | bytes 442376 | tf_op jit(solution)/shard_map/ppermute | solution.py:274
  89.1 6.4 %collective-permute-start.19 = (f32[32,8,128]{2,1,0:T(8,128)S(1)}, f32[32,8,128]{2,1,0:T(8,128)S(1)}, u32[]{:S(2)}, u32[]{:S(2)}) collective-permute-start(f32[32,8,128]{2,1,0:T(8,128)S(1)} %pad_maximum_fusion.4), channel_id=1, source_target_pairs={{0,1},{1,0},{2,3},{3,2},{4,5},{5,4},{6,7},{7,6},{8,9},{9,8},{10,11... | collective-permute-start | bytes 393224 | tf_op jit(solution)/shard_map/ppermute | solution.py:274
  92.9 9.1 %collective-permute-start.22 = (f32[72,8,128]{2,1,0:T(8,128)S(1)}, f32[72,8,128]{2,1,0:T(8,128)S(1)}, u32[]{:S(2)}, u32[]{:S(2)}) collective-permute-start(f32[72,8,128]{2,1,0:T(8,128)S(1)} %constant_dynamic-update-slice_fusion.30.near_b), channel_id=1, source_target_pairs={{0,1},{1,0},{2,3},{3,2},{4,5},{5,4},{6,7},{7,6},{8,9},{9,8},{10,11... | collective-permute-start | bytes 884744 | tf_op jit(solution)/shard_map/ppermute | solution.py:274
  95.6 6.4 %collective-permute-start.20 = (f32[64,8,128]{2,1,0:T(8,128)S(1)}, f32[64,8,128]{2,1,0:T(8,128)S(1)}, u32[]{:S(2)}, u32[]{:S(2)}) collective-permute-start(f32[64,8,128]{2,1,0:T(8,128)S(1)} %constant_dynamic-update-slice_fusion.25.near_a), channel_id=1, source_target_pairs={{0,2},{1,3},{2,0},{3,1},{4,6},{5,7},{6,4},{7,5},{8,10},{9,11},{10,... | collective-permute-start | bytes 786440 | tf_op jit(solution)/shard_map/ppermute | solution.py:274
  106.5 5.1 %collective-permute-start.25 = (f32[17,8,128]{2,1,0:T(8,128)S(1)}, f32[17,8,128]{2,1,0:T(8,128)S(1)}, u32[]{:S(2)}, u32[]{:S(2)}) collective-permute-start(f32[17,8,128]{2,1,0:T(8,128)S(1)} %pad_maximum_fusion.8), channel_id=1, source_target_pairs={{0,4},{1,5},{2,6},{3,7},{4,0},{5,1},{6,2},{7,3},{8,12},{9,13},{10,... | collective-permute-start | bytes 208904 | tf_op jit(solution)/shard_map/ppermute | solution.py:274
  107.2 8.6 %collective-permute-start.26 = (f32[17,8,128]{2,1,0:T(8,128)S(1)}, f32[17,8,128]{2,1,0:T(8,128)S(1)}, u32[]{:S(2)}, u32[]{:S(2)}) collective-permute-start(f32[17,8,128]{2,1,0:T(8,128)S(1)} %pad_maximum_fusion.8), channel_id=1, source_target_pairs={{0,8},{1,9},{2,10},{3,11},{4,12},{5,13},{6,14},{7,15},{8,0},{9,1},... | collective-permute-start | bytes 208904 | tf_op jit(solution)/shard_map/ppermute | solution.py:274
  108.4 7.4 %collective-permute-start.27 = (f32[17,8,128]{2,1,0:T(8,128)S(1)}, f32[17,8,128]{2,1,0:T(8,128)S(1)}, u32[]{:S(2)}, u32[]{:S(2)}) collective-permute-start(f32[17,8,128]{2,1,0:T(8,128)S(1)} %pad_maximum_fusion.8), channel_id=1, source_target_pairs={{0,12},{1,13},{2,14},{3,15},{4,8},{5,9},{6,10},{7,11},{8,4},{9,5},... | collective-permute-start | bytes 208904 | tf_op jit(solution)/shard_map/ppermute | solution.py:274
  110.9 12.7 %collective-permute-start.32 = (f32[64,2,8,128]{3,2,1,0:T(8,128)S(1)}, f32[64,2,8,128]{3,2,1,0:T(8,128)S(1)}, u32[]{:S(2)}, u32[]{:S(2)}) collective-permute-start(f32[64,2,8,128]{3,2,1,0:T(8,128)S(1)} %get-tuple-element.93.mine), channel_id=1, source_target_pairs={{0,16},{16,0},{1,17},{17,1},{2,18},{18,2},{3,19},{19,3},{4,20},{20... | collective-permute-start | bytes 1572872 | tf_op jit(solution)/shard_map/ppermute | solution.py:281
  115.9 5.2 %collective-permute-start.30 = (f32[36,8,128]{2,1,0:T(8,128)S(1)}, f32[36,8,128]{2,1,0:T(8,128)S(1)}, u32[]{:S(2)}, u32[]{:S(2)}) collective-permute-start(f32[36,8,128]{2,1,0:T(8,128)S(1)} %pad_maximum_fusion.2), channel_id=1, source_target_pairs={{0,2},{1,3},{2,0},{3,1},{4,6},{5,7},{6,4},{7,5},{8,10},{9,11},{10,... | collective-permute-start | bytes 442376 | tf_op jit(solution)/shard_map/ppermute | solution.py:274
  116.9 5.7 %collective-permute-start.28 = (f32[32,8,128]{2,1,0:T(8,128)S(1)}, f32[32,8,128]{2,1,0:T(8,128)S(1)}, u32[]{:S(2)}, u32[]{:S(2)}) collective-permute-start(f32[32,8,128]{2,1,0:T(8,128)S(1)} %pad_maximum_fusion.5), channel_id=1, source_target_pairs={{0,1},{1,0},{2,3},{3,2},{4,5},{5,4},{6,7},{7,6},{8,9},{9,8},{10,11... | collective-permute-start | bytes 393224 | tf_op jit(solution)/shard_map/ppermute | solution.py:274
  121.1 8.0 %collective-permute-start.31 = (f32[72,8,128]{2,1,0:T(8,128)S(1)}, f32[72,8,128]{2,1,0:T(8,128)S(1)}, u32[]{:S(2)}, u32[]{:S(2)}) collective-permute-start(f32[72,8,128]{2,1,0:T(8,128)S(1)} %constant_dynamic-update-slice_fusion.40.near_b), channel_id=1, source_target_pairs={{0,1},{1,0},{2,3},{3,2},{4,5},{5,4},{6,7},{7,6},{8,9},{9,8},{10,11... | collective-permute-start | bytes 884744 | tf_op jit(solution)/shard_map/ppermute | solution.py:274
  122.6 6.4 %collective-permute-start.29 = (f32[64,8,128]{2,1,0:T(8,128)S(1)}, f32[64,8,128]{2,1,0:T(8,128)S(1)}, u32[]{:S(2)}, u32[]{:S(2)}) collective-permute-start(f32[64,8,128]{2,1,0:T(8,128)S(1)} %constant_dynamic-update-slice_fusion.35.near_a), channel_id=1, source_target_pairs={{0,2},{1,3},{2,0},{3,1},{4,6},{5,7},{6,4},{7,5},{8,10},{9,11},{10,... | collective-permute-start | bytes 786440 | tf_op jit(solution)/shard_map/ppermute | solution.py:274
  132.2 12.9 %collective-permute-start.33 = (f32[64,2,8,128]{3,2,1,0:T(8,128)S(1)}, f32[64,2,8,128]{3,2,1,0:T(8,128)S(1)}, u32[]{:S(2)}, u32[]{:S(2)}) collective-permute-start(f32[64,2,8,128]{3,2,1,0:T(8,128)S(1)} %get-tuple-element.108.mine), channel_id=1, source_target_pairs={{0,16},{16,0},{1,17},{17,1},{2,18},{18,2},{3,19},{19,3},{4,20},{20... | collective-permute-start | bytes 1572872 | tf_op jit(solution)/shard_map/ppermute | solution.py:281
  (3 other events, 57.8 us)

commit v14 on v11

--- a/solution.py
+++ b/solution.py
@@ -278,7 +278,7 @@
     lines = -(-room * nh // SUBLANES)
     deep = -(-room // SUBLANES)
     extra = lines + deep
-    cut = room // 2
+    cut = max(1, 5 * room // 8)
     first = cut * nh
     second = (room - cut) * nh + extra
     nz = nsub // 4

time: 144 us -> 145 us (level)
  transfers between devices with their start and end apart: 39 -> 39, of which waited for: 23 -> 22; matrix products, arithmetic and copies ran while one was open for 1% -> 0% of each run, Pallas kernels for 4% -> 4%
where the time goes in v14:
time: 145 us
  waiting for transfers between devices  58 us (40%)
  starting transfers between devices  47.2 us (33%)
  Pallas kernels  21.7 us (15%)
  blocking collectives  11.4 us (8%)
  other arithmetic  3.76 us (3%)
    ppermute x33, waiting for transfers between devices, swap(): return lax.ppermute(value, 'sub', [(i, i ^ far) for i in range(nsub)])  54.2 us
    ppermute x33, starting transfers between devices, swap(): return lax.ppermute(value, 'sub', [(i, i ^ far) for i in range(nsub)])  47 us
    pallas_call x9, Pallas kernels, call(): pl.pallas_call(kernel, out_shape=tuple(out_shape) if several else out_sha...  18.3 us
    all_to_all x1, blocking collectives, on_device(): lax.all_to_all(own, ('body', 'sub'), split_axis=0, concat_axis=0, tiled=T...  11.4 us
    ppermute x6, waiting for transfers between devices, sibling(): lax.ppermute(value, 'body', [(i, nbody - 1 - i) for i in range(nbody)])  3.77 us
    pallas_call x1, Pallas kernels, on_device(): pl.pallas_call(functools.partial(start_kernel, nh, cut, room, lines, extr...  3.47 us
  transfers between devices with their start and end apart: 39, of which 22 were waited for; matrix products, arithmetic and copies ran while one was open for 0% of the time, Pallas kernels for 4%

profile of v14, /device:TPU:0, one launch (start us, length us, event | category | flops | bytes accessed | tf_op | source)
XLA Modules:
  0.0 144.6 jit_solution(1730804745130318090)
XLA Ops:
  6.1 3.0 %collective-permute-start.3 = (f32[36,8,128]{2,1,0:T(8,128)S(1)}, f32[36,8,128]{2,1,0:T(8,128)S(1)}, u32[]{:S(2)}, u32[]{:S(2)}) collective-permute-start(f32[36,8,128]{2,1,0:T(8,128)S(1)} %get-tuple-element.75), channel_id=1, source_target_pairs={{0,1},{1,0},{2,3},{3,2},{4,5},{5,4},{6,7},{7,6},{8,9},{9,8},{10,11... | collective-permute-start | bytes 442376 | tf_op jit(solution)/shard_map/ppermute | solution.py:288
  9.9 1.6 %collective-permute-start = (f32[40,8,128]{2,1,0:T(8,128)S(1)}, f32[40,8,128]{2,1,0:T(8,128)S(1)}, u32[]{:S(2)}, u32[]{:S(2)}) collective-permute-start(f32[40,8,128]{2,1,0:T(8,128)S(1)} %get-tuple-element.70), channel_id=1, source_target_pairs={{0,4},{1,5},{2,6},{3,7},{4,0},{5,1},{6,2},{7,3},{8,12},{9,13},{10,... | collective-permute-start | bytes 491528 | tf_op jit(solution)/shard_map/ppermute | solution.py:288
  11.5 2.6 %collective-permute-start.1 = (f32[40,8,128]{2,1,0:T(8,128)S(1)}, f32[40,8,128]{2,1,0:T(8,128)S(1)}, u32[]{:S(2)}, u32[]{:S(2)}) collective-permute-start(f32[40,8,128]{2,1,0:T(8,128)S(1)} %get-tuple-element.71), channel_id=1, source_target_pairs={{0,8},{1,9},{2,10},{3,11},{4,12},{5,13},{6,14},{7,15},{8,0},{9,1},... | collective-permute-start | bytes 491528 | tf_op jit(solution)/shard_map/ppermute | solution.py:288
  16.1 3.5 %shard_map.75.block = bf16[2048,2048]{1,0:T(8,128)(2,1)S(1)} custom-call(bf16[2048,2048]{1,0:T(8,128)(2,1)} %bitcast.62), custom_call_target="tpu_custom_call" | custom-call | bytes 16777216 | tf_op jit(solution)/shard_map/pallas_call | solution.py:25
  19.6 3.0 %collective-permute-done.4.refs_9_ = f32[36,8,128]{2,1,0:T(8,128)S(1)} collective-permute-done((f32[36,8,128]{2,1,0:T(8,128)S(1)}, f32[36,8,128]{2,1,0:T(8,128)S(1)}, u32[]{:S(2)}, u32[]{:S(2)}) %collective-permute-start.4) | collective-permute-done | bytes 147488 | tf_op jit(solution)/shard_map/ppermute | solution.py:288
  22.6 4.0 %collective-permute-done.1.refs_2_ = f32[40,8,128]{2,1,0:T(8,128)S(1)} collective-permute-done((f32[40,8,128]{2,1,0:T(8,128)S(1)}, f32[40,8,128]{2,1,0:T(8,128)S(1)}, u32[]{:S(2)}, u32[]{:S(2)}) %collective-permute-start.1) | collective-permute-done | bytes 163872 | tf_op jit(solution)/shard_map/ppermute | solution.py:288
  26.7 2.2 %collective-permute-start.11 = (f32[36,8,128]{2,1,0:T(8,128)S(1)}, f32[36,8,128]{2,1,0:T(8,128)S(1)}, u32[]{:S(2)}, u32[]{:S(2)}) collective-permute-start(f32[36,8,128]{2,1,0:T(8,128)S(1)} %pad_maximum_fusion.5), channel_id=1, source_target_pairs={{0,12},{1,13},{2,14},{3,15},{4,8},{5,9},{6,10},{7,11},{8,4},{9,5},... | collective-permute-start | bytes 442376 | tf_op jit(solution)/shard_map/ppermute | solution.py:288
  28.9 3.5 %collective-permute-start.10 = (f32[36,8,128]{2,1,0:T(8,128)S(1)}, f32[36,8,128]{2,1,0:T(8,128)S(1)}, u32[]{:S(2)}, u32[]{:S(2)}) collective-permute-start(f32[36,8,128]{2,1,0:T(8,128)S(1)} %pad_maximum_fusion.4), channel_id=1, source_target_pairs={{0,8},{1,9},{2,10},{3,11},{4,12},{5,13},{6,14},{7,15},{8,0},{9,1},... | collective-permute-start | bytes 442376 | tf_op jit(solution)/shard_map/ppermute | solution.py:288
  36.2 3.8 %collective-permute-start.9 = (f32[36,8,128]{2,1,0:T(8,128)S(1)}, f32[36,8,128]{2,1,0:T(8,128)S(1)}, u32[]{:S(2)}, u32[]{:S(2)}) collective-permute-start(f32[36,8,128]{2,1,0:T(8,128)S(1)} %pad_maximum_fusion.3), channel_id=1, source_target_pairs={{0,4},{1,5},{2,6},{3,7},{4,0},{5,1},{6,2},{7,3},{8,12},{9,13},{10,... | collective-permute-start | bytes 442376 | tf_op jit(solution)/shard_map/ppermute | solution.py:288
  41.0 2.1 %collective-permute-done.9.refs_11_ = f32[36,8,128]{2,1,0:T(8,128)S(1)} collective-permute-done((f32[36,8,128]{2,1,0:T(8,128)S(1)}, f32[36,8,128]{2,1,0:T(8,128)S(1)}, u32[]{:S(2)}, u32[]{:S(2)}) %collective-permute-start.9) | collective-permute-done | bytes 147488 | tf_op jit(solution)/shard_map/ppermute | solution.py:288
  43.2 3.5 %shard_map.76 = (s32[128]{0:T(128)S(1)}, s32[128]{0:T(128)S(1)}, f32[128]{0:T(128)S(1)}, f32[128,2,8,128]{3,2,1,0:T(8,128)S(1)}, f32[32,8,128]{2,1,0:T(8,128)S(1)}, /*index=5*/f32[17,8,128]{2,1,0:T(8,128)S(1)}) custom-call(bf16[2048,2048]{1,0:T(8,128)(2,1)S(1)} %shard_map.75.block, f32[40,8,128]{2,1,0:T(8,128)S(1)} %get-tuple-element.79.refs_0_, ...), custom_call_target="tpu_custom_call" | custom-call | tf_op jit(solution)/shard_map/pallas_call | solution.py:364
  48.0 2.1 %collective-permute-start.13 = (f32[17,8,128]{2,1,0:T(8,128)S(1)}, f32[17,8,128]{2,1,0:T(8,128)S(1)}, u32[]{:S(2)}, u32[]{:S(2)}) collective-permute-start(f32[17,8,128]{2,1,0:T(8,128)S(1)} %pad_maximum_fusion.12), channel_id=1, source_target_pairs={{0,4},{1,5},{2,6},{3,7},{4,0},{5,1},{6,2},{7,3},{8,12},{9,13},{10,... | collective-permute-start | bytes 208904 | tf_op jit(solution)/shard_map/ppermute | solution.py:288
  50.9 1.6 %collective-permute-start.15 = (f32[17,8,128]{2,1,0:T(8,128)S(1)}, f32[17,8,128]{2,1,0:T(8,128)S(1)}, u32[]{:S(2)}, u32[]{:S(2)}) collective-permute-start(f32[17,8,128]{2,1,0:T(8,128)S(1)} %pad_maximum_fusion.12), channel_id=1, source_target_pairs={{0,12},{1,13},{2,14},{3,15},{4,8},{5,9},{6,10},{7,11},{8,4},{9,5},... | collective-permute-start | bytes 208904 | tf_op jit(solution)/shard_map/ppermute | solution.py:288
  52.6 5.9 %collective-permute-done.14 = f32[17,8,128]{2,1,0:T(8,128)S(1)} collective-permute-done((f32[17,8,128]{2,1,0:T(8,128)S(1)}, f32[17,8,128]{2,1,0:T(8,128)S(1)}, u32[]{:S(2)}, u32[]{:S(2)}) %collective-permute-start.14) | collective-permute-done | bytes 69664 | tf_op jit(solution)/shard_map/ppermute | solution.py:288
  60.8 3.0 %collective-permute-done.18 = f32[36,8,128]{2,1,0:T(8,128)S(1)} collective-permute-done((f32[36,8,128]{2,1,0:T(8,128)S(1)}, f32[36,8,128]{2,1,0:T(8,128)S(1)}, u32[]{:S(2)}, u32[]{:S(2)}) %collective-permute-start.18) | collective-permute-done | bytes 147488 | tf_op jit(solution)/shard_map/ppermute | solution.py:288
  64.4 1.9 %collective-permute-done.16 = f32[32,8,128]{2,1,0:T(8,128)S(1)} collective-permute-done((f32[32,8,128]{2,1,0:T(8,128)S(1)}, f32[32,8,128]{2,1,0:T(8,128)S(1)}, u32[]{:S(2)}, u32[]{:S(2)}) %collective-permute-start.16) | collective-permute-done | bytes 131104 | tf_op jit(solution)/shard_map/ppermute | solution.py:288
  66.4 6.4 %collective-permute-done.17.far_a = f32[64,8,128]{2,1,0:T(8,128)S(1)} collective-permute-done((f32[64,8,128]{2,1,0:T(8,128)S(1)}, f32[64,8,128]{2,1,0:T(8,128)S(1)}, u32[]{:S(2)}, u32[]{:S(2)}) %collective-permute-start.17) | collective-permute-done | bytes 262176 | tf_op jit(solution)/shard_map/ppermute | solution.py:288
  72.7 3.0 %shard_map.77 = (f32[128,2,8,128]{3,2,1,0:T(8,128)S(1)}, f32[128,2,8,128]{3,2,1,0:T(8,128)S(1)}, f32[17,8,128]{2,1,0:T(8,128)S(1)}, f32[64,2,8,128]{3,2,1,0:T(8,128)S(1)}, f32[8,128]{1,0:T(8,128)S(1)}) custom-call(s32[128]{0:T(128)S(1)} %get-tuple-element.87.place, s32[128]{0:T(128)S(1)} %get-tuple-element.88.away, f32[128]{0:T(128)S(1)} %get-tuple-element.89.keep, ...), custom_call_target="tpu_custom_call" | custom-call | tf_op jit(solution)/shard_map/pallas_call | solution.py:25
  77.7 1.7 %collective-permute-start.22 = (f32[17,8,128]{2,1,0:T(8,128)S(1)}, f32[17,8,128]{2,1,0:T(8,128)S(1)}, u32[]{:S(2)}, u32[]{:S(2)}) collective-permute-start(f32[17,8,128]{2,1,0:T(8,128)S(1)} %pad_maximum_fusion.13), channel_id=1, source_target_pairs={{0,8},{1,9},{2,10},{3,11},{4,12},{5,13},{6,14},{7,15},{8,0},{9,1},... | collective-permute-start | bytes 208904 | tf_op jit(solution)/shard_map/ppermute | solution.py:288
  79.4 2.1 %collective-permute-start.23 = (f32[17,8,128]{2,1,0:T(8,128)S(1)}, f32[17,8,128]{2,1,0:T(8,128)S(1)}, u32[]{:S(2)}, u32[]{:S(2)}) collective-permute-start(f32[17,8,128]{2,1,0:T(8,128)S(1)} %pad_maximum_fusion.13), channel_id=1, source_target_pairs={{0,12},{1,13},{2,14},{3,15},{4,8},{5,9},{6,10},{7,11},{8,4},{9,5},... | collective-permute-start | bytes 208904 | tf_op jit(solution)/shard_map/ppermute | solution.py:288
  82.2 4.2 %collective-permute-done.22 = f32[17,8,128]{2,1,0:T(8,128)S(1)} collective-permute-done((f32[17,8,128]{2,1,0:T(8,128)S(1)}, f32[17,8,128]{2,1,0:T(8,128)S(1)}, u32[]{:S(2)}, u32[]{:S(2)}) %collective-permute-start.22) | collective-permute-done | bytes 69664 | tf_op jit(solution)/shard_map/ppermute | solution.py:288
  88.5 3.1 %collective-permute-done.26 = f32[36,8,128]{2,1,0:T(8,128)S(1)} collective-permute-done((f32[36,8,128]{2,1,0:T(8,128)S(1)}, f32[36,8,128]{2,1,0:T(8,128)S(1)}, u32[]{:S(2)}, u32[]{:S(2)}) %collective-permute-start.26) | collective-permute-done | bytes 147488 | tf_op jit(solution)/shard_map/ppermute | solution.py:288
  95.2 4.8 %collective-permute-done.25.far_a = f32[64,8,128]{2,1,0:T(8,128)S(1)} collective-permute-done((f32[64,8,128]{2,1,0:T(8,128)S(1)}, f32[64,8,128]{2,1,0:T(8,128)S(1)}, u32[]{:S(2)}, u32[]{:S(2)}) %collective-permute-start.25) | collective-permute-done | bytes 262176 | tf_op jit(solution)/shard_map/ppermute | solution.py:288
  100.0 3.1 %shard_map.79 = (f32[128,2,8,128]{3,2,1,0:T(8,128)S(1)}, f32[128,2,8,128]{3,2,1,0:T(8,128)S(1)}, f32[17,8,128]{2,1,0:T(8,128)S(1)}, f32[64,2,8,128]{3,2,1,0:T(8,128)S(1)}, f32[8,128]{1,0:T(8,128)S(1)}) custom-call(s32[128]{0:T(128)S(1)} %get-tuple-element.87.place, s32[128]{0:T(128)S(1)} %get-tuple-element.88.away, f32[128]{0:T(128)S(1)} %get-tuple-element.89.keep, ...), custom_call_target="tpu_custom_call" | custom-call | tf_op jit(solution)/shard_map/pallas_call | solution.py:25
  105.3 1.6 %collective-permute-start.31 = (f32[17,8,128]{2,1,0:T(8,128)S(1)}, f32[17,8,128]{2,1,0:T(8,128)S(1)}, u32[]{:S(2)}, u32[]{:S(2)}) collective-permute-start(f32[17,8,128]{2,1,0:T(8,128)S(1)} %pad_maximum_fusion.14), channel_id=1, source_target_pairs={{0,8},{1,9},{2,10},{3,11},{4,12},{5,13},{6,14},{7,15},{8,0},{9,1},... | collective-permute-start | bytes 208904 | tf_op jit(solution)/shard_map/ppermute | solution.py:288
  106.9 2.0 %collective-permute-start.32 = (f32[17,8,128]{2,1,0:T(8,128)S(1)}, f32[17,8,128]{2,1,0:T(8,128)S(1)}, u32[]{:S(2)}, u32[]{:S(2)}) collective-permute-start(f32[17,8,128]{2,1,0:T(8,128)S(1)} %pad_maximum_fusion.14), channel_id=1, source_target_pairs={{0,12},{1,13},{2,14},{3,15},{4,8},{5,9},{6,10},{7,11},{8,4},{9,5},... | collective-permute-start | bytes 208904 | tf_op jit(solution)/shard_map/ppermute | solution.py:288
  109.6 4.3 %collective-permute-done.31 = f32[17,8,128]{2,1,0:T(8,128)S(1)} collective-permute-done((f32[17,8,128]{2,1,0:T(8,128)S(1)}, f32[17,8,128]{2,1,0:T(8,128)S(1)}, u32[]{:S(2)}, u32[]{:S(2)}) %collective-permute-start.31) | collective-permute-done | bytes 69664 | tf_op jit(solution)/shard_map/ppermute | solution.py:288
  116.0 3.1 %collective-permute-done.35 = f32[36,8,128]{2,1,0:T(8,128)S(1)} collective-permute-done((f32[36,8,128]{2,1,0:T(8,128)S(1)}, f32[36,8,128]{2,1,0:T(8,128)S(1)}, u32[]{:S(2)}, u32[]{:S(2)}) %collective-permute-start.35) | collective-permute-done | bytes 147488 | tf_op jit(solution)/shard_map/ppermute | solution.py:288
  123.6 4.2 %collective-permute-done.34.far_a = f32[64,8,128]{2,1,0:T(8,128)S(1)} collective-permute-done((f32[64,8,128]{2,1,0:T(8,128)S(1)}, f32[64,8,128]{2,1,0:T(8,128)S(1)}, u32[]{:S(2)}, u32[]{:S(2)}) %collective-permute-start.34) | collective-permute-done | bytes 262176 | tf_op jit(solution)/shard_map/ppermute | solution.py:288
  127.8 3.2 %shard_map.81 = (f32[32,8,128]{2,1,0:T(8,128)S(1)}, f32[64,2,8,128]{3,2,1,0:T(8,128)S(1)}, f32[8,128]{1,0:T(8,128)S(1)}) custom-call(s32[128]{0:T(128)S(1)} %get-tuple-element.87.place, s32[128]{0:T(128)S(1)} %get-tuple-element.88.away, f32[128]{0:T(128)S(1)} %get-tuple-element.89.keep, s32[64]{0:T(128)S(1)} %get-tuple-element.90.picked, ...), custom_call_target="tpu_custom_call" | custom-call | tf_op jit(solution)/shard_map/pallas_call | solution.py:25
  131.1 11.4 %all_to_all.5.sums = f32[32,8,128]{2,1,0:T(8,128)S(1)} all-to-all(f32[32,8,128]{2,1,0:T(8,128)S(1)} %get-tuple-element.124), channel_id=1, replica_groups=mesh['body'=2,'sub'=16] {'body','sub'}, dimensions={0} | all-to-all | bytes 262144 | tf_op jit(solution)/shard_map/all_to_all | solution.py:428
  142.5 2.2 %shard_map.82 = f32[8,64,256]{2,1,0:T(8,128)} custom-call(f32[64]{0:T(128)S(1)} %get-tuple-element.210.keep, f32[32,8,128]{2,1,0:T(8,128)S(1)} %all_to_all.5.sums, f32[8,128]{1,0:T(8,128)S(1)} %get-tuple-element.125.known, f32[64,256]{1,0:T(8,128)S(1)} %copy-done, f32[64,2,8,128]{3,2,1,0:T(8,128)S(1)} %get-tuple-element.126.mine, ...), custom_call_target="tpu_custom_call" | custom-call | tf_op jit(solution)/shard_map/pallas_call | solution.py:25
  (134 shorter events, 36.6 us)
Async XLA Ops:
  6.1 9.7 %collective-permute-start.3 = (f32[36,8,128]{2,1,0:T(8,128)S(1)}, f32[36,8,128]{2,1,0:T(8,128)S(1)}, u32[]{:S(2)}, u32[]{:S(2)}) collective-permute-start(f32[36,8,128]{2,1,0:T(8,128)S(1)} %get-tuple-element.75), channel_id=1, source_target_pairs={{0,1},{1,0},{2,3},{3,2},{4,5},{5,4},{6,7},{7,6},{8,9},{9,8},{10,11... | collective-permute-start | bytes 442376 | tf_op jit(solution)/shard_map/ppermute | solution.py:288
  9.9 12.7 %collective-permute-start = (f32[40,8,128]{2,1,0:T(8,128)S(1)}, f32[40,8,128]{2,1,0:T(8,128)S(1)}, u32[]{:S(2)}, u32[]{:S(2)}) collective-permute-start(f32[40,8,128]{2,1,0:T(8,128)S(1)} %get-tuple-element.70), channel_id=1, source_target_pairs={{0,4},{1,5},{2,6},{3,7},{4,0},{5,1},{6,2},{7,3},{8,12},{9,13},{10,... | collective-permute-start | bytes 491528 | tf_op jit(solution)/shard_map/ppermute | solution.py:288
  11.5 15.1 %collective-permute-start.1 = (f32[40,8,128]{2,1,0:T(8,128)S(1)}, f32[40,8,128]{2,1,0:T(8,128)S(1)}, u32[]{:S(2)}, u32[]{:S(2)}) collective-permute-start(f32[40,8,128]{2,1,0:T(8,128)S(1)} %get-tuple-element.71), channel_id=1, source_target_pairs={{0,8},{1,9},{2,10},{3,11},{4,12},{5,13},{6,14},{7,15},{8,0},{9,1},... | collective-permute-start | bytes 491528 | tf_op jit(solution)/shard_map/ppermute | solution.py:288
  14.1 12.5 %collective-permute-start.2 = (f32[40,8,128]{2,1,0:T(8,128)S(1)}, f32[40,8,128]{2,1,0:T(8,128)S(1)}, u32[]{:S(2)}, u32[]{:S(2)}) collective-permute-start(f32[40,8,128]{2,1,0:T(8,128)S(1)} %get-tuple-element.72), channel_id=1, source_target_pairs={{0,12},{1,13},{2,14},{3,15},{4,8},{5,9},{6,10},{7,11},{8,4},{9,5},... | collective-permute-start | bytes 491528 | tf_op jit(solution)/shard_map/ppermute | solution.py:288
  14.4 8.3 %collective-permute-start.4 = (f32[36,8,128]{2,1,0:T(8,128)S(1)}, f32[36,8,128]{2,1,0:T(8,128)S(1)}, u32[]{:S(2)}, u32[]{:S(2)}) collective-permute-start(f32[36,8,128]{2,1,0:T(8,128)S(1)} %get-tuple-element.76), channel_id=1, source_target_pairs={{0,2},{1,3},{2,0},{3,1},{4,6},{5,7},{6,4},{7,5},{8,10},{9,11},{10,... | collective-permute-start | bytes 442376 | tf_op jit(solution)/shard_map/ppermute | solution.py:288
  15.9 6.7 %collective-permute-start.5 = (f32[36,8,128]{2,1,0:T(8,128)S(1)}, f32[36,8,128]{2,1,0:T(8,128)S(1)}, u32[]{:S(2)}, u32[]{:S(2)}) collective-permute-start(f32[36,8,128]{2,1,0:T(8,128)S(1)} %get-tuple-element.77), channel_id=1, source_target_pairs={{0,3},{1,2},{2,1},{3,0},{4,7},{5,6},{6,5},{7,4},{8,11},{9,10},{10,... | collective-permute-start | bytes 442376 | tf_op jit(solution)/shard_map/ppermute | solution.py:288
  26.7 9.5 %collective-permute-start.11 = (f32[36,8,128]{2,1,0:T(8,128)S(1)}, f32[36,8,128]{2,1,0:T(8,128)S(1)}, u32[]{:S(2)}, u32[]{:S(2)}) collective-permute-start(f32[36,8,128]{2,1,0:T(8,128)S(1)} %pad_maximum_fusion.5), channel_id=1, source_target_pairs={{0,12},{1,13},{2,14},{3,15},{4,8},{5,9},{6,10},{7,11},{8,4},{9,5},... | collective-permute-start | bytes 442376 | tf_op jit(solution)/shard_map/ppermute | solution.py:288
  28.9 12.1 %collective-permute-start.10 = (f32[36,8,128]{2,1,0:T(8,128)S(1)}, f32[36,8,128]{2,1,0:T(8,128)S(1)}, u32[]{:S(2)}, u32[]{:S(2)}) collective-permute-start(f32[36,8,128]{2,1,0:T(8,128)S(1)} %pad_maximum_fusion.4), channel_id=1, source_target_pairs={{0,8},{1,9},{2,10},{3,11},{4,12},{5,13},{6,14},{7,15},{8,0},{9,1},... | collective-permute-start | bytes 442376 | tf_op jit(solution)/shard_map/ppermute | solution.py:288
  32.5 10.6 %collective-permute-start.8 = (f32[40,8,128]{2,1,0:T(8,128)S(1)}, f32[40,8,128]{2,1,0:T(8,128)S(1)}, u32[]{:S(2)}, u32[]{:S(2)}) collective-permute-start(f32[40,8,128]{2,1,0:T(8,128)S(1)} %pad_maximum_fusion.2), channel_id=1, source_target_pairs={{0,3},{1,2},{2,1},{3,0},{4,7},{5,6},{6,5},{7,4},{8,11},{9,10},{10,... | collective-permute-start | bytes 491528 | tf_op jit(solution)/shard_map/ppermute | solution.py:288
  34.1 9.1 %collective-permute-start.7 = (f32[40,8,128]{2,1,0:T(8,128)S(1)}, f32[40,8,128]{2,1,0:T(8,128)S(1)}, u32[]{:S(2)}, u32[]{:S(2)}) collective-permute-start(f32[40,8,128]{2,1,0:T(8,128)S(1)} %pad_maximum_fusion.1), channel_id=1, source_target_pairs={{0,2},{1,3},{2,0},{3,1},{4,6},{5,7},{6,4},{7,5},{8,10},{9,11},{10,... | collective-permute-start | bytes 491528 | tf_op jit(solution)/shard_map/ppermute | solution.py:288
  34.7 8.5 %collective-permute-start.6 = (f32[40,8,128]{2,1,0:T(8,128)S(1)}, f32[40,8,128]{2,1,0:T(8,128)S(1)}, u32[]{:S(2)}, u32[]{:S(2)}) collective-permute-start(f32[40,8,128]{2,1,0:T(8,128)S(1)} %pad_maximum_fusion), channel_id=1, source_target_pairs={{0,1},{1,0},{2,3},{3,2},{4,5},{5,4},{6,7},{7,6},{8,9},{9,8},{10,11... | collective-permute-start | bytes 491528 | tf_op jit(solution)/shard_map/ppermute | solution.py:288
  36.2 6.9 %collective-permute-start.9 = (f32[36,8,128]{2,1,0:T(8,128)S(1)}, f32[36,8,128]{2,1,0:T(8,128)S(1)}, u32[]{:S(2)}, u32[]{:S(2)}) collective-permute-start(f32[36,8,128]{2,1,0:T(8,128)S(1)} %pad_maximum_fusion.3), channel_id=1, source_target_pairs={{0,4},{1,5},{2,6},{3,7},{4,0},{5,1},{6,2},{7,3},{8,12},{9,13},{10,... | collective-permute-start | bytes 442376 | tf_op jit(solution)/shard_map/ppermute | solution.py:288
  50.1 8.4 %collective-permute-start.14 = (f32[17,8,128]{2,1,0:T(8,128)S(1)}, f32[17,8,128]{2,1,0:T(8,128)S(1)}, u32[]{:S(2)}, u32[]{:S(2)}) collective-permute-start(f32[17,8,128]{2,1,0:T(8,128)S(1)} %pad_maximum_fusion.12), channel_id=1, source_target_pairs={{0,8},{1,9},{2,10},{3,11},{4,12},{5,13},{6,14},{7,15},{8,0},{9,1},... | collective-permute-start | bytes 208904 | tf_op jit(solution)/shard_map/ppermute | solution.py:288
  50.9 7.6 %collective-permute-start.15 = (f32[17,8,128]{2,1,0:T(8,128)S(1)}, f32[17,8,128]{2,1,0:T(8,128)S(1)}, u32[]{:S(2)}, u32[]{:S(2)}) collective-permute-start(f32[17,8,128]{2,1,0:T(8,128)S(1)} %pad_maximum_fusion.12), channel_id=1, source_target_pairs={{0,12},{1,13},{2,14},{3,15},{4,8},{5,9},{6,10},{7,11},{8,4},{9,5},... | collective-permute-start | bytes 208904 | tf_op jit(solution)/shard_map/ppermute | solution.py:288
  58.6 5.2 %collective-permute-start.18 = (f32[36,8,128]{2,1,0:T(8,128)S(1)}, f32[36,8,128]{2,1,0:T(8,128)S(1)}, u32[]{:S(2)}, u32[]{:S(2)}) collective-permute-start(f32[36,8,128]{2,1,0:T(8,128)S(1)} %pad_maximum_fusion.6), channel_id=1, source_target_pairs={{0,2},{1,3},{2,0},{3,1},{4,6},{5,7},{6,4},{7,5},{8,10},{9,11},{10,... | collective-permute-start | bytes 442376 | tf_op jit(solution)/shard_map/ppermute | solution.py:288
  60.2 6.1 %collective-permute-start.16 = (f32[32,8,128]{2,1,0:T(8,128)S(1)}, f32[32,8,128]{2,1,0:T(8,128)S(1)}, u32[]{:S(2)}, u32[]{:S(2)}) collective-permute-start(f32[32,8,128]{2,1,0:T(8,128)S(1)} %pad_maximum_fusion.9), channel_id=1, source_target_pairs={{0,1},{1,0},{2,3},{3,2},{4,5},{5,4},{6,7},{7,6},{8,9},{9,8},{10,11... | collective-permute-start | bytes 393224 | tf_op jit(solution)/shard_map/ppermute | solution.py:288
  63.8 9.0 %collective-permute-start.19 = (f32[72,8,128]{2,1,0:T(8,128)S(1)}, f32[72,8,128]{2,1,0:T(8,128)S(1)}, u32[]{:S(2)}, u32[]{:S(2)}) collective-permute-start(f32[72,8,128]{2,1,0:T(8,128)S(1)} %constant_dynamic-update-slice_fusion.5.near_b), channel_id=1, source_target_pairs={{0,1},{1,0},{2,3},{3,2},{4,5},{5,4},{6,7},{7,6},{8,9},{9,8},{10,11... | collective-permute-start | bytes 884744 | tf_op jit(solution)/shard_map/ppermute | solution.py:288
  66.3 6.4 %collective-permute-start.17 = (f32[64,8,128]{2,1,0:T(8,128)S(1)}, f32[64,8,128]{2,1,0:T(8,128)S(1)}, u32[]{:S(2)}, u32[]{:S(2)}) collective-permute-start(f32[64,8,128]{2,1,0:T(8,128)S(1)} %constant_dynamic-update-slice_fusion.near_a), channel_id=1, source_target_pairs={{0,2},{1,3},{2,0},{3,1},{4,6},{5,7},{6,4},{7,5},{8,10},{9,11},{10,... | collective-permute-start | bytes 786440 | tf_op jit(solution)/shard_map/ppermute | solution.py:288
  77.7 8.7 %collective-permute-start.22 = (f32[17,8,128]{2,1,0:T(8,128)S(1)}, f32[17,8,128]{2,1,0:T(8,128)S(1)}, u32[]{:S(2)}, u32[]{:S(2)}) collective-permute-start(f32[17,8,128]{2,1,0:T(8,128)S(1)} %pad_maximum_fusion.13), channel_id=1, source_target_pairs={{0,8},{1,9},{2,10},{3,11},{4,12},{5,13},{6,14},{7,15},{8,0},{9,1},... | collective-permute-start | bytes 208904 | tf_op jit(solution)/shard_map/ppermute | solution.py:288
  79.4 7.0 %collective-permute-start.23 = (f32[17,8,128]{2,1,0:T(8,128)S(1)}, f32[17,8,128]{2,1,0:T(8,128)S(1)}, u32[]{:S(2)}, u32[]{:S(2)}) collective-permute-start(f32[17,8,128]{2,1,0:T(8,128)S(1)} %pad_maximum_fusion.13), channel_id=1, source_target_pairs={{0,12},{1,13},{2,14},{3,15},{4,8},{5,9},{6,10},{7,11},{8,4},{9,5},... | collective-permute-start | bytes 208904 | tf_op jit(solution)/shard_map/ppermute | solution.py:288
  81.5 12.8 %collective-permute-start.28 = (f32[64,2,8,128]{3,2,1,0:T(8,128)S(1)}, f32[64,2,8,128]{3,2,1,0:T(8,128)S(1)}, u32[]{:S(2)}, u32[]{:S(2)}) collective-permute-start(f32[64,2,8,128]{3,2,1,0:T(8,128)S(1)} %get-tuple-element.98.mine), channel_id=1, source_target_pairs={{0,16},{16,0},{1,17},{17,1},{2,18},{18,2},{3,19},{19,3},{4,20},{20... | collective-permute-start | bytes 1572872 | tf_op jit(solution)/shard_map/ppermute | solution.py:291
  86.4 5.2 %collective-permute-start.26 = (f32[36,8,128]{2,1,0:T(8,128)S(1)}, f32[36,8,128]{2,1,0:T(8,128)S(1)}, u32[]{:S(2)}, u32[]{:S(2)}) collective-permute-start(f32[36,8,128]{2,1,0:T(8,128)S(1)} %pad_maximum_fusion.7), channel_id=1, source_target_pairs={{0,2},{1,3},{2,0},{3,1},{4,6},{5,7},{6,4},{7,5},{8,10},{9,11},{10,... | collective-permute-start | bytes 442376 | tf_op jit(solution)/shard_map/ppermute | solution.py:288
  87.3 6.2 %collective-permute-start.24 = (f32[32,8,128]{2,1,0:T(8,128)S(1)}, f32[32,8,128]{2,1,0:T(8,128)S(1)}, u32[]{:S(2)}, u32[]{:S(2)}) collective-permute-start(f32[32,8,128]{2,1,0:T(8,128)S(1)} %pad_maximum_fusion.10), channel_id=1, source_target_pairs={{0,1},{1,0},{2,3},{3,2},{4,5},{5,4},{6,7},{7,6},{8,9},{9,8},{10,11... | collective-permute-start | bytes 393224 | tf_op jit(solution)/shard_map/ppermute | solution.py:288
  91.6 8.4 %collective-permute-start.27 = (f32[72,8,128]{2,1,0:T(8,128)S(1)}, f32[72,8,128]{2,1,0:T(8,128)S(1)}, u32[]{:S(2)}, u32[]{:S(2)}) collective-permute-start(f32[72,8,128]{2,1,0:T(8,128)S(1)} %constant_dynamic-update-slice_fusion.15.near_b), channel_id=1, source_target_pairs={{0,1},{1,0},{2,3},{3,2},{4,5},{5,4},{6,7},{7,6},{8,9},{9,8},{10,11... | collective-permute-start | bytes 884744 | tf_op jit(solution)/shard_map/ppermute | solution.py:288
  93.5 6.4 %collective-permute-start.25 = (f32[64,8,128]{2,1,0:T(8,128)S(1)}, f32[64,8,128]{2,1,0:T(8,128)S(1)}, u32[]{:S(2)}, u32[]{:S(2)}) collective-permute-start(f32[64,8,128]{2,1,0:T(8,128)S(1)} %constant_dynamic-update-slice_fusion.10.near_a), channel_id=1, source_target_pairs={{0,2},{1,3},{2,0},{3,1},{4,6},{5,7},{6,4},{7,5},{8,10},{9,11},{10,... | collective-permute-start | bytes 786440 | tf_op jit(solution)/shard_map/ppermute | solution.py:288
  105.3 8.6 %collective-permute-start.31 = (f32[17,8,128]{2,1,0:T(8,128)S(1)}, f32[17,8,128]{2,1,0:T(8,128)S(1)}, u32[]{:S(2)}, u32[]{:S(2)}) collective-permute-start(f32[17,8,128]{2,1,0:T(8,128)S(1)} %pad_maximum_fusion.14), channel_id=1, source_target_pairs={{0,8},{1,9},{2,10},{3,11},{4,12},{5,13},{6,14},{7,15},{8,0},{9,1},... | collective-permute-start | bytes 208904 | tf_op jit(solution)/shard_map/ppermute | solution.py:288
  106.9 7.0 %collective-permute-start.32 = (f32[17,8,128]{2,1,0:T(8,128)S(1)}, f32[17,8,128]{2,1,0:T(8,128)S(1)}, u32[]{:S(2)}, u32[]{:S(2)}) collective-permute-start(f32[17,8,128]{2,1,0:T(8,128)S(1)} %pad_maximum_fusion.14), channel_id=1, source_target_pairs={{0,12},{1,13},{2,14},{3,15},{4,8},{5,9},{6,10},{7,11},{8,4},{9,5},... | collective-permute-start | bytes 208904 | tf_op jit(solution)/shard_map/ppermute | solution.py:288
  108.9 13.7 %collective-permute-start.37 = (f32[64,2,8,128]{3,2,1,0:T(8,128)S(1)}, f32[64,2,8,128]{3,2,1,0:T(8,128)S(1)}, u32[]{:S(2)}, u32[]{:S(2)}) collective-permute-start(f32[64,2,8,128]{3,2,1,0:T(8,128)S(1)} %get-tuple-element.111.mine), channel_id=1, source_target_pairs={{0,16},{16,0},{1,17},{17,1},{2,18},{18,2},{3,19},{19,3},{4,20},{20... | collective-permute-start | bytes 1572872 | tf_op jit(solution)/shard_map/ppermute | solution.py:291
  114.9 6.4 %collective-permute-start.33 = (f32[32,8,128]{2,1,0:T(8,128)S(1)}, f32[32,8,128]{2,1,0:T(8,128)S(1)}, u32[]{:S(2)}, u32[]{:S(2)}) collective-permute-start(f32[32,8,128]{2,1,0:T(8,128)S(1)} %pad_maximum_fusion.11), channel_id=1, source_target_pairs={{0,1},{1,0},{2,3},{3,2},{4,5},{5,4},{6,7},{7,6},{8,9},{9,8},{10,11... | collective-permute-start | bytes 393224 | tf_op jit(solution)/shard_map/ppermute | solution.py:288
  119.1 8.7 %collective-permute-start.36 = (f32[72,8,128]{2,1,0:T(8,128)S(1)}, f32[72,8,128]{2,1,0:T(8,128)S(1)}, u32[]{:S(2)}, u32[]{:S(2)}) collective-permute-start(f32[72,8,128]{2,1,0:T(8,128)S(1)} %constant_dynamic-update-slice_fusion.25.near_b), channel_id=1, source_target_pairs={{0,1},{1,0},{2,3},{3,2},{4,5},{5,4},{6,7},{7,6},{8,9},{9,8},{10,11... | collective-permute-start | bytes 884744 | tf_op jit(solution)/shard_map/ppermute | solution.py:288
  121.4 6.4 %collective-permute-start.34 = (f32[64,8,128]{2,1,0:T(8,128)S(1)}, f32[64,8,128]{2,1,0:T(8,128)S(1)}, u32[]{:S(2)}, u32[]{:S(2)}) collective-permute-start(f32[64,8,128]{2,1,0:T(8,128)S(1)} %constant_dynamic-update-slice_fusion.20.near_a), channel_id=1, source_target_pairs={{0,2},{1,3},{2,0},{3,1},{4,6},{5,7},{6,4},{7,5},{8,10},{9,11},{10,... | collective-permute-start | bytes 786440 | tf_op jit(solution)/shard_map/ppermute | solution.py:288
  131.0 11.5 %collective-permute-start.38 = (f32[64,2,8,128]{3,2,1,0:T(8,128)S(1)}, f32[64,2,8,128]{3,2,1,0:T(8,128)S(1)}, u32[]{:S(2)}, u32[]{:S(2)}) collective-permute-start(f32[64,2,8,128]{3,2,1,0:T(8,128)S(1)} %get-tuple-element.126.mine), channel_id=1, source_target_pairs={{0,16},{16,0},{1,17},{17,1},{2,18},{18,2},{3,19},{19,3},{4,20},{20... | collective-permute-start | bytes 1572872 | tf_op jit(solution)/shard_map/ppermute | solution.py:291
  (8 other events, 71.6 us)

commit v15 on v11

--- a/solution.py
+++ b/solution.py
@@ -39,17 +39,10 @@
 
 def respond(block, load, gamma, energy, answer, last=False):
     ntile, ncase, width = load.shape
-    each = 2
-    total = jnp.zeros((2 * ncase, ntile * width), jnp.float32)
-    for j in range(ntile // each):
-        value = jnp.concatenate([load[j * each + i] for i in range(each)], axis=1)
-        high = value.astype(jnp.bfloat16)
-        low = (value - high.astype(jnp.float32)).astype(jnp.bfloat16)
-        total = total + jnp.dot(
-            jnp.concatenate([high, low], axis=0),
-            block[j * each * width : (j + 1) * each * width, :],
-            preferred_element_type=jnp.float32,
-        )
+    value = jnp.concatenate([load[i] for i in range(ntile)], axis=1)
+    high = value.astype(jnp.bfloat16)
+    low = (value - high.astype(jnp.float32)).astype(jnp.bfloat16)
+    total = jnp.dot(jnp.concatenate([high, low], axis=0), block[...], preferred_element_type=jnp.float32)
     total = total[:ncase] + total[ncase:]
     work = 0.5 * energy
     for i in range(ntile):
@@ -290,10 +283,11 @@
     def sibling(value):
         return lax.ppermute(value, "body", [(i, nbody - 1 - i) for i in range(nbody)])
 
+    small = jnp.stack([plate_owner[:, 0], found_owner[:, 0], slot_pairs[:, 0], slot_pairs[:, 1], active])
+    plate, foundation, plate_slot, found_slot, active = lax.optimization_barrier(small)
     keep = active.astype(jnp.float32)
-    plate, foundation = plate_owner[:, 0], found_owner[:, 0]
     owner, other = jnp.where(side == 0, plate, foundation), jnp.where(side == 0, foundation, plate)
-    slot, other_slot = (jnp.where(side == i, slot_pairs[:, 0], slot_pairs[:, 1]) for i in range(2))
+    slot, other_slot = jnp.where(side == 0, plate_slot, found_slot), jnp.where(side == 0, found_slot, plate_slot)
     index = jnp.arange(npatch, dtype=jnp.int32)
     earlier = (owner[None, :] == owner[:, None]) & (index[None, :] < index[:, None])
     rank = jnp.sum(earlier.astype(jnp.int32), axis=1)

time: 144 us -> 143 us (level)
  other arithmetic: 3.76 us -> 1.6 us
  waiting for transfers between devices: 56.8 us -> 58.7 us
  starting transfers between devices: 47.3 us -> 45.5 us
  local copies, waits for them, and re-layouts: 1 us -> 2.46 us
    ppermute x33, waiting for transfers between devices: 53 us -> 54.9 us  [swap(): return lax.ppermute(value, 'sub', [(i, i ^ far) for i in range(nsub)])]
    ppermute x33, starting transfers between devices: 47.1 us -> 45.3 us  [swap(): return lax.ppermute(value, 'sub', [(i, i ^ far) for i in range(nsub)])]
    another operation x0 -> x2, local copies, waits for them, and re-layouts: none -> 1.46 us  [on_device(): jnp.stack([plate_owner[:, 0], found_owner[:, 0], slot_pairs[:, 0], slot_p...]
where the time goes in v15:
time: 143 us
  waiting for transfers between devices  58.7 us (41%)
  starting transfers between devices  45.5 us (32%)
  Pallas kernels  21.8 us (15%)
  blocking collectives  11.2 us (8%)
  local copies, waits for them, and re-layouts  2.46 us (2%)
  other arithmetic  1.6 us (1%)
    ppermute x33, waiting for transfers between devices, swap(): return lax.ppermute(value, 'sub', [(i, i ^ far) for i in range(nsub)])  54.9 us
    ppermute x33, starting transfers between devices, swap(): return lax.ppermute(value, 'sub', [(i, i ^ far) for i in range(nsub)])  45.3 us
    pallas_call x9, Pallas kernels, call(): pl.pallas_call(kernel, out_shape=tuple(out_shape) if several else out_sha...  18.3 us
    all_to_all x1, blocking collectives, on_device(): lax.all_to_all(own, ('body', 'sub'), split_axis=0, concat_axis=0, tiled=T...  11.2 us
    ppermute x6, waiting for transfers between devices, sibling(): lax.ppermute(value, 'body', [(i, nbody - 1 - i) for i in range(nbody)])  3.77 us
    pallas_call x1, Pallas kernels, on_device(): pl.pallas_call(functools.partial(start_kernel, nh, cut, room, lines, extr...  3.45 us
  transfers between devices with their start and end apart: 39, of which 23 were waited for; matrix products, arithmetic and copies ran while one was open for 1% of the time, Pallas kernels for 4%

profile of v15, /device:TPU:0, one launch (start us, length us, event | category | flops | bytes accessed | tf_op | source)
XLA Modules:
  0.0 142.8 jit_solution(5988607704506488357)
XLA Ops:
  4.2 3.1 %collective-permute-start = (f32[32,8,128]{2,1,0:T(8,128)S(1)}, f32[32,8,128]{2,1,0:T(8,128)S(1)}, u32[]{:S(2)}, u32[]{:S(2)}) collective-permute-start(f32[32,8,128]{2,1,0:T(8,128)S(1)} %get-tuple-element.70), channel_id=1, source_target_pairs={{0,4},{1,5},{2,6},{3,7},{4,0},{5,1},{6,2},{7,3},{8,12},{9,13},{10,... | collective-permute-start | bytes 393224 | tf_op jit(solution)/shard_map/ppermute | solution.py:281
  12.8 2.6 %collective-permute-start.1 = (f32[32,8,128]{2,1,0:T(8,128)S(1)}, f32[32,8,128]{2,1,0:T(8,128)S(1)}, u32[]{:S(2)}, u32[]{:S(2)}) collective-permute-start(f32[32,8,128]{2,1,0:T(8,128)S(1)} %get-tuple-element.71), channel_id=1, source_target_pairs={{0,8},{1,9},{2,10},{3,11},{4,12},{5,13},{6,14},{7,15},{8,0},{9,1},... | collective-permute-start | bytes 393224 | tf_op jit(solution)/shard_map/ppermute | solution.py:281
  15.4 3.5 %shard_map.75.block = bf16[2048,2048]{1,0:T(8,128)(2,1)S(1)} custom-call(bf16[2048,2048]{1,0:T(8,128)(2,1)} %bitcast.118), custom_call_target="tpu_custom_call" | custom-call | bytes 16777216 | tf_op jit(solution)/shard_map/pallas_call | solution.py:25
  18.9 5.1 %collective-permute-done.1.refs_2_ = f32[32,8,128]{2,1,0:T(8,128)S(1)} collective-permute-done((f32[32,8,128]{2,1,0:T(8,128)S(1)}, f32[32,8,128]{2,1,0:T(8,128)S(1)}, u32[]{:S(2)}, u32[]{:S(2)}) %collective-permute-start.1) | collective-permute-done | bytes 131104 | tf_op jit(solution)/shard_map/ppermute | solution.py:281
  24.2 3.1 %collective-permute-start.11 = (f32[44,8,128]{2,1,0:T(8,128)S(1)}, f32[44,8,128]{2,1,0:T(8,128)S(1)}, u32[]{:S(2)}, u32[]{:S(2)}) collective-permute-start(f32[44,8,128]{2,1,0:T(8,128)S(1)} %pad_maximum_fusion.2), channel_id=1, source_target_pairs={{0,12},{1,13},{2,14},{3,15},{4,8},{5,9},{6,10},{7,11},{8,4},{9,5},... | collective-permute-start | bytes 540680 | tf_op jit(solution)/shard_map/ppermute | solution.py:281
  28.9 2.8 %collective-permute-start.8 = (f32[32,8,128]{2,1,0:T(8,128)S(1)}, f32[32,8,128]{2,1,0:T(8,128)S(1)}, u32[]{:S(2)}, u32[]{:S(2)}) collective-permute-start(f32[32,8,128]{2,1,0:T(8,128)S(1)} %pad_maximum_fusion.8), channel_id=1, source_target_pairs={{0,3},{1,2},{2,1},{3,0},{4,7},{5,6},{6,5},{7,4},{8,11},{9,10},{10,... | collective-permute-start | bytes 393224 | tf_op jit(solution)/shard_map/ppermute | solution.py:281
  32.3 2.6 %collective-permute-done.8.refs_6_ = f32[32,8,128]{2,1,0:T(8,128)S(1)} collective-permute-done((f32[32,8,128]{2,1,0:T(8,128)S(1)}, f32[32,8,128]{2,1,0:T(8,128)S(1)}, u32[]{:S(2)}, u32[]{:S(2)}) %collective-permute-start.8) | collective-permute-done | bytes 131104 | tf_op jit(solution)/shard_map/ppermute | solution.py:281
  34.9 1.8 %collective-permute-start.6 = (f32[32,8,128]{2,1,0:T(8,128)S(1)}, f32[32,8,128]{2,1,0:T(8,128)S(1)}, u32[]{:S(2)}, u32[]{:S(2)}) collective-permute-start(f32[32,8,128]{2,1,0:T(8,128)S(1)} %pad_maximum_fusion.6), channel_id=1, source_target_pairs={{0,1},{1,0},{2,3},{3,2},{4,5},{5,4},{6,7},{7,6},{8,9},{9,8},{10,11... | collective-permute-start | bytes 393224 | tf_op jit(solution)/shard_map/ppermute | solution.py:281
  36.7 3.1 %collective-permute-done.6.refs_4_ = f32[32,8,128]{2,1,0:T(8,128)S(1)} collective-permute-done((f32[32,8,128]{2,1,0:T(8,128)S(1)}, f32[32,8,128]{2,1,0:T(8,128)S(1)}, u32[]{:S(2)}, u32[]{:S(2)}) %collective-permute-start.6) | collective-permute-done | bytes 131104 | tf_op jit(solution)/shard_map/ppermute | solution.py:281
  39.9 2.8 %collective-permute-done.10.refs_12_ = f32[44,8,128]{2,1,0:T(8,128)S(1)} collective-permute-done((f32[44,8,128]{2,1,0:T(8,128)S(1)}, f32[44,8,128]{2,1,0:T(8,128)S(1)}, u32[]{:S(2)}, u32[]{:S(2)}) %collective-permute-start.10) | collective-permute-done | bytes 180256 | tf_op jit(solution)/shard_map/ppermute | solution.py:281
  42.7 3.5 %shard_map.76 = (s32[128]{0:T(128)S(1)}, s32[128]{0:T(128)S(1)}, f32[128]{0:T(128)S(1)}, f32[128,2,8,128]{3,2,1,0:T(8,128)S(1)}, f32[32,8,128]{2,1,0:T(8,128)S(1)}, /*index=5*/f32[17,8,128]{2,1,0:T(8,128)S(1)}) custom-call(bf16[2048,2048]{1,0:T(8,128)(2,1)S(1)} %shard_map.75.block, f32[32,8,128]{2,1,0:T(8,128)S(1)} %get-tuple-element.79.refs_0_, ...), custom_call_target="tpu_custom_call" | custom-call | tf_op jit(solution)/shard_map/pallas_call | solution.py:358
  47.6 2.8 %collective-permute-start.14 = (f32[17,8,128]{2,1,0:T(8,128)S(1)}, f32[17,8,128]{2,1,0:T(8,128)S(1)}, u32[]{:S(2)}, u32[]{:S(2)}) collective-permute-start(f32[17,8,128]{2,1,0:T(8,128)S(1)} %pad_maximum_fusion.12), channel_id=1, source_target_pairs={{0,8},{1,9},{2,10},{3,11},{4,12},{5,13},{6,14},{7,15},{8,0},{9,1},... | collective-permute-start | bytes 208904 | tf_op jit(solution)/shard_map/ppermute | solution.py:281
  50.4 1.6 %collective-permute-start.15 = (f32[17,8,128]{2,1,0:T(8,128)S(1)}, f32[17,8,128]{2,1,0:T(8,128)S(1)}, u32[]{:S(2)}, u32[]{:S(2)}) collective-permute-start(f32[17,8,128]{2,1,0:T(8,128)S(1)} %pad_maximum_fusion.12), channel_id=1, source_target_pairs={{0,12},{1,13},{2,14},{3,15},{4,8},{5,9},{6,10},{7,11},{8,4},{9,5},... | collective-permute-start | bytes 208904 | tf_op jit(solution)/shard_map/ppermute | solution.py:281
  53.0 2.7 %collective-permute-done.14 = f32[17,8,128]{2,1,0:T(8,128)S(1)} collective-permute-done((f32[17,8,128]{2,1,0:T(8,128)S(1)}, f32[17,8,128]{2,1,0:T(8,128)S(1)}, u32[]{:S(2)}, u32[]{:S(2)}) %collective-permute-start.14) | collective-permute-done | bytes 69664 | tf_op jit(solution)/shard_map/ppermute | solution.py:281
  56.6 1.6 %collective-permute-start.18 = (f32[36,8,128]{2,1,0:T(8,128)S(1)}, f32[36,8,128]{2,1,0:T(8,128)S(1)}, u32[]{:S(2)}, u32[]{:S(2)}) collective-permute-start(f32[36,8,128]{2,1,0:T(8,128)S(1)} %pad_maximum_fusion.3), channel_id=1, source_target_pairs={{0,2},{1,3},{2,0},{3,1},{4,6},{5,7},{6,4},{7,5},{8,10},{9,11},{10,... | collective-permute-start | bytes 442376 | tf_op jit(solution)/shard_map/ppermute | solution.py:281
  59.8 2.0 %collective-permute-done.18 = f32[36,8,128]{2,1,0:T(8,128)S(1)} collective-permute-done((f32[36,8,128]{2,1,0:T(8,128)S(1)}, f32[36,8,128]{2,1,0:T(8,128)S(1)}, u32[]{:S(2)}, u32[]{:S(2)}) %collective-permute-start.18) | collective-permute-done | bytes 147488 | tf_op jit(solution)/shard_map/ppermute | solution.py:281
  65.0 6.1 %collective-permute-done.17.far_a = f32[64,8,128]{2,1,0:T(8,128)S(1)} collective-permute-done((f32[64,8,128]{2,1,0:T(8,128)S(1)}, f32[64,8,128]{2,1,0:T(8,128)S(1)}, u32[]{:S(2)}, u32[]{:S(2)}) %collective-permute-start.17) | collective-permute-done | bytes 262176 | tf_op jit(solution)/shard_map/ppermute | solution.py:281
  71.1 3.0 %shard_map.77 = (f32[128,2,8,128]{3,2,1,0:T(8,128)S(1)}, f32[128,2,8,128]{3,2,1,0:T(8,128)S(1)}, f32[17,8,128]{2,1,0:T(8,128)S(1)}, f32[64,2,8,128]{3,2,1,0:T(8,128)S(1)}, f32[8,128]{1,0:T(8,128)S(1)}) custom-call(s32[128]{0:T(128)S(1)} %get-tuple-element.87.place, s32[128]{0:T(128)S(1)} %get-tuple-element.88.away, f32[128]{0:T(128)S(1)} %get-tuple-element.89.keep, ...), custom_call_target="tpu_custom_call" | custom-call | tf_op jit(solution)/shard_map/pallas_call | solution.py:25
  76.0 2.3 %collective-permute-start.22 = (f32[17,8,128]{2,1,0:T(8,128)S(1)}, f32[17,8,128]{2,1,0:T(8,128)S(1)}, u32[]{:S(2)}, u32[]{:S(2)}) collective-permute-start(f32[17,8,128]{2,1,0:T(8,128)S(1)} %pad_maximum_fusion.13), channel_id=1, source_target_pairs={{0,8},{1,9},{2,10},{3,11},{4,12},{5,13},{6,14},{7,15},{8,0},{9,1},... | collective-permute-start | bytes 208904 | tf_op jit(solution)/shard_map/ppermute | solution.py:281
  78.2 1.7 %collective-permute-start.23 = (f32[17,8,128]{2,1,0:T(8,128)S(1)}, f32[17,8,128]{2,1,0:T(8,128)S(1)}, u32[]{:S(2)}, u32[]{:S(2)}) collective-permute-start(f32[17,8,128]{2,1,0:T(8,128)S(1)} %pad_maximum_fusion.13), channel_id=1, source_target_pairs={{0,12},{1,13},{2,14},{3,15},{4,8},{5,9},{6,10},{7,11},{8,4},{9,5},... | collective-permute-start | bytes 208904 | tf_op jit(solution)/shard_map/ppermute | solution.py:281
  80.7 4.0 %collective-permute-done.22 = f32[17,8,128]{2,1,0:T(8,128)S(1)} collective-permute-done((f32[17,8,128]{2,1,0:T(8,128)S(1)}, f32[17,8,128]{2,1,0:T(8,128)S(1)}, u32[]{:S(2)}, u32[]{:S(2)}) %collective-permute-start.22) | collective-permute-done | bytes 69664 | tf_op jit(solution)/shard_map/ppermute | solution.py:281
  86.9 3.1 %collective-permute-done.26 = f32[36,8,128]{2,1,0:T(8,128)S(1)} collective-permute-done((f32[36,8,128]{2,1,0:T(8,128)S(1)}, f32[36,8,128]{2,1,0:T(8,128)S(1)}, u32[]{:S(2)}, u32[]{:S(2)}) %collective-permute-start.26) | collective-permute-done | bytes 147488 | tf_op jit(solution)/shard_map/ppermute | solution.py:281
  93.3 5.2 %collective-permute-done.25.far_a = f32[64,8,128]{2,1,0:T(8,128)S(1)} collective-permute-done((f32[64,8,128]{2,1,0:T(8,128)S(1)}, f32[64,8,128]{2,1,0:T(8,128)S(1)}, u32[]{:S(2)}, u32[]{:S(2)}) %collective-permute-start.25) | collective-permute-done | bytes 262176 | tf_op jit(solution)/shard_map/ppermute | solution.py:281
  98.6 3.2 %shard_map.79 = (f32[128,2,8,128]{3,2,1,0:T(8,128)S(1)}, f32[128,2,8,128]{3,2,1,0:T(8,128)S(1)}, f32[17,8,128]{2,1,0:T(8,128)S(1)}, f32[64,2,8,128]{3,2,1,0:T(8,128)S(1)}, f32[8,128]{1,0:T(8,128)S(1)}) custom-call(s32[128]{0:T(128)S(1)} %get-tuple-element.87.place, s32[128]{0:T(128)S(1)} %get-tuple-element.88.away, f32[128]{0:T(128)S(1)} %get-tuple-element.89.keep, ...), custom_call_target="tpu_custom_call" | custom-call | tf_op jit(solution)/shard_map/pallas_call | solution.py:25
  105.6 1.9 %collective-permute-start.32 = (f32[17,8,128]{2,1,0:T(8,128)S(1)}, f32[17,8,128]{2,1,0:T(8,128)S(1)}, u32[]{:S(2)}, u32[]{:S(2)}) collective-permute-start(f32[17,8,128]{2,1,0:T(8,128)S(1)} %pad_maximum_fusion.14), channel_id=1, source_target_pairs={{0,12},{1,13},{2,14},{3,15},{4,8},{5,9},{6,10},{7,11},{8,4},{9,5},... | collective-permute-start | bytes 208904 | tf_op jit(solution)/shard_map/ppermute | solution.py:281
  107.6 5.2 %collective-permute-done.31 = f32[17,8,128]{2,1,0:T(8,128)S(1)} collective-permute-done((f32[17,8,128]{2,1,0:T(8,128)S(1)}, f32[17,8,128]{2,1,0:T(8,128)S(1)}, u32[]{:S(2)}, u32[]{:S(2)}) %collective-permute-start.31) | collective-permute-done | bytes 69664 | tf_op jit(solution)/shard_map/ppermute | solution.py:281
  114.9 3.1 %collective-permute-done.35 = f32[36,8,128]{2,1,0:T(8,128)S(1)} collective-permute-done((f32[36,8,128]{2,1,0:T(8,128)S(1)}, f32[36,8,128]{2,1,0:T(8,128)S(1)}, u32[]{:S(2)}, u32[]{:S(2)}) %collective-permute-start.35) | collective-permute-done | bytes 147488 | tf_op jit(solution)/shard_map/ppermute | solution.py:281
  119.7 1.7 %collective-permute-start.34 = (f32[64,8,128]{2,1,0:T(8,128)S(1)}, f32[64,8,128]{2,1,0:T(8,128)S(1)}, u32[]{:S(2)}, u32[]{:S(2)}) collective-permute-start(f32[64,8,128]{2,1,0:T(8,128)S(1)} %constant_dynamic-update-slice_fusion.20.near_a), channel_id=1, source_target_pairs={{0,2},{1,3},{2,0},{3,1},{4,6},{5,7},{6,4},{7,5},{8,10},{9,11},{10,... | collective-permute-start | bytes 786440 | tf_op jit(solution)/shard_map/ppermute | solution.py:281
  122.5 3.7 %collective-permute-done.34.far_a = f32[64,8,128]{2,1,0:T(8,128)S(1)} collective-permute-done((f32[64,8,128]{2,1,0:T(8,128)S(1)}, f32[64,8,128]{2,1,0:T(8,128)S(1)}, u32[]{:S(2)}, u32[]{:S(2)}) %collective-permute-start.34) | collective-permute-done | bytes 262176 | tf_op jit(solution)/shard_map/ppermute | solution.py:281
  126.2 3.2 %shard_map.81 = (f32[32,8,128]{2,1,0:T(8,128)S(1)}, f32[64,2,8,128]{3,2,1,0:T(8,128)S(1)}, f32[8,128]{1,0:T(8,128)S(1)}) custom-call(s32[128]{0:T(128)S(1)} %get-tuple-element.87.place, s32[128]{0:T(128)S(1)} %get-tuple-element.88.away, f32[128]{0:T(128)S(1)} %get-tuple-element.89.keep, s32[64]{0:T(128)S(1)} %get-tuple-element.90.picked, ...), custom_call_target="tpu_custom_call" | custom-call | tf_op jit(solution)/shard_map/pallas_call | solution.py:25
  129.4 11.2 %all_to_all.5.sums = f32[32,8,128]{2,1,0:T(8,128)S(1)} all-to-all(f32[32,8,128]{2,1,0:T(8,128)S(1)} %get-tuple-element.124), channel_id=1, replica_groups=mesh['body'=2,'sub'=16] {'body','sub'}, dimensions={0} | all-to-all | bytes 262144 | tf_op jit(solution)/shard_map/all_to_all | solution.py:422
  140.6 2.2 %shard_map.82 = f32[8,64,256]{2,1,0:T(8,128)} custom-call(f32[64]{0:T(128)S(1)} %get-tuple-element.207.keep, f32[32,8,128]{2,1,0:T(8,128)S(1)} %all_to_all.5.sums, f32[8,128]{1,0:T(8,128)S(1)} %get-tuple-element.125.known, f32[64,256]{1,0:T(8,128)S(1)} %copy-done, f32[64,2,8,128]{3,2,1,0:T(8,128)S(1)} %get-tuple-element.126.mine, ...), custom_call_target="tpu_custom_call" | custom-call | tf_op jit(solution)/shard_map/pallas_call | solution.py:25
  (137 shorter events, 36.7 us)
Async XLA Ops:
  4.2 11.3 %collective-permute-start = (f32[32,8,128]{2,1,0:T(8,128)S(1)}, f32[32,8,128]{2,1,0:T(8,128)S(1)}, u32[]{:S(2)}, u32[]{:S(2)}) collective-permute-start(f32[32,8,128]{2,1,0:T(8,128)S(1)} %get-tuple-element.70), channel_id=1, source_target_pairs={{0,4},{1,5},{2,6},{3,7},{4,0},{5,1},{6,2},{7,3},{8,12},{9,13},{10,... | collective-permute-start | bytes 393224 | tf_op jit(solution)/shard_map/ppermute | solution.py:281
  9.3 14.8 %collective-permute-start.3 = (f32[44,8,128]{2,1,0:T(8,128)S(1)}, f32[44,8,128]{2,1,0:T(8,128)S(1)}, u32[]{:S(2)}, u32[]{:S(2)}) collective-permute-start(f32[44,8,128]{2,1,0:T(8,128)S(1)} %get-tuple-element.75), channel_id=1, source_target_pairs={{0,1},{1,0},{2,3},{3,2},{4,5},{5,4},{6,7},{7,6},{8,9},{9,8},{10,11... | collective-permute-start | bytes 540680 | tf_op jit(solution)/shard_map/ppermute | solution.py:281
  10.8 13.2 %collective-permute-start.4 = (f32[44,8,128]{2,1,0:T(8,128)S(1)}, f32[44,8,128]{2,1,0:T(8,128)S(1)}, u32[]{:S(2)}, u32[]{:S(2)}) collective-permute-start(f32[44,8,128]{2,1,0:T(8,128)S(1)} %get-tuple-element.76), channel_id=1, source_target_pairs={{0,2},{1,3},{2,0},{3,1},{4,6},{5,7},{6,4},{7,5},{8,10},{9,11},{10,... | collective-permute-start | bytes 540680 | tf_op jit(solution)/shard_map/ppermute | solution.py:281
  12.4 11.7 %collective-permute-start.5 = (f32[44,8,128]{2,1,0:T(8,128)S(1)}, f32[44,8,128]{2,1,0:T(8,128)S(1)}, u32[]{:S(2)}, u32[]{:S(2)}) collective-permute-start(f32[44,8,128]{2,1,0:T(8,128)S(1)} %get-tuple-element.77), channel_id=1, source_target_pairs={{0,3},{1,2},{2,1},{3,0},{4,7},{5,6},{6,5},{7,4},{8,11},{9,10},{10,... | collective-permute-start | bytes 540680 | tf_op jit(solution)/shard_map/ppermute | solution.py:281
  12.8 11.2 %collective-permute-start.1 = (f32[32,8,128]{2,1,0:T(8,128)S(1)}, f32[32,8,128]{2,1,0:T(8,128)S(1)}, u32[]{:S(2)}, u32[]{:S(2)}) collective-permute-start(f32[32,8,128]{2,1,0:T(8,128)S(1)} %get-tuple-element.71), channel_id=1, source_target_pairs={{0,8},{1,9},{2,10},{3,11},{4,12},{5,13},{6,14},{7,15},{8,0},{9,1},... | collective-permute-start | bytes 393224 | tf_op jit(solution)/shard_map/ppermute | solution.py:281
  15.4 8.6 %collective-permute-start.2 = (f32[32,8,128]{2,1,0:T(8,128)S(1)}, f32[32,8,128]{2,1,0:T(8,128)S(1)}, u32[]{:S(2)}, u32[]{:S(2)}) collective-permute-start(f32[32,8,128]{2,1,0:T(8,128)S(1)} %get-tuple-element.72), channel_id=1, source_target_pairs={{0,12},{1,13},{2,14},{3,15},{4,8},{5,9},{6,10},{7,11},{8,4},{9,5},... | collective-permute-start | bytes 393224 | tf_op jit(solution)/shard_map/ppermute | solution.py:281
  24.2 15.7 %collective-permute-start.11 = (f32[44,8,128]{2,1,0:T(8,128)S(1)}, f32[44,8,128]{2,1,0:T(8,128)S(1)}, u32[]{:S(2)}, u32[]{:S(2)}) collective-permute-start(f32[44,8,128]{2,1,0:T(8,128)S(1)} %pad_maximum_fusion.2), channel_id=1, source_target_pairs={{0,12},{1,13},{2,14},{3,15},{4,8},{5,9},{6,10},{7,11},{8,4},{9,5},... | collective-permute-start | bytes 540680 | tf_op jit(solution)/shard_map/ppermute | solution.py:281
  27.3 15.4 %collective-permute-start.10 = (f32[44,8,128]{2,1,0:T(8,128)S(1)}, f32[44,8,128]{2,1,0:T(8,128)S(1)}, u32[]{:S(2)}, u32[]{:S(2)}) collective-permute-start(f32[44,8,128]{2,1,0:T(8,128)S(1)} %pad_maximum_fusion.1), channel_id=1, source_target_pairs={{0,8},{1,9},{2,10},{3,11},{4,12},{5,13},{6,14},{7,15},{8,0},{9,1},... | collective-permute-start | bytes 540680 | tf_op jit(solution)/shard_map/ppermute | solution.py:281
  28.4 14.3 %collective-permute-start.9 = (f32[44,8,128]{2,1,0:T(8,128)S(1)}, f32[44,8,128]{2,1,0:T(8,128)S(1)}, u32[]{:S(2)}, u32[]{:S(2)}) collective-permute-start(f32[44,8,128]{2,1,0:T(8,128)S(1)} %pad_maximum_fusion), channel_id=1, source_target_pairs={{0,4},{1,5},{2,6},{3,7},{4,0},{5,1},{6,2},{7,3},{8,12},{9,13},{10,... | collective-permute-start | bytes 540680 | tf_op jit(solution)/shard_map/ppermute | solution.py:281
  28.9 6.0 %collective-permute-start.8 = (f32[32,8,128]{2,1,0:T(8,128)S(1)}, f32[32,8,128]{2,1,0:T(8,128)S(1)}, u32[]{:S(2)}, u32[]{:S(2)}) collective-permute-start(f32[32,8,128]{2,1,0:T(8,128)S(1)} %pad_maximum_fusion.8), channel_id=1, source_target_pairs={{0,3},{1,2},{2,1},{3,0},{4,7},{5,6},{6,5},{7,4},{8,11},{9,10},{10,... | collective-permute-start | bytes 393224 | tf_op jit(solution)/shard_map/ppermute | solution.py:281
  47.5 5.4 %collective-permute-start.13 = (f32[17,8,128]{2,1,0:T(8,128)S(1)}, f32[17,8,128]{2,1,0:T(8,128)S(1)}, u32[]{:S(2)}, u32[]{:S(2)}) collective-permute-start(f32[17,8,128]{2,1,0:T(8,128)S(1)} %pad_maximum_fusion.12), channel_id=1, source_target_pairs={{0,4},{1,5},{2,6},{3,7},{4,0},{5,1},{6,2},{7,3},{8,12},{9,13},{10,... | collective-permute-start | bytes 208904 | tf_op jit(solution)/shard_map/ppermute | solution.py:281
  47.6 8.0 %collective-permute-start.14 = (f32[17,8,128]{2,1,0:T(8,128)S(1)}, f32[17,8,128]{2,1,0:T(8,128)S(1)}, u32[]{:S(2)}, u32[]{:S(2)}) collective-permute-start(f32[17,8,128]{2,1,0:T(8,128)S(1)} %pad_maximum_fusion.12), channel_id=1, source_target_pairs={{0,8},{1,9},{2,10},{3,11},{4,12},{5,13},{6,14},{7,15},{8,0},{9,1},... | collective-permute-start | bytes 208904 | tf_op jit(solution)/shard_map/ppermute | solution.py:281
  50.4 6.2 %collective-permute-start.15 = (f32[17,8,128]{2,1,0:T(8,128)S(1)}, f32[17,8,128]{2,1,0:T(8,128)S(1)}, u32[]{:S(2)}, u32[]{:S(2)}) collective-permute-start(f32[17,8,128]{2,1,0:T(8,128)S(1)} %pad_maximum_fusion.12), channel_id=1, source_target_pairs={{0,12},{1,13},{2,14},{3,15},{4,8},{5,9},{6,10},{7,11},{8,4},{9,5},... | collective-permute-start | bytes 208904 | tf_op jit(solution)/shard_map/ppermute | solution.py:281
  56.6 5.2 %collective-permute-start.18 = (f32[36,8,128]{2,1,0:T(8,128)S(1)}, f32[36,8,128]{2,1,0:T(8,128)S(1)}, u32[]{:S(2)}, u32[]{:S(2)}) collective-permute-start(f32[36,8,128]{2,1,0:T(8,128)S(1)} %pad_maximum_fusion.3), channel_id=1, source_target_pairs={{0,2},{1,3},{2,0},{3,1},{4,6},{5,7},{6,4},{7,5},{8,10},{9,11},{10,... | collective-permute-start | bytes 442376 | tf_op jit(solution)/shard_map/ppermute | solution.py:281
  58.2 6.4 %collective-permute-start.16 = (f32[32,8,128]{2,1,0:T(8,128)S(1)}, f32[32,8,128]{2,1,0:T(8,128)S(1)}, u32[]{:S(2)}, u32[]{:S(2)}) collective-permute-start(f32[32,8,128]{2,1,0:T(8,128)S(1)} %pad_maximum_fusion.9), channel_id=1, source_target_pairs={{0,1},{1,0},{2,3},{3,2},{4,5},{5,4},{6,7},{7,6},{8,9},{9,8},{10,11... | collective-permute-start | bytes 393224 | tf_op jit(solution)/shard_map/ppermute | solution.py:281
  61.8 9.3 %collective-permute-start.19 = (f32[72,8,128]{2,1,0:T(8,128)S(1)}, f32[72,8,128]{2,1,0:T(8,128)S(1)}, u32[]{:S(2)}, u32[]{:S(2)}) collective-permute-start(f32[72,8,128]{2,1,0:T(8,128)S(1)} %constant_dynamic-update-slice_fusion.5.near_b), channel_id=1, source_target_pairs={{0,1},{1,0},{2,3},{3,2},{4,5},{5,4},{6,7},{7,6},{8,9},{9,8},{10,11... | collective-permute-start | bytes 884744 | tf_op jit(solution)/shard_map/ppermute | solution.py:281
  64.7 6.4 %collective-permute-start.17 = (f32[64,8,128]{2,1,0:T(8,128)S(1)}, f32[64,8,128]{2,1,0:T(8,128)S(1)}, u32[]{:S(2)}, u32[]{:S(2)}) collective-permute-start(f32[64,8,128]{2,1,0:T(8,128)S(1)} %constant_dynamic-update-slice_fusion.near_a), channel_id=1, source_target_pairs={{0,2},{1,3},{2,0},{3,1},{4,6},{5,7},{6,4},{7,5},{8,10},{9,11},{10,... | collective-permute-start | bytes 786440 | tf_op jit(solution)/shard_map/ppermute | solution.py:281
  75.5 5.2 %collective-permute-start.21 = (f32[17,8,128]{2,1,0:T(8,128)S(1)}, f32[17,8,128]{2,1,0:T(8,128)S(1)}, u32[]{:S(2)}, u32[]{:S(2)}) collective-permute-start(f32[17,8,128]{2,1,0:T(8,128)S(1)} %pad_maximum_fusion.13), channel_id=1, source_target_pairs={{0,4},{1,5},{2,6},{3,7},{4,0},{5,1},{6,2},{7,3},{8,12},{9,13},{10,... | collective-permute-start | bytes 208904 | tf_op jit(solution)/shard_map/ppermute | solution.py:281
  76.0 8.8 %collective-permute-start.22 = (f32[17,8,128]{2,1,0:T(8,128)S(1)}, f32[17,8,128]{2,1,0:T(8,128)S(1)}, u32[]{:S(2)}, u32[]{:S(2)}) collective-permute-start(f32[17,8,128]{2,1,0:T(8,128)S(1)} %pad_maximum_fusion.13), channel_id=1, source_target_pairs={{0,8},{1,9},{2,10},{3,11},{4,12},{5,13},{6,14},{7,15},{8,0},{9,1},... | collective-permute-start | bytes 208904 | tf_op jit(solution)/shard_map/ppermute | solution.py:281
  78.2 6.5 %collective-permute-start.23 = (f32[17,8,128]{2,1,0:T(8,128)S(1)}, f32[17,8,128]{2,1,0:T(8,128)S(1)}, u32[]{:S(2)}, u32[]{:S(2)}) collective-permute-start(f32[17,8,128]{2,1,0:T(8,128)S(1)} %pad_maximum_fusion.13), channel_id=1, source_target_pairs={{0,12},{1,13},{2,14},{3,15},{4,8},{5,9},{6,10},{7,11},{8,4},{9,5},... | collective-permute-start | bytes 208904 | tf_op jit(solution)/shard_map/ppermute | solution.py:281
  79.9 12.6 %collective-permute-start.28 = (f32[64,2,8,128]{3,2,1,0:T(8,128)S(1)}, f32[64,2,8,128]{3,2,1,0:T(8,128)S(1)}, u32[]{:S(2)}, u32[]{:S(2)}) collective-permute-start(f32[64,2,8,128]{3,2,1,0:T(8,128)S(1)} %get-tuple-element.98.mine), channel_id=1, source_target_pairs={{0,16},{16,0},{1,17},{17,1},{2,18},{18,2},{3,19},{19,3},{4,20},{20... | collective-permute-start | bytes 1572872 | tf_op jit(solution)/shard_map/ppermute | solution.py:284
  84.8 5.2 %collective-permute-start.26 = (f32[36,8,128]{2,1,0:T(8,128)S(1)}, f32[36,8,128]{2,1,0:T(8,128)S(1)}, u32[]{:S(2)}, u32[]{:S(2)}) collective-permute-start(f32[36,8,128]{2,1,0:T(8,128)S(1)} %pad_maximum_fusion.4), channel_id=1, source_target_pairs={{0,2},{1,3},{2,0},{3,1},{4,6},{5,7},{6,4},{7,5},{8,10},{9,11},{10,... | collective-permute-start | bytes 442376 | tf_op jit(solution)/shard_map/ppermute | solution.py:281
  85.9 6.2 %collective-permute-start.24 = (f32[32,8,128]{2,1,0:T(8,128)S(1)}, f32[32,8,128]{2,1,0:T(8,128)S(1)}, u32[]{:S(2)}, u32[]{:S(2)}) collective-permute-start(f32[32,8,128]{2,1,0:T(8,128)S(1)} %pad_maximum_fusion.10), channel_id=1, source_target_pairs={{0,1},{1,0},{2,3},{3,2},{4,5},{5,4},{6,7},{7,6},{8,9},{9,8},{10,11... | collective-permute-start | bytes 393224 | tf_op jit(solution)/shard_map/ppermute | solution.py:281
  90.0 8.6 %collective-permute-start.27 = (f32[72,8,128]{2,1,0:T(8,128)S(1)}, f32[72,8,128]{2,1,0:T(8,128)S(1)}, u32[]{:S(2)}, u32[]{:S(2)}) collective-permute-start(f32[72,8,128]{2,1,0:T(8,128)S(1)} %constant_dynamic-update-slice_fusion.15.near_b), channel_id=1, source_target_pairs={{0,1},{1,0},{2,3},{3,2},{4,5},{5,4},{6,7},{7,6},{8,9},{9,8},{10,11... | collective-permute-start | bytes 884744 | tf_op jit(solution)/shard_map/ppermute | solution.py:281
  92.1 6.4 %collective-permute-start.25 = (f32[64,8,128]{2,1,0:T(8,128)S(1)}, f32[64,8,128]{2,1,0:T(8,128)S(1)}, u32[]{:S(2)}, u32[]{:S(2)}) collective-permute-start(f32[64,8,128]{2,1,0:T(8,128)S(1)} %constant_dynamic-update-slice_fusion.10.near_a), channel_id=1, source_target_pairs={{0,2},{1,3},{2,0},{3,1},{4,6},{5,7},{6,4},{7,5},{8,10},{9,11},{10,... | collective-permute-start | bytes 786440 | tf_op jit(solution)/shard_map/ppermute | solution.py:281
  104.3 8.5 %collective-permute-start.31 = (f32[17,8,128]{2,1,0:T(8,128)S(1)}, f32[17,8,128]{2,1,0:T(8,128)S(1)}, u32[]{:S(2)}, u32[]{:S(2)}) collective-permute-start(f32[17,8,128]{2,1,0:T(8,128)S(1)} %pad_maximum_fusion.14), channel_id=1, source_target_pairs={{0,8},{1,9},{2,10},{3,11},{4,12},{5,13},{6,14},{7,15},{8,0},{9,1},... | collective-permute-start | bytes 208904 | tf_op jit(solution)/shard_map/ppermute | solution.py:281
  105.6 7.2 %collective-permute-start.32 = (f32[17,8,128]{2,1,0:T(8,128)S(1)}, f32[17,8,128]{2,1,0:T(8,128)S(1)}, u32[]{:S(2)}, u32[]{:S(2)}) collective-permute-start(f32[17,8,128]{2,1,0:T(8,128)S(1)} %pad_maximum_fusion.14), channel_id=1, source_target_pairs={{0,12},{1,13},{2,14},{3,15},{4,8},{5,9},{6,10},{7,11},{8,4},{9,5},... | collective-permute-start | bytes 208904 | tf_op jit(solution)/shard_map/ppermute | solution.py:281
  107.5 14.0 %collective-permute-start.37 = (f32[64,2,8,128]{3,2,1,0:T(8,128)S(1)}, f32[64,2,8,128]{3,2,1,0:T(8,128)S(1)}, u32[]{:S(2)}, u32[]{:S(2)}) collective-permute-start(f32[64,2,8,128]{3,2,1,0:T(8,128)S(1)} %get-tuple-element.111.mine), channel_id=1, source_target_pairs={{0,16},{16,0},{1,17},{17,1},{2,18},{18,2},{3,19},{19,3},{4,20},{20... | collective-permute-start | bytes 1572872 | tf_op jit(solution)/shard_map/ppermute | solution.py:284
  113.6 6.1 %collective-permute-start.33 = (f32[32,8,128]{2,1,0:T(8,128)S(1)}, f32[32,8,128]{2,1,0:T(8,128)S(1)}, u32[]{:S(2)}, u32[]{:S(2)}) collective-permute-start(f32[32,8,128]{2,1,0:T(8,128)S(1)} %pad_maximum_fusion.11), channel_id=1, source_target_pairs={{0,1},{1,0},{2,3},{3,2},{4,5},{5,4},{6,7},{7,6},{8,9},{9,8},{10,11... | collective-permute-start | bytes 393224 | tf_op jit(solution)/shard_map/ppermute | solution.py:281
  118.0 8.1 %collective-permute-start.36 = (f32[72,8,128]{2,1,0:T(8,128)S(1)}, f32[72,8,128]{2,1,0:T(8,128)S(1)}, u32[]{:S(2)}, u32[]{:S(2)}) collective-permute-start(f32[72,8,128]{2,1,0:T(8,128)S(1)} %constant_dynamic-update-slice_fusion.25.near_b), channel_id=1, source_target_pairs={{0,1},{1,0},{2,3},{3,2},{4,5},{5,4},{6,7},{7,6},{8,9},{9,8},{10,11... | collective-permute-start | bytes 884744 | tf_op jit(solution)/shard_map/ppermute | solution.py:281
  119.7 6.4 %collective-permute-start.34 = (f32[64,8,128]{2,1,0:T(8,128)S(1)}, f32[64,8,128]{2,1,0:T(8,128)S(1)}, u32[]{:S(2)}, u32[]{:S(2)}) collective-permute-start(f32[64,8,128]{2,1,0:T(8,128)S(1)} %constant_dynamic-update-slice_fusion.20.near_a), channel_id=1, source_target_pairs={{0,2},{1,3},{2,0},{3,1},{4,6},{5,7},{6,4},{7,5},{8,10},{9,11},{10,... | collective-permute-start | bytes 786440 | tf_op jit(solution)/shard_map/ppermute | solution.py:281
  129.4 11.2 %collective-permute-start.38 = (f32[64,2,8,128]{3,2,1,0:T(8,128)S(1)}, f32[64,2,8,128]{3,2,1,0:T(8,128)S(1)}, u32[]{:S(2)}, u32[]{:S(2)}) collective-permute-start(f32[64,2,8,128]{3,2,1,0:T(8,128)S(1)} %get-tuple-element.126.mine), channel_id=1, source_target_pairs={{0,16},{16,0},{1,17},{17,1},{2,18},{18,2},{3,19},{19,3},{4,20},{20... | collective-permute-start | bytes 1572872 | tf_op jit(solution)/shard_map/ppermute | solution.py:284
  (8 other events, 69.8 us)

commit v16 on v15

--- a/solution.py
+++ b/solution.py
@@ -343,7 +343,8 @@
         scratch=[pltpu.SemaphoreType.DMA((nslot,))],
         cost=pl.CostEstimate(flops=0, bytes_accessed=4 * block.size, transcendentals=0),
     )
-    a_z, b_near, block = lax.optimization_barrier((a_z, b_near, block))
+    a_z, b_near, block = lax.optimization_barrier((a_z[::-1], b_near, block))
+    a_z = a_z[::-1]
     b_far = [
         swap(jnp.concatenate([part[z * second : (z + 1) * second] for part in b_near]), 4 * z)
         for z in range(1, nz)
@@ -393,6 +394,7 @@
             lists = update(step - 1, lists, known, part)
         spread_out = jnp.concatenate([spread_out[: per - 1], own[per - 1 :] + spread_out[per - 1 :]])
         parts = [spread_out] + [swap(spread_out, 4 * z) for z in range(1, nz)]
+        parts = lax.optimization_barrier(parts[::-1])[::-1]
         a = jnp.concatenate([part[:half] for part in parts])
         b = jnp.concatenate([part[half:] for part in parts])
         far_a, far_b = swap(a, 1), swap(b, 2)

time: 143 us -> 140 us (0.979)
  waiting for transfers between devices: 58.7 us -> 53.7 us
    ppermute x33, waiting for transfers between devices: 54.9 us -> 50 us  [swap(): return lax.ppermute(value, 'sub', [(i, i ^ far) for i in range(nsub)])]
  transfers between devices with their start and end apart: 39 -> 39, of which waited for: 23 -> 21; matrix products, arithmetic and copies ran while one was open for 1% -> 1% of each run, Pallas kernels for 4% -> 4%
where the time goes in v16:
time: 140 us
  waiting for transfers between devices  53.7 us (38%)
  starting transfers between devices  46.6 us (33%)
  Pallas kernels  21.8 us (16%)
  blocking collectives  11.8 us (8%)
  local copies, waits for them, and re-layouts  2.49 us (2%)
  other arithmetic  1.58 us (1%)
    ppermute x33, waiting for transfers between devices, swap(): return lax.ppermute(value, 'sub', [(i, i ^ far) for i in range(nsub)])  50 us
    ppermute x33, starting transfers between devices, swap(): return lax.ppermute(value, 'sub', [(i, i ^ far) for i in range(nsub)])  46.4 us
    pallas_call x9, Pallas kernels, call(): pl.pallas_call(kernel, out_shape=tuple(out_shape) if several else out_sha...  18.3 us
    all_to_all x1, blocking collectives, on_device(): lax.all_to_all(own, ('body', 'sub'), split_axis=0, concat_axis=0, tiled=T...  11.8 us
    ppermute x6, waiting for transfers between devices, sibling(): lax.ppermute(value, 'body', [(i, nbody - 1 - i) for i in range(nbody)])  3.77 us
    pallas_call x1, Pallas kernels, on_device(): pl.pallas_call(functools.partial(start_kernel, nh, cut, room, lines, extr...  3.46 us
  transfers between devices with their start and end apart: 39, of which 21 were waited for; matrix products, arithmetic and copies ran while one was open for 1% of the time, Pallas kernels for 4%

profile of v16, /device:TPU:0, one launch (start us, length us, event | category | flops | bytes accessed | tf_op | source)
XLA Modules:
  0.0 139.6 jit_solution(17171274978799961341)
XLA Ops:
  4.2 5.1 %collective-permute-start = (f32[32,8,128]{2,1,0:T(8,128)S(1)}, f32[32,8,128]{2,1,0:T(8,128)S(1)}, u32[]{:S(2)}, u32[]{:S(2)}) collective-permute-start(f32[32,8,128]{2,1,0:T(8,128)S(1)} %get-tuple-element.81), channel_id=1, source_target_pairs={{0,12},{1,13},{2,14},{3,15},{4,8},{5,9},{6,10},{7,11},{8,4},{9,5},... | collective-permute-start | bytes 393224 | tf_op jit(solution)/shard_map/ppermute | solution.py:281
  15.5 3.5 %shard_map.75.block = bf16[2048,2048]{1,0:T(8,128)(2,1)S(1)} custom-call(bf16[2048,2048]{1,0:T(8,128)(2,1)} %bitcast.118), custom_call_target="tpu_custom_call" | custom-call | bytes 16777216 | tf_op jit(solution)/shard_map/pallas_call | solution.py:25
  18.9 2.8 %collective-permute-done.1.refs_2_ = f32[32,8,128]{2,1,0:T(8,128)S(1)} collective-permute-done((f32[32,8,128]{2,1,0:T(8,128)S(1)}, f32[32,8,128]{2,1,0:T(8,128)S(1)}, u32[]{:S(2)}, u32[]{:S(2)}) %collective-permute-start.1) | collective-permute-done | bytes 131104 | tf_op jit(solution)/shard_map/ppermute | solution.py:281
  23.9 3.3 %collective-permute-start.9 = (f32[44,8,128]{2,1,0:T(8,128)S(1)}, f32[44,8,128]{2,1,0:T(8,128)S(1)}, u32[]{:S(2)}, u32[]{:S(2)}) collective-permute-start(f32[44,8,128]{2,1,0:T(8,128)S(1)} %pad_maximum_fusion), channel_id=1, source_target_pairs={{0,4},{1,5},{2,6},{3,7},{4,0},{5,1},{6,2},{7,3},{8,12},{9,13},{10,... | collective-permute-start | bytes 540680 | tf_op jit(solution)/shard_map/ppermute | solution.py:281
  27.3 1.9 %collective-permute-start.8 = (f32[32,8,128]{2,1,0:T(8,128)S(1)}, f32[32,8,128]{2,1,0:T(8,128)S(1)}, u32[]{:S(2)}, u32[]{:S(2)}) collective-permute-start(f32[32,8,128]{2,1,0:T(8,128)S(1)} %pad_maximum_fusion.8), channel_id=1, source_target_pairs={{0,3},{1,2},{2,1},{3,0},{4,7},{5,6},{6,5},{7,4},{8,11},{9,10},{10,... | collective-permute-start | bytes 393224 | tf_op jit(solution)/shard_map/ppermute | solution.py:281
  30.1 3.9 %collective-permute-done.8.refs_6_ = f32[32,8,128]{2,1,0:T(8,128)S(1)} collective-permute-done((f32[32,8,128]{2,1,0:T(8,128)S(1)}, f32[32,8,128]{2,1,0:T(8,128)S(1)}, u32[]{:S(2)}, u32[]{:S(2)}) %collective-permute-start.8) | collective-permute-done | bytes 131104 | tf_op jit(solution)/shard_map/ppermute | solution.py:281
  34.9 4.0 %collective-permute-done.6.refs_4_ = f32[32,8,128]{2,1,0:T(8,128)S(1)} collective-permute-done((f32[32,8,128]{2,1,0:T(8,128)S(1)}, f32[32,8,128]{2,1,0:T(8,128)S(1)}, u32[]{:S(2)}, u32[]{:S(2)}) %collective-permute-start.6) | collective-permute-done | bytes 131104 | tf_op jit(solution)/shard_map/ppermute | solution.py:281
  39.0 3.5 %shard_map.76 = (s32[128]{0:T(128)S(1)}, s32[128]{0:T(128)S(1)}, f32[128]{0:T(128)S(1)}, f32[128,2,8,128]{3,2,1,0:T(8,128)S(1)}, f32[32,8,128]{2,1,0:T(8,128)S(1)}, /*index=5*/f32[17,8,128]{2,1,0:T(8,128)S(1)}) custom-call(bf16[2048,2048]{1,0:T(8,128)(2,1)S(1)} %shard_map.75.block, f32[32,8,128]{2,1,0:T(8,128)S(1)} %get-tuple-element.91.refs_0_, ...), custom_call_target="tpu_custom_call" | custom-call | tf_op jit(solution)/shard_map/pallas_call | solution.py:359
  43.8 1.9 %collective-permute-start.13 = (f32[17,8,128]{2,1,0:T(8,128)S(1)}, f32[17,8,128]{2,1,0:T(8,128)S(1)}, u32[]{:S(2)}, u32[]{:S(2)}) collective-permute-start(f32[17,8,128]{2,1,0:T(8,128)S(1)} %pad_maximum_fusion.12), channel_id=1, source_target_pairs={{0,12},{1,13},{2,14},{3,15},{4,8},{5,9},{6,10},{7,11},{8,4},{9,5},... | collective-permute-start | bytes 208904 | tf_op jit(solution)/shard_map/ppermute | solution.py:281
  45.7 2.6 %collective-permute-start.15 = (f32[17,8,128]{2,1,0:T(8,128)S(1)}, f32[17,8,128]{2,1,0:T(8,128)S(1)}, u32[]{:S(2)}, u32[]{:S(2)}) collective-permute-start(f32[17,8,128]{2,1,0:T(8,128)S(1)} %pad_maximum_fusion.12), channel_id=1, source_target_pairs={{0,4},{1,5},{2,6},{3,7},{4,0},{5,1},{6,2},{7,3},{8,12},{9,13},{10,... | collective-permute-start | bytes 208904 | tf_op jit(solution)/shard_map/ppermute | solution.py:281
  48.3 2.5 %collective-permute-done.13 = f32[17,8,128]{2,1,0:T(8,128)S(1)} collective-permute-done((f32[17,8,128]{2,1,0:T(8,128)S(1)}, f32[17,8,128]{2,1,0:T(8,128)S(1)}, u32[]{:S(2)}, u32[]{:S(2)}) %collective-permute-start.13) | collective-permute-done | bytes 69664 | tf_op jit(solution)/shard_map/ppermute | solution.py:281
  50.8 2.1 %collective-permute-done.14 = f32[17,8,128]{2,1,0:T(8,128)S(1)} collective-permute-done((f32[17,8,128]{2,1,0:T(8,128)S(1)}, f32[17,8,128]{2,1,0:T(8,128)S(1)}, u32[]{:S(2)}, u32[]{:S(2)}) %collective-permute-start.14) | collective-permute-done | bytes 69664 | tf_op jit(solution)/shard_map/ppermute | solution.py:281
  55.4 3.5 %collective-permute-done.18 = f32[36,8,128]{2,1,0:T(8,128)S(1)} collective-permute-done((f32[36,8,128]{2,1,0:T(8,128)S(1)}, f32[36,8,128]{2,1,0:T(8,128)S(1)}, u32[]{:S(2)}, u32[]{:S(2)}) %collective-permute-start.18) | collective-permute-done | bytes 147488 | tf_op jit(solution)/shard_map/ppermute | solution.py:281
  61.2 5.8 %collective-permute-done.17.far_a = f32[64,8,128]{2,1,0:T(8,128)S(1)} collective-permute-done((f32[64,8,128]{2,1,0:T(8,128)S(1)}, f32[64,8,128]{2,1,0:T(8,128)S(1)}, u32[]{:S(2)}, u32[]{:S(2)}) %collective-permute-start.17) | collective-permute-done | bytes 262176 | tf_op jit(solution)/shard_map/ppermute | solution.py:281
  67.0 3.0 %shard_map.77 = (f32[128,2,8,128]{3,2,1,0:T(8,128)S(1)}, f32[128,2,8,128]{3,2,1,0:T(8,128)S(1)}, f32[17,8,128]{2,1,0:T(8,128)S(1)}, f32[64,2,8,128]{3,2,1,0:T(8,128)S(1)}, f32[8,128]{1,0:T(8,128)S(1)}) custom-call(s32[128]{0:T(128)S(1)} %get-tuple-element.99.place, s32[128]{0:T(128)S(1)} %get-tuple-element.100.away, f32[128]{0:T(128)S(1)} %get-tuple-element.101.keep, ...), custom_call_target="tpu_custom_call" | custom-call | tf_op jit(solution)/shard_map/pallas_call | solution.py:25
  71.3 2.4 %collective-permute-start.21 = (f32[17,8,128]{2,1,0:T(8,128)S(1)}, f32[17,8,128]{2,1,0:T(8,128)S(1)}, u32[]{:S(2)}, u32[]{:S(2)}) collective-permute-start(f32[17,8,128]{2,1,0:T(8,128)S(1)} %pad_maximum_fusion.13), channel_id=1, source_target_pairs={{0,12},{1,13},{2,14},{3,15},{4,8},{5,9},{6,10},{7,11},{8,4},{9,5},... | collective-permute-start | bytes 208904 | tf_op jit(solution)/shard_map/ppermute | solution.py:281
  73.8 2.0 %collective-permute-start.23 = (f32[17,8,128]{2,1,0:T(8,128)S(1)}, f32[17,8,128]{2,1,0:T(8,128)S(1)}, u32[]{:S(2)}, u32[]{:S(2)}) collective-permute-start(f32[17,8,128]{2,1,0:T(8,128)S(1)} %pad_maximum_fusion.13), channel_id=1, source_target_pairs={{0,4},{1,5},{2,6},{3,7},{4,0},{5,1},{6,2},{7,3},{8,12},{9,13},{10,... | collective-permute-start | bytes 208904 | tf_op jit(solution)/shard_map/ppermute | solution.py:281
  75.8 2.5 %collective-permute-done.21 = f32[17,8,128]{2,1,0:T(8,128)S(1)} collective-permute-done((f32[17,8,128]{2,1,0:T(8,128)S(1)}, f32[17,8,128]{2,1,0:T(8,128)S(1)}, u32[]{:S(2)}, u32[]{:S(2)}) %collective-permute-start.21) | collective-permute-done | bytes 69664 | tf_op jit(solution)/shard_map/ppermute | solution.py:281
  78.3 2.1 %collective-permute-done.22 = f32[17,8,128]{2,1,0:T(8,128)S(1)} collective-permute-done((f32[17,8,128]{2,1,0:T(8,128)S(1)}, f32[17,8,128]{2,1,0:T(8,128)S(1)}, u32[]{:S(2)}, u32[]{:S(2)}) %collective-permute-start.22) | collective-permute-done | bytes 69664 | tf_op jit(solution)/shard_map/ppermute | solution.py:281
  83.3 3.0 %collective-permute-done.26 = f32[36,8,128]{2,1,0:T(8,128)S(1)} collective-permute-done((f32[36,8,128]{2,1,0:T(8,128)S(1)}, f32[36,8,128]{2,1,0:T(8,128)S(1)}, u32[]{:S(2)}, u32[]{:S(2)}) %collective-permute-start.26) | collective-permute-done | bytes 147488 | tf_op jit(solution)/shard_map/ppermute | solution.py:281
  87.4 1.8 %collective-permute-start.25 = (f32[64,8,128]{2,1,0:T(8,128)S(1)}, f32[64,8,128]{2,1,0:T(8,128)S(1)}, u32[]{:S(2)}, u32[]{:S(2)}) collective-permute-start(f32[64,8,128]{2,1,0:T(8,128)S(1)} %constant_dynamic-update-slice_fusion.10.near_a), channel_id=1, source_target_pairs={{0,2},{1,3},{2,0},{3,1},{4,6},{5,7},{6,4},{7,5},{8,10},{9,11},{10,... | collective-permute-start | bytes 786440 | tf_op jit(solution)/shard_map/ppermute | solution.py:281
  90.0 4.5 %collective-permute-done.25.far_a = f32[64,8,128]{2,1,0:T(8,128)S(1)} collective-permute-done((f32[64,8,128]{2,1,0:T(8,128)S(1)}, f32[64,8,128]{2,1,0:T(8,128)S(1)}, u32[]{:S(2)}, u32[]{:S(2)}) %collective-permute-start.25) | collective-permute-done | bytes 262176 | tf_op jit(solution)/shard_map/ppermute | solution.py:281
  94.6 3.2 %shard_map.79 = (f32[128,2,8,128]{3,2,1,0:T(8,128)S(1)}, f32[128,2,8,128]{3,2,1,0:T(8,128)S(1)}, f32[17,8,128]{2,1,0:T(8,128)S(1)}, f32[64,2,8,128]{3,2,1,0:T(8,128)S(1)}, f32[8,128]{1,0:T(8,128)S(1)}) custom-call(s32[128]{0:T(128)S(1)} %get-tuple-element.99.place, s32[128]{0:T(128)S(1)} %get-tuple-element.100.away, f32[128]{0:T(128)S(1)} %get-tuple-element.101.keep, ...), custom_call_target="tpu_custom_call" | custom-call | tf_op jit(solution)/shard_map/pallas_call | solution.py:25
  99.0 2.4 %collective-permute-start.30 = (f32[17,8,128]{2,1,0:T(8,128)S(1)}, f32[17,8,128]{2,1,0:T(8,128)S(1)}, u32[]{:S(2)}, u32[]{:S(2)}) collective-permute-start(f32[17,8,128]{2,1,0:T(8,128)S(1)} %pad_maximum_fusion.14), channel_id=1, source_target_pairs={{0,12},{1,13},{2,14},{3,15},{4,8},{5,9},{6,10},{7,11},{8,4},{9,5},... | collective-permute-start | bytes 208904 | tf_op jit(solution)/shard_map/ppermute | solution.py:281
  101.4 2.0 %collective-permute-start.32 = (f32[17,8,128]{2,1,0:T(8,128)S(1)}, f32[17,8,128]{2,1,0:T(8,128)S(1)}, u32[]{:S(2)}, u32[]{:S(2)}) collective-permute-start(f32[17,8,128]{2,1,0:T(8,128)S(1)} %pad_maximum_fusion.14), channel_id=1, source_target_pairs={{0,4},{1,5},{2,6},{3,7},{4,0},{5,1},{6,2},{7,3},{8,12},{9,13},{10,... | collective-permute-start | bytes 208904 | tf_op jit(solution)/shard_map/ppermute | solution.py:281
  103.5 2.5 %collective-permute-done.30 = f32[17,8,128]{2,1,0:T(8,128)S(1)} collective-permute-done((f32[17,8,128]{2,1,0:T(8,128)S(1)}, f32[17,8,128]{2,1,0:T(8,128)S(1)}, u32[]{:S(2)}, u32[]{:S(2)}) %collective-permute-start.30) | collective-permute-done | bytes 69664 | tf_op jit(solution)/shard_map/ppermute | solution.py:281
  106.0 2.1 %collective-permute-done.31 = f32[17,8,128]{2,1,0:T(8,128)S(1)} collective-permute-done((f32[17,8,128]{2,1,0:T(8,128)S(1)}, f32[17,8,128]{2,1,0:T(8,128)S(1)}, u32[]{:S(2)}, u32[]{:S(2)}) %collective-permute-start.31) | collective-permute-done | bytes 69664 | tf_op jit(solution)/shard_map/ppermute | solution.py:281
  111.0 3.0 %collective-permute-done.35 = f32[36,8,128]{2,1,0:T(8,128)S(1)} collective-permute-done((f32[36,8,128]{2,1,0:T(8,128)S(1)}, f32[36,8,128]{2,1,0:T(8,128)S(1)}, u32[]{:S(2)}, u32[]{:S(2)}) %collective-permute-start.35) | collective-permute-done | bytes 147488 | tf_op jit(solution)/shard_map/ppermute | solution.py:281
  117.8 4.6 %collective-permute-done.34.far_a = f32[64,8,128]{2,1,0:T(8,128)S(1)} collective-permute-done((f32[64,8,128]{2,1,0:T(8,128)S(1)}, f32[64,8,128]{2,1,0:T(8,128)S(1)}, u32[]{:S(2)}, u32[]{:S(2)}) %collective-permute-start.34) | collective-permute-done | bytes 262176 | tf_op jit(solution)/shard_map/ppermute | solution.py:281
  122.4 3.2 %shard_map.81 = (f32[32,8,128]{2,1,0:T(8,128)S(1)}, f32[64,2,8,128]{3,2,1,0:T(8,128)S(1)}, f32[8,128]{1,0:T(8,128)S(1)}) custom-call(s32[128]{0:T(128)S(1)} %get-tuple-element.99.place, s32[128]{0:T(128)S(1)} %get-tuple-element.100.away, f32[128]{0:T(128)S(1)} %get-tuple-element.101.keep, s32[64]{0:T(128)S(1)} %get-tuple-element.102.picked, ...), custom_call_target="tpu_custom_call" | custom-call | tf_op jit(solution)/shard_map/pallas_call | solution.py:25
  125.6 11.8 %all_to_all.5.sums = f32[32,8,128]{2,1,0:T(8,128)S(1)} all-to-all(f32[32,8,128]{2,1,0:T(8,128)S(1)} %get-tuple-element.148), channel_id=1, replica_groups=mesh['body'=2,'sub'=16] {'body','sub'}, dimensions={0} | all-to-all | bytes 262144 | tf_op jit(solution)/shard_map/all_to_all | solution.py:424
  137.5 2.2 %shard_map.82 = f32[8,64,256]{2,1,0:T(8,128)} custom-call(f32[64]{0:T(128)S(1)} %get-tuple-element.231.keep, f32[32,8,128]{2,1,0:T(8,128)S(1)} %all_to_all.5.sums, f32[8,128]{1,0:T(8,128)S(1)} %get-tuple-element.149.known, f32[64,256]{1,0:T(8,128)S(1)} %copy-done, f32[64,2,8,128]{3,2,1,0:T(8,128)S(1)} %get-tuple-element.150.mine, ...), custom_call_target="tpu_custom_call" | custom-call | tf_op jit(solution)/shard_map/pallas_call | solution.py:25
  (137 shorter events, 34.3 us)
Async XLA Ops:
  4.2 10.7 %collective-permute-start = (f32[32,8,128]{2,1,0:T(8,128)S(1)}, f32[32,8,128]{2,1,0:T(8,128)S(1)}, u32[]{:S(2)}, u32[]{:S(2)}) collective-permute-start(f32[32,8,128]{2,1,0:T(8,128)S(1)} %get-tuple-element.81), channel_id=1, source_target_pairs={{0,12},{1,13},{2,14},{3,15},{4,8},{5,9},{6,10},{7,11},{8,4},{9,5},... | collective-permute-start | bytes 393224 | tf_op jit(solution)/shard_map/ppermute | solution.py:281
  11.3 10.5 %collective-permute-start.3 = (f32[44,8,128]{2,1,0:T(8,128)S(1)}, f32[44,8,128]{2,1,0:T(8,128)S(1)}, u32[]{:S(2)}, u32[]{:S(2)}) collective-permute-start(f32[44,8,128]{2,1,0:T(8,128)S(1)} %get-tuple-element.87), channel_id=1, source_target_pairs={{0,1},{1,0},{2,3},{3,2},{4,5},{5,4},{6,7},{7,6},{8,9},{9,8},{10,11... | collective-permute-start | bytes 540680 | tf_op jit(solution)/shard_map/ppermute | solution.py:281
  12.9 9.6 %collective-permute-start.4 = (f32[44,8,128]{2,1,0:T(8,128)S(1)}, f32[44,8,128]{2,1,0:T(8,128)S(1)}, u32[]{:S(2)}, u32[]{:S(2)}) collective-permute-start(f32[44,8,128]{2,1,0:T(8,128)S(1)} %get-tuple-element.88), channel_id=1, source_target_pairs={{0,2},{1,3},{2,0},{3,1},{4,6},{5,7},{6,4},{7,5},{8,10},{9,11},{10,... | collective-permute-start | bytes 540680 | tf_op jit(solution)/shard_map/ppermute | solution.py:281
  14.4 8.1 %collective-permute-start.5 = (f32[44,8,128]{2,1,0:T(8,128)S(1)}, f32[44,8,128]{2,1,0:T(8,128)S(1)}, u32[]{:S(2)}, u32[]{:S(2)}) collective-permute-start(f32[44,8,128]{2,1,0:T(8,128)S(1)} %get-tuple-element.89), channel_id=1, source_target_pairs={{0,3},{1,2},{2,1},{3,0},{4,7},{5,6},{6,5},{7,4},{8,11},{9,10},{10,... | collective-permute-start | bytes 540680 | tf_op jit(solution)/shard_map/ppermute | solution.py:281
  14.9 6.9 %collective-permute-start.1 = (f32[32,8,128]{2,1,0:T(8,128)S(1)}, f32[32,8,128]{2,1,0:T(8,128)S(1)}, u32[]{:S(2)}, u32[]{:S(2)}) collective-permute-start(f32[32,8,128]{2,1,0:T(8,128)S(1)} %get-tuple-element.82), channel_id=1, source_target_pairs={{0,8},{1,9},{2,10},{3,11},{4,12},{5,13},{6,14},{7,15},{8,0},{9,1},... | collective-permute-start | bytes 393224 | tf_op jit(solution)/shard_map/ppermute | solution.py:281
  14.9 6.9 %collective-permute-start.2 = (f32[32,8,128]{2,1,0:T(8,128)S(1)}, f32[32,8,128]{2,1,0:T(8,128)S(1)}, u32[]{:S(2)}, u32[]{:S(2)}) collective-permute-start(f32[32,8,128]{2,1,0:T(8,128)S(1)} %get-tuple-element.83), channel_id=1, source_target_pairs={{0,4},{1,5},{2,6},{3,7},{4,0},{5,1},{6,2},{7,3},{8,12},{9,13},{10,... | collective-permute-start | bytes 393224 | tf_op jit(solution)/shard_map/ppermute | solution.py:281
  22.6 16.4 %collective-permute-start.11 = (f32[44,8,128]{2,1,0:T(8,128)S(1)}, f32[44,8,128]{2,1,0:T(8,128)S(1)}, u32[]{:S(2)}, u32[]{:S(2)}) collective-permute-start(f32[44,8,128]{2,1,0:T(8,128)S(1)} %pad_maximum_fusion.2), channel_id=1, source_target_pairs={{0,12},{1,13},{2,14},{3,15},{4,8},{5,9},{6,10},{7,11},{8,4},{9,5},... | collective-permute-start | bytes 540680 | tf_op jit(solution)/shard_map/ppermute | solution.py:281
  23.5 15.5 %collective-permute-start.10 = (f32[44,8,128]{2,1,0:T(8,128)S(1)}, f32[44,8,128]{2,1,0:T(8,128)S(1)}, u32[]{:S(2)}, u32[]{:S(2)}) collective-permute-start(f32[44,8,128]{2,1,0:T(8,128)S(1)} %pad_maximum_fusion.1), channel_id=1, source_target_pairs={{0,8},{1,9},{2,10},{3,11},{4,12},{5,13},{6,14},{7,15},{8,0},{9,1},... | collective-permute-start | bytes 540680 | tf_op jit(solution)/shard_map/ppermute | solution.py:281
  23.9 15.1 %collective-permute-start.9 = (f32[44,8,128]{2,1,0:T(8,128)S(1)}, f32[44,8,128]{2,1,0:T(8,128)S(1)}, u32[]{:S(2)}, u32[]{:S(2)}) collective-permute-start(f32[44,8,128]{2,1,0:T(8,128)S(1)} %pad_maximum_fusion), channel_id=1, source_target_pairs={{0,4},{1,5},{2,6},{3,7},{4,0},{5,1},{6,2},{7,3},{8,12},{9,13},{10,... | collective-permute-start | bytes 540680 | tf_op jit(solution)/shard_map/ppermute | solution.py:281
  27.3 6.8 %collective-permute-start.8 = (f32[32,8,128]{2,1,0:T(8,128)S(1)}, f32[32,8,128]{2,1,0:T(8,128)S(1)}, u32[]{:S(2)}, u32[]{:S(2)}) collective-permute-start(f32[32,8,128]{2,1,0:T(8,128)S(1)} %pad_maximum_fusion.8), channel_id=1, source_target_pairs={{0,3},{1,2},{2,1},{3,0},{4,7},{5,6},{6,5},{7,4},{8,11},{9,10},{10,... | collective-permute-start | bytes 393224 | tf_op jit(solution)/shard_map/ppermute | solution.py:281
  29.1 5.8 %collective-permute-start.7 = (f32[32,8,128]{2,1,0:T(8,128)S(1)}, f32[32,8,128]{2,1,0:T(8,128)S(1)}, u32[]{:S(2)}, u32[]{:S(2)}) collective-permute-start(f32[32,8,128]{2,1,0:T(8,128)S(1)} %pad_maximum_fusion.7), channel_id=1, source_target_pairs={{0,2},{1,3},{2,0},{3,1},{4,6},{5,7},{6,4},{7,5},{8,10},{9,11},{10,... | collective-permute-start | bytes 393224 | tf_op jit(solution)/shard_map/ppermute | solution.py:281
  43.8 7.0 %collective-permute-start.13 = (f32[17,8,128]{2,1,0:T(8,128)S(1)}, f32[17,8,128]{2,1,0:T(8,128)S(1)}, u32[]{:S(2)}, u32[]{:S(2)}) collective-permute-start(f32[17,8,128]{2,1,0:T(8,128)S(1)} %pad_maximum_fusion.12), channel_id=1, source_target_pairs={{0,12},{1,13},{2,14},{3,15},{4,8},{5,9},{6,10},{7,11},{8,4},{9,5},... | collective-permute-start | bytes 208904 | tf_op jit(solution)/shard_map/ppermute | solution.py:281
  45.7 7.2 %collective-permute-start.14 = (f32[17,8,128]{2,1,0:T(8,128)S(1)}, f32[17,8,128]{2,1,0:T(8,128)S(1)}, u32[]{:S(2)}, u32[]{:S(2)}) collective-permute-start(f32[17,8,128]{2,1,0:T(8,128)S(1)} %pad_maximum_fusion.12), channel_id=1, source_target_pairs={{0,8},{1,9},{2,10},{3,11},{4,12},{5,13},{6,14},{7,15},{8,0},{9,1},... | collective-permute-start | bytes 208904 | tf_op jit(solution)/shard_map/ppermute | solution.py:281
  45.7 7.2 %collective-permute-start.15 = (f32[17,8,128]{2,1,0:T(8,128)S(1)}, f32[17,8,128]{2,1,0:T(8,128)S(1)}, u32[]{:S(2)}, u32[]{:S(2)}) collective-permute-start(f32[17,8,128]{2,1,0:T(8,128)S(1)} %pad_maximum_fusion.12), channel_id=1, source_target_pairs={{0,4},{1,5},{2,6},{3,7},{4,0},{5,1},{6,2},{7,3},{8,12},{9,13},{10,... | collective-permute-start | bytes 208904 | tf_op jit(solution)/shard_map/ppermute | solution.py:281
  53.0 5.8 %collective-permute-start.18 = (f32[36,8,128]{2,1,0:T(8,128)S(1)}, f32[36,8,128]{2,1,0:T(8,128)S(1)}, u32[]{:S(2)}, u32[]{:S(2)}) collective-permute-start(f32[36,8,128]{2,1,0:T(8,128)S(1)} %pad_maximum_fusion.3), channel_id=1, source_target_pairs={{0,2},{1,3},{2,0},{3,1},{4,6},{5,7},{6,4},{7,5},{8,10},{9,11},{10,... | collective-permute-start | bytes 442376 | tf_op jit(solution)/shard_map/ppermute | solution.py:281
  58.9 8.2 %collective-permute-start.19 = (f32[72,8,128]{2,1,0:T(8,128)S(1)}, f32[72,8,128]{2,1,0:T(8,128)S(1)}, u32[]{:S(2)}, u32[]{:S(2)}) collective-permute-start(f32[72,8,128]{2,1,0:T(8,128)S(1)} %constant_dynamic-update-slice_fusion.5.near_b), channel_id=1, source_target_pairs={{0,1},{1,0},{2,3},{3,2},{4,5},{5,4},{6,7},{7,6},{8,9},{9,8},{10,11... | collective-permute-start | bytes 884744 | tf_op jit(solution)/shard_map/ppermute | solution.py:281
  59.9 7.2 %collective-permute-start.17 = (f32[64,8,128]{2,1,0:T(8,128)S(1)}, f32[64,8,128]{2,1,0:T(8,128)S(1)}, u32[]{:S(2)}, u32[]{:S(2)}) collective-permute-start(f32[64,8,128]{2,1,0:T(8,128)S(1)} %constant_dynamic-update-slice_fusion.near_a), channel_id=1, source_target_pairs={{0,2},{1,3},{2,0},{3,1},{4,6},{5,7},{6,4},{7,5},{8,10},{9,11},{10,... | collective-permute-start | bytes 786440 | tf_op jit(solution)/shard_map/ppermute | solution.py:281
  71.3 7.0 %collective-permute-start.21 = (f32[17,8,128]{2,1,0:T(8,128)S(1)}, f32[17,8,128]{2,1,0:T(8,128)S(1)}, u32[]{:S(2)}, u32[]{:S(2)}) collective-permute-start(f32[17,8,128]{2,1,0:T(8,128)S(1)} %pad_maximum_fusion.13), channel_id=1, source_target_pairs={{0,12},{1,13},{2,14},{3,15},{4,8},{5,9},{6,10},{7,11},{8,4},{9,5},... | collective-permute-start | bytes 208904 | tf_op jit(solution)/shard_map/ppermute | solution.py:281
  73.8 6.6 %collective-permute-start.22 = (f32[17,8,128]{2,1,0:T(8,128)S(1)}, f32[17,8,128]{2,1,0:T(8,128)S(1)}, u32[]{:S(2)}, u32[]{:S(2)}) collective-permute-start(f32[17,8,128]{2,1,0:T(8,128)S(1)} %pad_maximum_fusion.13), channel_id=1, source_target_pairs={{0,8},{1,9},{2,10},{3,11},{4,12},{5,13},{6,14},{7,15},{8,0},{9,1},... | collective-permute-start | bytes 208904 | tf_op jit(solution)/shard_map/ppermute | solution.py:281
  73.8 6.6 %collective-permute-start.23 = (f32[17,8,128]{2,1,0:T(8,128)S(1)}, f32[17,8,128]{2,1,0:T(8,128)S(1)}, u32[]{:S(2)}, u32[]{:S(2)}) collective-permute-start(f32[17,8,128]{2,1,0:T(8,128)S(1)} %pad_maximum_fusion.13), channel_id=1, source_target_pairs={{0,4},{1,5},{2,6},{3,7},{4,0},{5,1},{6,2},{7,3},{8,12},{9,13},{10,... | collective-permute-start | bytes 208904 | tf_op jit(solution)/shard_map/ppermute | solution.py:281
  75.8 13.4 %collective-permute-start.28 = (f32[64,2,8,128]{3,2,1,0:T(8,128)S(1)}, f32[64,2,8,128]{3,2,1,0:T(8,128)S(1)}, u32[]{:S(2)}, u32[]{:S(2)}) collective-permute-start(f32[64,2,8,128]{3,2,1,0:T(8,128)S(1)} %get-tuple-element.118.mine), channel_id=1, source_target_pairs={{0,16},{16,0},{1,17},{17,1},{2,18},{18,2},{3,19},{19,3},{4,20},{20... | collective-permute-start | bytes 1572872 | tf_op jit(solution)/shard_map/ppermute | solution.py:284
  80.5 5.8 %collective-permute-start.26 = (f32[36,8,128]{2,1,0:T(8,128)S(1)}, f32[36,8,128]{2,1,0:T(8,128)S(1)}, u32[]{:S(2)}, u32[]{:S(2)}) collective-permute-start(f32[36,8,128]{2,1,0:T(8,128)S(1)} %pad_maximum_fusion.4), channel_id=1, source_target_pairs={{0,2},{1,3},{2,0},{3,1},{4,6},{5,7},{6,4},{7,5},{8,10},{9,11},{10,... | collective-permute-start | bytes 442376 | tf_op jit(solution)/shard_map/ppermute | solution.py:281
  86.4 8.2 %collective-permute-start.27 = (f32[72,8,128]{2,1,0:T(8,128)S(1)}, f32[72,8,128]{2,1,0:T(8,128)S(1)}, u32[]{:S(2)}, u32[]{:S(2)}) collective-permute-start(f32[72,8,128]{2,1,0:T(8,128)S(1)} %constant_dynamic-update-slice_fusion.15.near_b), channel_id=1, source_target_pairs={{0,1},{1,0},{2,3},{3,2},{4,5},{5,4},{6,7},{7,6},{8,9},{9,8},{10,11... | collective-permute-start | bytes 884744 | tf_op jit(solution)/shard_map/ppermute | solution.py:281
  87.4 7.2 %collective-permute-start.25 = (f32[64,8,128]{2,1,0:T(8,128)S(1)}, f32[64,8,128]{2,1,0:T(8,128)S(1)}, u32[]{:S(2)}, u32[]{:S(2)}) collective-permute-start(f32[64,8,128]{2,1,0:T(8,128)S(1)} %constant_dynamic-update-slice_fusion.10.near_a), channel_id=1, source_target_pairs={{0,2},{1,3},{2,0},{3,1},{4,6},{5,7},{6,4},{7,5},{8,10},{9,11},{10,... | collective-permute-start | bytes 786440 | tf_op jit(solution)/shard_map/ppermute | solution.py:281
  99.0 7.0 %collective-permute-start.30 = (f32[17,8,128]{2,1,0:T(8,128)S(1)}, f32[17,8,128]{2,1,0:T(8,128)S(1)}, u32[]{:S(2)}, u32[]{:S(2)}) collective-permute-start(f32[17,8,128]{2,1,0:T(8,128)S(1)} %pad_maximum_fusion.14), channel_id=1, source_target_pairs={{0,12},{1,13},{2,14},{3,15},{4,8},{5,9},{6,10},{7,11},{8,4},{9,5},... | collective-permute-start | bytes 208904 | tf_op jit(solution)/shard_map/ppermute | solution.py:281
  101.4 6.7 %collective-permute-start.31 = (f32[17,8,128]{2,1,0:T(8,128)S(1)}, f32[17,8,128]{2,1,0:T(8,128)S(1)}, u32[]{:S(2)}, u32[]{:S(2)}) collective-permute-start(f32[17,8,128]{2,1,0:T(8,128)S(1)} %pad_maximum_fusion.14), channel_id=1, source_target_pairs={{0,8},{1,9},{2,10},{3,11},{4,12},{5,13},{6,14},{7,15},{8,0},{9,1},... | collective-permute-start | bytes 208904 | tf_op jit(solution)/shard_map/ppermute | solution.py:281
  101.4 6.7 %collective-permute-start.32 = (f32[17,8,128]{2,1,0:T(8,128)S(1)}, f32[17,8,128]{2,1,0:T(8,128)S(1)}, u32[]{:S(2)}, u32[]{:S(2)}) collective-permute-start(f32[17,8,128]{2,1,0:T(8,128)S(1)} %pad_maximum_fusion.14), channel_id=1, source_target_pairs={{0,4},{1,5},{2,6},{3,7},{4,0},{5,1},{6,2},{7,3},{8,12},{9,13},{10,... | collective-permute-start | bytes 208904 | tf_op jit(solution)/shard_map/ppermute | solution.py:281
  103.5 13.3 %collective-permute-start.37 = (f32[64,2,8,128]{3,2,1,0:T(8,128)S(1)}, f32[64,2,8,128]{3,2,1,0:T(8,128)S(1)}, u32[]{:S(2)}, u32[]{:S(2)}) collective-permute-start(f32[64,2,8,128]{3,2,1,0:T(8,128)S(1)} %get-tuple-element.135.mine), channel_id=1, source_target_pairs={{0,16},{16,0},{1,17},{17,1},{2,18},{18,2},{3,19},{19,3},{4,20},{20... | collective-permute-start | bytes 1572872 | tf_op jit(solution)/shard_map/ppermute | solution.py:284
  108.2 5.8 %collective-permute-start.35 = (f32[36,8,128]{2,1,0:T(8,128)S(1)}, f32[36,8,128]{2,1,0:T(8,128)S(1)}, u32[]{:S(2)}, u32[]{:S(2)}) collective-permute-start(f32[36,8,128]{2,1,0:T(8,128)S(1)} %pad_maximum_fusion.5), channel_id=1, source_target_pairs={{0,2},{1,3},{2,0},{3,1},{4,6},{5,7},{6,4},{7,5},{8,10},{9,11},{10,... | collective-permute-start | bytes 442376 | tf_op jit(solution)/shard_map/ppermute | solution.py:281
  114.1 8.3 %collective-permute-start.36 = (f32[72,8,128]{2,1,0:T(8,128)S(1)}, f32[72,8,128]{2,1,0:T(8,128)S(1)}, u32[]{:S(2)}, u32[]{:S(2)}) collective-permute-start(f32[72,8,128]{2,1,0:T(8,128)S(1)} %constant_dynamic-update-slice_fusion.25.near_b), channel_id=1, source_target_pairs={{0,1},{1,0},{2,3},{3,2},{4,5},{5,4},{6,7},{7,6},{8,9},{9,8},{10,11... | collective-permute-start | bytes 884744 | tf_op jit(solution)/shard_map/ppermute | solution.py:281
  115.2 7.1 %collective-permute-start.34 = (f32[64,8,128]{2,1,0:T(8,128)S(1)}, f32[64,8,128]{2,1,0:T(8,128)S(1)}, u32[]{:S(2)}, u32[]{:S(2)}) collective-permute-start(f32[64,8,128]{2,1,0:T(8,128)S(1)} %constant_dynamic-update-slice_fusion.20.near_a), channel_id=1, source_target_pairs={{0,2},{1,3},{2,0},{3,1},{4,6},{5,7},{6,4},{7,5},{8,10},{9,11},{10,... | collective-permute-start | bytes 786440 | tf_op jit(solution)/shard_map/ppermute | solution.py:281
  125.6 11.9 %collective-permute-start.38 = (f32[64,2,8,128]{3,2,1,0:T(8,128)S(1)}, f32[64,2,8,128]{3,2,1,0:T(8,128)S(1)}, u32[]{:S(2)}, u32[]{:S(2)}) collective-permute-start(f32[64,2,8,128]{3,2,1,0:T(8,128)S(1)} %get-tuple-element.150.mine), channel_id=1, source_target_pairs={{0,16},{16,0},{1,17},{17,1},{2,18},{18,2},{3,19},{19,3},{4,20},{20... | collective-permute-start | bytes 1572872 | tf_op jit(solution)/shard_map/ppermute | solution.py:284
  (8 other events, 71.2 us)

commit v17 on v16

--- a/solution.py
+++ b/solution.py
@@ -163,8 +163,8 @@
     for piece in (near_a, far_a, near_b, far_b):
         resp[at : at + piece.shape[0]] = piece[...]
         at += piece.shape[0]
-    each = own.shape[0] // 2 + 1
-    sums = tree([piece[i + each - 1] for piece in (near_b, far_b) for i in range(0, piece.shape[0], each)])
+    size = near_b.shape[0] // 2
+    sums = tree([piece[i + size - 1] for piece in (near_b, far_b) for i in (0, size)])
     gamma, alpha, beta = steps(first, sums, known[...])
     lane = lax.broadcasted_iota(jnp.int32, (ncase, width), 1)
     known_out[...] = jnp.where(lane == 0, gamma, jnp.where(lane == 1, alpha, beta))
@@ -298,7 +298,7 @@
     def found(away):
         x_bit, y_bit, z_part = away & 1, (away >> 1) & 1, away >> 2
         found_a = ((y_bit * 2 + x_bit) * nz + z_part) * half + other_slot * nh
-        found_b = ((x_bit * 2 + y_bit) * nz + z_part) * (half + 1) + (other_slot - nslot // 2) * nh
+        found_b = (x_bit * 2 + y_bit) * (nz * half + 1) + z_part * half + (other_slot - nslot // 2) * nh
         return jnp.where(other_slot < nslot // 2, found_a, nsub * half + found_b)
 
     facts = jnp.stack([slot * nh, found(owner ^ other)], axis=1).astype(jnp.float32)
@@ -349,13 +349,17 @@
         swap(jnp.concatenate([part[z * second : (z + 1) * second] for part in b_near]), 4 * z)
         for z in range(1, nz)
     ]
+    signal = sibling(a_z[1][:1])
     a_far = [
-        swap(jnp.concatenate([part[m * first : (m + 1) * first] for part in a_z]), m) for m in range(1, 4)
+        swap(jnp.concatenate([part[m * first : (m + 1) * first] for part in a_z] + [signal]), m)
+        for m in range(1, 4)
     ]
+    a_far, b_far = lax.optimization_barrier((a_far, b_far[::-1]))
+    b_far = b_far[::-1]
     field = f32(nrow, nh, ncase, LANES)
     answer = f32(per, ncase, LANES)
     load = pltpu.VMEM((nslot * nh, ncase, LANES), jnp.float32)
-    spread = pltpu.VMEM((nsub * per, ncase, LANES), jnp.float32)
+    spread = pltpu.VMEM((nsub * 2 * half + 4, ncase, LANES), jnp.float32)
     near, far, on, home_r, comp, own = pl.pallas_call(
         functools.partial(start_kernel, nh, cut, room, lines, extra, nz),
         out_shape=(jax.ShapeDtypeStruct((nrow,), jnp.int32),) * 2
@@ -394,9 +398,10 @@
             lists = update(step - 1, lists, known, part)
         spread_out = jnp.concatenate([spread_out[: per - 1], own[per - 1 :] + spread_out[per - 1 :]])
         parts = [spread_out] + [swap(spread_out, 4 * z) for z in range(1, nz)]
-        parts = lax.optimization_barrier(parts[::-1])[::-1]
+        parts = lax.optimization_barrier(parts)
         a = jnp.concatenate([part[:half] for part in parts])
-        b = jnp.concatenate([part[half:] for part in parts])
+        sums = tree([part[per - 1 :] for part in parts])
+        b = jnp.concatenate([part[half : per - 1] for part in parts] + [sums])
         far_a, far_b = swap(a, 1), swap(b, 2)
         a, b = jnp.concatenate([a, far_a]), jnp.concatenate([b, far_b])
         far_a, far_b = swap(a, 2), swap(b, 1)

time: 140 us -> 141 us (level)
    ppermute x6 -> x7, waiting for transfers between devices: 3.77 us -> 3.77 us  [sibling(): lax.ppermute(value, 'body', [(i, nbody - 1 - i) for i in range(nbody)])]
  transfers between devices with their start and end apart: 39 -> 40, of which waited for: 21 -> 22; matrix products, arithmetic and copies ran while one was open for 1% -> 1% of each run, Pallas kernels for 4% -> 4%
where the time goes in v17:
time: 141 us; the launch traced here: 140 us
  waiting for transfers between devices  54.3 us (39%)
  starting transfers between devices  47.3 us (34%)
  Pallas kernels  21.8 us (15%)
  blocking collectives  11.3 us (8%)
  local copies, waits for them, and re-layouts  2.48 us (2%)
  other arithmetic  1.53 us (1%)
    ppermute x33, waiting for transfers between devices, swap(): return lax.ppermute(value, 'sub', [(i, i ^ far) for i in range(nsub)])  50.6 us
    ppermute x33, starting transfers between devices, swap(): return lax.ppermute(value, 'sub', [(i, i ^ far) for i in range(nsub)])  47.1 us
    pallas_call x9, Pallas kernels, call(): pl.pallas_call(kernel, out_shape=tuple(out_shape) if several else out_sha...  18.3 us
    all_to_all x1, blocking collectives, on_device(): lax.all_to_all(own, ('body', 'sub'), split_axis=0, concat_axis=0, tiled=T...  11.3 us
    ppermute x7, waiting for transfers between devices, sibling(): lax.ppermute(value, 'body', [(i, nbody - 1 - i) for i in range(nbody)])  3.77 us
    pallas_call x1, Pallas kernels, on_device(): pl.pallas_call(functools.partial(start_kernel, nh, cut, room, lines, extr...  3.45 us
  transfers between devices with their start and end apart: 40, of which 22 were waited for; matrix products, arithmetic and copies ran while one was open for 1% of the time, Pallas kernels for 4%

profile of v17, /device:TPU:0, one launch (start us, length us, event | category | flops | bytes accessed | tf_op | source)
XLA Modules:
  0.0 140.3 jit_solution(12481164592978933213)
XLA Ops:
  4.2 5.1 %collective-permute-start = (f32[32,8,128]{2,1,0:T(8,128)S(1)}, f32[32,8,128]{2,1,0:T(8,128)S(1)}, u32[]{:S(2)}, u32[]{:S(2)}) collective-permute-start(f32[32,8,128]{2,1,0:T(8,128)S(1)} %get-tuple-element.87), channel_id=1, source_target_pairs={{0,12},{1,13},{2,14},{3,15},{4,8},{5,9},{6,10},{7,11},{8,4},{9,5},... | collective-permute-start | bytes 393224 | tf_op jit(solution)/shard_map/ppermute | solution.py:281
  15.5 3.5 %shard_map.75.block = bf16[2048,2048]{1,0:T(8,128)(2,1)S(1)} custom-call(bf16[2048,2048]{1,0:T(8,128)(2,1)} %bitcast.118), custom_call_target="tpu_custom_call" | custom-call | bytes 16777216 | tf_op jit(solution)/shard_map/pallas_call | solution.py:25
  19.0 2.8 %collective-permute-done.1.refs_2_ = f32[32,8,128]{2,1,0:T(8,128)S(1)} collective-permute-done((f32[32,8,128]{2,1,0:T(8,128)S(1)}, f32[32,8,128]{2,1,0:T(8,128)S(1)}, u32[]{:S(2)}, u32[]{:S(2)}) %collective-permute-start.1) | collective-permute-done | bytes 131104 | tf_op jit(solution)/shard_map/ppermute | solution.py:281
  24.0 2.5 %collective-permute-start.9 = (f32[33,8,128]{2,1,0:T(8,128)S(1)}, f32[33,8,128]{2,1,0:T(8,128)S(1)}, u32[]{:S(2)}, u32[]{:S(2)}) collective-permute-start(f32[33,8,128]{2,1,0:T(8,128)S(1)} %get-tuple-element.247), channel_id=1, source_target_pairs={{0,3},{1,2},{2,1},{3,0},{4,7},{5,6},{6,5},{7,4},{8,11},{9,10},{10,... | collective-permute-start | bytes 405512 | tf_op jit(solution)/shard_map/ppermute | solution.py:281
  26.6 2.7 %collective-permute-start.12 = (f32[44,8,128]{2,1,0:T(8,128)S(1)}, f32[44,8,128]{2,1,0:T(8,128)S(1)}, u32[]{:S(2)}, u32[]{:S(2)}) collective-permute-start(f32[44,8,128]{2,1,0:T(8,128)S(1)} %pad_maximum_fusion.2), channel_id=1, source_target_pairs={{0,4},{1,5},{2,6},{3,7},{4,0},{5,1},{6,2},{7,3},{8,12},{9,13},{10,... | collective-permute-start | bytes 540680 | tf_op jit(solution)/shard_map/ppermute | solution.py:281
  31.9 2.3 %collective-permute-done.8.refs_5_ = f32[33,8,128]{2,1,0:T(8,128)S(1)} collective-permute-done((f32[33,8,128]{2,1,0:T(8,128)S(1)}, f32[33,8,128]{2,1,0:T(8,128)S(1)}, u32[]{:S(2)}, u32[]{:S(2)}) %collective-permute-start.8) | collective-permute-done | bytes 135200 | tf_op jit(solution)/shard_map/ppermute | solution.py:281
  35.4 4.9 %collective-permute-done.11.refs_12_ = f32[44,8,128]{2,1,0:T(8,128)S(1)} collective-permute-done((f32[44,8,128]{2,1,0:T(8,128)S(1)}, f32[44,8,128]{2,1,0:T(8,128)S(1)}, u32[]{:S(2)}, u32[]{:S(2)}) %collective-permute-start.11) | collective-permute-done | bytes 180256 | tf_op jit(solution)/shard_map/ppermute | solution.py:281
  40.4 3.5 %shard_map.76 = (s32[128]{0:T(128)S(1)}, s32[128]{0:T(128)S(1)}, f32[128]{0:T(128)S(1)}, f32[128,2,8,128]{3,2,1,0:T(8,128)S(1)}, f32[32,8,128]{2,1,0:T(8,128)S(1)}, /*index=5*/f32[17,8,128]{2,1,0:T(8,128)S(1)}) custom-call(bf16[2048,2048]{1,0:T(8,128)(2,1)S(1)} %shard_map.75.block, f32[32,8,128]{2,1,0:T(8,128)S(1)} %get-tuple-element.97.refs_0_, ...), custom_call_target="tpu_custom_call" | custom-call | tf_op jit(solution)/shard_map/pallas_call | solution.py:363
  45.2 2.4 %collective-permute-start.16 = (f32[17,8,128]{2,1,0:T(8,128)S(1)}, f32[17,8,128]{2,1,0:T(8,128)S(1)}, u32[]{:S(2)}, u32[]{:S(2)}) collective-permute-start(f32[17,8,128]{2,1,0:T(8,128)S(1)} %pad_maximum_fusion.6), channel_id=1, source_target_pairs={{0,12},{1,13},{2,14},{3,15},{4,8},{5,9},{6,10},{7,11},{8,4},{9,5},... | collective-permute-start | bytes 208904 | tf_op jit(solution)/shard_map/ppermute | solution.py:281
  47.6 2.0 %collective-permute-start.14 = (f32[17,8,128]{2,1,0:T(8,128)S(1)}, f32[17,8,128]{2,1,0:T(8,128)S(1)}, u32[]{:S(2)}, u32[]{:S(2)}) collective-permute-start(f32[17,8,128]{2,1,0:T(8,128)S(1)} %pad_maximum_fusion.6), channel_id=1, source_target_pairs={{0,4},{1,5},{2,6},{3,7},{4,0},{5,1},{6,2},{7,3},{8,12},{9,13},{10,... | collective-permute-start | bytes 208904 | tf_op jit(solution)/shard_map/ppermute | solution.py:281
  49.6 2.5 %collective-permute-done.16 = f32[17,8,128]{2,1,0:T(8,128)S(1)} collective-permute-done((f32[17,8,128]{2,1,0:T(8,128)S(1)}, f32[17,8,128]{2,1,0:T(8,128)S(1)}, u32[]{:S(2)}, u32[]{:S(2)}) %collective-permute-start.16) | collective-permute-done | bytes 69664 | tf_op jit(solution)/shard_map/ppermute | solution.py:281
  52.1 2.1 %collective-permute-done.15 = f32[17,8,128]{2,1,0:T(8,128)S(1)} collective-permute-done((f32[17,8,128]{2,1,0:T(8,128)S(1)}, f32[17,8,128]{2,1,0:T(8,128)S(1)}, u32[]{:S(2)}, u32[]{:S(2)}) %collective-permute-start.15) | collective-permute-done | bytes 69664 | tf_op jit(solution)/shard_map/ppermute | solution.py:281
  57.5 2.4 %collective-permute-done.19 = f32[33,8,128]{2,1,0:T(8,128)S(1)} collective-permute-done((f32[33,8,128]{2,1,0:T(8,128)S(1)}, f32[33,8,128]{2,1,0:T(8,128)S(1)}, u32[]{:S(2)}, u32[]{:S(2)}) %collective-permute-start.19) | collective-permute-done | bytes 135200 | tf_op jit(solution)/shard_map/ppermute | solution.py:281
  63.1 5.6 %collective-permute-done.18.far_a = f32[64,8,128]{2,1,0:T(8,128)S(1)} collective-permute-done((f32[64,8,128]{2,1,0:T(8,128)S(1)}, f32[64,8,128]{2,1,0:T(8,128)S(1)}, u32[]{:S(2)}, u32[]{:S(2)}) %collective-permute-start.18) | collective-permute-done | bytes 262176 | tf_op jit(solution)/shard_map/ppermute | solution.py:281
  68.7 3.0 %shard_map.77 = (f32[128,2,8,128]{3,2,1,0:T(8,128)S(1)}, f32[128,2,8,128]{3,2,1,0:T(8,128)S(1)}, f32[17,8,128]{2,1,0:T(8,128)S(1)}, f32[64,2,8,128]{3,2,1,0:T(8,128)S(1)}, f32[8,128]{1,0:T(8,128)S(1)}) custom-call(s32[128]{0:T(128)S(1)} %get-tuple-element.111.place, s32[128]{0:T(128)S(1)} %get-tuple-element.112.away, f32[128]{0:T(128)S(1)} %get-tuple-element.113.keep, ...), custom_call_target="tpu_custom_call" | custom-call | tf_op jit(solution)/shard_map/pallas_call | solution.py:25
  73.0 2.4 %collective-permute-start.24 = (f32[17,8,128]{2,1,0:T(8,128)S(1)}, f32[17,8,128]{2,1,0:T(8,128)S(1)}, u32[]{:S(2)}, u32[]{:S(2)}) collective-permute-start(f32[17,8,128]{2,1,0:T(8,128)S(1)} %pad_maximum_fusion.7), channel_id=1, source_target_pairs={{0,12},{1,13},{2,14},{3,15},{4,8},{5,9},{6,10},{7,11},{8,4},{9,5},... | collective-permute-start | bytes 208904 | tf_op jit(solution)/shard_map/ppermute | solution.py:281
  75.5 2.0 %collective-permute-start.22 = (f32[17,8,128]{2,1,0:T(8,128)S(1)}, f32[17,8,128]{2,1,0:T(8,128)S(1)}, u32[]{:S(2)}, u32[]{:S(2)}) collective-permute-start(f32[17,8,128]{2,1,0:T(8,128)S(1)} %pad_maximum_fusion.7), channel_id=1, source_target_pairs={{0,4},{1,5},{2,6},{3,7},{4,0},{5,1},{6,2},{7,3},{8,12},{9,13},{10,... | collective-permute-start | bytes 208904 | tf_op jit(solution)/shard_map/ppermute | solution.py:281
  77.5 2.5 %collective-permute-done.24 = f32[17,8,128]{2,1,0:T(8,128)S(1)} collective-permute-done((f32[17,8,128]{2,1,0:T(8,128)S(1)}, f32[17,8,128]{2,1,0:T(8,128)S(1)}, u32[]{:S(2)}, u32[]{:S(2)}) %collective-permute-start.24) | collective-permute-done | bytes 69664 | tf_op jit(solution)/shard_map/ppermute | solution.py:281
  80.0 2.1 %collective-permute-done.23 = f32[17,8,128]{2,1,0:T(8,128)S(1)} collective-permute-done((f32[17,8,128]{2,1,0:T(8,128)S(1)}, f32[17,8,128]{2,1,0:T(8,128)S(1)}, u32[]{:S(2)}, u32[]{:S(2)}) %collective-permute-start.23) | collective-permute-done | bytes 69664 | tf_op jit(solution)/shard_map/ppermute | solution.py:281
  84.4 3.4 %collective-permute-done.27 = f32[33,8,128]{2,1,0:T(8,128)S(1)} collective-permute-done((f32[33,8,128]{2,1,0:T(8,128)S(1)}, f32[33,8,128]{2,1,0:T(8,128)S(1)}, u32[]{:S(2)}, u32[]{:S(2)}) %collective-permute-start.27) | collective-permute-done | bytes 135200 | tf_op jit(solution)/shard_map/ppermute | solution.py:281
  90.9 5.3 %collective-permute-done.26.far_a = f32[64,8,128]{2,1,0:T(8,128)S(1)} collective-permute-done((f32[64,8,128]{2,1,0:T(8,128)S(1)}, f32[64,8,128]{2,1,0:T(8,128)S(1)}, u32[]{:S(2)}, u32[]{:S(2)}) %collective-permute-start.26) | collective-permute-done | bytes 262176 | tf_op jit(solution)/shard_map/ppermute | solution.py:281
  96.2 3.2 %shard_map.79 = (f32[128,2,8,128]{3,2,1,0:T(8,128)S(1)}, f32[128,2,8,128]{3,2,1,0:T(8,128)S(1)}, f32[17,8,128]{2,1,0:T(8,128)S(1)}, f32[64,2,8,128]{3,2,1,0:T(8,128)S(1)}, f32[8,128]{1,0:T(8,128)S(1)}) custom-call(s32[128]{0:T(128)S(1)} %get-tuple-element.111.place, s32[128]{0:T(128)S(1)} %get-tuple-element.112.away, f32[128]{0:T(128)S(1)} %get-tuple-element.113.keep, ...), custom_call_target="tpu_custom_call" | custom-call | tf_op jit(solution)/shard_map/pallas_call | solution.py:25
  100.7 2.3 %collective-permute-start.33 = (f32[17,8,128]{2,1,0:T(8,128)S(1)}, f32[17,8,128]{2,1,0:T(8,128)S(1)}, u32[]{:S(2)}, u32[]{:S(2)}) collective-permute-start(f32[17,8,128]{2,1,0:T(8,128)S(1)} %pad_maximum_fusion.8), channel_id=1, source_target_pairs={{0,12},{1,13},{2,14},{3,15},{4,8},{5,9},{6,10},{7,11},{8,4},{9,5},... | collective-permute-start | bytes 208904 | tf_op jit(solution)/shard_map/ppermute | solution.py:281
  103.0 2.1 %collective-permute-start.31 = (f32[17,8,128]{2,1,0:T(8,128)S(1)}, f32[17,8,128]{2,1,0:T(8,128)S(1)}, u32[]{:S(2)}, u32[]{:S(2)}) collective-permute-start(f32[17,8,128]{2,1,0:T(8,128)S(1)} %pad_maximum_fusion.8), channel_id=1, source_target_pairs={{0,4},{1,5},{2,6},{3,7},{4,0},{5,1},{6,2},{7,3},{8,12},{9,13},{10,... | collective-permute-start | bytes 208904 | tf_op jit(solution)/shard_map/ppermute | solution.py:281
  105.2 2.5 %collective-permute-done.33 = f32[17,8,128]{2,1,0:T(8,128)S(1)} collective-permute-done((f32[17,8,128]{2,1,0:T(8,128)S(1)}, f32[17,8,128]{2,1,0:T(8,128)S(1)}, u32[]{:S(2)}, u32[]{:S(2)}) %collective-permute-start.33) | collective-permute-done | bytes 69664 | tf_op jit(solution)/shard_map/ppermute | solution.py:281
  107.6 2.1 %collective-permute-done.32 = f32[17,8,128]{2,1,0:T(8,128)S(1)} collective-permute-done((f32[17,8,128]{2,1,0:T(8,128)S(1)}, f32[17,8,128]{2,1,0:T(8,128)S(1)}, u32[]{:S(2)}, u32[]{:S(2)}) %collective-permute-start.32) | collective-permute-done | bytes 69664 | tf_op jit(solution)/shard_map/ppermute | solution.py:281
  112.4 3.1 %collective-permute-done.36 = f32[33,8,128]{2,1,0:T(8,128)S(1)} collective-permute-done((f32[33,8,128]{2,1,0:T(8,128)S(1)}, f32[33,8,128]{2,1,0:T(8,128)S(1)}, u32[]{:S(2)}, u32[]{:S(2)}) %collective-permute-start.36) | collective-permute-done | bytes 135200 | tf_op jit(solution)/shard_map/ppermute | solution.py:281
  116.3 1.7 %collective-permute-start.35 = (f32[64,8,128]{2,1,0:T(8,128)S(1)}, f32[64,8,128]{2,1,0:T(8,128)S(1)}, u32[]{:S(2)}, u32[]{:S(2)}) collective-permute-start(f32[64,8,128]{2,1,0:T(8,128)S(1)} %constant_dynamic-update-slice_fusion.47.near_a), channel_id=1, source_target_pairs={{0,2},{1,3},{2,0},{3,1},{4,6},{5,7},{6,4},{7,5},{8,10},{9,11},{10,... | collective-permute-start | bytes 786440 | tf_op jit(solution)/shard_map/ppermute | solution.py:281
  119.0 4.5 %collective-permute-done.35.far_a = f32[64,8,128]{2,1,0:T(8,128)S(1)} collective-permute-done((f32[64,8,128]{2,1,0:T(8,128)S(1)}, f32[64,8,128]{2,1,0:T(8,128)S(1)}, u32[]{:S(2)}, u32[]{:S(2)}) %collective-permute-start.35) | collective-permute-done | bytes 262176 | tf_op jit(solution)/shard_map/ppermute | solution.py:281
  123.5 3.2 %shard_map.81 = (f32[32,8,128]{2,1,0:T(8,128)S(1)}, f32[64,2,8,128]{3,2,1,0:T(8,128)S(1)}, f32[8,128]{1,0:T(8,128)S(1)}) custom-call(s32[128]{0:T(128)S(1)} %get-tuple-element.111.place, s32[128]{0:T(128)S(1)} %get-tuple-element.112.away, f32[128]{0:T(128)S(1)} %get-tuple-element.113.keep, s32[64]{0:T(128)S(1)} %get-tuple-element.114.picked, ...), custom_call_target="tpu_custom_call" | custom-call | tf_op jit(solution)/shard_map/pallas_call | solution.py:25
  126.8 11.3 %all_to_all.5.sums = f32[32,8,128]{2,1,0:T(8,128)S(1)} all-to-all(f32[32,8,128]{2,1,0:T(8,128)S(1)} %get-tuple-element.160), channel_id=1, replica_groups=mesh['body'=2,'sub'=16] {'body','sub'}, dimensions={0} | all-to-all | bytes 262144 | tf_op jit(solution)/shard_map/all_to_all | solution.py:429
  138.1 2.2 %shard_map.82 = f32[8,64,256]{2,1,0:T(8,128)} custom-call(f32[64]{0:T(128)S(1)} %get-tuple-element.252.keep, f32[32,8,128]{2,1,0:T(8,128)S(1)} %all_to_all.5.sums, f32[8,128]{1,0:T(8,128)S(1)} %get-tuple-element.161.known, f32[64,256]{1,0:T(8,128)S(1)} %copy-done, f32[64,2,8,128]{3,2,1,0:T(8,128)S(1)} %get-tuple-element.162.mine, ...), custom_call_target="tpu_custom_call" | custom-call | tf_op jit(solution)/shard_map/pallas_call | solution.py:25
  (129 shorter events, 36.5 us)
Async XLA Ops:
  4.2 10.7 %collective-permute-start = (f32[32,8,128]{2,1,0:T(8,128)S(1)}, f32[32,8,128]{2,1,0:T(8,128)S(1)}, u32[]{:S(2)}, u32[]{:S(2)}) collective-permute-start(f32[32,8,128]{2,1,0:T(8,128)S(1)} %get-tuple-element.87), channel_id=1, source_target_pairs={{0,12},{1,13},{2,14},{3,15},{4,8},{5,9},{6,10},{7,11},{8,4},{9,5},... | collective-permute-start | bytes 393224 | tf_op jit(solution)/shard_map/ppermute | solution.py:281
  11.3 10.5 %collective-permute-start.3 = (f32[44,8,128]{2,1,0:T(8,128)S(1)}, f32[44,8,128]{2,1,0:T(8,128)S(1)}, u32[]{:S(2)}, u32[]{:S(2)}) collective-permute-start(f32[44,8,128]{2,1,0:T(8,128)S(1)} %get-tuple-element.93), channel_id=1, source_target_pairs={{0,1},{1,0},{2,3},{3,2},{4,5},{5,4},{6,7},{7,6},{8,9},{9,8},{10,11... | collective-permute-start | bytes 540680 | tf_op jit(solution)/shard_map/ppermute | solution.py:281
  12.9 9.6 %collective-permute-start.4 = (f32[44,8,128]{2,1,0:T(8,128)S(1)}, f32[44,8,128]{2,1,0:T(8,128)S(1)}, u32[]{:S(2)}, u32[]{:S(2)}) collective-permute-start(f32[44,8,128]{2,1,0:T(8,128)S(1)} %get-tuple-element.94), channel_id=1, source_target_pairs={{0,2},{1,3},{2,0},{3,1},{4,6},{5,7},{6,4},{7,5},{8,10},{9,11},{10,... | collective-permute-start | bytes 540680 | tf_op jit(solution)/shard_map/ppermute | solution.py:281
  14.4 8.1 %collective-permute-start.5 = (f32[44,8,128]{2,1,0:T(8,128)S(1)}, f32[44,8,128]{2,1,0:T(8,128)S(1)}, u32[]{:S(2)}, u32[]{:S(2)}) collective-permute-start(f32[44,8,128]{2,1,0:T(8,128)S(1)} %get-tuple-element.95), channel_id=1, source_target_pairs={{0,3},{1,2},{2,1},{3,0},{4,7},{5,6},{6,5},{7,4},{8,11},{9,10},{10,... | collective-permute-start | bytes 540680 | tf_op jit(solution)/shard_map/ppermute | solution.py:281
  14.9 6.9 %collective-permute-start.1 = (f32[32,8,128]{2,1,0:T(8,128)S(1)}, f32[32,8,128]{2,1,0:T(8,128)S(1)}, u32[]{:S(2)}, u32[]{:S(2)}) collective-permute-start(f32[32,8,128]{2,1,0:T(8,128)S(1)} %get-tuple-element.88), channel_id=1, source_target_pairs={{0,8},{1,9},{2,10},{3,11},{4,12},{5,13},{6,14},{7,15},{8,0},{9,1},... | collective-permute-start | bytes 393224 | tf_op jit(solution)/shard_map/ppermute | solution.py:281
  14.9 6.9 %collective-permute-start.2 = (f32[32,8,128]{2,1,0:T(8,128)S(1)}, f32[32,8,128]{2,1,0:T(8,128)S(1)}, u32[]{:S(2)}, u32[]{:S(2)}) collective-permute-start(f32[32,8,128]{2,1,0:T(8,128)S(1)} %get-tuple-element.89), channel_id=1, source_target_pairs={{0,4},{1,5},{2,6},{3,7},{4,0},{5,1},{6,2},{7,3},{8,12},{9,13},{10,... | collective-permute-start | bytes 393224 | tf_op jit(solution)/shard_map/ppermute | solution.py:281
  22.6 12.8 %collective-permute-start.10 = (f32[44,8,128]{2,1,0:T(8,128)S(1)}, f32[44,8,128]{2,1,0:T(8,128)S(1)}, u32[]{:S(2)}, u32[]{:S(2)}) collective-permute-start(f32[44,8,128]{2,1,0:T(8,128)S(1)} %pad_maximum_fusion), channel_id=1, source_target_pairs={{0,12},{1,13},{2,14},{3,15},{4,8},{5,9},{6,10},{7,11},{8,4},{9,5},... | collective-permute-start | bytes 540680 | tf_op jit(solution)/shard_map/ppermute | solution.py:281
  23.5 16.8 %collective-permute-start.11 = (f32[44,8,128]{2,1,0:T(8,128)S(1)}, f32[44,8,128]{2,1,0:T(8,128)S(1)}, u32[]{:S(2)}, u32[]{:S(2)}) collective-permute-start(f32[44,8,128]{2,1,0:T(8,128)S(1)} %pad_maximum_fusion.1), channel_id=1, source_target_pairs={{0,8},{1,9},{2,10},{3,11},{4,12},{5,13},{6,14},{7,15},{8,0},{9,1},... | collective-permute-start | bytes 540680 | tf_op jit(solution)/shard_map/ppermute | solution.py:281
  24.0 6.4 %collective-permute-start.9 = (f32[33,8,128]{2,1,0:T(8,128)S(1)}, f32[33,8,128]{2,1,0:T(8,128)S(1)}, u32[]{:S(2)}, u32[]{:S(2)}) collective-permute-start(f32[33,8,128]{2,1,0:T(8,128)S(1)} %get-tuple-element.247), channel_id=1, source_target_pairs={{0,3},{1,2},{2,1},{3,0},{4,7},{5,6},{6,5},{7,4},{8,11},{9,10},{10,... | collective-permute-start | bytes 405512 | tf_op jit(solution)/shard_map/ppermute | solution.py:281
  26.6 13.8 %collective-permute-start.12 = (f32[44,8,128]{2,1,0:T(8,128)S(1)}, f32[44,8,128]{2,1,0:T(8,128)S(1)}, u32[]{:S(2)}, u32[]{:S(2)}) collective-permute-start(f32[44,8,128]{2,1,0:T(8,128)S(1)} %pad_maximum_fusion.2), channel_id=1, source_target_pairs={{0,4},{1,5},{2,6},{3,7},{4,0},{5,1},{6,2},{7,3},{8,12},{9,13},{10,... | collective-permute-start | bytes 540680 | tf_op jit(solution)/shard_map/ppermute | solution.py:281
  45.2 7.0 %collective-permute-start.16 = (f32[17,8,128]{2,1,0:T(8,128)S(1)}, f32[17,8,128]{2,1,0:T(8,128)S(1)}, u32[]{:S(2)}, u32[]{:S(2)}) collective-permute-start(f32[17,8,128]{2,1,0:T(8,128)S(1)} %pad_maximum_fusion.6), channel_id=1, source_target_pairs={{0,12},{1,13},{2,14},{3,15},{4,8},{5,9},{6,10},{7,11},{8,4},{9,5},... | collective-permute-start | bytes 208904 | tf_op jit(solution)/shard_map/ppermute | solution.py:281
  47.6 6.6 %collective-permute-start.15 = (f32[17,8,128]{2,1,0:T(8,128)S(1)}, f32[17,8,128]{2,1,0:T(8,128)S(1)}, u32[]{:S(2)}, u32[]{:S(2)}) collective-permute-start(f32[17,8,128]{2,1,0:T(8,128)S(1)} %pad_maximum_fusion.6), channel_id=1, source_target_pairs={{0,8},{1,9},{2,10},{3,11},{4,12},{5,13},{6,14},{7,15},{8,0},{9,1},... | collective-permute-start | bytes 208904 | tf_op jit(solution)/shard_map/ppermute | solution.py:281
  47.6 6.6 %collective-permute-start.14 = (f32[17,8,128]{2,1,0:T(8,128)S(1)}, f32[17,8,128]{2,1,0:T(8,128)S(1)}, u32[]{:S(2)}, u32[]{:S(2)}) collective-permute-start(f32[17,8,128]{2,1,0:T(8,128)S(1)} %pad_maximum_fusion.6), channel_id=1, source_target_pairs={{0,4},{1,5},{2,6},{3,7},{4,0},{5,1},{6,2},{7,3},{8,12},{9,13},{10,... | collective-permute-start | bytes 208904 | tf_op jit(solution)/shard_map/ppermute | solution.py:281
  54.4 5.6 %collective-permute-start.19 = (f32[33,8,128]{2,1,0:T(8,128)S(1)}, f32[33,8,128]{2,1,0:T(8,128)S(1)}, u32[]{:S(2)}, u32[]{:S(2)}) collective-permute-start(f32[33,8,128]{2,1,0:T(8,128)S(1)} %get-tuple-element.171), channel_id=1, source_target_pairs={{0,2},{1,3},{2,0},{3,1},{4,6},{5,7},{6,4},{7,5},{8,10},{9,11},{10,... | collective-permute-start | bytes 405512 | tf_op jit(solution)/shard_map/ppermute | solution.py:281
  56.0 5.5 %collective-permute-start.17 = (f32[32,8,128]{2,1,0:T(8,128)S(1)}, f32[32,8,128]{2,1,0:T(8,128)S(1)}, u32[]{:S(2)}, u32[]{:S(2)}) collective-permute-start(f32[32,8,128]{2,1,0:T(8,128)S(1)} %pad_maximum_fusion.3), channel_id=1, source_target_pairs={{0,1},{1,0},{2,3},{3,2},{4,5},{5,4},{6,7},{7,6},{8,9},{9,8},{10,11... | collective-permute-start | bytes 393224 | tf_op jit(solution)/shard_map/ppermute | solution.py:281
  60.0 8.7 %collective-permute-start.20 = (f32[66,8,128]{2,1,0:T(8,128)S(1)}, f32[66,8,128]{2,1,0:T(8,128)S(1)}, u32[]{:S(2)}, u32[]{:S(2)}) collective-permute-start(f32[66,8,128]{2,1,0:T(8,128)S(1)} %constant_dynamic-update-slice_fusion.25.near_b), channel_id=1, source_target_pairs={{0,1},{1,0},{2,3},{3,2},{4,5},{5,4},{6,7},{7,6},{8,9},{9,8},{10,11... | collective-permute-start | bytes 811016 | tf_op jit(solution)/shard_map/ppermute | solution.py:281
  61.5 7.2 %collective-permute-start.18 = (f32[64,8,128]{2,1,0:T(8,128)S(1)}, f32[64,8,128]{2,1,0:T(8,128)S(1)}, u32[]{:S(2)}, u32[]{:S(2)}) collective-permute-start(f32[64,8,128]{2,1,0:T(8,128)S(1)} %constant_dynamic-update-slice_fusion.15.near_a), channel_id=1, source_target_pairs={{0,2},{1,3},{2,0},{3,1},{4,6},{5,7},{6,4},{7,5},{8,10},{9,11},{10,... | collective-permute-start | bytes 786440 | tf_op jit(solution)/shard_map/ppermute | solution.py:281
  73.0 7.0 %collective-permute-start.24 = (f32[17,8,128]{2,1,0:T(8,128)S(1)}, f32[17,8,128]{2,1,0:T(8,128)S(1)}, u32[]{:S(2)}, u32[]{:S(2)}) collective-permute-start(f32[17,8,128]{2,1,0:T(8,128)S(1)} %pad_maximum_fusion.7), channel_id=1, source_target_pairs={{0,12},{1,13},{2,14},{3,15},{4,8},{5,9},{6,10},{7,11},{8,4},{9,5},... | collective-permute-start | bytes 208904 | tf_op jit(solution)/shard_map/ppermute | solution.py:281
  75.5 6.6 %collective-permute-start.23 = (f32[17,8,128]{2,1,0:T(8,128)S(1)}, f32[17,8,128]{2,1,0:T(8,128)S(1)}, u32[]{:S(2)}, u32[]{:S(2)}) collective-permute-start(f32[17,8,128]{2,1,0:T(8,128)S(1)} %pad_maximum_fusion.7), channel_id=1, source_target_pairs={{0,8},{1,9},{2,10},{3,11},{4,12},{5,13},{6,14},{7,15},{8,0},{9,1},... | collective-permute-start | bytes 208904 | tf_op jit(solution)/shard_map/ppermute | solution.py:281
  75.5 6.6 %collective-permute-start.22 = (f32[17,8,128]{2,1,0:T(8,128)S(1)}, f32[17,8,128]{2,1,0:T(8,128)S(1)}, u32[]{:S(2)}, u32[]{:S(2)}) collective-permute-start(f32[17,8,128]{2,1,0:T(8,128)S(1)} %pad_maximum_fusion.7), channel_id=1, source_target_pairs={{0,4},{1,5},{2,6},{3,7},{4,0},{5,1},{6,2},{7,3},{8,12},{9,13},{10,... | collective-permute-start | bytes 208904 | tf_op jit(solution)/shard_map/ppermute | solution.py:281
  77.5 12.5 %collective-permute-start.29 = (f32[64,2,8,128]{3,2,1,0:T(8,128)S(1)}, f32[64,2,8,128]{3,2,1,0:T(8,128)S(1)}, u32[]{:S(2)}, u32[]{:S(2)}) collective-permute-start(f32[64,2,8,128]{3,2,1,0:T(8,128)S(1)} %get-tuple-element.130.mine), channel_id=1, source_target_pairs={{0,16},{16,0},{1,17},{17,1},{2,18},{18,2},{3,19},{19,3},{4,20},{20... | collective-permute-start | bytes 1572872 | tf_op jit(solution)/shard_map/ppermute | solution.py:284
  82.2 5.6 %collective-permute-start.27 = (f32[33,8,128]{2,1,0:T(8,128)S(1)}, f32[33,8,128]{2,1,0:T(8,128)S(1)}, u32[]{:S(2)}, u32[]{:S(2)}) collective-permute-start(f32[33,8,128]{2,1,0:T(8,128)S(1)} %get-tuple-element.169), channel_id=1, source_target_pairs={{0,2},{1,3},{2,0},{3,1},{4,6},{5,7},{6,4},{7,5},{8,10},{9,11},{10,... | collective-permute-start | bytes 405512 | tf_op jit(solution)/shard_map/ppermute | solution.py:281
  87.8 8.4 %collective-permute-start.28 = (f32[66,8,128]{2,1,0:T(8,128)S(1)}, f32[66,8,128]{2,1,0:T(8,128)S(1)}, u32[]{:S(2)}, u32[]{:S(2)}) collective-permute-start(f32[66,8,128]{2,1,0:T(8,128)S(1)} %constant_dynamic-update-slice_fusion.41.near_b), channel_id=1, source_target_pairs={{0,1},{1,0},{2,3},{3,2},{4,5},{5,4},{6,7},{7,6},{8,9},{9,8},{10,11... | collective-permute-start | bytes 811016 | tf_op jit(solution)/shard_map/ppermute | solution.py:281
  89.0 7.2 %collective-permute-start.26 = (f32[64,8,128]{2,1,0:T(8,128)S(1)}, f32[64,8,128]{2,1,0:T(8,128)S(1)}, u32[]{:S(2)}, u32[]{:S(2)}) collective-permute-start(f32[64,8,128]{2,1,0:T(8,128)S(1)} %constant_dynamic-update-slice_fusion.31.near_a), channel_id=1, source_target_pairs={{0,2},{1,3},{2,0},{3,1},{4,6},{5,7},{6,4},{7,5},{8,10},{9,11},{10,... | collective-permute-start | bytes 786440 | tf_op jit(solution)/shard_map/ppermute | solution.py:281
  100.7 7.0 %collective-permute-start.33 = (f32[17,8,128]{2,1,0:T(8,128)S(1)}, f32[17,8,128]{2,1,0:T(8,128)S(1)}, u32[]{:S(2)}, u32[]{:S(2)}) collective-permute-start(f32[17,8,128]{2,1,0:T(8,128)S(1)} %pad_maximum_fusion.8), channel_id=1, source_target_pairs={{0,12},{1,13},{2,14},{3,15},{4,8},{5,9},{6,10},{7,11},{8,4},{9,5},... | collective-permute-start | bytes 208904 | tf_op jit(solution)/shard_map/ppermute | solution.py:281
  103.0 6.7 %collective-permute-start.32 = (f32[17,8,128]{2,1,0:T(8,128)S(1)}, f32[17,8,128]{2,1,0:T(8,128)S(1)}, u32[]{:S(2)}, u32[]{:S(2)}) collective-permute-start(f32[17,8,128]{2,1,0:T(8,128)S(1)} %pad_maximum_fusion.8), channel_id=1, source_target_pairs={{0,8},{1,9},{2,10},{3,11},{4,12},{5,13},{6,14},{7,15},{8,0},{9,1},... | collective-permute-start | bytes 208904 | tf_op jit(solution)/shard_map/ppermute | solution.py:281
  103.0 6.7 %collective-permute-start.31 = (f32[17,8,128]{2,1,0:T(8,128)S(1)}, f32[17,8,128]{2,1,0:T(8,128)S(1)}, u32[]{:S(2)}, u32[]{:S(2)}) collective-permute-start(f32[17,8,128]{2,1,0:T(8,128)S(1)} %pad_maximum_fusion.8), channel_id=1, source_target_pairs={{0,4},{1,5},{2,6},{3,7},{4,0},{5,1},{6,2},{7,3},{8,12},{9,13},{10,... | collective-permute-start | bytes 208904 | tf_op jit(solution)/shard_map/ppermute | solution.py:281
  105.1 12.8 %collective-permute-start.38 = (f32[64,2,8,128]{3,2,1,0:T(8,128)S(1)}, f32[64,2,8,128]{3,2,1,0:T(8,128)S(1)}, u32[]{:S(2)}, u32[]{:S(2)}) collective-permute-start(f32[64,2,8,128]{3,2,1,0:T(8,128)S(1)} %get-tuple-element.147.mine), channel_id=1, source_target_pairs={{0,16},{16,0},{1,17},{17,1},{2,18},{18,2},{3,19},{19,3},{4,20},{20... | collective-permute-start | bytes 1572872 | tf_op jit(solution)/shard_map/ppermute | solution.py:284
  109.9 5.6 %collective-permute-start.36 = (f32[33,8,128]{2,1,0:T(8,128)S(1)}, f32[33,8,128]{2,1,0:T(8,128)S(1)}, u32[]{:S(2)}, u32[]{:S(2)}) collective-permute-start(f32[33,8,128]{2,1,0:T(8,128)S(1)} %get-tuple-element.167), channel_id=1, source_target_pairs={{0,2},{1,3},{2,0},{3,1},{4,6},{5,7},{6,4},{7,5},{8,10},{9,11},{10,... | collective-permute-start | bytes 405512 | tf_op jit(solution)/shard_map/ppermute | solution.py:281
  115.5 8.0 %collective-permute-start.37 = (f32[66,8,128]{2,1,0:T(8,128)S(1)}, f32[66,8,128]{2,1,0:T(8,128)S(1)}, u32[]{:S(2)}, u32[]{:S(2)}) collective-permute-start(f32[66,8,128]{2,1,0:T(8,128)S(1)} %constant_dynamic-update-slice_fusion.57.near_b), channel_id=1, source_target_pairs={{0,1},{1,0},{2,3},{3,2},{4,5},{5,4},{6,7},{7,6},{8,9},{9,8},{10,11... | collective-permute-start | bytes 811016 | tf_op jit(solution)/shard_map/ppermute | solution.py:281
  116.3 7.2 %collective-permute-start.35 = (f32[64,8,128]{2,1,0:T(8,128)S(1)}, f32[64,8,128]{2,1,0:T(8,128)S(1)}, u32[]{:S(2)}, u32[]{:S(2)}) collective-permute-start(f32[64,8,128]{2,1,0:T(8,128)S(1)} %constant_dynamic-update-slice_fusion.47.near_a), channel_id=1, source_target_pairs={{0,2},{1,3},{2,0},{3,1},{4,6},{5,7},{6,4},{7,5},{8,10},{9,11},{10,... | collective-permute-start | bytes 786440 | tf_op jit(solution)/shard_map/ppermute | solution.py:281
  126.7 11.4 %collective-permute-start.39 = (f32[64,2,8,128]{3,2,1,0:T(8,128)S(1)}, f32[64,2,8,128]{3,2,1,0:T(8,128)S(1)}, u32[]{:S(2)}, u32[]{:S(2)}) collective-permute-start(f32[64,2,8,128]{3,2,1,0:T(8,128)S(1)} %get-tuple-element.162.mine), channel_id=1, source_target_pairs={{0,16},{16,0},{1,17},{17,1},{2,18},{18,2},{3,19},{19,3},{4,20},{20... | collective-permute-start | bytes 1572872 | tf_op jit(solution)/shard_map/ppermute | solution.py:284
  (9 other events, 72.3 us)

commit v18 on v16

--- a/solution.py
+++ b/solution.py
@@ -37,7 +37,9 @@
     return jnp.sum(value, axis=1, keepdims=True)
 
 
-def respond(block, load, gamma, energy, answer, last=False):
+def respond(block, loads, gamma, energy, answer, last=False):
+    load = loads[0]
+    load[...] = functools.reduce(jnp.add, [part[...] for part in loads])
     ntile, ncase, width = load.shape
     value = jnp.concatenate([load[i] for i in range(ntile)], axis=1)
     high = value.astype(jnp.bfloat16)
@@ -97,7 +99,7 @@
     a_far, refs = refs[:3], refs[3:]
     b_near, refs = refs[:4], refs[4:]
     b_far, refs = refs[: nz - 1], refs[nz - 1 :]
-    near, far, on, r_out, comp, answer, load, facts, sems = refs
+    near, far, on, r_out, comp, answer, *loads, facts, sems = refs
     first, second = cut * nh, (room - cut) * nh
     blocks = []
     for z in range(nz):
@@ -110,7 +112,8 @@
         rows = pl.ds(at_two + second + lines, extra - lines)
         copies.append(pltpu.make_async_copy(two.at[rows], facts.at[i], sems.at[i]))
         copies[-1].start()
-    load[...] = jnp.zeros_like(load)
+    for load in loads:
+        load[...] = jnp.zeros_like(load)
     gamma = energy = jnp.zeros(r_out.shape[2:], jnp.float32)
     for i, (one, at_one, two, at_two) in enumerate(blocks):
         at_comp = at_two + second
@@ -127,13 +130,13 @@
             else:
                 r = two[at_two + (j - cut) * nh : at_two + (j - cut + 1) * nh]
             r_out[row] = r
-            load[pl.ds(slot, nh)] += r
+            loads[j % len(loads)][pl.ds(slot, nh)] += r
             for h in range(nh):
                 line, sub = divmod(j * nh + h, SUBLANES)
                 square = r[h] * r[h]
                 gamma = gamma + square
                 energy = energy + two[at_comp + line, sub : sub + 1, :] * square
-    respond(block, load, gamma, energy, answer)
+    respond(block, loads, gamma, energy, answer)
 
 
 def tree(values):
@@ -156,8 +159,9 @@
         s_in, *refs = refs
     if not last:
         r, s, *refs = refs
-    answer, part, known_out, load, resp = refs
-    load[...] = jnp.zeros_like(load)
+    answer, part, known_out, *loads, resp = refs
+    for load in loads:
+        load[...] = jnp.zeros_like(load)
     nrow, _, ncase, width = r_in.shape
     at = 0
     for piece in (near_a, far_a, near_b, far_b):
@@ -193,14 +197,14 @@
                 residual = residual - alpha * image
                 if not last:
                     r[row, h], s[row, h] = residual, image
-                load[near + h] += residual
+                loads[j % len(loads)][near + h] += residual
                 square = residual * residual
                 gamma = gamma + square
                 energy = energy + c * square
         return gamma, energy
 
     gamma, energy = lax.fori_loop(0, nrow // room, pair, (zero, zero))
-    respond(block, load, gamma, energy, answer, last=last)
+    respond(block, loads, gamma, energy, answer, last=last)
 
 
 def list_kernel(first, keep, known, comp, mine, theirs, *refs):
@@ -354,7 +358,7 @@
     ]
     field = f32(nrow, nh, ncase, LANES)
     answer = f32(per, ncase, LANES)
-    load = pltpu.VMEM((nslot * nh, ncase, LANES), jnp.float32)
+    loads = [pltpu.VMEM((nslot * nh, ncase, LANES), jnp.float32)] * 4
     spread = pltpu.VMEM((nsub * per, ncase, LANES), jnp.float32)
     near, far, on, home_r, comp, own = pl.pallas_call(
         functools.partial(start_kernel, nh, cut, room, lines, extra, nz),
@@ -363,7 +367,7 @@
         in_specs=[VMEM] * (2 * nz + 7),
         out_specs=(SMEM,) * 3 + (VMEM,) * 3,
         scratch_shapes=[
-            load,
+            *loads,
             pltpu.SMEM((nsub, deep, SUBLANES, LANES), jnp.float32),
             pltpu.SemaphoreType.DMA((nsub,)),
         ],
@@ -419,7 +423,7 @@
             known,
             block,
             *state,
-            scratch=[load, spread],
+            scratch=[*loads, spread],
         )
     sums = lax.all_to_all(own, ("body", "sub"), split_axis=0, concat_axis=0, tiled=True)
     return call(

time: 140 us -> 139 us (level)
  transfers between devices with their start and end apart: 39 -> 39, of which waited for: 21 -> 20; matrix products, arithmetic and copies ran while one was open for 1% -> 1% of each run, Pallas kernels for 4% -> 4%
where the time goes in v18:
time: 139 us
  waiting for transfers between devices  54.1 us (39%)
  starting transfers between devices  46.3 us (33%)
  Pallas kernels  20.9 us (15%)
  blocking collectives  11.8 us (8%)
  local copies, waits for them, and re-layouts  2.49 us (2%)
  other arithmetic  1.58 us (1%)
    ppermute x33, waiting for transfers between devices, swap(): return lax.ppermute(value, 'sub', [(i, i ^ far) for i in range(nsub)])  50.3 us
    ppermute x33, starting transfers between devices, swap(): return lax.ppermute(value, 'sub', [(i, i ^ far) for i in range(nsub)])  46.2 us
    pallas_call x9, Pallas kernels, call(): pl.pallas_call(kernel, out_shape=tuple(out_shape) if several else out_sha...  17.5 us
    all_to_all x1, blocking collectives, on_device(): lax.all_to_all(own, ('body', 'sub'), split_axis=0, concat_axis=0, tiled=T...  11.8 us
    ppermute x6, waiting for transfers between devices, sibling(): lax.ppermute(value, 'body', [(i, nbody - 1 - i) for i in range(nbody)])  3.76 us
    pallas_call x1, Pallas kernels, on_device(): pl.pallas_call(functools.partial(start_kernel, nh, cut, room, lines, extr...  3.44 us
  transfers between devices with their start and end apart: 39, of which 20 were waited for; matrix products, arithmetic and copies ran while one was open for 1% of the time, Pallas kernels for 4%

profile of v18, /device:TPU:0, one launch (start us, length us, event | category | flops | bytes accessed | tf_op | source)
XLA Modules:
  0.0 138.8 jit_solution(17205176588306733678)
XLA Ops:
  4.2 5.1 %collective-permute-start = (f32[32,8,128]{2,1,0:T(8,128)S(1)}, f32[32,8,128]{2,1,0:T(8,128)S(1)}, u32[]{:S(2)}, u32[]{:S(2)}) collective-permute-start(f32[32,8,128]{2,1,0:T(8,128)S(1)} %get-tuple-element.81), channel_id=1, source_target_pairs={{0,12},{1,13},{2,14},{3,15},{4,8},{5,9},{6,10},{7,11},{8,4},{9,5},... | collective-permute-start | bytes 393224 | tf_op jit(solution)/shard_map/ppermute | solution.py:285
  15.5 3.5 %shard_map.75.block = bf16[2048,2048]{1,0:T(8,128)(2,1)S(1)} custom-call(bf16[2048,2048]{1,0:T(8,128)(2,1)} %bitcast.118), custom_call_target="tpu_custom_call" | custom-call | bytes 16777216 | tf_op jit(solution)/shard_map/pallas_call | solution.py:25
  18.9 2.8 %collective-permute-done.1.refs_2_ = f32[32,8,128]{2,1,0:T(8,128)S(1)} collective-permute-done((f32[32,8,128]{2,1,0:T(8,128)S(1)}, f32[32,8,128]{2,1,0:T(8,128)S(1)}, u32[]{:S(2)}, u32[]{:S(2)}) %collective-permute-start.1) | collective-permute-done | bytes 131104 | tf_op jit(solution)/shard_map/ppermute | solution.py:285
  23.9 3.3 %collective-permute-start.9 = (f32[44,8,128]{2,1,0:T(8,128)S(1)}, f32[44,8,128]{2,1,0:T(8,128)S(1)}, u32[]{:S(2)}, u32[]{:S(2)}) collective-permute-start(f32[44,8,128]{2,1,0:T(8,128)S(1)} %pad_maximum_fusion), channel_id=1, source_target_pairs={{0,4},{1,5},{2,6},{3,7},{4,0},{5,1},{6,2},{7,3},{8,12},{9,13},{10,... | collective-permute-start | bytes 540680 | tf_op jit(solution)/shard_map/ppermute | solution.py:285
  27.3 1.9 %collective-permute-start.8 = (f32[32,8,128]{2,1,0:T(8,128)S(1)}, f32[32,8,128]{2,1,0:T(8,128)S(1)}, u32[]{:S(2)}, u32[]{:S(2)}) collective-permute-start(f32[32,8,128]{2,1,0:T(8,128)S(1)} %pad_maximum_fusion.8), channel_id=1, source_target_pairs={{0,3},{1,2},{2,1},{3,0},{4,7},{5,6},{6,5},{7,4},{8,11},{9,10},{10,... | collective-permute-start | bytes 393224 | tf_op jit(solution)/shard_map/ppermute | solution.py:285
  30.1 3.9 %collective-permute-done.8.refs_6_ = f32[32,8,128]{2,1,0:T(8,128)S(1)} collective-permute-done((f32[32,8,128]{2,1,0:T(8,128)S(1)}, f32[32,8,128]{2,1,0:T(8,128)S(1)}, u32[]{:S(2)}, u32[]{:S(2)}) %collective-permute-start.8) | collective-permute-done | bytes 131104 | tf_op jit(solution)/shard_map/ppermute | solution.py:285
  34.9 4.0 %collective-permute-done.6.refs_4_ = f32[32,8,128]{2,1,0:T(8,128)S(1)} collective-permute-done((f32[32,8,128]{2,1,0:T(8,128)S(1)}, f32[32,8,128]{2,1,0:T(8,128)S(1)}, u32[]{:S(2)}, u32[]{:S(2)}) %collective-permute-start.6) | collective-permute-done | bytes 131104 | tf_op jit(solution)/shard_map/ppermute | solution.py:285
  39.0 3.4 %shard_map.76 = (s32[128]{0:T(128)S(1)}, s32[128]{0:T(128)S(1)}, f32[128]{0:T(128)S(1)}, f32[128,2,8,128]{3,2,1,0:T(8,128)S(1)}, f32[32,8,128]{2,1,0:T(8,128)S(1)}, /*index=5*/f32[17,8,128]{2,1,0:T(8,128)S(1)}) custom-call(bf16[2048,2048]{1,0:T(8,128)(2,1)S(1)} %shard_map.75.block, f32[32,8,128]{2,1,0:T(8,128)S(1)} %get-tuple-element.91.refs_0_, ...), custom_call_target="tpu_custom_call" | custom-call | tf_op jit(solution)/shard_map/pallas_call | solution.py:363
  43.8 1.9 %collective-permute-start.13 = (f32[17,8,128]{2,1,0:T(8,128)S(1)}, f32[17,8,128]{2,1,0:T(8,128)S(1)}, u32[]{:S(2)}, u32[]{:S(2)}) collective-permute-start(f32[17,8,128]{2,1,0:T(8,128)S(1)} %pad_maximum_fusion.12), channel_id=1, source_target_pairs={{0,12},{1,13},{2,14},{3,15},{4,8},{5,9},{6,10},{7,11},{8,4},{9,5},... | collective-permute-start | bytes 208904 | tf_op jit(solution)/shard_map/ppermute | solution.py:285
  45.7 2.6 %collective-permute-start.15 = (f32[17,8,128]{2,1,0:T(8,128)S(1)}, f32[17,8,128]{2,1,0:T(8,128)S(1)}, u32[]{:S(2)}, u32[]{:S(2)}) collective-permute-start(f32[17,8,128]{2,1,0:T(8,128)S(1)} %pad_maximum_fusion.12), channel_id=1, source_target_pairs={{0,4},{1,5},{2,6},{3,7},{4,0},{5,1},{6,2},{7,3},{8,12},{9,13},{10,... | collective-permute-start | bytes 208904 | tf_op jit(solution)/shard_map/ppermute | solution.py:285
  48.3 2.5 %collective-permute-done.13 = f32[17,8,128]{2,1,0:T(8,128)S(1)} collective-permute-done((f32[17,8,128]{2,1,0:T(8,128)S(1)}, f32[17,8,128]{2,1,0:T(8,128)S(1)}, u32[]{:S(2)}, u32[]{:S(2)}) %collective-permute-start.13) | collective-permute-done | bytes 69664 | tf_op jit(solution)/shard_map/ppermute | solution.py:285
  50.8 2.1 %collective-permute-done.14 = f32[17,8,128]{2,1,0:T(8,128)S(1)} collective-permute-done((f32[17,8,128]{2,1,0:T(8,128)S(1)}, f32[17,8,128]{2,1,0:T(8,128)S(1)}, u32[]{:S(2)}, u32[]{:S(2)}) %collective-permute-start.14) | collective-permute-done | bytes 69664 | tf_op jit(solution)/shard_map/ppermute | solution.py:285
  55.4 3.5 %collective-permute-done.18 = f32[36,8,128]{2,1,0:T(8,128)S(1)} collective-permute-done((f32[36,8,128]{2,1,0:T(8,128)S(1)}, f32[36,8,128]{2,1,0:T(8,128)S(1)}, u32[]{:S(2)}, u32[]{:S(2)}) %collective-permute-start.18) | collective-permute-done | bytes 147488 | tf_op jit(solution)/shard_map/ppermute | solution.py:285
  61.2 5.9 %collective-permute-done.17.far_a = f32[64,8,128]{2,1,0:T(8,128)S(1)} collective-permute-done((f32[64,8,128]{2,1,0:T(8,128)S(1)}, f32[64,8,128]{2,1,0:T(8,128)S(1)}, u32[]{:S(2)}, u32[]{:S(2)}) %collective-permute-start.17) | collective-permute-done | bytes 262176 | tf_op jit(solution)/shard_map/ppermute | solution.py:285
  67.0 2.7 %shard_map.77 = (f32[128,2,8,128]{3,2,1,0:T(8,128)S(1)}, f32[128,2,8,128]{3,2,1,0:T(8,128)S(1)}, f32[17,8,128]{2,1,0:T(8,128)S(1)}, f32[64,2,8,128]{3,2,1,0:T(8,128)S(1)}, f32[8,128]{1,0:T(8,128)S(1)}) custom-call(s32[128]{0:T(128)S(1)} %get-tuple-element.99.place, s32[128]{0:T(128)S(1)} %get-tuple-element.100.away, f32[128]{0:T(128)S(1)} %get-tuple-element.101.keep, ...), custom_call_target="tpu_custom_call" | custom-call | tf_op jit(solution)/shard_map/pallas_call | solution.py:25
  71.0 2.4 %collective-permute-start.21 = (f32[17,8,128]{2,1,0:T(8,128)S(1)}, f32[17,8,128]{2,1,0:T(8,128)S(1)}, u32[]{:S(2)}, u32[]{:S(2)}) collective-permute-start(f32[17,8,128]{2,1,0:T(8,128)S(1)} %pad_maximum_fusion.13), channel_id=1, source_target_pairs={{0,12},{1,13},{2,14},{3,15},{4,8},{5,9},{6,10},{7,11},{8,4},{9,5},... | collective-permute-start | bytes 208904 | tf_op jit(solution)/shard_map/ppermute | solution.py:285
  73.4 2.0 %collective-permute-start.23 = (f32[17,8,128]{2,1,0:T(8,128)S(1)}, f32[17,8,128]{2,1,0:T(8,128)S(1)}, u32[]{:S(2)}, u32[]{:S(2)}) collective-permute-start(f32[17,8,128]{2,1,0:T(8,128)S(1)} %pad_maximum_fusion.13), channel_id=1, source_target_pairs={{0,4},{1,5},{2,6},{3,7},{4,0},{5,1},{6,2},{7,3},{8,12},{9,13},{10,... | collective-permute-start | bytes 208904 | tf_op jit(solution)/shard_map/ppermute | solution.py:285
  75.5 2.5 %collective-permute-done.21 = f32[17,8,128]{2,1,0:T(8,128)S(1)} collective-permute-done((f32[17,8,128]{2,1,0:T(8,128)S(1)}, f32[17,8,128]{2,1,0:T(8,128)S(1)}, u32[]{:S(2)}, u32[]{:S(2)}) %collective-permute-start.21) | collective-permute-done | bytes 69664 | tf_op jit(solution)/shard_map/ppermute | solution.py:285
  78.0 2.1 %collective-permute-done.22 = f32[17,8,128]{2,1,0:T(8,128)S(1)} collective-permute-done((f32[17,8,128]{2,1,0:T(8,128)S(1)}, f32[17,8,128]{2,1,0:T(8,128)S(1)}, u32[]{:S(2)}, u32[]{:S(2)}) %collective-permute-start.22) | collective-permute-done | bytes 69664 | tf_op jit(solution)/shard_map/ppermute | solution.py:285
  83.0 3.0 %collective-permute-done.26 = f32[36,8,128]{2,1,0:T(8,128)S(1)} collective-permute-done((f32[36,8,128]{2,1,0:T(8,128)S(1)}, f32[36,8,128]{2,1,0:T(8,128)S(1)}, u32[]{:S(2)}, u32[]{:S(2)}) %collective-permute-start.26) | collective-permute-done | bytes 147488 | tf_op jit(solution)/shard_map/ppermute | solution.py:285
  89.7 4.7 %collective-permute-done.25.far_a = f32[64,8,128]{2,1,0:T(8,128)S(1)} collective-permute-done((f32[64,8,128]{2,1,0:T(8,128)S(1)}, f32[64,8,128]{2,1,0:T(8,128)S(1)}, u32[]{:S(2)}, u32[]{:S(2)}) %collective-permute-start.25) | collective-permute-done | bytes 262176 | tf_op jit(solution)/shard_map/ppermute | solution.py:285
  94.4 2.9 %shard_map.79 = (f32[128,2,8,128]{3,2,1,0:T(8,128)S(1)}, f32[128,2,8,128]{3,2,1,0:T(8,128)S(1)}, f32[17,8,128]{2,1,0:T(8,128)S(1)}, f32[64,2,8,128]{3,2,1,0:T(8,128)S(1)}, f32[8,128]{1,0:T(8,128)S(1)}) custom-call(s32[128]{0:T(128)S(1)} %get-tuple-element.99.place, s32[128]{0:T(128)S(1)} %get-tuple-element.100.away, f32[128]{0:T(128)S(1)} %get-tuple-element.101.keep, ...), custom_call_target="tpu_custom_call" | custom-call | tf_op jit(solution)/shard_map/pallas_call | solution.py:25
  98.6 2.2 %collective-permute-start.30 = (f32[17,8,128]{2,1,0:T(8,128)S(1)}, f32[17,8,128]{2,1,0:T(8,128)S(1)}, u32[]{:S(2)}, u32[]{:S(2)}) collective-permute-start(f32[17,8,128]{2,1,0:T(8,128)S(1)} %pad_maximum_fusion.14), channel_id=1, source_target_pairs={{0,12},{1,13},{2,14},{3,15},{4,8},{5,9},{6,10},{7,11},{8,4},{9,5},... | collective-permute-start | bytes 208904 | tf_op jit(solution)/shard_map/ppermute | solution.py:285
  100.8 2.2 %collective-permute-start.32 = (f32[17,8,128]{2,1,0:T(8,128)S(1)}, f32[17,8,128]{2,1,0:T(8,128)S(1)}, u32[]{:S(2)}, u32[]{:S(2)}) collective-permute-start(f32[17,8,128]{2,1,0:T(8,128)S(1)} %pad_maximum_fusion.14), channel_id=1, source_target_pairs={{0,4},{1,5},{2,6},{3,7},{4,0},{5,1},{6,2},{7,3},{8,12},{9,13},{10,... | collective-permute-start | bytes 208904 | tf_op jit(solution)/shard_map/ppermute | solution.py:285
  103.0 2.5 %collective-permute-done.30 = f32[17,8,128]{2,1,0:T(8,128)S(1)} collective-permute-done((f32[17,8,128]{2,1,0:T(8,128)S(1)}, f32[17,8,128]{2,1,0:T(8,128)S(1)}, u32[]{:S(2)}, u32[]{:S(2)}) %collective-permute-start.30) | collective-permute-done | bytes 69664 | tf_op jit(solution)/shard_map/ppermute | solution.py:285
  105.5 2.1 %collective-permute-done.31 = f32[17,8,128]{2,1,0:T(8,128)S(1)} collective-permute-done((f32[17,8,128]{2,1,0:T(8,128)S(1)}, f32[17,8,128]{2,1,0:T(8,128)S(1)}, u32[]{:S(2)}, u32[]{:S(2)}) %collective-permute-start.31) | collective-permute-done | bytes 69664 | tf_op jit(solution)/shard_map/ppermute | solution.py:285
  107.8 1.6 %collective-permute-start.35 = (f32[36,8,128]{2,1,0:T(8,128)S(1)}, f32[36,8,128]{2,1,0:T(8,128)S(1)}, u32[]{:S(2)}, u32[]{:S(2)}) collective-permute-start(f32[36,8,128]{2,1,0:T(8,128)S(1)} %pad_maximum_fusion.5), channel_id=1, source_target_pairs={{0,2},{1,3},{2,0},{3,1},{4,6},{5,7},{6,4},{7,5},{8,10},{9,11},{10,... | collective-permute-start | bytes 442376 | tf_op jit(solution)/shard_map/ppermute | solution.py:285
  110.4 3.2 %collective-permute-done.35 = f32[36,8,128]{2,1,0:T(8,128)S(1)} collective-permute-done((f32[36,8,128]{2,1,0:T(8,128)S(1)}, f32[36,8,128]{2,1,0:T(8,128)S(1)}, u32[]{:S(2)}, u32[]{:S(2)}) %collective-permute-start.35) | collective-permute-done | bytes 147488 | tf_op jit(solution)/shard_map/ppermute | solution.py:285
  117.2 4.6 %collective-permute-done.34.far_a = f32[64,8,128]{2,1,0:T(8,128)S(1)} collective-permute-done((f32[64,8,128]{2,1,0:T(8,128)S(1)}, f32[64,8,128]{2,1,0:T(8,128)S(1)}, u32[]{:S(2)}, u32[]{:S(2)}) %collective-permute-start.34) | collective-permute-done | bytes 262176 | tf_op jit(solution)/shard_map/ppermute | solution.py:285
  121.8 2.9 %shard_map.81 = (f32[32,8,128]{2,1,0:T(8,128)S(1)}, f32[64,2,8,128]{3,2,1,0:T(8,128)S(1)}, f32[8,128]{1,0:T(8,128)S(1)}) custom-call(s32[128]{0:T(128)S(1)} %get-tuple-element.99.place, s32[128]{0:T(128)S(1)} %get-tuple-element.100.away, f32[128]{0:T(128)S(1)} %get-tuple-element.101.keep, s32[64]{0:T(128)S(1)} %get-tuple-element.102.picked, ...), custom_call_target="tpu_custom_call" | custom-call | tf_op jit(solution)/shard_map/pallas_call | solution.py:25
  124.8 11.8 %all_to_all.5.sums = f32[32,8,128]{2,1,0:T(8,128)S(1)} all-to-all(f32[32,8,128]{2,1,0:T(8,128)S(1)} %get-tuple-element.148), channel_id=1, replica_groups=mesh['body'=2,'sub'=16] {'body','sub'}, dimensions={0} | all-to-all | bytes 262144 | tf_op jit(solution)/shard_map/all_to_all | solution.py:428
  136.6 2.2 %shard_map.82 = f32[8,64,256]{2,1,0:T(8,128)} custom-call(f32[64]{0:T(128)S(1)} %get-tuple-element.231.keep, f32[32,8,128]{2,1,0:T(8,128)S(1)} %all_to_all.5.sums, f32[8,128]{1,0:T(8,128)S(1)} %get-tuple-element.149.known, f32[64,256]{1,0:T(8,128)S(1)} %copy-done, f32[64,2,8,128]{3,2,1,0:T(8,128)S(1)} %get-tuple-element.150.mine, ...), custom_call_target="tpu_custom_call" | custom-call | tf_op jit(solution)/shard_map/pallas_call | solution.py:25
  (137 shorter events, 34.1 us)
Async XLA Ops:
  4.2 10.7 %collective-permute-start = (f32[32,8,128]{2,1,0:T(8,128)S(1)}, f32[32,8,128]{2,1,0:T(8,128)S(1)}, u32[]{:S(2)}, u32[]{:S(2)}) collective-permute-start(f32[32,8,128]{2,1,0:T(8,128)S(1)} %get-tuple-element.81), channel_id=1, source_target_pairs={{0,12},{1,13},{2,14},{3,15},{4,8},{5,9},{6,10},{7,11},{8,4},{9,5},... | collective-permute-start | bytes 393224 | tf_op jit(solution)/shard_map/ppermute | solution.py:285
  11.3 10.5 %collective-permute-start.3 = (f32[44,8,128]{2,1,0:T(8,128)S(1)}, f32[44,8,128]{2,1,0:T(8,128)S(1)}, u32[]{:S(2)}, u32[]{:S(2)}) collective-permute-start(f32[44,8,128]{2,1,0:T(8,128)S(1)} %get-tuple-element.87), channel_id=1, source_target_pairs={{0,1},{1,0},{2,3},{3,2},{4,5},{5,4},{6,7},{7,6},{8,9},{9,8},{10,11... | collective-permute-start | bytes 540680 | tf_op jit(solution)/shard_map/ppermute | solution.py:285
  12.9 9.6 %collective-permute-start.4 = (f32[44,8,128]{2,1,0:T(8,128)S(1)}, f32[44,8,128]{2,1,0:T(8,128)S(1)}, u32[]{:S(2)}, u32[]{:S(2)}) collective-permute-start(f32[44,8,128]{2,1,0:T(8,128)S(1)} %get-tuple-element.88), channel_id=1, source_target_pairs={{0,2},{1,3},{2,0},{3,1},{4,6},{5,7},{6,4},{7,5},{8,10},{9,11},{10,... | collective-permute-start | bytes 540680 | tf_op jit(solution)/shard_map/ppermute | solution.py:285
  14.4 8.1 %collective-permute-start.5 = (f32[44,8,128]{2,1,0:T(8,128)S(1)}, f32[44,8,128]{2,1,0:T(8,128)S(1)}, u32[]{:S(2)}, u32[]{:S(2)}) collective-permute-start(f32[44,8,128]{2,1,0:T(8,128)S(1)} %get-tuple-element.89), channel_id=1, source_target_pairs={{0,3},{1,2},{2,1},{3,0},{4,7},{5,6},{6,5},{7,4},{8,11},{9,10},{10,... | collective-permute-start | bytes 540680 | tf_op jit(solution)/shard_map/ppermute | solution.py:285
  14.9 6.9 %collective-permute-start.1 = (f32[32,8,128]{2,1,0:T(8,128)S(1)}, f32[32,8,128]{2,1,0:T(8,128)S(1)}, u32[]{:S(2)}, u32[]{:S(2)}) collective-permute-start(f32[32,8,128]{2,1,0:T(8,128)S(1)} %get-tuple-element.82), channel_id=1, source_target_pairs={{0,8},{1,9},{2,10},{3,11},{4,12},{5,13},{6,14},{7,15},{8,0},{9,1},... | collective-permute-start | bytes 393224 | tf_op jit(solution)/shard_map/ppermute | solution.py:285
  14.9 6.9 %collective-permute-start.2 = (f32[32,8,128]{2,1,0:T(8,128)S(1)}, f32[32,8,128]{2,1,0:T(8,128)S(1)}, u32[]{:S(2)}, u32[]{:S(2)}) collective-permute-start(f32[32,8,128]{2,1,0:T(8,128)S(1)} %get-tuple-element.83), channel_id=1, source_target_pairs={{0,4},{1,5},{2,6},{3,7},{4,0},{5,1},{6,2},{7,3},{8,12},{9,13},{10,... | collective-permute-start | bytes 393224 | tf_op jit(solution)/shard_map/ppermute | solution.py:285
  22.6 16.4 %collective-permute-start.11 = (f32[44,8,128]{2,1,0:T(8,128)S(1)}, f32[44,8,128]{2,1,0:T(8,128)S(1)}, u32[]{:S(2)}, u32[]{:S(2)}) collective-permute-start(f32[44,8,128]{2,1,0:T(8,128)S(1)} %pad_maximum_fusion.2), channel_id=1, source_target_pairs={{0,12},{1,13},{2,14},{3,15},{4,8},{5,9},{6,10},{7,11},{8,4},{9,5},... | collective-permute-start | bytes 540680 | tf_op jit(solution)/shard_map/ppermute | solution.py:285
  23.5 15.5 %collective-permute-start.10 = (f32[44,8,128]{2,1,0:T(8,128)S(1)}, f32[44,8,128]{2,1,0:T(8,128)S(1)}, u32[]{:S(2)}, u32[]{:S(2)}) collective-permute-start(f32[44,8,128]{2,1,0:T(8,128)S(1)} %pad_maximum_fusion.1), channel_id=1, source_target_pairs={{0,8},{1,9},{2,10},{3,11},{4,12},{5,13},{6,14},{7,15},{8,0},{9,1},... | collective-permute-start | bytes 540680 | tf_op jit(solution)/shard_map/ppermute | solution.py:285
  23.9 15.1 %collective-permute-start.9 = (f32[44,8,128]{2,1,0:T(8,128)S(1)}, f32[44,8,128]{2,1,0:T(8,128)S(1)}, u32[]{:S(2)}, u32[]{:S(2)}) collective-permute-start(f32[44,8,128]{2,1,0:T(8,128)S(1)} %pad_maximum_fusion), channel_id=1, source_target_pairs={{0,4},{1,5},{2,6},{3,7},{4,0},{5,1},{6,2},{7,3},{8,12},{9,13},{10,... | collective-permute-start | bytes 540680 | tf_op jit(solution)/shard_map/ppermute | solution.py:285
  27.3 6.8 %collective-permute-start.8 = (f32[32,8,128]{2,1,0:T(8,128)S(1)}, f32[32,8,128]{2,1,0:T(8,128)S(1)}, u32[]{:S(2)}, u32[]{:S(2)}) collective-permute-start(f32[32,8,128]{2,1,0:T(8,128)S(1)} %pad_maximum_fusion.8), channel_id=1, source_target_pairs={{0,3},{1,2},{2,1},{3,0},{4,7},{5,6},{6,5},{7,4},{8,11},{9,10},{10,... | collective-permute-start | bytes 393224 | tf_op jit(solution)/shard_map/ppermute | solution.py:285
  29.1 5.8 %collective-permute-start.7 = (f32[32,8,128]{2,1,0:T(8,128)S(1)}, f32[32,8,128]{2,1,0:T(8,128)S(1)}, u32[]{:S(2)}, u32[]{:S(2)}) collective-permute-start(f32[32,8,128]{2,1,0:T(8,128)S(1)} %pad_maximum_fusion.7), channel_id=1, source_target_pairs={{0,2},{1,3},{2,0},{3,1},{4,6},{5,7},{6,4},{7,5},{8,10},{9,11},{10,... | collective-permute-start | bytes 393224 | tf_op jit(solution)/shard_map/ppermute | solution.py:285
  43.8 7.0 %collective-permute-start.13 = (f32[17,8,128]{2,1,0:T(8,128)S(1)}, f32[17,8,128]{2,1,0:T(8,128)S(1)}, u32[]{:S(2)}, u32[]{:S(2)}) collective-permute-start(f32[17,8,128]{2,1,0:T(8,128)S(1)} %pad_maximum_fusion.12), channel_id=1, source_target_pairs={{0,12},{1,13},{2,14},{3,15},{4,8},{5,9},{6,10},{7,11},{8,4},{9,5},... | collective-permute-start | bytes 208904 | tf_op jit(solution)/shard_map/ppermute | solution.py:285
  45.7 7.2 %collective-permute-start.14 = (f32[17,8,128]{2,1,0:T(8,128)S(1)}, f32[17,8,128]{2,1,0:T(8,128)S(1)}, u32[]{:S(2)}, u32[]{:S(2)}) collective-permute-start(f32[17,8,128]{2,1,0:T(8,128)S(1)} %pad_maximum_fusion.12), channel_id=1, source_target_pairs={{0,8},{1,9},{2,10},{3,11},{4,12},{5,13},{6,14},{7,15},{8,0},{9,1},... | collective-permute-start | bytes 208904 | tf_op jit(solution)/shard_map/ppermute | solution.py:285
  45.7 7.2 %collective-permute-start.15 = (f32[17,8,128]{2,1,0:T(8,128)S(1)}, f32[17,8,128]{2,1,0:T(8,128)S(1)}, u32[]{:S(2)}, u32[]{:S(2)}) collective-permute-start(f32[17,8,128]{2,1,0:T(8,128)S(1)} %pad_maximum_fusion.12), channel_id=1, source_target_pairs={{0,4},{1,5},{2,6},{3,7},{4,0},{5,1},{6,2},{7,3},{8,12},{9,13},{10,... | collective-permute-start | bytes 208904 | tf_op jit(solution)/shard_map/ppermute | solution.py:285
  53.0 5.8 %collective-permute-start.18 = (f32[36,8,128]{2,1,0:T(8,128)S(1)}, f32[36,8,128]{2,1,0:T(8,128)S(1)}, u32[]{:S(2)}, u32[]{:S(2)}) collective-permute-start(f32[36,8,128]{2,1,0:T(8,128)S(1)} %pad_maximum_fusion.3), channel_id=1, source_target_pairs={{0,2},{1,3},{2,0},{3,1},{4,6},{5,7},{6,4},{7,5},{8,10},{9,11},{10,... | collective-permute-start | bytes 442376 | tf_op jit(solution)/shard_map/ppermute | solution.py:285
  58.8 8.2 %collective-permute-start.19 = (f32[72,8,128]{2,1,0:T(8,128)S(1)}, f32[72,8,128]{2,1,0:T(8,128)S(1)}, u32[]{:S(2)}, u32[]{:S(2)}) collective-permute-start(f32[72,8,128]{2,1,0:T(8,128)S(1)} %constant_dynamic-update-slice_fusion.5.near_b), channel_id=1, source_target_pairs={{0,1},{1,0},{2,3},{3,2},{4,5},{5,4},{6,7},{7,6},{8,9},{9,8},{10,11... | collective-permute-start | bytes 884744 | tf_op jit(solution)/shard_map/ppermute | solution.py:285
  59.9 7.2 %collective-permute-start.17 = (f32[64,8,128]{2,1,0:T(8,128)S(1)}, f32[64,8,128]{2,1,0:T(8,128)S(1)}, u32[]{:S(2)}, u32[]{:S(2)}) collective-permute-start(f32[64,8,128]{2,1,0:T(8,128)S(1)} %constant_dynamic-update-slice_fusion.near_a), channel_id=1, source_target_pairs={{0,2},{1,3},{2,0},{3,1},{4,6},{5,7},{6,4},{7,5},{8,10},{9,11},{10,... | collective-permute-start | bytes 786440 | tf_op jit(solution)/shard_map/ppermute | solution.py:285
  71.0 7.0 %collective-permute-start.21 = (f32[17,8,128]{2,1,0:T(8,128)S(1)}, f32[17,8,128]{2,1,0:T(8,128)S(1)}, u32[]{:S(2)}, u32[]{:S(2)}) collective-permute-start(f32[17,8,128]{2,1,0:T(8,128)S(1)} %pad_maximum_fusion.13), channel_id=1, source_target_pairs={{0,12},{1,13},{2,14},{3,15},{4,8},{5,9},{6,10},{7,11},{8,4},{9,5},... | collective-permute-start | bytes 208904 | tf_op jit(solution)/shard_map/ppermute | solution.py:285
  73.4 6.7 %collective-permute-start.22 = (f32[17,8,128]{2,1,0:T(8,128)S(1)}, f32[17,8,128]{2,1,0:T(8,128)S(1)}, u32[]{:S(2)}, u32[]{:S(2)}) collective-permute-start(f32[17,8,128]{2,1,0:T(8,128)S(1)} %pad_maximum_fusion.13), channel_id=1, source_target_pairs={{0,8},{1,9},{2,10},{3,11},{4,12},{5,13},{6,14},{7,15},{8,0},{9,1},... | collective-permute-start | bytes 208904 | tf_op jit(solution)/shard_map/ppermute | solution.py:285
  73.4 6.7 %collective-permute-start.23 = (f32[17,8,128]{2,1,0:T(8,128)S(1)}, f32[17,8,128]{2,1,0:T(8,128)S(1)}, u32[]{:S(2)}, u32[]{:S(2)}) collective-permute-start(f32[17,8,128]{2,1,0:T(8,128)S(1)} %pad_maximum_fusion.13), channel_id=1, source_target_pairs={{0,4},{1,5},{2,6},{3,7},{4,0},{5,1},{6,2},{7,3},{8,12},{9,13},{10,... | collective-permute-start | bytes 208904 | tf_op jit(solution)/shard_map/ppermute | solution.py:285
  75.5 13.3 %collective-permute-start.28 = (f32[64,2,8,128]{3,2,1,0:T(8,128)S(1)}, f32[64,2,8,128]{3,2,1,0:T(8,128)S(1)}, u32[]{:S(2)}, u32[]{:S(2)}) collective-permute-start(f32[64,2,8,128]{3,2,1,0:T(8,128)S(1)} %get-tuple-element.118.mine), channel_id=1, source_target_pairs={{0,16},{16,0},{1,17},{17,1},{2,18},{18,2},{3,19},{19,3},{4,20},{20... | collective-permute-start | bytes 1572872 | tf_op jit(solution)/shard_map/ppermute | solution.py:288
  80.2 5.8 %collective-permute-start.26 = (f32[36,8,128]{2,1,0:T(8,128)S(1)}, f32[36,8,128]{2,1,0:T(8,128)S(1)}, u32[]{:S(2)}, u32[]{:S(2)}) collective-permute-start(f32[36,8,128]{2,1,0:T(8,128)S(1)} %pad_maximum_fusion.4), channel_id=1, source_target_pairs={{0,2},{1,3},{2,0},{3,1},{4,6},{5,7},{6,4},{7,5},{8,10},{9,11},{10,... | collective-permute-start | bytes 442376 | tf_op jit(solution)/shard_map/ppermute | solution.py:285
  86.0 8.3 %collective-permute-start.27 = (f32[72,8,128]{2,1,0:T(8,128)S(1)}, f32[72,8,128]{2,1,0:T(8,128)S(1)}, u32[]{:S(2)}, u32[]{:S(2)}) collective-permute-start(f32[72,8,128]{2,1,0:T(8,128)S(1)} %constant_dynamic-update-slice_fusion.15.near_b), channel_id=1, source_target_pairs={{0,1},{1,0},{2,3},{3,2},{4,5},{5,4},{6,7},{7,6},{8,9},{9,8},{10,11... | collective-permute-start | bytes 884744 | tf_op jit(solution)/shard_map/ppermute | solution.py:285
  87.2 7.2 %collective-permute-start.25 = (f32[64,8,128]{2,1,0:T(8,128)S(1)}, f32[64,8,128]{2,1,0:T(8,128)S(1)}, u32[]{:S(2)}, u32[]{:S(2)}) collective-permute-start(f32[64,8,128]{2,1,0:T(8,128)S(1)} %constant_dynamic-update-slice_fusion.10.near_a), channel_id=1, source_target_pairs={{0,2},{1,3},{2,0},{3,1},{4,6},{5,7},{6,4},{7,5},{8,10},{9,11},{10,... | collective-permute-start | bytes 786440 | tf_op jit(solution)/shard_map/ppermute | solution.py:285
  98.6 7.0 %collective-permute-start.30 = (f32[17,8,128]{2,1,0:T(8,128)S(1)}, f32[17,8,128]{2,1,0:T(8,128)S(1)}, u32[]{:S(2)}, u32[]{:S(2)}) collective-permute-start(f32[17,8,128]{2,1,0:T(8,128)S(1)} %pad_maximum_fusion.14), channel_id=1, source_target_pairs={{0,12},{1,13},{2,14},{3,15},{4,8},{5,9},{6,10},{7,11},{8,4},{9,5},... | collective-permute-start | bytes 208904 | tf_op jit(solution)/shard_map/ppermute | solution.py:285
  100.8 6.8 %collective-permute-start.31 = (f32[17,8,128]{2,1,0:T(8,128)S(1)}, f32[17,8,128]{2,1,0:T(8,128)S(1)}, u32[]{:S(2)}, u32[]{:S(2)}) collective-permute-start(f32[17,8,128]{2,1,0:T(8,128)S(1)} %pad_maximum_fusion.14), channel_id=1, source_target_pairs={{0,8},{1,9},{2,10},{3,11},{4,12},{5,13},{6,14},{7,15},{8,0},{9,1},... | collective-permute-start | bytes 208904 | tf_op jit(solution)/shard_map/ppermute | solution.py:285
  100.8 6.8 %collective-permute-start.32 = (f32[17,8,128]{2,1,0:T(8,128)S(1)}, f32[17,8,128]{2,1,0:T(8,128)S(1)}, u32[]{:S(2)}, u32[]{:S(2)}) collective-permute-start(f32[17,8,128]{2,1,0:T(8,128)S(1)} %pad_maximum_fusion.14), channel_id=1, source_target_pairs={{0,4},{1,5},{2,6},{3,7},{4,0},{5,1},{6,2},{7,3},{8,12},{9,13},{10,... | collective-permute-start | bytes 208904 | tf_op jit(solution)/shard_map/ppermute | solution.py:285
  103.0 13.1 %collective-permute-start.37 = (f32[64,2,8,128]{3,2,1,0:T(8,128)S(1)}, f32[64,2,8,128]{3,2,1,0:T(8,128)S(1)}, u32[]{:S(2)}, u32[]{:S(2)}) collective-permute-start(f32[64,2,8,128]{3,2,1,0:T(8,128)S(1)} %get-tuple-element.135.mine), channel_id=1, source_target_pairs={{0,16},{16,0},{1,17},{17,1},{2,18},{18,2},{3,19},{19,3},{4,20},{20... | collective-permute-start | bytes 1572872 | tf_op jit(solution)/shard_map/ppermute | solution.py:288
  107.8 5.8 %collective-permute-start.35 = (f32[36,8,128]{2,1,0:T(8,128)S(1)}, f32[36,8,128]{2,1,0:T(8,128)S(1)}, u32[]{:S(2)}, u32[]{:S(2)}) collective-permute-start(f32[36,8,128]{2,1,0:T(8,128)S(1)} %pad_maximum_fusion.5), channel_id=1, source_target_pairs={{0,2},{1,3},{2,0},{3,1},{4,6},{5,7},{6,4},{7,5},{8,10},{9,11},{10,... | collective-permute-start | bytes 442376 | tf_op jit(solution)/shard_map/ppermute | solution.py:285
  113.6 8.2 %collective-permute-start.36 = (f32[72,8,128]{2,1,0:T(8,128)S(1)}, f32[72,8,128]{2,1,0:T(8,128)S(1)}, u32[]{:S(2)}, u32[]{:S(2)}) collective-permute-start(f32[72,8,128]{2,1,0:T(8,128)S(1)} %constant_dynamic-update-slice_fusion.25.near_b), channel_id=1, source_target_pairs={{0,1},{1,0},{2,3},{3,2},{4,5},{5,4},{6,7},{7,6},{8,9},{9,8},{10,11... | collective-permute-start | bytes 884744 | tf_op jit(solution)/shard_map/ppermute | solution.py:285
  114.6 7.2 %collective-permute-start.34 = (f32[64,8,128]{2,1,0:T(8,128)S(1)}, f32[64,8,128]{2,1,0:T(8,128)S(1)}, u32[]{:S(2)}, u32[]{:S(2)}) collective-permute-start(f32[64,8,128]{2,1,0:T(8,128)S(1)} %constant_dynamic-update-slice_fusion.20.near_a), channel_id=1, source_target_pairs={{0,2},{1,3},{2,0},{3,1},{4,6},{5,7},{6,4},{7,5},{8,10},{9,11},{10,... | collective-permute-start | bytes 786440 | tf_op jit(solution)/shard_map/ppermute | solution.py:285
  124.7 11.9 %collective-permute-start.38 = (f32[64,2,8,128]{3,2,1,0:T(8,128)S(1)}, f32[64,2,8,128]{3,2,1,0:T(8,128)S(1)}, u32[]{:S(2)}, u32[]{:S(2)}) collective-permute-start(f32[64,2,8,128]{3,2,1,0:T(8,128)S(1)} %get-tuple-element.150.mine), channel_id=1, source_target_pairs={{0,16},{16,0},{1,17},{17,1},{2,18},{18,2},{3,19},{19,3},{4,20},{20... | collective-permute-start | bytes 1572872 | tf_op jit(solution)/shard_map/ppermute | solution.py:288
  (8 other events, 71.1 us)

commit v19 on v18

--- a/solution.py
+++ b/solution.py
@@ -203,7 +203,7 @@
                 energy = energy + c * square
         return gamma, energy
 
-    gamma, energy = lax.fori_loop(0, nrow // room, pair, (zero, zero))
+    gamma, energy = lax.fori_loop(0, nrow // room, pair, (zero, zero), unroll=2)
     respond(block, loads, gamma, energy, answer, last=last)
 
 
@@ -358,7 +358,7 @@
     ]
     field = f32(nrow, nh, ncase, LANES)
     answer = f32(per, ncase, LANES)
-    loads = [pltpu.VMEM((nslot * nh, ncase, LANES), jnp.float32)] * 4
+    loads = [pltpu.VMEM((nslot * nh, ncase, LANES), jnp.float32)] * 8
     spread = pltpu.VMEM((nsub * per, ncase, LANES), jnp.float32)
     near, far, on, home_r, comp, own = pl.pallas_call(
         functools.partial(start_kernel, nh, cut, room, lines, extra, nz),

time: 139 us -> 139 us (level)
  no operation moved by 1% of the time
where the time goes in v19:
time: 139 us
  waiting for transfers between devices  54.1 us (39%)
  starting transfers between devices  46.3 us (33%)
  Pallas kernels  20.7 us (15%)
  blocking collectives  11.8 us (8%)
  local copies, waits for them, and re-layouts  2.49 us (2%)
  other arithmetic  1.58 us (1%)
    ppermute x33, waiting for transfers between devices, swap(): return lax.ppermute(value, 'sub', [(i, i ^ far) for i in range(nsub)])  50.3 us
    ppermute x33, starting transfers between devices, swap(): return lax.ppermute(value, 'sub', [(i, i ^ far) for i in range(nsub)])  46.2 us
    pallas_call x9, Pallas kernels, call(): pl.pallas_call(kernel, out_shape=tuple(out_shape) if several else out_sha...  17.3 us
    all_to_all x1, blocking collectives, on_device(): lax.all_to_all(own, ('body', 'sub'), split_axis=0, concat_axis=0, tiled=T...  11.8 us
    ppermute x6, waiting for transfers between devices, sibling(): lax.ppermute(value, 'body', [(i, nbody - 1 - i) for i in range(nbody)])  3.78 us
    pallas_call x1, Pallas kernels, on_device(): pl.pallas_call(functools.partial(start_kernel, nh, cut, room, lines, extr...  3.44 us
  transfers between devices with their start and end apart: 39, of which 20 were waited for; matrix products, arithmetic and copies ran while one was open for 1% of the time, Pallas kernels for 4%

profile of v19, /device:TPU:0, one launch (start us, length us, event | category | flops | bytes accessed | tf_op | source)
XLA Modules:
  0.0 138.6 jit_solution(4624210477782880398)
XLA Ops:
  4.2 5.1 %collective-permute-start = (f32[32,8,128]{2,1,0:T(8,128)S(1)}, f32[32,8,128]{2,1,0:T(8,128)S(1)}, u32[]{:S(2)}, u32[]{:S(2)}) collective-permute-start(f32[32,8,128]{2,1,0:T(8,128)S(1)} %get-tuple-element.81), channel_id=1, source_target_pairs={{0,12},{1,13},{2,14},{3,15},{4,8},{5,9},{6,10},{7,11},{8,4},{9,5},... | collective-permute-start | bytes 393224 | tf_op jit(solution)/shard_map/ppermute | solution.py:285
  15.5 3.5 %shard_map.75.block = bf16[2048,2048]{1,0:T(8,128)(2,1)S(1)} custom-call(bf16[2048,2048]{1,0:T(8,128)(2,1)} %bitcast.118), custom_call_target="tpu_custom_call" | custom-call | bytes 16777216 | tf_op jit(solution)/shard_map/pallas_call | solution.py:25
  18.9 2.8 %collective-permute-done.1.refs_2_ = f32[32,8,128]{2,1,0:T(8,128)S(1)} collective-permute-done((f32[32,8,128]{2,1,0:T(8,128)S(1)}, f32[32,8,128]{2,1,0:T(8,128)S(1)}, u32[]{:S(2)}, u32[]{:S(2)}) %collective-permute-start.1) | collective-permute-done | bytes 131104 | tf_op jit(solution)/shard_map/ppermute | solution.py:285
  23.9 3.3 %collective-permute-start.9 = (f32[44,8,128]{2,1,0:T(8,128)S(1)}, f32[44,8,128]{2,1,0:T(8,128)S(1)}, u32[]{:S(2)}, u32[]{:S(2)}) collective-permute-start(f32[44,8,128]{2,1,0:T(8,128)S(1)} %pad_maximum_fusion), channel_id=1, source_target_pairs={{0,4},{1,5},{2,6},{3,7},{4,0},{5,1},{6,2},{7,3},{8,12},{9,13},{10,... | collective-permute-start | bytes 540680 | tf_op jit(solution)/shard_map/ppermute | solution.py:285
  27.3 1.9 %collective-permute-start.8 = (f32[32,8,128]{2,1,0:T(8,128)S(1)}, f32[32,8,128]{2,1,0:T(8,128)S(1)}, u32[]{:S(2)}, u32[]{:S(2)}) collective-permute-start(f32[32,8,128]{2,1,0:T(8,128)S(1)} %pad_maximum_fusion.8), channel_id=1, source_target_pairs={{0,3},{1,2},{2,1},{3,0},{4,7},{5,6},{6,5},{7,4},{8,11},{9,10},{10,... | collective-permute-start | bytes 393224 | tf_op jit(solution)/shard_map/ppermute | solution.py:285
  30.1 3.9 %collective-permute-done.8.refs_6_ = f32[32,8,128]{2,1,0:T(8,128)S(1)} collective-permute-done((f32[32,8,128]{2,1,0:T(8,128)S(1)}, f32[32,8,128]{2,1,0:T(8,128)S(1)}, u32[]{:S(2)}, u32[]{:S(2)}) %collective-permute-start.8) | collective-permute-done | bytes 131104 | tf_op jit(solution)/shard_map/ppermute | solution.py:285
  34.9 4.0 %collective-permute-done.6.refs_4_ = f32[32,8,128]{2,1,0:T(8,128)S(1)} collective-permute-done((f32[32,8,128]{2,1,0:T(8,128)S(1)}, f32[32,8,128]{2,1,0:T(8,128)S(1)}, u32[]{:S(2)}, u32[]{:S(2)}) %collective-permute-start.6) | collective-permute-done | bytes 131104 | tf_op jit(solution)/shard_map/ppermute | solution.py:285
  39.0 3.4 %shard_map.76 = (s32[128]{0:T(128)S(1)}, s32[128]{0:T(128)S(1)}, f32[128]{0:T(128)S(1)}, f32[128,2,8,128]{3,2,1,0:T(8,128)S(1)}, f32[32,8,128]{2,1,0:T(8,128)S(1)}, /*index=5*/f32[17,8,128]{2,1,0:T(8,128)S(1)}) custom-call(bf16[2048,2048]{1,0:T(8,128)(2,1)S(1)} %shard_map.75.block, f32[32,8,128]{2,1,0:T(8,128)S(1)} %get-tuple-element.91.refs_0_, ...), custom_call_target="tpu_custom_call" | custom-call | tf_op jit(solution)/shard_map/pallas_call | solution.py:363
  43.8 1.9 %collective-permute-start.13 = (f32[17,8,128]{2,1,0:T(8,128)S(1)}, f32[17,8,128]{2,1,0:T(8,128)S(1)}, u32[]{:S(2)}, u32[]{:S(2)}) collective-permute-start(f32[17,8,128]{2,1,0:T(8,128)S(1)} %pad_maximum_fusion.12), channel_id=1, source_target_pairs={{0,12},{1,13},{2,14},{3,15},{4,8},{5,9},{6,10},{7,11},{8,4},{9,5},... | collective-permute-start | bytes 208904 | tf_op jit(solution)/shard_map/ppermute | solution.py:285
  45.7 2.6 %collective-permute-start.15 = (f32[17,8,128]{2,1,0:T(8,128)S(1)}, f32[17,8,128]{2,1,0:T(8,128)S(1)}, u32[]{:S(2)}, u32[]{:S(2)}) collective-permute-start(f32[17,8,128]{2,1,0:T(8,128)S(1)} %pad_maximum_fusion.12), channel_id=1, source_target_pairs={{0,4},{1,5},{2,6},{3,7},{4,0},{5,1},{6,2},{7,3},{8,12},{9,13},{10,... | collective-permute-start | bytes 208904 | tf_op jit(solution)/shard_map/ppermute | solution.py:285
  48.3 2.5 %collective-permute-done.13 = f32[17,8,128]{2,1,0:T(8,128)S(1)} collective-permute-done((f32[17,8,128]{2,1,0:T(8,128)S(1)}, f32[17,8,128]{2,1,0:T(8,128)S(1)}, u32[]{:S(2)}, u32[]{:S(2)}) %collective-permute-start.13) | collective-permute-done | bytes 69664 | tf_op jit(solution)/shard_map/ppermute | solution.py:285
  50.8 2.1 %collective-permute-done.14 = f32[17,8,128]{2,1,0:T(8,128)S(1)} collective-permute-done((f32[17,8,128]{2,1,0:T(8,128)S(1)}, f32[17,8,128]{2,1,0:T(8,128)S(1)}, u32[]{:S(2)}, u32[]{:S(2)}) %collective-permute-start.14) | collective-permute-done | bytes 69664 | tf_op jit(solution)/shard_map/ppermute | solution.py:285
  53.0 1.6 %collective-permute-start.18 = (f32[36,8,128]{2,1,0:T(8,128)S(1)}, f32[36,8,128]{2,1,0:T(8,128)S(1)}, u32[]{:S(2)}, u32[]{:S(2)}) collective-permute-start(f32[36,8,128]{2,1,0:T(8,128)S(1)} %pad_maximum_fusion.3), channel_id=1, source_target_pairs={{0,2},{1,3},{2,0},{3,1},{4,6},{5,7},{6,4},{7,5},{8,10},{9,11},{10,... | collective-permute-start | bytes 442376 | tf_op jit(solution)/shard_map/ppermute | solution.py:285
  55.4 3.5 %collective-permute-done.18 = f32[36,8,128]{2,1,0:T(8,128)S(1)} collective-permute-done((f32[36,8,128]{2,1,0:T(8,128)S(1)}, f32[36,8,128]{2,1,0:T(8,128)S(1)}, u32[]{:S(2)}, u32[]{:S(2)}) %collective-permute-start.18) | collective-permute-done | bytes 147488 | tf_op jit(solution)/shard_map/ppermute | solution.py:285
  61.2 5.8 %collective-permute-done.17.far_a = f32[64,8,128]{2,1,0:T(8,128)S(1)} collective-permute-done((f32[64,8,128]{2,1,0:T(8,128)S(1)}, f32[64,8,128]{2,1,0:T(8,128)S(1)}, u32[]{:S(2)}, u32[]{:S(2)}) %collective-permute-start.17) | collective-permute-done | bytes 262176 | tf_op jit(solution)/shard_map/ppermute | solution.py:285
  67.0 2.6 %shard_map.77 = (f32[128,2,8,128]{3,2,1,0:T(8,128)S(1)}, f32[128,2,8,128]{3,2,1,0:T(8,128)S(1)}, f32[17,8,128]{2,1,0:T(8,128)S(1)}, f32[64,2,8,128]{3,2,1,0:T(8,128)S(1)}, f32[8,128]{1,0:T(8,128)S(1)}) custom-call(s32[128]{0:T(128)S(1)} %get-tuple-element.99.place, s32[128]{0:T(128)S(1)} %get-tuple-element.100.away, f32[128]{0:T(128)S(1)} %get-tuple-element.101.keep, ...), custom_call_target="tpu_custom_call" | custom-call | tf_op jit(solution)/shard_map/pallas_call | solution.py:25
  71.0 2.4 %collective-permute-start.21 = (f32[17,8,128]{2,1,0:T(8,128)S(1)}, f32[17,8,128]{2,1,0:T(8,128)S(1)}, u32[]{:S(2)}, u32[]{:S(2)}) collective-permute-start(f32[17,8,128]{2,1,0:T(8,128)S(1)} %pad_maximum_fusion.13), channel_id=1, source_target_pairs={{0,12},{1,13},{2,14},{3,15},{4,8},{5,9},{6,10},{7,11},{8,4},{9,5},... | collective-permute-start | bytes 208904 | tf_op jit(solution)/shard_map/ppermute | solution.py:285
  73.4 2.0 %collective-permute-start.23 = (f32[17,8,128]{2,1,0:T(8,128)S(1)}, f32[17,8,128]{2,1,0:T(8,128)S(1)}, u32[]{:S(2)}, u32[]{:S(2)}) collective-permute-start(f32[17,8,128]{2,1,0:T(8,128)S(1)} %pad_maximum_fusion.13), channel_id=1, source_target_pairs={{0,4},{1,5},{2,6},{3,7},{4,0},{5,1},{6,2},{7,3},{8,12},{9,13},{10,... | collective-permute-start | bytes 208904 | tf_op jit(solution)/shard_map/ppermute | solution.py:285
  75.4 2.5 %collective-permute-done.21 = f32[17,8,128]{2,1,0:T(8,128)S(1)} collective-permute-done((f32[17,8,128]{2,1,0:T(8,128)S(1)}, f32[17,8,128]{2,1,0:T(8,128)S(1)}, u32[]{:S(2)}, u32[]{:S(2)}) %collective-permute-start.21) | collective-permute-done | bytes 69664 | tf_op jit(solution)/shard_map/ppermute | solution.py:285
  77.9 2.1 %collective-permute-done.22 = f32[17,8,128]{2,1,0:T(8,128)S(1)} collective-permute-done((f32[17,8,128]{2,1,0:T(8,128)S(1)}, f32[17,8,128]{2,1,0:T(8,128)S(1)}, u32[]{:S(2)}, u32[]{:S(2)}) %collective-permute-start.22) | collective-permute-done | bytes 69664 | tf_op jit(solution)/shard_map/ppermute | solution.py:285
  82.9 3.0 %collective-permute-done.26 = f32[36,8,128]{2,1,0:T(8,128)S(1)} collective-permute-done((f32[36,8,128]{2,1,0:T(8,128)S(1)}, f32[36,8,128]{2,1,0:T(8,128)S(1)}, u32[]{:S(2)}, u32[]{:S(2)}) %collective-permute-start.26) | collective-permute-done | bytes 147488 | tf_op jit(solution)/shard_map/ppermute | solution.py:285
  89.6 4.7 %collective-permute-done.25.far_a = f32[64,8,128]{2,1,0:T(8,128)S(1)} collective-permute-done((f32[64,8,128]{2,1,0:T(8,128)S(1)}, f32[64,8,128]{2,1,0:T(8,128)S(1)}, u32[]{:S(2)}, u32[]{:S(2)}) %collective-permute-start.25) | collective-permute-done | bytes 262176 | tf_op jit(solution)/shard_map/ppermute | solution.py:285
  94.3 2.8 %shard_map.79 = (f32[128,2,8,128]{3,2,1,0:T(8,128)S(1)}, f32[128,2,8,128]{3,2,1,0:T(8,128)S(1)}, f32[17,8,128]{2,1,0:T(8,128)S(1)}, f32[64,2,8,128]{3,2,1,0:T(8,128)S(1)}, f32[8,128]{1,0:T(8,128)S(1)}) custom-call(s32[128]{0:T(128)S(1)} %get-tuple-element.99.place, s32[128]{0:T(128)S(1)} %get-tuple-element.100.away, f32[128]{0:T(128)S(1)} %get-tuple-element.101.keep, ...), custom_call_target="tpu_custom_call" | custom-call | tf_op jit(solution)/shard_map/pallas_call | solution.py:25
  98.5 2.2 %collective-permute-start.30 = (f32[17,8,128]{2,1,0:T(8,128)S(1)}, f32[17,8,128]{2,1,0:T(8,128)S(1)}, u32[]{:S(2)}, u32[]{:S(2)}) collective-permute-start(f32[17,8,128]{2,1,0:T(8,128)S(1)} %pad_maximum_fusion.14), channel_id=1, source_target_pairs={{0,12},{1,13},{2,14},{3,15},{4,8},{5,9},{6,10},{7,11},{8,4},{9,5},... | collective-permute-start | bytes 208904 | tf_op jit(solution)/shard_map/ppermute | solution.py:285
  100.7 2.2 %collective-permute-start.32 = (f32[17,8,128]{2,1,0:T(8,128)S(1)}, f32[17,8,128]{2,1,0:T(8,128)S(1)}, u32[]{:S(2)}, u32[]{:S(2)}) collective-permute-start(f32[17,8,128]{2,1,0:T(8,128)S(1)} %pad_maximum_fusion.14), channel_id=1, source_target_pairs={{0,4},{1,5},{2,6},{3,7},{4,0},{5,1},{6,2},{7,3},{8,12},{9,13},{10,... | collective-permute-start | bytes 208904 | tf_op jit(solution)/shard_map/ppermute | solution.py:285
  102.9 2.5 %collective-permute-done.30 = f32[17,8,128]{2,1,0:T(8,128)S(1)} collective-permute-done((f32[17,8,128]{2,1,0:T(8,128)S(1)}, f32[17,8,128]{2,1,0:T(8,128)S(1)}, u32[]{:S(2)}, u32[]{:S(2)}) %collective-permute-start.30) | collective-permute-done | bytes 69664 | tf_op jit(solution)/shard_map/ppermute | solution.py:285
  105.4 2.1 %collective-permute-done.31 = f32[17,8,128]{2,1,0:T(8,128)S(1)} collective-permute-done((f32[17,8,128]{2,1,0:T(8,128)S(1)}, f32[17,8,128]{2,1,0:T(8,128)S(1)}, u32[]{:S(2)}, u32[]{:S(2)}) %collective-permute-start.31) | collective-permute-done | bytes 69664 | tf_op jit(solution)/shard_map/ppermute | solution.py:285
  110.2 3.2 %collective-permute-done.35 = f32[36,8,128]{2,1,0:T(8,128)S(1)} collective-permute-done((f32[36,8,128]{2,1,0:T(8,128)S(1)}, f32[36,8,128]{2,1,0:T(8,128)S(1)}, u32[]{:S(2)}, u32[]{:S(2)}) %collective-permute-start.35) | collective-permute-done | bytes 147488 | tf_op jit(solution)/shard_map/ppermute | solution.py:285
  117.0 4.6 %collective-permute-done.34.far_a = f32[64,8,128]{2,1,0:T(8,128)S(1)} collective-permute-done((f32[64,8,128]{2,1,0:T(8,128)S(1)}, f32[64,8,128]{2,1,0:T(8,128)S(1)}, u32[]{:S(2)}, u32[]{:S(2)}) %collective-permute-start.34) | collective-permute-done | bytes 262176 | tf_op jit(solution)/shard_map/ppermute | solution.py:285
  121.7 2.9 %shard_map.81 = (f32[32,8,128]{2,1,0:T(8,128)S(1)}, f32[64,2,8,128]{3,2,1,0:T(8,128)S(1)}, f32[8,128]{1,0:T(8,128)S(1)}) custom-call(s32[128]{0:T(128)S(1)} %get-tuple-element.99.place, s32[128]{0:T(128)S(1)} %get-tuple-element.100.away, f32[128]{0:T(128)S(1)} %get-tuple-element.101.keep, s32[64]{0:T(128)S(1)} %get-tuple-element.102.picked, ...), custom_call_target="tpu_custom_call" | custom-call | tf_op jit(solution)/shard_map/pallas_call | solution.py:25
  124.6 11.8 %all_to_all.5.sums = f32[32,8,128]{2,1,0:T(8,128)S(1)} all-to-all(f32[32,8,128]{2,1,0:T(8,128)S(1)} %get-tuple-element.148), channel_id=1, replica_groups=mesh['body'=2,'sub'=16] {'body','sub'}, dimensions={0} | all-to-all | bytes 262144 | tf_op jit(solution)/shard_map/all_to_all | solution.py:428
  136.5 2.2 %shard_map.82 = f32[8,64,256]{2,1,0:T(8,128)} custom-call(f32[64]{0:T(128)S(1)} %get-tuple-element.231.keep, f32[32,8,128]{2,1,0:T(8,128)S(1)} %all_to_all.5.sums, f32[8,128]{1,0:T(8,128)S(1)} %get-tuple-element.149.known, f32[64,256]{1,0:T(8,128)S(1)} %copy-done, f32[64,2,8,128]{3,2,1,0:T(8,128)S(1)} %get-tuple-element.150.mine, ...), custom_call_target="tpu_custom_call" | custom-call | tf_op jit(solution)/shard_map/pallas_call | solution.py:25
  (137 shorter events, 34.1 us)
Async XLA Ops:
  4.2 10.7 %collective-permute-start = (f32[32,8,128]{2,1,0:T(8,128)S(1)}, f32[32,8,128]{2,1,0:T(8,128)S(1)}, u32[]{:S(2)}, u32[]{:S(2)}) collective-permute-start(f32[32,8,128]{2,1,0:T(8,128)S(1)} %get-tuple-element.81), channel_id=1, source_target_pairs={{0,12},{1,13},{2,14},{3,15},{4,8},{5,9},{6,10},{7,11},{8,4},{9,5},... | collective-permute-start | bytes 393224 | tf_op jit(solution)/shard_map/ppermute | solution.py:285
  11.3 10.5 %collective-permute-start.3 = (f32[44,8,128]{2,1,0:T(8,128)S(1)}, f32[44,8,128]{2,1,0:T(8,128)S(1)}, u32[]{:S(2)}, u32[]{:S(2)}) collective-permute-start(f32[44,8,128]{2,1,0:T(8,128)S(1)} %get-tuple-element.87), channel_id=1, source_target_pairs={{0,1},{1,0},{2,3},{3,2},{4,5},{5,4},{6,7},{7,6},{8,9},{9,8},{10,11... | collective-permute-start | bytes 540680 | tf_op jit(solution)/shard_map/ppermute | solution.py:285
  12.9 9.6 %collective-permute-start.4 = (f32[44,8,128]{2,1,0:T(8,128)S(1)}, f32[44,8,128]{2,1,0:T(8,128)S(1)}, u32[]{:S(2)}, u32[]{:S(2)}) collective-permute-start(f32[44,8,128]{2,1,0:T(8,128)S(1)} %get-tuple-element.88), channel_id=1, source_target_pairs={{0,2},{1,3},{2,0},{3,1},{4,6},{5,7},{6,4},{7,5},{8,10},{9,11},{10,... | collective-permute-start | bytes 540680 | tf_op jit(solution)/shard_map/ppermute | solution.py:285
  14.4 8.1 %collective-permute-start.5 = (f32[44,8,128]{2,1,0:T(8,128)S(1)}, f32[44,8,128]{2,1,0:T(8,128)S(1)}, u32[]{:S(2)}, u32[]{:S(2)}) collective-permute-start(f32[44,8,128]{2,1,0:T(8,128)S(1)} %get-tuple-element.89), channel_id=1, source_target_pairs={{0,3},{1,2},{2,1},{3,0},{4,7},{5,6},{6,5},{7,4},{8,11},{9,10},{10,... | collective-permute-start | bytes 540680 | tf_op jit(solution)/shard_map/ppermute | solution.py:285
  14.9 6.9 %collective-permute-start.1 = (f32[32,8,128]{2,1,0:T(8,128)S(1)}, f32[32,8,128]{2,1,0:T(8,128)S(1)}, u32[]{:S(2)}, u32[]{:S(2)}) collective-permute-start(f32[32,8,128]{2,1,0:T(8,128)S(1)} %get-tuple-element.82), channel_id=1, source_target_pairs={{0,8},{1,9},{2,10},{3,11},{4,12},{5,13},{6,14},{7,15},{8,0},{9,1},... | collective-permute-start | bytes 393224 | tf_op jit(solution)/shard_map/ppermute | solution.py:285
  14.9 6.9 %collective-permute-start.2 = (f32[32,8,128]{2,1,0:T(8,128)S(1)}, f32[32,8,128]{2,1,0:T(8,128)S(1)}, u32[]{:S(2)}, u32[]{:S(2)}) collective-permute-start(f32[32,8,128]{2,1,0:T(8,128)S(1)} %get-tuple-element.83), channel_id=1, source_target_pairs={{0,4},{1,5},{2,6},{3,7},{4,0},{5,1},{6,2},{7,3},{8,12},{9,13},{10,... | collective-permute-start | bytes 393224 | tf_op jit(solution)/shard_map/ppermute | solution.py:285
  22.6 16.4 %collective-permute-start.11 = (f32[44,8,128]{2,1,0:T(8,128)S(1)}, f32[44,8,128]{2,1,0:T(8,128)S(1)}, u32[]{:S(2)}, u32[]{:S(2)}) collective-permute-start(f32[44,8,128]{2,1,0:T(8,128)S(1)} %pad_maximum_fusion.2), channel_id=1, source_target_pairs={{0,12},{1,13},{2,14},{3,15},{4,8},{5,9},{6,10},{7,11},{8,4},{9,5},... | collective-permute-start | bytes 540680 | tf_op jit(solution)/shard_map/ppermute | solution.py:285
  23.5 15.5 %collective-permute-start.10 = (f32[44,8,128]{2,1,0:T(8,128)S(1)}, f32[44,8,128]{2,1,0:T(8,128)S(1)}, u32[]{:S(2)}, u32[]{:S(2)}) collective-permute-start(f32[44,8,128]{2,1,0:T(8,128)S(1)} %pad_maximum_fusion.1), channel_id=1, source_target_pairs={{0,8},{1,9},{2,10},{3,11},{4,12},{5,13},{6,14},{7,15},{8,0},{9,1},... | collective-permute-start | bytes 540680 | tf_op jit(solution)/shard_map/ppermute | solution.py:285
  23.9 15.1 %collective-permute-start.9 = (f32[44,8,128]{2,1,0:T(8,128)S(1)}, f32[44,8,128]{2,1,0:T(8,128)S(1)}, u32[]{:S(2)}, u32[]{:S(2)}) collective-permute-start(f32[44,8,128]{2,1,0:T(8,128)S(1)} %pad_maximum_fusion), channel_id=1, source_target_pairs={{0,4},{1,5},{2,6},{3,7},{4,0},{5,1},{6,2},{7,3},{8,12},{9,13},{10,... | collective-permute-start | bytes 540680 | tf_op jit(solution)/shard_map/ppermute | solution.py:285
  27.3 6.8 %collective-permute-start.8 = (f32[32,8,128]{2,1,0:T(8,128)S(1)}, f32[32,8,128]{2,1,0:T(8,128)S(1)}, u32[]{:S(2)}, u32[]{:S(2)}) collective-permute-start(f32[32,8,128]{2,1,0:T(8,128)S(1)} %pad_maximum_fusion.8), channel_id=1, source_target_pairs={{0,3},{1,2},{2,1},{3,0},{4,7},{5,6},{6,5},{7,4},{8,11},{9,10},{10,... | collective-permute-start | bytes 393224 | tf_op jit(solution)/shard_map/ppermute | solution.py:285
  29.1 5.8 %collective-permute-start.7 = (f32[32,8,128]{2,1,0:T(8,128)S(1)}, f32[32,8,128]{2,1,0:T(8,128)S(1)}, u32[]{:S(2)}, u32[]{:S(2)}) collective-permute-start(f32[32,8,128]{2,1,0:T(8,128)S(1)} %pad_maximum_fusion.7), channel_id=1, source_target_pairs={{0,2},{1,3},{2,0},{3,1},{4,6},{5,7},{6,4},{7,5},{8,10},{9,11},{10,... | collective-permute-start | bytes 393224 | tf_op jit(solution)/shard_map/ppermute | solution.py:285
  43.8 7.0 %collective-permute-start.13 = (f32[17,8,128]{2,1,0:T(8,128)S(1)}, f32[17,8,128]{2,1,0:T(8,128)S(1)}, u32[]{:S(2)}, u32[]{:S(2)}) collective-permute-start(f32[17,8,128]{2,1,0:T(8,128)S(1)} %pad_maximum_fusion.12), channel_id=1, source_target_pairs={{0,12},{1,13},{2,14},{3,15},{4,8},{5,9},{6,10},{7,11},{8,4},{9,5},... | collective-permute-start | bytes 208904 | tf_op jit(solution)/shard_map/ppermute | solution.py:285
  45.7 7.2 %collective-permute-start.14 = (f32[17,8,128]{2,1,0:T(8,128)S(1)}, f32[17,8,128]{2,1,0:T(8,128)S(1)}, u32[]{:S(2)}, u32[]{:S(2)}) collective-permute-start(f32[17,8,128]{2,1,0:T(8,128)S(1)} %pad_maximum_fusion.12), channel_id=1, source_target_pairs={{0,8},{1,9},{2,10},{3,11},{4,12},{5,13},{6,14},{7,15},{8,0},{9,1},... | collective-permute-start | bytes 208904 | tf_op jit(solution)/shard_map/ppermute | solution.py:285
  45.7 7.2 %collective-permute-start.15 = (f32[17,8,128]{2,1,0:T(8,128)S(1)}, f32[17,8,128]{2,1,0:T(8,128)S(1)}, u32[]{:S(2)}, u32[]{:S(2)}) collective-permute-start(f32[17,8,128]{2,1,0:T(8,128)S(1)} %pad_maximum_fusion.12), channel_id=1, source_target_pairs={{0,4},{1,5},{2,6},{3,7},{4,0},{5,1},{6,2},{7,3},{8,12},{9,13},{10,... | collective-permute-start | bytes 208904 | tf_op jit(solution)/shard_map/ppermute | solution.py:285
  53.0 5.8 %collective-permute-start.18 = (f32[36,8,128]{2,1,0:T(8,128)S(1)}, f32[36,8,128]{2,1,0:T(8,128)S(1)}, u32[]{:S(2)}, u32[]{:S(2)}) collective-permute-start(f32[36,8,128]{2,1,0:T(8,128)S(1)} %pad_maximum_fusion.3), channel_id=1, source_target_pairs={{0,2},{1,3},{2,0},{3,1},{4,6},{5,7},{6,4},{7,5},{8,10},{9,11},{10,... | collective-permute-start | bytes 442376 | tf_op jit(solution)/shard_map/ppermute | solution.py:285
  58.8 8.2 %collective-permute-start.19 = (f32[72,8,128]{2,1,0:T(8,128)S(1)}, f32[72,8,128]{2,1,0:T(8,128)S(1)}, u32[]{:S(2)}, u32[]{:S(2)}) collective-permute-start(f32[72,8,128]{2,1,0:T(8,128)S(1)} %constant_dynamic-update-slice_fusion.5.near_b), channel_id=1, source_target_pairs={{0,1},{1,0},{2,3},{3,2},{4,5},{5,4},{6,7},{7,6},{8,9},{9,8},{10,11... | collective-permute-start | bytes 884744 | tf_op jit(solution)/shard_map/ppermute | solution.py:285
  59.9 7.2 %collective-permute-start.17 = (f32[64,8,128]{2,1,0:T(8,128)S(1)}, f32[64,8,128]{2,1,0:T(8,128)S(1)}, u32[]{:S(2)}, u32[]{:S(2)}) collective-permute-start(f32[64,8,128]{2,1,0:T(8,128)S(1)} %constant_dynamic-update-slice_fusion.near_a), channel_id=1, source_target_pairs={{0,2},{1,3},{2,0},{3,1},{4,6},{5,7},{6,4},{7,5},{8,10},{9,11},{10,... | collective-permute-start | bytes 786440 | tf_op jit(solution)/shard_map/ppermute | solution.py:285
  71.0 7.0 %collective-permute-start.21 = (f32[17,8,128]{2,1,0:T(8,128)S(1)}, f32[17,8,128]{2,1,0:T(8,128)S(1)}, u32[]{:S(2)}, u32[]{:S(2)}) collective-permute-start(f32[17,8,128]{2,1,0:T(8,128)S(1)} %pad_maximum_fusion.13), channel_id=1, source_target_pairs={{0,12},{1,13},{2,14},{3,15},{4,8},{5,9},{6,10},{7,11},{8,4},{9,5},... | collective-permute-start | bytes 208904 | tf_op jit(solution)/shard_map/ppermute | solution.py:285
  73.4 6.7 %collective-permute-start.22 = (f32[17,8,128]{2,1,0:T(8,128)S(1)}, f32[17,8,128]{2,1,0:T(8,128)S(1)}, u32[]{:S(2)}, u32[]{:S(2)}) collective-permute-start(f32[17,8,128]{2,1,0:T(8,128)S(1)} %pad_maximum_fusion.13), channel_id=1, source_target_pairs={{0,8},{1,9},{2,10},{3,11},{4,12},{5,13},{6,14},{7,15},{8,0},{9,1},... | collective-permute-start | bytes 208904 | tf_op jit(solution)/shard_map/ppermute | solution.py:285
  73.4 6.7 %collective-permute-start.23 = (f32[17,8,128]{2,1,0:T(8,128)S(1)}, f32[17,8,128]{2,1,0:T(8,128)S(1)}, u32[]{:S(2)}, u32[]{:S(2)}) collective-permute-start(f32[17,8,128]{2,1,0:T(8,128)S(1)} %pad_maximum_fusion.13), channel_id=1, source_target_pairs={{0,4},{1,5},{2,6},{3,7},{4,0},{5,1},{6,2},{7,3},{8,12},{9,13},{10,... | collective-permute-start | bytes 208904 | tf_op jit(solution)/shard_map/ppermute | solution.py:285
  75.4 13.3 %collective-permute-start.28 = (f32[64,2,8,128]{3,2,1,0:T(8,128)S(1)}, f32[64,2,8,128]{3,2,1,0:T(8,128)S(1)}, u32[]{:S(2)}, u32[]{:S(2)}) collective-permute-start(f32[64,2,8,128]{3,2,1,0:T(8,128)S(1)} %get-tuple-element.118.mine), channel_id=1, source_target_pairs={{0,16},{16,0},{1,17},{17,1},{2,18},{18,2},{3,19},{19,3},{4,20},{20... | collective-permute-start | bytes 1572872 | tf_op jit(solution)/shard_map/ppermute | solution.py:288
  80.1 5.8 %collective-permute-start.26 = (f32[36,8,128]{2,1,0:T(8,128)S(1)}, f32[36,8,128]{2,1,0:T(8,128)S(1)}, u32[]{:S(2)}, u32[]{:S(2)}) collective-permute-start(f32[36,8,128]{2,1,0:T(8,128)S(1)} %pad_maximum_fusion.4), channel_id=1, source_target_pairs={{0,2},{1,3},{2,0},{3,1},{4,6},{5,7},{6,4},{7,5},{8,10},{9,11},{10,... | collective-permute-start | bytes 442376 | tf_op jit(solution)/shard_map/ppermute | solution.py:285
  86.0 8.4 %collective-permute-start.27 = (f32[72,8,128]{2,1,0:T(8,128)S(1)}, f32[72,8,128]{2,1,0:T(8,128)S(1)}, u32[]{:S(2)}, u32[]{:S(2)}) collective-permute-start(f32[72,8,128]{2,1,0:T(8,128)S(1)} %constant_dynamic-update-slice_fusion.15.near_b), channel_id=1, source_target_pairs={{0,1},{1,0},{2,3},{3,2},{4,5},{5,4},{6,7},{7,6},{8,9},{9,8},{10,11... | collective-permute-start | bytes 884744 | tf_op jit(solution)/shard_map/ppermute | solution.py:285
  87.2 7.2 %collective-permute-start.25 = (f32[64,8,128]{2,1,0:T(8,128)S(1)}, f32[64,8,128]{2,1,0:T(8,128)S(1)}, u32[]{:S(2)}, u32[]{:S(2)}) collective-permute-start(f32[64,8,128]{2,1,0:T(8,128)S(1)} %constant_dynamic-update-slice_fusion.10.near_a), channel_id=1, source_target_pairs={{0,2},{1,3},{2,0},{3,1},{4,6},{5,7},{6,4},{7,5},{8,10},{9,11},{10,... | collective-permute-start | bytes 786440 | tf_op jit(solution)/shard_map/ppermute | solution.py:285
  98.5 7.0 %collective-permute-start.30 = (f32[17,8,128]{2,1,0:T(8,128)S(1)}, f32[17,8,128]{2,1,0:T(8,128)S(1)}, u32[]{:S(2)}, u32[]{:S(2)}) collective-permute-start(f32[17,8,128]{2,1,0:T(8,128)S(1)} %pad_maximum_fusion.14), channel_id=1, source_target_pairs={{0,12},{1,13},{2,14},{3,15},{4,8},{5,9},{6,10},{7,11},{8,4},{9,5},... | collective-permute-start | bytes 208904 | tf_op jit(solution)/shard_map/ppermute | solution.py:285
  100.7 6.8 %collective-permute-start.31 = (f32[17,8,128]{2,1,0:T(8,128)S(1)}, f32[17,8,128]{2,1,0:T(8,128)S(1)}, u32[]{:S(2)}, u32[]{:S(2)}) collective-permute-start(f32[17,8,128]{2,1,0:T(8,128)S(1)} %pad_maximum_fusion.14), channel_id=1, source_target_pairs={{0,8},{1,9},{2,10},{3,11},{4,12},{5,13},{6,14},{7,15},{8,0},{9,1},... | collective-permute-start | bytes 208904 | tf_op jit(solution)/shard_map/ppermute | solution.py:285
  100.7 6.8 %collective-permute-start.32 = (f32[17,8,128]{2,1,0:T(8,128)S(1)}, f32[17,8,128]{2,1,0:T(8,128)S(1)}, u32[]{:S(2)}, u32[]{:S(2)}) collective-permute-start(f32[17,8,128]{2,1,0:T(8,128)S(1)} %pad_maximum_fusion.14), channel_id=1, source_target_pairs={{0,4},{1,5},{2,6},{3,7},{4,0},{5,1},{6,2},{7,3},{8,12},{9,13},{10,... | collective-permute-start | bytes 208904 | tf_op jit(solution)/shard_map/ppermute | solution.py:285
  102.9 13.1 %collective-permute-start.37 = (f32[64,2,8,128]{3,2,1,0:T(8,128)S(1)}, f32[64,2,8,128]{3,2,1,0:T(8,128)S(1)}, u32[]{:S(2)}, u32[]{:S(2)}) collective-permute-start(f32[64,2,8,128]{3,2,1,0:T(8,128)S(1)} %get-tuple-element.135.mine), channel_id=1, source_target_pairs={{0,16},{16,0},{1,17},{17,1},{2,18},{18,2},{3,19},{19,3},{4,20},{20... | collective-permute-start | bytes 1572872 | tf_op jit(solution)/shard_map/ppermute | solution.py:288
  107.6 5.8 %collective-permute-start.35 = (f32[36,8,128]{2,1,0:T(8,128)S(1)}, f32[36,8,128]{2,1,0:T(8,128)S(1)}, u32[]{:S(2)}, u32[]{:S(2)}) collective-permute-start(f32[36,8,128]{2,1,0:T(8,128)S(1)} %pad_maximum_fusion.5), channel_id=1, source_target_pairs={{0,2},{1,3},{2,0},{3,1},{4,6},{5,7},{6,4},{7,5},{8,10},{9,11},{10,... | collective-permute-start | bytes 442376 | tf_op jit(solution)/shard_map/ppermute | solution.py:285
  113.5 8.2 %collective-permute-start.36 = (f32[72,8,128]{2,1,0:T(8,128)S(1)}, f32[72,8,128]{2,1,0:T(8,128)S(1)}, u32[]{:S(2)}, u32[]{:S(2)}) collective-permute-start(f32[72,8,128]{2,1,0:T(8,128)S(1)} %constant_dynamic-update-slice_fusion.25.near_b), channel_id=1, source_target_pairs={{0,1},{1,0},{2,3},{3,2},{4,5},{5,4},{6,7},{7,6},{8,9},{9,8},{10,11... | collective-permute-start | bytes 884744 | tf_op jit(solution)/shard_map/ppermute | solution.py:285
  114.5 7.2 %collective-permute-start.34 = (f32[64,8,128]{2,1,0:T(8,128)S(1)}, f32[64,8,128]{2,1,0:T(8,128)S(1)}, u32[]{:S(2)}, u32[]{:S(2)}) collective-permute-start(f32[64,8,128]{2,1,0:T(8,128)S(1)} %constant_dynamic-update-slice_fusion.20.near_a), channel_id=1, source_target_pairs={{0,2},{1,3},{2,0},{3,1},{4,6},{5,7},{6,4},{7,5},{8,10},{9,11},{10,... | collective-permute-start | bytes 786440 | tf_op jit(solution)/shard_map/ppermute | solution.py:285
  124.5 11.9 %collective-permute-start.38 = (f32[64,2,8,128]{3,2,1,0:T(8,128)S(1)}, f32[64,2,8,128]{3,2,1,0:T(8,128)S(1)}, u32[]{:S(2)}, u32[]{:S(2)}) collective-permute-start(f32[64,2,8,128]{3,2,1,0:T(8,128)S(1)} %get-tuple-element.150.mine), channel_id=1, source_target_pairs={{0,16},{16,0},{1,17},{17,1},{2,18},{18,2},{3,19},{19,3},{4,20},{20... | collective-permute-start | bytes 1572872 | tf_op jit(solution)/shard_map/ppermute | solution.py:288
  (8 other events, 71.0 us)
